TPU v7x, 32 devices: a whole 2x2x4 slice. The times are simulated.
32 devices in a mesh: grp: 2 (over x), term: 16 (over z, y, core).
Axes of the slice: x: 2, y: 2, z: 4, core: 2. Of those that a mesh axis runs over, the one named last changes fastest.
Arguments:
- wavefunction: bfloat16 [6, 512, 512], P('grp', 'term'), parts along dimension 0
- diagonal: bfloat16 [6, 512, 512], P('grp', 'term'), parts along dimension 0, may hold values from 1 to 10
- left_blocks: bfloat16 [256, 512, 512], P(('grp', 'term')), parts along dimension 0, may hold values from -0.25 to 0.25
- right_blocks: bfloat16 [256, 512, 512], P(('grp', 'term')), parts along dimension 0, may hold values from -0.09375 to 0.09375
- block_source: int32 [256], P(('grp', 'term')), parts along dimension 0, may hold values from 0 to 2
- block_target: int32 [256], P(('grp', 'term')), parts along dimension 0, may hold values from 0 to 2
- live_count: int32 [32], P(('grp', 'term')), parts along dimension 0, may hold values from 1 to 8, as said below
Outputs:
- first_image: float32 [6, 512, 512], P('grp', 'term'), parts along dimension 0
- second_vector: float32 [6, 512, 512], P('grp', 'term'), parts along dimension 0
- second_image: float32 [6, 512, 512], P('grp', 'term'), parts along dimension 0
There are 2 independent parts, one for each index of `grp`. A program takes and returns all parts, laid end to end along the dimension named above; each array names one. Nothing has to cross between parts.
Inputs may be any that keep to these rules, and one draw needn't show every extreme that they name: A device's used slots are its first live_count slots; some device uses all 8 in every draw.
All inputs are finite; a program needn't handle non-finite values.
Results may differ from a plain program's by a relative error of at most 0.0032.
Values may be sent and summed in bfloat16 or wider, within the bound.
No kernel may reach another device: no remote copies, remote signals or barrier semaphores. Data moves between devices by JAX's collectives and lax.ppermute only.
A program may use at most 64 MiB of HBM per device.

v0:
```python
import jax
import jax.numpy as jnp
from jax import lax
from jax.sharding import PartitionSpec as P


def block_loop(field_rounded, left_ops, right_ops, sources, targets, last_slot, partial_sum):

    def add_block(slot_index, running):
        left_op = lax.dynamic_index_in_dim(left_ops, slot_index, 0, keepdims=False)
        right_op = lax.dynamic_index_in_dim(right_ops, slot_index, 0, keepdims=False)
        source = lax.dynamic_index_in_dim(sources, slot_index, 0, keepdims=False)
        target = lax.dynamic_index_in_dim(targets, slot_index, 0, keepdims=False)
        piece = lax.dynamic_index_in_dim(field_rounded, source, 0, keepdims=False)
        product = jnp.dot(left_op, piece, preferred_element_type=jnp.float32).astype(jnp.bfloat16)
        term_value = jnp.dot(product, right_op.T, preferred_element_type=jnp.float32)
        before = lax.dynamic_index_in_dim(running, target, 0, keepdims=False)
        return lax.dynamic_update_index_in_dim(running, before + term_value, target, 0)

    return lax.fori_loop(0, last_slot, add_block, partial_sum)


def on_device(
    wavefunction, diagonal, left_blocks, right_blocks, block_source, block_target, live_count
):
    devices = lax.axis_size("term")
    position = lax.axis_index("term")
    row_count = wavefunction.shape[1]
    sector_count = wavefunction.shape[0]
    width = wavefunction.shape[2]
    entries = float(sector_count * row_count * devices * width)
    own_count = live_count[0]
    diag_own = diagonal.astype(jnp.float32)
    whole_wave = lax.all_gather(wavefunction, "term", axis=1, tiled=True).astype(jnp.float32)
    scale = jnp.sqrt(jnp.sum(whole_wave * whole_wave) / entries)
    start_whole = whole_wave / scale
    empty_sum = jnp.zeros(start_whole.shape, jnp.float32)
    first_terms = block_loop(
        start_whole.astype(jnp.bfloat16),
        left_blocks,
        right_blocks,
        block_source,
        block_target,
        own_count,
        empty_sum,
    )
    row_start = position * row_count
    whole_diag = lax.all_gather(diagonal, "term", axis=1, tiled=True).astype(jnp.float32)
    first_whole = lax.psum(first_terms, "term") + whole_diag * start_whole
    ritz_value = jnp.sum(start_whole * first_whole) / entries
    correction = (first_whole - ritz_value * start_whole) / jnp.maximum(
        jnp.abs(whole_diag - ritz_value), 1.0
    )
    correlation = jnp.sum(start_whole * correction) / entries
    projected = correction - correlation * start_whole
    second_whole = projected / jnp.sqrt(jnp.sum(projected * projected) / entries)
    first_image = lax.dynamic_slice_in_dim(first_whole, row_start, row_count, 1)
    second_vector = lax.dynamic_slice_in_dim(second_whole, row_start, row_count, 1)
    second_rounded = second_whole.astype(jnp.bfloat16)
    second_terms = block_loop(
        second_rounded, left_blocks, right_blocks, block_source, block_target, own_count, empty_sum
    )
    second_image = (
        lax.psum_scatter(second_terms, "term", scatter_dimension=1, tiled=True)
        + diag_own * second_vector
    )
    return (first_image, second_vector, second_image)


def solution(mesh):
    placed = (
        P("grp", "term", None),
        P("grp", "term", None),
        P(("grp", "term"), None, None),
        P(("grp", "term"), None, None),
        P(("grp", "term")),
        P(("grp", "term")),
        P(("grp", "term")),
    )
    return jax.shard_map(
        on_device,
        mesh=mesh,
        in_specs=placed,
        out_specs=(P("grp", "term", None), P("grp", "term", None), P("grp", "term", None)),
        check_vma=False,
    )
```

profile of v0, /device:TPU:0, one launch (start us, length us, event | category | flops | bytes accessed | tf_op | source)
XLA Modules:
  0.0 418.6 jit_solution(733760555475617403)
XLA Ops:
  8.7 43.9 %all-gather.3.cloned.1.call-done = bf16[3,512,512]{2,1,0:T(8,128)(2,1)} async-done(((bf16[3,32,512]{2,1,0:T(8,128)(2,1)}), bf16[3,512,512]{2,1,0:T(8,128)(2,1)}) %all-gather.3.cloned.1.call-update) | async-done | bytes 1572880 | tf_op jit(solution)/shard_map/all_gather | solution.py:34
  52.6 2.8 fusion.28
  56.2 1.7 fusion.33
  57.9 2.1 broadcast_in_dim.10.clone
  59.9 50.4 %while.20 = (s32[]{:T(128)}, f32[3,512,512]{2,1,0:T(8,128)}, s32[]{:T(128)}, s32[8]{0:T(128)S(1)}, bf16[8,512,512]{2,1,0:T(8,128)(2,1)}, /*index=5*/s32[8]{0:T(1...) while((s32[]{:T(128)}, f32[3,512,512]{2,1,0:T(8,128)}, ...), condition=%wide.region_2.3_spmd, body=%wide.region_1.2_spmd.sunk | while | flops 537395200 | bytes 5769471 | solution.py:20
  65.7 1.3 constant_dynamic-slice_fusion.7
  67.0 2.9 fusion.47
  75.6 1.3 constant_dynamic-slice_fusion.7
  76.9 3.0 fusion.47
  85.6 1.3 constant_dynamic-slice_fusion.7
  86.9 2.9 fusion.47
  95.5 1.3 constant_dynamic-slice_fusion.7
  96.9 2.9 fusion.47
  105.5 1.3 constant_dynamic-slice_fusion.7
  106.8 2.9 fusion.47
  110.5 132.2 %all-reduce.2.cloned.1.call-done = f32[3,512,512]{2,1,0:T(8,128)} async-done(((f32[3,512,512]{2,1,0:T(8,128)}), f32[3,512,512]{2,1,0:T(8,128)}) %all-reduce.2.cloned.1.call-update) | async-done | bytes 3145744 | tf_op jit(solution)/shard_map/psum | solution.py:49
  242.7 5.4 %multiply_reduce_fusion.2 = (f32[]{:T(128)}, f32[3,512,512]{2,1,0:T(8,128)}) fusion(f32[]{:T(128)S(6)} %sqrt.6, bf16[3,512,512]{2,1,0:T(8,128)(2,1)S(1)} %copy-done, f32[3,512,512]{2,1,0:T(8,128)} %all-reduce.2.cloned.1.call-done, bf16[3,512,512]{2,1,0:T(8,128)(2,1)} %all-gather.5.cloned.1.call-done), kind=kLoop, calls=%fused_computation.36 | loop fusion | flops 5505023 | bytes 9437192 | tf_op jit(solution)/shard_map/reduce_sum | solution.py:50
  248.7 3.7 multiply_reduce_fusion.1
  253.1 5.6 %multiply_reduce_fusion = (f32[]{:T(128)}, f32[3,512,512]{2,1,0:T(8,128)}) fusion(f32[]{:T(128)S(6)} %div.32, bf16[3,512,512]{2,1,0:T(8,128)(2,1)S(1)} %copy-done.1, f32[3,512,512]{2,1,0:T(8,128)} %get-tuple-element.130, f32[]{:T(128)S(6)} %sqrt.6, bf16[3,512,512]{2,1,0:T(8,128)(2,1)S(1)} %copy-done, f32[]{:T(128)S(6)} %div.30), kind=kLoop, calls=%fused_computation.33 | loop fusion | flops 10223615 | bytes 9437200 | tf_op jit(solution)/shard_map/reduce_sum | solution.py:56
  259.4 4.1 fusion.34
  263.5 2.1 broadcast_in_dim.10
  265.6 50.5 %while.21 = (s32[]{:T(128)}, f32[3,512,512]{2,1,0:T(8,128)}, s32[]{:T(128)}, s32[8]{0:T(128)S(1)}, bf16[8,512,512]{2,1,0:T(8,128)(2,1)}, /*index=5*/s32[8]{0:T(1...) while((s32[]{:T(128)}, f32[3,512,512]{2,1,0:T(8,128)}, ...), condition=%wide.region_8.9_spmd, body=%wide.region_7.8_spmd.sunk | while | flops 537395200 | bytes 5769471 | solution.py:20
  271.3 1.3 constant_dynamic-slice_fusion.8
  272.6 2.9 fusion.51
  281.3 1.3 constant_dynamic-slice_fusion.8
  282.6 2.9 fusion.51
  292.6 3.0 fusion.51
  302.5 2.9 fusion.51
  312.5 2.9 fusion.51
  316.1 1.6 constant_dynamic-slice_fusion.3
  317.7 92.5 %reduce-scatter.2.cloned.1.call-done = f32[3,32,512]{2,1,0:T(8,128)} async-done(((f32[3,512,512]{2,1,0:T(8,128)}), f32[3,32,512]{2,1,0:T(8,128)}) %reduce-scatter.2.cloned.1.call-update) | async-done | bytes 196624 | tf_op jit(solution)/shard_map/reduce_scatter | solution.py:64
  410.2 1.8 multiply_add_fusion
  (42 shorter events, 17.3 us)
Async XLA Ops:
  7.2 45.5 %all-gather.3.cloned.1.call-start = ((), (), s32[]{:S(2)}) async-start(), calls=%async_computation.1 | async-start | bytes 1671168 | tf_op jit(solution)/shard_map/all_gather | solution.py:34
  7.9 102.6 %all-gather.5.cloned.1.call-start = ((), (), s32[]{:S(2)}) async-start(), calls=%async_computation.3 | async-start | bytes 1671168 | tf_op jit(solution)/shard_map/all_gather | solution.py:48
  8.6 234.0 %all-reduce.2.cloned.1.call-start = ((), (), s32[]{:S(2)}) async-start(), calls=%async_computation.2 | async-start | bytes 6291456 | tf_op jit(solution)/shard_map/psum | solution.py:49
  56.1 3.8 copy-start.3
  56.2 3.8 copy-start.4
  110.4 132.3 %copy-start = (bf16[3,512,512]{2,1,0:T(8,128)(2,1)S(1)}, bf16[3,512,512]{2,1,0:T(8,128)(2,1)}, u32[]{:S(2)}) copy-start(bf16[3,512,512]{2,1,0:T(8,128)(2,1)} %all-gather.3.cloned.1.call-done) | copy-start | bytes 4718596
  110.4 299.8 %reduce-scatter.2.cloned.1.call-start = ((), (), s32[]{:S(2)}) async-start(), calls=%async_computation.4 | async-start | bytes 3342336 | tf_op jit(solution)/shard_map/reduce_scatter | solution.py:64
  110.5 138.2 %copy-start.1 = (bf16[3,512,512]{2,1,0:T(8,128)(2,1)S(1)}, bf16[3,512,512]{2,1,0:T(8,128)(2,1)}, u32[]{:S(2)}) copy-start(bf16[3,512,512]{2,1,0:T(8,128)(2,1)} %all-gather.5.cloned.1.call-done) | copy-start | bytes 4718596
  316.1 94.2 %copy-start.2 = (bf16[3,32,512]{2,1,0:T(8,128)(2,1)S(1)}, bf16[3,32,512]{2,1,0:T(8,128)(2,1)}, u32[]{:S(2)}) copy-start(bf16[3,32,512]{2,1,0:T(8,128)(2,1)} %param.12) | copy-start | bytes 294916
Sparse Core Ops, SparseCore 0:
  10.2 42.3 all-gather.2
  54.8 38.5 all-gather.4
  110.5 132.0 all-reduce.1
  316.2 93.9 reduce-scatter.1
where the time goes:
time: 421 us; the launch traced here: 419 us
  waiting for transfers between devices  270 us (64%)
  loops' own time  46.9 us (11%)
  local copies, waits for them, and re-layouts  30.6 us (7%)
  matrix products  29.2 us (7%)
  other arithmetic  25.2 us (6%)
  between operations  16.5 us (4%)
    psum x1, waiting for transfers between devices, on_device(): first_whole = lax.psum(first_terms, 'term') + whole_diag * start_whole  132 us
    reduce_scatter x1, waiting for transfers between devices, on_device(): lax.psum_scatter(second_terms, 'term', scatter_dimension=1, tiled=True)  92.5 us
    another operation x2, loops' own time, block_loop(): return lax.fori_loop(0, last_slot, add_block, partial_sum)  46.9 us
    all_gather x1, waiting for transfers between devices, on_device(): lax.all_gather(wavefunction, 'term', axis=1, tiled=True).astype(jnp.float32)  43.9 us
    dot_general x10, matrix products, add_block(): jnp.dot(product, right_op.T, preferred_element_type=jnp.float32)  29.2 us
    dynamic_slice x10, local copies, waits for them, and re-layouts, add_block(): before = lax.dynamic_index_in_dim(running, target, 0, keepdims=False)  13 us
  transfers between devices with their start and end apart: 4, of which 3 were waited for; matrix products, arithmetic and copies ran while one was open for 8% of the time, Pallas kernels for 0%

commit v1 on v0

v1 whole, which is shorter than its diff:
```python
import functools

import jax
import jax.numpy as jnp
from jax import lax
from jax.experimental import pallas as pl
from jax.experimental.pallas import tpu as pltpu
from jax.sharding import PartitionSpec as P

VMEM = pl.BlockSpec(memory_space=pltpu.VMEM)
SMEM = pl.BlockSpec(memory_space=pltpu.SMEM)
ANY = pl.BlockSpec(memory_space=pl.ANY)
PARAMS = pltpu.CompilerParams(vmem_limit_bytes=48 * 1024 * 1024)


def fold(values):
    sectors, rows, width = values.shape
    summed = jnp.sum(values.reshape(sectors * rows // 8, 8, width), axis=0)
    return sum(summed[:, k * 128 : (k + 1) * 128] for k in range(width // 128))


def blocks_kernel(
    normalize, kept, rows, entries, sources, targets, live, offsets, *refs
):
    pieces = len(kept)
    field_refs, (left_hbm, right_hbm) = refs[:pieces], refs[pieces : pieces + 2]
    outs = refs[pieces + 2 :]
    keep_ref, send_ref, dot_ref, scale_ref = outs[:4]
    left, right, field, total, left_sem, right_sem = outs[4:]
    slots = left.shape[0]
    used = live[0]

    def copies(slot):
        return (
            pltpu.make_async_copy(left_hbm.at[slot], left.at[slot], left_sem.at[slot]),
            pltpu.make_async_copy(right_hbm.at[slot], right.at[slot], right_sem.at[slot]),
        )

    for slot in range(slots):

        @pl.when(slot < used)
        def _():
            for copy in copies(slot):
                copy.start()

    total[...] = jnp.zeros_like(total)
    if normalize:
        square = jnp.zeros((8, 128), jnp.float32)
        for ref in field_refs:
            value = ref[...].astype(jnp.float32)
            square += fold(value * value)
        scale = jnp.sqrt(jnp.sum(square) / entries)
    else:
        scale = jnp.float32(1.0)
    scale_ref[0] = scale
    for index, ref in enumerate(field_refs):
        place = pl.ds(pl.multiple_of(offsets[index], rows), rows)
        if normalize:
            field[:, place, :] = (ref[...].astype(jnp.float32) / scale).astype(jnp.bfloat16)
        else:
            field[:, place, :] = ref[...]

    def add_block(slot, carry):
        for copy in copies(slot):
            copy.wait()
        product = jnp.dot(
            left[slot], field[sources[slot]], preferred_element_type=jnp.float32
        ).astype(jnp.bfloat16)
        total[targets[slot]] += lax.dot_general(
            product, right[slot], (((1,), (1,)), ((), ())), preferred_element_type=jnp.float32
        )
        return carry

    lax.fori_loop(0, used, add_block, 0)

    dot = jnp.zeros((8, 128), jnp.float32)
    n_keep = n_send = 0
    for index, ref in enumerate(field_refs):
        place = pl.ds(pl.multiple_of(offsets[index], rows), rows)
        value = total[:, place, :]
        if normalize:
            dot += fold(value * ref[...].astype(jnp.float32))
        if kept[index]:
            keep_ref[n_keep] = value
            n_keep += 1
        else:
            send_ref[n_send] = value.astype(jnp.bfloat16)
            n_send += 1
    dot_ref[...] = dot / scale


def apply_blocks(pieces, kept, offsets, left, right, sources, targets, live, normalize, entries):
    sectors, rows, width = pieces[0].shape
    order = left.shape[1]
    slots = left.shape[0]
    n_keep = sum(kept)
    n_send = max(len(kept) - n_keep, 1)
    return pl.pallas_call(
        functools.partial(blocks_kernel, normalize, kept, rows, entries),
        grid_spec=pltpu.PrefetchScalarGridSpec(
            num_scalar_prefetch=4,
            in_specs=[VMEM] * len(pieces) + [ANY, ANY],
            out_specs=[VMEM, VMEM, VMEM, SMEM],
            scratch_shapes=[
                pltpu.VMEM(left.shape, left.dtype),
                pltpu.VMEM(right.shape, right.dtype),
                pltpu.VMEM((sectors, order, width), jnp.bfloat16),
                pltpu.VMEM((sectors, order, width), jnp.float32),
                pltpu.SemaphoreType.DMA((slots,)),
                pltpu.SemaphoreType.DMA((slots,)),
            ],
        ),
        out_shape=[
            jax.ShapeDtypeStruct((n_keep, sectors, rows, width), jnp.float32),
            jax.ShapeDtypeStruct((n_send, sectors, rows, width), jnp.bfloat16),
            jax.ShapeDtypeStruct((8, 128), jnp.float32),
            jax.ShapeDtypeStruct((1,), jnp.float32),
        ],
        compiler_params=PARAMS,
        cost_estimate=pl.CostEstimate(
            flops=4 * slots * order * order * width,
            bytes_accessed=4 * slots * order * order,
            transcendentals=0,
        ),
    )(sources, targets, live, offsets, *pieces, left, right)


def pair_kernel(keep_ref, other_ref, own_ref, *send_refs):
    own_ref[...] = keep_ref[0] + other_ref[0].astype(jnp.float32)
    for index, ref in enumerate(send_refs):
        value = keep_ref[index + 1] + other_ref[index + 1].astype(jnp.float32)
        ref[...] = value.astype(jnp.bfloat16)


def pair_sums(keep, other):
    count, *shape = keep.shape
    return pl.pallas_call(
        pair_kernel,
        in_specs=[VMEM, VMEM],
        out_specs=[VMEM] * count,
        out_shape=[jax.ShapeDtypeStruct(shape, jnp.float32)]
        + [jax.ShapeDtypeStruct(shape, jnp.bfloat16)] * (count - 1),
        compiler_params=PARAMS,
    )(keep, other)


def add_parts(own_ref, part_refs):
    value = own_ref[...]
    for ref in part_refs:
        value = value + ref[...].astype(jnp.float32)
    return value


def step_kernel(entries, ritz_ref, scale_ref, wave_ref, diag_ref, own_ref, *refs):
    *part_refs, first_ref, terms_ref, correction_ref, rounded_ref, dots_ref = refs
    start = wave_ref[...].astype(jnp.float32) / scale_ref[0]
    diag = diag_ref[...].astype(jnp.float32)
    ritz = jnp.sum(ritz_ref[...]) / entries
    terms = add_parts(own_ref, part_refs)
    first = terms + diag * start
    correction = (first - ritz * start) / jnp.maximum(jnp.abs(diag - ritz), 1.0)
    first_ref[...] = first
    terms_ref[...] = terms
    correction_ref[...] = correction
    rounded_ref[...] = correction.astype(jnp.bfloat16)
    dots_ref[0] = fold(start * correction)
    dots_ref[1] = fold(correction * correction)


def davidson_step(ritz, scale, wave, diag, own, parts, entries):
    full = jax.ShapeDtypeStruct(wave.shape, jnp.float32)
    return pl.pallas_call(
        functools.partial(step_kernel, entries),
        in_specs=[VMEM, SMEM] + [VMEM] * (3 + len(parts)),
        out_specs=[VMEM] * 5,
        out_shape=[
            full,
            full,
            full,
            jax.ShapeDtypeStruct(wave.shape, jnp.bfloat16),
            jax.ShapeDtypeStruct((2, 8, 128), jnp.float32),
        ],
        compiler_params=PARAMS,
    )(ritz, scale, wave, diag, own, *parts)


def finish_kernel(
    entries, dots_ref, scale_ref, wave_ref, diag_ref, terms_ref, correction_ref, own_ref, *refs
):
    *part_refs, vector_ref, image_ref = refs
    start = wave_ref[...].astype(jnp.float32) / scale_ref[0]
    along = jnp.sum(dots_ref[0]) / entries
    norm = jnp.sqrt(jnp.sum(dots_ref[1]) / entries - along * along)
    second = (correction_ref[...] - along * start) / norm
    vector_ref[...] = second
    image = (add_parts(own_ref, part_refs) - along * terms_ref[...]) / norm
    image_ref[...] = image + diag_ref[...].astype(jnp.float32) * second


def finish(dots, scale, wave, diag, terms, correction, own, parts, entries):
    full = jax.ShapeDtypeStruct(wave.shape, jnp.float32)
    return pl.pallas_call(
        functools.partial(finish_kernel, entries),
        in_specs=[VMEM, SMEM] + [VMEM] * (5 + len(parts)),
        out_specs=[VMEM] * 2,
        out_shape=[full, full],
        compiler_params=PARAMS,
    )(dots, scale, wave, diag, terms, correction, own, *parts)


class DirectPlan:
    def __init__(self, rows):
        self.rows = rows
        me = lax.axis_index("term")
        offsets, self.kept = [], []
        for dc in range(2):
            for dz in range(4):
                for dy in range(2):
                    z, y, c = (me // 4 - dz + 4) % 4, (me // 2 % 2 + dy) % 2, (me % 2 + dc) % 2
                    offsets.append(((z * 2 + y) * 2 + c) * rows)
                    self.kept.append(dc == 0)
        self.offsets = jnp.stack(offsets).astype(jnp.int32)

    @staticmethod
    def shift(value, dz, dy, dc):
        pairs = []
        for index in range(16):
            z, y, c = index // 4, index // 2 % 2, index % 2
            pairs.append((index, (((z + dz) % 4) * 2 + (y + dy) % 2) * 2 + (c + dc) % 2))
        return lax.ppermute(value, "term", pairs)

    def gather(self, own):
        along_z = [own] + [self.shift(own, dz, 0, 0) for dz in (1, 2, 3)]
        chips = []
        for piece in along_z:
            chips += [piece, self.shift(piece, 0, 1, 0)]
        return chips + [self.shift(piece, 0, 0, 1) for piece in chips]

    def scatter(self, keep, send):
        other = self.shift(send, 0, 0, 1)
        own, *sums = pair_sums(keep, other)
        parts = []
        for index, value in enumerate(sums):
            dz, dy = (index + 1) // 2, (index + 1) % 2
            parts.append(self.shift(value, (4 - dz) % 4, dy, 0))
        return own, parts


class WholePlan:
    def __init__(self):
        self.kept = [True]
        self.offsets = jnp.zeros((1,), jnp.int32)

    def gather(self, own):
        return [lax.all_gather(own, "term", axis=1, tiled=True)]

    def scatter(self, keep, send):
        return lax.psum_scatter(keep[0], "term", scatter_dimension=1, tiled=True), []


def on_device(
    wavefunction, diagonal, left_blocks, right_blocks, block_source, block_target, live_count
):
    devices = lax.axis_size("term")
    sectors, rows, width = wavefunction.shape
    entries = float(sectors * rows * devices * width)
    plan = DirectPlan(rows) if devices == 16 else WholePlan()
    blocks = (left_blocks, right_blocks, block_source, block_target, live_count)

    def apply(pieces, normalize):
        keep, send, dot, scale = apply_blocks(
            pieces, plan.kept, plan.offsets, *blocks, normalize, entries
        )
        return (*plan.scatter(keep, send), dot, scale)

    own, parts, dot, scale = apply(plan.gather(wavefunction), True)
    start = wavefunction.astype(jnp.float32) / scale[0]
    dot = dot + fold(diagonal.astype(jnp.float32) * start * start)
    ritz = lax.psum(dot, "term")
    first_image, terms, correction, rounded, dots = davidson_step(
        ritz, scale, wavefunction, diagonal, own, parts, entries
    )
    dots = lax.psum(dots, "term")
    own, parts, _, _ = apply(plan.gather(rounded), False)
    second_vector, second_image = finish(
        dots, scale, wavefunction, diagonal, terms, correction, own, parts, entries
    )
    return (first_image, second_vector, second_image)


def solution(mesh):
    placed = (
        P("grp", "term", None),
        P("grp", "term", None),
        P(("grp", "term"), None, None),
        P(("grp", "term"), None, None),
        P(("grp", "term")),
        P(("grp", "term")),
        P(("grp", "term")),
    )
    return jax.shard_map(
        on_device,
        mesh=mesh,
        in_specs=placed,
        out_specs=(P("grp", "term", None), P("grp", "term", None), P("grp", "term", None)),
        check_vma=False,
    )
```

time: 421 us -> 155 us (0.37)
  waiting for transfers between devices: 270 us -> 29.4 us
  blocking collectives: 0 us -> 66.9 us
  loops' own time: 46.9 us -> 0 us
  starting transfers between devices: 0.15 us -> 37.3 us
  matrix products: 29.2 us -> 0 us
  local copies, waits for them, and re-layouts: 30.6 us -> 2.32 us
  other arithmetic: 25.2 us -> 0.68 us
  Pallas kernels: 0 us -> 16.6 us
  between operations: 16.5 us -> 1.57 us
    psum x1 -> x0, waiting for transfers between devices: 132 us -> none  [on_device(): first_whole = lax.psum(first_terms, 'term') + whole_diag * start_whole]
    reduce_scatter x1 -> x0, waiting for transfers between devices: 92.5 us -> none  [on_device(): lax.psum_scatter(second_terms, 'term', scatter_dimension=1, tiled=True)]
    psum x0 -> x2, blocking collectives: none -> 66.9 us  [the longest x1 33.7 us: on_device(): dots = lax.psum(dots, 'term')]
    another operation x2 -> x0, loops' own time: 46.9 us -> none  [block_loop(): return lax.fori_loop(0, last_slot, add_block, partial_sum)]
    all_gather x2 -> x0, waiting for transfers between devices: 43.9 us -> none  [the longest x1 43.9 us: on_device(): lax.all_gather(wavefunction, 'term', axis=1, tiled=True).astype(jnp.float32)]
    ppermute x0 -> x46, starting transfers between devices: none -> 37.3 us  [shift(): return lax.ppermute(value, 'term', pairs)]
    ppermute x0 -> x46, waiting for transfers between devices: none -> 29.4 us  [shift(): return lax.ppermute(value, 'term', pairs)]
    dot_general x10 -> x0, matrix products: 29.2 us -> none  [add_block(): jnp.dot(product, right_op.T, preferred_element_type=jnp.float32)]
  transfers between devices with their start and end apart: 4 -> 46, of which waited for: 3 -> 12; matrix products, arithmetic and copies ran while one was open for 8% -> 1% of each run, Pallas kernels for 0% -> 0%
where the time goes in v1:
time: 155 us
  blocking collectives  66.9 us (43%)
  starting transfers between devices  37.3 us (24%)
  waiting for transfers between devices  29.4 us (19%)
  Pallas kernels  16.6 us (11%)
  local copies, waits for them, and re-layouts  2.32 us (1%)
  between operations  1.57 us (1%)
    ppermute x46, starting transfers between devices, shift(): return lax.ppermute(value, 'term', pairs)  37.3 us
    psum x1, blocking collectives, on_device(): dots = lax.psum(dots, 'term')  33.7 us
    psum x1, blocking collectives, on_device(): ritz = lax.psum(dot, 'term')  33.2 us
    ppermute x46, waiting for transfers between devices, shift(): return lax.ppermute(value, 'term', pairs)  29.4 us
    pallas_call x2, Pallas kernels, apply_blocks(): pl.pallas_call(functools.partial(blocks_kernel, normalize, kept, rows, en...  13.2 us
  transfers between devices with their start and end apart: 46, of which 12 were waited for; matrix products, arithmetic and copies ran while one was open for 1% of the time, Pallas kernels for 0%

profile of v1, /device:TPU:0, one launch (start us, length us, event | category | flops | bytes accessed | tf_op | source)
XLA Modules:
  0.0 154.8 jit_solution(18175636253623370114)
XLA Ops:
  0.6 5.1 %collective-permute-start.5 = (bf16[3,32,512]{2,1,0:T(8,128)(2,1)}, bf16[3,32,512]{2,1,0:T(8,128)(2,1)S(1)}, u32[]{:S(2)}, u32[]{:S(2)}) collective-permute-start(bf16[3,32,512]{2,1,0:T(8,128)(2,1)} %wave_ref.3), channel_id=1, source_target_pairs={{0,12},{1,13},{2,14},{3,15},{4,0},{5,1},{6,2},{7,3},{8,4},{9,5},{1... | collective-permute-start | bytes 294920 | tf_op jit(solution)/shard_map/ppermute | solution.py:230
  5.7 1.0 collective-permute-start.1
  6.7 1.5 collective-permute-start
  8.3 1.0 collective-permute-done.5.refs_6_
  9.3 1.5 collective-permute-start.6
  10.8 4.4 %collective-permute-done.3.refs_4_ = bf16[3,32,512]{2,1,0:T(8,128)(2,1)S(1)} collective-permute-done((bf16[3,32,512]{2,1,0:T(8,128)(2,1)}, bf16[3,32,512]{2,1,0:T(8,128)(2,1)S(1)}, u32[]{:S(2)}, u32[]{:S(2)}) %collective-permute-start.3) | collective-permute-done | bytes 98336 | tf_op jit(solution)/shard_map/ppermute | solution.py:230
  15.3 1.5 collective-permute-start.4
  17.9 3.0 %collective-permute-done.4.refs_5_ = bf16[3,32,512]{2,1,0:T(8,128)(2,1)S(1)} collective-permute-done((bf16[3,32,512]{2,1,0:T(8,128)(2,1)S(1)}, bf16[3,32,512]{2,1,0:T(8,128)(2,1)S(1)}, u32[]{:S(2)}, u32[]{:S(2)}) %collective-permute-start.4) | collective-permute-done | bytes 98336 | tf_op jit(solution)/shard_map/ppermute | solution.py:230
  20.9 1.6 %collective-permute-done.2.refs_3_ = bf16[3,32,512]{2,1,0:T(8,128)(2,1)S(1)} collective-permute-done((bf16[3,32,512]{2,1,0:T(8,128)(2,1)S(1)}, bf16[3,32,512]{2,1,0:T(8,128)(2,1)S(1)}, u32[]{:S(2)}, u32[]{:S(2)}) %collective-permute-start.2) | collective-permute-done | bytes 98336 | tf_op jit(solution)/shard_map/ppermute | solution.py:230
  23.9 0.9 copy-done
  26.1 6.8 %shard_map.94 = (f32[8,3,32,512]{3,2,1,0:T(8,128)S(1)}, bf16[8,3,32,512]{3,2,1,0:T(8,128)(2,1)S(1)}, f32[8,128]{1,0:T(8,128)S(1)}, f32[1]{0:T(128)}) custom-call(s32[8]{0:T(128)S(1)} %copy-done.3, s32[8]{0:T(128)S(1)} %copy-done.5, s32[1]{0:T(128)S(6)} %copy.10.live, s32[16]{0:T(128)S(1)} %stack.67.offsets, bf16[3,32,512]{2,1,0:T(8,128)(2,1)S(1)} %copy-done, ...), custom_call_target="tpu_custom_call" | custom-call | flops 4294967296 | bytes 8388608 | tf_op jit(solution)/shard_map/pallas_call | solution.py:98
  33.0 2.3 %collective-permute-done.15.other_ref = bf16[8,3,32,512]{3,2,1,0:T(8,128)(2,1)S(1)} collective-permute-done((bf16[8,3,32,512]{3,2,1,0:T(8,128)(2,1)S(1)}, bf16[8,3,32,512]{3,2,1,0:T(8,128)(2,1)S(1)}, u32[]{:S(2)}, u32[]{:S(2)}) %collective-permute-start.15) | collective-permute-done | bytes 786464 | tf_op jit(solution)/shard_map/ppermute | solution.py:230
  35.4 3.5 %collective-permute-start.16 = (bf16[3,32,512]{2,1,0:T(8,128)(2,1)S(1)}, bf16[3,32,512]{2,1,0:T(8,128)(2,1)S(1)}, u32[]{:S(2)}, u32[]{:S(2)}) collective-permute-start(bf16[3,32,512]{2,1,0:T(8,128)(2,1)S(1)} %get-tuple-element.37), channel_id=1, source_target_pairs={{0,2},{1,3},{2,0},{3,1},{4,6},{5,7},{6,4},{7,5},{8,10},{9,11},{10,... | collective-permute-start | bytes 294920 | tf_op jit(solution)/shard_map/ppermute | solution.py:230
  39.6 2.8 %collective-permute-start.18 = (bf16[3,32,512]{2,1,0:T(8,128)(2,1)S(1)}, bf16[3,32,512]{2,1,0:T(8,128)(2,1)S(1)}, u32[]{:S(2)}, u32[]{:S(2)}) collective-permute-start(bf16[3,32,512]{2,1,0:T(8,128)(2,1)S(1)} %get-tuple-element.39), channel_id=1, source_target_pairs={{0,14},{1,15},{2,12},{3,13},{4,2},{5,3},{6,0},{7,1},{8,6},{9,7},{1... | collective-permute-start | bytes 294920 | tf_op jit(solution)/shard_map/ppermute | solution.py:230
  42.7 3.8 %collective-permute-start.20 = (bf16[3,32,512]{2,1,0:T(8,128)(2,1)S(1)}, bf16[3,32,512]{2,1,0:T(8,128)(2,1)S(1)}, u32[]{:S(2)}, u32[]{:S(2)}) collective-permute-start(bf16[3,32,512]{2,1,0:T(8,128)(2,1)S(1)} %get-tuple-element.41), channel_id=1, source_target_pairs={{0,10},{1,11},{2,8},{3,9},{4,14},{5,15},{6,12},{7,13},{8,2},{9,3},... | collective-permute-start | bytes 294920 | tf_op jit(solution)/shard_map/ppermute | solution.py:230
  47.1 33.2 %psum.14.ritz_ref = f32[8,128]{1,0:T(8,128)S(1)} all-reduce(f32[8,128]{1,0:T(8,128)S(1)} %fusion), channel_id=1, replica_groups=mesh['grp'=2,'term'=16] {'term'}, use_global_device_ids=true, to_apply=%region_1.2 | all-reduce | flops 1024 | bytes 8192 | tf_op jit(solution)/shard_map/psum | solution.py:279
  80.3 1.5 shard_map.96
  81.8 2.0 %collective-permute-start.24 = (bf16[3,32,512]{2,1,0:T(8,128)(2,1)S(1)}, bf16[3,32,512]{2,1,0:T(8,128)(2,1)S(1)}, u32[]{:S(2)}, u32[]{:S(2)}) collective-permute-start(bf16[3,32,512]{2,1,0:T(8,128)(2,1)S(1)} %get-tuple-element.48.refs_0_), channel_id=1, source_target_pairs={{0,4},{1,5},{2,6},{3,7},{4,8},{5,9},{6,10},{7,11},{8,12},{9,13},{1... | collective-permute-start | bytes 294920 | tf_op jit(solution)/shard_map/ppermute | solution.py:230
  83.9 4.1 %collective-permute-done.28.refs_6_ = bf16[3,32,512]{2,1,0:T(8,128)(2,1)S(1)} collective-permute-done((bf16[3,32,512]{2,1,0:T(8,128)(2,1)S(1)}, bf16[3,32,512]{2,1,0:T(8,128)(2,1)S(1)}, u32[]{:S(2)}, u32[]{:S(2)}) %collective-permute-start.28) | collective-permute-done | bytes 98336 | tf_op jit(solution)/shard_map/ppermute | solution.py:230
  88.0 4.2 %collective-permute-done.26.refs_4_ = bf16[3,32,512]{2,1,0:T(8,128)(2,1)S(1)} collective-permute-done((bf16[3,32,512]{2,1,0:T(8,128)(2,1)S(1)}, bf16[3,32,512]{2,1,0:T(8,128)(2,1)S(1)}, u32[]{:S(2)}, u32[]{:S(2)}) %collective-permute-start.26) | collective-permute-done | bytes 98336 | tf_op jit(solution)/shard_map/ppermute | solution.py:230
  92.2 2.0 %collective-permute-start.25 = (bf16[3,32,512]{2,1,0:T(8,128)(2,1)S(1)}, bf16[3,32,512]{2,1,0:T(8,128)(2,1)S(1)}, u32[]{:S(2)}, u32[]{:S(2)}) collective-permute-start(bf16[3,32,512]{2,1,0:T(8,128)(2,1)S(1)} %collective-permute-done.24.refs_2_), channel_id=1, source_target_pairs={{0,2},{1,3},{2,0},{3,1},{4,6},{5,7},{6,4},{7,5},{8,10},{9,11},{10,... | collective-permute-start | bytes 294920 | tf_op jit(solution)/shard_map/ppermute | solution.py:230
  94.8 3.0 %collective-permute-done.27.refs_5_ = bf16[3,32,512]{2,1,0:T(8,128)(2,1)S(1)} collective-permute-done((bf16[3,32,512]{2,1,0:T(8,128)(2,1)S(1)}, bf16[3,32,512]{2,1,0:T(8,128)(2,1)S(1)}, u32[]{:S(2)}, u32[]{:S(2)}) %collective-permute-start.27) | collective-permute-done | bytes 98336 | tf_op jit(solution)/shard_map/ppermute | solution.py:230
  97.8 1.7 %collective-permute-done.25.refs_3_ = bf16[3,32,512]{2,1,0:T(8,128)(2,1)S(1)} collective-permute-done((bf16[3,32,512]{2,1,0:T(8,128)(2,1)S(1)}, bf16[3,32,512]{2,1,0:T(8,128)(2,1)S(1)}, u32[]{:S(2)}, u32[]{:S(2)}) %collective-permute-start.25) | collective-permute-done | bytes 98336 | tf_op jit(solution)/shard_map/ppermute | solution.py:230
  99.6 1.3 collective-permute-done.33.refs_11_
  100.8 6.4 %shard_map.97 = (f32[8,3,32,512]{3,2,1,0:T(8,128)S(1)}, bf16[8,3,32,512]{3,2,1,0:T(8,128)(2,1)S(1)}, f32[8,128]{1,0:T(8,128)}, f32[1]{0:T(128)}) custom-call(s32[8]{0:T(128)S(1)} %copy-done.4, s32[8]{0:T(128)S(1)} %copy-done.6, s32[1]{0:T(128)S(6)} %copy.10.live, s32[16]{0:T(128)S(1)} %stack.67.offsets, bf16[3,32,512]{2,1,0:T(8,128)(2,1)S(1)} %get-tuple-element.48.refs_0_, ...), custom_call_target="tpu_custom_call" | custom-call | flops 4294967296 | bytes 8388608 | tf_op jit(solution)/shard_map/pallas_call | solution.py:98
  107.3 2.3 %collective-permute-done.38.other_ref = bf16[8,3,32,512]{3,2,1,0:T(8,128)(2,1)S(1)} collective-permute-done((bf16[8,3,32,512]{3,2,1,0:T(8,128)(2,1)S(1)}, bf16[8,3,32,512]{3,2,1,0:T(8,128)(2,1)S(1)}, u32[]{:S(2)}, u32[]{:S(2)}) %collective-permute-start.38) | collective-permute-done | bytes 786464 | tf_op jit(solution)/shard_map/ppermute | solution.py:230
  109.8 2.3 %collective-permute-start.39 = (bf16[3,32,512]{2,1,0:T(8,128)(2,1)S(1)}, bf16[3,32,512]{2,1,0:T(8,128)(2,1)S(1)}, u32[]{:S(2)}, u32[]{:S(2)}) collective-permute-start(bf16[3,32,512]{2,1,0:T(8,128)(2,1)S(1)} %get-tuple-element.52), channel_id=1, source_target_pairs={{0,2},{1,3},{2,0},{3,1},{4,6},{5,7},{6,4},{7,5},{8,10},{9,11},{10,... | collective-permute-start | bytes 294920 | tf_op jit(solution)/shard_map/ppermute | solution.py:230
  112.1 2.8 %collective-permute-start.41 = (bf16[3,32,512]{2,1,0:T(8,128)(2,1)S(1)}, bf16[3,32,512]{2,1,0:T(8,128)(2,1)S(1)}, u32[]{:S(2)}, u32[]{:S(2)}) collective-permute-start(bf16[3,32,512]{2,1,0:T(8,128)(2,1)S(1)} %get-tuple-element.54), channel_id=1, source_target_pairs={{0,14},{1,15},{2,12},{3,13},{4,2},{5,3},{6,0},{7,1},{8,6},{9,7},{1... | collective-permute-start | bytes 294920 | tf_op jit(solution)/shard_map/ppermute | solution.py:230
  115.0 2.7 %collective-permute-start.43 = (bf16[3,32,512]{2,1,0:T(8,128)(2,1)S(1)}, bf16[3,32,512]{2,1,0:T(8,128)(2,1)S(1)}, u32[]{:S(2)}, u32[]{:S(2)}) collective-permute-start(bf16[3,32,512]{2,1,0:T(8,128)(2,1)S(1)} %get-tuple-element.56), channel_id=1, source_target_pairs={{0,10},{1,11},{2,8},{3,9},{4,14},{5,15},{6,12},{7,13},{8,2},{9,3},... | collective-permute-start | bytes 294920 | tf_op jit(solution)/shard_map/ppermute | solution.py:230
  117.9 1.5 collective-permute-start.45
  119.4 33.7 %psum.15.dots_ref = f32[2,8,128]{2,1,0:T(8,128)S(1)} all-reduce(f32[2,8,128]{2,1,0:T(8,128)S(1)} %get-tuple-element.45), channel_id=1, replica_groups=mesh['grp'=2,'term'=16] {'term'}, use_global_device_ids=true, to_apply=%region_2.3 | all-reduce | flops 2048 | bytes 16384 | tf_op jit(solution)/shard_map/psum | solution.py:283
  153.2 1.6 %shard_map.99 = (f32[3,32,512]{2,1,0:T(8,128)}, f32[3,32,512]{2,1,0:T(8,128)}) custom-call(f32[2,8,128]{2,1,0:T(8,128)S(1)} %psum.15.dots_ref, f32[1]{0:T(128)} %get-tuple-element.33.scale_ref, bf16[3,32,512]{2,1,0:T(8,128)(2,1)S(1)} %copy-done.1, bf16[3,32,512]{2,1,0:T(8,128)(2,1)S(1)} %copy-done.2, f32[3,32,512]{2,1,0:T(8,128)S(1)} %get-tuple-element.46.terms_ref, ...), custom_call_target="tpu_custom_call" | custom-call | tf_op jit(solution)/shard_map/pallas_call | solution.py:202
  (86 shorter events, 6.2 us)
Async XLA Ops:
  0.6 8.7 %collective-permute-start.5 = (bf16[3,32,512]{2,1,0:T(8,128)(2,1)}, bf16[3,32,512]{2,1,0:T(8,128)(2,1)S(1)}, u32[]{:S(2)}, u32[]{:S(2)}) collective-permute-start(bf16[3,32,512]{2,1,0:T(8,128)(2,1)} %wave_ref.3), channel_id=1, source_target_pairs={{0,12},{1,13},{2,14},{3,15},{4,0},{5,1},{6,2},{7,3},{8,4},{9,5},{1... | collective-permute-start | bytes 294920 | tf_op jit(solution)/shard_map/ppermute | solution.py:230
  5.7 9.5 %collective-permute-start.3 = (bf16[3,32,512]{2,1,0:T(8,128)(2,1)}, bf16[3,32,512]{2,1,0:T(8,128)(2,1)S(1)}, u32[]{:S(2)}, u32[]{:S(2)}) collective-permute-start(bf16[3,32,512]{2,1,0:T(8,128)(2,1)} %wave_ref.3), channel_id=1, source_target_pairs={{0,8},{1,9},{2,10},{3,11},{4,12},{5,13},{6,14},{7,15},{8,0},{9,1},... | collective-permute-start | bytes 294920 | tf_op jit(solution)/shard_map/ppermute | solution.py:230
  5.7 9.6 %collective-permute-start.1 = (bf16[3,32,512]{2,1,0:T(8,128)(2,1)}, bf16[3,32,512]{2,1,0:T(8,128)(2,1)S(1)}, u32[]{:S(2)}, u32[]{:S(2)}) collective-permute-start(bf16[3,32,512]{2,1,0:T(8,128)(2,1)} %wave_ref.3), channel_id=1, source_target_pairs={{0,4},{1,5},{2,6},{3,7},{4,8},{5,9},{6,10},{7,11},{8,12},{9,13},{1... | collective-permute-start | bytes 294920 | tf_op jit(solution)/shard_map/ppermute | solution.py:230
  6.7 10.1 %collective-permute-start = (bf16[3,32,512]{2,1,0:T(8,128)(2,1)}, bf16[3,32,512]{2,1,0:T(8,128)(2,1)S(1)}, u32[]{:S(2)}, u32[]{:S(2)}) collective-permute-start(bf16[3,32,512]{2,1,0:T(8,128)(2,1)} %wave_ref.3), channel_id=1, source_target_pairs={{0,2},{1,3},{2,0},{3,1},{4,6},{5,7},{6,4},{7,5},{8,10},{9,11},{10,... | collective-permute-start | bytes 294920 | tf_op jit(solution)/shard_map/ppermute | solution.py:230
  9.3 8.1 %collective-permute-start.13 = (bf16[3,32,512]{2,1,0:T(8,128)(2,1)S(1)}, bf16[3,32,512]{2,1,0:T(8,128)(2,1)S(1)}, u32[]{:S(2)}, u32[]{:S(2)}) collective-permute-start(bf16[3,32,512]{2,1,0:T(8,128)(2,1)S(1)} %collective-permute-done.5.refs_6_), channel_id=1, source_target_pairs={{0,1},{1,0},{2,3},{3,2},{4,5},{5,4},{6,7},{7,6},{8,9},{9,8},{10,11... | collective-permute-start | bytes 294920 | tf_op jit(solution)/shard_map/ppermute | solution.py:230
  9.3 8.1 %collective-permute-start.6 = (bf16[3,32,512]{2,1,0:T(8,128)(2,1)S(1)}, bf16[3,32,512]{2,1,0:T(8,128)(2,1)S(1)}, u32[]{:S(2)}, u32[]{:S(2)}) collective-permute-start(bf16[3,32,512]{2,1,0:T(8,128)(2,1)S(1)} %collective-permute-done.5.refs_6_), channel_id=1, source_target_pairs={{0,2},{1,3},{2,0},{3,1},{4,6},{5,7},{6,4},{7,5},{8,10},{9,11},{10,... | collective-permute-start | bytes 294920 | tf_op jit(solution)/shard_map/ppermute | solution.py:230
  15.3 5.6 %collective-permute-start.4 = (bf16[3,32,512]{2,1,0:T(8,128)(2,1)S(1)}, bf16[3,32,512]{2,1,0:T(8,128)(2,1)S(1)}, u32[]{:S(2)}, u32[]{:S(2)}) collective-permute-start(bf16[3,32,512]{2,1,0:T(8,128)(2,1)S(1)} %collective-permute-done.3.refs_4_), channel_id=1, source_target_pairs={{0,2},{1,3},{2,0},{3,1},{4,6},{5,7},{6,4},{7,5},{8,10},{9,11},{10,... | collective-permute-start | bytes 294920 | tf_op jit(solution)/shard_map/ppermute | solution.py:230
  16.8 5.7 %collective-permute-start.2 = (bf16[3,32,512]{2,1,0:T(8,128)(2,1)S(1)}, bf16[3,32,512]{2,1,0:T(8,128)(2,1)S(1)}, u32[]{:S(2)}, u32[]{:S(2)}) collective-permute-start(bf16[3,32,512]{2,1,0:T(8,128)(2,1)S(1)} %collective-permute-done.1.refs_2_), channel_id=1, source_target_pairs={{0,2},{1,3},{2,0},{3,1},{4,6},{5,7},{6,4},{7,5},{8,10},{9,11},{10,... | collective-permute-start | bytes 294920 | tf_op jit(solution)/shard_map/ppermute | solution.py:230
  17.4 6.0 %collective-permute-start.9 = (bf16[3,32,512]{2,1,0:T(8,128)(2,1)S(1)}, bf16[3,32,512]{2,1,0:T(8,128)(2,1)S(1)}, u32[]{:S(2)}, u32[]{:S(2)}) collective-permute-start(bf16[3,32,512]{2,1,0:T(8,128)(2,1)S(1)} %collective-permute-done.1.refs_2_), channel_id=1, source_target_pairs={{0,1},{1,0},{2,3},{3,2},{4,5},{5,4},{6,7},{7,6},{8,9},{9,8},{10,11... | collective-permute-start | bytes 294920 | tf_op jit(solution)/shard_map/ppermute | solution.py:230
  17.4 6.0 %collective-permute-start.8 = (bf16[3,32,512]{2,1,0:T(8,128)(2,1)S(1)}, bf16[3,32,512]{2,1,0:T(8,128)(2,1)S(1)}, u32[]{:S(2)}, u32[]{:S(2)}) collective-permute-start(bf16[3,32,512]{2,1,0:T(8,128)(2,1)S(1)} %collective-permute-done.refs_1_), channel_id=1, source_target_pairs={{0,1},{1,0},{2,3},{3,2},{4,5},{5,4},{6,7},{7,6},{8,9},{9,8},{10,11... | collective-permute-start | bytes 294920 | tf_op jit(solution)/shard_map/ppermute | solution.py:230
  35.4 11.1 %collective-permute-start.16 = (bf16[3,32,512]{2,1,0:T(8,128)(2,1)S(1)}, bf16[3,32,512]{2,1,0:T(8,128)(2,1)S(1)}, u32[]{:S(2)}, u32[]{:S(2)}) collective-permute-start(bf16[3,32,512]{2,1,0:T(8,128)(2,1)S(1)} %get-tuple-element.37), channel_id=1, source_target_pairs={{0,2},{1,3},{2,0},{3,1},{4,6},{5,7},{6,4},{7,5},{8,10},{9,11},{10,... | collective-permute-start | bytes 294920 | tf_op jit(solution)/shard_map/ppermute | solution.py:230
  38.9 7.6 %collective-permute-start.17 = (bf16[3,32,512]{2,1,0:T(8,128)(2,1)S(1)}, bf16[3,32,512]{2,1,0:T(8,128)(2,1)S(1)}, u32[]{:S(2)}, u32[]{:S(2)}) collective-permute-start(bf16[3,32,512]{2,1,0:T(8,128)(2,1)S(1)} %get-tuple-element.38), channel_id=1, source_target_pairs={{0,12},{1,13},{2,14},{3,15},{4,0},{5,1},{6,2},{7,3},{8,4},{9,5},{1... | collective-permute-start | bytes 294920 | tf_op jit(solution)/shard_map/ppermute | solution.py:230
  39.6 40.7 %collective-permute-start.18 = (bf16[3,32,512]{2,1,0:T(8,128)(2,1)S(1)}, bf16[3,32,512]{2,1,0:T(8,128)(2,1)S(1)}, u32[]{:S(2)}, u32[]{:S(2)}) collective-permute-start(bf16[3,32,512]{2,1,0:T(8,128)(2,1)S(1)} %get-tuple-element.39), channel_id=1, source_target_pairs={{0,14},{1,15},{2,12},{3,13},{4,2},{5,3},{6,0},{7,1},{8,6},{9,7},{1... | collective-permute-start | bytes 294920 | tf_op jit(solution)/shard_map/ppermute | solution.py:230
  42.4 37.9 %collective-permute-start.19 = (bf16[3,32,512]{2,1,0:T(8,128)(2,1)S(1)}, bf16[3,32,512]{2,1,0:T(8,128)(2,1)S(1)}, u32[]{:S(2)}, u32[]{:S(2)}) collective-permute-start(bf16[3,32,512]{2,1,0:T(8,128)(2,1)S(1)} %get-tuple-element.40), channel_id=1, source_target_pairs={{0,8},{1,9},{2,10},{3,11},{4,12},{5,13},{6,14},{7,15},{8,0},{9,1},... | collective-permute-start | bytes 294920 | tf_op jit(solution)/shard_map/ppermute | solution.py:230
  42.7 37.6 %collective-permute-start.20 = (bf16[3,32,512]{2,1,0:T(8,128)(2,1)S(1)}, bf16[3,32,512]{2,1,0:T(8,128)(2,1)S(1)}, u32[]{:S(2)}, u32[]{:S(2)}) collective-permute-start(bf16[3,32,512]{2,1,0:T(8,128)(2,1)S(1)} %get-tuple-element.41), channel_id=1, source_target_pairs={{0,10},{1,11},{2,8},{3,9},{4,14},{5,15},{6,12},{7,13},{8,2},{9,3},... | collective-permute-start | bytes 294920 | tf_op jit(solution)/shard_map/ppermute | solution.py:230
  46.5 33.8 %collective-permute-start.21 = (bf16[3,32,512]{2,1,0:T(8,128)(2,1)S(1)}, bf16[3,32,512]{2,1,0:T(8,128)(2,1)S(1)}, u32[]{:S(2)}, u32[]{:S(2)}) collective-permute-start(bf16[3,32,512]{2,1,0:T(8,128)(2,1)S(1)} %get-tuple-element.42), channel_id=1, source_target_pairs={{0,4},{1,5},{2,6},{3,7},{4,8},{5,9},{6,10},{7,11},{8,12},{9,13},{1... | collective-permute-start | bytes 294920 | tf_op jit(solution)/shard_map/ppermute | solution.py:230
  46.5 33.8 %collective-permute-start.22 = (bf16[3,32,512]{2,1,0:T(8,128)(2,1)S(1)}, bf16[3,32,512]{2,1,0:T(8,128)(2,1)S(1)}, u32[]{:S(2)}, u32[]{:S(2)}) collective-permute-start(bf16[3,32,512]{2,1,0:T(8,128)(2,1)S(1)} %get-tuple-element.43), channel_id=1, source_target_pairs={{0,6},{1,7},{2,4},{3,5},{4,10},{5,11},{6,8},{7,9},{8,14},{9,15},{1... | collective-permute-start | bytes 294920 | tf_op jit(solution)/shard_map/ppermute | solution.py:230
  81.8 6.1 %collective-permute-start.28 = (bf16[3,32,512]{2,1,0:T(8,128)(2,1)S(1)}, bf16[3,32,512]{2,1,0:T(8,128)(2,1)S(1)}, u32[]{:S(2)}, u32[]{:S(2)}) collective-permute-start(bf16[3,32,512]{2,1,0:T(8,128)(2,1)S(1)} %get-tuple-element.48.refs_0_), channel_id=1, source_target_pairs={{0,12},{1,13},{2,14},{3,15},{4,0},{5,1},{6,2},{7,3},{8,4},{9,5},{1... | collective-permute-start | bytes 294920 | tf_op jit(solution)/shard_map/ppermute | solution.py:230
  81.8 6.1 %collective-permute-start.30 = (bf16[3,32,512]{2,1,0:T(8,128)(2,1)S(1)}, bf16[3,32,512]{2,1,0:T(8,128)(2,1)S(1)}, u32[]{:S(2)}, u32[]{:S(2)}) collective-permute-start(bf16[3,32,512]{2,1,0:T(8,128)(2,1)S(1)} %get-tuple-element.48.refs_0_), channel_id=1, source_target_pairs={{0,1},{1,0},{2,3},{3,2},{4,5},{5,4},{6,7},{7,6},{8,9},{9,8},{10,11... | collective-permute-start | bytes 294920 | tf_op jit(solution)/shard_map/ppermute | solution.py:230
  81.8 10.4 %collective-permute-start.26 = (bf16[3,32,512]{2,1,0:T(8,128)(2,1)S(1)}, bf16[3,32,512]{2,1,0:T(8,128)(2,1)S(1)}, u32[]{:S(2)}, u32[]{:S(2)}) collective-permute-start(bf16[3,32,512]{2,1,0:T(8,128)(2,1)S(1)} %get-tuple-element.48.refs_0_), channel_id=1, source_target_pairs={{0,8},{1,9},{2,10},{3,11},{4,12},{5,13},{6,14},{7,15},{8,0},{9,1},... | collective-permute-start | bytes 294920 | tf_op jit(solution)/shard_map/ppermute | solution.py:230
  81.8 10.4 %collective-permute-start.24 = (bf16[3,32,512]{2,1,0:T(8,128)(2,1)S(1)}, bf16[3,32,512]{2,1,0:T(8,128)(2,1)S(1)}, u32[]{:S(2)}, u32[]{:S(2)}) collective-permute-start(bf16[3,32,512]{2,1,0:T(8,128)(2,1)S(1)} %get-tuple-element.48.refs_0_), channel_id=1, source_target_pairs={{0,4},{1,5},{2,6},{3,7},{4,8},{5,9},{6,10},{7,11},{8,12},{9,13},{1... | collective-permute-start | bytes 294920 | tf_op jit(solution)/shard_map/ppermute | solution.py:230
  83.9 8.4 %collective-permute-start.23 = (bf16[3,32,512]{2,1,0:T(8,128)(2,1)S(1)}, bf16[3,32,512]{2,1,0:T(8,128)(2,1)S(1)}, u32[]{:S(2)}, u32[]{:S(2)}) collective-permute-start(bf16[3,32,512]{2,1,0:T(8,128)(2,1)S(1)} %get-tuple-element.48.refs_0_), channel_id=1, source_target_pairs={{0,2},{1,3},{2,0},{3,1},{4,6},{5,7},{6,4},{7,5},{8,10},{9,11},{10,... | collective-permute-start | bytes 294920 | tf_op jit(solution)/shard_map/ppermute | solution.py:230
  88.0 6.3 %collective-permute-start.36 = (bf16[3,32,512]{2,1,0:T(8,128)(2,1)S(1)}, bf16[3,32,512]{2,1,0:T(8,128)(2,1)S(1)}, u32[]{:S(2)}, u32[]{:S(2)}) collective-permute-start(bf16[3,32,512]{2,1,0:T(8,128)(2,1)S(1)} %collective-permute-done.28.refs_6_), channel_id=1, source_target_pairs={{0,1},{1,0},{2,3},{3,2},{4,5},{5,4},{6,7},{7,6},{8,9},{9,8},{10,11... | collective-permute-start | bytes 294920 | tf_op jit(solution)/shard_map/ppermute | solution.py:230
  88.0 6.3 %collective-permute-start.29 = (bf16[3,32,512]{2,1,0:T(8,128)(2,1)S(1)}, bf16[3,32,512]{2,1,0:T(8,128)(2,1)S(1)}, u32[]{:S(2)}, u32[]{:S(2)}) collective-permute-start(bf16[3,32,512]{2,1,0:T(8,128)(2,1)S(1)} %collective-permute-done.28.refs_6_), channel_id=1, source_target_pairs={{0,2},{1,3},{2,0},{3,1},{4,6},{5,7},{6,4},{7,5},{8,10},{9,11},{10,... | collective-permute-start | bytes 294920 | tf_op jit(solution)/shard_map/ppermute | solution.py:230
  92.2 7.3 %collective-permute-start.25 = (bf16[3,32,512]{2,1,0:T(8,128)(2,1)S(1)}, bf16[3,32,512]{2,1,0:T(8,128)(2,1)S(1)}, u32[]{:S(2)}, u32[]{:S(2)}) collective-permute-start(bf16[3,32,512]{2,1,0:T(8,128)(2,1)S(1)} %collective-permute-done.24.refs_2_), channel_id=1, source_target_pairs={{0,2},{1,3},{2,0},{3,1},{4,6},{5,7},{6,4},{7,5},{8,10},{9,11},{10,... | collective-permute-start | bytes 294920 | tf_op jit(solution)/shard_map/ppermute | solution.py:230
  109.8 7.9 %collective-permute-start.39 = (bf16[3,32,512]{2,1,0:T(8,128)(2,1)S(1)}, bf16[3,32,512]{2,1,0:T(8,128)(2,1)S(1)}, u32[]{:S(2)}, u32[]{:S(2)}) collective-permute-start(bf16[3,32,512]{2,1,0:T(8,128)(2,1)S(1)} %get-tuple-element.52), channel_id=1, source_target_pairs={{0,2},{1,3},{2,0},{3,1},{4,6},{5,7},{6,4},{7,5},{8,10},{9,11},{10,... | collective-permute-start | bytes 294920 | tf_op jit(solution)/shard_map/ppermute | solution.py:230
  112.1 5.9 %collective-permute-start.40 = (bf16[3,32,512]{2,1,0:T(8,128)(2,1)S(1)}, bf16[3,32,512]{2,1,0:T(8,128)(2,1)S(1)}, u32[]{:S(2)}, u32[]{:S(2)}) collective-permute-start(bf16[3,32,512]{2,1,0:T(8,128)(2,1)S(1)} %get-tuple-element.53), channel_id=1, source_target_pairs={{0,12},{1,13},{2,14},{3,15},{4,0},{5,1},{6,2},{7,3},{8,4},{9,5},{1... | collective-permute-start | bytes 294920 | tf_op jit(solution)/shard_map/ppermute | solution.py:230
  112.1 41.1 %collective-permute-start.41 = (bf16[3,32,512]{2,1,0:T(8,128)(2,1)S(1)}, bf16[3,32,512]{2,1,0:T(8,128)(2,1)S(1)}, u32[]{:S(2)}, u32[]{:S(2)}) collective-permute-start(bf16[3,32,512]{2,1,0:T(8,128)(2,1)S(1)} %get-tuple-element.54), channel_id=1, source_target_pairs={{0,14},{1,15},{2,12},{3,13},{4,2},{5,3},{6,0},{7,1},{8,6},{9,7},{1... | collective-permute-start | bytes 294920 | tf_op jit(solution)/shard_map/ppermute | solution.py:230
  114.9 38.3 %collective-permute-start.42 = (bf16[3,32,512]{2,1,0:T(8,128)(2,1)S(1)}, bf16[3,32,512]{2,1,0:T(8,128)(2,1)S(1)}, u32[]{:S(2)}, u32[]{:S(2)}) collective-permute-start(bf16[3,32,512]{2,1,0:T(8,128)(2,1)S(1)} %get-tuple-element.55), channel_id=1, source_target_pairs={{0,8},{1,9},{2,10},{3,11},{4,12},{5,13},{6,14},{7,15},{8,0},{9,1},... | collective-permute-start | bytes 294920 | tf_op jit(solution)/shard_map/ppermute | solution.py:230
  115.0 38.1 %collective-permute-start.43 = (bf16[3,32,512]{2,1,0:T(8,128)(2,1)S(1)}, bf16[3,32,512]{2,1,0:T(8,128)(2,1)S(1)}, u32[]{:S(2)}, u32[]{:S(2)}) collective-permute-start(bf16[3,32,512]{2,1,0:T(8,128)(2,1)S(1)} %get-tuple-element.56), channel_id=1, source_target_pairs={{0,10},{1,11},{2,8},{3,9},{4,14},{5,15},{6,12},{7,13},{8,2},{9,3},... | collective-permute-start | bytes 294920 | tf_op jit(solution)/shard_map/ppermute | solution.py:230
  117.7 35.5 %collective-permute-start.44 = (bf16[3,32,512]{2,1,0:T(8,128)(2,1)S(1)}, bf16[3,32,512]{2,1,0:T(8,128)(2,1)S(1)}, u32[]{:S(2)}, u32[]{:S(2)}) collective-permute-start(bf16[3,32,512]{2,1,0:T(8,128)(2,1)S(1)} %get-tuple-element.57), channel_id=1, source_target_pairs={{0,4},{1,5},{2,6},{3,7},{4,8},{5,9},{6,10},{7,11},{8,12},{9,13},{1... | collective-permute-start | bytes 294920 | tf_op jit(solution)/shard_map/ppermute | solution.py:230
  117.9 35.3 %collective-permute-start.45 = (bf16[3,32,512]{2,1,0:T(8,128)(2,1)S(1)}, bf16[3,32,512]{2,1,0:T(8,128)(2,1)S(1)}, u32[]{:S(2)}, u32[]{:S(2)}) collective-permute-start(bf16[3,32,512]{2,1,0:T(8,128)(2,1)S(1)} %get-tuple-element.58), channel_id=1, source_target_pairs={{0,6},{1,7},{2,4},{3,5},{4,10},{5,11},{6,8},{7,9},{8,14},{9,15},{1... | collective-permute-start | bytes 294920 | tf_op jit(solution)/shard_map/ppermute | solution.py:230
  (21 other events, 271.3 us)

commit v2 on v0

v2 whole, which is shorter than its diff:
```python
import functools

import jax
import jax.numpy as jnp
from jax import lax
from jax.experimental import pallas as pl
from jax.experimental.pallas import tpu as pltpu
from jax.sharding import PartitionSpec as P

VMEM = pl.BlockSpec(memory_space=pltpu.VMEM)
SMEM = pl.BlockSpec(memory_space=pltpu.SMEM)
HBM = pl.BlockSpec(memory_space=pltpu.HBM)
PARAMS = pltpu.CompilerParams(vmem_limit_bytes=48 * 1024 * 1024)
HALF = 16
LANES = 128


def fold(value):
    rows, width = value.shape
    summed = jnp.sum(value.reshape(rows // 8, 8, width), axis=0)
    return sum(summed[:, k * 128 : (k + 1) * 128] for k in range(width // 128))


def fold_all(value):
    return sum(fold(value[s]) for s in range(value.shape[0]))


def message_shape(sectors, rows, width):
    return (HALF, sectors * (rows // HALF) * width + LANES)


def write_scalar(ref, index, scalar):
    whole = jnp.full((HALF, LANES), scalar, jnp.float32)
    high = whole.astype(jnp.bfloat16).astype(jnp.float32)
    rest = whole - high
    middle = rest.astype(jnp.bfloat16).astype(jnp.float32)
    low = rest - middle
    row = lax.broadcasted_iota(jnp.int32, whole.shape, 0)
    lane = lax.broadcasted_iota(jnp.int32, whole.shape, 1)
    value = jnp.where(row == 0, high, jnp.where(row == 1, middle, jnp.where(row == 2, low, 0.0)))
    value = jnp.where(lane == 0, value, 0.0)
    ref[index, :, ref.shape[2] - LANES :] = value.astype(jnp.bfloat16)


def read_scalar(ref, indices):
    return jnp.sum(
        sum(ref[i, :, ref.shape[2] - LANES :].astype(jnp.float32) for i in indices)
    )


def write_piece(ref, index, sector, value):
    rows, width = value.shape
    for h in range(rows // HALF):
        at = (sector * (rows // HALF) + h) * width
        ref[index, :, at : at + width] = value[h * HALF : (h + 1) * HALF].astype(jnp.bfloat16)


def read_piece(ref, index, sector, rows, width):
    parts = []
    for h in range(rows // HALF):
        at = (sector * (rows // HALF) + h) * width
        parts.append(ref[index, :, at : at + width].astype(jnp.float32))
    return jnp.concatenate(parts, axis=0)


def position(me_ref):
    me = me_ref[0]
    return me // 4, me // 2 % 2, me % 2


def blocks_kernel(first, direct, rows, entries, me_ref, *refs):
    n_field = 2 if direct else 1
    field_refs, refs = refs[:n_field], refs[n_field:]
    if first:
        (wave_ref, diag_ref), refs = refs[:2], refs[2:]
    else:
        (scale_ref, wave_ref, correction_ref, dots_ref), refs = refs[:4], refs[4:]
    ints_hbm, (left_hbm, right_hbm), refs = refs[:3], refs[3:5], refs[5:]
    keep_ref, send_ref, dot_ref, out_ref = refs[:4]
    left, right, field, total, sources, targets, live, left_sem, right_sem, int_sem = refs[4:]
    slots, width = left.shape[0], total.shape[2]
    sectors = total.shape[0]
    in_messages = direct and not first

    int_copies = [
        pltpu.make_async_copy(src, dst, int_sem.at[k])
        for k, (src, dst) in enumerate(zip(ints_hbm, (sources, targets, live)))
    ]
    for copy in int_copies:
        copy.start()

    def copies(slot):
        return (
            pltpu.make_async_copy(left_hbm.at[slot], left.at[slot], left_sem.at[slot]),
            pltpu.make_async_copy(right_hbm.at[slot], right.at[slot], right_sem.at[slot]),
        )

    for slot in range(slots):
        for copy in copies(slot):
            copy.start()

    core = me_ref[0] % 2
    pieces = []
    for k, ref in enumerate(field_refs):
        for i in range(ref.shape[0]):
            at = pl.multiple_of((i * 2 + (core + k) % 2) * rows, rows) if direct else 0
            for s in range(sectors):
                if in_messages:
                    read = functools.partial(read_piece, ref, i, s, rows, width)
                else:
                    read = lambda ref=ref, i=i, s=s: ref[i, s].astype(jnp.float32)
                pieces.append((k, i, s, pl.ds(at, rows), read))

    total[...] = jnp.zeros_like(total)
    dot = jnp.zeros((8, 128), jnp.float32)
    if first:
        for *_, read in pieces:
            value = read()
            dot += fold(value * value)
        scale = jnp.sqrt(jnp.sum(dot) / entries)
        out_ref[0] = scale
        for _, _, s, place, read in pieces:
            field[s, place, :] = (read() / scale).astype(jnp.bfloat16)
    else:
        for _, _, s, place, read in pieces:
            field[s, place, :] = read().astype(jnp.bfloat16)

    for copy in int_copies:
        copy.wait()
    used = live[0]

    def add_block(slot, carry):
        for copy in copies(slot):
            copy.wait()

        @pl.when(slot < used)
        def _():
            product = jnp.dot(
                left[slot], field[sources[slot]], preferred_element_type=jnp.float32
            ).astype(jnp.bfloat16)
            total[targets[slot]] += lax.dot_general(
                product, right[slot], (((1,), (1,)), ((), ())), preferred_element_type=jnp.float32
            )

        return carry

    lax.fori_loop(0, slots, add_block, 0)

    dot = jnp.zeros((8, 128), jnp.float32)
    for k, i, s, place, read in pieces:
        value = total[s, place, :]
        if first:
            dot += fold(value * read())
        if k == 0:
            keep_ref[i, s] = value
        else:
            write_piece(send_ref, i, s, value)
    if first:
        start = wave_ref[...].astype(jnp.float32) / scale
        dot = dot / scale + fold_all(diag_ref[...].astype(jnp.float32) * start * start)
    else:
        if direct:
            count = field_refs[0].shape[0]
            along = sum(read_scalar(ref, range(count)) for ref in field_refs) / entries
        else:
            along = jnp.sum(dots_ref[...]) / entries
        out_ref[0] = along
        start = wave_ref[...].astype(jnp.float32) / scale_ref[0]
        projected = correction_ref[...] - along * start
        dot = fold_all(projected * projected)
    dot_ref[...] = dot
    if direct:
        scalar = jnp.sum(dot)
        for i in range(send_ref.shape[0]):
            write_scalar(send_ref, i, scalar)


def apply_blocks(me, fields, own, blocks, first, entries):
    left, right, *ints = blocks
    slots, order, width = left.shape
    sectors = own[0 if first else 1].shape[0]
    direct = len(fields) == 2
    rows = own[0 if first else 1].shape[1] if direct else order
    count = fields[0].shape[0]
    if direct:
        kept = (count, sectors, rows, width)
        sent = (count,) + message_shape(sectors, rows, width)
    else:
        kept, sent = (1, sectors, order, width), (1, HALF, LANES)
    own_specs = [VMEM, VMEM] if first else [SMEM, VMEM, VMEM, VMEM]
    return pl.pallas_call(
        functools.partial(blocks_kernel, first, direct, rows, entries),
        in_specs=[SMEM] + [VMEM] * len(fields) + own_specs + [HBM] * 5,
        out_specs=[VMEM, VMEM, VMEM, SMEM],
        scratch_shapes=[
            pltpu.VMEM(left.shape, left.dtype),
            pltpu.VMEM(right.shape, right.dtype),
            pltpu.VMEM((sectors, order, width), jnp.bfloat16),
            pltpu.VMEM((sectors, order, width), jnp.float32),
            pltpu.SMEM((slots,), jnp.int32),
            pltpu.SMEM((slots,), jnp.int32),
            pltpu.SMEM((1,), jnp.int32),
            pltpu.SemaphoreType.DMA((slots,)),
            pltpu.SemaphoreType.DMA((slots,)),
            pltpu.SemaphoreType.DMA((3,)),
        ],
        out_shape=[
            jax.ShapeDtypeStruct(kept, jnp.float32),
            jax.ShapeDtypeStruct(sent, jnp.bfloat16),
            jax.ShapeDtypeStruct((8, 128), jnp.float32),
            jax.ShapeDtypeStruct((1,), jnp.float32),
        ],
        compiler_params=PARAMS,
        cost_estimate=pl.CostEstimate(
            flops=4 * slots * order * order * width,
            bytes_accessed=4 * slots * order * order,
            transcendentals=0,
        ),
    )(me, *fields, *own, *ints, left, right)


def core_kernel(me_ref, keep_ref, other_ref, dot_ref, kept_ref, send_ref, sum_ref):
    _, y, _ = position(me_ref)
    sectors, rows, width = keep_ref.shape[1:]
    scalar = jnp.sum(dot_ref[...]) + read_scalar(other_ref, [0])
    sum_ref[0] = scalar
    for z in range(kept_ref.shape[0]):
        mine, theirs = z * 2 + y, z * 2 + 1 - y
        for s in range(sectors):
            kept_ref[z, s] = keep_ref[mine, s] + read_piece(other_ref, mine, s, rows, width)
            value = keep_ref[theirs, s] + read_piece(other_ref, theirs, s, rows, width)
            write_piece(send_ref, z, s, value)
        write_scalar(send_ref, z, scalar)


def add_core(me, keep, other, dot):
    count, *piece = keep.shape
    return pl.pallas_call(
        core_kernel,
        in_specs=[SMEM, VMEM, VMEM, VMEM],
        out_specs=[VMEM, VMEM, SMEM],
        out_shape=[
            jax.ShapeDtypeStruct((count // 2, *piece), jnp.float32),
            jax.ShapeDtypeStruct((count // 2, *message_shape(*piece)), jnp.bfloat16),
            jax.ShapeDtypeStruct((1,), jnp.float32),
        ],
        compiler_params=PARAMS,
    )(me, keep, other, dot)


def row_kernel(keep_ref, other_ref, sum_ref, send_ref):
    sectors, rows, width = keep_ref.shape[1:]
    scalar = sum_ref[0] + read_scalar(other_ref, [0])
    for z in range(keep_ref.shape[0]):
        for s in range(sectors):
            value = keep_ref[z, s] + read_piece(other_ref, z, s, rows, width)
            write_piece(send_ref, z, s, value)
        write_scalar(send_ref, z, scalar)


def add_row(keep, other, summed):
    return pl.pallas_call(
        row_kernel,
        in_specs=[VMEM, VMEM, SMEM],
        out_specs=VMEM,
        out_shape=jax.ShapeDtypeStruct(other.shape, jnp.bfloat16),
        compiler_params=PARAMS,
    )(keep, other, summed)


def own_terms(direct, refs, sector, rows, width):
    if not direct:
        return refs[0][sector]
    ref = refs[0]
    return sum(read_piece(ref, i, sector, rows, width) for i in range(ref.shape[0]))


def own_scalar(direct, refs):
    return read_scalar(refs[0], range(refs[0].shape[0])) if direct else jnp.sum(refs[1][...])


def step_kernel(direct, entries, scale_ref, wave_ref, diag_ref, *refs):
    n_in = 1 if direct else 2
    ins, (first_ref, terms_ref, correction_ref, rounded_ref, dots_ref) = refs[:n_in], refs[n_in:]
    sectors, rows, width = wave_ref.shape
    ritz = own_scalar(direct, ins) / entries
    dots = jnp.zeros((8, 128), jnp.float32)
    for s in range(sectors):
        start = wave_ref[s].astype(jnp.float32) / scale_ref[0]
        diag = diag_ref[s].astype(jnp.float32)
        terms = own_terms(direct, ins, s, rows, width)
        first = terms + diag * start
        correction = (first - ritz * start) / jnp.maximum(jnp.abs(diag - ritz), 1.0)
        first_ref[s] = first
        terms_ref[s] = terms
        correction_ref[s] = correction
        dots += fold(start * correction)
        if direct:
            for i in range(rounded_ref.shape[0]):
                write_piece(rounded_ref, i, s, correction)
        else:
            rounded_ref[s] = correction.astype(jnp.bfloat16)
    dots_ref[...] = dots
    if direct:
        scalar = jnp.sum(dots)
        for i in range(rounded_ref.shape[0]):
            write_scalar(rounded_ref, i, scalar)


def davidson_step(scale, wave, diag, ins, entries, copies):
    full = jax.ShapeDtypeStruct(wave.shape, jnp.float32)
    direct = len(ins) == 1
    rounded = (copies, *message_shape(*wave.shape)) if direct else wave.shape
    return pl.pallas_call(
        functools.partial(step_kernel, direct, entries),
        in_specs=[SMEM, VMEM, VMEM] + [VMEM] * len(ins),
        out_specs=[VMEM] * 5,
        out_shape=[
            full,
            full,
            full,
            jax.ShapeDtypeStruct(rounded, jnp.bfloat16),
            jax.ShapeDtypeStruct((8, 128), jnp.float32),
        ],
        compiler_params=PARAMS,
    )(scale, wave, diag, *ins)


def finish_kernel(
    direct, entries, along_ref, scale_ref, wave_ref, diag_ref, terms_ref, correction_ref, *refs
):
    *ins, vector_ref, image_ref = refs
    sectors, rows, width = wave_ref.shape
    along = along_ref[0]
    norm = jnp.sqrt(own_scalar(direct, ins) / entries)
    for s in range(sectors):
        start = wave_ref[s].astype(jnp.float32) / scale_ref[0]
        second = (correction_ref[s] - along * start) / norm
        vector_ref[s] = second
        image = (own_terms(direct, ins, s, rows, width) - along * terms_ref[s]) / norm
        image_ref[s] = image + diag_ref[s].astype(jnp.float32) * second


def finish(along, scale, wave, diag, terms, correction, ins, entries):
    full = jax.ShapeDtypeStruct(wave.shape, jnp.float32)
    return pl.pallas_call(
        functools.partial(finish_kernel, len(ins) == 1, entries),
        in_specs=[SMEM, SMEM] + [VMEM] * (4 + len(ins)),
        out_specs=[VMEM] * 2,
        out_shape=[full, full],
        compiler_params=PARAMS,
    )(along, scale, wave, diag, terms, correction, *ins)


def flip(value, bit):
    return lax.ppermute(value, "term", [(i, i ^ bit) for i in range(16)])


class DirectPlan:
    copies = 8

    def gather(self, copies):
        groups = [[chip * 2 + c for chip in range(8)] for c in range(2)]
        mine = lax.all_to_all(copies, "term", 0, 0, axis_index_groups=groups)
        return [mine, flip(mine, 1)]

    def gather_first(self, own):
        return self.gather(jnp.broadcast_to(own[None], (self.copies, *own.shape)))

    def scatter(self, me, keep, send, dot):
        keep, send, summed = add_core(me, keep, flip(send, 1), dot)
        sums = add_row(keep, flip(send, 2), summed)
        groups = [[z * 4 + y * 2 + c for z in range(4)] for y in range(2) for c in range(2)]
        return [lax.all_to_all(sums, "term", 0, 0, axis_index_groups=groups)]


class WholePlan:
    copies = 1

    def gather(self, own):
        return [lax.all_gather(own, "term", axis=1, tiled=True)[None]]

    gather_first = gather

    def scatter(self, me, keep, send, dot):
        rows = lax.psum_scatter(keep[0], "term", scatter_dimension=1, tiled=True)
        return [rows, lax.psum(dot, "term")]


def on_device(
    wavefunction, diagonal, left_blocks, right_blocks, block_source, block_target, live_count
):
    devices = lax.axis_size("term")
    sectors, rows, width = wavefunction.shape
    entries = float(sectors * rows * devices * width)
    plan = DirectPlan() if devices == 16 else WholePlan()
    direct = devices == 16
    me = lax.axis_index("term").astype(jnp.int32).reshape(1)
    blocks = (left_blocks, right_blocks, block_source, block_target, live_count)

    fields = plan.gather_first(wavefunction)
    own = (wavefunction, diagonal)
    keep, send, dot, scale = apply_blocks(me, fields, own, blocks, True, entries)
    ins = plan.scatter(me, keep, send, dot)
    first_image, terms, correction, rounded, dots = davidson_step(
        scale, wavefunction, diagonal, ins, entries, plan.copies
    )
    fields = plan.gather(rounded)
    if not direct:
        dots = lax.psum(dots, "term")
    own = (scale, wavefunction, correction, dots)
    keep, send, dot, along = apply_blocks(me, fields, own, blocks, False, entries)
    ins = plan.scatter(me, keep, send, dot)
    second_vector, second_image = finish(
        along, scale, wavefunction, diagonal, terms, correction, ins, entries
    )
    return (first_image, second_vector, second_image)


def solution(mesh):
    placed = (
        P("grp", "term", None),
        P("grp", "term", None),
        P(("grp", "term"), None, None),
        P(("grp", "term"), None, None),
        P(("grp", "term")),
        P(("grp", "term")),
        P(("grp", "term")),
    )
    return jax.shard_map(
        on_device,
        mesh=mesh,
        in_specs=placed,
        out_specs=(P("grp", "term", None), P("grp", "term", None), P("grp", "term", None)),
        check_vma=False,
    )
```

time: 421 us -> 140 us (0.33)
  waiting for transfers between devices: 270 us -> 29.2 us
  blocking collectives: 0 us -> 80.5 us
  loops' own time: 46.9 us -> 0 us
  matrix products: 29.2 us -> 0 us
  local copies, waits for them, and re-layouts: 30.6 us -> 4.09 us
  other arithmetic: 25.2 us -> 0 us
  Pallas kernels: 0 us -> 16.3 us
  between operations: 16.5 us -> 1.38 us
  starting transfers between devices: 0.15 us -> 8.39 us
    psum x1 -> x0, waiting for transfers between devices: 132 us -> none  [on_device(): first_whole = lax.psum(first_terms, 'term') + whole_diag * start_whole]
    reduce_scatter x1 -> x0, waiting for transfers between devices: 92.5 us -> none  [on_device(): lax.psum_scatter(second_terms, 'term', scatter_dimension=1, tiled=True)]
    all_to_all x0 -> x4, blocking collectives: none -> 80.5 us  [the longest x2 51.7 us: gather(): mine = lax.all_to_all(copies, 'term', 0, 0, axis_index_groups=groups)]
    another operation x2 -> x0, loops' own time: 46.9 us -> none  [block_loop(): return lax.fori_loop(0, last_slot, add_block, partial_sum)]
    all_gather x2 -> x0, waiting for transfers between devices: 43.9 us -> none  [the longest x1 43.9 us: on_device(): lax.all_gather(wavefunction, 'term', axis=1, tiled=True).astype(jnp.float32)]
    dot_general x10 -> x0, matrix products: 29.2 us -> none  [add_block(): jnp.dot(product, right_op.T, preferred_element_type=jnp.float32)]
    ppermute x0 -> x6, waiting for transfers between devices: none -> 29.2 us  [flip(): return lax.ppermute(value, 'term', [(i, i ^ bit) for i in range(16)])]
    dynamic_slice x31 -> x0, local copies, waits for them, and re-layouts: 26.4 us -> none  [the longest x10 13 us: add_block(): before = lax.dynamic_index_in_dim(running, target, 0, keepdims=False)]
  transfers between devices with their start and end apart: 4 -> 6, of which waited for: 3 -> 6; matrix products, arithmetic and copies ran while one was open for 8% -> 0% of each run, Pallas kernels for 0% -> 0%
where the time goes in v2:
time: 140 us
  blocking collectives  80.5 us (58%)
  waiting for transfers between devices  29.2 us (21%)
  Pallas kernels  16.3 us (12%)
  starting transfers between devices  8.39 us (6%)
  local copies, waits for them, and re-layouts  4.09 us (3%)
    all_to_all x2, blocking collectives, gather(): mine = lax.all_to_all(copies, 'term', 0, 0, axis_index_groups=groups)  51.7 us
    ppermute x6, waiting for transfers between devices, flip(): return lax.ppermute(value, 'term', [(i, i ^ bit) for i in range(16)])  29.2 us
    all_to_all x2, blocking collectives, scatter(): return [lax.all_to_all(sums, 'term', 0, 0, axis_index_groups=groups)]  28.8 us
    pallas_call x2, Pallas kernels, apply_blocks(): pl.pallas_call(functools.partial(blocks_kernel, first, direct, rows, entr...  9.72 us
    ppermute x6, starting transfers between devices, flip(): return lax.ppermute(value, 'term', [(i, i ^ bit) for i in range(16)])  8.39 us
    unnamed x16, local copies, waits for them, and re-layouts  3.12 us
  transfers between devices with their start and end apart: 6, of which 6 were waited for; matrix products, arithmetic and copies ran while one was open for 0% of the time, Pallas kernels for 0%

profile of v2, /device:TPU:0, one launch (start us, length us, event | category | flops | bytes accessed | tf_op | source)
XLA Modules:
  0.0 139.8 jit_solution(9603127449907535263)
XLA Ops:
  0.6 1.0 broadcast_in_dim.2
  1.6 27.2 %all_to_all.20.refs_0_ = bf16[8,3,32,512]{3,2,1,0:T(8,128)(2,1)S(1)} all-to-all(bf16[8,3,32,512]{3,2,1,0:T(8,128)(2,1)S(1)} %broadcast_in_dim.2), channel_id=1, replica_groups={{0,2,4,6,8,10,12,14},{1,3,5,7,9,11,13,15},{16,18,20,22,24,26,28,30},{17..., dimensions={0} | all-to-all | bytes 1572864 | tf_op jit(solution)/shard_map/all_to_all | solution.py:364
  29.5 1.6 %collective-permute-done.refs_1_ = bf16[8,3,32,512]{3,2,1,0:T(8,128)(2,1)S(1)} collective-permute-done((bf16[8,3,32,512]{3,2,1,0:T(8,128)(2,1)S(1)}, bf16[8,3,32,512]{3,2,1,0:T(8,128)(2,1)S(1)}, u32[]{:S(2)}, u32[]{:S(2)}) %collective-permute-start) | collective-permute-done | bytes 786464 | tf_op jit(solution)/shard_map/ppermute | solution.py:356
  31.1 0.9 copy-done
  32.0 0.9 copy-done.2
  32.9 0.7 copy-done.4
  33.6 0.7 copy-done.6
  34.2 4.8 %shard_map.94 = (f32[8,3,32,512]{3,2,1,0:T(8,128)S(1)}, bf16[8,16,3200]{2,1,0:T(8,128)(2,1)S(1)}, f32[8,128]{1,0:T(8,128)S(1)}, f32[1]{0:T(128)}) custom-call(s32[1]{0:T(128)} %bitcast.me_ref, bf16[8,3,32,512]{3,2,1,0:T(8,128)(2,1)S(1)} %all_to_all.20.refs_0_, bf16[8,3,32,512]{3,2,1,0:T(8,128)(2,1)S(1)} %collective-permute-done.refs_1_, ...), custom_call_target="tpu_custom_call" | custom-call | flops 4294967296 | bytes 8388608 | tf_op jit(solution)/shard_map/pallas_call | solution.py:191
  39.0 0.0 copy-start.1
  39.0 0.0 copy-start.3
  39.0 0.0 copy-start.5
  39.0 0.0 copy-start.7
  39.0 3.1 %collective-permute-start.1 = (bf16[8,16,3200]{2,1,0:T(8,128)(2,1)S(1)}, bf16[8,16,3200]{2,1,0:T(8,128)(2,1)S(1)}, u32[]{:S(2)}, u32[]{:S(2)}) collective-permute-start(bf16[8,16,3200]{2,1,0:T(8,128)(2,1)S(1)} %get-tuple-element.26), channel_id=1, source_target_pairs={{0,1},{1,0},{2,3},{3,2},{4,5},{5,4},{6,7},{7,6},{8,9},{9,8},{10,11... | collective-permute-start | bytes 2457608 | tf_op jit(solution)/shard_map/ppermute | solution.py:356
  42.1 2.0 %collective-permute-done.1.other_ref = bf16[8,16,3200]{2,1,0:T(8,128)(2,1)S(1)} collective-permute-done((bf16[8,16,3200]{2,1,0:T(8,128)(2,1)S(1)}, bf16[8,16,3200]{2,1,0:T(8,128)(2,1)S(1)}, u32[]{:S(2)}, u32[]{:S(2)}) %collective-permute-start.1) | collective-permute-done | bytes 819232 | tf_op jit(solution)/shard_map/ppermute | solution.py:356
  44.1 0.6 shard_map.95
  44.7 1.5 %collective-permute-start.2 = (bf16[4,16,3200]{2,1,0:T(8,128)(2,1)S(1)}, bf16[4,16,3200]{2,1,0:T(8,128)(2,1)S(1)}, u32[]{:S(2)}, u32[]{:S(2)}) collective-permute-start(bf16[4,16,3200]{2,1,0:T(8,128)(2,1)S(1)} %get-tuple-element.29), channel_id=1, source_target_pairs={{0,2},{1,3},{2,0},{3,1},{4,6},{5,7},{6,4},{7,5},{8,10},{9,11},{10,... | collective-permute-start | bytes 1228808 | tf_op jit(solution)/shard_map/ppermute | solution.py:356
  46.2 10.3 %collective-permute-done.2.other_ref = bf16[4,16,3200]{2,1,0:T(8,128)(2,1)S(1)} collective-permute-done((bf16[4,16,3200]{2,1,0:T(8,128)(2,1)S(1)}, bf16[4,16,3200]{2,1,0:T(8,128)(2,1)S(1)}, u32[]{:S(2)}, u32[]{:S(2)}) %collective-permute-start.2) | collective-permute-done | bytes 409632 | tf_op jit(solution)/shard_map/ppermute | solution.py:356
  56.5 0.8 shard_map.96
  57.3 14.4 %all_to_all.21.refs_0_ = bf16[4,16,3200]{2,1,0:T(8,128)(2,1)S(1)} all-to-all(bf16[4,16,3200]{2,1,0:T(8,128)(2,1)S(1)} %shard_map.96), channel_id=1, replica_groups={{0,4,8,12},{1,5,9,13},{2,6,10,14},{3,7,11,15},{16,20,24,28},{17,21,25,2..., dimensions={0} | all-to-all | bytes 819200 | tf_op jit(solution)/shard_map/all_to_all | solution.py:374
  71.7 1.5 %shard_map.97 = (f32[3,32,512]{2,1,0:T(8,128)}, f32[3,32,512]{2,1,0:T(8,128)S(1)}, f32[3,32,512]{2,1,0:T(8,128)S(1)}, bf16[8,16,3200]{2,1,0:T(8,128)(2,1)S(1)}, f32[8,128]{1,0:T(8,128)S(1)}) custom-call(f32[1]{0:T(128)} %get-tuple-element.24.scale_ref.refs_2_, bf16[3,32,512]{2,1,0:T(8,128)(2,1)S(1)} %copy-done.1, bf16[3,32,512]{2,1,0:T(8,128)(2,1)S(1)} %copy-done.3, ...), custom_call_target="tpu_custom_call" | custom-call | tf_op jit(solution)/shard_map/pallas_call | solution.py:314
  73.2 24.5 %all_to_all.22.refs_0_ = bf16[8,16,3200]{2,1,0:T(8,128)(2,1)S(1)} all-to-all(bf16[8,16,3200]{2,1,0:T(8,128)(2,1)S(1)} %get-tuple-element.32), channel_id=1, replica_groups={{0,2,4,6,8,10,12,14},{1,3,5,7,9,11,13,15},{16,18,20,22,24,26,28,30},{17..., dimensions={0} | all-to-all | bytes 1638400 | tf_op jit(solution)/shard_map/all_to_all | solution.py:364
  97.7 0.0 collective-permute-start.3
  97.7 2.3 %collective-permute-done.3.refs_1_ = bf16[8,16,3200]{2,1,0:T(8,128)(2,1)S(1)} collective-permute-done((bf16[8,16,3200]{2,1,0:T(8,128)(2,1)S(1)}, bf16[8,16,3200]{2,1,0:T(8,128)(2,1)S(1)}, u32[]{:S(2)}, u32[]{:S(2)}) %collective-permute-start.3) | collective-permute-done | bytes 819232 | tf_op jit(solution)/shard_map/ppermute | solution.py:356
  100.1 5.0 %shard_map.98 = (f32[8,3,32,512]{3,2,1,0:T(8,128)S(1)}, bf16[8,16,3200]{2,1,0:T(8,128)(2,1)S(1)}, f32[8,128]{1,0:T(8,128)S(1)}, f32[1]{0:T(128)}) custom-call(s32[1]{0:T(128)} %bitcast.me_ref, bf16[8,16,3200]{2,1,0:T(8,128)(2,1)S(1)} %all_to_all.22.refs_0_, bf16[8,16,3200]{2,1,0:T(8,128)(2,1)S(1)} %collective-permute-done.3.refs_1_, ...), custom_call_target="tpu_custom_call" | custom-call | flops 4294967296 | bytes 8388608 | tf_op jit(solution)/shard_map/pallas_call | solution.py:191
  105.0 3.0 %collective-permute-start.4 = (bf16[8,16,3200]{2,1,0:T(8,128)(2,1)S(1)}, bf16[8,16,3200]{2,1,0:T(8,128)(2,1)S(1)}, u32[]{:S(2)}, u32[]{:S(2)}) collective-permute-start(bf16[8,16,3200]{2,1,0:T(8,128)(2,1)S(1)} %get-tuple-element.38), channel_id=1, source_target_pairs={{0,1},{1,0},{2,3},{3,2},{4,5},{5,4},{6,7},{7,6},{8,9},{9,8},{10,11... | collective-permute-start | bytes 2457608 | tf_op jit(solution)/shard_map/ppermute | solution.py:356
  108.1 2.0 %collective-permute-done.4.other_ref = bf16[8,16,3200]{2,1,0:T(8,128)(2,1)S(1)} collective-permute-done((bf16[8,16,3200]{2,1,0:T(8,128)(2,1)S(1)}, bf16[8,16,3200]{2,1,0:T(8,128)(2,1)S(1)}, u32[]{:S(2)}, u32[]{:S(2)}) %collective-permute-start.4) | collective-permute-done | bytes 819232 | tf_op jit(solution)/shard_map/ppermute | solution.py:356
  110.0 0.6 shard_map.99
  110.7 0.8 collective-permute-start.5
  111.4 11.0 %collective-permute-done.5.other_ref = bf16[4,16,3200]{2,1,0:T(8,128)(2,1)S(1)} collective-permute-done((bf16[4,16,3200]{2,1,0:T(8,128)(2,1)S(1)}, bf16[4,16,3200]{2,1,0:T(8,128)(2,1)S(1)}, u32[]{:S(2)}, u32[]{:S(2)}) %collective-permute-start.5) | collective-permute-done | bytes 409632 | tf_op jit(solution)/shard_map/ppermute | solution.py:356
  122.5 0.8 shard_map.100
  123.2 14.4 %all_to_all.23.refs_0_ = bf16[4,16,3200]{2,1,0:T(8,128)(2,1)S(1)} all-to-all(bf16[4,16,3200]{2,1,0:T(8,128)(2,1)S(1)} %shard_map.100), channel_id=1, replica_groups={{0,4,8,12},{1,5,9,13},{2,6,10,14},{3,7,11,15},{16,20,24,28},{17,21,25,2..., dimensions={0} | all-to-all | bytes 819200 | tf_op jit(solution)/shard_map/all_to_all | solution.py:374
  137.6 2.2 %shard_map.101 = (f32[3,32,512]{2,1,0:T(8,128)}, f32[3,32,512]{2,1,0:T(8,128)}) custom-call(f32[1]{0:T(128)} %get-tuple-element.35.along_ref, f32[1]{0:T(128)} %get-tuple-element.24.scale_ref.refs_2_, bf16[3,32,512]{2,1,0:T(8,128)(2,1)S(1)} %copy-done.1, bf16[3,32,512]{2,1,0:T(8,128)(2,1)S(1)} %copy-done.3, f32[3,32,512]{2,1,0:T(8,128)S(1)} %get-tuple-element.36.terms_ref, ...), custom_call_target="tpu_custom_call" | custom-call | tf_op jit(solution)/shard_map/pallas_call | solution.py:346
  (9 shorter events, 0.0 us)
Async XLA Ops:
  28.8 2.3 %collective-permute-start = (bf16[8,3,32,512]{3,2,1,0:T(8,128)(2,1)S(1)}, bf16[8,3,32,512]{3,2,1,0:T(8,128)(2,1)S(1)}, u32[]{:S(2)}, u32[]{:S(2)}) collective-permute-start(bf16[8,3,32,512]{3,2,1,0:T(8,128)(2,1)S(1)} %all_to_all.20.refs_0_), channel_id=1, source_target_pairs={{0,1},{1,0},{2,3},{3,2},{4,5},{5,4},{6,7},{7,6},{8,9},{9,8},{10,11... | collective-permute-start | bytes 2359304 | tf_op jit(solution)/shard_map/ppermute | solution.py:356
  31.1 0.9 copy-start
  32.0 0.9 copy-start.2
  32.9 0.7 copy-start.4
  33.6 0.7 copy-start.6
  39.0 32.7 %copy-start.1 = (bf16[3,32,512]{2,1,0:T(8,128)(2,1)S(1)}, bf16[3,32,512]{2,1,0:T(8,128)(2,1)}, u32[]{:S(2)}) copy-start(bf16[3,32,512]{2,1,0:T(8,128)(2,1)} %wave_ref.3) | copy-start | bytes 294916
  39.0 32.7 %copy-start.3 = (bf16[3,32,512]{2,1,0:T(8,128)(2,1)S(1)}, bf16[3,32,512]{2,1,0:T(8,128)(2,1)}, u32[]{:S(2)}) copy-start(bf16[3,32,512]{2,1,0:T(8,128)(2,1)} %diag_ref.3) | copy-start | bytes 294916
  39.0 61.1 %copy-start.5 = (s32[8]{0:T(128)S(1)}, s32[8]{0:T(128)}, u32[]{:S(2)}) copy-start(s32[8]{0:T(128)} %refs_6_.2) | copy-start | bytes 100
  39.0 61.0 %copy-start.7 = (s32[8]{0:T(128)S(1)}, s32[8]{0:T(128)}, u32[]{:S(2)}) copy-start(s32[8]{0:T(128)} %refs_7_.3) | copy-start | bytes 100
  39.0 5.0 %collective-permute-start.1 = (bf16[8,16,3200]{2,1,0:T(8,128)(2,1)S(1)}, bf16[8,16,3200]{2,1,0:T(8,128)(2,1)S(1)}, u32[]{:S(2)}, u32[]{:S(2)}) collective-permute-start(bf16[8,16,3200]{2,1,0:T(8,128)(2,1)S(1)} %get-tuple-element.26), channel_id=1, source_target_pairs={{0,1},{1,0},{2,3},{3,2},{4,5},{5,4},{6,7},{7,6},{8,9},{9,8},{10,11... | collective-permute-start | bytes 2457608 | tf_op jit(solution)/shard_map/ppermute | solution.py:356
  44.7 11.8 %collective-permute-start.2 = (bf16[4,16,3200]{2,1,0:T(8,128)(2,1)S(1)}, bf16[4,16,3200]{2,1,0:T(8,128)(2,1)S(1)}, u32[]{:S(2)}, u32[]{:S(2)}) collective-permute-start(bf16[4,16,3200]{2,1,0:T(8,128)(2,1)S(1)} %get-tuple-element.29), channel_id=1, source_target_pairs={{0,2},{1,3},{2,0},{3,1},{4,6},{5,7},{6,4},{7,5},{8,10},{9,11},{10,... | collective-permute-start | bytes 1228808 | tf_op jit(solution)/shard_map/ppermute | solution.py:356
  97.7 2.3 %collective-permute-start.3 = (bf16[8,16,3200]{2,1,0:T(8,128)(2,1)S(1)}, bf16[8,16,3200]{2,1,0:T(8,128)(2,1)S(1)}, u32[]{:S(2)}, u32[]{:S(2)}) collective-permute-start(bf16[8,16,3200]{2,1,0:T(8,128)(2,1)S(1)} %all_to_all.22.refs_0_), channel_id=1, source_target_pairs={{0,1},{1,0},{2,3},{3,2},{4,5},{5,4},{6,7},{7,6},{8,9},{9,8},{10,11... | collective-permute-start | bytes 2457608 | tf_op jit(solution)/shard_map/ppermute | solution.py:356
  105.0 5.0 %collective-permute-start.4 = (bf16[8,16,3200]{2,1,0:T(8,128)(2,1)S(1)}, bf16[8,16,3200]{2,1,0:T(8,128)(2,1)S(1)}, u32[]{:S(2)}, u32[]{:S(2)}) collective-permute-start(bf16[8,16,3200]{2,1,0:T(8,128)(2,1)S(1)} %get-tuple-element.38), channel_id=1, source_target_pairs={{0,1},{1,0},{2,3},{3,2},{4,5},{5,4},{6,7},{7,6},{8,9},{9,8},{10,11... | collective-permute-start | bytes 2457608 | tf_op jit(solution)/shard_map/ppermute | solution.py:356
  110.7 11.8 %collective-permute-start.5 = (bf16[4,16,3200]{2,1,0:T(8,128)(2,1)S(1)}, bf16[4,16,3200]{2,1,0:T(8,128)(2,1)S(1)}, u32[]{:S(2)}, u32[]{:S(2)}) collective-permute-start(bf16[4,16,3200]{2,1,0:T(8,128)(2,1)S(1)} %get-tuple-element.41), channel_id=1, source_target_pairs={{0,2},{1,3},{2,0},{3,1},{4,6},{5,7},{6,4},{7,5},{8,10},{9,11},{10,... | collective-permute-start | bytes 1228808 | tf_op jit(solution)/shard_map/ppermute | solution.py:356

commit v3 on v2

v3 whole, which is shorter than its diff:
```python
import functools

import jax
import jax.numpy as jnp
from jax import lax
from jax.experimental import pallas as pl
from jax.experimental.pallas import tpu as pltpu
from jax.sharding import PartitionSpec as P

VMEM = pl.BlockSpec(memory_space=pltpu.VMEM)
SMEM = pl.BlockSpec(memory_space=pltpu.SMEM)
HBM = pl.BlockSpec(memory_space=pltpu.HBM)
PARAMS = pltpu.CompilerParams(vmem_limit_bytes=48 * 1024 * 1024)
HALF = 16
LANES = 128


def fold(value):
    rows, width = value.shape
    summed = jnp.sum(value.reshape(rows // 8, 8, width), axis=0)
    return sum(summed[:, k * 128 : (k + 1) * 128] for k in range(width // 128))


def fold_all(value):
    return sum(fold(value[s]) for s in range(value.shape[0]))


def message_shape(sectors, rows, width):
    return (HALF, sectors * (rows // HALF) * width + LANES)


def write_lanes(ref, lanes):
    whole = jnp.broadcast_to(lanes, (HALF, LANES))
    high = whole.astype(jnp.bfloat16).astype(jnp.float32)
    rest = whole - high
    middle = rest.astype(jnp.bfloat16).astype(jnp.float32)
    low = rest - middle
    row = lax.broadcasted_iota(jnp.int32, whole.shape, 0)
    value = jnp.where(row == 0, high, jnp.where(row == 1, middle, jnp.where(row == 2, low, 0.0)))
    ref[:, ref.shape[1] - LANES :] = value.astype(jnp.bfloat16)


def read_lanes(ref):
    return jnp.sum(ref[:, ref.shape[1] - LANES :].astype(jnp.float32), axis=0, keepdims=True)


def message_parts(sectors, rows, width):
    for s in range(sectors):
        for h in range(rows // HALF):
            at = (s * (rows // HALF) + h) * width
            yield s, h * HALF, slice(at, at + width)


def chip_at(place):
    place = lax.rem(place + 8, 8)
    return jnp.where(place < 4, 2 * place, 15 - 2 * place)


def ring_place(me):
    chip, core = me // 2, me % 2
    place = jnp.where(chip % 2 == 0, chip // 2, (15 - chip) // 2)
    return place, core


def ahead(me, distance, half, core=None):
    place, own = ring_place(me)
    core = own if core is None else core
    return chip_at(place + (1 - 2 * core) * distance) * 2 + half


CHAIN = ((4, True), (3, True), (3, False), (2, True), (2, False), (1, True), (1, False), (0, True))


def chain_devices(me, core):
    return [ahead(me, d, core if own else 1 - core, core) for d, own in CHAIN]


def gathered_devices(me):
    core = me % 2
    devices = []
    for sign, mine in ((-1, core), (1, 1 - core)):
        devices.append(ahead(me, 0, mine))
        for d in (1, 2, 3):
            devices += [ahead(me, sign * d, mine), ahead(me, sign * d, 1 - mine)]
        devices.append(ahead(me, 4, mine))
    return devices


def blocks_kernel(first, direct, rows, entries, me_ref, *refs):
    n_field = 16 if direct else 1
    field_refs, refs = refs[:n_field], refs[n_field:]
    if first:
        (wave_ref, diag_ref), refs = refs[:2], refs[2:]
    else:
        (scale_ref, wave_ref, correction_ref, dots_ref), refs = refs[:4], refs[4:]
    ints_hbm, (left_hbm, right_hbm), refs = refs[:3], refs[3:5], refs[5:]
    keep_ref, near_ref, far_ref, dot_ref, out_ref = refs[:5]
    left, right, field, total, sources, targets, live, left_sem, right_sem, int_sem = refs[5:]
    slots, width = left.shape[0], total.shape[2]
    sectors = total.shape[0]

    int_copies = [
        pltpu.make_async_copy(src, dst, int_sem.at[k])
        for k, (src, dst) in enumerate(zip(ints_hbm, (sources, targets, live)))
    ]
    for copy in int_copies:
        copy.start()

    def copies(slot):
        return (
            pltpu.make_async_copy(left_hbm.at[slot], left.at[slot], left_sem.at[slot]),
            pltpu.make_async_copy(right_hbm.at[slot], right.at[slot], right_sem.at[slot]),
        )

    for slot in range(slots):
        for copy in copies(slot):
            copy.start()

    me = me_ref[0]
    pieces = []
    owners = gathered_devices(me) if direct else [0]
    for ref, owner in zip(field_refs, owners):
        at = pl.multiple_of(owner * rows, rows) if direct else 0
        if direct and not first:
            for s, row, lanes in message_parts(sectors, rows, width):
                pieces.append((ref, (slice(None), lanes), s, pl.ds(at + row, HALF)))
        else:
            for s in range(sectors):
                pieces.append((ref, (s,), s, pl.ds(at, rows if direct else field.shape[1])))

    total[...] = jnp.zeros_like(total)
    dot = jnp.zeros((8, 128), jnp.float32)
    if first:
        for ref, part, _, _ in pieces:
            value = ref[part].astype(jnp.float32)
            dot += fold(value * value)
        scale = jnp.sqrt(jnp.sum(dot) / entries)
        out_ref[0] = scale
        for ref, part, s, place in pieces:
            field[s, place, :] = (ref[part].astype(jnp.float32) / scale).astype(jnp.bfloat16)
    else:
        for ref, part, s, place in pieces:
            field[s, place, :] = ref[part]

    for copy in int_copies:
        copy.wait()
    used = live[0]

    def add_block(slot, carry):
        for copy in copies(slot):
            copy.wait()

        @pl.when(slot < used)
        def _():
            product = jnp.dot(
                left[slot], field[sources[slot]], preferred_element_type=jnp.float32
            ).astype(jnp.bfloat16)
            total[targets[slot]] += lax.dot_general(
                product, right[slot], (((1,), (1,)), ((), ())), preferred_element_type=jnp.float32
            )

        return carry

    lax.fori_loop(0, slots, add_block, 0)

    dot = jnp.zeros((8, 128), jnp.float32)
    if first:
        for ref, part, s, place in pieces:
            dot += fold(total[s, place, :] * ref[part].astype(jnp.float32))
        start = wave_ref[...].astype(jnp.float32) / scale
        dot = dot / scale + fold_all(diag_ref[...].astype(jnp.float32) * start * start)
    else:
        if direct:
            along = jnp.sum(sum(read_lanes(ref) for ref in field_refs)) / entries
        else:
            along = jnp.sum(dots_ref[...]) / entries
        out_ref[0] = along
        start = wave_ref[...].astype(jnp.float32) / scale_ref[0]
        projected = correction_ref[...] - along * start
        dot = fold_all(projected * projected)
    dot_ref[...] = dot
    if not direct:
        keep_ref[0] = total[...]
        return
    lanes = jnp.sum(dot, axis=0, keepdims=True)
    core = me % 2
    for k, owner in enumerate(chain_devices(me, core)):
        at = pl.multiple_of(owner * rows, rows)
        for s in range(sectors):
            keep_ref[k, s] = total[s, pl.ds(at, rows), :]
    for k, owner in enumerate(chain_devices(me, 1 - core)):
        at = pl.multiple_of(owner * rows, rows)
        ref = near_ref.at[k] if k < near_ref.shape[0] else far_ref.at[k - near_ref.shape[0]]
        for s, row, part in message_parts(sectors, rows, width):
            ref[:, part] = total[s, pl.ds(at + row, HALF), :].astype(jnp.bfloat16)
        write_lanes(ref, lanes)


def apply_blocks(me, fields, own, blocks, first, entries):
    left, right, *ints = blocks
    slots, order, width = left.shape
    sectors, rows, _ = own[0 if first else 1].shape
    direct = len(fields) == 16
    if direct:
        kept, message = (8, sectors, rows, width), message_shape(sectors, rows, width)
    else:
        kept, message = (1, sectors, order, width), (HALF, LANES)
    own_specs = [VMEM, VMEM] if first else [SMEM, VMEM, VMEM, VMEM]
    return pl.pallas_call(
        functools.partial(blocks_kernel, first, direct, rows, entries),
        in_specs=[SMEM] + [VMEM] * len(fields) + own_specs + [HBM] * 5,
        out_specs=[VMEM, VMEM, VMEM, VMEM, SMEM],
        scratch_shapes=[
            pltpu.VMEM(left.shape, left.dtype),
            pltpu.VMEM(right.shape, right.dtype),
            pltpu.VMEM((sectors, order, width), jnp.bfloat16),
            pltpu.VMEM((sectors, order, width), jnp.float32),
            pltpu.SMEM((slots,), jnp.int32),
            pltpu.SMEM((slots,), jnp.int32),
            pltpu.SMEM((1,), jnp.int32),
            pltpu.SemaphoreType.DMA((slots,)),
            pltpu.SemaphoreType.DMA((slots,)),
            pltpu.SemaphoreType.DMA((3,)),
        ],
        out_shape=[
            jax.ShapeDtypeStruct(kept, jnp.float32),
            jax.ShapeDtypeStruct((3, *message), jnp.bfloat16),
            jax.ShapeDtypeStruct((5, *message), jnp.bfloat16),
            jax.ShapeDtypeStruct((8, 128), jnp.float32),
            jax.ShapeDtypeStruct((1,), jnp.float32),
        ],
        compiler_params=PARAMS,
        cost_estimate=pl.CostEstimate(
            flops=4 * slots * order * order * width,
            bytes_accessed=4 * slots * order * order,
            transcendentals=0,
        ),
    )(me, *fields, *own, *ints, left, right)


def chain_kernel(links, keep_ref, other_ref, dot_ref, *refs):
    n_in = sum(arrived for _, _, arrived in links)
    arrived_refs, out_refs = list(refs[:n_in]), refs[n_in:]
    sectors, rows, width = keep_ref.shape[1:]
    for (k, other, arrived), out_ref in zip(links, out_refs):
        arrived_ref = arrived_refs.pop(0) if arrived else None
        for s, row, part in message_parts(sectors, rows, width):
            value = keep_ref[k, s, row : row + HALF, :]
            value += other_ref[other, :, part].astype(jnp.float32)
            if arrived:
                value += arrived_ref[:, part].astype(jnp.float32)
            out_ref[:, part] = value.astype(jnp.bfloat16)
        lanes = jnp.sum(dot_ref[...], axis=0, keepdims=True) + read_lanes(other_ref.at[other])
        if arrived:
            lanes += read_lanes(arrived_ref)
        write_lanes(out_ref, lanes)


def chain(links, keep, other, dot, *arrived):
    out = [jax.ShapeDtypeStruct(other.shape[1:], jnp.bfloat16)] * len(links)
    return pl.pallas_call(
        functools.partial(chain_kernel, links),
        in_specs=[VMEM] * (3 + len(arrived)),
        out_specs=[VMEM] * len(links),
        out_shape=out,
        compiler_params=PARAMS,
    )(keep, other, dot, *arrived)


def own_terms(direct, refs, sector):
    if not direct:
        return refs[0][sector]
    keep_ref, other_ref, _, *arrived_refs = refs
    own = keep_ref.shape[0] - 1
    parts = []
    for s, row, part in message_parts(*keep_ref.shape[1:]):
        if s == sector:
            value = keep_ref[own, s, row : row + HALF, :]
            value += other_ref[other_ref.shape[0] - 1, :, part].astype(jnp.float32)
            for ref in arrived_refs:
                value += ref[:, part].astype(jnp.float32)
            parts.append(value)
    return jnp.concatenate(parts, axis=0)


def own_scalar(direct, refs):
    if not direct:
        return jnp.sum(refs[1][...])
    _, other_ref, dot_ref, *arrived_refs = refs
    lanes = jnp.sum(dot_ref[...], axis=0, keepdims=True)
    lanes += read_lanes(other_ref.at[other_ref.shape[0] - 1])
    return jnp.sum(lanes + sum(read_lanes(ref) for ref in arrived_refs))


def step_kernel(direct, entries, scale_ref, wave_ref, diag_ref, *refs):
    n_in = 5 if direct else 2
    ins, (first_ref, terms_ref, correction_ref, rounded_ref, dots_ref) = refs[:n_in], refs[n_in:]
    sectors, rows, width = wave_ref.shape
    ritz = own_scalar(direct, ins) / entries
    dots = jnp.zeros((8, 128), jnp.float32)
    for s in range(sectors):
        start = wave_ref[s].astype(jnp.float32) / scale_ref[0]
        diag = diag_ref[s].astype(jnp.float32)
        terms = own_terms(direct, ins, s)
        first = terms + diag * start
        correction = (first - ritz * start) / jnp.maximum(jnp.abs(diag - ritz), 1.0)
        first_ref[s] = first
        terms_ref[s] = terms
        correction_ref[s] = correction
        dots += fold(start * correction)
        if direct:
            for t, row, part in message_parts(sectors, rows, width):
                if t == s:
                    rounded_ref[:, part] = correction[row : row + HALF].astype(jnp.bfloat16)
        else:
            rounded_ref[s] = correction.astype(jnp.bfloat16)
    dots_ref[...] = dots
    if direct:
        write_lanes(rounded_ref, jnp.sum(dots, axis=0, keepdims=True))


def davidson_step(scale, wave, diag, ins, entries):
    full = jax.ShapeDtypeStruct(wave.shape, jnp.float32)
    direct = len(ins) == 5
    rounded = message_shape(*wave.shape) if direct else wave.shape
    return pl.pallas_call(
        functools.partial(step_kernel, direct, entries),
        in_specs=[SMEM, VMEM, VMEM] + [VMEM] * len(ins),
        out_specs=[VMEM] * 5,
        out_shape=[
            full,
            full,
            full,
            jax.ShapeDtypeStruct(rounded, jnp.bfloat16),
            jax.ShapeDtypeStruct((8, 128), jnp.float32),
        ],
        compiler_params=PARAMS,
    )(scale, wave, diag, *ins)


def finish_kernel(
    direct, entries, along_ref, scale_ref, wave_ref, diag_ref, terms_ref, correction_ref, *refs
):
    *ins, vector_ref, image_ref = refs
    sectors, rows, width = wave_ref.shape
    along = along_ref[0]
    norm = jnp.sqrt(own_scalar(direct, ins) / entries)
    for s in range(sectors):
        start = wave_ref[s].astype(jnp.float32) / scale_ref[0]
        second = (correction_ref[s] - along * start) / norm
        vector_ref[s] = second
        image = (own_terms(direct, ins, s) - along * terms_ref[s]) / norm
        image_ref[s] = image + diag_ref[s].astype(jnp.float32) * second


def finish(along, scale, wave, diag, terms, correction, ins, entries):
    full = jax.ShapeDtypeStruct(wave.shape, jnp.float32)
    return pl.pallas_call(
        functools.partial(finish_kernel, len(ins) == 5, entries),
        in_specs=[SMEM, SMEM] + [VMEM] * (4 + len(ins)),
        out_specs=[VMEM] * 2,
        out_shape=[full, full],
        compiler_params=PARAMS,
    )(along, scale, wave, diag, terms, correction, *ins)


def flip(value):
    return lax.ppermute(value, "term", [(i, i ^ 1) for i in range(16)])


def hop(value):
    order = [0, 2, 4, 6, 7, 5, 3, 1]
    pairs = []
    for place in range(8):
        for core, step in ((0, 1), (1, 7)):
            pairs.append((order[place] * 2 + core, order[(place + step) % 8] * 2 + core))
    return lax.ppermute(value, "term", pairs)


class RingPlan:
    def gather(self, own):
        partner = flip(own)
        mine, theirs = [own], [partner]
        one, two = own, partner
        for _ in range(3):
            one = hop(one)
            two = hop(two)
            mine += [one, two]
            theirs += [flip(one), flip(two)]
        one = hop(one)
        return mine + [one] + theirs + [flip(one)]

    def scatter(self, keep, near, far, dot):
        near = flip(near)
        near, far = lax.optimization_barrier((near, far))
        far = flip(far)
        one, two = chain(((0, 0, False), (2, 2, False)), keep, near, dot)
        one = hop(one)
        two = hop(two)
        (one,) = chain(((1, 1, True),), keep, near, dot, one)
        one = hop(one)
        (two,) = chain(((4, 1, True),), keep, far, dot, two)
        two = hop(two)
        (one,) = chain(((3, 0, True),), keep, far, dot, one)
        one = hop(one)
        (two,) = chain(((6, 3, True),), keep, far, dot, two)
        two = hop(two)
        (one,) = chain(((5, 2, True),), keep, far, dot, one)
        one = hop(one)
        return [keep, far, dot, one, flip(two)]


class WholePlan:
    def gather(self, own):
        return [lax.all_gather(own, "term", axis=1, tiled=True)]

    def scatter(self, keep, near, far, dot):
        rows = lax.psum_scatter(keep[0], "term", scatter_dimension=1, tiled=True)
        return [rows, lax.psum(dot, "term")]


def on_device(
    wavefunction, diagonal, left_blocks, right_blocks, block_source, block_target, live_count
):
    devices = lax.axis_size("term")
    sectors, rows, width = wavefunction.shape
    entries = float(sectors * rows * devices * width)
    plan = RingPlan() if devices == 16 else WholePlan()
    me = lax.axis_index("term").astype(jnp.int32).reshape(1)
    blocks = (left_blocks, right_blocks, block_source, block_target, live_count)

    own = (wavefunction, diagonal)
    *terms, scale = apply_blocks(me, plan.gather(wavefunction), own, blocks, True, entries)
    first_image, terms, correction, rounded, dots = davidson_step(
        scale, wavefunction, diagonal, plan.scatter(*terms), entries
    )
    fields = plan.gather(rounded)
    if devices != 16:
        dots = lax.psum(dots, "term")
    own = (scale, wavefunction, correction, dots)
    *second_terms, along = apply_blocks(me, fields, own, blocks, False, entries)
    second_vector, second_image = finish(
        along, scale, wavefunction, diagonal, terms, correction, plan.scatter(*second_terms), entries
    )
    return (first_image, second_vector, second_image)


def solution(mesh):
    placed = (
        P("grp", "term", None),
        P("grp", "term", None),
        P(("grp", "term"), None, None),
        P(("grp", "term"), None, None),
        P(("grp", "term")),
        P(("grp", "term")),
        P(("grp", "term")),
    )
    return jax.shard_map(
        on_device,
        mesh=mesh,
        in_specs=placed,
        out_specs=(P("grp", "term", None), P("grp", "term", None), P("grp", "term", None)),
        check_vma=False,
    )
```

time: 140 us -> 108 us (0.77)
  blocking collectives: 80.5 us -> 0 us
  starting transfers between devices: 8.39 us -> 59.4 us
  waiting for transfers between devices: 29.2 us -> 24.9 us
    all_to_all x4 -> x0, blocking collectives: 80.5 us -> none  [the longest x2 51.7 us: gather(): mine = lax.all_to_all(copies, 'term', 0, 0, axis_index_groups=groups)]
    ppermute x6 -> x50, starting transfers between devices: 8.39 us -> 59.4 us  [the longest x28 55.4 us: hop(): return lax.ppermute(value, 'term', pairs)]
    ppermute x6 -> x50, waiting for transfers between devices: 29.2 us -> 24.9 us  [the longest x28 19.8 us: hop(): return lax.ppermute(value, 'term', pairs)]
    pallas_call x2, Pallas kernels: 9.72 us -> 13.3 us  [apply_blocks(): pl.pallas_call(functools.partial(blocks_kernel, first, direct, rows, entr...]
    pallas_call x5 -> x13, Pallas kernels: 5.02 us -> 2.93 us  [the longest x1 2.21 us: finish(): pl.pallas_call(functools.partial(finish_kernel, len(ins) == 5, entries),...]
  transfers between devices with their start and end apart: 6 -> 50, of which waited for: 6 -> 18; matrix products, arithmetic and copies ran while one was open for 0% -> 0% of each run, Pallas kernels for 0% -> 1%
where the time goes in v3:
time: 108 us; the launch traced here: 107 us
  starting transfers between devices  59.4 us (55%)
  waiting for transfers between devices  24.9 us (23%)
  Pallas kernels  17.7 us (16%)
  local copies, waits for them, and re-layouts  3.12 us (3%)
  between operations  1.46 us (1%)
    ppermute x28, starting transfers between devices, hop(): return lax.ppermute(value, 'term', pairs)  55.4 us
    ppermute x28, waiting for transfers between devices, hop(): return lax.ppermute(value, 'term', pairs)  19.8 us
    pallas_call x2, Pallas kernels, apply_blocks(): pl.pallas_call(functools.partial(blocks_kernel, first, direct, rows, entr...  13.3 us
    ppermute x22, waiting for transfers between devices, flip(): return lax.ppermute(value, 'term', [(i, i ^ 1) for i in range(16)])  5.1 us
    ppermute x22, starting transfers between devices, flip(): return lax.ppermute(value, 'term', [(i, i ^ 1) for i in range(16)])  4.01 us
    unnamed x16, local copies, waits for them, and re-layouts  3.12 us
    pallas_call x1, Pallas kernels, finish(): pl.pallas_call(functools.partial(finish_kernel, len(ins) == 5, entries),...  2.21 us
  transfers between devices with their start and end apart: 50, of which 18 were waited for; matrix products, arithmetic and copies ran while one was open for 0% of the time, Pallas kernels for 1%

profile of v3, /device:TPU:0, one launch (start us, length us, event | category | flops | bytes accessed | tf_op | source)
XLA Modules:
  0.0 106.5 jit_solution(507863535846416338)
XLA Ops:
  1.1 2.6 %collective-permute-start = (bf16[3,32,512]{2,1,0:T(8,128)(2,1)}, bf16[3,32,512]{2,1,0:T(8,128)(2,1)S(1)}, u32[]{:S(2)}, u32[]{:S(2)}) collective-permute-start(bf16[3,32,512]{2,1,0:T(8,128)(2,1)} %wave_ref.3), channel_id=1, source_target_pairs={{0,4},{1,3},{4,8},{5,1},{8,12},{9,5},{12,14},{13,9},{14,10},{15,13... | collective-permute-start | bytes 294920 | tf_op jit(solution)/shard_map/ppermute | solution.py:377
  6.5 2.1 %collective-permute-start.3 = (bf16[3,32,512]{2,1,0:T(8,128)(2,1)S(1)}, bf16[3,32,512]{2,1,0:T(8,128)(2,1)S(1)}, u32[]{:S(2)}, u32[]{:S(2)}) collective-permute-start(bf16[3,32,512]{2,1,0:T(8,128)(2,1)S(1)} %collective-permute-done.refs_1_), channel_id=1, source_target_pairs={{0,4},{1,3},{4,8},{5,1},{8,12},{9,5},{12,14},{13,9},{14,10},{15,13... | collective-permute-start | bytes 294920 | tf_op jit(solution)/shard_map/ppermute | solution.py:377
  11.2 2.1 %collective-permute-start.5 = (bf16[3,32,512]{2,1,0:T(8,128)(2,1)S(1)}, bf16[3,32,512]{2,1,0:T(8,128)(2,1)S(1)}, u32[]{:S(2)}, u32[]{:S(2)}) collective-permute-start(bf16[3,32,512]{2,1,0:T(8,128)(2,1)S(1)} %collective-permute-done.3.refs_3_), channel_id=1, source_target_pairs={{0,4},{1,3},{4,8},{5,1},{8,12},{9,5},{12,14},{13,9},{14,10},{15,13... | collective-permute-start | bytes 294920 | tf_op jit(solution)/shard_map/ppermute | solution.py:377
  15.8 2.1 %collective-permute-start.7 = (bf16[3,32,512]{2,1,0:T(8,128)(2,1)S(1)}, bf16[3,32,512]{2,1,0:T(8,128)(2,1)S(1)}, u32[]{:S(2)}, u32[]{:S(2)}) collective-permute-start(bf16[3,32,512]{2,1,0:T(8,128)(2,1)S(1)} %collective-permute-done.5.refs_5_), channel_id=1, source_target_pairs={{0,4},{1,3},{4,8},{5,1},{8,12},{9,5},{12,14},{13,9},{14,10},{15,13... | collective-permute-start | bytes 294920 | tf_op jit(solution)/shard_map/ppermute | solution.py:377
  24.8 6.8 %shard_map.94 = (f32[8,3,32,512]{3,2,1,0:T(8,128)S(1)}, bf16[3,16,3200]{2,1,0:T(8,128)(2,1)S(1)}, bf16[5,16,3200]{2,1,0:T(8,128)(2,1)S(1)}, f32[8,128]{1,0:T(8,128)S(1)}, f32[1]{0:T(128)}) custom-call(s32[1]{0:T(128)} %bitcast.me_ref, bf16[3,32,512]{2,1,0:T(8,128)(2,1)S(1)} %copy-done, bf16[3,32,512]{2,1,0:T(8,128)(2,1)S(1)} %collective-permute-done.refs_1_, ...), custom_call_target="tpu_custom_call" | custom-call | flops 4294967296 | bytes 8388608 | tf_op jit(solution)/shard_map/pallas_call | solution.py:209
  31.7 1.6 %collective-permute-done.15.other_ref = bf16[3,16,3200]{2,1,0:T(8,128)(2,1)S(1)} collective-permute-done((bf16[3,16,3200]{2,1,0:T(8,128)(2,1)S(1)}, bf16[3,16,3200]{2,1,0:T(8,128)(2,1)S(1)}, u32[]{:S(2)}, u32[]{:S(2)}) %collective-permute-start.15) | collective-permute-done | bytes 307232 | tf_op jit(solution)/shard_map/ppermute | solution.py:368
  33.5 2.8 %collective-permute-start.17 = (bf16[16,3200]{1,0:T(8,128)(2,1)S(1)}, bf16[16,3200]{1,0:T(8,128)(2,1)S(1)}, u32[]{:S(2)}, u32[]{:S(2)}) collective-permute-start(bf16[16,3200]{1,0:T(8,128)(2,1)S(1)} %get-tuple-element.35), channel_id=1, source_target_pairs={{0,4},{1,3},{4,8},{5,1},{8,12},{9,5},{12,14},{13,9},{14,10},{15,13... | collective-permute-start | bytes 307208 | tf_op jit(solution)/shard_map/ppermute | solution.py:377
  36.5 2.1 %collective-permute-done.17.refs_0_ = bf16[16,3200]{1,0:T(8,128)(2,1)S(1)} collective-permute-done((bf16[16,3200]{1,0:T(8,128)(2,1)S(1)}, bf16[16,3200]{1,0:T(8,128)(2,1)S(1)}, u32[]{:S(2)}, u32[]{:S(2)}) %collective-permute-start.17) | collective-permute-done | bytes 102432 | tf_op jit(solution)/shard_map/ppermute | solution.py:377
  38.6 2.5 %collective-permute-start.18 = (bf16[16,3200]{1,0:T(8,128)(2,1)S(1)}, bf16[16,3200]{1,0:T(8,128)(2,1)S(1)}, u32[]{:S(2)}, u32[]{:S(2)}) collective-permute-start(bf16[16,3200]{1,0:T(8,128)(2,1)S(1)} %shard_map.96), channel_id=1, source_target_pairs={{0,4},{1,3},{4,8},{5,1},{8,12},{9,5},{12,14},{13,9},{14,10},{15,13... | collective-permute-start | bytes 307208 | tf_op jit(solution)/shard_map/ppermute | solution.py:377
  43.4 2.5 %collective-permute-start.19 = (bf16[16,3200]{1,0:T(8,128)(2,1)S(1)}, bf16[16,3200]{1,0:T(8,128)(2,1)S(1)}, u32[]{:S(2)}, u32[]{:S(2)}) collective-permute-start(bf16[16,3200]{1,0:T(8,128)(2,1)S(1)} %shard_map.97), channel_id=1, source_target_pairs={{0,4},{1,3},{4,8},{5,1},{8,12},{9,5},{12,14},{13,9},{14,10},{15,13... | collective-permute-start | bytes 307208 | tf_op jit(solution)/shard_map/ppermute | solution.py:377
  45.9 1.6 %collective-permute-start.23 = (bf16[16,3200]{1,0:T(8,128)(2,1)S(1)}, bf16[16,3200]{1,0:T(8,128)(2,1)S(1)}, u32[]{:S(2)}, u32[]{:S(2)}) collective-permute-start(bf16[16,3200]{1,0:T(8,128)(2,1)S(1)} %shard_map.100), channel_id=1, source_target_pairs={{0,4},{1,3},{4,8},{5,1},{8,12},{9,5},{12,14},{13,9},{14,10},{15,13... | collective-permute-start | bytes 307208 | tf_op jit(solution)/shard_map/ppermute | solution.py:377
  48.2 2.5 %collective-permute-start.20 = (bf16[16,3200]{1,0:T(8,128)(2,1)S(1)}, bf16[16,3200]{1,0:T(8,128)(2,1)S(1)}, u32[]{:S(2)}, u32[]{:S(2)}) collective-permute-start(bf16[16,3200]{1,0:T(8,128)(2,1)S(1)} %shard_map.98), channel_id=1, source_target_pairs={{0,4},{1,3},{4,8},{5,1},{8,12},{9,5},{12,14},{13,9},{14,10},{15,13... | collective-permute-start | bytes 307208 | tf_op jit(solution)/shard_map/ppermute | solution.py:377
  50.7 2.6 %collective-permute-done.20.refs_3_ = bf16[16,3200]{1,0:T(8,128)(2,1)S(1)} collective-permute-done((bf16[16,3200]{1,0:T(8,128)(2,1)S(1)}, bf16[16,3200]{1,0:T(8,128)(2,1)S(1)}, u32[]{:S(2)}, u32[]{:S(2)}) %collective-permute-start.20) | collective-permute-done | bytes 102432 | tf_op jit(solution)/shard_map/ppermute | solution.py:377
  54.8 2.0 %collective-permute-start.25 = (bf16[16,3200]{1,0:T(8,128)(2,1)S(1)}, bf16[16,3200]{1,0:T(8,128)(2,1)S(1)}, u32[]{:S(2)}, u32[]{:S(2)}) collective-permute-start(bf16[16,3200]{1,0:T(8,128)(2,1)S(1)} %get-tuple-element.38.refs_0_), channel_id=1, source_target_pairs={{0,4},{1,3},{4,8},{5,1},{8,12},{9,5},{12,14},{13,9},{14,10},{15,13... | collective-permute-start | bytes 307208 | tf_op jit(solution)/shard_map/ppermute | solution.py:377
  56.8 1.6 %collective-permute-start.27 = (bf16[16,3200]{1,0:T(8,128)(2,1)S(1)}, bf16[16,3200]{1,0:T(8,128)(2,1)S(1)}, u32[]{:S(2)}, u32[]{:S(2)}) collective-permute-start(bf16[16,3200]{1,0:T(8,128)(2,1)S(1)} %collective-permute-done.26.refs_8_), channel_id=1, source_target_pairs={{0,4},{1,3},{4,8},{5,1},{8,12},{9,5},{12,14},{13,9},{14,10},{15,13... | collective-permute-start | bytes 307208 | tf_op jit(solution)/shard_map/ppermute | solution.py:377
  59.5 2.0 %collective-permute-start.28 = (bf16[16,3200]{1,0:T(8,128)(2,1)S(1)}, bf16[16,3200]{1,0:T(8,128)(2,1)S(1)}, u32[]{:S(2)}, u32[]{:S(2)}) collective-permute-start(bf16[16,3200]{1,0:T(8,128)(2,1)S(1)} %collective-permute-done.25.refs_1_), channel_id=1, source_target_pairs={{0,4},{1,3},{4,8},{5,1},{8,12},{9,5},{12,14},{13,9},{14,10},{15,13... | collective-permute-start | bytes 307208 | tf_op jit(solution)/shard_map/ppermute | solution.py:377
  61.5 1.6 %collective-permute-start.29 = (bf16[16,3200]{1,0:T(8,128)(2,1)S(1)}, bf16[16,3200]{1,0:T(8,128)(2,1)S(1)}, u32[]{:S(2)}, u32[]{:S(2)}) collective-permute-start(bf16[16,3200]{1,0:T(8,128)(2,1)S(1)} %collective-permute-done.27.refs_2_), channel_id=1, source_target_pairs={{0,4},{1,3},{4,8},{5,1},{8,12},{9,5},{12,14},{13,9},{14,10},{15,13... | collective-permute-start | bytes 307208 | tf_op jit(solution)/shard_map/ppermute | solution.py:377
  64.1 2.0 %collective-permute-start.30 = (bf16[16,3200]{1,0:T(8,128)(2,1)S(1)}, bf16[16,3200]{1,0:T(8,128)(2,1)S(1)}, u32[]{:S(2)}, u32[]{:S(2)}) collective-permute-start(bf16[16,3200]{1,0:T(8,128)(2,1)S(1)} %collective-permute-done.28.refs_3_), channel_id=1, source_target_pairs={{0,4},{1,3},{4,8},{5,1},{8,12},{9,5},{12,14},{13,9},{14,10},{15,13... | collective-permute-start | bytes 307208 | tf_op jit(solution)/shard_map/ppermute | solution.py:377
  66.6 1.6 %collective-permute-start.31 = (bf16[16,3200]{1,0:T(8,128)(2,1)S(1)}, bf16[16,3200]{1,0:T(8,128)(2,1)S(1)}, u32[]{:S(2)}, u32[]{:S(2)}) collective-permute-start(bf16[16,3200]{1,0:T(8,128)(2,1)S(1)} %collective-permute-done.29.refs_4_), channel_id=1, source_target_pairs={{0,4},{1,3},{4,8},{5,1},{8,12},{9,5},{12,14},{13,9},{14,10},{15,13... | collective-permute-start | bytes 307208 | tf_op jit(solution)/shard_map/ppermute | solution.py:377
  68.8 2.0 %collective-permute-start.32 = (bf16[16,3200]{1,0:T(8,128)(2,1)S(1)}, bf16[16,3200]{1,0:T(8,128)(2,1)S(1)}, u32[]{:S(2)}, u32[]{:S(2)}) collective-permute-start(bf16[16,3200]{1,0:T(8,128)(2,1)S(1)} %collective-permute-done.30.refs_5_), channel_id=1, source_target_pairs={{0,4},{1,3},{4,8},{5,1},{8,12},{9,5},{12,14},{13,9},{14,10},{15,13... | collective-permute-start | bytes 307208 | tf_op jit(solution)/shard_map/ppermute | solution.py:377
  71.8 1.6 %collective-permute-done.32.refs_7_ = bf16[16,3200]{1,0:T(8,128)(2,1)S(1)} collective-permute-done((bf16[16,3200]{1,0:T(8,128)(2,1)S(1)}, bf16[16,3200]{1,0:T(8,128)(2,1)S(1)}, u32[]{:S(2)}, u32[]{:S(2)}) %collective-permute-start.32) | collective-permute-done | bytes 102432 | tf_op jit(solution)/shard_map/ppermute | solution.py:377
  74.8 6.5 %shard_map.102 = (f32[8,3,32,512]{3,2,1,0:T(8,128)S(1)}, bf16[3,16,3200]{2,1,0:T(8,128)(2,1)S(1)}, bf16[5,16,3200]{2,1,0:T(8,128)(2,1)S(1)}, f32[8,128]{1,0:T(8,128)S(1)}, f32[1]{0:T(128)}) custom-call(s32[1]{0:T(128)} %bitcast.me_ref, bf16[16,3200]{1,0:T(8,128)(2,1)S(1)} %get-tuple-element.38.refs_0_, bf16[16,3200]{1,0:T(8,128)(2,1)S(1)} %collective-permute-done.25.refs_1_, ...), custom_call_target="tpu_custom_call" | custom-call | flops 4294967296 | bytes 8388608 | tf_op jit(solution)/shard_map/pallas_call | solution.py:209
  81.3 1.6 %collective-permute-done.40.other_ref = bf16[3,16,3200]{2,1,0:T(8,128)(2,1)S(1)} collective-permute-done((bf16[3,16,3200]{2,1,0:T(8,128)(2,1)S(1)}, bf16[3,16,3200]{2,1,0:T(8,128)(2,1)S(1)}, u32[]{:S(2)}, u32[]{:S(2)}) %collective-permute-start.40) | collective-permute-done | bytes 307232 | tf_op jit(solution)/shard_map/ppermute | solution.py:368
  83.1 2.8 %collective-permute-start.42 = (bf16[16,3200]{1,0:T(8,128)(2,1)S(1)}, bf16[16,3200]{1,0:T(8,128)(2,1)S(1)}, u32[]{:S(2)}, u32[]{:S(2)}) collective-permute-start(bf16[16,3200]{1,0:T(8,128)(2,1)S(1)} %get-tuple-element.49), channel_id=1, source_target_pairs={{0,4},{1,3},{4,8},{5,1},{8,12},{9,5},{12,14},{13,9},{14,10},{15,13... | collective-permute-start | bytes 307208 | tf_op jit(solution)/shard_map/ppermute | solution.py:377
  86.4 1.7 %collective-permute-done.42.refs_0_ = bf16[16,3200]{1,0:T(8,128)(2,1)S(1)} collective-permute-done((bf16[16,3200]{1,0:T(8,128)(2,1)S(1)}, bf16[16,3200]{1,0:T(8,128)(2,1)S(1)}, u32[]{:S(2)}, u32[]{:S(2)}) %collective-permute-start.42) | collective-permute-done | bytes 102432 | tf_op jit(solution)/shard_map/ppermute | solution.py:377
  88.2 2.5 %collective-permute-start.43 = (bf16[16,3200]{1,0:T(8,128)(2,1)S(1)}, bf16[16,3200]{1,0:T(8,128)(2,1)S(1)}, u32[]{:S(2)}, u32[]{:S(2)}) collective-permute-start(bf16[16,3200]{1,0:T(8,128)(2,1)S(1)} %shard_map.104), channel_id=1, source_target_pairs={{0,4},{1,3},{4,8},{5,1},{8,12},{9,5},{12,14},{13,9},{14,10},{15,13... | collective-permute-start | bytes 307208 | tf_op jit(solution)/shard_map/ppermute | solution.py:377
  90.7 2.9 %collective-permute-start.47 = (bf16[16,3200]{1,0:T(8,128)(2,1)S(1)}, bf16[16,3200]{1,0:T(8,128)(2,1)S(1)}, u32[]{:S(2)}, u32[]{:S(2)}) collective-permute-start(bf16[16,3200]{1,0:T(8,128)(2,1)S(1)} %shard_map.107), channel_id=1, source_target_pairs={{0,4},{1,3},{4,8},{5,1},{8,12},{9,5},{12,14},{13,9},{14,10},{15,13... | collective-permute-start | bytes 307208 | tf_op jit(solution)/shard_map/ppermute | solution.py:377
  93.7 2.3 %collective-permute-start.44 = (bf16[16,3200]{1,0:T(8,128)(2,1)S(1)}, bf16[16,3200]{1,0:T(8,128)(2,1)S(1)}, u32[]{:S(2)}, u32[]{:S(2)}) collective-permute-start(bf16[16,3200]{1,0:T(8,128)(2,1)S(1)} %shard_map.105), channel_id=1, source_target_pairs={{0,4},{1,3},{4,8},{5,1},{8,12},{9,5},{12,14},{13,9},{14,10},{15,13... | collective-permute-start | bytes 307208 | tf_op jit(solution)/shard_map/ppermute | solution.py:377
  96.1 2.5 %collective-permute-start.48 = (bf16[16,3200]{1,0:T(8,128)(2,1)S(1)}, bf16[16,3200]{1,0:T(8,128)(2,1)S(1)}, u32[]{:S(2)}, u32[]{:S(2)}) collective-permute-start(bf16[16,3200]{1,0:T(8,128)(2,1)S(1)} %shard_map.108), channel_id=1, source_target_pairs={{0,4},{1,3},{4,8},{5,1},{8,12},{9,5},{12,14},{13,9},{14,10},{15,13... | collective-permute-start | bytes 307208 | tf_op jit(solution)/shard_map/ppermute | solution.py:377
  98.6 2.2 %collective-permute-start.45 = (bf16[16,3200]{1,0:T(8,128)(2,1)S(1)}, bf16[16,3200]{1,0:T(8,128)(2,1)S(1)}, u32[]{:S(2)}, u32[]{:S(2)}) collective-permute-start(bf16[16,3200]{1,0:T(8,128)(2,1)S(1)} %shard_map.106), channel_id=1, source_target_pairs={{0,4},{1,3},{4,8},{5,1},{8,12},{9,5},{12,14},{13,9},{14,10},{15,13... | collective-permute-start | bytes 307208 | tf_op jit(solution)/shard_map/ppermute | solution.py:377
  100.8 3.5 %collective-permute-done.45.refs_3_ = bf16[16,3200]{1,0:T(8,128)(2,1)S(1)} collective-permute-done((bf16[16,3200]{1,0:T(8,128)(2,1)S(1)}, bf16[16,3200]{1,0:T(8,128)(2,1)S(1)}, u32[]{:S(2)}, u32[]{:S(2)}) %collective-permute-start.45) | collective-permute-done | bytes 102432 | tf_op jit(solution)/shard_map/ppermute | solution.py:377
  104.3 2.2 %shard_map.109 = (f32[3,32,512]{2,1,0:T(8,128)}, f32[3,32,512]{2,1,0:T(8,128)}) custom-call(f32[1]{0:T(128)} %get-tuple-element.41.along_ref, f32[1]{0:T(128)} %get-tuple-element.28.scale_ref.refs_16_, bf16[3,32,512]{2,1,0:T(8,128)(2,1)S(1)} %copy-done.1, bf16[3,32,512]{2,1,0:T(8,128)(2,1)S(1)} %copy-done.3, f32[3,32,512]{2,1,0:T(8,128)S(1)} %get-tuple-element.42.terms_ref, ...), custom_call_target="tpu_custom_call" | custom-call | tf_op jit(solution)/shard_map/pallas_call | solution.py:358
  (100 shorter events, 26.4 us)
Async XLA Ops:
  1.1 5.4 %collective-permute-start = (bf16[3,32,512]{2,1,0:T(8,128)(2,1)}, bf16[3,32,512]{2,1,0:T(8,128)(2,1)S(1)}, u32[]{:S(2)}, u32[]{:S(2)}) collective-permute-start(bf16[3,32,512]{2,1,0:T(8,128)(2,1)} %wave_ref.3), channel_id=1, source_target_pairs={{0,4},{1,3},{4,8},{5,1},{8,12},{9,5},{12,14},{13,9},{14,10},{15,13... | collective-permute-start | bytes 294920 | tf_op jit(solution)/shard_map/ppermute | solution.py:377
  3.8 4.8 %collective-permute-start.2 = (bf16[3,32,512]{2,1,0:T(8,128)(2,1)S(1)}, bf16[3,32,512]{2,1,0:T(8,128)(2,1)S(1)}, u32[]{:S(2)}, u32[]{:S(2)}) collective-permute-start(bf16[3,32,512]{2,1,0:T(8,128)(2,1)S(1)} %collective-permute-done.1.refs_8_), channel_id=1, source_target_pairs={{0,4},{1,3},{4,8},{5,1},{8,12},{9,5},{12,14},{13,9},{14,10},{15,13... | collective-permute-start | bytes 294920 | tf_op jit(solution)/shard_map/ppermute | solution.py:377
  6.5 4.6 %collective-permute-start.3 = (bf16[3,32,512]{2,1,0:T(8,128)(2,1)S(1)}, bf16[3,32,512]{2,1,0:T(8,128)(2,1)S(1)}, u32[]{:S(2)}, u32[]{:S(2)}) collective-permute-start(bf16[3,32,512]{2,1,0:T(8,128)(2,1)S(1)} %collective-permute-done.refs_1_), channel_id=1, source_target_pairs={{0,4},{1,3},{4,8},{5,1},{8,12},{9,5},{12,14},{13,9},{14,10},{15,13... | collective-permute-start | bytes 294920 | tf_op jit(solution)/shard_map/ppermute | solution.py:377
  8.6 5.1 %collective-permute-start.4 = (bf16[3,32,512]{2,1,0:T(8,128)(2,1)S(1)}, bf16[3,32,512]{2,1,0:T(8,128)(2,1)S(1)}, u32[]{:S(2)}, u32[]{:S(2)}) collective-permute-start(bf16[3,32,512]{2,1,0:T(8,128)(2,1)S(1)} %collective-permute-done.2.refs_2_), channel_id=1, source_target_pairs={{0,4},{1,3},{4,8},{5,1},{8,12},{9,5},{12,14},{13,9},{14,10},{15,13... | collective-permute-start | bytes 294920 | tf_op jit(solution)/shard_map/ppermute | solution.py:377
  13.2 4.6 %collective-permute-start.8 = (bf16[3,32,512]{2,1,0:T(8,128)(2,1)S(1)}, bf16[3,32,512]{2,1,0:T(8,128)(2,1)S(1)}, u32[]{:S(2)}, u32[]{:S(2)}) collective-permute-start(bf16[3,32,512]{2,1,0:T(8,128)(2,1)S(1)} %collective-permute-done.refs_1_), channel_id=1, source_target_pairs={{0,1},{1,0},{2,3},{3,2},{4,5},{5,4},{6,7},{7,6},{8,9},{9,8},{10,11... | collective-permute-start | bytes 294920 | tf_op jit(solution)/shard_map/ppermute | solution.py:368
  13.2 5.1 %collective-permute-start.9 = (bf16[3,32,512]{2,1,0:T(8,128)(2,1)S(1)}, bf16[3,32,512]{2,1,0:T(8,128)(2,1)S(1)}, u32[]{:S(2)}, u32[]{:S(2)}) collective-permute-start(bf16[3,32,512]{2,1,0:T(8,128)(2,1)S(1)} %collective-permute-done.2.refs_2_), channel_id=1, source_target_pairs={{0,1},{1,0},{2,3},{3,2},{4,5},{5,4},{6,7},{7,6},{8,9},{9,8},{10,11... | collective-permute-start | bytes 294920 | tf_op jit(solution)/shard_map/ppermute | solution.py:368
  13.7 4.7 %collective-permute-start.6 = (bf16[3,32,512]{2,1,0:T(8,128)(2,1)S(1)}, bf16[3,32,512]{2,1,0:T(8,128)(2,1)S(1)}, u32[]{:S(2)}, u32[]{:S(2)}) collective-permute-start(bf16[3,32,512]{2,1,0:T(8,128)(2,1)S(1)} %collective-permute-done.4.refs_4_), channel_id=1, source_target_pairs={{0,4},{1,3},{4,8},{5,1},{8,12},{9,5},{12,14},{13,9},{14,10},{15,13... | collective-permute-start | bytes 294920 | tf_op jit(solution)/shard_map/ppermute | solution.py:377
  33.3 7.8 %collective-permute-start.16 = (bf16[5,16,3200]{2,1,0:T(8,128)(2,1)S(1)}, bf16[5,16,3200]{2,1,0:T(8,128)(2,1)S(1)}, u32[]{:S(2)}, u32[]{:S(2)}) collective-permute-start(bf16[5,16,3200]{2,1,0:T(8,128)(2,1)S(1)} %get-tuple-element.32), channel_id=1, source_target_pairs={{0,1},{1,0},{2,3},{3,2},{4,5},{5,4},{6,7},{7,6},{8,9},{9,8},{10,11... | collective-permute-start | bytes 1536008 | tf_op jit(solution)/shard_map/ppermute | solution.py:368
  33.5 5.1 %collective-permute-start.17 = (bf16[16,3200]{1,0:T(8,128)(2,1)S(1)}, bf16[16,3200]{1,0:T(8,128)(2,1)S(1)}, u32[]{:S(2)}, u32[]{:S(2)}) collective-permute-start(bf16[16,3200]{1,0:T(8,128)(2,1)S(1)} %get-tuple-element.35), channel_id=1, source_target_pairs={{0,4},{1,3},{4,8},{5,1},{8,12},{9,5},{12,14},{13,9},{14,10},{15,13... | collective-permute-start | bytes 307208 | tf_op jit(solution)/shard_map/ppermute | solution.py:377
  36.3 4.8 %collective-permute-start.21 = (bf16[16,3200]{1,0:T(8,128)(2,1)S(1)}, bf16[16,3200]{1,0:T(8,128)(2,1)S(1)}, u32[]{:S(2)}, u32[]{:S(2)}) collective-permute-start(bf16[16,3200]{1,0:T(8,128)(2,1)S(1)} %get-tuple-element.36), channel_id=1, source_target_pairs={{0,4},{1,3},{4,8},{5,1},{8,12},{9,5},{12,14},{13,9},{14,10},{15,13... | collective-permute-start | bytes 307208 | tf_op jit(solution)/shard_map/ppermute | solution.py:377
  38.6 4.7 %collective-permute-start.18 = (bf16[16,3200]{1,0:T(8,128)(2,1)S(1)}, bf16[16,3200]{1,0:T(8,128)(2,1)S(1)}, u32[]{:S(2)}, u32[]{:S(2)}) collective-permute-start(bf16[16,3200]{1,0:T(8,128)(2,1)S(1)} %shard_map.96), channel_id=1, source_target_pairs={{0,4},{1,3},{4,8},{5,1},{8,12},{9,5},{12,14},{13,9},{14,10},{15,13... | collective-permute-start | bytes 307208 | tf_op jit(solution)/shard_map/ppermute | solution.py:377
  41.2 4.7 %collective-permute-start.22 = (bf16[16,3200]{1,0:T(8,128)(2,1)S(1)}, bf16[16,3200]{1,0:T(8,128)(2,1)S(1)}, u32[]{:S(2)}, u32[]{:S(2)}) collective-permute-start(bf16[16,3200]{1,0:T(8,128)(2,1)S(1)} %shard_map.99), channel_id=1, source_target_pairs={{0,4},{1,3},{4,8},{5,1},{8,12},{9,5},{12,14},{13,9},{14,10},{15,13... | collective-permute-start | bytes 307208 | tf_op jit(solution)/shard_map/ppermute | solution.py:377
  43.4 4.7 %collective-permute-start.19 = (bf16[16,3200]{1,0:T(8,128)(2,1)S(1)}, bf16[16,3200]{1,0:T(8,128)(2,1)S(1)}, u32[]{:S(2)}, u32[]{:S(2)}) collective-permute-start(bf16[16,3200]{1,0:T(8,128)(2,1)S(1)} %shard_map.97), channel_id=1, source_target_pairs={{0,4},{1,3},{4,8},{5,1},{8,12},{9,5},{12,14},{13,9},{14,10},{15,13... | collective-permute-start | bytes 307208 | tf_op jit(solution)/shard_map/ppermute | solution.py:377
  45.9 4.7 %collective-permute-start.23 = (bf16[16,3200]{1,0:T(8,128)(2,1)S(1)}, bf16[16,3200]{1,0:T(8,128)(2,1)S(1)}, u32[]{:S(2)}, u32[]{:S(2)}) collective-permute-start(bf16[16,3200]{1,0:T(8,128)(2,1)S(1)} %shard_map.100), channel_id=1, source_target_pairs={{0,4},{1,3},{4,8},{5,1},{8,12},{9,5},{12,14},{13,9},{14,10},{15,13... | collective-permute-start | bytes 307208 | tf_op jit(solution)/shard_map/ppermute | solution.py:377
  48.2 5.1 %collective-permute-start.20 = (bf16[16,3200]{1,0:T(8,128)(2,1)S(1)}, bf16[16,3200]{1,0:T(8,128)(2,1)S(1)}, u32[]{:S(2)}, u32[]{:S(2)}) collective-permute-start(bf16[16,3200]{1,0:T(8,128)(2,1)S(1)} %shard_map.98), channel_id=1, source_target_pairs={{0,4},{1,3},{4,8},{5,1},{8,12},{9,5},{12,14},{13,9},{14,10},{15,13... | collective-permute-start | bytes 307208 | tf_op jit(solution)/shard_map/ppermute | solution.py:377
  54.8 4.7 %collective-permute-start.25 = (bf16[16,3200]{1,0:T(8,128)(2,1)S(1)}, bf16[16,3200]{1,0:T(8,128)(2,1)S(1)}, u32[]{:S(2)}, u32[]{:S(2)}) collective-permute-start(bf16[16,3200]{1,0:T(8,128)(2,1)S(1)} %get-tuple-element.38.refs_0_), channel_id=1, source_target_pairs={{0,4},{1,3},{4,8},{5,1},{8,12},{9,5},{12,14},{13,9},{14,10},{15,13... | collective-permute-start | bytes 307208 | tf_op jit(solution)/shard_map/ppermute | solution.py:377
  56.8 4.7 %collective-permute-start.27 = (bf16[16,3200]{1,0:T(8,128)(2,1)S(1)}, bf16[16,3200]{1,0:T(8,128)(2,1)S(1)}, u32[]{:S(2)}, u32[]{:S(2)}) collective-permute-start(bf16[16,3200]{1,0:T(8,128)(2,1)S(1)} %collective-permute-done.26.refs_8_), channel_id=1, source_target_pairs={{0,4},{1,3},{4,8},{5,1},{8,12},{9,5},{12,14},{13,9},{14,10},{15,13... | collective-permute-start | bytes 307208 | tf_op jit(solution)/shard_map/ppermute | solution.py:377
  59.5 4.7 %collective-permute-start.28 = (bf16[16,3200]{1,0:T(8,128)(2,1)S(1)}, bf16[16,3200]{1,0:T(8,128)(2,1)S(1)}, u32[]{:S(2)}, u32[]{:S(2)}) collective-permute-start(bf16[16,3200]{1,0:T(8,128)(2,1)S(1)} %collective-permute-done.25.refs_1_), channel_id=1, source_target_pairs={{0,4},{1,3},{4,8},{5,1},{8,12},{9,5},{12,14},{13,9},{14,10},{15,13... | collective-permute-start | bytes 307208 | tf_op jit(solution)/shard_map/ppermute | solution.py:377
  61.5 5.2 %collective-permute-start.29 = (bf16[16,3200]{1,0:T(8,128)(2,1)S(1)}, bf16[16,3200]{1,0:T(8,128)(2,1)S(1)}, u32[]{:S(2)}, u32[]{:S(2)}) collective-permute-start(bf16[16,3200]{1,0:T(8,128)(2,1)S(1)} %collective-permute-done.27.refs_2_), channel_id=1, source_target_pairs={{0,4},{1,3},{4,8},{5,1},{8,12},{9,5},{12,14},{13,9},{14,10},{15,13... | collective-permute-start | bytes 307208 | tf_op jit(solution)/shard_map/ppermute | solution.py:377
  64.1 4.7 %collective-permute-start.30 = (bf16[16,3200]{1,0:T(8,128)(2,1)S(1)}, bf16[16,3200]{1,0:T(8,128)(2,1)S(1)}, u32[]{:S(2)}, u32[]{:S(2)}) collective-permute-start(bf16[16,3200]{1,0:T(8,128)(2,1)S(1)} %collective-permute-done.28.refs_3_), channel_id=1, source_target_pairs={{0,4},{1,3},{4,8},{5,1},{8,12},{9,5},{12,14},{13,9},{14,10},{15,13... | collective-permute-start | bytes 307208 | tf_op jit(solution)/shard_map/ppermute | solution.py:377
  66.1 4.7 %collective-permute-start.33 = (bf16[16,3200]{1,0:T(8,128)(2,1)S(1)}, bf16[16,3200]{1,0:T(8,128)(2,1)S(1)}, u32[]{:S(2)}, u32[]{:S(2)}) collective-permute-start(bf16[16,3200]{1,0:T(8,128)(2,1)S(1)} %collective-permute-done.25.refs_1_), channel_id=1, source_target_pairs={{0,1},{1,0},{2,3},{3,2},{4,5},{5,4},{6,7},{7,6},{8,9},{9,8},{10,11... | collective-permute-start | bytes 307208 | tf_op jit(solution)/shard_map/ppermute | solution.py:368
  66.1 5.2 %collective-permute-start.34 = (bf16[16,3200]{1,0:T(8,128)(2,1)S(1)}, bf16[16,3200]{1,0:T(8,128)(2,1)S(1)}, u32[]{:S(2)}, u32[]{:S(2)}) collective-permute-start(bf16[16,3200]{1,0:T(8,128)(2,1)S(1)} %collective-permute-done.27.refs_2_), channel_id=1, source_target_pairs={{0,1},{1,0},{2,3},{3,2},{4,5},{5,4},{6,7},{7,6},{8,9},{9,8},{10,11... | collective-permute-start | bytes 307208 | tf_op jit(solution)/shard_map/ppermute | solution.py:368
  66.6 4.7 %collective-permute-start.31 = (bf16[16,3200]{1,0:T(8,128)(2,1)S(1)}, bf16[16,3200]{1,0:T(8,128)(2,1)S(1)}, u32[]{:S(2)}, u32[]{:S(2)}) collective-permute-start(bf16[16,3200]{1,0:T(8,128)(2,1)S(1)} %collective-permute-done.29.refs_4_), channel_id=1, source_target_pairs={{0,4},{1,3},{4,8},{5,1},{8,12},{9,5},{12,14},{13,9},{14,10},{15,13... | collective-permute-start | bytes 307208 | tf_op jit(solution)/shard_map/ppermute | solution.py:377
  68.8 4.7 %collective-permute-start.32 = (bf16[16,3200]{1,0:T(8,128)(2,1)S(1)}, bf16[16,3200]{1,0:T(8,128)(2,1)S(1)}, u32[]{:S(2)}, u32[]{:S(2)}) collective-permute-start(bf16[16,3200]{1,0:T(8,128)(2,1)S(1)} %collective-permute-done.30.refs_5_), channel_id=1, source_target_pairs={{0,4},{1,3},{4,8},{5,1},{8,12},{9,5},{12,14},{13,9},{14,10},{15,13... | collective-permute-start | bytes 307208 | tf_op jit(solution)/shard_map/ppermute | solution.py:377
  82.9 7.7 %collective-permute-start.41 = (bf16[5,16,3200]{2,1,0:T(8,128)(2,1)S(1)}, bf16[5,16,3200]{2,1,0:T(8,128)(2,1)S(1)}, u32[]{:S(2)}, u32[]{:S(2)}) collective-permute-start(bf16[5,16,3200]{2,1,0:T(8,128)(2,1)S(1)} %get-tuple-element.46), channel_id=1, source_target_pairs={{0,1},{1,0},{2,3},{3,2},{4,5},{5,4},{6,7},{7,6},{8,9},{9,8},{10,11... | collective-permute-start | bytes 1536008 | tf_op jit(solution)/shard_map/ppermute | solution.py:368
  83.1 5.0 %collective-permute-start.42 = (bf16[16,3200]{1,0:T(8,128)(2,1)S(1)}, bf16[16,3200]{1,0:T(8,128)(2,1)S(1)}, u32[]{:S(2)}, u32[]{:S(2)}) collective-permute-start(bf16[16,3200]{1,0:T(8,128)(2,1)S(1)} %get-tuple-element.49), channel_id=1, source_target_pairs={{0,4},{1,3},{4,8},{5,1},{8,12},{9,5},{12,14},{13,9},{14,10},{15,13... | collective-permute-start | bytes 307208 | tf_op jit(solution)/shard_map/ppermute | solution.py:377
  85.9 4.8 %collective-permute-start.46 = (bf16[16,3200]{1,0:T(8,128)(2,1)S(1)}, bf16[16,3200]{1,0:T(8,128)(2,1)S(1)}, u32[]{:S(2)}, u32[]{:S(2)}) collective-permute-start(bf16[16,3200]{1,0:T(8,128)(2,1)S(1)} %get-tuple-element.50), channel_id=1, source_target_pairs={{0,4},{1,3},{4,8},{5,1},{8,12},{9,5},{12,14},{13,9},{14,10},{15,13... | collective-permute-start | bytes 307208 | tf_op jit(solution)/shard_map/ppermute | solution.py:377
  88.2 5.4 %collective-permute-start.43 = (bf16[16,3200]{1,0:T(8,128)(2,1)S(1)}, bf16[16,3200]{1,0:T(8,128)(2,1)S(1)}, u32[]{:S(2)}, u32[]{:S(2)}) collective-permute-start(bf16[16,3200]{1,0:T(8,128)(2,1)S(1)} %shard_map.104), channel_id=1, source_target_pairs={{0,4},{1,3},{4,8},{5,1},{8,12},{9,5},{12,14},{13,9},{14,10},{15,13... | collective-permute-start | bytes 307208 | tf_op jit(solution)/shard_map/ppermute | solution.py:377
  90.7 5.3 %collective-permute-start.47 = (bf16[16,3200]{1,0:T(8,128)(2,1)S(1)}, bf16[16,3200]{1,0:T(8,128)(2,1)S(1)}, u32[]{:S(2)}, u32[]{:S(2)}) collective-permute-start(bf16[16,3200]{1,0:T(8,128)(2,1)S(1)} %shard_map.107), channel_id=1, source_target_pairs={{0,4},{1,3},{4,8},{5,1},{8,12},{9,5},{12,14},{13,9},{14,10},{15,13... | collective-permute-start | bytes 307208 | tf_op jit(solution)/shard_map/ppermute | solution.py:377
  93.7 4.8 %collective-permute-start.44 = (bf16[16,3200]{1,0:T(8,128)(2,1)S(1)}, bf16[16,3200]{1,0:T(8,128)(2,1)S(1)}, u32[]{:S(2)}, u32[]{:S(2)}) collective-permute-start(bf16[16,3200]{1,0:T(8,128)(2,1)S(1)} %shard_map.105), channel_id=1, source_target_pairs={{0,4},{1,3},{4,8},{5,1},{8,12},{9,5},{12,14},{13,9},{14,10},{15,13... | collective-permute-start | bytes 307208 | tf_op jit(solution)/shard_map/ppermute | solution.py:377
  96.1 4.7 %collective-permute-start.48 = (bf16[16,3200]{1,0:T(8,128)(2,1)S(1)}, bf16[16,3200]{1,0:T(8,128)(2,1)S(1)}, u32[]{:S(2)}, u32[]{:S(2)}) collective-permute-start(bf16[16,3200]{1,0:T(8,128)(2,1)S(1)} %shard_map.108), channel_id=1, source_target_pairs={{0,4},{1,3},{4,8},{5,1},{8,12},{9,5},{12,14},{13,9},{14,10},{15,13... | collective-permute-start | bytes 307208 | tf_op jit(solution)/shard_map/ppermute | solution.py:377
  98.6 5.7 %collective-permute-start.45 = (bf16[16,3200]{1,0:T(8,128)(2,1)S(1)}, bf16[16,3200]{1,0:T(8,128)(2,1)S(1)}, u32[]{:S(2)}, u32[]{:S(2)}) collective-permute-start(bf16[16,3200]{1,0:T(8,128)(2,1)S(1)} %shard_map.106), channel_id=1, source_target_pairs={{0,4},{1,3},{4,8},{5,1},{8,12},{9,5},{12,14},{13,9},{14,10},{15,13... | collective-permute-start | bytes 307208 | tf_op jit(solution)/shard_map/ppermute | solution.py:377
  (26 other events, 149.0 us)

commit v4 on v3

--- a/solution.py
+++ b/solution.py
@@ -79,32 +79,33 @@
     core = me % 2
     devices = []
     for sign, mine in ((-1, core), (1, 1 - core)):
-        devices.append(ahead(me, 0, mine))
+        devices += [ahead(me, 0, mine), ahead(me, sign, mine)]
         for d in (1, 2, 3):
-            devices += [ahead(me, sign * d, mine), ahead(me, sign * d, 1 - mine)]
-        devices.append(ahead(me, 4, mine))
+            devices += [ahead(me, sign * (d + 1), mine), ahead(me, sign * d, 1 - mine)]
     return devices
 
 
+def is_pair(ref, raw):
+    return len(ref.shape) == (4 if raw else 3)
+
+
 def blocks_kernel(first, direct, rows, entries, me_ref, *refs):
-    n_field = 16 if direct else 1
+    n_field = 10 if direct else 1
     field_refs, refs = refs[:n_field], refs[n_field:]
+    if direct:
+        views = []
+        for ref in field_refs:
+            views += [ref.at[k] for k in range(ref.shape[0])] if is_pair(ref, first) else [ref]
+        field_refs = views
     if first:
-        (wave_ref, diag_ref), refs = refs[:2], refs[2:]
+        square_ref, *refs = refs
     else:
         (scale_ref, wave_ref, correction_ref, dots_ref), refs = refs[:4], refs[4:]
-    ints_hbm, (left_hbm, right_hbm), refs = refs[:3], refs[3:5], refs[5:]
+    (sources, targets, live), (left_hbm, right_hbm), refs = refs[:3], refs[3:5], refs[5:]
     keep_ref, near_ref, far_ref, dot_ref, out_ref = refs[:5]
-    left, right, field, total, sources, targets, live, left_sem, right_sem, int_sem = refs[5:]
+    left, right, field, total, left_sem, right_sem = refs[5:]
     slots, width = left.shape[0], total.shape[2]
     sectors = total.shape[0]
-
-    int_copies = [
-        pltpu.make_async_copy(src, dst, int_sem.at[k])
-        for k, (src, dst) in enumerate(zip(ints_hbm, (sources, targets, live)))
-    ]
-    for copy in int_copies:
-        copy.start()
 
     def copies(slot):
         return (
@@ -142,8 +143,6 @@
         for ref, part, s, place in pieces:
             field[s, place, :] = ref[part]
 
-    for copy in int_copies:
-        copy.wait()
     used = live[0]
 
     def add_block(slot, carry):
@@ -167,8 +166,7 @@
     if first:
         for ref, part, s, place in pieces:
             dot += fold(total[s, place, :] * ref[part].astype(jnp.float32))
-        start = wave_ref[...].astype(jnp.float32) / scale
-        dot = dot / scale + fold_all(diag_ref[...].astype(jnp.float32) * start * start)
+        dot = dot / scale + square_ref[...] / scale / scale
     else:
         if direct:
             along = jnp.sum(sum(read_lanes(ref) for ref in field_refs)) / entries
@@ -199,33 +197,30 @@
 def apply_blocks(me, fields, own, blocks, first, entries):
     left, right, *ints = blocks
     slots, order, width = left.shape
-    sectors, rows, _ = own[0 if first else 1].shape
-    direct = len(fields) == 16
+    direct = len(fields) == 10
+    sectors = fields[0].shape[0] if first or not direct else own[1].shape[0]
+    rows = fields[0].shape[1] if first else own[1].shape[1]
     if direct:
         kept, message = (8, sectors, rows, width), message_shape(sectors, rows, width)
     else:
         kept, message = (1, sectors, order, width), (HALF, LANES)
-    own_specs = [VMEM, VMEM] if first else [SMEM, VMEM, VMEM, VMEM]
+    own_specs = [VMEM] if first else [SMEM, VMEM, VMEM, VMEM]
     return pl.pallas_call(
         functools.partial(blocks_kernel, first, direct, rows, entries),
-        in_specs=[SMEM] + [VMEM] * len(fields) + own_specs + [HBM] * 5,
+        in_specs=[SMEM] + [VMEM] * len(fields) + own_specs + [SMEM] * 3 + [HBM] * 2,
         out_specs=[VMEM, VMEM, VMEM, VMEM, SMEM],
         scratch_shapes=[
             pltpu.VMEM(left.shape, left.dtype),
             pltpu.VMEM(right.shape, right.dtype),
             pltpu.VMEM((sectors, order, width), jnp.bfloat16),
             pltpu.VMEM((sectors, order, width), jnp.float32),
-            pltpu.SMEM((slots,), jnp.int32),
-            pltpu.SMEM((slots,), jnp.int32),
-            pltpu.SMEM((1,), jnp.int32),
             pltpu.SemaphoreType.DMA((slots,)),
             pltpu.SemaphoreType.DMA((slots,)),
-            pltpu.SemaphoreType.DMA((3,)),
         ],
         out_shape=[
             jax.ShapeDtypeStruct(kept, jnp.float32),
-            jax.ShapeDtypeStruct((3, *message), jnp.bfloat16),
-            jax.ShapeDtypeStruct((5, *message), jnp.bfloat16),
+            jax.ShapeDtypeStruct((1, *message), jnp.bfloat16),
+            jax.ShapeDtypeStruct((7, *message), jnp.bfloat16),
             jax.ShapeDtypeStruct((8, 128), jnp.float32),
             jax.ShapeDtypeStruct((1,), jnp.float32),
         ],
@@ -239,46 +234,99 @@
 
 
 def chain_kernel(links, keep_ref, other_ref, dot_ref, *refs):
-    n_in = sum(arrived for _, _, arrived in links)
-    arrived_refs, out_refs = list(refs[:n_in]), refs[n_in:]
+    *arrived_refs, out_ref = refs
     sectors, rows, width = keep_ref.shape[1:]
-    for (k, other, arrived), out_ref in zip(links, out_refs):
-        arrived_ref = arrived_refs.pop(0) if arrived else None
+    for place, (k, other, arrived) in enumerate(links):
+        arrived_ref = arrived_refs[0].at[place] if arrived else None
         for s, row, part in message_parts(sectors, rows, width):
             value = keep_ref[k, s, row : row + HALF, :]
             value += other_ref[other, :, part].astype(jnp.float32)
             if arrived:
                 value += arrived_ref[:, part].astype(jnp.float32)
-            out_ref[:, part] = value.astype(jnp.bfloat16)
+            out_ref[place, :, part] = value.astype(jnp.bfloat16)
         lanes = jnp.sum(dot_ref[...], axis=0, keepdims=True) + read_lanes(other_ref.at[other])
         if arrived:
             lanes += read_lanes(arrived_ref)
-        write_lanes(out_ref, lanes)
+        write_lanes(out_ref.at[place], lanes)
 
 
 def chain(links, keep, other, dot, *arrived):
-    out = [jax.ShapeDtypeStruct(other.shape[1:], jnp.bfloat16)] * len(links)
     return pl.pallas_call(
         functools.partial(chain_kernel, links),
         in_specs=[VMEM] * (3 + len(arrived)),
-        out_specs=[VMEM] * len(links),
-        out_shape=out,
+        out_specs=VMEM,
+        out_shape=jax.ShapeDtypeStruct((len(links), *other.shape[1:]), jnp.bfloat16),
         compiler_params=PARAMS,
     )(keep, other, dot, *arrived)
+
+
+def pair_kernel(one_ref, two_ref, out_ref):
+    out_ref[0] = one_ref[...]
+    out_ref[1] = two_ref[...]
+
+
+def pair(one, two):
+    return pl.pallas_call(
+        pair_kernel,
+        in_specs=[VMEM, VMEM],
+        out_specs=VMEM,
+        out_shape=jax.ShapeDtypeStruct((2, *one.shape), one.dtype),
+        compiler_params=PARAMS,
+    )(one, two)
+
+
+def second_kernel(both_ref, out_ref):
+    out_ref[...] = both_ref[1]
+
+
+def second(both):
+    return pl.pallas_call(
+        second_kernel,
+        in_specs=[VMEM],
+        out_specs=VMEM,
+        out_shape=jax.ShapeDtypeStruct(both.shape[1:], both.dtype),
+        compiler_params=PARAMS,
+    )(both)
+
+
+def prepare_kernel(wave_ref, diag_ref, *refs):
+    (source_ref, target_ref, live_ref, _), outs = refs[:4], refs[4:]
+    own_ref, square_ref, source_out, target_out, live_out = outs
+    own_ref[...] = wave_ref[...]
+    wave = wave_ref[...].astype(jnp.float32)
+    square_ref[...] = fold_all(diag_ref[...].astype(jnp.float32) * wave * wave)
+    for k in range(source_ref.shape[0]):
+        source_out[k] = source_ref[k]
+        target_out[k] = target_ref[k]
+    live_out[0] = live_ref[0]
+
+
+def prepare(wave, diag, ints, after):
+    return pl.pallas_call(
+        prepare_kernel,
+        in_specs=[VMEM, VMEM, SMEM, SMEM, SMEM, HBM],
+        out_specs=[VMEM, VMEM, SMEM, SMEM, SMEM],
+        out_shape=[
+            jax.ShapeDtypeStruct(wave.shape, wave.dtype),
+            jax.ShapeDtypeStruct((8, 128), jnp.float32),
+            *(jax.ShapeDtypeStruct(i.shape, i.dtype) for i in ints),
+        ],
+        compiler_params=PARAMS,
+    )(wave, diag, *ints, after)
 
 
 def own_terms(direct, refs, sector):
     if not direct:
         return refs[0][sector]
-    keep_ref, other_ref, _, *arrived_refs = refs
+    keep_ref, other_ref, _, ours_ref, theirs_ref = refs
     own = keep_ref.shape[0] - 1
     parts = []
     for s, row, part in message_parts(*keep_ref.shape[1:]):
         if s == sector:
             value = keep_ref[own, s, row : row + HALF, :]
             value += other_ref[other_ref.shape[0] - 1, :, part].astype(jnp.float32)
-            for ref in arrived_refs:
-                value += ref[:, part].astype(jnp.float32)
+            value += ours_ref[0, :, part].astype(jnp.float32)
+            value += theirs_ref[:, part].astype(jnp.float32)
             parts.append(value)
     return jnp.concatenate(parts, axis=0)
 
@@ -286,10 +334,10 @@
 def own_scalar(direct, refs):
     if not direct:
         return jnp.sum(refs[1][...])
-    _, other_ref, dot_ref, *arrived_refs = refs
+    _, other_ref, dot_ref, ours_ref, theirs_ref = refs
     lanes = jnp.sum(dot_ref[...], axis=0, keepdims=True)
     lanes += read_lanes(other_ref.at[other_ref.shape[0] - 1])
-    return jnp.sum(lanes + sum(read_lanes(ref) for ref in arrived_refs))
+    return jnp.sum(lanes + read_lanes(ours_ref.at[0]) + read_lanes(theirs_ref))
 
 
 def step_kernel(direct, entries, scale_ref, wave_ref, diag_ref, *refs):
@@ -378,41 +426,36 @@
 
 
 class RingPlan:
-    def gather(self, own):
+    def gather(self, own, meanwhile=None):
+        arrived = hop(own)
         partner = flip(own)
-        mine, theirs = [own], [partner]
-        one, two = own, partner
-        for _ in range(3):
-            one = hop(one)
-            two = hop(two)
-            mine += [one, two]
-            theirs += [flip(one), flip(two)]
-        one = hop(one)
-        return mine + [one] + theirs + [flip(one)]
+        both = pair(arrived, partner)
+        beside = None if meanwhile is None else meanwhile(both)
+        mine, theirs = [own, arrived], [partner, flip(arrived)]
+        for step in range(3):
+            both = hop(both)
+            if step == 1 and beside is not None:
+                both, beside = lax.optimization_barrier((both, beside))
+                mine[0] = beside[0]
+            mine.append(both)
+            theirs.append(flip(both))
+        return mine + theirs, beside
 
     def scatter(self, keep, near, far, dot):
         near = flip(near)
         near, far = lax.optimization_barrier((near, far))
         far = flip(far)
-        one, two = chain(((0, 0, False), (2, 2, False)), keep, near, dot)
-        one = hop(one)
-        two = hop(two)
-        (one,) = chain(((1, 1, True),), keep, near, dot, one)
-        one = hop(one)
-        (two,) = chain(((4, 1, True),), keep, far, dot, two)
-        two = hop(two)
-        (one,) = chain(((3, 0, True),), keep, far, dot, one)
-        one = hop(one)
-        (two,) = chain(((6, 3, True),), keep, far, dot, two)
-        two = hop(two)
-        (one,) = chain(((5, 2, True),), keep, far, dot, one)
-        one = hop(one)
-        return [keep, far, dot, one, flip(two)]
+        message = hop(chain(((0, 0, False),), keep, near, dot))
+        message = hop(chain(((1, 0, True), (2, 1, False)), keep, far, dot, message))
+        message = hop(chain(((3, 2, True), (4, 3, True)), keep, far, dot, message))
+        message = hop(chain(((5, 4, True), (6, 5, True)), keep, far, dot, message))
+        return [keep, far, dot, message, flip(second(message))]
 
 
 class WholePlan:
-    def gather(self, own):
-        return [lax.all_gather(own, "term", axis=1, tiled=True)]
+    def gather(self, own, meanwhile=None):
+        whole = lax.all_gather(own, "term", axis=1, tiled=True)
+        return [whole], None if meanwhile is None else meanwhile(own)
 
     def scatter(self, keep, near, far, dot):
         rows = lax.psum_scatter(keep[0], "term", scatter_dimension=1, tiled=True)
@@ -427,14 +470,16 @@
     entries = float(sectors * rows * devices * width)
     plan = RingPlan() if devices == 16 else WholePlan()
     me = lax.axis_index("term").astype(jnp.int32).reshape(1)
-    blocks = (left_blocks, right_blocks, block_source, block_target, live_count)
-
-    own = (wavefunction, diagonal)
-    *terms, scale = apply_blocks(me, plan.gather(wavefunction), own, blocks, True, entries)
+    ints = (block_source, block_target, live_count)
+
+    beside = functools.partial(prepare, wavefunction, diagonal, ints)
+    fields, (_, square, *ints) = plan.gather(wavefunction, beside)
+    blocks = (left_blocks, right_blocks, *ints)
+    *terms, scale = apply_blocks(me, fields, (square,), blocks, True, entries)
     first_image, terms, correction, rounded, dots = davidson_step(
         scale, wavefunction, diagonal, plan.scatter(*terms), entries
     )
-    fields = plan.gather(rounded)
+    fields, _ = plan.gather(rounded)
     if devices != 16:
         dots = lax.psum(dots, "term")
     own = (scale, wavefunction, correction, dots)

time: 108 us -> 125 us (1.16)
  waiting for transfers between devices: 24.9 us -> 81.7 us
  starting transfers between devices: 59.4 us -> 14.6 us
  Pallas kernels: 17.7 us -> 23.9 us
    ppermute x28 -> x16, waiting for transfers between devices: 19.8 us -> 73.9 us  [hop(): return lax.ppermute(value, 'term', pairs)]
    ppermute x28 -> x16, starting transfers between devices: 55.4 us -> 8.99 us  [hop(): return lax.ppermute(value, 'term', pairs)]
    pallas_call x2, Pallas kernels: 13.3 us -> 18.5 us  [apply_blocks(): pl.pallas_call(functools.partial(blocks_kernel, first, direct, rows, entr...]
    ppermute x22 -> x16, waiting for transfers between devices: 5.1 us -> 7.82 us  [flip(): return lax.ppermute(value, 'term', [(i, i ^ 1) for i in range(16)])]
    ppermute x22 -> x16, starting transfers between devices: 4.01 us -> 5.57 us  [flip(): return lax.ppermute(value, 'term', [(i, i ^ 1) for i in range(16)])]
    unnamed x16 -> x12, local copies, waits for them, and re-layouts: 3.12 us -> 3.1 us
  transfers between devices with their start and end apart: 50 -> 32, of which waited for: 18 -> 22; matrix products, arithmetic and copies ran while one was open for 0% -> 0% of each run, Pallas kernels for 1% -> 1%
where the time goes in v4:
time: 125 us
  waiting for transfers between devices  81.7 us (65%)
  Pallas kernels  23.9 us (19%)
  starting transfers between devices  14.6 us (12%)
  local copies, waits for them, and re-layouts  3.1 us (2%)
  between operations  1.48 us (1%)
    ppermute x16, waiting for transfers between devices, hop(): return lax.ppermute(value, 'term', pairs)  73.9 us
    pallas_call x2, Pallas kernels, apply_blocks(): pl.pallas_call(functools.partial(blocks_kernel, first, direct, rows, entr...  18.5 us
    ppermute x16, starting transfers between devices, hop(): return lax.ppermute(value, 'term', pairs)  8.99 us
    ppermute x16, waiting for transfers between devices, flip(): return lax.ppermute(value, 'term', [(i, i ^ 1) for i in range(16)])  7.82 us
    ppermute x16, starting transfers between devices, flip(): return lax.ppermute(value, 'term', [(i, i ^ 1) for i in range(16)])  5.57 us
    unnamed x12, local copies, waits for them, and re-layouts  3.1 us
  transfers between devices with their start and end apart: 32, of which 22 were waited for; matrix products, arithmetic and copies ran while one was open for 0% of the time, Pallas kernels for 1%

profile of v4, /device:TPU:0, one launch (start us, length us, event | category | flops | bytes accessed | tf_op | source)
XLA Modules:
  0.0 124.7 jit_solution(15967759869702078248)
XLA Ops:
  1.1 2.6 %collective-permute-start = (bf16[3,32,512]{2,1,0:T(8,128)(2,1)}, bf16[3,32,512]{2,1,0:T(8,128)(2,1)S(1)}, u32[]{:S(2)}, u32[]{:S(2)}) collective-permute-start(bf16[3,32,512]{2,1,0:T(8,128)(2,1)} %wave_ref.5), channel_id=1, source_target_pairs={{0,4},{1,3},{4,8},{5,1},{8,12},{9,5},{12,14},{13,9},{14,10},{15,13... | collective-permute-start | bytes 294920 | tf_op jit(solution)/shard_map/ppermute | solution.py:425
  3.8 2.7 %collective-permute-done.one_ref.refs_1_ = bf16[3,32,512]{2,1,0:T(8,128)(2,1)S(1)} collective-permute-done((bf16[3,32,512]{2,1,0:T(8,128)(2,1)}, bf16[3,32,512]{2,1,0:T(8,128)(2,1)S(1)}, u32[]{:S(2)}, u32[]{:S(2)}) %collective-permute-start) | collective-permute-done | bytes 98336 | tf_op jit(solution)/shard_map/ppermute | solution.py:425
  6.6 2.1 %collective-permute-start.2 = (bf16[2,3,32,512]{3,2,1,0:T(8,128)(2,1)S(1)}, bf16[2,3,32,512]{3,2,1,0:T(8,128)(2,1)S(1)}, u32[]{:S(2)}, u32[]{:S(2)}) collective-permute-start(bf16[2,3,32,512]{3,2,1,0:T(8,128)(2,1)S(1)} %shard_map.94.refs_3_), channel_id=1, source_target_pairs={{0,4},{1,3},{4,8},{5,1},{8,12},{9,5},{12,14},{13,9},{14,10},{15,13... | collective-permute-start | bytes 589832 | tf_op jit(solution)/shard_map/ppermute | solution.py:425
  8.7 3.6 %collective-permute-done.2.refs_2_ = bf16[2,3,32,512]{3,2,1,0:T(8,128)(2,1)S(1)} collective-permute-done((bf16[2,3,32,512]{3,2,1,0:T(8,128)(2,1)S(1)}, bf16[2,3,32,512]{3,2,1,0:T(8,128)(2,1)S(1)}, u32[]{:S(2)}, u32[]{:S(2)}) %collective-permute-start.2) | collective-permute-done | bytes 196640 | tf_op jit(solution)/shard_map/ppermute | solution.py:425
  12.3 2.1 %collective-permute-start.3 = (bf16[2,3,32,512]{3,2,1,0:T(8,128)(2,1)S(1)}, bf16[2,3,32,512]{3,2,1,0:T(8,128)(2,1)S(1)}, u32[]{:S(2)}, u32[]{:S(2)}) collective-permute-start(bf16[2,3,32,512]{3,2,1,0:T(8,128)(2,1)S(1)} %collective-permute-done.2.refs_2_), channel_id=1, source_target_pairs={{0,4},{1,3},{4,8},{5,1},{8,12},{9,5},{12,14},{13,9},{14,10},{15,13... | collective-permute-start | bytes 589832 | tf_op jit(solution)/shard_map/ppermute | solution.py:425
  18.1 1.2 shard_map.95
  19.3 1.6 %collective-permute-start.4 = (bf16[2,3,32,512]{3,2,1,0:T(8,128)(2,1)S(1)}, bf16[2,3,32,512]{3,2,1,0:T(8,128)(2,1)S(1)}, u32[]{:S(2)}, u32[]{:S(2)}) collective-permute-start(bf16[2,3,32,512]{3,2,1,0:T(8,128)(2,1)S(1)} %collective-permute-done.3.refs_3_), channel_id=1, source_target_pairs={{0,4},{1,3},{4,8},{5,1},{8,12},{9,5},{12,14},{13,9},{14,10},{15,13... | collective-permute-start | bytes 589832 | tf_op jit(solution)/shard_map/ppermute | solution.py:425
  21.4 3.6 %collective-permute-done.4.refs_4_ = bf16[2,3,32,512]{3,2,1,0:T(8,128)(2,1)S(1)} collective-permute-done((bf16[2,3,32,512]{3,2,1,0:T(8,128)(2,1)S(1)}, bf16[2,3,32,512]{3,2,1,0:T(8,128)(2,1)S(1)}, u32[]{:S(2)}, u32[]{:S(2)}) %collective-permute-start.4) | collective-permute-done | bytes 196640 | tf_op jit(solution)/shard_map/ppermute | solution.py:425
  25.5 1.1 collective-permute-done.5.refs_6_
  26.6 9.2 %shard_map.96 = (f32[8,3,32,512]{3,2,1,0:T(8,128)S(1)}, bf16[1,16,3200]{2,1,0:T(8,128)(2,1)S(1)}, bf16[7,16,3200]{2,1,0:T(8,128)(2,1)S(1)}, f32[8,128]{1,0:T(8,128)S(1)}, f32[1]{0:T(128)}) custom-call(s32[1]{0:T(128)} %bitcast.me_ref, bf16[3,32,512]{2,1,0:T(8,128)(2,1)S(1)} %get-tuple-element.40.refs_0_, ...), custom_call_target="tpu_custom_call" | custom-call | flops 4294967296 | bytes 8388608 | tf_op jit(solution)/shard_map/pallas_call | solution.py:208
  35.8 1.0 collective-permute-start.9
  36.8 0.9 collective-permute-done.9.other_ref
  38.2 4.6 %collective-permute-done.11.refs_0_ = bf16[1,16,3200]{2,1,0:T(8,128)(2,1)S(1)} collective-permute-done((bf16[1,16,3200]{2,1,0:T(8,128)(2,1)S(1)}, bf16[1,16,3200]{2,1,0:T(8,128)(2,1)S(1)}, u32[]{:S(2)}, u32[]{:S(2)}) %collective-permute-start.11) | collective-permute-done | bytes 102432 | tf_op jit(solution)/shard_map/ppermute | solution.py:425
  43.0 5.7 %collective-permute-done.12.refs_0_ = bf16[2,16,3200]{2,1,0:T(8,128)(2,1)S(1)} collective-permute-done((bf16[2,16,3200]{2,1,0:T(8,128)(2,1)S(1)}, bf16[2,16,3200]{2,1,0:T(8,128)(2,1)S(1)}, u32[]{:S(2)}, u32[]{:S(2)}) %collective-permute-start.12) | collective-permute-done | bytes 204832 | tf_op jit(solution)/shard_map/ppermute | solution.py:425
  48.9 5.7 %collective-permute-done.13.refs_0_ = bf16[2,16,3200]{2,1,0:T(8,128)(2,1)S(1)} collective-permute-done((bf16[2,16,3200]{2,1,0:T(8,128)(2,1)S(1)}, bf16[2,16,3200]{2,1,0:T(8,128)(2,1)S(1)}, u32[]{:S(2)}, u32[]{:S(2)}) %collective-permute-start.13) | collective-permute-done | bytes 204832 | tf_op jit(solution)/shard_map/ppermute | solution.py:425
  54.8 5.7 %collective-permute-done.14.both_ref.refs_3_ = bf16[2,16,3200]{2,1,0:T(8,128)(2,1)S(1)} collective-permute-done((bf16[2,16,3200]{2,1,0:T(8,128)(2,1)S(1)}, bf16[2,16,3200]{2,1,0:T(8,128)(2,1)S(1)}, u32[]{:S(2)}, u32[]{:S(2)}) %collective-permute-start.14) | collective-permute-done | bytes 204832 | tf_op jit(solution)/shard_map/ppermute | solution.py:425
  60.7 1.3 %collective-permute-done.15.refs_4_ = bf16[16,3200]{1,0:T(8,128)(2,1)S(1)} collective-permute-done((bf16[16,3200]{1,0:T(8,128)(2,1)S(1)}, bf16[16,3200]{1,0:T(8,128)(2,1)S(1)}, u32[]{:S(2)}, u32[]{:S(2)}) %collective-permute-start.15) | collective-permute-done | bytes 102432 | tf_op jit(solution)/shard_map/ppermute | solution.py:416
  62.0 1.4 %shard_map.102 = (f32[3,32,512]{2,1,0:T(8,128)}, f32[3,32,512]{2,1,0:T(8,128)S(1)}, f32[3,32,512]{2,1,0:T(8,128)S(1)}, bf16[16,3200]{1,0:T(8,128)(2,1)S(1)}, f32[8,128]{1,0:T(8,128)S(1)}) custom-call(f32[1]{0:T(128)} %get-tuple-element.46.scale_ref.refs_10_, bf16[3,32,512]{2,1,0:T(8,128)(2,1)S(1)} %copy-done.1, bf16[3,32,512]{2,1,0:T(8,128)(2,1)S(1)} %copy-done.3, ...), custom_call_target="tpu_custom_call" | custom-call | tf_op jit(solution)/shard_map/pallas_call | solution.py:374
  63.5 1.1 collective-permute-done.17.two_ref.refs_5_
  64.6 3.5 %collective-permute-done.16.one_ref.refs_1_ = bf16[16,3200]{1,0:T(8,128)(2,1)S(1)} collective-permute-done((bf16[16,3200]{1,0:T(8,128)(2,1)S(1)}, bf16[16,3200]{1,0:T(8,128)(2,1)S(1)}, u32[]{:S(2)}, u32[]{:S(2)}) %collective-permute-start.16) | collective-permute-done | bytes 102432 | tf_op jit(solution)/shard_map/ppermute | solution.py:425
  68.2 5.7 %collective-permute-done.18.refs_2_ = bf16[2,16,3200]{2,1,0:T(8,128)(2,1)S(1)} collective-permute-done((bf16[2,16,3200]{2,1,0:T(8,128)(2,1)S(1)}, bf16[2,16,3200]{2,1,0:T(8,128)(2,1)S(1)}, u32[]{:S(2)}, u32[]{:S(2)}) %collective-permute-start.18) | collective-permute-done | bytes 204832 | tf_op jit(solution)/shard_map/ppermute | solution.py:425
  74.0 5.8 %collective-permute-done.19.refs_3_ = bf16[2,16,3200]{2,1,0:T(8,128)(2,1)S(1)} collective-permute-done((bf16[2,16,3200]{2,1,0:T(8,128)(2,1)S(1)}, bf16[2,16,3200]{2,1,0:T(8,128)(2,1)S(1)}, u32[]{:S(2)}, u32[]{:S(2)}) %collective-permute-start.19) | collective-permute-done | bytes 204832 | tf_op jit(solution)/shard_map/ppermute | solution.py:425
  80.3 5.2 %collective-permute-done.20.refs_4_ = bf16[2,16,3200]{2,1,0:T(8,128)(2,1)S(1)} collective-permute-done((bf16[2,16,3200]{2,1,0:T(8,128)(2,1)S(1)}, bf16[2,16,3200]{2,1,0:T(8,128)(2,1)S(1)}, u32[]{:S(2)}, u32[]{:S(2)}) %collective-permute-start.20) | collective-permute-done | bytes 204832 | tf_op jit(solution)/shard_map/ppermute | solution.py:425
  86.0 1.1 collective-permute-done.21.refs_6_
  87.1 9.3 %shard_map.104 = (f32[8,3,32,512]{3,2,1,0:T(8,128)S(1)}, bf16[1,16,3200]{2,1,0:T(8,128)(2,1)S(1)}, bf16[7,16,3200]{2,1,0:T(8,128)(2,1)S(1)}, f32[8,128]{1,0:T(8,128)S(1)}, f32[1]{0:T(128)}) custom-call(s32[1]{0:T(128)} %bitcast.me_ref, bf16[16,3200]{1,0:T(8,128)(2,1)S(1)} %get-tuple-element.54.refs_0_, ...), custom_call_target="tpu_custom_call" | custom-call | flops 4294967296 | bytes 8388608 | tf_op jit(solution)/shard_map/pallas_call | solution.py:208
  96.4 1.0 collective-permute-start.25
  98.8 4.6 %collective-permute-done.27.refs_0_ = bf16[1,16,3200]{2,1,0:T(8,128)(2,1)S(1)} collective-permute-done((bf16[1,16,3200]{2,1,0:T(8,128)(2,1)S(1)}, bf16[1,16,3200]{2,1,0:T(8,128)(2,1)S(1)}, u32[]{:S(2)}, u32[]{:S(2)}) %collective-permute-start.27) | collective-permute-done | bytes 102432 | tf_op jit(solution)/shard_map/ppermute | solution.py:425
  103.6 5.7 %collective-permute-done.28.refs_0_ = bf16[2,16,3200]{2,1,0:T(8,128)(2,1)S(1)} collective-permute-done((bf16[2,16,3200]{2,1,0:T(8,128)(2,1)S(1)}, bf16[2,16,3200]{2,1,0:T(8,128)(2,1)S(1)}, u32[]{:S(2)}, u32[]{:S(2)}) %collective-permute-start.28) | collective-permute-done | bytes 204832 | tf_op jit(solution)/shard_map/ppermute | solution.py:425
  109.5 5.7 %collective-permute-done.29.refs_0_ = bf16[2,16,3200]{2,1,0:T(8,128)(2,1)S(1)} collective-permute-done((bf16[2,16,3200]{2,1,0:T(8,128)(2,1)S(1)}, bf16[2,16,3200]{2,1,0:T(8,128)(2,1)S(1)}, u32[]{:S(2)}, u32[]{:S(2)}) %collective-permute-start.29) | collective-permute-done | bytes 204832 | tf_op jit(solution)/shard_map/ppermute | solution.py:425
  115.4 5.7 %collective-permute-done.30.both_ref.refs_3_ = bf16[2,16,3200]{2,1,0:T(8,128)(2,1)S(1)} collective-permute-done((bf16[2,16,3200]{2,1,0:T(8,128)(2,1)S(1)}, bf16[2,16,3200]{2,1,0:T(8,128)(2,1)S(1)}, u32[]{:S(2)}, u32[]{:S(2)}) %collective-permute-start.30) | collective-permute-done | bytes 204832 | tf_op jit(solution)/shard_map/ppermute | solution.py:425
  121.3 1.3 %collective-permute-done.31.refs_4_ = bf16[16,3200]{1,0:T(8,128)(2,1)S(1)} collective-permute-done((bf16[16,3200]{1,0:T(8,128)(2,1)S(1)}, bf16[16,3200]{1,0:T(8,128)(2,1)S(1)}, u32[]{:S(2)}, u32[]{:S(2)}) %collective-permute-start.31) | collective-permute-done | bytes 102432 | tf_op jit(solution)/shard_map/ppermute | solution.py:416
  122.6 2.2 %shard_map.110 = (f32[3,32,512]{2,1,0:T(8,128)}, f32[3,32,512]{2,1,0:T(8,128)}) custom-call(f32[1]{0:T(128)} %get-tuple-element.57.along_ref, f32[1]{0:T(128)} %get-tuple-element.46.scale_ref.refs_10_, bf16[3,32,512]{2,1,0:T(8,128)(2,1)S(1)} %copy-done.1, bf16[3,32,512]{2,1,0:T(8,128)(2,1)S(1)} %copy-done.3, f32[3,32,512]{2,1,0:T(8,128)S(1)} %get-tuple-element.58.terms_ref, ...), custom_call_target="tpu_custom_call" | custom-call | tf_op jit(solution)/shard_map/pallas_call | solution.py:406
  (61 shorter events, 8.8 us)
Async XLA Ops:
  0.6 3.2 %collective-permute-start.1 = (bf16[3,32,512]{2,1,0:T(8,128)(2,1)}, bf16[3,32,512]{2,1,0:T(8,128)(2,1)S(1)}, u32[]{:S(2)}, u32[]{:S(2)}) collective-permute-start(bf16[3,32,512]{2,1,0:T(8,128)(2,1)} %wave_ref.5), channel_id=1, source_target_pairs={{0,1},{1,0},{2,3},{3,2},{4,5},{5,4},{6,7},{7,6},{8,9},{9,8},{10,11... | collective-permute-start | bytes 294920 | tf_op jit(solution)/shard_map/ppermute | solution.py:416
  1.1 5.4 %collective-permute-start = (bf16[3,32,512]{2,1,0:T(8,128)(2,1)}, bf16[3,32,512]{2,1,0:T(8,128)(2,1)S(1)}, u32[]{:S(2)}, u32[]{:S(2)}) collective-permute-start(bf16[3,32,512]{2,1,0:T(8,128)(2,1)} %wave_ref.5), channel_id=1, source_target_pairs={{0,4},{1,3},{4,8},{5,1},{8,12},{9,5},{12,14},{13,9},{14,10},{15,13... | collective-permute-start | bytes 294920 | tf_op jit(solution)/shard_map/ppermute | solution.py:425
  6.6 5.7 %collective-permute-start.2 = (bf16[2,3,32,512]{3,2,1,0:T(8,128)(2,1)S(1)}, bf16[2,3,32,512]{3,2,1,0:T(8,128)(2,1)S(1)}, u32[]{:S(2)}, u32[]{:S(2)}) collective-permute-start(bf16[2,3,32,512]{3,2,1,0:T(8,128)(2,1)S(1)} %shard_map.94.refs_3_), channel_id=1, source_target_pairs={{0,4},{1,3},{4,8},{5,1},{8,12},{9,5},{12,14},{13,9},{14,10},{15,13... | collective-permute-start | bytes 589832 | tf_op jit(solution)/shard_map/ppermute | solution.py:425
  12.3 7.0 %collective-permute-start.3 = (bf16[2,3,32,512]{3,2,1,0:T(8,128)(2,1)S(1)}, bf16[2,3,32,512]{3,2,1,0:T(8,128)(2,1)S(1)}, u32[]{:S(2)}, u32[]{:S(2)}) collective-permute-start(bf16[2,3,32,512]{3,2,1,0:T(8,128)(2,1)S(1)} %collective-permute-done.2.refs_2_), channel_id=1, source_target_pairs={{0,4},{1,3},{4,8},{5,1},{8,12},{9,5},{12,14},{13,9},{14,10},{15,13... | collective-permute-start | bytes 589832 | tf_op jit(solution)/shard_map/ppermute | solution.py:425
  19.3 5.7 %collective-permute-start.4 = (bf16[2,3,32,512]{3,2,1,0:T(8,128)(2,1)S(1)}, bf16[2,3,32,512]{3,2,1,0:T(8,128)(2,1)S(1)}, u32[]{:S(2)}, u32[]{:S(2)}) collective-permute-start(bf16[2,3,32,512]{3,2,1,0:T(8,128)(2,1)S(1)} %collective-permute-done.3.refs_3_), channel_id=1, source_target_pairs={{0,4},{1,3},{4,8},{5,1},{8,12},{9,5},{12,14},{13,9},{14,10},{15,13... | collective-permute-start | bytes 589832 | tf_op jit(solution)/shard_map/ppermute | solution.py:425
  20.9 5.7 %collective-permute-start.6 = (bf16[2,3,32,512]{3,2,1,0:T(8,128)(2,1)S(1)}, bf16[2,3,32,512]{3,2,1,0:T(8,128)(2,1)S(1)}, u32[]{:S(2)}, u32[]{:S(2)}) collective-permute-start(bf16[2,3,32,512]{3,2,1,0:T(8,128)(2,1)S(1)} %collective-permute-done.2.refs_2_), channel_id=1, source_target_pairs={{0,1},{1,0},{2,3},{3,2},{4,5},{5,4},{6,7},{7,6},{8,9},{9,8},{10,11... | collective-permute-start | bytes 589832 | tf_op jit(solution)/shard_map/ppermute | solution.py:416
  20.9 5.7 %collective-permute-start.7 = (bf16[2,3,32,512]{3,2,1,0:T(8,128)(2,1)S(1)}, bf16[2,3,32,512]{3,2,1,0:T(8,128)(2,1)S(1)}, u32[]{:S(2)}, u32[]{:S(2)}) collective-permute-start(bf16[2,3,32,512]{3,2,1,0:T(8,128)(2,1)S(1)} %collective-permute-done.3.refs_3_), channel_id=1, source_target_pairs={{0,1},{1,0},{2,3},{3,2},{4,5},{5,4},{6,7},{7,6},{8,9},{9,8},{10,11... | collective-permute-start | bytes 589832 | tf_op jit(solution)/shard_map/ppermute | solution.py:416
  25.0 1.6 %collective-permute-start.8 = (bf16[2,3,32,512]{3,2,1,0:T(8,128)(2,1)S(1)}, bf16[2,3,32,512]{3,2,1,0:T(8,128)(2,1)S(1)}, u32[]{:S(2)}, u32[]{:S(2)}) collective-permute-start(bf16[2,3,32,512]{3,2,1,0:T(8,128)(2,1)S(1)} %collective-permute-done.4.refs_4_), channel_id=1, source_target_pairs={{0,1},{1,0},{2,3},{3,2},{4,5},{5,4},{6,7},{7,6},{8,9},{9,8},{10,11... | collective-permute-start | bytes 589832 | tf_op jit(solution)/shard_map/ppermute | solution.py:416
  25.0 1.6 %collective-permute-start.5 = (bf16[3,32,512]{2,1,0:T(8,128)(2,1)S(1)}, bf16[3,32,512]{2,1,0:T(8,128)(2,1)S(1)}, u32[]{:S(2)}, u32[]{:S(2)}) collective-permute-start(bf16[3,32,512]{2,1,0:T(8,128)(2,1)S(1)} %collective-permute-done.one_ref.refs_1_), channel_id=1, source_target_pairs={{0,1},{1,0},{2,3},{3,2},{4,5},{5,4},{6,7},{7,6},{8,9},{9,8},{10,11... | collective-permute-start | bytes 294920 | tf_op jit(solution)/shard_map/ppermute | solution.py:416
  35.8 2.0 %collective-permute-start.9 = (bf16[1,16,3200]{2,1,0:T(8,128)(2,1)S(1)}, bf16[1,16,3200]{2,1,0:T(8,128)(2,1)S(1)}, u32[]{:S(2)}, u32[]{:S(2)}) collective-permute-start(bf16[1,16,3200]{2,1,0:T(8,128)(2,1)S(1)} %get-tuple-element.48), channel_id=1, source_target_pairs={{0,1},{1,0},{2,3},{3,2},{4,5},{5,4},{6,7},{7,6},{8,9},{9,8},{10,11... | collective-permute-start | bytes 307208 | tf_op jit(solution)/shard_map/ppermute | solution.py:416
  37.7 5.1 %collective-permute-start.10 = (bf16[7,16,3200]{2,1,0:T(8,128)(2,1)S(1)}, bf16[7,16,3200]{2,1,0:T(8,128)(2,1)S(1)}, u32[]{:S(2)}, u32[]{:S(2)}) collective-permute-start(bf16[7,16,3200]{2,1,0:T(8,128)(2,1)S(1)} %get-tuple-element.50), channel_id=1, source_target_pairs={{0,1},{1,0},{2,3},{3,2},{4,5},{5,4},{6,7},{7,6},{8,9},{9,8},{10,11... | collective-permute-start | bytes 2150408 | tf_op jit(solution)/shard_map/ppermute | solution.py:416
  38.1 4.7 %collective-permute-start.11 = (bf16[1,16,3200]{2,1,0:T(8,128)(2,1)S(1)}, bf16[1,16,3200]{2,1,0:T(8,128)(2,1)S(1)}, u32[]{:S(2)}, u32[]{:S(2)}) collective-permute-start(bf16[1,16,3200]{2,1,0:T(8,128)(2,1)S(1)} %shard_map.97), channel_id=1, source_target_pairs={{0,4},{1,3},{4,8},{5,1},{8,12},{9,5},{12,14},{13,9},{14,10},{15,13... | collective-permute-start | bytes 307208 | tf_op jit(solution)/shard_map/ppermute | solution.py:425
  42.9 5.8 %collective-permute-start.12 = (bf16[2,16,3200]{2,1,0:T(8,128)(2,1)S(1)}, bf16[2,16,3200]{2,1,0:T(8,128)(2,1)S(1)}, u32[]{:S(2)}, u32[]{:S(2)}) collective-permute-start(bf16[2,16,3200]{2,1,0:T(8,128)(2,1)S(1)} %shard_map.98), channel_id=1, source_target_pairs={{0,4},{1,3},{4,8},{5,1},{8,12},{9,5},{12,14},{13,9},{14,10},{15,13... | collective-permute-start | bytes 614408 | tf_op jit(solution)/shard_map/ppermute | solution.py:425
  48.9 5.8 %collective-permute-start.13 = (bf16[2,16,3200]{2,1,0:T(8,128)(2,1)S(1)}, bf16[2,16,3200]{2,1,0:T(8,128)(2,1)S(1)}, u32[]{:S(2)}, u32[]{:S(2)}) collective-permute-start(bf16[2,16,3200]{2,1,0:T(8,128)(2,1)S(1)} %shard_map.99), channel_id=1, source_target_pairs={{0,4},{1,3},{4,8},{5,1},{8,12},{9,5},{12,14},{13,9},{14,10},{15,13... | collective-permute-start | bytes 614408 | tf_op jit(solution)/shard_map/ppermute | solution.py:425
  54.8 5.8 %collective-permute-start.14 = (bf16[2,16,3200]{2,1,0:T(8,128)(2,1)S(1)}, bf16[2,16,3200]{2,1,0:T(8,128)(2,1)S(1)}, u32[]{:S(2)}, u32[]{:S(2)}) collective-permute-start(bf16[2,16,3200]{2,1,0:T(8,128)(2,1)S(1)} %shard_map.100), channel_id=1, source_target_pairs={{0,4},{1,3},{4,8},{5,1},{8,12},{9,5},{12,14},{13,9},{14,10},{15,13... | collective-permute-start | bytes 614408 | tf_op jit(solution)/shard_map/ppermute | solution.py:425
  60.6 1.4 %collective-permute-start.15 = (bf16[16,3200]{1,0:T(8,128)(2,1)S(1)}, bf16[16,3200]{1,0:T(8,128)(2,1)S(1)}, u32[]{:S(2)}, u32[]{:S(2)}) collective-permute-start(bf16[16,3200]{1,0:T(8,128)(2,1)S(1)} %shard_map.101), channel_id=1, source_target_pairs={{0,1},{1,0},{2,3},{3,2},{4,5},{5,4},{6,7},{7,6},{8,9},{9,8},{10,11... | collective-permute-start | bytes 307208 | tf_op jit(solution)/shard_map/ppermute | solution.py:416
  63.3 1.3 %collective-permute-start.17 = (bf16[16,3200]{1,0:T(8,128)(2,1)S(1)}, bf16[16,3200]{1,0:T(8,128)(2,1)S(1)}, u32[]{:S(2)}, u32[]{:S(2)}) collective-permute-start(bf16[16,3200]{1,0:T(8,128)(2,1)S(1)} %get-tuple-element.54.refs_0_), channel_id=1, source_target_pairs={{0,1},{1,0},{2,3},{3,2},{4,5},{5,4},{6,7},{7,6},{8,9},{9,8},{10,11... | collective-permute-start | bytes 307208 | tf_op jit(solution)/shard_map/ppermute | solution.py:416
  63.5 4.7 %collective-permute-start.16 = (bf16[16,3200]{1,0:T(8,128)(2,1)S(1)}, bf16[16,3200]{1,0:T(8,128)(2,1)S(1)}, u32[]{:S(2)}, u32[]{:S(2)}) collective-permute-start(bf16[16,3200]{1,0:T(8,128)(2,1)S(1)} %get-tuple-element.54.refs_0_), channel_id=1, source_target_pairs={{0,4},{1,3},{4,8},{5,1},{8,12},{9,5},{12,14},{13,9},{14,10},{15,13... | collective-permute-start | bytes 307208 | tf_op jit(solution)/shard_map/ppermute | solution.py:425
  68.2 5.8 %collective-permute-start.18 = (bf16[2,16,3200]{2,1,0:T(8,128)(2,1)S(1)}, bf16[2,16,3200]{2,1,0:T(8,128)(2,1)S(1)}, u32[]{:S(2)}, u32[]{:S(2)}) collective-permute-start(bf16[2,16,3200]{2,1,0:T(8,128)(2,1)S(1)} %shard_map.103), channel_id=1, source_target_pairs={{0,4},{1,3},{4,8},{5,1},{8,12},{9,5},{12,14},{13,9},{14,10},{15,13... | collective-permute-start | bytes 614408 | tf_op jit(solution)/shard_map/ppermute | solution.py:425
  74.0 5.8 %collective-permute-start.19 = (bf16[2,16,3200]{2,1,0:T(8,128)(2,1)S(1)}, bf16[2,16,3200]{2,1,0:T(8,128)(2,1)S(1)}, u32[]{:S(2)}, u32[]{:S(2)}) collective-permute-start(bf16[2,16,3200]{2,1,0:T(8,128)(2,1)S(1)} %collective-permute-done.18.refs_2_), channel_id=1, source_target_pairs={{0,4},{1,3},{4,8},{5,1},{8,12},{9,5},{12,14},{13,9},{14,10},{15,13... | collective-permute-start | bytes 614408 | tf_op jit(solution)/shard_map/ppermute | solution.py:425
  79.7 5.8 %collective-permute-start.20 = (bf16[2,16,3200]{2,1,0:T(8,128)(2,1)S(1)}, bf16[2,16,3200]{2,1,0:T(8,128)(2,1)S(1)}, u32[]{:S(2)}, u32[]{:S(2)}) collective-permute-start(bf16[2,16,3200]{2,1,0:T(8,128)(2,1)S(1)} %collective-permute-done.19.refs_3_), channel_id=1, source_target_pairs={{0,4},{1,3},{4,8},{5,1},{8,12},{9,5},{12,14},{13,9},{14,10},{15,13... | collective-permute-start | bytes 614408 | tf_op jit(solution)/shard_map/ppermute | solution.py:425
  79.7 7.4 %collective-permute-start.22 = (bf16[2,16,3200]{2,1,0:T(8,128)(2,1)S(1)}, bf16[2,16,3200]{2,1,0:T(8,128)(2,1)S(1)}, u32[]{:S(2)}, u32[]{:S(2)}) collective-permute-start(bf16[2,16,3200]{2,1,0:T(8,128)(2,1)S(1)} %collective-permute-done.18.refs_2_), channel_id=1, source_target_pairs={{0,1},{1,0},{2,3},{3,2},{4,5},{5,4},{6,7},{7,6},{8,9},{9,8},{10,11... | collective-permute-start | bytes 614408 | tf_op jit(solution)/shard_map/ppermute | solution.py:416
  79.8 7.4 %collective-permute-start.23 = (bf16[2,16,3200]{2,1,0:T(8,128)(2,1)S(1)}, bf16[2,16,3200]{2,1,0:T(8,128)(2,1)S(1)}, u32[]{:S(2)}, u32[]{:S(2)}) collective-permute-start(bf16[2,16,3200]{2,1,0:T(8,128)(2,1)S(1)} %collective-permute-done.19.refs_3_), channel_id=1, source_target_pairs={{0,1},{1,0},{2,3},{3,2},{4,5},{5,4},{6,7},{7,6},{8,9},{9,8},{10,11... | collective-permute-start | bytes 614408 | tf_op jit(solution)/shard_map/ppermute | solution.py:416
  85.5 1.6 %collective-permute-start.24 = (bf16[2,16,3200]{2,1,0:T(8,128)(2,1)S(1)}, bf16[2,16,3200]{2,1,0:T(8,128)(2,1)S(1)}, u32[]{:S(2)}, u32[]{:S(2)}) collective-permute-start(bf16[2,16,3200]{2,1,0:T(8,128)(2,1)S(1)} %collective-permute-done.20.refs_4_), channel_id=1, source_target_pairs={{0,1},{1,0},{2,3},{3,2},{4,5},{5,4},{6,7},{7,6},{8,9},{9,8},{10,11... | collective-permute-start | bytes 614408 | tf_op jit(solution)/shard_map/ppermute | solution.py:416
  85.5 1.6 %collective-permute-start.21 = (bf16[16,3200]{1,0:T(8,128)(2,1)S(1)}, bf16[16,3200]{1,0:T(8,128)(2,1)S(1)}, u32[]{:S(2)}, u32[]{:S(2)}) collective-permute-start(bf16[16,3200]{1,0:T(8,128)(2,1)S(1)} %collective-permute-done.16.one_ref.refs_1_), channel_id=1, source_target_pairs={{0,1},{1,0},{2,3},{3,2},{4,5},{5,4},{6,7},{7,6},{8,9},{9,8},{10,11... | collective-permute-start | bytes 307208 | tf_op jit(solution)/shard_map/ppermute | solution.py:416
  96.4 1.9 %collective-permute-start.25 = (bf16[1,16,3200]{2,1,0:T(8,128)(2,1)S(1)}, bf16[1,16,3200]{2,1,0:T(8,128)(2,1)S(1)}, u32[]{:S(2)}, u32[]{:S(2)}) collective-permute-start(bf16[1,16,3200]{2,1,0:T(8,128)(2,1)S(1)} %get-tuple-element.60), channel_id=1, source_target_pairs={{0,1},{1,0},{2,3},{3,2},{4,5},{5,4},{6,7},{7,6},{8,9},{9,8},{10,11... | collective-permute-start | bytes 307208 | tf_op jit(solution)/shard_map/ppermute | solution.py:416
  98.4 5.1 %collective-permute-start.26 = (bf16[7,16,3200]{2,1,0:T(8,128)(2,1)S(1)}, bf16[7,16,3200]{2,1,0:T(8,128)(2,1)S(1)}, u32[]{:S(2)}, u32[]{:S(2)}) collective-permute-start(bf16[7,16,3200]{2,1,0:T(8,128)(2,1)S(1)} %get-tuple-element.62), channel_id=1, source_target_pairs={{0,1},{1,0},{2,3},{3,2},{4,5},{5,4},{6,7},{7,6},{8,9},{9,8},{10,11... | collective-permute-start | bytes 2150408 | tf_op jit(solution)/shard_map/ppermute | solution.py:416
  98.8 4.7 %collective-permute-start.27 = (bf16[1,16,3200]{2,1,0:T(8,128)(2,1)S(1)}, bf16[1,16,3200]{2,1,0:T(8,128)(2,1)S(1)}, u32[]{:S(2)}, u32[]{:S(2)}) collective-permute-start(bf16[1,16,3200]{2,1,0:T(8,128)(2,1)S(1)} %shard_map.105), channel_id=1, source_target_pairs={{0,4},{1,3},{4,8},{5,1},{8,12},{9,5},{12,14},{13,9},{14,10},{15,13... | collective-permute-start | bytes 307208 | tf_op jit(solution)/shard_map/ppermute | solution.py:425
  103.6 5.8 %collective-permute-start.28 = (bf16[2,16,3200]{2,1,0:T(8,128)(2,1)S(1)}, bf16[2,16,3200]{2,1,0:T(8,128)(2,1)S(1)}, u32[]{:S(2)}, u32[]{:S(2)}) collective-permute-start(bf16[2,16,3200]{2,1,0:T(8,128)(2,1)S(1)} %shard_map.106), channel_id=1, source_target_pairs={{0,4},{1,3},{4,8},{5,1},{8,12},{9,5},{12,14},{13,9},{14,10},{15,13... | collective-permute-start | bytes 614408 | tf_op jit(solution)/shard_map/ppermute | solution.py:425
  109.5 5.8 %collective-permute-start.29 = (bf16[2,16,3200]{2,1,0:T(8,128)(2,1)S(1)}, bf16[2,16,3200]{2,1,0:T(8,128)(2,1)S(1)}, u32[]{:S(2)}, u32[]{:S(2)}) collective-permute-start(bf16[2,16,3200]{2,1,0:T(8,128)(2,1)S(1)} %shard_map.107), channel_id=1, source_target_pairs={{0,4},{1,3},{4,8},{5,1},{8,12},{9,5},{12,14},{13,9},{14,10},{15,13... | collective-permute-start | bytes 614408 | tf_op jit(solution)/shard_map/ppermute | solution.py:425
  115.4 5.8 %collective-permute-start.30 = (bf16[2,16,3200]{2,1,0:T(8,128)(2,1)S(1)}, bf16[2,16,3200]{2,1,0:T(8,128)(2,1)S(1)}, u32[]{:S(2)}, u32[]{:S(2)}) collective-permute-start(bf16[2,16,3200]{2,1,0:T(8,128)(2,1)S(1)} %shard_map.108), channel_id=1, source_target_pairs={{0,4},{1,3},{4,8},{5,1},{8,12},{9,5},{12,14},{13,9},{14,10},{15,13... | collective-permute-start | bytes 614408 | tf_op jit(solution)/shard_map/ppermute | solution.py:425
  121.2 1.4 %collective-permute-start.31 = (bf16[16,3200]{1,0:T(8,128)(2,1)S(1)}, bf16[16,3200]{1,0:T(8,128)(2,1)S(1)}, u32[]{:S(2)}, u32[]{:S(2)}) collective-permute-start(bf16[16,3200]{1,0:T(8,128)(2,1)S(1)} %shard_map.109), channel_id=1, source_target_pairs={{0,1},{1,0},{2,3},{3,2},{4,5},{5,4},{6,7},{7,6},{8,9},{9,8},{10,11... | collective-permute-start | bytes 307208 | tf_op jit(solution)/shard_map/ppermute | solution.py:416
  (6 other events, 50.7 us)

commit v5 on v4

--- a/solution.py
+++ b/solution.py
@@ -26,7 +26,17 @@
 
 
 def message_shape(sectors, rows, width):
-    return (HALF, sectors * (rows // HALF) * width + LANES)
+    return (HALF, rows // HALF * sectors * width + LANES)
+
+
+def quarter_shapes(sectors, width):
+    return (HALF, sectors * width + LANES), (HALF, sectors * width)
+
+
+def lanes_at(ref):
+    lanes = ref.shape[1] - LANES
+    first = lanes if lanes % 1024 else lanes // 2
+    return slice(first, first + LANES)
 
 
 def write_lanes(ref, lanes):
@@ -37,18 +47,23 @@
     low = rest - middle
     row = lax.broadcasted_iota(jnp.int32, whole.shape, 0)
     value = jnp.where(row == 0, high, jnp.where(row == 1, middle, jnp.where(row == 2, low, 0.0)))
-    ref[:, ref.shape[1] - LANES :] = value.astype(jnp.bfloat16)
+    ref[:, lanes_at(ref)] = value.astype(jnp.bfloat16)
 
 
 def read_lanes(ref):
-    return jnp.sum(ref[:, ref.shape[1] - LANES :].astype(jnp.float32), axis=0, keepdims=True)
+    return jnp.sum(ref[:, lanes_at(ref)].astype(jnp.float32), axis=0, keepdims=True)
 
 
 def message_parts(sectors, rows, width):
+    for h in range(rows // HALF):
+        for s in range(sectors):
+            at = (h * sectors + s) * width + (LANES if h else 0)
+            yield s, h * HALF, slice(at, at + width)
+
+
+def quarter_parts(sectors, width):
     for s in range(sectors):
-        for h in range(rows // HALF):
-            at = (s * (rows // HALF) + h) * width
-            yield s, h * HALF, slice(at, at + width)
+        yield s, slice(s * width, (s + 1) * width)
 
 
 def chip_at(place):
@@ -85,17 +100,13 @@
     return devices
 
 
-def is_pair(ref, raw):
-    return len(ref.shape) == (4 if raw else 3)
-
-
 def blocks_kernel(first, direct, rows, entries, me_ref, *refs):
     n_field = 10 if direct else 1
     field_refs, refs = refs[:n_field], refs[n_field:]
     if direct:
         views = []
         for ref in field_refs:
-            views += [ref.at[k] for k in range(ref.shape[0])] if is_pair(ref, first) else [ref]
+            views += [ref.at[k] for k in range(ref.shape[0])] if len(ref.shape) == 3 else [ref]
         field_refs = views
     if first:
         square_ref, *refs = refs
@@ -122,12 +133,12 @@
     owners = gathered_devices(me) if direct else [0]
     for ref, owner in zip(field_refs, owners):
         at = pl.multiple_of(owner * rows, rows) if direct else 0
-        if direct and not first:
+        if direct:
             for s, row, lanes in message_parts(sectors, rows, width):
                 pieces.append((ref, (slice(None), lanes), s, pl.ds(at + row, HALF)))
         else:
             for s in range(sectors):
-                pieces.append((ref, (s,), s, pl.ds(at, rows if direct else field.shape[1])))
+                pieces.append((ref, (s,), s, pl.ds(at, field.shape[1])))
 
     total[...] = jnp.zeros_like(total)
     dot = jnp.zeros((8, 128), jnp.float32)
@@ -137,8 +148,9 @@
             dot += fold(value * value)
         scale = jnp.sqrt(jnp.sum(dot) / entries)
         out_ref[0] = scale
+        inverse = 1.0 / scale
         for ref, part, s, place in pieces:
-            field[s, place, :] = (ref[part].astype(jnp.float32) / scale).astype(jnp.bfloat16)
+            field[s, place, :] = (ref[part].astype(jnp.float32) * inverse).astype(jnp.bfloat16)
     else:
         for ref, part, s, place in pieces:
             field[s, place, :] = ref[part]
@@ -194,12 +206,11 @@
         write_lanes(ref, lanes)
 
 
-def apply_blocks(me, fields, own, blocks, first, entries):
+def apply_blocks(me, fields, own, blocks, shape, first, entries):
     left, right, *ints = blocks
     slots, order, width = left.shape
     direct = len(fields) == 10
-    sectors = fields[0].shape[0] if first or not direct else own[1].shape[0]
-    rows = fields[0].shape[1] if first else own[1].shape[1]
+    sectors, rows, _ = shape
     if direct:
         kept, message = (8, sectors, rows, width), message_shape(sectors, rows, width)
     else:
@@ -233,66 +244,98 @@
     )(me, *fields, *own, *ints, left, right)
 
 
-def chain_kernel(links, keep_ref, other_ref, dot_ref, *refs):
+def chain_kernel(k, other, h, keep_ref, other_ref, dot_ref, *refs):
     *arrived_refs, out_ref = refs
     sectors, rows, width = keep_ref.shape[1:]
-    for place, (k, other, arrived) in enumerate(links):
-        arrived_ref = arrived_refs[0].at[place] if arrived else None
-        for s, row, part in message_parts(sectors, rows, width):
-            value = keep_ref[k, s, row : row + HALF, :]
-            value += other_ref[other, :, part].astype(jnp.float32)
-            if arrived:
-                value += arrived_ref[:, part].astype(jnp.float32)
-            out_ref[place, :, part] = value.astype(jnp.bfloat16)
+    places = [p for p in message_parts(sectors, rows, width) if p[1] == h * HALF]
+    for (s, row, part), (_, lanes) in zip(places, quarter_parts(sectors, width)):
+        value = keep_ref[k, s, row : row + HALF, :]
+        value += other_ref[other, :, part].astype(jnp.float32)
+        for ref in arrived_refs:
+            value += ref[:, lanes].astype(jnp.float32)
+        out_ref[:, lanes] = value.astype(jnp.bfloat16)
+    if h == 0:
         lanes = jnp.sum(dot_ref[...], axis=0, keepdims=True) + read_lanes(other_ref.at[other])
-        if arrived:
-            lanes += read_lanes(arrived_ref)
-        write_lanes(out_ref.at[place], lanes)
-
-
-def chain(links, keep, other, dot, *arrived):
-    return pl.pallas_call(
-        functools.partial(chain_kernel, links),
+        for ref in arrived_refs:
+            lanes += read_lanes(ref)
+        write_lanes(out_ref, lanes)
+
+
+def chain(k, other, h, keep, terms, dot, *arrived):
+    sectors, _, width = keep.shape[1:]
+    return pl.pallas_call(
+        functools.partial(chain_kernel, k, other, h),
         in_specs=[VMEM] * (3 + len(arrived)),
         out_specs=VMEM,
-        out_shape=jax.ShapeDtypeStruct((len(links), *other.shape[1:]), jnp.bfloat16),
-        compiler_params=PARAMS,
-    )(keep, other, dot, *arrived)
-
-
-def pair_kernel(one_ref, two_ref, out_ref):
-    out_ref[0] = one_ref[...]
-    out_ref[1] = two_ref[...]
-
-
-def pair(one, two):
-    return pl.pallas_call(
-        pair_kernel,
-        in_specs=[VMEM, VMEM],
+        out_shape=jax.ShapeDtypeStruct(quarter_shapes(sectors, width)[h], jnp.bfloat16),
+        compiler_params=PARAMS,
+    )(keep, terms, dot, *arrived)
+
+
+def pack_kernel(*refs):
+    *quarter_refs, out_ref = refs
+    for k in range(len(quarter_refs) // 2):
+        first = quarter_refs[2 * k].shape[1]
+        out_ref[k, :, :first] = quarter_refs[2 * k][...]
+        out_ref[k, :, first:] = quarter_refs[2 * k + 1][...]
+
+
+def pack(*quarters):
+    lanes = quarters[0].shape[1] + quarters[1].shape[1]
+    return pl.pallas_call(
+        pack_kernel,
+        in_specs=[VMEM] * len(quarters),
         out_specs=VMEM,
-        out_shape=jax.ShapeDtypeStruct((2, *one.shape), one.dtype),
-        compiler_params=PARAMS,
-    )(one, two)
-
-
-def second_kernel(both_ref, out_ref):
-    out_ref[...] = both_ref[1]
-
-
-def second(both):
-    return pl.pallas_call(
-        second_kernel,
+        out_shape=jax.ShapeDtypeStruct((len(quarters) // 2, HALF, lanes), jnp.bfloat16),
+        compiler_params=PARAMS,
+    )(*quarters)
+
+
+def split_kernel(whole_ref, one_ref, two_ref):
+    first = one_ref.shape[1]
+    one_ref[...] = whole_ref[:, :first]
+    two_ref[...] = whole_ref[:, first:]
+
+
+def split(whole, sectors, width):
+    return pl.pallas_call(
+        split_kernel,
         in_specs=[VMEM],
-        out_specs=VMEM,
-        out_shape=jax.ShapeDtypeStruct(both.shape[1:], both.dtype),
-        compiler_params=PARAMS,
-    )(both)
+        out_specs=[VMEM] * 2,
+        out_shape=[jax.ShapeDtypeStruct(q, whole.dtype) for q in quarter_shapes(sectors, width)],
+        compiler_params=PARAMS,
+    )(whole)
+
+
+def message_kernel(wave_ref, whole_ref, one_ref, two_ref):
+    sectors, rows, width = wave_ref.shape
+    first = one_ref.shape[1]
+    for s, row, part in message_parts(sectors, rows, width):
+        value = wave_ref[s, row : row + HALF, :]
+        whole_ref[:, part] = value
+        if row == 0:
+            one_ref[:, part] = value
+        else:
+            two_ref[:, part.start - first : part.stop - first] = value
+    for ref in (whole_ref, one_ref):
+        write_lanes(ref, jnp.zeros((1, LANES), jnp.float32))
+
+
+def as_message(wave):
+    sectors, rows, width = wave.shape
+    shapes = (message_shape(sectors, rows, width), *quarter_shapes(sectors, width))
+    return pl.pallas_call(
+        message_kernel,
+        in_specs=[VMEM],
+        out_specs=[VMEM] * 3,
+        out_shape=[jax.ShapeDtypeStruct(q, wave.dtype) for q in shapes],
+        compiler_params=PARAMS,
+    )(wave)
 
 
 def prepare_kernel(wave_ref, diag_ref, *refs):
     (source_ref, target_ref, live_ref, _), outs = refs[:4], refs[4:]
-    own_ref, square_ref, source_out, target_out, live_out = outs
-    own_ref[...] = wave_ref[...]
+    square_ref, source_out, target_out, live_out = outs
     wave = wave_ref[...].astype(jnp.float32)
     square_ref[...] = fold_all(diag_ref[...].astype(jnp.float32) * wave * wave)
     for k in range(source_ref.shape[0]):
@@ -305,9 +348,8 @@
     return pl.pallas_call(
         prepare_kernel,
         in_specs=[VMEM, VMEM, SMEM, SMEM, SMEM, HBM],
-        out_specs=[VMEM, VMEM, SMEM, SMEM, SMEM],
+        out_specs=[VMEM, SMEM, SMEM, SMEM],
         out_shape=[
-            jax.ShapeDtypeStruct(wave.shape, wave.dtype),
             jax.ShapeDtypeStruct((8, 128), jnp.float32),
             *(jax.ShapeDtypeStruct(i.shape, i.dtype) for i in ints),
         ],
@@ -318,15 +360,16 @@
 def own_terms(direct, refs, sector):
     if not direct:
         return refs[0][sector]
-    keep_ref, other_ref, _, ours_ref, theirs_ref = refs
-    own = keep_ref.shape[0] - 1
+    keep_ref, other_ref, _, *arrived_refs = refs
+    own, width = keep_ref.shape[0] - 1, keep_ref.shape[3]
     parts = []
     for s, row, part in message_parts(*keep_ref.shape[1:]):
         if s == sector:
             value = keep_ref[own, s, row : row + HALF, :]
             value += other_ref[other_ref.shape[0] - 1, :, part].astype(jnp.float32)
-            value += ours_ref[0, :, part].astype(jnp.float32)
-            value += theirs_ref[:, part].astype(jnp.float32)
+            lanes = slice(s * width, (s + 1) * width)
+            for ref in arrived_refs[row // HALF :: 2]:
+                value += ref[:, lanes].astype(jnp.float32)
             parts.append(value)
     return jnp.concatenate(parts, axis=0)
 
@@ -334,15 +377,16 @@
 def own_scalar(direct, refs):
     if not direct:
         return jnp.sum(refs[1][...])
-    _, other_ref, dot_ref, ours_ref, theirs_ref = refs
+    _, other_ref, dot_ref, *arrived_refs = refs
     lanes = jnp.sum(dot_ref[...], axis=0, keepdims=True)
     lanes += read_lanes(other_ref.at[other_ref.shape[0] - 1])
-    return jnp.sum(lanes + read_lanes(ours_ref.at[0]) + read_lanes(theirs_ref))
+    return jnp.sum(lanes + sum(read_lanes(ref) for ref in arrived_refs[::2]))
 
 
 def step_kernel(direct, entries, scale_ref, wave_ref, diag_ref, *refs):
-    n_in = 5 if direct else 2
-    ins, (first_ref, terms_ref, correction_ref, rounded_ref, dots_ref) = refs[:n_in], refs[n_in:]
+    n_in = 7 if direct else 2
+    ins, outs = refs[:n_in], refs[n_in:]
+    first_ref, terms_ref, correction_ref, dots_ref, *rounded_refs = outs
     sectors, rows, width = wave_ref.shape
     ritz = own_scalar(direct, ins) / entries
     dots = jnp.zeros((8, 128), jnp.float32)
@@ -359,28 +403,35 @@
         if direct:
             for t, row, part in message_parts(sectors, rows, width):
                 if t == s:
-                    rounded_ref[:, part] = correction[row : row + HALF].astype(jnp.bfloat16)
+                    value = correction[row : row + HALF].astype(jnp.bfloat16)
+                    rounded_refs[0][:, part] = value
+                    lanes = slice(s * width, (s + 1) * width)
+                    rounded_refs[1 + row // HALF][:, lanes] = value
         else:
-            rounded_ref[s] = correction.astype(jnp.bfloat16)
+            rounded_refs[0][s] = correction.astype(jnp.bfloat16)
     dots_ref[...] = dots
     if direct:
-        write_lanes(rounded_ref, jnp.sum(dots, axis=0, keepdims=True))
+        for ref in rounded_refs[:2]:
+            write_lanes(ref, jnp.sum(dots, axis=0, keepdims=True))
 
 
 def davidson_step(scale, wave, diag, ins, entries):
     full = jax.ShapeDtypeStruct(wave.shape, jnp.float32)
-    direct = len(ins) == 5
-    rounded = message_shape(*wave.shape) if direct else wave.shape
+    direct = len(ins) == 7
+    sectors, rows, width = wave.shape
+    rounded = [wave.shape]
+    if direct:
+        rounded = [message_shape(sectors, rows, width), *quarter_shapes(sectors, width)]
     return pl.pallas_call(
         functools.partial(step_kernel, direct, entries),
         in_specs=[SMEM, VMEM, VMEM] + [VMEM] * len(ins),
-        out_specs=[VMEM] * 5,
+        out_specs=[VMEM] * (4 + len(rounded)),
         out_shape=[
             full,
             full,
             full,
-            jax.ShapeDtypeStruct(rounded, jnp.bfloat16),
             jax.ShapeDtypeStruct((8, 128), jnp.float32),
+            *(jax.ShapeDtypeStruct(shape, jnp.bfloat16) for shape in rounded),
         ],
         compiler_params=PARAMS,
     )(scale, wave, diag, *ins)
@@ -404,7 +455,7 @@
 def finish(along, scale, wave, diag, terms, correction, ins, entries):
     full = jax.ShapeDtypeStruct(wave.shape, jnp.float32)
     return pl.pallas_call(
-        functools.partial(finish_kernel, len(ins) == 5, entries),
+        functools.partial(finish_kernel, len(ins) == 7, entries),
         in_specs=[SMEM, SMEM] + [VMEM] * (4 + len(ins)),
         out_specs=[VMEM] * 2,
         out_shape=[full, full],
@@ -426,34 +477,53 @@
 
 
 class RingPlan:
-    def gather(self, own, meanwhile=None):
-        arrived = hop(own)
+    def __init__(self, shape):
+        self.sectors, _, self.width = shape
+
+    def message(self, wave):
+        return as_message(wave)
+
+    def gather(self, message, meanwhile=None):
+        own, *one = message
+        one = [hop(q) for q in one]
         partner = flip(own)
-        both = pair(arrived, partner)
-        beside = None if meanwhile is None else meanwhile(both)
+        two = split(partner, self.sectors, self.width)
+        arrived = pack(*one)
+        beside = None if meanwhile is None else meanwhile(arrived)
         mine, theirs = [own, arrived], [partner, flip(arrived)]
         for step in range(3):
-            both = hop(both)
+            one = [hop(q) for q in one]
+            two = [hop(q) for q in two]
             if step == 1 and beside is not None:
-                both, beside = lax.optimization_barrier((both, beside))
-                mine[0] = beside[0]
-            mine.append(both)
-            theirs.append(flip(both))
+                two[1], beside = lax.optimization_barrier((two[1], beside))
+            arrived = pack(*one, *two)
+            mine.append(arrived)
+            theirs.append(flip(arrived))
         return mine + theirs, beside
 
     def scatter(self, keep, near, far, dot):
         near = flip(near)
         near, far = lax.optimization_barrier((near, far))
         far = flip(far)
-        message = hop(chain(((0, 0, False),), keep, near, dot))
-        message = hop(chain(((1, 0, True), (2, 1, False)), keep, far, dot, message))
-        message = hop(chain(((3, 2, True), (4, 3, True)), keep, far, dot, message))
-        message = hop(chain(((5, 4, True), (6, 5, True)), keep, far, dot, message))
-        return [keep, far, dot, message, flip(second(message))]
+        one = [hop(chain(0, 0, h, keep, near, dot)) for h in (0, 1)]
+        two = []
+        for k in (1, 3, 5):
+            arrived = zip((0, 1), one)
+            one = [hop(chain(k, k - 1, h, keep, far, dot, q)) for h, q in arrived]
+            arrived = zip((0, 1), two) if two else ((0,), (1,))
+            two = [hop(chain(k + 1, k, h, keep, far, dot, *q)) for h, *q in arrived]
+        return [keep, far, dot, *one, *(flip(q) for q in two)]
 
 
 class WholePlan:
-    def gather(self, own, meanwhile=None):
+    def __init__(self, shape):
+        pass
+
+    def message(self, wave):
+        return [wave]
+
+    def gather(self, message, meanwhile=None):
+        (own,) = message
         whole = lax.all_gather(own, "term", axis=1, tiled=True)
         return [whole], None if meanwhile is None else meanwhile(own)
 
@@ -468,22 +538,26 @@
     devices = lax.axis_size("term")
     sectors, rows, width = wavefunction.shape
     entries = float(sectors * rows * devices * width)
-    plan = RingPlan() if devices == 16 else WholePlan()
+    plan = (RingPlan if devices == 16 else WholePlan)(wavefunction.shape)
     me = lax.axis_index("term").astype(jnp.int32).reshape(1)
     ints = (block_source, block_target, live_count)
 
     beside = functools.partial(prepare, wavefunction, diagonal, ints)
-    fields, (_, square, *ints) = plan.gather(wavefunction, beside)
+    fields, (square, *ints) = plan.gather(plan.message(wavefunction), beside)
     blocks = (left_blocks, right_blocks, *ints)
-    *terms, scale = apply_blocks(me, fields, (square,), blocks, True, entries)
-    first_image, terms, correction, rounded, dots = davidson_step(
+    *terms, scale = apply_blocks(
+        me, fields, (square,), blocks, wavefunction.shape, True, entries
+    )
+    first_image, terms, correction, dots, *rounded = davidson_step(
         scale, wavefunction, diagonal, plan.scatter(*terms), entries
     )
     fields, _ = plan.gather(rounded)
     if devices != 16:
         dots = lax.psum(dots, "term")
     own = (scale, wavefunction, correction, dots)
-    *second_terms, along = apply_blocks(me, fields, own, blocks, False, entries)
+    *second_terms, along = apply_blocks(
+        me, fields, own, blocks, wavefunction.shape, False, entries
+    )
     second_vector, second_image = finish(
         along, scale, wavefunction, diagonal, terms, correction, plan.scatter(*second_terms), entries
     )

time: 125 us -> 118 us (0.944)
  waiting for transfers between devices: 81.7 us -> 22.8 us
  starting transfers between devices: 14.6 us -> 68.9 us
  Pallas kernels: 23.9 us -> 20.8 us
    ppermute x16 -> x56, waiting for transfers between devices: 73.9 us -> 18.2 us  [hop(): return lax.ppermute(value, 'term', pairs)]
    ppermute x16 -> x56, starting transfers between devices: 8.99 us -> 62.8 us  [hop(): return lax.ppermute(value, 'term', pairs)]
    pallas_call x2, Pallas kernels: 18.5 us -> 15 us  [apply_blocks(): pl.pallas_call(functools.partial(blocks_kernel, first, direct, rows, entr...]
    ppermute x16 -> x18, waiting for transfers between devices: 7.82 us -> 4.57 us  [flip(): return lax.ppermute(value, 'term', [(i, i ^ 1) for i in range(16)])]
    unnamed x12 -> x14, local copies, waits for them, and re-layouts: 3.1 us -> 3.99 us
    ppermute x16 -> x18, starting transfers between devices: 5.57 us -> 6.07 us  [flip(): return lax.ppermute(value, 'term', [(i, i ^ 1) for i in range(16)])]
    pallas_call x13 -> x40, Pallas kernels: 2.84 us -> 3.19 us  [the longest x1 2.21 us: finish(): pl.pallas_call(functools.partial(finish_kernel, len(ins) == 7, entries),...]
  transfers between devices with their start and end apart: 32 -> 74, of which waited for: 22 -> 21; matrix products, arithmetic and copies ran while one was open for 0% -> 0% of each run, Pallas kernels for 1% -> 2%
where the time goes in v5:
time: 118 us
  starting transfers between devices  68.9 us (58%)
  waiting for transfers between devices  22.8 us (19%)
  Pallas kernels  20.8 us (18%)
  local copies, waits for them, and re-layouts  3.99 us (3%)
  between operations  1.59 us (1%)
    ppermute x56, starting transfers between devices, hop(): return lax.ppermute(value, 'term', pairs)  62.8 us
    ppermute x56, waiting for transfers between devices, hop(): return lax.ppermute(value, 'term', pairs)  18.2 us
    pallas_call x2, Pallas kernels, apply_blocks(): pl.pallas_call(functools.partial(blocks_kernel, first, direct, rows, entr...  15 us
    ppermute x18, starting transfers between devices, flip(): return lax.ppermute(value, 'term', [(i, i ^ 1) for i in range(16)])  6.07 us
    ppermute x18, waiting for transfers between devices, flip(): return lax.ppermute(value, 'term', [(i, i ^ 1) for i in range(16)])  4.57 us
    unnamed x14, local copies, waits for them, and re-layouts  3.99 us
  transfers between devices with their start and end apart: 74, of which 21 were waited for; matrix products, arithmetic and copies ran while one was open for 0% of the time, Pallas kernels for 2%

profile of v5, /device:TPU:0, one launch (start us, length us, event | category | flops | bytes accessed | tf_op | source)
XLA Modules:
  0.0 118.0 jit_solution(5240848103840847775)
XLA Ops:
  2.1 2.6 %collective-permute-start = (bf16[16,1664]{1,0:T(8,128)(2,1)S(1)}, bf16[16,1664]{1,0:T(8,128)(2,1)S(1)}, u32[]{:S(2)}, u32[]{:S(2)}) collective-permute-start(bf16[16,1664]{1,0:T(8,128)(2,1)S(1)} %get-tuple-element.43), channel_id=1, source_target_pairs={{0,4},{1,3},{4,8},{5,1},{8,12},{9,5},{12,14},{13,9},{14,10},{15,13... | collective-permute-start | bytes 159752 | tf_op jit(solution)/shard_map/ppermute | solution.py:476
  4.7 1.6 %collective-permute-start.1 = (bf16[16,1536]{1,0:T(8,128)(2,1)S(1)}, bf16[16,1536]{1,0:T(8,128)(2,1)S(1)}, u32[]{:S(2)}, u32[]{:S(2)}) collective-permute-start(bf16[16,1536]{1,0:T(8,128)(2,1)S(1)} %get-tuple-element.44), channel_id=1, source_target_pairs={{0,4},{1,3},{4,8},{5,1},{8,12},{9,5},{12,14},{13,9},{14,10},{15,13... | collective-permute-start | bytes 147464 | tf_op jit(solution)/shard_map/ppermute | solution.py:476
  6.8 2.1 %collective-permute-start.2 = (bf16[16,1664]{1,0:T(8,128)(2,1)S(1)}, bf16[16,1664]{1,0:T(8,128)(2,1)S(1)}, u32[]{:S(2)}, u32[]{:S(2)}) collective-permute-start(bf16[16,1664]{1,0:T(8,128)(2,1)S(1)} %collective-permute-done.refs_0_), channel_id=1, source_target_pairs={{0,4},{1,3},{4,8},{5,1},{8,12},{9,5},{12,14},{13,9},{14,10},{15,13... | collective-permute-start | bytes 159752 | tf_op jit(solution)/shard_map/ppermute | solution.py:476
  8.8 1.6 %collective-permute-start.5 = (bf16[16,1664]{1,0:T(8,128)(2,1)S(1)}, bf16[16,1664]{1,0:T(8,128)(2,1)S(1)}, u32[]{:S(2)}, u32[]{:S(2)}) collective-permute-start(bf16[16,1664]{1,0:T(8,128)(2,1)S(1)} %get-tuple-element.45), channel_id=1, source_target_pairs={{0,4},{1,3},{4,8},{5,1},{8,12},{9,5},{12,14},{13,9},{14,10},{15,13... | collective-permute-start | bytes 159752 | tf_op jit(solution)/shard_map/ppermute | solution.py:476
  10.5 1.6 %collective-permute-start.3 = (bf16[16,1536]{1,0:T(8,128)(2,1)S(1)}, bf16[16,1536]{1,0:T(8,128)(2,1)S(1)}, u32[]{:S(2)}, u32[]{:S(2)}) collective-permute-start(bf16[16,1536]{1,0:T(8,128)(2,1)S(1)} %collective-permute-done.1.refs_1_), channel_id=1, source_target_pairs={{0,4},{1,3},{4,8},{5,1},{8,12},{9,5},{12,14},{13,9},{14,10},{15,13... | collective-permute-start | bytes 147464 | tf_op jit(solution)/shard_map/ppermute | solution.py:476
  14.6 1.6 %collective-permute-start.8 = (bf16[16,1536]{1,0:T(8,128)(2,1)S(1)}, bf16[16,1536]{1,0:T(8,128)(2,1)S(1)}, u32[]{:S(2)}, u32[]{:S(2)}) collective-permute-start(bf16[16,1536]{1,0:T(8,128)(2,1)S(1)} %collective-permute-done.3.refs_1_), channel_id=1, source_target_pairs={{0,4},{1,3},{4,8},{5,1},{8,12},{9,5},{12,14},{13,9},{14,10},{15,13... | collective-permute-start | bytes 147464 | tf_op jit(solution)/shard_map/ppermute | solution.py:476
  23.8 1.6 %collective-permute-start.12 = (bf16[16,1536]{1,0:T(8,128)(2,1)S(1)}, bf16[16,1536]{1,0:T(8,128)(2,1)S(1)}, u32[]{:S(2)}, u32[]{:S(2)}) collective-permute-start(bf16[16,1536]{1,0:T(8,128)(2,1)S(1)} %collective-permute-done.8.refs_1_), channel_id=1, source_target_pairs={{0,4},{1,3},{4,8},{5,1},{8,12},{9,5},{12,14},{13,9},{14,10},{15,13... | collective-permute-start | bytes 147464 | tf_op jit(solution)/shard_map/ppermute | solution.py:476
  31.1 7.2 %shard_map.101 = (f32[8,3,32,512]{3,2,1,0:T(8,128)S(1)}, bf16[1,16,3200]{2,1,0:T(8,128)(2,1)S(1)}, bf16[7,16,3200]{2,1,0:T(8,128)(2,1)S(1)}, f32[8,128]{1,0:T(8,128)S(1)}, f32[1]{0:T(128)}) custom-call(s32[1]{0:T(128)} %bitcast.me_ref, bf16[16,3200]{1,0:T(8,128)(2,1)S(1)} %get-tuple-element.42.refs_0_, bf16[1,16,3200]{2,1,0:T(8,128)(2,1)S(1)} %shard_map.95.refs_3_.refs_1_, ...), custom_call_target="tpu_custom_call" | custom-call | flops 4294967296 | bytes 8388608 | tf_op jit(solution)/shard_map/pallas_call | solution.py:219
  38.3 1.7 %collective-permute-start.19 = (bf16[1,16,3200]{2,1,0:T(8,128)(2,1)S(1)}, bf16[1,16,3200]{2,1,0:T(8,128)(2,1)S(1)}, u32[]{:S(2)}, u32[]{:S(2)}) collective-permute-start(bf16[1,16,3200]{2,1,0:T(8,128)(2,1)S(1)} %get-tuple-element.58), channel_id=1, source_target_pairs={{0,1},{1,0},{2,3},{3,2},{4,5},{5,4},{6,7},{7,6},{8,9},{9,8},{10,11... | collective-permute-start | bytes 307208 | tf_op jit(solution)/shard_map/ppermute | solution.py:467
  43.2 1.7 %collective-permute-start.29 = (bf16[16,1664]{1,0:T(8,128)(2,1)S(1)}, bf16[16,1664]{1,0:T(8,128)(2,1)S(1)}, u32[]{:S(2)}, u32[]{:S(2)}) collective-permute-start(bf16[16,1664]{1,0:T(8,128)(2,1)S(1)} %shard_map.110), channel_id=1, source_target_pairs={{0,4},{1,3},{4,8},{5,1},{8,12},{9,5},{12,14},{13,9},{14,10},{15,13... | collective-permute-start | bytes 159752 | tf_op jit(solution)/shard_map/ppermute | solution.py:476
  45.6 1.6 %collective-permute-start.22 = (bf16[16,1664]{1,0:T(8,128)(2,1)S(1)}, bf16[16,1664]{1,0:T(8,128)(2,1)S(1)}, u32[]{:S(2)}, u32[]{:S(2)}) collective-permute-start(bf16[16,1664]{1,0:T(8,128)(2,1)S(1)} %shard_map.103), channel_id=1, source_target_pairs={{0,4},{1,3},{4,8},{5,1},{8,12},{9,5},{12,14},{13,9},{14,10},{15,13... | collective-permute-start | bytes 159752 | tf_op jit(solution)/shard_map/ppermute | solution.py:476
  47.4 1.7 %collective-permute-start.30 = (bf16[16,1664]{1,0:T(8,128)(2,1)S(1)}, bf16[16,1664]{1,0:T(8,128)(2,1)S(1)}, u32[]{:S(2)}, u32[]{:S(2)}) collective-permute-start(bf16[16,1664]{1,0:T(8,128)(2,1)S(1)} %shard_map.111), channel_id=1, source_target_pairs={{0,4},{1,3},{4,8},{5,1},{8,12},{9,5},{12,14},{13,9},{14,10},{15,13... | collective-permute-start | bytes 159752 | tf_op jit(solution)/shard_map/ppermute | solution.py:476
  52.0 1.7 %collective-permute-start.31 = (bf16[16,1664]{1,0:T(8,128)(2,1)S(1)}, bf16[16,1664]{1,0:T(8,128)(2,1)S(1)}, u32[]{:S(2)}, u32[]{:S(2)}) collective-permute-start(bf16[16,1664]{1,0:T(8,128)(2,1)S(1)} %shard_map.112), channel_id=1, source_target_pairs={{0,4},{1,3},{4,8},{5,1},{8,12},{9,5},{12,14},{13,9},{14,10},{15,13... | collective-permute-start | bytes 159752 | tf_op jit(solution)/shard_map/ppermute | solution.py:476
  56.2 1.7 %collective-permute-done.27.refs_0_ = bf16[16,1536]{1,0:T(8,128)(2,1)S(1)} collective-permute-done((bf16[16,1536]{1,0:T(8,128)(2,1)S(1)}, bf16[16,1536]{1,0:T(8,128)(2,1)S(1)}, u32[]{:S(2)}, u32[]{:S(2)}) %collective-permute-start.27) | collective-permute-done | bytes 49184 | tf_op jit(solution)/shard_map/ppermute | solution.py:476
  58.9 3.2 %collective-permute-done.28.refs_4_ = bf16[16,1536]{1,0:T(8,128)(2,1)S(1)} collective-permute-done((bf16[16,1536]{1,0:T(8,128)(2,1)S(1)}, bf16[16,1536]{1,0:T(8,128)(2,1)S(1)}, u32[]{:S(2)}, u32[]{:S(2)}) %collective-permute-start.28) | collective-permute-done | bytes 49184 | tf_op jit(solution)/shard_map/ppermute | solution.py:476
  64.9 2.7 %collective-permute-done.37.refs_0_ = bf16[16,1664]{1,0:T(8,128)(2,1)S(1)} collective-permute-done((bf16[16,1664]{1,0:T(8,128)(2,1)S(1)}, bf16[16,1664]{1,0:T(8,128)(2,1)S(1)}, u32[]{:S(2)}, u32[]{:S(2)}) %collective-permute-start.37) | collective-permute-done | bytes 53280 | tf_op jit(solution)/shard_map/ppermute | solution.py:476
  70.0 1.7 %collective-permute-start.43 = (bf16[16,1536]{1,0:T(8,128)(2,1)S(1)}, bf16[16,1536]{1,0:T(8,128)(2,1)S(1)}, u32[]{:S(2)}, u32[]{:S(2)}) collective-permute-start(bf16[16,1536]{1,0:T(8,128)(2,1)S(1)} %get-tuple-element.68), channel_id=1, source_target_pairs={{0,4},{1,3},{4,8},{5,1},{8,12},{9,5},{12,14},{13,9},{14,10},{15,13... | collective-permute-start | bytes 147464 | tf_op jit(solution)/shard_map/ppermute | solution.py:476
  74.2 1.7 %collective-permute-start.47 = (bf16[16,1536]{1,0:T(8,128)(2,1)S(1)}, bf16[16,1536]{1,0:T(8,128)(2,1)S(1)}, u32[]{:S(2)}, u32[]{:S(2)}) collective-permute-start(bf16[16,1536]{1,0:T(8,128)(2,1)S(1)} %collective-permute-done.43.refs_3_), channel_id=1, source_target_pairs={{0,4},{1,3},{4,8},{5,1},{8,12},{9,5},{12,14},{13,9},{14,10},{15,13... | collective-permute-start | bytes 147464 | tf_op jit(solution)/shard_map/ppermute | solution.py:476
  78.3 1.7 %collective-permute-start.51 = (bf16[16,1536]{1,0:T(8,128)(2,1)S(1)}, bf16[16,1536]{1,0:T(8,128)(2,1)S(1)}, u32[]{:S(2)}, u32[]{:S(2)}) collective-permute-start(bf16[16,1536]{1,0:T(8,128)(2,1)S(1)} %collective-permute-done.47.refs_3_), channel_id=1, source_target_pairs={{0,4},{1,3},{4,8},{5,1},{8,12},{9,5},{12,14},{13,9},{14,10},{15,13... | collective-permute-start | bytes 147464 | tf_op jit(solution)/shard_map/ppermute | solution.py:476
  80.1 1.5 %collective-permute-done.49.refs_1_ = bf16[16,1536]{1,0:T(8,128)(2,1)S(1)} collective-permute-done((bf16[16,1536]{1,0:T(8,128)(2,1)S(1)}, bf16[16,1536]{1,0:T(8,128)(2,1)S(1)}, u32[]{:S(2)}, u32[]{:S(2)}) %collective-permute-start.49) | collective-permute-done | bytes 49184 | tf_op jit(solution)/shard_map/ppermute | solution.py:476
  84.1 7.8 %shard_map.122 = (f32[8,3,32,512]{3,2,1,0:T(8,128)S(1)}, bf16[1,16,3200]{2,1,0:T(8,128)(2,1)S(1)}, bf16[7,16,3200]{2,1,0:T(8,128)(2,1)S(1)}, f32[8,128]{1,0:T(8,128)S(1)}, f32[1]{0:T(128)}) custom-call(s32[1]{0:T(128)} %bitcast.me_ref, bf16[16,3200]{1,0:T(8,128)(2,1)S(1)} %get-tuple-element.64.refs_0_, bf16[1,16,3200]{2,1,0:T(8,128)(2,1)S(1)} %shard_map.117.refs_1_, ...), custom_call_target="tpu_custom_call" | custom-call | flops 4294967296 | bytes 8388608 | tf_op jit(solution)/shard_map/pallas_call | solution.py:219
  91.9 1.8 %collective-permute-start.56 = (bf16[1,16,3200]{2,1,0:T(8,128)(2,1)S(1)}, bf16[1,16,3200]{2,1,0:T(8,128)(2,1)S(1)}, u32[]{:S(2)}, u32[]{:S(2)}) collective-permute-start(bf16[1,16,3200]{2,1,0:T(8,128)(2,1)S(1)} %get-tuple-element.74), channel_id=1, source_target_pairs={{0,1},{1,0},{2,3},{3,2},{4,5},{5,4},{6,7},{7,6},{8,9},{9,8},{10,11... | collective-permute-start | bytes 307208 | tf_op jit(solution)/shard_map/ppermute | solution.py:467
  95.1 1.6 %collective-permute-start.58 = (bf16[16,1664]{1,0:T(8,128)(2,1)S(1)}, bf16[16,1664]{1,0:T(8,128)(2,1)S(1)}, u32[]{:S(2)}, u32[]{:S(2)}) collective-permute-start(bf16[16,1664]{1,0:T(8,128)(2,1)S(1)} %shard_map.123), channel_id=1, source_target_pairs={{0,4},{1,3},{4,8},{5,1},{8,12},{9,5},{12,14},{13,9},{14,10},{15,13... | collective-permute-start | bytes 159752 | tf_op jit(solution)/shard_map/ppermute | solution.py:476
  96.9 1.8 %collective-permute-start.66 = (bf16[16,1664]{1,0:T(8,128)(2,1)S(1)}, bf16[16,1664]{1,0:T(8,128)(2,1)S(1)}, u32[]{:S(2)}, u32[]{:S(2)}) collective-permute-start(bf16[16,1664]{1,0:T(8,128)(2,1)S(1)} %shard_map.131), channel_id=1, source_target_pairs={{0,4},{1,3},{4,8},{5,1},{8,12},{9,5},{12,14},{13,9},{14,10},{15,13... | collective-permute-start | bytes 159752 | tf_op jit(solution)/shard_map/ppermute | solution.py:476
  99.3 1.9 %collective-permute-start.59 = (bf16[16,1664]{1,0:T(8,128)(2,1)S(1)}, bf16[16,1664]{1,0:T(8,128)(2,1)S(1)}, u32[]{:S(2)}, u32[]{:S(2)}) collective-permute-start(bf16[16,1664]{1,0:T(8,128)(2,1)S(1)} %shard_map.124), channel_id=1, source_target_pairs={{0,4},{1,3},{4,8},{5,1},{8,12},{9,5},{12,14},{13,9},{14,10},{15,13... | collective-permute-start | bytes 159752 | tf_op jit(solution)/shard_map/ppermute | solution.py:476
  101.3 1.8 %collective-permute-start.67 = (bf16[16,1664]{1,0:T(8,128)(2,1)S(1)}, bf16[16,1664]{1,0:T(8,128)(2,1)S(1)}, u32[]{:S(2)}, u32[]{:S(2)}) collective-permute-start(bf16[16,1664]{1,0:T(8,128)(2,1)S(1)} %shard_map.132), channel_id=1, source_target_pairs={{0,4},{1,3},{4,8},{5,1},{8,12},{9,5},{12,14},{13,9},{14,10},{15,13... | collective-permute-start | bytes 159752 | tf_op jit(solution)/shard_map/ppermute | solution.py:476
  103.1 1.8 %collective-permute-start.63 = (bf16[16,1536]{1,0:T(8,128)(2,1)S(1)}, bf16[16,1536]{1,0:T(8,128)(2,1)S(1)}, u32[]{:S(2)}, u32[]{:S(2)}) collective-permute-start(bf16[16,1536]{1,0:T(8,128)(2,1)S(1)} %shard_map.128), channel_id=1, source_target_pairs={{0,4},{1,3},{4,8},{5,1},{8,12},{9,5},{12,14},{13,9},{14,10},{15,13... | collective-permute-start | bytes 147464 | tf_op jit(solution)/shard_map/ppermute | solution.py:476
  105.7 1.8 %collective-permute-start.68 = (bf16[16,1664]{1,0:T(8,128)(2,1)S(1)}, bf16[16,1664]{1,0:T(8,128)(2,1)S(1)}, u32[]{:S(2)}, u32[]{:S(2)}) collective-permute-start(bf16[16,1664]{1,0:T(8,128)(2,1)S(1)} %shard_map.133), channel_id=1, source_target_pairs={{0,4},{1,3},{4,8},{5,1},{8,12},{9,5},{12,14},{13,9},{14,10},{15,13... | collective-permute-start | bytes 159752 | tf_op jit(solution)/shard_map/ppermute | solution.py:476
  107.5 1.6 %collective-permute-start.64 = (bf16[16,1536]{1,0:T(8,128)(2,1)S(1)}, bf16[16,1536]{1,0:T(8,128)(2,1)S(1)}, u32[]{:S(2)}, u32[]{:S(2)}) collective-permute-start(bf16[16,1536]{1,0:T(8,128)(2,1)S(1)} %shard_map.129), channel_id=1, source_target_pairs={{0,4},{1,3},{4,8},{5,1},{8,12},{9,5},{12,14},{13,9},{14,10},{15,13... | collective-permute-start | bytes 147464 | tf_op jit(solution)/shard_map/ppermute | solution.py:476
  111.7 1.6 %collective-permute-start.65 = (bf16[16,1536]{1,0:T(8,128)(2,1)S(1)}, bf16[16,1536]{1,0:T(8,128)(2,1)S(1)}, u32[]{:S(2)}, u32[]{:S(2)}) collective-permute-start(bf16[16,1536]{1,0:T(8,128)(2,1)S(1)} %shard_map.130), channel_id=1, source_target_pairs={{0,4},{1,3},{4,8},{5,1},{8,12},{9,5},{12,14},{13,9},{14,10},{15,13... | collective-permute-start | bytes 147464 | tf_op jit(solution)/shard_map/ppermute | solution.py:476
  113.3 2.5 %collective-permute-done.65.refs_4_ = bf16[16,1536]{1,0:T(8,128)(2,1)S(1)} collective-permute-done((bf16[16,1536]{1,0:T(8,128)(2,1)S(1)}, bf16[16,1536]{1,0:T(8,128)(2,1)S(1)}, u32[]{:S(2)}, u32[]{:S(2)}) %collective-permute-start.65) | collective-permute-done | bytes 49184 | tf_op jit(solution)/shard_map/ppermute | solution.py:476
  115.8 2.2 %shard_map.137 = (f32[3,32,512]{2,1,0:T(8,128)}, f32[3,32,512]{2,1,0:T(8,128)}) custom-call(f32[1]{0:T(128)} %get-tuple-element.71.along_ref, f32[1]{0:T(128)} %get-tuple-element.56.scale_ref.refs_10_, bf16[3,32,512]{2,1,0:T(8,128)(2,1)S(1)} %copy-done.2, bf16[3,32,512]{2,1,0:T(8,128)(2,1)S(1)} %copy-done.4, f32[3,32,512]{2,1,0:T(8,128)S(1)} %get-tuple-element.72.terms_ref, ...), custom_call_target="tpu_custom_call" | custom-call | tf_op jit(solution)/shard_map/pallas_call | solution.py:457
  (174 shorter events, 46.0 us)
Async XLA Ops:
  1.5 7.3 %collective-permute-start.4 = (bf16[16,3200]{1,0:T(8,128)(2,1)S(1)}, bf16[16,3200]{1,0:T(8,128)(2,1)S(1)}, u32[]{:S(2)}, u32[]{:S(2)}) collective-permute-start(bf16[16,3200]{1,0:T(8,128)(2,1)S(1)} %get-tuple-element.42.refs_0_), channel_id=1, source_target_pairs={{0,1},{1,0},{2,3},{3,2},{4,5},{5,4},{6,7},{7,6},{8,9},{9,8},{10,11... | collective-permute-start | bytes 307208 | tf_op jit(solution)/shard_map/ppermute | solution.py:467
  2.1 4.7 %collective-permute-start = (bf16[16,1664]{1,0:T(8,128)(2,1)S(1)}, bf16[16,1664]{1,0:T(8,128)(2,1)S(1)}, u32[]{:S(2)}, u32[]{:S(2)}) collective-permute-start(bf16[16,1664]{1,0:T(8,128)(2,1)S(1)} %get-tuple-element.43), channel_id=1, source_target_pairs={{0,4},{1,3},{4,8},{5,1},{8,12},{9,5},{12,14},{13,9},{14,10},{15,13... | collective-permute-start | bytes 159752 | tf_op jit(solution)/shard_map/ppermute | solution.py:476
  4.7 5.8 %collective-permute-start.1 = (bf16[16,1536]{1,0:T(8,128)(2,1)S(1)}, bf16[16,1536]{1,0:T(8,128)(2,1)S(1)}, u32[]{:S(2)}, u32[]{:S(2)}) collective-permute-start(bf16[16,1536]{1,0:T(8,128)(2,1)S(1)} %get-tuple-element.44), channel_id=1, source_target_pairs={{0,4},{1,3},{4,8},{5,1},{8,12},{9,5},{12,14},{13,9},{14,10},{15,13... | collective-permute-start | bytes 147464 | tf_op jit(solution)/shard_map/ppermute | solution.py:476
  6.8 6.8 %collective-permute-start.2 = (bf16[16,1664]{1,0:T(8,128)(2,1)S(1)}, bf16[16,1664]{1,0:T(8,128)(2,1)S(1)}, u32[]{:S(2)}, u32[]{:S(2)}) collective-permute-start(bf16[16,1664]{1,0:T(8,128)(2,1)S(1)} %collective-permute-done.refs_0_), channel_id=1, source_target_pairs={{0,4},{1,3},{4,8},{5,1},{8,12},{9,5},{12,14},{13,9},{14,10},{15,13... | collective-permute-start | bytes 159752 | tf_op jit(solution)/shard_map/ppermute | solution.py:476
  8.8 5.2 %collective-permute-start.5 = (bf16[16,1664]{1,0:T(8,128)(2,1)S(1)}, bf16[16,1664]{1,0:T(8,128)(2,1)S(1)}, u32[]{:S(2)}, u32[]{:S(2)}) collective-permute-start(bf16[16,1664]{1,0:T(8,128)(2,1)S(1)} %get-tuple-element.45), channel_id=1, source_target_pairs={{0,4},{1,3},{4,8},{5,1},{8,12},{9,5},{12,14},{13,9},{14,10},{15,13... | collective-permute-start | bytes 159752 | tf_op jit(solution)/shard_map/ppermute | solution.py:476
  14.6 9.1 %collective-permute-start.8 = (bf16[16,1536]{1,0:T(8,128)(2,1)S(1)}, bf16[16,1536]{1,0:T(8,128)(2,1)S(1)}, u32[]{:S(2)}, u32[]{:S(2)}) collective-permute-start(bf16[16,1536]{1,0:T(8,128)(2,1)S(1)} %collective-permute-done.3.refs_1_), channel_id=1, source_target_pairs={{0,4},{1,3},{4,8},{5,1},{8,12},{9,5},{12,14},{13,9},{14,10},{15,13... | collective-permute-start | bytes 147464 | tf_op jit(solution)/shard_map/ppermute | solution.py:476
  16.2 9.1 %collective-permute-start.10 = (bf16[16,1536]{1,0:T(8,128)(2,1)S(1)}, bf16[16,1536]{1,0:T(8,128)(2,1)S(1)}, u32[]{:S(2)}, u32[]{:S(2)}) collective-permute-start(bf16[16,1536]{1,0:T(8,128)(2,1)S(1)} %collective-permute-done.6.refs_3_), channel_id=1, source_target_pairs={{0,4},{1,3},{4,8},{5,1},{8,12},{9,5},{12,14},{13,9},{14,10},{15,13... | collective-permute-start | bytes 147464 | tf_op jit(solution)/shard_map/ppermute | solution.py:476
  17.7 10.2 %collective-permute-start.11 = (bf16[16,1664]{1,0:T(8,128)(2,1)S(1)}, bf16[16,1664]{1,0:T(8,128)(2,1)S(1)}, u32[]{:S(2)}, u32[]{:S(2)}) collective-permute-start(bf16[16,1664]{1,0:T(8,128)(2,1)S(1)} %collective-permute-done.7.refs_0_), channel_id=1, source_target_pairs={{0,4},{1,3},{4,8},{5,1},{8,12},{9,5},{12,14},{13,9},{14,10},{15,13... | collective-permute-start | bytes 159752 | tf_op jit(solution)/shard_map/ppermute | solution.py:476
  18.3 11.1 %collective-permute-start.13 = (bf16[16,1664]{1,0:T(8,128)(2,1)S(1)}, bf16[16,1664]{1,0:T(8,128)(2,1)S(1)}, u32[]{:S(2)}, u32[]{:S(2)}) collective-permute-start(bf16[16,1664]{1,0:T(8,128)(2,1)S(1)} %collective-permute-done.9.refs_2_), channel_id=1, source_target_pairs={{0,4},{1,3},{4,8},{5,1},{8,12},{9,5},{12,14},{13,9},{14,10},{15,13... | collective-permute-start | bytes 159752 | tf_op jit(solution)/shard_map/ppermute | solution.py:476
  45.0 5.4 %collective-permute-start.33 = (bf16[16,1536]{1,0:T(8,128)(2,1)S(1)}, bf16[16,1536]{1,0:T(8,128)(2,1)S(1)}, u32[]{:S(2)}, u32[]{:S(2)}) collective-permute-start(bf16[16,1536]{1,0:T(8,128)(2,1)S(1)} %shard_map.113), channel_id=1, source_target_pairs={{0,4},{1,3},{4,8},{5,1},{8,12},{9,5},{12,14},{13,9},{14,10},{15,13... | collective-permute-start | bytes 147464 | tf_op jit(solution)/shard_map/ppermute | solution.py:476
  45.6 5.0 %collective-permute-start.22 = (bf16[16,1664]{1,0:T(8,128)(2,1)S(1)}, bf16[16,1664]{1,0:T(8,128)(2,1)S(1)}, u32[]{:S(2)}, u32[]{:S(2)}) collective-permute-start(bf16[16,1664]{1,0:T(8,128)(2,1)S(1)} %shard_map.103), channel_id=1, source_target_pairs={{0,4},{1,3},{4,8},{5,1},{8,12},{9,5},{12,14},{13,9},{14,10},{15,13... | collective-permute-start | bytes 159752 | tf_op jit(solution)/shard_map/ppermute | solution.py:476
  47.4 4.5 %collective-permute-start.30 = (bf16[16,1664]{1,0:T(8,128)(2,1)S(1)}, bf16[16,1664]{1,0:T(8,128)(2,1)S(1)}, u32[]{:S(2)}, u32[]{:S(2)}) collective-permute-start(bf16[16,1664]{1,0:T(8,128)(2,1)S(1)} %shard_map.111), channel_id=1, source_target_pairs={{0,4},{1,3},{4,8},{5,1},{8,12},{9,5},{12,14},{13,9},{14,10},{15,13... | collective-permute-start | bytes 159752 | tf_op jit(solution)/shard_map/ppermute | solution.py:476
  49.1 4.6 %collective-permute-start.26 = (bf16[16,1536]{1,0:T(8,128)(2,1)S(1)}, bf16[16,1536]{1,0:T(8,128)(2,1)S(1)}, u32[]{:S(2)}, u32[]{:S(2)}) collective-permute-start(bf16[16,1536]{1,0:T(8,128)(2,1)S(1)} %shard_map.107), channel_id=1, source_target_pairs={{0,4},{1,3},{4,8},{5,1},{8,12},{9,5},{12,14},{13,9},{14,10},{15,13... | collective-permute-start | bytes 147464 | tf_op jit(solution)/shard_map/ppermute | solution.py:476
  50.4 4.3 %collective-permute-start.34 = (bf16[16,1536]{1,0:T(8,128)(2,1)S(1)}, bf16[16,1536]{1,0:T(8,128)(2,1)S(1)}, u32[]{:S(2)}, u32[]{:S(2)}) collective-permute-start(bf16[16,1536]{1,0:T(8,128)(2,1)S(1)} %shard_map.114), channel_id=1, source_target_pairs={{0,4},{1,3},{4,8},{5,1},{8,12},{9,5},{12,14},{13,9},{14,10},{15,13... | collective-permute-start | bytes 147464 | tf_op jit(solution)/shard_map/ppermute | solution.py:476
  50.6 4.7 %collective-permute-start.23 = (bf16[16,1664]{1,0:T(8,128)(2,1)S(1)}, bf16[16,1664]{1,0:T(8,128)(2,1)S(1)}, u32[]{:S(2)}, u32[]{:S(2)}) collective-permute-start(bf16[16,1664]{1,0:T(8,128)(2,1)S(1)} %shard_map.104), channel_id=1, source_target_pairs={{0,4},{1,3},{4,8},{5,1},{8,12},{9,5},{12,14},{13,9},{14,10},{15,13... | collective-permute-start | bytes 159752 | tf_op jit(solution)/shard_map/ppermute | solution.py:476
  55.3 6.8 %collective-permute-start.24 = (bf16[16,1664]{1,0:T(8,128)(2,1)S(1)}, bf16[16,1664]{1,0:T(8,128)(2,1)S(1)}, u32[]{:S(2)}, u32[]{:S(2)}) collective-permute-start(bf16[16,1664]{1,0:T(8,128)(2,1)S(1)} %shard_map.105), channel_id=1, source_target_pairs={{0,4},{1,3},{4,8},{5,1},{8,12},{9,5},{12,14},{13,9},{14,10},{15,13... | collective-permute-start | bytes 159752 | tf_op jit(solution)/shard_map/ppermute | solution.py:476
  56.2 5.8 %collective-permute-start.32 = (bf16[16,1664]{1,0:T(8,128)(2,1)S(1)}, bf16[16,1664]{1,0:T(8,128)(2,1)S(1)}, u32[]{:S(2)}, u32[]{:S(2)}) collective-permute-start(bf16[16,1664]{1,0:T(8,128)(2,1)S(1)} %collective-permute-done.31), channel_id=1, source_target_pairs={{0,1},{1,0},{2,3},{3,2},{4,5},{5,4},{6,7},{7,6},{8,9},{9,8},{10,11... | collective-permute-start | bytes 159752 | tf_op jit(solution)/shard_map/ppermute | solution.py:467
  63.5 5.1 %collective-permute-start.41 = (bf16[16,3200]{1,0:T(8,128)(2,1)S(1)}, bf16[16,3200]{1,0:T(8,128)(2,1)S(1)}, u32[]{:S(2)}, u32[]{:S(2)}) collective-permute-start(bf16[16,3200]{1,0:T(8,128)(2,1)S(1)} %get-tuple-element.64.refs_0_), channel_id=1, source_target_pairs={{0,1},{1,0},{2,3},{3,2},{4,5},{5,4},{6,7},{7,6},{8,9},{9,8},{10,11... | collective-permute-start | bytes 307208 | tf_op jit(solution)/shard_map/ppermute | solution.py:467
  64.4 4.7 %collective-permute-start.38 = (bf16[16,1536]{1,0:T(8,128)(2,1)S(1)}, bf16[16,1536]{1,0:T(8,128)(2,1)S(1)}, u32[]{:S(2)}, u32[]{:S(2)}) collective-permute-start(bf16[16,1536]{1,0:T(8,128)(2,1)S(1)} %get-tuple-element.66), channel_id=1, source_target_pairs={{0,4},{1,3},{4,8},{5,1},{8,12},{9,5},{12,14},{13,9},{14,10},{15,13... | collective-permute-start | bytes 147464 | tf_op jit(solution)/shard_map/ppermute | solution.py:476
  68.6 4.3 %collective-permute-start.42 = (bf16[16,1664]{1,0:T(8,128)(2,1)S(1)}, bf16[16,1664]{1,0:T(8,128)(2,1)S(1)}, u32[]{:S(2)}, u32[]{:S(2)}) collective-permute-start(bf16[16,1664]{1,0:T(8,128)(2,1)S(1)} %get-tuple-element.67), channel_id=1, source_target_pairs={{0,4},{1,3},{4,8},{5,1},{8,12},{9,5},{12,14},{13,9},{14,10},{15,13... | collective-permute-start | bytes 159752 | tf_op jit(solution)/shard_map/ppermute | solution.py:476
  75.9 5.7 %collective-permute-start.48 = (bf16[16,1664]{1,0:T(8,128)(2,1)S(1)}, bf16[16,1664]{1,0:T(8,128)(2,1)S(1)}, u32[]{:S(2)}, u32[]{:S(2)}) collective-permute-start(bf16[16,1664]{1,0:T(8,128)(2,1)S(1)} %collective-permute-done.44.refs_0_), channel_id=1, source_target_pairs={{0,4},{1,3},{4,8},{5,1},{8,12},{9,5},{12,14},{13,9},{14,10},{15,13... | collective-permute-start | bytes 159752 | tf_op jit(solution)/shard_map/ppermute | solution.py:476
  77.0 5.4 %collective-permute-start.50 = (bf16[16,1664]{1,0:T(8,128)(2,1)S(1)}, bf16[16,1664]{1,0:T(8,128)(2,1)S(1)}, u32[]{:S(2)}, u32[]{:S(2)}) collective-permute-start(bf16[16,1664]{1,0:T(8,128)(2,1)S(1)} %collective-permute-done.46.refs_2_), channel_id=1, source_target_pairs={{0,4},{1,3},{4,8},{5,1},{8,12},{9,5},{12,14},{13,9},{14,10},{15,13... | collective-permute-start | bytes 159752 | tf_op jit(solution)/shard_map/ppermute | solution.py:476
  96.9 4.3 %collective-permute-start.66 = (bf16[16,1664]{1,0:T(8,128)(2,1)S(1)}, bf16[16,1664]{1,0:T(8,128)(2,1)S(1)}, u32[]{:S(2)}, u32[]{:S(2)}) collective-permute-start(bf16[16,1664]{1,0:T(8,128)(2,1)S(1)} %shard_map.131), channel_id=1, source_target_pairs={{0,4},{1,3},{4,8},{5,1},{8,12},{9,5},{12,14},{13,9},{14,10},{15,13... | collective-permute-start | bytes 159752 | tf_op jit(solution)/shard_map/ppermute | solution.py:476
  98.7 4.4 %collective-permute-start.62 = (bf16[16,1536]{1,0:T(8,128)(2,1)S(1)}, bf16[16,1536]{1,0:T(8,128)(2,1)S(1)}, u32[]{:S(2)}, u32[]{:S(2)}) collective-permute-start(bf16[16,1536]{1,0:T(8,128)(2,1)S(1)} %shard_map.127), channel_id=1, source_target_pairs={{0,4},{1,3},{4,8},{5,1},{8,12},{9,5},{12,14},{13,9},{14,10},{15,13... | collective-permute-start | bytes 147464 | tf_op jit(solution)/shard_map/ppermute | solution.py:476
  98.8 6.1 %collective-permute-start.70 = (bf16[16,1536]{1,0:T(8,128)(2,1)S(1)}, bf16[16,1536]{1,0:T(8,128)(2,1)S(1)}, u32[]{:S(2)}, u32[]{:S(2)}) collective-permute-start(bf16[16,1536]{1,0:T(8,128)(2,1)S(1)} %shard_map.134), channel_id=1, source_target_pairs={{0,4},{1,3},{4,8},{5,1},{8,12},{9,5},{12,14},{13,9},{14,10},{15,13... | collective-permute-start | bytes 147464 | tf_op jit(solution)/shard_map/ppermute | solution.py:476
  99.3 5.7 %collective-permute-start.59 = (bf16[16,1664]{1,0:T(8,128)(2,1)S(1)}, bf16[16,1664]{1,0:T(8,128)(2,1)S(1)}, u32[]{:S(2)}, u32[]{:S(2)}) collective-permute-start(bf16[16,1664]{1,0:T(8,128)(2,1)S(1)} %shard_map.124), channel_id=1, source_target_pairs={{0,4},{1,3},{4,8},{5,1},{8,12},{9,5},{12,14},{13,9},{14,10},{15,13... | collective-permute-start | bytes 159752 | tf_op jit(solution)/shard_map/ppermute | solution.py:476
  101.3 4.4 %collective-permute-start.67 = (bf16[16,1664]{1,0:T(8,128)(2,1)S(1)}, bf16[16,1664]{1,0:T(8,128)(2,1)S(1)}, u32[]{:S(2)}, u32[]{:S(2)}) collective-permute-start(bf16[16,1664]{1,0:T(8,128)(2,1)S(1)} %shard_map.132), channel_id=1, source_target_pairs={{0,4},{1,3},{4,8},{5,1},{8,12},{9,5},{12,14},{13,9},{14,10},{15,13... | collective-permute-start | bytes 159752 | tf_op jit(solution)/shard_map/ppermute | solution.py:476
  103.1 4.4 %collective-permute-start.63 = (bf16[16,1536]{1,0:T(8,128)(2,1)S(1)}, bf16[16,1536]{1,0:T(8,128)(2,1)S(1)}, u32[]{:S(2)}, u32[]{:S(2)}) collective-permute-start(bf16[16,1536]{1,0:T(8,128)(2,1)S(1)} %shard_map.128), channel_id=1, source_target_pairs={{0,4},{1,3},{4,8},{5,1},{8,12},{9,5},{12,14},{13,9},{14,10},{15,13... | collective-permute-start | bytes 147464 | tf_op jit(solution)/shard_map/ppermute | solution.py:476
  105.0 4.6 %collective-permute-start.60 = (bf16[16,1664]{1,0:T(8,128)(2,1)S(1)}, bf16[16,1664]{1,0:T(8,128)(2,1)S(1)}, u32[]{:S(2)}, u32[]{:S(2)}) collective-permute-start(bf16[16,1664]{1,0:T(8,128)(2,1)S(1)} %shard_map.125), channel_id=1, source_target_pairs={{0,4},{1,3},{4,8},{5,1},{8,12},{9,5},{12,14},{13,9},{14,10},{15,13... | collective-permute-start | bytes 159752 | tf_op jit(solution)/shard_map/ppermute | solution.py:476
  105.7 4.5 %collective-permute-start.68 = (bf16[16,1664]{1,0:T(8,128)(2,1)S(1)}, bf16[16,1664]{1,0:T(8,128)(2,1)S(1)}, u32[]{:S(2)}, u32[]{:S(2)}) collective-permute-start(bf16[16,1664]{1,0:T(8,128)(2,1)S(1)} %shard_map.133), channel_id=1, source_target_pairs={{0,4},{1,3},{4,8},{5,1},{8,12},{9,5},{12,14},{13,9},{14,10},{15,13... | collective-permute-start | bytes 159752 | tf_op jit(solution)/shard_map/ppermute | solution.py:476
  109.7 6.1 %collective-permute-start.61 = (bf16[16,1664]{1,0:T(8,128)(2,1)S(1)}, bf16[16,1664]{1,0:T(8,128)(2,1)S(1)}, u32[]{:S(2)}, u32[]{:S(2)}) collective-permute-start(bf16[16,1664]{1,0:T(8,128)(2,1)S(1)} %shard_map.126), channel_id=1, source_target_pairs={{0,4},{1,3},{4,8},{5,1},{8,12},{9,5},{12,14},{13,9},{14,10},{15,13... | collective-permute-start | bytes 159752 | tf_op jit(solution)/shard_map/ppermute | solution.py:476
  110.2 5.7 %collective-permute-start.69 = (bf16[16,1664]{1,0:T(8,128)(2,1)S(1)}, bf16[16,1664]{1,0:T(8,128)(2,1)S(1)}, u32[]{:S(2)}, u32[]{:S(2)}) collective-permute-start(bf16[16,1664]{1,0:T(8,128)(2,1)S(1)} %collective-permute-done.68), channel_id=1, source_target_pairs={{0,1},{1,0},{2,3},{3,2},{4,5},{5,4},{6,7},{7,6},{8,9},{9,8},{10,11... | collective-permute-start | bytes 159752 | tf_op jit(solution)/shard_map/ppermute | solution.py:467
  (49 other events, 176.6 us)

commit v6 on v0

--- a/solution.py
+++ b/solution.py
@@ -1,7 +1,523 @@
+import functools
+
 import jax
 import jax.numpy as jnp
 from jax import lax
+from jax.experimental import pallas as pl
+from jax.experimental.pallas import tpu as pltpu
 from jax.sharding import PartitionSpec as P
+
+VMEM = pl.BlockSpec(memory_space=pltpu.VMEM)
+SMEM = pl.BlockSpec(memory_space=pltpu.SMEM)
+HBM = pl.BlockSpec(memory_space=pltpu.HBM)
+PARAMS = pltpu.CompilerParams(vmem_limit_bytes=32 * 1024 * 1024)
+HALF = 16
+LANES = 128
+
+
+def fold(value):
+    rows, width = value.shape
+    summed = jnp.sum(value.reshape(rows // 8, 8, width), axis=0)
+    return sum(summed[:, k * 128 : (k + 1) * 128] for k in range(width // 128))
+
+
+def down(value):
+    return jnp.sum(value, axis=0, keepdims=True)
+
+
+def halves(rows, width, start=0):
+    for h in range(rows // HALF):
+        yield h * HALF, slice(start + h * width, start + (h + 1) * width)
+
+
+def write_lanes(ref, at, lanes):
+    whole = jnp.broadcast_to(lanes, (HALF, LANES))
+    high = whole.astype(jnp.bfloat16).astype(jnp.float32)
+    rest = whole - high
+    middle = rest.astype(jnp.bfloat16).astype(jnp.float32)
+    low = rest - middle
+    row = lax.broadcasted_iota(jnp.int32, whole.shape, 0)
+    value = jnp.where(row == 0, high, jnp.where(row == 1, middle, jnp.where(row == 2, low, 0.0)))
+    ref[:, at : at + LANES] = value.astype(jnp.bfloat16)
+
+
+def read_lanes(ref, at):
+    return down(ref[:, at : at + LANES].astype(jnp.float32))
+
+
+def chip_at(place):
+    place = lax.rem(place + 8, 8)
+    return jnp.where(place < 4, 2 * place, 15 - 2 * place)
+
+
+def ring_place(me):
+    chip, core = me // 2, me % 2
+    place = jnp.where(chip % 2 == 0, chip // 2, (15 - chip) // 2)
+    return place, core
+
+
+def ahead(me, distance, half, core=None):
+    place, own = ring_place(me)
+    core = own if core is None else core
+    return chip_at(place + (1 - 2 * core) * distance) * 2 + half
+
+
+CHAIN = ((4, True), (3, True), (3, False), (2, True), (2, False), (1, True), (1, False), (0, True))
+
+
+def chain_device(me, core, k):
+    distance, own = CHAIN[k]
+    return ahead(me, distance, core if own else 1 - core, core)
+
+
+def gathered_devices(me):
+    core = me % 2
+    devices = []
+    for sign, mine in ((-1, core), (1, 1 - core)):
+        devices += [ahead(me, 0, mine), ahead(me, sign, mine)]
+        for d in (1, 2, 3):
+            devices += [ahead(me, sign * (d + 1), mine), ahead(me, sign * d, 1 - mine)]
+    return devices
+
+
+def message_kernel(wave_ref, *out_refs):
+    sectors, rows, width = wave_ref.shape
+    for s in range(sectors):
+        for row, part in halves(rows, width):
+            out_refs[s][0, :, part] = wave_ref[s, row : row + HALF, :]
+
+
+def as_messages(wave):
+    sectors, rows, width = wave.shape
+    shape = (1, HALF, rows // HALF * width)
+    return pl.pallas_call(
+        message_kernel,
+        in_specs=[VMEM],
+        out_specs=[VMEM] * sectors,
+        out_shape=[jax.ShapeDtypeStruct(shape, wave.dtype)] * sectors,
+        compiler_params=PARAMS,
+    )(wave)
+
+
+def pair_kernel(one_ref, two_ref, out_ref):
+    out_ref[0] = one_ref[0]
+    out_ref[1] = two_ref[0]
+
+
+def pair(one, two):
+    return pl.pallas_call(
+        pair_kernel,
+        in_specs=[VMEM, VMEM],
+        out_specs=VMEM,
+        out_shape=jax.ShapeDtypeStruct((2, *one.shape[1:]), one.dtype),
+        compiler_params=PARAMS,
+    )(one, two)
+
+
+def pack_kernel(*refs):
+    *in_refs, out_ref = refs
+    at = 0
+    for ref in in_refs:
+        for k in range(ref.shape[0]):
+            out_ref[at, :, : ref.shape[2]] = ref[k]
+            at += 1
+
+
+def pack(*messages):
+    lanes = max(m.shape[2] for m in messages)
+    count = sum(m.shape[0] for m in messages)
+    return pl.pallas_call(
+        pack_kernel,
+        in_specs=[VMEM] * len(messages),
+        out_specs=VMEM,
+        out_shape=jax.ShapeDtypeStruct((count, HALF, lanes), messages[0].dtype),
+        compiler_params=PARAMS,
+    )(*messages)
+
+
+def prepare_kernel(diag_ref, _, *refs):
+    *wave_refs, square_ref = refs
+    sectors, rows, width = diag_ref.shape
+    square = jnp.zeros((8, 128), jnp.float32)
+    for s in range(sectors):
+        for row, part in halves(rows, width):
+            wave = wave_refs[s][0, :, part].astype(jnp.float32)
+            square += fold(diag_ref[s, row : row + HALF, :].astype(jnp.float32) * wave * wave)
+    square_ref[...] = square
+
+
+def prepare(diag, waves, after):
+    return pl.pallas_call(
+        prepare_kernel,
+        in_specs=[VMEM, HBM] + [VMEM] * len(waves),
+        out_specs=VMEM,
+        out_shape=jax.ShapeDtypeStruct((8, 128), jnp.float32),
+        compiler_params=PARAMS,
+    )(diag, after, *waves)
+
+
+def blocks_kernel(first, sectors, rows, entries, me_ref, ints_ref, *refs):
+    packed_ref, refs = refs[0], refs[1:]
+    views = []
+    for s in range(sectors):
+        mine, (partner, last), refs = refs[:5], refs[5:7], refs[7:]
+        view = [ref.at[k] for ref in mine for k in range(ref.shape[0])]
+        view += [partner.at[0], *(packed_ref.at[s * 5 + k] for k in range(5)), last.at[0], last.at[1]]
+        views.append(view)
+    if first:
+        (square_ref,), refs = refs[:1], refs[1:]
+    else:
+        (scale_ref, wave_ref), corrections, refs = refs[:2], refs[2 : 2 + sectors], refs[2 + sectors :]
+    left_hbm, right_hbm, *refs = refs
+    total, near_ref, far_ref, dot_ref, out_ref, left, right, field, left_sem, right_sem = refs
+    slots, width = left.shape[0], total.shape[2]
+    data = rows // HALF * width
+
+    def copies(slot):
+        return (
+            pltpu.make_async_copy(left_hbm.at[slot], left.at[slot], left_sem.at[slot]),
+            pltpu.make_async_copy(right_hbm.at[slot], right.at[slot], right_sem.at[slot]),
+        )
+
+    for slot in range(slots):
+        for copy in copies(slot):
+            copy.start()
+
+    me = me_ref[0]
+    pieces = []
+    for k, owner in enumerate(gathered_devices(me)):
+        for s in range(sectors):
+            ref = views[s][k]
+            for row, part in halves(rows, width):
+                at = pl.ds(pl.multiple_of(owner * rows + row, HALF), HALF)
+                pieces.append((ref, part, s, at))
+
+    total[...] = jnp.zeros_like(total)
+    if first:
+        dot = jnp.zeros((8, 128), jnp.float32)
+        for ref, part, _, _ in pieces:
+            value = ref[:, part].astype(jnp.float32)
+            dot += fold(value * value)
+        scale = jnp.sqrt(jnp.sum(dot) / entries)
+        out_ref[0] = scale
+        inverse = 1.0 / scale
+        for ref, part, s, at in pieces:
+            field[s, at, :] = (ref[:, part].astype(jnp.float32) * inverse).astype(jnp.bfloat16)
+    else:
+        for ref, part, s, at in pieces:
+            field[s, at, :] = ref[:, part]
+
+    used = ints_ref[2 * slots]
+
+    def add_pair(step, carry):
+        one, two = 2 * step, 2 * step + 1
+        for slot in (one, two):
+            for copy in copies(slot):
+                copy.wait()
+
+        @pl.when(one < used)
+        def _():
+            products = [
+                jnp.dot(
+                    left[slot], field[ints_ref[slot]], preferred_element_type=jnp.float32
+                ).astype(jnp.bfloat16)
+                for slot in (one, two)
+            ]
+            products[1] = jnp.where(two < used, products[1], jnp.zeros_like(products[1]))
+            for slot, product in zip((one, two), products):
+                total[ints_ref[slots + slot]] += lax.dot_general(
+                    product,
+                    right[slot],
+                    (((1,), (1,)), ((), ())),
+                    preferred_element_type=jnp.float32,
+                )
+
+        return carry
+
+    lax.fori_loop(0, slots // 2, add_pair, 0)
+
+    dot = jnp.zeros((8, 128), jnp.float32)
+    if first:
+        for ref, part, s, at in pieces:
+            dot += fold(total[s, at, :] * ref[:, part].astype(jnp.float32))
+        dot = dot * inverse + square_ref[...] * inverse * inverse
+    else:
+        lanes = sum(read_lanes(view, data) for view in views[sectors - 1])
+        along = jnp.sum(lanes) / entries
+        out_ref[0] = along
+        for s in range(sectors):
+            start = wave_ref[s].astype(jnp.float32) / scale_ref[0]
+            projected = corrections[s][...] - along * start
+            dot += fold(projected * projected)
+    dot_ref[...] = dot
+    lanes = down(dot)
+    core = me % 2
+    for k in range(len(CHAIN)):
+        owner = chain_device(me, 1 - core, k)
+        ref = near_ref.at[k] if k < near_ref.shape[0] else far_ref.at[k - near_ref.shape[0]]
+        for s in range(sectors):
+            for row, part in halves(rows, width, s * data):
+                at = pl.ds(pl.multiple_of(owner * rows + row, HALF), HALF)
+                ref[:, part] = total[s, at, :].astype(jnp.bfloat16)
+        write_lanes(ref, sectors * data, lanes)
+
+
+def apply_blocks(me, ints, fields, packed, own, left, right, shape, first, entries):
+    slots, order, width = left.shape
+    sectors, rows, _ = shape
+    piece = (HALF, sectors * (rows // HALF) * width + LANES)
+    pieces = [packed]
+    for mine, partner, last in fields:
+        pieces += [*mine, partner, last]
+    own_specs = [VMEM] if first else [SMEM] + [VMEM] * (1 + sectors)
+    return pl.pallas_call(
+        functools.partial(blocks_kernel, first, sectors, rows, entries),
+        in_specs=[SMEM, SMEM] + [VMEM] * len(pieces) + own_specs + [HBM] * 2,
+        out_specs=[VMEM, VMEM, VMEM, VMEM, SMEM],
+        scratch_shapes=[
+            pltpu.VMEM(left.shape, left.dtype),
+            pltpu.VMEM(right.shape, right.dtype),
+            pltpu.VMEM((sectors, order, width), jnp.bfloat16),
+            pltpu.SemaphoreType.DMA((slots,)),
+            pltpu.SemaphoreType.DMA((slots,)),
+        ],
+        out_shape=[
+            jax.ShapeDtypeStruct((sectors, order, width), jnp.float32),
+            jax.ShapeDtypeStruct((1, *piece), jnp.bfloat16),
+            jax.ShapeDtypeStruct((len(CHAIN) - 1, *piece), jnp.bfloat16),
+            jax.ShapeDtypeStruct((8, 128), jnp.float32),
+            jax.ShapeDtypeStruct((1,), jnp.float32),
+        ],
+        compiler_params=PARAMS,
+        cost_estimate=pl.CostEstimate(
+            flops=4 * slots * order * order * width,
+            bytes_accessed=4 * slots * order * order,
+            transcendentals=0,
+        ),
+    )(me, ints, *pieces, *own, left, right)
+
+
+def chip_terms(me, core, k, s, rows, row, part, total, other):
+    at = pl.multiple_of(chain_device(me, core, k) * rows + row, HALF)
+    return total[s, pl.ds(at, HALF), :] + other[:, part].astype(jnp.float32)
+
+
+def chain_kernel(links, s, rows, me_ref, total_ref, dot_ref, *refs):
+    n_other = max(other for _, other, _, _ in links) + 1
+    other_refs, (*arrived_refs, out_ref) = refs[:n_other], refs[n_other:]
+    sectors, _, width = total_ref.shape
+    data = rows // HALF * width
+    me = me_ref[0]
+    for place, (k, which, index, arrived) in enumerate(links):
+        other = other_refs[which].at[index]
+        for row, lanes in halves(rows, width):
+            part = slice(s * data + lanes.start, s * data + lanes.stop)
+            value = chip_terms(me, me % 2, k, s, rows, row, part, total_ref, other)
+            if arrived:
+                value += arrived_refs[0][place, :, lanes].astype(jnp.float32)
+            out_ref[place, :, lanes] = value.astype(jnp.bfloat16)
+        if s == 0:
+            lanes = down(dot_ref[...]) + read_lanes(other, sectors * data)
+            if arrived:
+                lanes += read_lanes(arrived_refs[0].at[place], data)
+            write_lanes(out_ref.at[place], data, lanes)
+
+
+def chain(links, s, rows, me, total, dot, others, *arrived):
+    width = total.shape[2]
+    lanes = rows // HALF * width + (LANES if s == 0 else 0)
+    n_other = max(other for _, other, _, _ in links) + 1
+    return pl.pallas_call(
+        functools.partial(chain_kernel, links, s, rows),
+        in_specs=[SMEM] + [VMEM] * (2 + n_other + len(arrived)),
+        out_specs=VMEM,
+        out_shape=jax.ShapeDtypeStruct((len(links), HALF, lanes), jnp.bfloat16),
+        compiler_params=PARAMS,
+    )(me, total, dot, *others[:n_other], *arrived)
+
+
+def own_terms(me, s, rows, total_ref, far_ref, ours_ref, theirs_ref):
+    width = total_ref.shape[2]
+    data = rows // HALF * width
+    last = len(CHAIN) - 1
+    values = []
+    for row, lanes in halves(rows, width):
+        part = slice(s * data + lanes.start, s * data + lanes.stop)
+        value = chip_terms(me, me % 2, last, s, rows, row, part, total_ref, far_ref.at[last - 1])
+        value += ours_ref[0, :, lanes].astype(jnp.float32)
+        value += theirs_ref[1, :, lanes].astype(jnp.float32)
+        values.append(value)
+    return jnp.concatenate(values, axis=0)
+
+
+def own_scalar(sectors, rows, dot_ref, total_ref, far_ref, ours_ref, theirs_ref):
+    data = rows // HALF * total_ref.shape[2]
+    lanes = down(dot_ref[...]) + read_lanes(far_ref.at[len(CHAIN) - 2], sectors * data)
+    lanes += read_lanes(ours_ref.at[0], data) + read_lanes(theirs_ref.at[1], data)
+    return jnp.sum(lanes)
+
+
+def step_kernel(s, entries, me_ref, scale_ref, wave_ref, diag_ref, dot_ref, *refs):
+    *sums, extra_ref, terms_ref, correction_ref, message_ref, dots_ref, ritz_ref = refs
+    sectors, rows, width = wave_ref.shape
+    if s == 0:
+        ritz = own_scalar(sectors, rows, dot_ref, *sums) / entries
+    else:
+        ritz = extra_ref[0]
+    ritz_ref[0] = ritz
+    start = wave_ref[s].astype(jnp.float32) * (1.0 / scale_ref[0])
+    diag = diag_ref[s].astype(jnp.float32)
+    terms = own_terms(me_ref[0], s, rows, *sums)
+    first = terms + diag * start
+    correction = (first - ritz * start) / jnp.maximum(jnp.abs(diag - ritz), 1.0)
+    terms_ref[...] = terms
+    correction_ref[...] = correction
+    dots = fold(start * correction)
+    if s > 0:
+        dots += dot_ref[...]
+    dots_ref[...] = dots
+    for row, part in halves(rows, width):
+        message_ref[0, :, part] = correction[row : row + HALF].astype(jnp.bfloat16)
+    if s == sectors - 1:
+        write_lanes(message_ref.at[0], rows // HALF * width, down(dots))
+
+
+def davidson_step(s, me, scale, wave, diag, dot, sums, extra, entries):
+    sectors, rows, width = wave.shape
+    lanes = rows // HALF * width + (LANES if s == sectors - 1 else 0)
+    return pl.pallas_call(
+        functools.partial(step_kernel, s, entries),
+        in_specs=[SMEM, SMEM] + [VMEM] * 7 + [SMEM],
+        out_specs=[VMEM] * 4 + [SMEM],
+        out_shape=[
+            jax.ShapeDtypeStruct((rows, width), jnp.float32),
+            jax.ShapeDtypeStruct((rows, width), jnp.float32),
+            jax.ShapeDtypeStruct((1, HALF, lanes), jnp.bfloat16),
+            jax.ShapeDtypeStruct((8, 128), jnp.float32),
+            jax.ShapeDtypeStruct((1,), jnp.float32),
+        ],
+        compiler_params=PARAMS,
+    )(me, scale, wave, diag, dot, *sums, extra)
+
+
+def finish_kernel(entries, me_ref, along_ref, scale_ref, wave_ref, diag_ref, dot_ref, *refs):
+    first_ref, vector_ref, image_ref = refs[-3:]
+    sectors, rows, width = wave_ref.shape
+    terms, corrections, refs = refs[:sectors], refs[sectors : 2 * sectors], refs[2 * sectors : -3]
+    total_ref, far_ref, *arrived = refs
+    along = along_ref[0]
+    square = own_scalar(sectors, rows, dot_ref, total_ref, far_ref, arrived[0], arrived[1])
+    inverse = 1.0 / jnp.sqrt(square / entries)
+    start_scale = 1.0 / scale_ref[0]
+    for s in range(sectors):
+        start = wave_ref[s].astype(jnp.float32) * start_scale
+        diag = diag_ref[s].astype(jnp.float32)
+        first_ref[s] = terms[s][...] + diag * start
+        second = (corrections[s][...] - along * start) * inverse
+        vector_ref[s] = second
+        image = own_terms(me_ref[0], s, rows, total_ref, far_ref, *arrived[2 * s : 2 * s + 2])
+        image_ref[s] = (image - along * terms[s][...]) * inverse + diag * second
+
+
+def finish(me, along, scale, wave, diag, dot, terms, corrections, total, far, arrived, entries):
+    full = jax.ShapeDtypeStruct(wave.shape, jnp.float32)
+    operands = (wave, diag, dot, *terms, *corrections, total, far, *arrived)
+    return pl.pallas_call(
+        functools.partial(finish_kernel, entries),
+        in_specs=[SMEM] * 3 + [VMEM] * len(operands),
+        out_specs=[VMEM] * 3,
+        out_shape=[full] * 3,
+        compiler_params=PARAMS,
+    )(me, along, scale, *operands)
+
+
+def flip(value):
+    return lax.ppermute(value, "term", [(i, i ^ 1) for i in range(16)])
+
+
+def hop(value):
+    order = [0, 2, 4, 6, 7, 5, 3, 1]
+    pairs = []
+    for place in range(8):
+        for core, step in ((0, 1), (1, 7)):
+            pairs.append((order[place] * 2 + core, order[(place + step) % 8] * 2 + core))
+    return lax.ppermute(value, "term", pairs)
+
+
+def gather(own):
+    partner = [flip(m) for m in own]
+    arrived = [hop(m) for m in own]
+    rounds = [arrived]
+    arrived = [hop(pair(m, p)) for m, p in zip(arrived, partner)]
+    rounds.append(arrived)
+    for _ in range(2):
+        arrived = [hop(m) for m in arrived]
+        rounds.append(arrived)
+    sectors = len(own)
+    packed = flip(pack(*(rounds[k][s] for s in range(sectors) for k in range(3))))
+    last = [flip(m) for m in arrived]
+    fields = []
+    for s in range(sectors):
+        mine = [own[s], *(r[s] for r in rounds)]
+        fields.append((mine, partner[s], last[s]))
+    return fields, packed
+
+
+def scatter(me, rows, total, near, far, dot):
+    sectors = total.shape[0]
+    near = flip(near)
+    near, far = lax.optimization_barrier((near, far))
+    far = flip(far)
+    others = (near, far)
+    links = ((0, 0, 0, False),)
+    arrived = [hop(chain(links, s, rows, me, total, dot, others)) for s in range(sectors)]
+    for k in (1, 3, 5):
+        links = ((k, 1, k - 1, True), (k + 1, 1, k, k > 1))
+        arrived = [
+            hop(chain(links, s, rows, me, total, dot, others, m)) for s, m in enumerate(arrived)
+        ]
+    return far, [(m, flip(m)) for m in arrived]
+
+
+def on_ring(
+    wavefunction, diagonal, left_blocks, right_blocks, block_source, block_target, live_count
+):
+    sectors, rows, width = wavefunction.shape
+    entries = float(sectors * rows * lax.axis_size("term") * width)
+    me = lax.axis_index("term").astype(jnp.int32).reshape(1)
+    ints = jnp.concatenate([block_source, block_target, live_count])
+    blocks = (left_blocks, right_blocks, wavefunction.shape)
+
+    waves = as_messages(wavefunction)
+    fields, packed = gather(waves)
+    square = prepare(diagonal, waves, fields[0][0][1])
+    total, near, far, dot, scale = apply_blocks(
+        me, ints, fields, packed, (square,), *blocks, True, entries
+    )
+    far, arrived = scatter(me, rows, total, near, far, dot)
+    terms, corrections, messages = [], [], []
+    ritz, dots = scale, dot
+    for s in range(sectors):
+        sums = (total, far, *arrived[s])
+        term, correction, message, dots, ritz = davidson_step(
+            s, me, scale, wavefunction, diagonal, dots, sums, ritz, entries
+        )
+        terms.append(term)
+        corrections.append(correction)
+        messages.append(message)
+    fields, packed = gather(messages)
+    own = (scale, wavefunction, *corrections)
+    total, near, far, dot, along = apply_blocks(
+        me, ints, fields, packed, own, *blocks, False, entries
+    )
+    far, arrived = scatter(me, rows, total, near, far, dot)
+    arrived = [m for both in arrived for m in both]
+    return tuple(
+        finish(
+            me, along, scale, wavefunction, diagonal, dot, terms, corrections, total, far, arrived,
+            entries,
+        )
+    )
 
 
 def block_loop(field_rounded, left_ops, right_ops, sources, targets, last_slot, partial_sum):
@@ -20,7 +536,7 @@
     return lax.fori_loop(0, last_slot, add_block, partial_sum)
 
 
-def on_device(
+def on_any(
     wavefunction, diagonal, left_blocks, right_blocks, block_source, block_target, live_count
 ):
     devices = lax.axis_size("term")
@@ -77,6 +593,7 @@
         P(("grp", "term")),
         P(("grp", "term")),
     )
+    on_device = on_ring if mesh.shape["term"] == 16 else on_any
     return jax.shard_map(
         on_device,
         mesh=mesh,

time: 421 us -> 128 us (0.30)
  waiting for transfers between devices: 270 us -> 34.1 us
  starting transfers between devices: 0.15 us -> 58.5 us
  loops' own time: 46.9 us -> 0 us
  matrix products: 29.2 us -> 0 us
  Pallas kernels: 0 us -> 25.9 us
  other arithmetic: 25.2 us -> 0.75 us
  local copies, waits for them, and re-layouts: 30.6 us -> 6.18 us
  between operations: 16.5 us -> 1.73 us
    psum x1 -> x0, waiting for transfers between devices: 132 us -> none  [on_device(): first_whole = lax.psum(first_terms, 'term') + whole_diag * start_whole]
    reduce_scatter x1 -> x0, waiting for transfers between devices: 92.5 us -> none  [on_device(): lax.psum_scatter(second_terms, 'term', scatter_dimension=1, tiled=True)]
    ppermute x0 -> x72, starting transfers between devices: none -> 58.5 us  [the longest x48 56.6 us: hop(): return lax.ppermute(value, 'term', pairs)]
    another operation x2 -> x0, loops' own time: 46.9 us -> none  [block_loop(): return lax.fori_loop(0, last_slot, add_block, partial_sum)]
    all_gather x2 -> x0, waiting for transfers between devices: 43.9 us -> none  [the longest x1 43.9 us: on_device(): lax.all_gather(wavefunction, 'term', axis=1, tiled=True).astype(jnp.float32)]
    ppermute x0 -> x72, waiting for transfers between devices: none -> 34.1 us  [the longest x48 29 us: hop(): return lax.ppermute(value, 'term', pairs)]
    dot_general x10 -> x0, matrix products: 29.2 us -> none  [add_block(): jnp.dot(product, right_op.T, preferred_element_type=jnp.float32)]
    dynamic_slice x31 -> x0, local copies, waits for them, and re-layouts: 26.4 us -> none  [the longest x10 13 us: add_block(): before = lax.dynamic_index_in_dim(running, target, 0, keepdims=False)]
  transfers between devices with their start and end apart: 4 -> 72, of which waited for: 3 -> 34; matrix products, arithmetic and copies ran while one was open for 8% -> 1% of each run, Pallas kernels for 0% -> 4%
where the time goes in v6:
time: 128 us; the launch traced here: 127 us
  starting transfers between devices  58.5 us (46%)
  waiting for transfers between devices  34.1 us (27%)
  Pallas kernels  25.9 us (20%)
  local copies, waits for them, and re-layouts  6.18 us (5%)
  between operations  1.73 us (1%)
    ppermute x48, starting transfers between devices, hop(): return lax.ppermute(value, 'term', pairs)  56.6 us
    ppermute x48, waiting for transfers between devices, hop(): return lax.ppermute(value, 'term', pairs)  29 us
    pallas_call x2, Pallas kernels, apply_blocks(): pl.pallas_call(functools.partial(blocks_kernel, first, sectors, rows, ent...  16.2 us
    pallas_call x3, Pallas kernels, davidson_step(): pl.pallas_call(functools.partial(step_kernel, s, entries), in_specs=[SMEM...  6.41 us
    unnamed x16, local copies, waits for them, and re-layouts  6.18 us
    ppermute x24, waiting for transfers between devices, flip(): return lax.ppermute(value, 'term', [(i, i ^ 1) for i in range(16)])  5.14 us
  transfers between devices with their start and end apart: 72, of which 34 were waited for; matrix products, arithmetic and copies ran while one was open for 1% of the time, Pallas kernels for 4%

profile of v6, /device:TPU:0, one launch (start us, length us, event | category | flops | bytes accessed | tf_op | source)
XLA Modules:
  0.0 127.2 jit_solution(15209554292032133583)
XLA Ops:
  2.0 2.6 %collective-permute-start = (bf16[1,16,1024]{2,1,0:T(8,128)(2,1)S(1)}, bf16[1,16,1024]{2,1,0:T(8,128)(2,1)S(1)}, u32[]{:S(2)}, u32[]{:S(2)}) collective-permute-start(bf16[1,16,1024]{2,1,0:T(8,128)(2,1)S(1)} %get-tuple-element.33.refs_0_.refs_1_), channel_id=1, source_target_pairs={{0,4},{1,3},{4,8},{5,1},{8,12},{9,5},{12,14},{13,9},{14,10},{15,13... | collective-permute-start | bytes 98312 | tf_op jit(solution)/shard_map/ppermute | solution.py:444
  6.3 1.6 %collective-permute-start.8 = (bf16[1,16,1024]{2,1,0:T(8,128)(2,1)S(1)}, bf16[1,16,1024]{2,1,0:T(8,128)(2,1)S(1)}, u32[]{:S(2)}, u32[]{:S(2)}) collective-permute-start(bf16[1,16,1024]{2,1,0:T(8,128)(2,1)S(1)} %get-tuple-element.35.refs_2_.refs_15_), channel_id=1, source_target_pairs={{0,4},{1,3},{4,8},{5,1},{8,12},{9,5},{12,14},{13,9},{14,10},{15,13... | collective-permute-start | bytes 98312 | tf_op jit(solution)/shard_map/ppermute | solution.py:444
  7.9 1.6 %collective-permute-start.2 = (bf16[2,16,1024]{2,1,0:T(8,128)(2,1)S(1)}, bf16[2,16,1024]{2,1,0:T(8,128)(2,1)S(1)}, u32[]{:S(2)}, u32[]{:S(2)}) collective-permute-start(bf16[2,16,1024]{2,1,0:T(8,128)(2,1)S(1)} %shard_map.95), channel_id=1, source_target_pairs={{0,4},{1,3},{4,8},{5,1},{8,12},{9,5},{12,14},{13,9},{14,10},{15,13... | collective-permute-start | bytes 196616 | tf_op jit(solution)/shard_map/ppermute | solution.py:444
  10.3 1.6 %collective-permute-start.10 = (bf16[2,16,1024]{2,1,0:T(8,128)(2,1)S(1)}, bf16[2,16,1024]{2,1,0:T(8,128)(2,1)S(1)}, u32[]{:S(2)}, u32[]{:S(2)}) collective-permute-start(bf16[2,16,1024]{2,1,0:T(8,128)(2,1)S(1)} %shard_map.97), channel_id=1, source_target_pairs={{0,4},{1,3},{4,8},{5,1},{8,12},{9,5},{12,14},{13,9},{14,10},{15,13... | collective-permute-start | bytes 196616 | tf_op jit(solution)/shard_map/ppermute | solution.py:444
  12.2 1.5 %collective-permute-start.3 = (bf16[2,16,1024]{2,1,0:T(8,128)(2,1)S(1)}, bf16[2,16,1024]{2,1,0:T(8,128)(2,1)S(1)}, u32[]{:S(2)}, u32[]{:S(2)}) collective-permute-start(bf16[2,16,1024]{2,1,0:T(8,128)(2,1)S(1)} %collective-permute-done.2.refs_1_.refs_3_), channel_id=1, source_target_pairs={{0,4},{1,3},{4,8},{5,1},{8,12},{9,5},{12,14},{13,9},{14,10},{15,13... | collective-permute-start | bytes 196616 | tf_op jit(solution)/shard_map/ppermute | solution.py:444
  14.6 1.6 %collective-permute-start.11 = (bf16[2,16,1024]{2,1,0:T(8,128)(2,1)S(1)}, bf16[2,16,1024]{2,1,0:T(8,128)(2,1)S(1)}, u32[]{:S(2)}, u32[]{:S(2)}) collective-permute-start(bf16[2,16,1024]{2,1,0:T(8,128)(2,1)S(1)} %collective-permute-done.10.refs_7_.refs_17_), channel_id=1, source_target_pairs={{0,4},{1,3},{4,8},{5,1},{8,12},{9,5},{12,14},{13,9},{14,10},{15,13... | collective-permute-start | bytes 196616 | tf_op jit(solution)/shard_map/ppermute | solution.py:444
  16.4 1.6 %collective-permute-done.7.refs_5_.refs_11_ = bf16[2,16,1024]{2,1,0:T(8,128)(2,1)S(1)} collective-permute-done((bf16[2,16,1024]{2,1,0:T(8,128)(2,1)S(1)}, bf16[2,16,1024]{2,1,0:T(8,128)(2,1)S(1)}, u32[]{:S(2)}, u32[]{:S(2)}) %collective-permute-start.7) | collective-permute-done | bytes 65568 | tf_op jit(solution)/shard_map/ppermute | solution.py:444
  19.0 1.6 %collective-permute-start.13 = (bf16[2,16,1024]{2,1,0:T(8,128)(2,1)S(1)}, bf16[2,16,1024]{2,1,0:T(8,128)(2,1)S(1)}, u32[]{:S(2)}, u32[]{:S(2)}) collective-permute-start(bf16[2,16,1024]{2,1,0:T(8,128)(2,1)S(1)} %collective-permute-done.3.refs_2_.refs_4_), channel_id=1, source_target_pairs={{0,4},{1,3},{4,8},{5,1},{8,12},{9,5},{12,14},{13,9},{14,10},{15,13... | collective-permute-start | bytes 196616 | tf_op jit(solution)/shard_map/ppermute | solution.py:444
  20.6 1.5 %collective-permute-start.15 = (bf16[2,16,1024]{2,1,0:T(8,128)(2,1)S(1)}, bf16[2,16,1024]{2,1,0:T(8,128)(2,1)S(1)}, u32[]{:S(2)}, u32[]{:S(2)}) collective-permute-start(bf16[2,16,1024]{2,1,0:T(8,128)(2,1)S(1)} %collective-permute-done.7.refs_5_.refs_11_), channel_id=1, source_target_pairs={{0,4},{1,3},{4,8},{5,1},{8,12},{9,5},{12,14},{13,9},{14,10},{15,13... | collective-permute-start | bytes 196616 | tf_op jit(solution)/shard_map/ppermute | solution.py:444
  24.9 1.5 %collective-permute-done.17.refs_19_ = bf16[2,16,1024]{2,1,0:T(8,128)(2,1)S(1)} collective-permute-done((bf16[2,16,1024]{2,1,0:T(8,128)(2,1)S(1)}, bf16[2,16,1024]{2,1,0:T(8,128)(2,1)S(1)}, u32[]{:S(2)}, u32[]{:S(2)}) %collective-permute-start.17) | collective-permute-done | bytes 65568 | tf_op jit(solution)/shard_map/ppermute | solution.py:444
  28.1 2.2 %copy-done.4 = bf16[8,512,512]{2,1,0:T(8,128)(2,1)S(1)} copy-done((bf16[8,512,512]{2,1,0:T(8,128)(2,1)S(1)}, bf16[8,512,512]{2,1,0:T(8,128)(2,1)}, u32[]{:S(2)}) %copy-start.4) | copy-done | bytes 4194328
  30.3 2.2 %copy-done.6 = bf16[8,512,512]{2,1,0:T(8,128)(2,1)S(1)} copy-done((bf16[8,512,512]{2,1,0:T(8,128)(2,1)S(1)}, bf16[8,512,512]{2,1,0:T(8,128)(2,1)}, u32[]{:S(2)}) %copy-start.6) | copy-done | bytes 4194328
  32.5 8.1 %shard_map.100 = (f32[3,512,512]{2,1,0:T(8,128)S(1)}, bf16[1,16,3200]{2,1,0:T(8,128)(2,1)S(1)}, bf16[7,16,3200]{2,1,0:T(8,128)(2,1)S(1)}, f32[8,128]{1,0:T(8,128)S(1)}, f32[1]{0:T(128)}) custom-call(s32[1]{0:T(128)} %bitcast.me_ref, s32[17]{0:T(128)S(1)} %pad_add_fusion.ints_ref, bf16[15,16,1024]{2,1,0:T(8,128)(2,1)S(1)} %collective-permute-done.12.refs_0_, ...), custom_call_target="tpu_custom_call" | custom-call | flops 4294967296 | bytes 8388608 | tf_op jit(solution)/shard_map/pallas_call | solution.py:273
  42.9 3.2 %collective-permute-done.21.refs_2_ = bf16[1,16,1152]{2,1,0:T(8,128)(2,1)S(1)} collective-permute-done((bf16[1,16,1152]{2,1,0:T(8,128)(2,1)S(1)}, bf16[1,16,1152]{2,1,0:T(8,128)(2,1)S(1)}, u32[]{:S(2)}, u32[]{:S(2)}) %collective-permute-start.21) | collective-permute-done | bytes 36896 | tf_op jit(solution)/shard_map/ppermute | solution.py:444
  47.2 2.4 %collective-permute-start.39 = (bf16[1,16,1024]{2,1,0:T(8,128)(2,1)S(1)}, bf16[1,16,1024]{2,1,0:T(8,128)(2,1)S(1)}, u32[]{:S(2)}, u32[]{:S(2)}) collective-permute-start(bf16[1,16,1024]{2,1,0:T(8,128)(2,1)S(1)} %shard_map.113), channel_id=1, source_target_pairs={{0,4},{1,3},{4,8},{5,1},{8,12},{9,5},{12,14},{13,9},{14,10},{15,13... | collective-permute-start | bytes 98312 | tf_op jit(solution)/shard_map/ppermute | solution.py:444
  51.8 1.8 %collective-permute-start.40 = (bf16[2,16,1024]{2,1,0:T(8,128)(2,1)S(1)}, bf16[2,16,1024]{2,1,0:T(8,128)(2,1)S(1)}, u32[]{:S(2)}, u32[]{:S(2)}) collective-permute-start(bf16[2,16,1024]{2,1,0:T(8,128)(2,1)S(1)} %shard_map.114), channel_id=1, source_target_pairs={{0,4},{1,3},{4,8},{5,1},{8,12},{9,5},{12,14},{13,9},{14,10},{15,13... | collective-permute-start | bytes 196616 | tf_op jit(solution)/shard_map/ppermute | solution.py:444
  56.2 1.8 %collective-permute-start.41 = (bf16[2,16,1024]{2,1,0:T(8,128)(2,1)S(1)}, bf16[2,16,1024]{2,1,0:T(8,128)(2,1)S(1)}, u32[]{:S(2)}, u32[]{:S(2)}) collective-permute-start(bf16[2,16,1024]{2,1,0:T(8,128)(2,1)S(1)} %shard_map.115), channel_id=1, source_target_pairs={{0,4},{1,3},{4,8},{5,1},{8,12},{9,5},{12,14},{13,9},{14,10},{15,13... | collective-permute-start | bytes 196616 | tf_op jit(solution)/shard_map/ppermute | solution.py:444
  60.5 1.8 %collective-permute-start.42 = (bf16[2,16,1024]{2,1,0:T(8,128)(2,1)S(1)}, bf16[2,16,1024]{2,1,0:T(8,128)(2,1)S(1)}, u32[]{:S(2)}, u32[]{:S(2)}) collective-permute-start(bf16[2,16,1024]{2,1,0:T(8,128)(2,1)S(1)} %shard_map.116), channel_id=1, source_target_pairs={{0,4},{1,3},{4,8},{5,1},{8,12},{9,5},{12,14},{13,9},{14,10},{15,13... | collective-permute-start | bytes 196616 | tf_op jit(solution)/shard_map/ppermute | solution.py:444
  62.5 1.5 %collective-permute-done.33.refs_2_ = bf16[2,16,1024]{2,1,0:T(8,128)(2,1)S(1)} collective-permute-done((bf16[2,16,1024]{2,1,0:T(8,128)(2,1)S(1)}, bf16[2,16,1024]{2,1,0:T(8,128)(2,1)S(1)}, u32[]{:S(2)}, u32[]{:S(2)}) %collective-permute-start.33) | collective-permute-done | bytes 65568 | tf_op jit(solution)/shard_map/ppermute | solution.py:444
  64.9 2.0 %shard_map.105 = (f32[32,512]{1,0:T(8,128)S(1)}, f32[32,512]{1,0:T(8,128)S(1)}, bf16[1,16,1024]{2,1,0:T(8,128)(2,1)S(1)}, f32[8,128]{1,0:T(8,128)S(1)}, f32[1]{0:T(128)}) custom-call(s32[1]{0:T(128)} %bitcast.me_ref, f32[1]{0:T(128)} %get-tuple-element.36.scale_ref.refs_4_.refs_22_, bf16[3,32,512]{2,1,0:T(8,128)(2,1)S(1)} %copy-done.1, ...), custom_call_target="tpu_custom_call" | custom-call | tf_op jit(solution)/shard_map/pallas_call | solution.py:388
  66.9 2.4 %shard_map.111 = (f32[32,512]{1,0:T(8,128)S(1)}, f32[32,512]{1,0:T(8,128)S(1)}, bf16[1,16,1024]{2,1,0:T(8,128)(2,1)S(1)}, f32[8,128]{1,0:T(8,128)S(1)}, f32[1]{0:T(128)}) custom-call(s32[1]{0:T(128)} %bitcast.me_ref, f32[1]{0:T(128)} %get-tuple-element.36.scale_ref.refs_4_.refs_22_, bf16[3,32,512]{2,1,0:T(8,128)(2,1)S(1)} %copy-done.1, ...), custom_call_target="tpu_custom_call" | custom-call | tf_op jit(solution)/shard_map/pallas_call | solution.py:388
  69.3 2.0 %shard_map.117 = (f32[32,512]{1,0:T(8,128)S(1)}, f32[32,512]{1,0:T(8,128)S(1)}, bf16[1,16,1152]{2,1,0:T(8,128)(2,1)S(1)}, f32[8,128]{1,0:T(8,128)}, f32[1]{0:T(128)}) custom-call(s32[1]{0:T(128)} %bitcast.me_ref, f32[1]{0:T(128)} %get-tuple-element.36.scale_ref.refs_4_.refs_22_, bf16[3,32,512]{2,1,0:T(8,128)(2,1)S(1)} %copy-done.1, ...), custom_call_target="tpu_custom_call" | custom-call | tf_op jit(solution)/shard_map/pallas_call | solution.py:388
  71.9 1.7 %collective-permute-start.44 = (bf16[1,16,1152]{2,1,0:T(8,128)(2,1)S(1)}, bf16[1,16,1152]{2,1,0:T(8,128)(2,1)S(1)}, u32[]{:S(2)}, u32[]{:S(2)}) collective-permute-start(bf16[1,16,1152]{2,1,0:T(8,128)(2,1)S(1)} %get-tuple-element.49.refs_15_), channel_id=1, source_target_pairs={{0,4},{1,3},{4,8},{5,1},{8,12},{9,5},{12,14},{13,9},{14,10},{15,13... | collective-permute-start | bytes 110600 | tf_op jit(solution)/shard_map/ppermute | solution.py:444
  75.9 1.7 %collective-permute-start.46 = (bf16[2,16,1152]{2,1,0:T(8,128)(2,1)S(1)}, bf16[2,16,1152]{2,1,0:T(8,128)(2,1)S(1)}, u32[]{:S(2)}, u32[]{:S(2)}) collective-permute-start(bf16[2,16,1152]{2,1,0:T(8,128)(2,1)S(1)} %shard_map.118), channel_id=1, source_target_pairs={{0,4},{1,3},{4,8},{5,1},{8,12},{9,5},{12,14},{13,9},{14,10},{15,13... | collective-permute-start | bytes 221192 | tf_op jit(solution)/shard_map/ppermute | solution.py:444
  80.3 1.6 %collective-permute-start.47 = (bf16[2,16,1152]{2,1,0:T(8,128)(2,1)S(1)}, bf16[2,16,1152]{2,1,0:T(8,128)(2,1)S(1)}, u32[]{:S(2)}, u32[]{:S(2)}) collective-permute-start(bf16[2,16,1152]{2,1,0:T(8,128)(2,1)S(1)} %collective-permute-done.46.refs_7_.refs_17_), channel_id=1, source_target_pairs={{0,4},{1,3},{4,8},{5,1},{8,12},{9,5},{12,14},{13,9},{14,10},{15,13... | collective-permute-start | bytes 221192 | tf_op jit(solution)/shard_map/ppermute | solution.py:444
  84.1 2.1 %collective-permute-done.38.refs_5_.refs_11_ = bf16[2,16,1024]{2,1,0:T(8,128)(2,1)S(1)} collective-permute-done((bf16[2,16,1024]{2,1,0:T(8,128)(2,1)S(1)}, bf16[2,16,1024]{2,1,0:T(8,128)(2,1)S(1)}, u32[]{:S(2)}, u32[]{:S(2)}) %collective-permute-start.38) | collective-permute-done | bytes 65568 | tf_op jit(solution)/shard_map/ppermute | solution.py:444
  95.0 8.1 %shard_map.120 = (f32[3,512,512]{2,1,0:T(8,128)S(1)}, bf16[1,16,3200]{2,1,0:T(8,128)(2,1)S(1)}, bf16[7,16,3200]{2,1,0:T(8,128)(2,1)S(1)}, f32[8,128]{1,0:T(8,128)S(1)}, f32[1]{0:T(128)}) custom-call(s32[1]{0:T(128)} %bitcast.me_ref, s32[17]{0:T(128)S(1)} %pad_add_fusion.ints_ref, bf16[15,16,1152]{2,1,0:T(8,128)(2,1)S(1)} %collective-permute-done.48.refs_0_, ...), custom_call_target="tpu_custom_call" | custom-call | flops 4294967296 | bytes 8388608 | tf_op jit(solution)/shard_map/pallas_call | solution.py:273
  105.6 1.9 %collective-permute-start.67 = (bf16[1,16,1024]{2,1,0:T(8,128)(2,1)S(1)}, bf16[1,16,1024]{2,1,0:T(8,128)(2,1)S(1)}, u32[]{:S(2)}, u32[]{:S(2)}) collective-permute-start(bf16[1,16,1024]{2,1,0:T(8,128)(2,1)S(1)} %shard_map.129), channel_id=1, source_target_pairs={{0,4},{1,3},{4,8},{5,1},{8,12},{9,5},{12,14},{13,9},{14,10},{15,13... | collective-permute-start | bytes 98312 | tf_op jit(solution)/shard_map/ppermute | solution.py:444
  111.6 1.5 %collective-permute-done.58.refs_2_ = bf16[2,16,1152]{2,1,0:T(8,128)(2,1)S(1)} collective-permute-done((bf16[2,16,1152]{2,1,0:T(8,128)(2,1)S(1)}, bf16[2,16,1152]{2,1,0:T(8,128)(2,1)S(1)}, u32[]{:S(2)}, u32[]{:S(2)}) %collective-permute-start.58) | collective-permute-done | bytes 73760 | tf_op jit(solution)/shard_map/ppermute | solution.py:444
  116.1 1.5 %collective-permute-done.59.refs_2_ = bf16[2,16,1152]{2,1,0:T(8,128)(2,1)S(1)} collective-permute-done((bf16[2,16,1152]{2,1,0:T(8,128)(2,1)S(1)}, bf16[2,16,1152]{2,1,0:T(8,128)(2,1)S(1)}, u32[]{:S(2)}, u32[]{:S(2)}) %collective-permute-start.59) | collective-permute-done | bytes 73760 | tf_op jit(solution)/shard_map/ppermute | solution.py:444
  120.6 1.5 %collective-permute-done.60.refs_8_ = bf16[2,16,1152]{2,1,0:T(8,128)(2,1)S(1)} collective-permute-done((bf16[2,16,1152]{2,1,0:T(8,128)(2,1)S(1)}, bf16[2,16,1152]{2,1,0:T(8,128)(2,1)S(1)}, u32[]{:S(2)}, u32[]{:S(2)}) %collective-permute-start.60) | collective-permute-done | bytes 73760 | tf_op jit(solution)/shard_map/ppermute | solution.py:444
  124.8 2.4 %shard_map.133 = (f32[3,32,512]{2,1,0:T(8,128)}, f32[3,32,512]{2,1,0:T(8,128)}, f32[3,32,512]{2,1,0:T(8,128)}) custom-call(s32[1]{0:T(128)} %bitcast.me_ref, f32[1]{0:T(128)} %get-tuple-element.53.along_ref, f32[1]{0:T(128)} %get-tuple-element.36.scale_ref.refs_4_.refs_22_, bf16[3,32,512]{2,1,0:T(8,128)(2,1)S(1)} %copy-done.1, ...), custom_call_target="tpu_custom_call" | custom-call | tf_op jit(solution)/shard_map/pallas_call | solution.py:425
  (169 shorter events, 53.5 us)
Async XLA Ops:
  1.5 4.7 %collective-permute-start.1 = (bf16[1,16,1024]{2,1,0:T(8,128)(2,1)S(1)}, bf16[1,16,1024]{2,1,0:T(8,128)(2,1)S(1)}, u32[]{:S(2)}, u32[]{:S(2)}) collective-permute-start(bf16[1,16,1024]{2,1,0:T(8,128)(2,1)S(1)} %get-tuple-element.33.refs_0_.refs_1_), channel_id=1, source_target_pairs={{0,1},{1,0},{2,3},{3,2},{4,5},{5,4},{6,7},{7,6},{8,9},{9,8},{10,11... | collective-permute-start | bytes 98312 | tf_op jit(solution)/shard_map/ppermute | solution.py:435
  2.0 5.8 %collective-permute-start = (bf16[1,16,1024]{2,1,0:T(8,128)(2,1)S(1)}, bf16[1,16,1024]{2,1,0:T(8,128)(2,1)S(1)}, u32[]{:S(2)}, u32[]{:S(2)}) collective-permute-start(bf16[1,16,1024]{2,1,0:T(8,128)(2,1)S(1)} %get-tuple-element.33.refs_0_.refs_1_), channel_id=1, source_target_pairs={{0,4},{1,3},{4,8},{5,1},{8,12},{9,5},{12,14},{13,9},{14,10},{15,13... | collective-permute-start | bytes 98312 | tf_op jit(solution)/shard_map/ppermute | solution.py:444
  4.7 4.8 %collective-permute-start.5 = (bf16[1,16,1024]{2,1,0:T(8,128)(2,1)S(1)}, bf16[1,16,1024]{2,1,0:T(8,128)(2,1)S(1)}, u32[]{:S(2)}, u32[]{:S(2)}) collective-permute-start(bf16[1,16,1024]{2,1,0:T(8,128)(2,1)S(1)} %get-tuple-element.34.refs_1_.refs_8_), channel_id=1, source_target_pairs={{0,1},{1,0},{2,3},{3,2},{4,5},{5,4},{6,7},{7,6},{8,9},{9,8},{10,11... | collective-permute-start | bytes 98312 | tf_op jit(solution)/shard_map/ppermute | solution.py:435
  4.8 4.6 %collective-permute-start.4 = (bf16[1,16,1024]{2,1,0:T(8,128)(2,1)S(1)}, bf16[1,16,1024]{2,1,0:T(8,128)(2,1)S(1)}, u32[]{:S(2)}, u32[]{:S(2)}) collective-permute-start(bf16[1,16,1024]{2,1,0:T(8,128)(2,1)S(1)} %get-tuple-element.34.refs_1_.refs_8_), channel_id=1, source_target_pairs={{0,4},{1,3},{4,8},{5,1},{8,12},{9,5},{12,14},{13,9},{14,10},{15,13... | collective-permute-start | bytes 98312 | tf_op jit(solution)/shard_map/ppermute | solution.py:444
  7.9 4.3 %collective-permute-start.2 = (bf16[2,16,1024]{2,1,0:T(8,128)(2,1)S(1)}, bf16[2,16,1024]{2,1,0:T(8,128)(2,1)S(1)}, u32[]{:S(2)}, u32[]{:S(2)}) collective-permute-start(bf16[2,16,1024]{2,1,0:T(8,128)(2,1)S(1)} %shard_map.95), channel_id=1, source_target_pairs={{0,4},{1,3},{4,8},{5,1},{8,12},{9,5},{12,14},{13,9},{14,10},{15,13... | collective-permute-start | bytes 196616 | tf_op jit(solution)/shard_map/ppermute | solution.py:444
  9.4 4.3 %collective-permute-start.6 = (bf16[2,16,1024]{2,1,0:T(8,128)(2,1)S(1)}, bf16[2,16,1024]{2,1,0:T(8,128)(2,1)S(1)}, u32[]{:S(2)}, u32[]{:S(2)}) collective-permute-start(bf16[2,16,1024]{2,1,0:T(8,128)(2,1)S(1)} %shard_map.96), channel_id=1, source_target_pairs={{0,4},{1,3},{4,8},{5,1},{8,12},{9,5},{12,14},{13,9},{14,10},{15,13... | collective-permute-start | bytes 196616 | tf_op jit(solution)/shard_map/ppermute | solution.py:444
  10.3 4.3 %collective-permute-start.10 = (bf16[2,16,1024]{2,1,0:T(8,128)(2,1)S(1)}, bf16[2,16,1024]{2,1,0:T(8,128)(2,1)S(1)}, u32[]{:S(2)}, u32[]{:S(2)}) collective-permute-start(bf16[2,16,1024]{2,1,0:T(8,128)(2,1)S(1)} %shard_map.97), channel_id=1, source_target_pairs={{0,4},{1,3},{4,8},{5,1},{8,12},{9,5},{12,14},{13,9},{14,10},{15,13... | collective-permute-start | bytes 196616 | tf_op jit(solution)/shard_map/ppermute | solution.py:444
  18.9 9.2 %collective-permute-start.12 = (bf16[15,16,1024]{2,1,0:T(8,128)(2,1)S(1)}, bf16[15,16,1024]{2,1,0:T(8,128)(2,1)S(1)}, u32[]{:S(2)}, u32[]{:S(2)}) collective-permute-start(bf16[15,16,1024]{2,1,0:T(8,128)(2,1)S(1)} %shard_map.98), channel_id=1, source_target_pairs={{0,1},{1,0},{2,3},{3,2},{4,5},{5,4},{6,7},{7,6},{8,9},{9,8},{10,11... | collective-permute-start | bytes 1474568 | tf_op jit(solution)/shard_map/ppermute | solution.py:435
  19.0 4.4 %collective-permute-start.13 = (bf16[2,16,1024]{2,1,0:T(8,128)(2,1)S(1)}, bf16[2,16,1024]{2,1,0:T(8,128)(2,1)S(1)}, u32[]{:S(2)}, u32[]{:S(2)}) collective-permute-start(bf16[2,16,1024]{2,1,0:T(8,128)(2,1)S(1)} %collective-permute-done.3.refs_2_.refs_4_), channel_id=1, source_target_pairs={{0,4},{1,3},{4,8},{5,1},{8,12},{9,5},{12,14},{13,9},{14,10},{15,13... | collective-permute-start | bytes 196616 | tf_op jit(solution)/shard_map/ppermute | solution.py:444
  23.4 4.7 %collective-permute-start.14 = (bf16[2,16,1024]{2,1,0:T(8,128)(2,1)S(1)}, bf16[2,16,1024]{2,1,0:T(8,128)(2,1)S(1)}, u32[]{:S(2)}, u32[]{:S(2)}) collective-permute-start(bf16[2,16,1024]{2,1,0:T(8,128)(2,1)S(1)} %collective-permute-done.13.refs_5_), channel_id=1, source_target_pairs={{0,1},{1,0},{2,3},{3,2},{4,5},{5,4},{6,7},{7,6},{8,9},{9,8},{10,11... | collective-permute-start | bytes 196616 | tf_op jit(solution)/shard_map/ppermute | solution.py:435
  46.2 7.3 %collective-permute-start.22 = (bf16[2,16,1152]{2,1,0:T(8,128)(2,1)S(1)}, bf16[2,16,1152]{2,1,0:T(8,128)(2,1)S(1)}, u32[]{:S(2)}, u32[]{:S(2)}) collective-permute-start(bf16[2,16,1152]{2,1,0:T(8,128)(2,1)S(1)} %shard_map.102), channel_id=1, source_target_pairs={{0,4},{1,3},{4,8},{5,1},{8,12},{9,5},{12,14},{13,9},{14,10},{15,13... | collective-permute-start | bytes 221192 | tf_op jit(solution)/shard_map/ppermute | solution.py:444
  47.2 4.6 %collective-permute-start.39 = (bf16[1,16,1024]{2,1,0:T(8,128)(2,1)S(1)}, bf16[1,16,1024]{2,1,0:T(8,128)(2,1)S(1)}, u32[]{:S(2)}, u32[]{:S(2)}) collective-permute-start(bf16[1,16,1024]{2,1,0:T(8,128)(2,1)S(1)} %shard_map.113), channel_id=1, source_target_pairs={{0,4},{1,3},{4,8},{5,1},{8,12},{9,5},{12,14},{13,9},{14,10},{15,13... | collective-permute-start | bytes 98312 | tf_op jit(solution)/shard_map/ppermute | solution.py:444
  51.8 4.3 %collective-permute-start.40 = (bf16[2,16,1024]{2,1,0:T(8,128)(2,1)S(1)}, bf16[2,16,1024]{2,1,0:T(8,128)(2,1)S(1)}, u32[]{:S(2)}, u32[]{:S(2)}) collective-permute-start(bf16[2,16,1024]{2,1,0:T(8,128)(2,1)S(1)} %shard_map.114), channel_id=1, source_target_pairs={{0,4},{1,3},{4,8},{5,1},{8,12},{9,5},{12,14},{13,9},{14,10},{15,13... | collective-permute-start | bytes 196616 | tf_op jit(solution)/shard_map/ppermute | solution.py:444
  53.6 4.4 %collective-permute-start.23 = (bf16[2,16,1152]{2,1,0:T(8,128)(2,1)S(1)}, bf16[2,16,1152]{2,1,0:T(8,128)(2,1)S(1)}, u32[]{:S(2)}, u32[]{:S(2)}) collective-permute-start(bf16[2,16,1152]{2,1,0:T(8,128)(2,1)S(1)} %shard_map.103), channel_id=1, source_target_pairs={{0,4},{1,3},{4,8},{5,1},{8,12},{9,5},{12,14},{13,9},{14,10},{15,13... | collective-permute-start | bytes 221192 | tf_op jit(solution)/shard_map/ppermute | solution.py:444
  56.2 4.3 %collective-permute-start.41 = (bf16[2,16,1024]{2,1,0:T(8,128)(2,1)S(1)}, bf16[2,16,1024]{2,1,0:T(8,128)(2,1)S(1)}, u32[]{:S(2)}, u32[]{:S(2)}) collective-permute-start(bf16[2,16,1024]{2,1,0:T(8,128)(2,1)S(1)} %shard_map.115), channel_id=1, source_target_pairs={{0,4},{1,3},{4,8},{5,1},{8,12},{9,5},{12,14},{13,9},{14,10},{15,13... | collective-permute-start | bytes 196616 | tf_op jit(solution)/shard_map/ppermute | solution.py:444
  58.1 4.4 %collective-permute-start.24 = (bf16[2,16,1152]{2,1,0:T(8,128)(2,1)S(1)}, bf16[2,16,1152]{2,1,0:T(8,128)(2,1)S(1)}, u32[]{:S(2)}, u32[]{:S(2)}) collective-permute-start(bf16[2,16,1152]{2,1,0:T(8,128)(2,1)S(1)} %shard_map.104), channel_id=1, source_target_pairs={{0,4},{1,3},{4,8},{5,1},{8,12},{9,5},{12,14},{13,9},{14,10},{15,13... | collective-permute-start | bytes 221192 | tf_op jit(solution)/shard_map/ppermute | solution.py:444
  59.7 4.3 %collective-permute-start.33 = (bf16[2,16,1024]{2,1,0:T(8,128)(2,1)S(1)}, bf16[2,16,1024]{2,1,0:T(8,128)(2,1)S(1)}, u32[]{:S(2)}, u32[]{:S(2)}) collective-permute-start(bf16[2,16,1024]{2,1,0:T(8,128)(2,1)S(1)} %shard_map.110), channel_id=1, source_target_pairs={{0,4},{1,3},{4,8},{5,1},{8,12},{9,5},{12,14},{13,9},{14,10},{15,13... | collective-permute-start | bytes 196616 | tf_op jit(solution)/shard_map/ppermute | solution.py:444
  64.8 4.5 %collective-permute-start.43 = (bf16[2,16,1024]{2,1,0:T(8,128)(2,1)S(1)}, bf16[2,16,1024]{2,1,0:T(8,128)(2,1)S(1)}, u32[]{:S(2)}, u32[]{:S(2)}) collective-permute-start(bf16[2,16,1024]{2,1,0:T(8,128)(2,1)S(1)} %collective-permute-done.42.refs_2_), channel_id=1, source_target_pairs={{0,1},{1,0},{2,3},{3,2},{4,5},{5,4},{6,7},{7,6},{8,9},{9,8},{10,11... | collective-permute-start | bytes 196616 | tf_op jit(solution)/shard_map/ppermute | solution.py:435
  75.9 4.4 %collective-permute-start.46 = (bf16[2,16,1152]{2,1,0:T(8,128)(2,1)S(1)}, bf16[2,16,1152]{2,1,0:T(8,128)(2,1)S(1)}, u32[]{:S(2)}, u32[]{:S(2)}) collective-permute-start(bf16[2,16,1152]{2,1,0:T(8,128)(2,1)S(1)} %shard_map.118), channel_id=1, source_target_pairs={{0,4},{1,3},{4,8},{5,1},{8,12},{9,5},{12,14},{13,9},{14,10},{15,13... | collective-permute-start | bytes 221192 | tf_op jit(solution)/shard_map/ppermute | solution.py:444
  77.6 4.3 %collective-permute-start.37 = (bf16[2,16,1024]{2,1,0:T(8,128)(2,1)S(1)}, bf16[2,16,1024]{2,1,0:T(8,128)(2,1)S(1)}, u32[]{:S(2)}, u32[]{:S(2)}) collective-permute-start(bf16[2,16,1024]{2,1,0:T(8,128)(2,1)S(1)} %shard_map.112), channel_id=1, source_target_pairs={{0,4},{1,3},{4,8},{5,1},{8,12},{9,5},{12,14},{13,9},{14,10},{15,13... | collective-permute-start | bytes 196616 | tf_op jit(solution)/shard_map/ppermute | solution.py:444
  80.3 6.9 %collective-permute-start.47 = (bf16[2,16,1152]{2,1,0:T(8,128)(2,1)S(1)}, bf16[2,16,1152]{2,1,0:T(8,128)(2,1)S(1)}, u32[]{:S(2)}, u32[]{:S(2)}) collective-permute-start(bf16[2,16,1152]{2,1,0:T(8,128)(2,1)S(1)} %collective-permute-done.46.refs_7_.refs_17_), channel_id=1, source_target_pairs={{0,4},{1,3},{4,8},{5,1},{8,12},{9,5},{12,14},{13,9},{14,10},{15,13... | collective-permute-start | bytes 221192 | tf_op jit(solution)/shard_map/ppermute | solution.py:444
  87.3 7.7 %collective-permute-start.48 = (bf16[15,16,1152]{2,1,0:T(8,128)(2,1)S(1)}, bf16[15,16,1152]{2,1,0:T(8,128)(2,1)S(1)}, u32[]{:S(2)}, u32[]{:S(2)}) collective-permute-start(bf16[15,16,1152]{2,1,0:T(8,128)(2,1)S(1)} %shard_map.119), channel_id=1, source_target_pairs={{0,1},{1,0},{2,3},{3,2},{4,5},{5,4},{6,7},{7,6},{8,9},{9,8},{10,11... | collective-permute-start | bytes 1658888 | tf_op jit(solution)/shard_map/ppermute | solution.py:435
  87.3 4.4 %collective-permute-start.53 = (bf16[2,16,1152]{2,1,0:T(8,128)(2,1)S(1)}, bf16[2,16,1152]{2,1,0:T(8,128)(2,1)S(1)}, u32[]{:S(2)}, u32[]{:S(2)}) collective-permute-start(bf16[2,16,1152]{2,1,0:T(8,128)(2,1)S(1)} %collective-permute-done.47.refs_8_.refs_18_), channel_id=1, source_target_pairs={{0,4},{1,3},{4,8},{5,1},{8,12},{9,5},{12,14},{13,9},{14,10},{15,13... | collective-permute-start | bytes 221192 | tf_op jit(solution)/shard_map/ppermute | solution.py:444
  105.6 4.5 %collective-permute-start.67 = (bf16[1,16,1024]{2,1,0:T(8,128)(2,1)S(1)}, bf16[1,16,1024]{2,1,0:T(8,128)(2,1)S(1)}, u32[]{:S(2)}, u32[]{:S(2)}) collective-permute-start(bf16[1,16,1024]{2,1,0:T(8,128)(2,1)S(1)} %shard_map.129), channel_id=1, source_target_pairs={{0,4},{1,3},{4,8},{5,1},{8,12},{9,5},{12,14},{13,9},{14,10},{15,13... | collective-permute-start | bytes 98312 | tf_op jit(solution)/shard_map/ppermute | solution.py:444
  108.7 4.4 %collective-permute-start.58 = (bf16[2,16,1152]{2,1,0:T(8,128)(2,1)S(1)}, bf16[2,16,1152]{2,1,0:T(8,128)(2,1)S(1)}, u32[]{:S(2)}, u32[]{:S(2)}) collective-permute-start(bf16[2,16,1152]{2,1,0:T(8,128)(2,1)S(1)} %shard_map.122), channel_id=1, source_target_pairs={{0,4},{1,3},{4,8},{5,1},{8,12},{9,5},{12,14},{13,9},{14,10},{15,13... | collective-permute-start | bytes 221192 | tf_op jit(solution)/shard_map/ppermute | solution.py:444
  109.6 4.4 %collective-permute-start.63 = (bf16[2,16,1024]{2,1,0:T(8,128)(2,1)S(1)}, bf16[2,16,1024]{2,1,0:T(8,128)(2,1)S(1)}, u32[]{:S(2)}, u32[]{:S(2)}) collective-permute-start(bf16[2,16,1024]{2,1,0:T(8,128)(2,1)S(1)} %shard_map.126), channel_id=1, source_target_pairs={{0,4},{1,3},{4,8},{5,1},{8,12},{9,5},{12,14},{13,9},{14,10},{15,13... | collective-permute-start | bytes 196616 | tf_op jit(solution)/shard_map/ppermute | solution.py:444
  110.2 4.6 %collective-permute-start.68 = (bf16[2,16,1024]{2,1,0:T(8,128)(2,1)S(1)}, bf16[2,16,1024]{2,1,0:T(8,128)(2,1)S(1)}, u32[]{:S(2)}, u32[]{:S(2)}) collective-permute-start(bf16[2,16,1024]{2,1,0:T(8,128)(2,1)S(1)} %shard_map.130), channel_id=1, source_target_pairs={{0,4},{1,3},{4,8},{5,1},{8,12},{9,5},{12,14},{13,9},{14,10},{15,13... | collective-permute-start | bytes 196616 | tf_op jit(solution)/shard_map/ppermute | solution.py:444
  113.2 4.4 %collective-permute-start.59 = (bf16[2,16,1152]{2,1,0:T(8,128)(2,1)S(1)}, bf16[2,16,1152]{2,1,0:T(8,128)(2,1)S(1)}, u32[]{:S(2)}, u32[]{:S(2)}) collective-permute-start(bf16[2,16,1152]{2,1,0:T(8,128)(2,1)S(1)} %shard_map.123), channel_id=1, source_target_pairs={{0,4},{1,3},{4,8},{5,1},{8,12},{9,5},{12,14},{13,9},{14,10},{15,13... | collective-permute-start | bytes 221192 | tf_op jit(solution)/shard_map/ppermute | solution.py:444
  114.1 4.4 %collective-permute-start.64 = (bf16[2,16,1024]{2,1,0:T(8,128)(2,1)S(1)}, bf16[2,16,1024]{2,1,0:T(8,128)(2,1)S(1)}, u32[]{:S(2)}, u32[]{:S(2)}) collective-permute-start(bf16[2,16,1024]{2,1,0:T(8,128)(2,1)S(1)} %shard_map.127), channel_id=1, source_target_pairs={{0,4},{1,3},{4,8},{5,1},{8,12},{9,5},{12,14},{13,9},{14,10},{15,13... | collective-permute-start | bytes 196616 | tf_op jit(solution)/shard_map/ppermute | solution.py:444
  114.8 4.4 %collective-permute-start.69 = (bf16[2,16,1024]{2,1,0:T(8,128)(2,1)S(1)}, bf16[2,16,1024]{2,1,0:T(8,128)(2,1)S(1)}, u32[]{:S(2)}, u32[]{:S(2)}) collective-permute-start(bf16[2,16,1024]{2,1,0:T(8,128)(2,1)S(1)} %shard_map.131), channel_id=1, source_target_pairs={{0,4},{1,3},{4,8},{5,1},{8,12},{9,5},{12,14},{13,9},{14,10},{15,13... | collective-permute-start | bytes 196616 | tf_op jit(solution)/shard_map/ppermute | solution.py:444
  117.6 4.4 %collective-permute-start.60 = (bf16[2,16,1152]{2,1,0:T(8,128)(2,1)S(1)}, bf16[2,16,1152]{2,1,0:T(8,128)(2,1)S(1)}, u32[]{:S(2)}, u32[]{:S(2)}) collective-permute-start(bf16[2,16,1152]{2,1,0:T(8,128)(2,1)S(1)} %shard_map.124), channel_id=1, source_target_pairs={{0,4},{1,3},{4,8},{5,1},{8,12},{9,5},{12,14},{13,9},{14,10},{15,13... | collective-permute-start | bytes 221192 | tf_op jit(solution)/shard_map/ppermute | solution.py:444
  119.2 4.3 %collective-permute-start.70 = (bf16[2,16,1024]{2,1,0:T(8,128)(2,1)S(1)}, bf16[2,16,1024]{2,1,0:T(8,128)(2,1)S(1)}, u32[]{:S(2)}, u32[]{:S(2)}) collective-permute-start(bf16[2,16,1024]{2,1,0:T(8,128)(2,1)S(1)} %shard_map.132), channel_id=1, source_target_pairs={{0,4},{1,3},{4,8},{5,1},{8,12},{9,5},{12,14},{13,9},{14,10},{15,13... | collective-permute-start | bytes 196616 | tf_op jit(solution)/shard_map/ppermute | solution.py:444
  (48 other events, 215.6 us)

commit v7 on v0

--- a/solution.py
+++ b/solution.py
@@ -1,7 +1,441 @@
+import functools
+
 import jax
 import jax.numpy as jnp
 from jax import lax
+from jax.experimental import pallas as pl
+from jax.experimental.pallas import tpu as pltpu
 from jax.sharding import PartitionSpec as P
+
+VMEM = pl.BlockSpec(memory_space=pltpu.VMEM)
+SMEM = pl.BlockSpec(memory_space=pltpu.SMEM)
+HBM = pl.BlockSpec(memory_space=pltpu.HBM)
+PARAMS = pltpu.CompilerParams(vmem_limit_bytes=48 * 1024 * 1024)
+HALF = 16
+LANES = 128
+
+
+def fold(value):
+    rows, width = value.shape
+    summed = jnp.sum(value.reshape(rows // 8, 8, width), axis=0)
+    return sum(summed[:, k * 128 : (k + 1) * 128] for k in range(width // 128))
+
+
+def down(value):
+    return jnp.sum(value, axis=0, keepdims=True)
+
+
+def halves(rows, width, start=0):
+    for h in range(rows // HALF):
+        yield h * HALF, slice(start + h * width, start + (h + 1) * width)
+
+
+def write_lanes(ref, at, lanes):
+    whole = jnp.broadcast_to(lanes, (HALF, LANES))
+    high = whole.astype(jnp.bfloat16).astype(jnp.float32)
+    rest = whole - high
+    middle = rest.astype(jnp.bfloat16).astype(jnp.float32)
+    low = rest - middle
+    row = lax.broadcasted_iota(jnp.int32, whole.shape, 0)
+    value = jnp.where(row == 0, high, jnp.where(row == 1, middle, jnp.where(row == 2, low, 0.0)))
+    ref[:, at : at + LANES] = value.astype(jnp.bfloat16)
+
+
+def read_lanes(ref, at):
+    return down(ref[:, at : at + LANES].astype(jnp.float32))
+
+
+def chip_at(place):
+    place = lax.rem(place + 8, 8)
+    return jnp.where(place < 4, 2 * place, 15 - 2 * place)
+
+
+def ring_place(me):
+    chip, core = me // 2, me % 2
+    place = jnp.where(chip % 2 == 0, chip // 2, (15 - chip) // 2)
+    return place, core
+
+
+def ahead(me, distance, half, core=None):
+    place, own = ring_place(me)
+    core = own if core is None else core
+    return chip_at(place + (1 - 2 * core) * distance) * 2 + half
+
+
+ROUNDS = 4
+
+
+def sent_devices(me, core):
+    devices = []
+    for k in range(ROUNDS):
+        for half in (core, 1 - core):
+            devices.append(ahead(me, ROUNDS - 1 - k + core, half, core))
+    return devices
+
+
+def gathered_devices(me):
+    core = me % 2
+    devices = [ahead(me, 0, core), ahead(me, 0, 1 - core)]
+    for k in (1, 2, 3):
+        devices += [ahead(me, -k, core), ahead(me, -k, 1 - core)]
+        devices += [ahead(me, k, 1 - core), ahead(me, k, core)]
+    return devices + [ahead(me, 4, 1), ahead(me, 4, 0)]
+
+
+def message_parts(sectors, rows, width):
+    for s in range(sectors):
+        for row, part in halves(rows, width, s * (rows // HALF) * width):
+            yield s, row, part
+
+
+def message_shape(sectors, rows, width):
+    return (HALF, rows // HALF * sectors * width + LANES)
+
+
+def prepare_kernel(wave_ref, diag_ref, _, own_ref, square_ref):
+    own_ref[...] = wave_ref[...]
+    square = jnp.zeros((8, 128), jnp.float32)
+    for s in range(wave_ref.shape[0]):
+        wave = wave_ref[s].astype(jnp.float32)
+        square += fold(diag_ref[s].astype(jnp.float32) * wave * wave)
+    square_ref[...] = square
+
+
+def prepare(wave, diag, after):
+    return pl.pallas_call(
+        prepare_kernel,
+        in_specs=[VMEM, VMEM, HBM],
+        out_specs=[VMEM, VMEM],
+        out_shape=[
+            jax.ShapeDtypeStruct(wave.shape, wave.dtype),
+            jax.ShapeDtypeStruct((8, 128), jnp.float32),
+        ],
+        compiler_params=PARAMS,
+    )(wave, diag, after)
+
+
+def blocks_kernel(first, shape, entries, me_ref, ints_ref, *refs):
+    sectors, rows, width = shape
+    field_refs, refs = refs[:18], refs[18:]
+    if first:
+        square_ref, *refs = refs
+    else:
+        scale_ref, wave_ref, correction_ref, *refs = refs
+    left_hbm, right_hbm, *refs = refs
+    total, near_ref, far_ref, dot_ref, out_ref, left, right, field, left_sem, right_sem = refs
+    slots = left.shape[0]
+
+    def copies(slot):
+        return (
+            pltpu.make_async_copy(left_hbm.at[slot], left.at[slot], left_sem.at[slot]),
+            pltpu.make_async_copy(right_hbm.at[slot], right.at[slot], right_sem.at[slot]),
+        )
+
+    for slot in range(slots):
+        for copy in copies(slot):
+            copy.start()
+
+    me = me_ref[0]
+    core = me % 2
+
+    def read(k, part):
+        if k < 14:
+            return field_refs[k][part]
+        return jnp.where(core == 1, field_refs[k][part], field_refs[k + 2][part])
+
+    pieces = []
+    for k, owner in enumerate(gathered_devices(me)):
+        at = pl.multiple_of(owner * rows, rows)
+        if first:
+            for s in range(sectors):
+                pieces.append((k, (s,), s, pl.ds(at, rows)))
+        else:
+            for s, row, part in message_parts(sectors, rows, width):
+                pieces.append((k, (slice(None), part), s, pl.ds(at + row, HALF)))
+
+    total[...] = jnp.zeros_like(total)
+    if first:
+        dot = jnp.zeros((8, 128), jnp.float32)
+        for k, part, _, _ in pieces:
+            value = read(k, part).astype(jnp.float32)
+            dot += fold(value * value)
+        scale = jnp.sqrt(jnp.sum(dot) / entries)
+        inverse = 1.0 / scale
+        out_ref[...] = jnp.full(out_ref.shape, scale, jnp.float32)
+        for k, part, s, at in pieces:
+            field[s, at, :] = (read(k, part).astype(jnp.float32) * inverse).astype(jnp.bfloat16)
+    else:
+        for k, part, s, at in pieces:
+            field[s, at, :] = read(k, part)
+
+    used = ints_ref[2 * slots]
+
+    def add_pair(step, carry):
+        one, two = 2 * step, 2 * step + 1
+        for slot in (one, two):
+            for copy in copies(slot):
+                copy.wait()
+
+        @pl.when(one < used)
+        def _():
+            products = [
+                jnp.dot(
+                    left[slot], field[ints_ref[slot]], preferred_element_type=jnp.float32
+                ).astype(jnp.bfloat16)
+                for slot in (one, two)
+            ]
+            products[1] = jnp.where(two < used, products[1], jnp.zeros_like(products[1]))
+            for slot, product in zip((one, two), products):
+                total[ints_ref[slots + slot]] += lax.dot_general(
+                    product,
+                    right[slot],
+                    (((1,), (1,)), ((), ())),
+                    preferred_element_type=jnp.float32,
+                )
+
+        return carry
+
+    lax.fori_loop(0, slots // 2, add_pair, 0)
+
+    dot = jnp.zeros((8, 128), jnp.float32)
+    if first:
+        for k, part, s, at in pieces:
+            dot += fold(total[s, at, :] * read(k, part).astype(jnp.float32))
+        dot = dot * inverse + square_ref[...] * inverse * inverse
+    else:
+        at = message_shape(*shape)[1] - LANES
+        lanes = sum(
+            read(k, (slice(None), slice(at, at + LANES))).astype(jnp.float32) for k in range(16)
+        )
+        along = jnp.sum(lanes) / entries
+        out_ref[...] = jnp.full(out_ref.shape, along, jnp.float32)
+        inverse = 1.0 / scale_ref[0:1, 0:1]
+        for s in range(sectors):
+            projected = correction_ref[s] - along * (wave_ref[s].astype(jnp.float32) * inverse)
+            dot += fold(projected * projected)
+    dot_ref[...] = dot
+    lanes = down(dot)
+    for k, owner in enumerate(sent_devices(me, 1 - core)):
+        at = pl.multiple_of(owner * rows, rows)
+        ref = near_ref.at[k] if k < near_ref.shape[0] else far_ref.at[k - near_ref.shape[0]]
+        for s, row, part in message_parts(*shape):
+            ref[:, part] = total[s, pl.ds(at + row, HALF), :].astype(jnp.bfloat16)
+        write_lanes(ref, ref.shape[1] - LANES, lanes)
+
+
+def apply_blocks(me, ints, fields, own, left, right, shape, first, entries):
+    slots, order, width = left.shape
+    sectors = shape[0]
+    message = message_shape(*shape)
+    return pl.pallas_call(
+        functools.partial(blocks_kernel, first, shape, entries),
+        in_specs=[SMEM, SMEM] + [VMEM] * (len(fields) + len(own)) + [HBM] * 2,
+        out_specs=[VMEM] * 5,
+        scratch_shapes=[
+            pltpu.VMEM(left.shape, left.dtype),
+            pltpu.VMEM(right.shape, right.dtype),
+            pltpu.VMEM((sectors, order, width), jnp.bfloat16),
+            pltpu.SemaphoreType.DMA((slots,)),
+            pltpu.SemaphoreType.DMA((slots,)),
+        ],
+        out_shape=[
+            jax.ShapeDtypeStruct((sectors, order, width), jnp.float32),
+            jax.ShapeDtypeStruct((2, *message), jnp.bfloat16),
+            jax.ShapeDtypeStruct((2 * ROUNDS - 2, *message), jnp.bfloat16),
+            jax.ShapeDtypeStruct((8, 128), jnp.float32),
+            jax.ShapeDtypeStruct((8, 128), jnp.float32),
+        ],
+        compiler_params=PARAMS,
+        cost_estimate=pl.CostEstimate(
+            flops=4 * slots * order * order * width,
+            bytes_accessed=4 * slots * order * order,
+            transcendentals=0,
+        ),
+    )(me, ints, *fields, *own, left, right)
+
+
+def chain_kernel(shape, k, index, me_ref, total_ref, dot_ref, other_ref, *refs):
+    *arrived_refs, out_ref = refs
+    _, rows, _ = shape
+    me = me_ref[0]
+    start = pl.multiple_of(sent_devices(me, me % 2)[k] * rows, rows)
+    for s, row, part in message_parts(*shape):
+        value = total_ref[s, pl.ds(start + row, HALF), :]
+        value += other_ref[index, :, part].astype(jnp.float32)
+        for ref in arrived_refs:
+            value += ref[:, part].astype(jnp.float32)
+        out_ref[:, part] = value.astype(jnp.bfloat16)
+    at = out_ref.shape[1] - LANES
+    lanes = down(dot_ref[...]) + read_lanes(other_ref.at[index], at)
+    for ref in arrived_refs:
+        lanes += read_lanes(ref, at)
+    write_lanes(out_ref, at, lanes)
+
+
+def chain(shape, k, index, me, total, dot, other, *arrived):
+    return pl.pallas_call(
+        functools.partial(chain_kernel, shape, k, index),
+        in_specs=[SMEM] + [VMEM] * (3 + len(arrived)),
+        out_specs=VMEM,
+        out_shape=jax.ShapeDtypeStruct(message_shape(*shape), jnp.bfloat16),
+        compiler_params=PARAMS,
+    )(me, total, dot, other, *arrived)
+
+
+def pick_kernel(me_ref, even_ref, odd_ref, out_ref):
+    out_ref[...] = jnp.where(me_ref[0] % 2 == 0, even_ref[...], odd_ref[...])
+
+
+def pick(me, even, odd):
+    return pl.pallas_call(
+        pick_kernel,
+        in_specs=[SMEM, VMEM, VMEM],
+        out_specs=VMEM,
+        out_shape=jax.ShapeDtypeStruct(even.shape, even.dtype),
+        compiler_params=PARAMS,
+    )(me, even, odd)
+
+
+def own_terms(shape, sector, ours, theirs):
+    values = []
+    for s, _, part in message_parts(*shape):
+        if s == sector:
+            values.append(ours[:, part].astype(jnp.float32) + theirs[:, part].astype(jnp.float32))
+    return jnp.concatenate(values, axis=0)
+
+
+def own_scalar(ours, theirs):
+    at = ours.shape[1] - LANES
+    return jnp.sum(read_lanes(ours, at) + read_lanes(theirs, at))
+
+
+def step_kernel(entries, scale_ref, wave_ref, diag_ref, ours_ref, theirs_ref, *refs):
+    first_ref, terms_ref, correction_ref, message_ref = refs
+    shape = wave_ref.shape
+    ritz = own_scalar(ours_ref, theirs_ref) / entries
+    inverse = 1.0 / scale_ref[0:1, 0:1]
+    dots = jnp.zeros((8, 128), jnp.float32)
+    for s in range(shape[0]):
+        start = wave_ref[s].astype(jnp.float32) * inverse
+        diag = diag_ref[s].astype(jnp.float32)
+        terms = own_terms(shape, s, ours_ref, theirs_ref)
+        first = terms + diag * start
+        correction = (first - ritz * start) / jnp.maximum(jnp.abs(diag - ritz), 1.0)
+        first_ref[s] = first
+        terms_ref[s] = terms
+        correction_ref[s] = correction
+        dots += fold(start * correction)
+        for t, row, part in message_parts(*shape):
+            if t == s:
+                message_ref[:, part] = correction[row : row + HALF].astype(jnp.bfloat16)
+    write_lanes(message_ref, message_ref.shape[1] - LANES, down(dots))
+
+
+def davidson_step(scale, wave, diag, sums, entries):
+    full = jax.ShapeDtypeStruct(wave.shape, jnp.float32)
+    return pl.pallas_call(
+        functools.partial(step_kernel, entries),
+        in_specs=[VMEM] * 5,
+        out_specs=[VMEM] * 4,
+        out_shape=[full, full, full, jax.ShapeDtypeStruct(message_shape(*wave.shape), jnp.bfloat16)],
+        compiler_params=PARAMS,
+    )(scale, wave, diag, *sums)
+
+
+def finish_kernel(entries, along_ref, scale_ref, wave_ref, diag_ref, *refs):
+    terms_ref, correction_ref, ours_ref, theirs_ref, vector_ref, image_ref = refs
+    shape = wave_ref.shape
+    along = along_ref[0:1, 0:1]
+    norm = jnp.sqrt(jnp.full((1, 1), own_scalar(ours_ref, theirs_ref) / entries, jnp.float32))
+    inverse = 1.0 / norm
+    start_scale = 1.0 / scale_ref[0:1, 0:1]
+    for s in range(shape[0]):
+        start = wave_ref[s].astype(jnp.float32) * start_scale
+        second = (correction_ref[s] - along * start) * inverse
+        vector_ref[s] = second
+        image = (own_terms(shape, s, ours_ref, theirs_ref) - along * terms_ref[s]) * inverse
+        image_ref[s] = image + diag_ref[s].astype(jnp.float32) * second
+
+
+def finish(along, scale, wave, diag, terms, correction, sums, entries):
+    full = jax.ShapeDtypeStruct(wave.shape, jnp.float32)
+    return pl.pallas_call(
+        functools.partial(finish_kernel, entries),
+        in_specs=[VMEM] * 8,
+        out_specs=[VMEM] * 2,
+        out_shape=[full, full],
+        compiler_params=PARAMS,
+    )(along, scale, wave, diag, terms, correction, *sums)
+
+
+def flip(value):
+    return lax.ppermute(value, "term", [(i, i ^ 1) for i in range(16)])
+
+
+def down_core(value):
+    return lax.ppermute(value, "term", [(i, i - 1) for i in range(1, 16, 2)])
+
+
+def hop(value, cores=(0, 1)):
+    order = [0, 2, 4, 6, 7, 5, 3, 1]
+    pairs = []
+    for place in range(8):
+        for core in cores:
+            there = order[(place + 1 - 2 * core) % 8]
+            pairs.append((order[place] * 2 + core, there * 2 + core))
+    return lax.ppermute(value, "term", pairs)
+
+
+def gather(own):
+    one, two = own, flip(own)
+    pieces = [one, two]
+    for _ in (1, 2, 3):
+        one, two = hop(one), hop(two)
+        pieces += [one, two, flip(one), flip(two)]
+    one, two = hop(one, (1,)), hop(two, (1,))
+    return pieces + [one, two, down_core(one), down_core(two)], two
+
+
+def scatter(shape, me, total, near, far, dot):
+    near = flip(near)
+    near, far = lax.optimization_barrier((near, far))
+    far = flip(far)
+    one = hop(chain(shape, 0, 0, me, total, dot, near))
+    two = hop(chain(shape, 1, 1, me, total, dot, near))
+    for k in (2, 4):
+        one = hop(chain(shape, k, k - 2, me, total, dot, far, one))
+        two = hop(chain(shape, k + 1, k - 1, me, total, dot, far, two))
+    one = chain(shape, 6, 4, me, total, dot, far, one)
+    two = chain(shape, 7, 5, me, total, dot, far, two)
+    one = pick(me, one, hop(one, (1,)))
+    two = pick(me, two, hop(two, (1,)))
+    return one, flip(two)
+
+
+def on_ring(
+    wavefunction, diagonal, left_blocks, right_blocks, block_source, block_target, live_count
+):
+    shape = wavefunction.shape
+    sectors, rows, width = shape
+    entries = float(sectors * rows * lax.axis_size("term") * width)
+    me = lax.axis_index("term").astype(jnp.int32).reshape(1)
+    ints = jnp.concatenate([block_source, block_target, live_count])
+    blocks = (left_blocks, right_blocks, shape)
+
+    fields, last = gather(wavefunction)
+    fields[0], square = prepare(wavefunction, diagonal, last)
+    total, near, far, dot, scale = apply_blocks(me, ints, fields, (square,), *blocks, True, entries)
+    first_image, terms, correction, message = davidson_step(
+        scale, wavefunction, diagonal, scatter(shape, me, total, near, far, dot), entries
+    )
+    fields, _ = gather(message)
+    own = (scale, wavefunction, correction)
+    total, near, far, dot, along = apply_blocks(me, ints, fields, own, *blocks, False, entries)
+    second_vector, second_image = finish(
+        along, scale, wavefunction, diagonal, terms, correction,
+        scatter(shape, me, total, near, far, dot), entries,
+    )
+    return (first_image, second_vector, second_image)
 
 
 def block_loop(field_rounded, left_ops, right_ops, sources, targets, last_slot, partial_sum):
@@ -20,7 +454,7 @@
     return lax.fori_loop(0, last_slot, add_block, partial_sum)
 
 
-def on_device(
+def on_any(
     wavefunction, diagonal, left_blocks, right_blocks, block_source, block_target, live_count
 ):
     devices = lax.axis_size("term")
@@ -77,6 +511,7 @@
         P(("grp", "term")),
         P(("grp", "term")),
     )
+    on_device = on_ring if mesh.shape["term"] == 16 else on_any
     return jax.shard_map(
         on_device,
         mesh=mesh,

time: 421 us -> 111 us (0.26)
  waiting for transfers between devices: 270 us -> 35.5 us
  starting transfers between devices: 0.15 us -> 51.5 us
  loops' own time: 46.9 us -> 0 us
  matrix products: 29.2 us -> 0 us
  local copies, waits for them, and re-layouts: 30.6 us -> 1.8 us
  other arithmetic: 25.2 us -> 0.75 us
  Pallas kernels: 0 us -> 19 us
  between operations: 16.5 us -> 1.68 us
    psum x1 -> x0, waiting for transfers between devices: 132 us -> none  [on_device(): first_whole = lax.psum(first_terms, 'term') + whole_diag * start_whole]
    reduce_scatter x1 -> x0, waiting for transfers between devices: 92.5 us -> none  [on_device(): lax.psum_scatter(second_terms, 'term', scatter_dimension=1, tiled=True)]
    ppermute x0 -> x56, starting transfers between devices: none -> 51.5 us  [the longest x32 34.6 us: hop(): return lax.ppermute(value, 'term', pairs)]
    another operation x2 -> x0, loops' own time: 46.9 us -> none  [block_loop(): return lax.fori_loop(0, last_slot, add_block, partial_sum)]
    all_gather x2 -> x0, waiting for transfers between devices: 43.9 us -> none  [the longest x1 43.9 us: on_device(): lax.all_gather(wavefunction, 'term', axis=1, tiled=True).astype(jnp.float32)]
    ppermute x0 -> x56, waiting for transfers between devices: none -> 35.5 us  [the longest x32 29.3 us: hop(): return lax.ppermute(value, 'term', pairs)]
    dot_general x10 -> x0, matrix products: 29.2 us -> none  [add_block(): jnp.dot(product, right_op.T, preferred_element_type=jnp.float32)]
    dynamic_slice x31 -> x0, local copies, waits for them, and re-layouts: 26.4 us -> none  [the longest x10 13 us: add_block(): before = lax.dynamic_index_in_dim(running, target, 0, keepdims=False)]
  transfers between devices with their start and end apart: 4 -> 56, of which waited for: 3 -> 24; matrix products, arithmetic and copies ran while one was open for 8% -> 1% of each run, Pallas kernels for 0% -> 1%
where the time goes in v7:
time: 111 us; the launch traced here: 110 us
  starting transfers between devices  51.5 us (46%)
  waiting for transfers between devices  35.5 us (32%)
  Pallas kernels  19 us (17%)
  local copies, waits for them, and re-layouts  1.8 us (2%)
  between operations  1.68 us (2%)
    ppermute x32, starting transfers between devices, hop(): return lax.ppermute(value, 'term', pairs)  34.6 us
    ppermute x32, waiting for transfers between devices, hop(): return lax.ppermute(value, 'term', pairs)  29.3 us
    pallas_call x2, Pallas kernels, apply_blocks(): pl.pallas_call(functools.partial(blocks_kernel, first, shape, entries), i...  16.2 us
    ppermute x20, starting transfers between devices, flip(): return lax.ppermute(value, 'term', [(i, i ^ 1) for i in range(16)])  11.8 us
    ppermute x4, starting transfers between devices, down_core(): return lax.ppermute(value, 'term', [(i, i - 1) for i in range(1, 16, 2)])  5.15 us
    ppermute x20, waiting for transfers between devices, flip(): return lax.ppermute(value, 'term', [(i, i ^ 1) for i in range(16)])  4.28 us
  transfers between devices with their start and end apart: 56, of which 24 were waited for; matrix products, arithmetic and copies ran while one was open for 1% of the time, Pallas kernels for 1%

profile of v7, /device:TPU:0, one launch (start us, length us, event | category | flops | bytes accessed | tf_op | source)
XLA Modules:
  0.0 110.2 jit_solution(5982284013120096912)
XLA Ops:
  1.1 2.6 %collective-permute-start.5 = (bf16[3,32,512]{2,1,0:T(8,128)(2,1)}, bf16[3,32,512]{2,1,0:T(8,128)(2,1)S(1)}, u32[]{:S(2)}, u32[]{:S(2)}) collective-permute-start(bf16[3,32,512]{2,1,0:T(8,128)(2,1)} %wave_ref.5), channel_id=1, source_target_pairs={{0,4},{1,3},{4,8},{5,1},{8,12},{9,5},{12,14},{13,9},{14,10},{15,13... | collective-permute-start | bytes 294920 | tf_op jit(solution)/shard_map/ppermute | solution.py:386
  3.8 1.6 %collective-permute-start.1 = (bf16[3,32,512]{2,1,0:T(8,128)(2,1)S(1)}, bf16[3,32,512]{2,1,0:T(8,128)(2,1)S(1)}, u32[]{:S(2)}, u32[]{:S(2)}) collective-permute-start(bf16[3,32,512]{2,1,0:T(8,128)(2,1)S(1)} %collective-permute-done.refs_1_), channel_id=1, source_target_pairs={{0,4},{1,3},{4,8},{5,1},{8,12},{9,5},{12,14},{13,9},{14,10},{15,13... | collective-permute-start | bytes 294920 | tf_op jit(solution)/shard_map/ppermute | solution.py:386
  5.4 1.2 %collective-permute-done.5.refs_2_ = bf16[3,32,512]{2,1,0:T(8,128)(2,1)S(1)} collective-permute-done((bf16[3,32,512]{2,1,0:T(8,128)(2,1)}, bf16[3,32,512]{2,1,0:T(8,128)(2,1)S(1)}, u32[]{:S(2)}, u32[]{:S(2)}) %collective-permute-start.5) | collective-permute-done | bytes 98336 | tf_op jit(solution)/shard_map/ppermute | solution.py:386
  6.5 2.1 %collective-permute-start.8 = (bf16[3,32,512]{2,1,0:T(8,128)(2,1)S(1)}, bf16[3,32,512]{2,1,0:T(8,128)(2,1)S(1)}, u32[]{:S(2)}, u32[]{:S(2)}) collective-permute-start(bf16[3,32,512]{2,1,0:T(8,128)(2,1)S(1)} %collective-permute-done.5.refs_2_), channel_id=1, source_target_pairs={{0,4},{1,3},{4,8},{5,1},{8,12},{9,5},{12,14},{13,9},{14,10},{15,13... | collective-permute-start | bytes 294920 | tf_op jit(solution)/shard_map/ppermute | solution.py:386
  8.6 1.6 %collective-permute-start.2 = (bf16[3,32,512]{2,1,0:T(8,128)(2,1)S(1)}, bf16[3,32,512]{2,1,0:T(8,128)(2,1)S(1)}, u32[]{:S(2)}, u32[]{:S(2)}) collective-permute-start(bf16[3,32,512]{2,1,0:T(8,128)(2,1)S(1)} %collective-permute-done.1.refs_3_), channel_id=1, source_target_pairs={{0,4},{1,3},{4,8},{5,1},{8,12},{9,5},{12,14},{13,9},{14,10},{15,13... | collective-permute-start | bytes 294920 | tf_op jit(solution)/shard_map/ppermute | solution.py:386
  11.2 2.1 %collective-permute-start.11 = (bf16[3,32,512]{2,1,0:T(8,128)(2,1)S(1)}, bf16[3,32,512]{2,1,0:T(8,128)(2,1)S(1)}, u32[]{:S(2)}, u32[]{:S(2)}) collective-permute-start(bf16[3,32,512]{2,1,0:T(8,128)(2,1)S(1)} %collective-permute-done.8.refs_6_), channel_id=1, source_target_pairs={{0,4},{1,3},{4,8},{5,1},{8,12},{9,5},{12,14},{13,9},{14,10},{15,13... | collective-permute-start | bytes 294920 | tf_op jit(solution)/shard_map/ppermute | solution.py:386
  13.2 1.6 %collective-permute-start.3 = (bf16[3,32,512]{2,1,0:T(8,128)(2,1)S(1)}, bf16[3,32,512]{2,1,0:T(8,128)(2,1)S(1)}, u32[]{:S(2)}, u32[]{:S(2)}) collective-permute-start(bf16[3,32,512]{2,1,0:T(8,128)(2,1)S(1)} %collective-permute-done.2.refs_7_), channel_id=1, source_target_pairs={{0,4},{1,3},{4,8},{5,1},{8,12},{9,5},{12,14},{13,9},{14,10},{15,13... | collective-permute-start | bytes 294920 | tf_op jit(solution)/shard_map/ppermute | solution.py:386
  16.4 1.4 %collective-permute-done.3.refs_11_ = bf16[3,32,512]{2,1,0:T(8,128)(2,1)S(1)} collective-permute-done((bf16[3,32,512]{2,1,0:T(8,128)(2,1)S(1)}, bf16[3,32,512]{2,1,0:T(8,128)(2,1)S(1)}, u32[]{:S(2)}, u32[]{:S(2)}) %collective-permute-start.3) | collective-permute-done | bytes 98336 | tf_op jit(solution)/shard_map/ppermute | solution.py:386
  19.2 2.3 %collective-permute-start.12 = (bf16[3,32,512]{2,1,0:T(8,128)(2,1)S(1)}, bf16[3,32,512]{2,1,0:T(8,128)(2,1)S(1)}, u32[]{:S(2)}, u32[]{:S(2)}) collective-permute-start(bf16[3,32,512]{2,1,0:T(8,128)(2,1)S(1)} %collective-permute-done.11.refs_10_), channel_id=1, source_target_pairs={{0,1},{1,0},{2,3},{3,2},{4,5},{5,4},{6,7},{7,6},{8,9},{9,8},{10,11... | collective-permute-start | bytes 294920 | tf_op jit(solution)/shard_map/ppermute | solution.py:372
  22.0 1.3 %collective-permute-start.15 = (bf16[3,32,512]{2,1,0:T(8,128)(2,1)S(1)}, bf16[3,32,512]{2,1,0:T(8,128)(2,1)S(1)}, u32[]{:S(2)}, u32[]{:S(2)}) collective-permute-start(bf16[3,32,512]{2,1,0:T(8,128)(2,1)S(1)} %collective-permute-done.14.refs_14_), channel_id=1, source_target_pairs={{1,0},{3,2},{5,4},{7,6},{9,8},{11,10},{13,12},{15,14},{17,16},{19,... | collective-permute-start | bytes 294920 | tf_op jit(solution)/shard_map/ppermute | solution.py:376
  23.3 1.3 %collective-permute-start.16 = (bf16[3,32,512]{2,1,0:T(8,128)(2,1)S(1)}, bf16[3,32,512]{2,1,0:T(8,128)(2,1)S(1)}, u32[]{:S(2)}, u32[]{:S(2)}) collective-permute-start(bf16[3,32,512]{2,1,0:T(8,128)(2,1)S(1)} %collective-permute-done.4._.refs_15_), channel_id=1, source_target_pairs={{1,0},{3,2},{5,4},{7,6},{9,8},{11,10},{13,12},{15,14},{17,16},{19,... | collective-permute-start | bytes 294920 | tf_op jit(solution)/shard_map/ppermute | solution.py:376
  27.2 8.5 %shard_map.95 = (f32[3,512,512]{2,1,0:T(8,128)S(1)}, bf16[2,16,3200]{2,1,0:T(8,128)(2,1)S(1)}, bf16[6,16,3200]{2,1,0:T(8,128)(2,1)S(1)}, f32[8,128]{1,0:T(8,128)S(1)}, f32[8,128]{1,0:T(8,128)S(1)}) custom-call(s32[1]{0:T(128)} %bitcast.me_ref, s32[17]{0:T(128)S(1)} %pad_add_fusion.ints_ref, bf16[3,32,512]{2,1,0:T(8,128)(2,1)S(1)} %get-tuple-element.25.refs_0_, ...), custom_call_target="tpu_custom_call" | custom-call | flops 4294967296 | bytes 8388608 | tf_op jit(solution)/shard_map/pallas_call | solution.py:230
  35.7 1.2 %collective-permute-start.17 = (bf16[2,16,3200]{2,1,0:T(8,128)(2,1)S(1)}, bf16[2,16,3200]{2,1,0:T(8,128)(2,1)S(1)}, u32[]{:S(2)}, u32[]{:S(2)}) collective-permute-start(bf16[2,16,3200]{2,1,0:T(8,128)(2,1)S(1)} %get-tuple-element.30), channel_id=1, source_target_pairs={{0,1},{1,0},{2,3},{3,2},{4,5},{5,4},{6,7},{7,6},{8,9},{9,8},{10,11... | collective-permute-start | bytes 614408 | tf_op jit(solution)/shard_map/ppermute | solution.py:372
  39.4 3.7 %collective-permute-done.23.refs_0_ = bf16[16,3200]{1,0:T(8,128)(2,1)S(1)} collective-permute-done((bf16[16,3200]{1,0:T(8,128)(2,1)S(1)}, bf16[16,3200]{1,0:T(8,128)(2,1)S(1)}, u32[]{:S(2)}, u32[]{:S(2)}) %collective-permute-start.23) | collective-permute-done | bytes 102432 | tf_op jit(solution)/shard_map/ppermute | solution.py:386
  45.2 2.7 %collective-permute-done.24.refs_0_ = bf16[16,3200]{1,0:T(8,128)(2,1)S(1)} collective-permute-done((bf16[16,3200]{1,0:T(8,128)(2,1)S(1)}, bf16[16,3200]{1,0:T(8,128)(2,1)S(1)}, u32[]{:S(2)}, u32[]{:S(2)}) %collective-permute-start.24) | collective-permute-done | bytes 102432 | tf_op jit(solution)/shard_map/ppermute | solution.py:386
  50.0 2.7 %collective-permute-done.25.refs_0_ = bf16[16,3200]{1,0:T(8,128)(2,1)S(1)} collective-permute-done((bf16[16,3200]{1,0:T(8,128)(2,1)S(1)}, bf16[16,3200]{1,0:T(8,128)(2,1)S(1)}, u32[]{:S(2)}, u32[]{:S(2)}) %collective-permute-start.25) | collective-permute-done | bytes 102432 | tf_op jit(solution)/shard_map/ppermute | solution.py:386
  57.1 1.2 %collective-permute-start.28 = (bf16[16,3200]{1,0:T(8,128)(2,1)S(1)}, bf16[16,3200]{1,0:T(8,128)(2,1)S(1)}, u32[]{:S(2)}, u32[]{:S(2)}) collective-permute-start(bf16[16,3200]{1,0:T(8,128)(2,1)S(1)} %get-tuple-element.35.refs_0_), channel_id=1, source_target_pairs={{0,1},{1,0},{2,3},{3,2},{4,5},{5,4},{6,7},{7,6},{8,9},{9,8},{10,11... | collective-permute-start | bytes 307208 | tf_op jit(solution)/shard_map/ppermute | solution.py:372
  58.3 1.5 %collective-permute-start.29 = (bf16[16,3200]{1,0:T(8,128)(2,1)S(1)}, bf16[16,3200]{1,0:T(8,128)(2,1)S(1)}, u32[]{:S(2)}, u32[]{:S(2)}) collective-permute-start(bf16[16,3200]{1,0:T(8,128)(2,1)S(1)} %get-tuple-element.35.refs_0_), channel_id=1, source_target_pairs={{0,4},{1,3},{4,8},{5,1},{8,12},{9,5},{12,14},{13,9},{14,10},{15,13... | collective-permute-start | bytes 307208 | tf_op jit(solution)/shard_map/ppermute | solution.py:386
  60.8 2.2 %collective-permute-done.29.refs_2_ = bf16[16,3200]{1,0:T(8,128)(2,1)S(1)} collective-permute-done((bf16[16,3200]{1,0:T(8,128)(2,1)S(1)}, bf16[16,3200]{1,0:T(8,128)(2,1)S(1)}, u32[]{:S(2)}, u32[]{:S(2)}) %collective-permute-start.29) | collective-permute-done | bytes 102432 | tf_op jit(solution)/shard_map/ppermute | solution.py:386
  63.0 1.5 %collective-permute-start.33 = (bf16[16,3200]{1,0:T(8,128)(2,1)S(1)}, bf16[16,3200]{1,0:T(8,128)(2,1)S(1)}, u32[]{:S(2)}, u32[]{:S(2)}) collective-permute-start(bf16[16,3200]{1,0:T(8,128)(2,1)S(1)} %collective-permute-done.29.refs_2_), channel_id=1, source_target_pairs={{0,4},{1,3},{4,8},{5,1},{8,12},{9,5},{12,14},{13,9},{14,10},{15,13... | collective-permute-start | bytes 307208 | tf_op jit(solution)/shard_map/ppermute | solution.py:386
  65.6 2.0 %collective-permute-done.33.refs_6_ = bf16[16,3200]{1,0:T(8,128)(2,1)S(1)} collective-permute-done((bf16[16,3200]{1,0:T(8,128)(2,1)S(1)}, bf16[16,3200]{1,0:T(8,128)(2,1)S(1)}, u32[]{:S(2)}, u32[]{:S(2)}) %collective-permute-start.33) | collective-permute-done | bytes 102432 | tf_op jit(solution)/shard_map/ppermute | solution.py:386
  67.6 1.5 %collective-permute-start.37 = (bf16[16,3200]{1,0:T(8,128)(2,1)S(1)}, bf16[16,3200]{1,0:T(8,128)(2,1)S(1)}, u32[]{:S(2)}, u32[]{:S(2)}) collective-permute-start(bf16[16,3200]{1,0:T(8,128)(2,1)S(1)} %collective-permute-done.33.refs_6_), channel_id=1, source_target_pairs={{0,4},{1,3},{4,8},{5,1},{8,12},{9,5},{12,14},{13,9},{14,10},{15,13... | collective-permute-start | bytes 307208 | tf_op jit(solution)/shard_map/ppermute | solution.py:386
  70.8 1.5 %collective-permute-done.37.refs_10_ = bf16[16,3200]{1,0:T(8,128)(2,1)S(1)} collective-permute-done((bf16[16,3200]{1,0:T(8,128)(2,1)S(1)}, bf16[16,3200]{1,0:T(8,128)(2,1)S(1)}, u32[]{:S(2)}, u32[]{:S(2)}) %collective-permute-start.37) | collective-permute-done | bytes 102432 | tf_op jit(solution)/shard_map/ppermute | solution.py:386
  74.5 2.0 %collective-permute-start.39 = (bf16[16,3200]{1,0:T(8,128)(2,1)S(1)}, bf16[16,3200]{1,0:T(8,128)(2,1)S(1)}, u32[]{:S(2)}, u32[]{:S(2)}) collective-permute-start(bf16[16,3200]{1,0:T(8,128)(2,1)S(1)} %collective-permute-done.37.refs_10_), channel_id=1, source_target_pairs={{0,1},{1,0},{2,3},{3,2},{4,5},{5,4},{6,7},{7,6},{8,9},{9,8},{10,11... | collective-permute-start | bytes 307208 | tf_op jit(solution)/shard_map/ppermute | solution.py:372
  77.0 1.3 %collective-permute-start.43 = (bf16[16,3200]{1,0:T(8,128)(2,1)S(1)}, bf16[16,3200]{1,0:T(8,128)(2,1)S(1)}, u32[]{:S(2)}, u32[]{:S(2)}) collective-permute-start(bf16[16,3200]{1,0:T(8,128)(2,1)S(1)} %collective-permute-done.41.refs_14_), channel_id=1, source_target_pairs={{1,0},{3,2},{5,4},{7,6},{9,8},{11,10},{13,12},{15,14},{17,16},{19,... | collective-permute-start | bytes 307208 | tf_op jit(solution)/shard_map/ppermute | solution.py:376
  78.3 1.3 %collective-permute-start.44 = (bf16[16,3200]{1,0:T(8,128)(2,1)S(1)}, bf16[16,3200]{1,0:T(8,128)(2,1)S(1)}, u32[]{:S(2)}, u32[]{:S(2)}) collective-permute-start(bf16[16,3200]{1,0:T(8,128)(2,1)S(1)} %collective-permute-done.42.refs_15_), channel_id=1, source_target_pairs={{1,0},{3,2},{5,4},{7,6},{9,8},{11,10},{13,12},{15,14},{17,16},{19,... | collective-permute-start | bytes 307208 | tf_op jit(solution)/shard_map/ppermute | solution.py:376
  80.2 1.3 %collective-permute-done.44.refs_17_ = bf16[16,3200]{1,0:T(8,128)(2,1)S(1)} collective-permute-done((bf16[16,3200]{1,0:T(8,128)(2,1)S(1)}, bf16[16,3200]{1,0:T(8,128)(2,1)S(1)}, u32[]{:S(2)}, u32[]{:S(2)}) %collective-permute-start.44) | collective-permute-done | bytes 102432 | tf_op jit(solution)/shard_map/ppermute | solution.py:376
  81.5 7.7 %shard_map.107 = (f32[3,512,512]{2,1,0:T(8,128)S(1)}, bf16[2,16,3200]{2,1,0:T(8,128)(2,1)S(1)}, bf16[6,16,3200]{2,1,0:T(8,128)(2,1)S(1)}, f32[8,128]{1,0:T(8,128)S(1)}, f32[8,128]{1,0:T(8,128)S(1)}) custom-call(s32[1]{0:T(128)} %bitcast.me_ref, s32[17]{0:T(128)S(1)} %pad_add_fusion.ints_ref, bf16[16,3200]{1,0:T(8,128)(2,1)S(1)} %get-tuple-element.35.refs_0_, ...), custom_call_target="tpu_custom_call" | custom-call | flops 4294967296 | bytes 8388608 | tf_op jit(solution)/shard_map/pallas_call | solution.py:230
  89.5 1.3 %collective-permute-done.45.other_ref = bf16[2,16,3200]{2,1,0:T(8,128)(2,1)S(1)} collective-permute-done((bf16[2,16,3200]{2,1,0:T(8,128)(2,1)S(1)}, bf16[2,16,3200]{2,1,0:T(8,128)(2,1)S(1)}, u32[]{:S(2)}, u32[]{:S(2)}) %collective-permute-start.45) | collective-permute-done | bytes 204832 | tf_op jit(solution)/shard_map/ppermute | solution.py:372
  92.2 3.5 %collective-permute-done.51.refs_0_ = bf16[16,3200]{1,0:T(8,128)(2,1)S(1)} collective-permute-done((bf16[16,3200]{1,0:T(8,128)(2,1)S(1)}, bf16[16,3200]{1,0:T(8,128)(2,1)S(1)}, u32[]{:S(2)}, u32[]{:S(2)}) %collective-permute-start.51) | collective-permute-done | bytes 102432 | tf_op jit(solution)/shard_map/ppermute | solution.py:386
  98.0 2.5 %collective-permute-done.52.refs_0_ = bf16[16,3200]{1,0:T(8,128)(2,1)S(1)} collective-permute-done((bf16[16,3200]{1,0:T(8,128)(2,1)S(1)}, bf16[16,3200]{1,0:T(8,128)(2,1)S(1)}, u32[]{:S(2)}, u32[]{:S(2)}) %collective-permute-start.52) | collective-permute-done | bytes 102432 | tf_op jit(solution)/shard_map/ppermute | solution.py:386
  102.8 2.5 %collective-permute-done.53.refs_0_ = bf16[16,3200]{1,0:T(8,128)(2,1)S(1)} collective-permute-done((bf16[16,3200]{1,0:T(8,128)(2,1)S(1)}, bf16[16,3200]{1,0:T(8,128)(2,1)S(1)}, u32[]{:S(2)}, u32[]{:S(2)}) %collective-permute-start.53) | collective-permute-done | bytes 102432 | tf_op jit(solution)/shard_map/ppermute | solution.py:386
  (114 shorter events, 35.8 us)
Async XLA Ops:
  1.1 5.4 %collective-permute-start.5 = (bf16[3,32,512]{2,1,0:T(8,128)(2,1)}, bf16[3,32,512]{2,1,0:T(8,128)(2,1)S(1)}, u32[]{:S(2)}, u32[]{:S(2)}) collective-permute-start(bf16[3,32,512]{2,1,0:T(8,128)(2,1)} %wave_ref.5), channel_id=1, source_target_pairs={{0,4},{1,3},{4,8},{5,1},{8,12},{9,5},{12,14},{13,9},{14,10},{15,13... | collective-permute-start | bytes 294920 | tf_op jit(solution)/shard_map/ppermute | solution.py:386
  3.8 4.8 %collective-permute-start.1 = (bf16[3,32,512]{2,1,0:T(8,128)(2,1)S(1)}, bf16[3,32,512]{2,1,0:T(8,128)(2,1)S(1)}, u32[]{:S(2)}, u32[]{:S(2)}) collective-permute-start(bf16[3,32,512]{2,1,0:T(8,128)(2,1)S(1)} %collective-permute-done.refs_1_), channel_id=1, source_target_pairs={{0,4},{1,3},{4,8},{5,1},{8,12},{9,5},{12,14},{13,9},{14,10},{15,13... | collective-permute-start | bytes 294920 | tf_op jit(solution)/shard_map/ppermute | solution.py:386
  14.8 6.6 %collective-permute-start.9 = (bf16[3,32,512]{2,1,0:T(8,128)(2,1)S(1)}, bf16[3,32,512]{2,1,0:T(8,128)(2,1)S(1)}, u32[]{:S(2)}, u32[]{:S(2)}) collective-permute-start(bf16[3,32,512]{2,1,0:T(8,128)(2,1)S(1)} %collective-permute-done.8.refs_6_), channel_id=1, source_target_pairs={{0,1},{1,0},{2,3},{3,2},{4,5},{5,4},{6,7},{7,6},{8,9},{9,8},{10,11... | collective-permute-start | bytes 294920 | tf_op jit(solution)/shard_map/ppermute | solution.py:372
  15.3 6.2 %collective-permute-start.7 = (bf16[3,32,512]{2,1,0:T(8,128)(2,1)S(1)}, bf16[3,32,512]{2,1,0:T(8,128)(2,1)S(1)}, u32[]{:S(2)}, u32[]{:S(2)}) collective-permute-start(bf16[3,32,512]{2,1,0:T(8,128)(2,1)S(1)} %collective-permute-done.1.refs_3_), channel_id=1, source_target_pairs={{0,1},{1,0},{2,3},{3,2},{4,5},{5,4},{6,7},{7,6},{8,9},{9,8},{10,11... | collective-permute-start | bytes 294920 | tf_op jit(solution)/shard_map/ppermute | solution.py:372
  15.8 6.2 %collective-permute-start.14 = (bf16[3,32,512]{2,1,0:T(8,128)(2,1)S(1)}, bf16[3,32,512]{2,1,0:T(8,128)(2,1)S(1)}, u32[]{:S(2)}, u32[]{:S(2)}) collective-permute-start(bf16[3,32,512]{2,1,0:T(8,128)(2,1)S(1)} %collective-permute-done.11.refs_10_), channel_id=1, source_target_pairs={{1,3},{5,1},{9,5},{13,9},{15,13},{11,15},{7,11},{3,7},{17,19},{21,... | collective-permute-start | bytes 294920 | tf_op jit(solution)/shard_map/ppermute | solution.py:386
  17.9 5.4 %collective-permute-start.4 = (bf16[3,32,512]{2,1,0:T(8,128)(2,1)S(1)}, bf16[3,32,512]{2,1,0:T(8,128)(2,1)S(1)}, u32[]{:S(2)}, u32[]{:S(2)}) collective-permute-start(bf16[3,32,512]{2,1,0:T(8,128)(2,1)S(1)} %collective-permute-done.3.refs_11_), channel_id=1, source_target_pairs={{1,3},{5,1},{9,5},{13,9},{15,13},{11,15},{7,11},{3,7},{17,19},{21,... | collective-permute-start | bytes 294920 | tf_op jit(solution)/shard_map/ppermute | solution.py:386
  19.2 8.0 %collective-permute-start.12 = (bf16[3,32,512]{2,1,0:T(8,128)(2,1)S(1)}, bf16[3,32,512]{2,1,0:T(8,128)(2,1)S(1)}, u32[]{:S(2)}, u32[]{:S(2)}) collective-permute-start(bf16[3,32,512]{2,1,0:T(8,128)(2,1)S(1)} %collective-permute-done.11.refs_10_), channel_id=1, source_target_pairs={{0,1},{1,0},{2,3},{3,2},{4,5},{5,4},{6,7},{7,6},{8,9},{9,8},{10,11... | collective-permute-start | bytes 294920 | tf_op jit(solution)/shard_map/ppermute | solution.py:372
  21.5 5.7 %collective-permute-start.10 = (bf16[3,32,512]{2,1,0:T(8,128)(2,1)S(1)}, bf16[3,32,512]{2,1,0:T(8,128)(2,1)S(1)}, u32[]{:S(2)}, u32[]{:S(2)}) collective-permute-start(bf16[3,32,512]{2,1,0:T(8,128)(2,1)S(1)} %collective-permute-done.2.refs_7_), channel_id=1, source_target_pairs={{0,1},{1,0},{2,3},{3,2},{4,5},{5,4},{6,7},{7,6},{8,9},{9,8},{10,11... | collective-permute-start | bytes 294920 | tf_op jit(solution)/shard_map/ppermute | solution.py:372
  21.6 5.6 %collective-permute-start.13 = (bf16[3,32,512]{2,1,0:T(8,128)(2,1)S(1)}, bf16[3,32,512]{2,1,0:T(8,128)(2,1)S(1)}, u32[]{:S(2)}, u32[]{:S(2)}) collective-permute-start(bf16[3,32,512]{2,1,0:T(8,128)(2,1)S(1)} %collective-permute-done.3.refs_11_), channel_id=1, source_target_pairs={{0,1},{1,0},{2,3},{3,2},{4,5},{5,4},{6,7},{7,6},{8,9},{9,8},{10,11... | collective-permute-start | bytes 294920 | tf_op jit(solution)/shard_map/ppermute | solution.py:372
  22.0 5.2 %collective-permute-start.15 = (bf16[3,32,512]{2,1,0:T(8,128)(2,1)S(1)}, bf16[3,32,512]{2,1,0:T(8,128)(2,1)S(1)}, u32[]{:S(2)}, u32[]{:S(2)}) collective-permute-start(bf16[3,32,512]{2,1,0:T(8,128)(2,1)S(1)} %collective-permute-done.14.refs_14_), channel_id=1, source_target_pairs={{1,0},{3,2},{5,4},{7,6},{9,8},{11,10},{13,12},{15,14},{17,16},{19,... | collective-permute-start | bytes 294920 | tf_op jit(solution)/shard_map/ppermute | solution.py:376
  38.0 5.1 %collective-permute-start.18 = (bf16[6,16,3200]{2,1,0:T(8,128)(2,1)S(1)}, bf16[6,16,3200]{2,1,0:T(8,128)(2,1)S(1)}, u32[]{:S(2)}, u32[]{:S(2)}) collective-permute-start(bf16[6,16,3200]{2,1,0:T(8,128)(2,1)S(1)} %get-tuple-element.32), channel_id=1, source_target_pairs={{0,1},{1,0},{2,3},{3,2},{4,5},{5,4},{6,7},{7,6},{8,9},{9,8},{10,11... | collective-permute-start | bytes 1843208 | tf_op jit(solution)/shard_map/ppermute | solution.py:372
  38.4 4.7 %collective-permute-start.23 = (bf16[16,3200]{1,0:T(8,128)(2,1)S(1)}, bf16[16,3200]{1,0:T(8,128)(2,1)S(1)}, u32[]{:S(2)}, u32[]{:S(2)}) collective-permute-start(bf16[16,3200]{1,0:T(8,128)(2,1)S(1)} %shard_map.101), channel_id=1, source_target_pairs={{0,4},{1,3},{4,8},{5,1},{8,12},{9,5},{12,14},{13,9},{14,10},{15,13... | collective-permute-start | bytes 307208 | tf_op jit(solution)/shard_map/ppermute | solution.py:386
  39.4 4.9 %collective-permute-start.19 = (bf16[16,3200]{1,0:T(8,128)(2,1)S(1)}, bf16[16,3200]{1,0:T(8,128)(2,1)S(1)}, u32[]{:S(2)}, u32[]{:S(2)}) collective-permute-start(bf16[16,3200]{1,0:T(8,128)(2,1)S(1)} %shard_map.96), channel_id=1, source_target_pairs={{0,4},{1,3},{4,8},{5,1},{8,12},{9,5},{12,14},{13,9},{14,10},{15,13... | collective-permute-start | bytes 307208 | tf_op jit(solution)/shard_map/ppermute | solution.py:386
  43.2 4.7 %collective-permute-start.24 = (bf16[16,3200]{1,0:T(8,128)(2,1)S(1)}, bf16[16,3200]{1,0:T(8,128)(2,1)S(1)}, u32[]{:S(2)}, u32[]{:S(2)}) collective-permute-start(bf16[16,3200]{1,0:T(8,128)(2,1)S(1)} %shard_map.102), channel_id=1, source_target_pairs={{0,4},{1,3},{4,8},{5,1},{8,12},{9,5},{12,14},{13,9},{14,10},{15,13... | collective-permute-start | bytes 307208 | tf_op jit(solution)/shard_map/ppermute | solution.py:386
  44.3 4.7 %collective-permute-start.20 = (bf16[16,3200]{1,0:T(8,128)(2,1)S(1)}, bf16[16,3200]{1,0:T(8,128)(2,1)S(1)}, u32[]{:S(2)}, u32[]{:S(2)}) collective-permute-start(bf16[16,3200]{1,0:T(8,128)(2,1)S(1)} %shard_map.97), channel_id=1, source_target_pairs={{0,4},{1,3},{4,8},{5,1},{8,12},{9,5},{12,14},{13,9},{14,10},{15,13... | collective-permute-start | bytes 307208 | tf_op jit(solution)/shard_map/ppermute | solution.py:386
  48.0 4.7 %collective-permute-start.25 = (bf16[16,3200]{1,0:T(8,128)(2,1)S(1)}, bf16[16,3200]{1,0:T(8,128)(2,1)S(1)}, u32[]{:S(2)}, u32[]{:S(2)}) collective-permute-start(bf16[16,3200]{1,0:T(8,128)(2,1)S(1)} %shard_map.103), channel_id=1, source_target_pairs={{0,4},{1,3},{4,8},{5,1},{8,12},{9,5},{12,14},{13,9},{14,10},{15,13... | collective-permute-start | bytes 307208 | tf_op jit(solution)/shard_map/ppermute | solution.py:386
  49.1 4.7 %collective-permute-start.21 = (bf16[16,3200]{1,0:T(8,128)(2,1)S(1)}, bf16[16,3200]{1,0:T(8,128)(2,1)S(1)}, u32[]{:S(2)}, u32[]{:S(2)}) collective-permute-start(bf16[16,3200]{1,0:T(8,128)(2,1)S(1)} %shard_map.98), channel_id=1, source_target_pairs={{0,4},{1,3},{4,8},{5,1},{8,12},{9,5},{12,14},{13,9},{14,10},{15,13... | collective-permute-start | bytes 307208 | tf_op jit(solution)/shard_map/ppermute | solution.py:386
  58.3 4.7 %collective-permute-start.29 = (bf16[16,3200]{1,0:T(8,128)(2,1)S(1)}, bf16[16,3200]{1,0:T(8,128)(2,1)S(1)}, u32[]{:S(2)}, u32[]{:S(2)}) collective-permute-start(bf16[16,3200]{1,0:T(8,128)(2,1)S(1)} %get-tuple-element.35.refs_0_), channel_id=1, source_target_pairs={{0,4},{1,3},{4,8},{5,1},{8,12},{9,5},{12,14},{13,9},{14,10},{15,13... | collective-permute-start | bytes 307208 | tf_op jit(solution)/shard_map/ppermute | solution.py:386
  59.8 4.7 %collective-permute-start.30 = (bf16[16,3200]{1,0:T(8,128)(2,1)S(1)}, bf16[16,3200]{1,0:T(8,128)(2,1)S(1)}, u32[]{:S(2)}, u32[]{:S(2)}) collective-permute-start(bf16[16,3200]{1,0:T(8,128)(2,1)S(1)} %collective-permute-done.28.refs_1_), channel_id=1, source_target_pairs={{0,4},{1,3},{4,8},{5,1},{8,12},{9,5},{12,14},{13,9},{14,10},{15,13... | collective-permute-start | bytes 307208 | tf_op jit(solution)/shard_map/ppermute | solution.py:386
  63.0 4.7 %collective-permute-start.33 = (bf16[16,3200]{1,0:T(8,128)(2,1)S(1)}, bf16[16,3200]{1,0:T(8,128)(2,1)S(1)}, u32[]{:S(2)}, u32[]{:S(2)}) collective-permute-start(bf16[16,3200]{1,0:T(8,128)(2,1)S(1)} %collective-permute-done.29.refs_2_), channel_id=1, source_target_pairs={{0,4},{1,3},{4,8},{5,1},{8,12},{9,5},{12,14},{13,9},{14,10},{15,13... | collective-permute-start | bytes 307208 | tf_op jit(solution)/shard_map/ppermute | solution.py:386
  64.5 4.7 %collective-permute-start.34 = (bf16[16,3200]{1,0:T(8,128)(2,1)S(1)}, bf16[16,3200]{1,0:T(8,128)(2,1)S(1)}, u32[]{:S(2)}, u32[]{:S(2)}) collective-permute-start(bf16[16,3200]{1,0:T(8,128)(2,1)S(1)} %collective-permute-done.30.refs_3_), channel_id=1, source_target_pairs={{0,4},{1,3},{4,8},{5,1},{8,12},{9,5},{12,14},{13,9},{14,10},{15,13... | collective-permute-start | bytes 307208 | tf_op jit(solution)/shard_map/ppermute | solution.py:386
  70.2 6.3 %collective-permute-start.35 = (bf16[16,3200]{1,0:T(8,128)(2,1)S(1)}, bf16[16,3200]{1,0:T(8,128)(2,1)S(1)}, u32[]{:S(2)}, u32[]{:S(2)}) collective-permute-start(bf16[16,3200]{1,0:T(8,128)(2,1)S(1)} %collective-permute-done.33.refs_6_), channel_id=1, source_target_pairs={{0,1},{1,0},{2,3},{3,2},{4,5},{5,4},{6,7},{7,6},{8,9},{9,8},{10,11... | collective-permute-start | bytes 307208 | tf_op jit(solution)/shard_map/ppermute | solution.py:372
  70.7 5.9 %collective-permute-start.32 = (bf16[16,3200]{1,0:T(8,128)(2,1)S(1)}, bf16[16,3200]{1,0:T(8,128)(2,1)S(1)}, u32[]{:S(2)}, u32[]{:S(2)}) collective-permute-start(bf16[16,3200]{1,0:T(8,128)(2,1)S(1)} %collective-permute-done.30.refs_3_), channel_id=1, source_target_pairs={{0,1},{1,0},{2,3},{3,2},{4,5},{5,4},{6,7},{7,6},{8,9},{9,8},{10,11... | collective-permute-start | bytes 307208 | tf_op jit(solution)/shard_map/ppermute | solution.py:372
  72.3 4.8 %collective-permute-start.41 = (bf16[16,3200]{1,0:T(8,128)(2,1)S(1)}, bf16[16,3200]{1,0:T(8,128)(2,1)S(1)}, u32[]{:S(2)}, u32[]{:S(2)}) collective-permute-start(bf16[16,3200]{1,0:T(8,128)(2,1)S(1)} %collective-permute-done.37.refs_10_), channel_id=1, source_target_pairs={{1,3},{5,1},{9,5},{13,9},{15,13},{11,15},{7,11},{3,7},{17,19},{21,... | collective-permute-start | bytes 307208 | tf_op jit(solution)/shard_map/ppermute | solution.py:386
  74.5 5.2 %collective-permute-start.39 = (bf16[16,3200]{1,0:T(8,128)(2,1)S(1)}, bf16[16,3200]{1,0:T(8,128)(2,1)S(1)}, u32[]{:S(2)}, u32[]{:S(2)}) collective-permute-start(bf16[16,3200]{1,0:T(8,128)(2,1)S(1)} %collective-permute-done.37.refs_10_), channel_id=1, source_target_pairs={{0,1},{1,0},{2,3},{3,2},{4,5},{5,4},{6,7},{7,6},{8,9},{9,8},{10,11... | collective-permute-start | bytes 307208 | tf_op jit(solution)/shard_map/ppermute | solution.py:372
  90.8 4.9 %collective-permute-start.46 = (bf16[6,16,3200]{2,1,0:T(8,128)(2,1)S(1)}, bf16[6,16,3200]{2,1,0:T(8,128)(2,1)S(1)}, u32[]{:S(2)}, u32[]{:S(2)}) collective-permute-start(bf16[6,16,3200]{2,1,0:T(8,128)(2,1)S(1)} %get-tuple-element.43), channel_id=1, source_target_pairs={{0,1},{1,0},{2,3},{3,2},{4,5},{5,4},{6,7},{7,6},{8,9},{9,8},{10,11... | collective-permute-start | bytes 1843208 | tf_op jit(solution)/shard_map/ppermute | solution.py:372
  91.0 4.7 %collective-permute-start.51 = (bf16[16,3200]{1,0:T(8,128)(2,1)S(1)}, bf16[16,3200]{1,0:T(8,128)(2,1)S(1)}, u32[]{:S(2)}, u32[]{:S(2)}) collective-permute-start(bf16[16,3200]{1,0:T(8,128)(2,1)S(1)} %shard_map.113), channel_id=1, source_target_pairs={{0,4},{1,3},{4,8},{5,1},{8,12},{9,5},{12,14},{13,9},{14,10},{15,13... | collective-permute-start | bytes 307208 | tf_op jit(solution)/shard_map/ppermute | solution.py:386
  92.2 4.7 %collective-permute-start.47 = (bf16[16,3200]{1,0:T(8,128)(2,1)S(1)}, bf16[16,3200]{1,0:T(8,128)(2,1)S(1)}, u32[]{:S(2)}, u32[]{:S(2)}) collective-permute-start(bf16[16,3200]{1,0:T(8,128)(2,1)S(1)} %shard_map.108), channel_id=1, source_target_pairs={{0,4},{1,3},{4,8},{5,1},{8,12},{9,5},{12,14},{13,9},{14,10},{15,13... | collective-permute-start | bytes 307208 | tf_op jit(solution)/shard_map/ppermute | solution.py:386
  95.8 4.7 %collective-permute-start.52 = (bf16[16,3200]{1,0:T(8,128)(2,1)S(1)}, bf16[16,3200]{1,0:T(8,128)(2,1)S(1)}, u32[]{:S(2)}, u32[]{:S(2)}) collective-permute-start(bf16[16,3200]{1,0:T(8,128)(2,1)S(1)} %shard_map.114), channel_id=1, source_target_pairs={{0,4},{1,3},{4,8},{5,1},{8,12},{9,5},{12,14},{13,9},{14,10},{15,13... | collective-permute-start | bytes 307208 | tf_op jit(solution)/shard_map/ppermute | solution.py:386
  97.0 4.7 %collective-permute-start.48 = (bf16[16,3200]{1,0:T(8,128)(2,1)S(1)}, bf16[16,3200]{1,0:T(8,128)(2,1)S(1)}, u32[]{:S(2)}, u32[]{:S(2)}) collective-permute-start(bf16[16,3200]{1,0:T(8,128)(2,1)S(1)} %shard_map.109), channel_id=1, source_target_pairs={{0,4},{1,3},{4,8},{5,1},{8,12},{9,5},{12,14},{13,9},{14,10},{15,13... | collective-permute-start | bytes 307208 | tf_op jit(solution)/shard_map/ppermute | solution.py:386
  100.6 4.7 %collective-permute-start.53 = (bf16[16,3200]{1,0:T(8,128)(2,1)S(1)}, bf16[16,3200]{1,0:T(8,128)(2,1)S(1)}, u32[]{:S(2)}, u32[]{:S(2)}) collective-permute-start(bf16[16,3200]{1,0:T(8,128)(2,1)S(1)} %shard_map.115), channel_id=1, source_target_pairs={{0,4},{1,3},{4,8},{5,1},{8,12},{9,5},{12,14},{13,9},{14,10},{15,13... | collective-permute-start | bytes 307208 | tf_op jit(solution)/shard_map/ppermute | solution.py:386
  101.7 4.7 %collective-permute-start.49 = (bf16[16,3200]{1,0:T(8,128)(2,1)S(1)}, bf16[16,3200]{1,0:T(8,128)(2,1)S(1)}, u32[]{:S(2)}, u32[]{:S(2)}) collective-permute-start(bf16[16,3200]{1,0:T(8,128)(2,1)S(1)} %shard_map.110), channel_id=1, source_target_pairs={{0,4},{1,3},{4,8},{5,1},{8,12},{9,5},{12,14},{13,9},{14,10},{15,13... | collective-permute-start | bytes 307208 | tf_op jit(solution)/shard_map/ppermute | solution.py:386
  (28 other events, 94.2 us)

commit v8 on v7

--- a/solution.py
+++ b/solution.py
@@ -282,20 +282,6 @@
     )(me, total, dot, other, *arrived)
 
 
-def pick_kernel(me_ref, even_ref, odd_ref, out_ref):
-    out_ref[...] = jnp.where(me_ref[0] % 2 == 0, even_ref[...], odd_ref[...])
-
-
-def pick(me, even, odd):
-    return pl.pallas_call(
-        pick_kernel,
-        in_specs=[SMEM, VMEM, VMEM],
-        out_specs=VMEM,
-        out_shape=jax.ShapeDtypeStruct(even.shape, even.dtype),
-        compiler_params=PARAMS,
-    )(me, even, odd)
-
-
 def own_terms(shape, sector, ours, theirs):
     values = []
     for s, _, part in message_parts(*shape):
@@ -372,16 +358,12 @@
     return lax.ppermute(value, "term", [(i, i ^ 1) for i in range(16)])
 
 
-def down_core(value):
-    return lax.ppermute(value, "term", [(i, i - 1) for i in range(1, 16, 2)])
-
-
 def hop(value, cores=(0, 1)):
     order = [0, 2, 4, 6, 7, 5, 3, 1]
     pairs = []
     for place in range(8):
-        for core in cores:
-            there = order[(place + 1 - 2 * core) % 8]
+        for core in (0, 1):
+            there = order[(place + 1 - 2 * core) % 8] if core in cores else order[place]
             pairs.append((order[place] * 2 + core, there * 2 + core))
     return lax.ppermute(value, "term", pairs)
 
@@ -389,11 +371,16 @@
 def gather(own):
     one, two = own, flip(own)
     pieces = [one, two]
+    flipped = ()
     for _ in (1, 2, 3):
         one, two = hop(one), hop(two)
-        pieces += [one, two, flip(one), flip(two)]
+        pieces += [one, two]
+        if flipped:
+            one, *flipped = lax.optimization_barrier((one, *flipped))
+        flipped = (flip(one), flip(two))
+        pieces += flipped
     one, two = hop(one, (1,)), hop(two, (1,))
-    return pieces + [one, two, down_core(one), down_core(two)], two
+    return pieces + [one, two, flip(one), flip(two)], two
 
 
 def scatter(shape, me, total, near, far, dot):
@@ -405,10 +392,8 @@
     for k in (2, 4):
         one = hop(chain(shape, k, k - 2, me, total, dot, far, one))
         two = hop(chain(shape, k + 1, k - 1, me, total, dot, far, two))
-    one = chain(shape, 6, 4, me, total, dot, far, one)
-    two = chain(shape, 7, 5, me, total, dot, far, two)
-    one = pick(me, one, hop(one, (1,)))
-    two = pick(me, two, hop(two, (1,)))
+    one = hop(chain(shape, 6, 4, me, total, dot, far, one), (1,))
+    two = hop(chain(shape, 7, 5, me, total, dot, far, two), (1,))
     return one, flip(two)
 
 

time: 111 us -> 112 us (level)
  starting transfers between devices: 51.5 us -> 67.6 us
  waiting for transfers between devices: 35.5 us -> 24.8 us
  Pallas kernels: 19 us -> 13.9 us
    ppermute x32, starting transfers between devices: 34.6 us -> 53.7 us  [hop(): return lax.ppermute(value, 'term', pairs)]
    ppermute x32, waiting for transfers between devices: 29.3 us -> 19.2 us  [hop(): return lax.ppermute(value, 'term', pairs)]
    ppermute x4 -> x0, starting transfers between devices: 5.15 us -> none  [down_core(): return lax.ppermute(value, 'term', [(i, i - 1) for i in range(1, 16, 2)])]
    pallas_call x2, Pallas kernels: 16.2 us -> 11.2 us  [apply_blocks(): pl.pallas_call(functools.partial(blocks_kernel, first, shape, entries), i...]
    ppermute x20 -> x24, starting transfers between devices: 11.8 us -> 13.9 us  [flip(): return lax.ppermute(value, 'term', [(i, i ^ 1) for i in range(16)])]
    ppermute x4 -> x0, waiting for transfers between devices: 1.89 us -> none  [down_core(): return lax.ppermute(value, 'term', [(i, i - 1) for i in range(1, 16, 2)])]
    ppermute x20 -> x24, waiting for transfers between devices: 4.28 us -> 5.54 us  [flip(): return lax.ppermute(value, 'term', [(i, i ^ 1) for i in range(16)])]
  transfers between devices with their start and end apart: 56 -> 56, of which waited for: 24 -> 23; matrix products, arithmetic and copies ran while one was open for 1% -> 1% of each run, Pallas kernels for 1% -> 1%
where the time goes in v8:
time: 112 us; the launch traced here: 110 us
  starting transfers between devices  67.6 us (60%)
  waiting for transfers between devices  24.8 us (22%)
  Pallas kernels  13.9 us (12%)
  local copies, waits for them, and re-layouts  1.8 us (2%)
  between operations  1.58 us (1%)
    ppermute x32, starting transfers between devices, hop(): return lax.ppermute(value, 'term', pairs)  53.7 us
    ppermute x32, waiting for transfers between devices, hop(): return lax.ppermute(value, 'term', pairs)  19.2 us
    ppermute x24, starting transfers between devices, flip(): return lax.ppermute(value, 'term', [(i, i ^ 1) for i in range(16)])  13.9 us
    pallas_call x2, Pallas kernels, apply_blocks(): pl.pallas_call(functools.partial(blocks_kernel, first, shape, entries), i...  11.2 us
    ppermute x24, waiting for transfers between devices, flip(): return lax.ppermute(value, 'term', [(i, i ^ 1) for i in range(16)])  5.54 us
  transfers between devices with their start and end apart: 56, of which 23 were waited for; matrix products, arithmetic and copies ran while one was open for 1% of the time, Pallas kernels for 1%

profile of v8, /device:TPU:0, one launch (start us, length us, event | category | flops | bytes accessed | tf_op | source)
XLA Modules:
  0.0 110.4 jit_solution(14715862685626703420)
XLA Ops:
  1.1 2.6 %collective-permute-start.5 = (bf16[3,32,512]{2,1,0:T(8,128)(2,1)}, bf16[3,32,512]{2,1,0:T(8,128)(2,1)S(1)}, u32[]{:S(2)}, u32[]{:S(2)}) collective-permute-start(bf16[3,32,512]{2,1,0:T(8,128)(2,1)} %wave_ref.5), channel_id=1, source_target_pairs={{0,4},{1,3},{4,8},{5,1},{8,12},{9,5},{12,14},{13,9},{14,10},{15,13... | collective-permute-start | bytes 294920 | tf_op jit(solution)/shard_map/ppermute | solution.py:368
  3.8 1.6 %collective-permute-start.1 = (bf16[3,32,512]{2,1,0:T(8,128)(2,1)S(1)}, bf16[3,32,512]{2,1,0:T(8,128)(2,1)S(1)}, u32[]{:S(2)}, u32[]{:S(2)}) collective-permute-start(bf16[3,32,512]{2,1,0:T(8,128)(2,1)S(1)} %collective-permute-done.refs_1_), channel_id=1, source_target_pairs={{0,4},{1,3},{4,8},{5,1},{8,12},{9,5},{12,14},{13,9},{14,10},{15,13... | collective-permute-start | bytes 294920 | tf_op jit(solution)/shard_map/ppermute | solution.py:368
  6.5 2.1 %collective-permute-start.8 = (bf16[3,32,512]{2,1,0:T(8,128)(2,1)S(1)}, bf16[3,32,512]{2,1,0:T(8,128)(2,1)S(1)}, u32[]{:S(2)}, u32[]{:S(2)}) collective-permute-start(bf16[3,32,512]{2,1,0:T(8,128)(2,1)S(1)} %collective-permute-done.5.refs_2_), channel_id=1, source_target_pairs={{0,4},{1,3},{4,8},{5,1},{8,12},{9,5},{12,14},{13,9},{14,10},{15,13... | collective-permute-start | bytes 294920 | tf_op jit(solution)/shard_map/ppermute | solution.py:368
  9.1 1.6 %collective-permute-start.2 = (bf16[3,32,512]{2,1,0:T(8,128)(2,1)S(1)}, bf16[3,32,512]{2,1,0:T(8,128)(2,1)S(1)}, u32[]{:S(2)}, u32[]{:S(2)}) collective-permute-start(bf16[3,32,512]{2,1,0:T(8,128)(2,1)S(1)} %collective-permute-done.1.refs_3_), channel_id=1, source_target_pairs={{0,4},{1,3},{4,8},{5,1},{8,12},{9,5},{12,14},{13,9},{14,10},{15,13... | collective-permute-start | bytes 294920 | tf_op jit(solution)/shard_map/ppermute | solution.py:368
  11.2 2.1 %collective-permute-start.11 = (bf16[3,32,512]{2,1,0:T(8,128)(2,1)S(1)}, bf16[3,32,512]{2,1,0:T(8,128)(2,1)S(1)}, u32[]{:S(2)}, u32[]{:S(2)}) collective-permute-start(bf16[3,32,512]{2,1,0:T(8,128)(2,1)S(1)} %collective-permute-done.8.refs_6_), channel_id=1, source_target_pairs={{0,4},{1,3},{4,8},{5,1},{8,12},{9,5},{12,14},{13,9},{14,10},{15,13... | collective-permute-start | bytes 294920 | tf_op jit(solution)/shard_map/ppermute | solution.py:368
  13.8 1.6 %collective-permute-start.3 = (bf16[3,32,512]{2,1,0:T(8,128)(2,1)S(1)}, bf16[3,32,512]{2,1,0:T(8,128)(2,1)S(1)}, u32[]{:S(2)}, u32[]{:S(2)}) collective-permute-start(bf16[3,32,512]{2,1,0:T(8,128)(2,1)S(1)} %collective-permute-done.2.refs_7_), channel_id=1, source_target_pairs={{0,4},{1,3},{4,8},{5,1},{8,12},{9,5},{12,14},{13,9},{14,10},{15,13... | collective-permute-start | bytes 294920 | tf_op jit(solution)/shard_map/ppermute | solution.py:368
  16.5 1.9 %collective-permute-done.3.refs_11_ = bf16[3,32,512]{2,1,0:T(8,128)(2,1)S(1)} collective-permute-done((bf16[3,32,512]{2,1,0:T(8,128)(2,1)S(1)}, bf16[3,32,512]{2,1,0:T(8,128)(2,1)S(1)}, u32[]{:S(2)}, u32[]{:S(2)}) %collective-permute-start.3) | collective-permute-done | bytes 98336 | tf_op jit(solution)/shard_map/ppermute | solution.py:368
  19.7 2.1 %collective-permute-start.12 = (bf16[3,32,512]{2,1,0:T(8,128)(2,1)S(1)}, bf16[3,32,512]{2,1,0:T(8,128)(2,1)S(1)}, u32[]{:S(2)}, u32[]{:S(2)}) collective-permute-start(bf16[3,32,512]{2,1,0:T(8,128)(2,1)S(1)} %collective-permute-done.11.refs_10_), channel_id=1, source_target_pairs={{0,1},{1,0},{2,3},{3,2},{4,5},{5,4},{6,7},{7,6},{8,9},{9,8},{10,11... | collective-permute-start | bytes 294920 | tf_op jit(solution)/shard_map/ppermute | solution.py:358
  26.0 6.0 %shard_map.95 = (f32[3,512,512]{2,1,0:T(8,128)S(1)}, bf16[2,16,3200]{2,1,0:T(8,128)(2,1)S(1)}, bf16[6,16,3200]{2,1,0:T(8,128)(2,1)S(1)}, f32[8,128]{1,0:T(8,128)S(1)}, f32[8,128]{1,0:T(8,128)S(1)}) custom-call(s32[1]{0:T(128)} %bitcast.me_ref, s32[17]{0:T(128)S(1)} %pad_add_fusion.ints_ref, bf16[3,32,512]{2,1,0:T(8,128)(2,1)S(1)} %get-tuple-element.29.refs_0_, ...), custom_call_target="tpu_custom_call" | custom-call | flops 4294967296 | bytes 8388608 | tf_op jit(solution)/shard_map/pallas_call | solution.py:230
  33.7 4.2 %collective-permute-start.23 = (bf16[16,3200]{1,0:T(8,128)(2,1)S(1)}, bf16[16,3200]{1,0:T(8,128)(2,1)S(1)}, u32[]{:S(2)}, u32[]{:S(2)}) collective-permute-start(bf16[16,3200]{1,0:T(8,128)(2,1)S(1)} %shard_map.100), channel_id=1, source_target_pairs={{0,4},{1,3},{4,8},{5,1},{8,12},{9,5},{12,14},{13,9},{14,10},{15,13... | collective-permute-start | bytes 307208 | tf_op jit(solution)/shard_map/ppermute | solution.py:368
  37.9 1.6 %collective-permute-start.19 = (bf16[16,3200]{1,0:T(8,128)(2,1)S(1)}, bf16[16,3200]{1,0:T(8,128)(2,1)S(1)}, u32[]{:S(2)}, u32[]{:S(2)}) collective-permute-start(bf16[16,3200]{1,0:T(8,128)(2,1)S(1)} %shard_map.96), channel_id=1, source_target_pairs={{0,4},{1,3},{4,8},{5,1},{8,12},{9,5},{12,14},{13,9},{14,10},{15,13... | collective-permute-start | bytes 307208 | tf_op jit(solution)/shard_map/ppermute | solution.py:368
  40.2 2.5 %collective-permute-start.24 = (bf16[16,3200]{1,0:T(8,128)(2,1)S(1)}, bf16[16,3200]{1,0:T(8,128)(2,1)S(1)}, u32[]{:S(2)}, u32[]{:S(2)}) collective-permute-start(bf16[16,3200]{1,0:T(8,128)(2,1)S(1)} %shard_map.101), channel_id=1, source_target_pairs={{0,4},{1,3},{4,8},{5,1},{8,12},{9,5},{12,14},{13,9},{14,10},{15,13... | collective-permute-start | bytes 307208 | tf_op jit(solution)/shard_map/ppermute | solution.py:368
  42.7 1.6 %collective-permute-start.20 = (bf16[16,3200]{1,0:T(8,128)(2,1)S(1)}, bf16[16,3200]{1,0:T(8,128)(2,1)S(1)}, u32[]{:S(2)}, u32[]{:S(2)}) collective-permute-start(bf16[16,3200]{1,0:T(8,128)(2,1)S(1)} %shard_map.97), channel_id=1, source_target_pairs={{0,4},{1,3},{4,8},{5,1},{8,12},{9,5},{12,14},{13,9},{14,10},{15,13... | collective-permute-start | bytes 307208 | tf_op jit(solution)/shard_map/ppermute | solution.py:368
  44.9 2.5 %collective-permute-start.25 = (bf16[16,3200]{1,0:T(8,128)(2,1)S(1)}, bf16[16,3200]{1,0:T(8,128)(2,1)S(1)}, u32[]{:S(2)}, u32[]{:S(2)}) collective-permute-start(bf16[16,3200]{1,0:T(8,128)(2,1)S(1)} %shard_map.102), channel_id=1, source_target_pairs={{0,4},{1,3},{4,8},{5,1},{8,12},{9,5},{12,14},{13,9},{14,10},{15,13... | collective-permute-start | bytes 307208 | tf_op jit(solution)/shard_map/ppermute | solution.py:368
  47.5 1.6 %collective-permute-start.21 = (bf16[16,3200]{1,0:T(8,128)(2,1)S(1)}, bf16[16,3200]{1,0:T(8,128)(2,1)S(1)}, u32[]{:S(2)}, u32[]{:S(2)}) collective-permute-start(bf16[16,3200]{1,0:T(8,128)(2,1)S(1)} %shard_map.98), channel_id=1, source_target_pairs={{0,4},{1,3},{4,8},{5,1},{8,12},{9,5},{12,14},{13,9},{14,10},{15,13... | collective-permute-start | bytes 307208 | tf_op jit(solution)/shard_map/ppermute | solution.py:368
  50.4 1.8 %collective-permute-done.21.refs_0_ = bf16[16,3200]{1,0:T(8,128)(2,1)S(1)} collective-permute-done((bf16[16,3200]{1,0:T(8,128)(2,1)S(1)}, bf16[16,3200]{1,0:T(8,128)(2,1)S(1)}, u32[]{:S(2)}, u32[]{:S(2)}) %collective-permute-start.21) | collective-permute-done | bytes 102432 | tf_op jit(solution)/shard_map/ppermute | solution.py:368
  56.2 1.7 %collective-permute-start.29 = (bf16[16,3200]{1,0:T(8,128)(2,1)S(1)}, bf16[16,3200]{1,0:T(8,128)(2,1)S(1)}, u32[]{:S(2)}, u32[]{:S(2)}) collective-permute-start(bf16[16,3200]{1,0:T(8,128)(2,1)S(1)} %get-tuple-element.41.refs_0_), channel_id=1, source_target_pairs={{0,4},{1,3},{4,8},{5,1},{8,12},{9,5},{12,14},{13,9},{14,10},{15,13... | collective-permute-start | bytes 307208 | tf_op jit(solution)/shard_map/ppermute | solution.py:368
  59.4 1.5 %collective-permute-done.29.refs_2_ = bf16[16,3200]{1,0:T(8,128)(2,1)S(1)} collective-permute-done((bf16[16,3200]{1,0:T(8,128)(2,1)S(1)}, bf16[16,3200]{1,0:T(8,128)(2,1)S(1)}, u32[]{:S(2)}, u32[]{:S(2)}) %collective-permute-start.29) | collective-permute-done | bytes 102432 | tf_op jit(solution)/shard_map/ppermute | solution.py:368
  60.9 1.7 %collective-permute-start.33 = (bf16[16,3200]{1,0:T(8,128)(2,1)S(1)}, bf16[16,3200]{1,0:T(8,128)(2,1)S(1)}, u32[]{:S(2)}, u32[]{:S(2)}) collective-permute-start(bf16[16,3200]{1,0:T(8,128)(2,1)S(1)} %collective-permute-done.29.refs_2_), channel_id=1, source_target_pairs={{0,4},{1,3},{4,8},{5,1},{8,12},{9,5},{12,14},{13,9},{14,10},{15,13... | collective-permute-start | bytes 307208 | tf_op jit(solution)/shard_map/ppermute | solution.py:368
  65.5 2.2 %collective-permute-done.34.refs_7_ = bf16[16,3200]{1,0:T(8,128)(2,1)S(1)} collective-permute-done((bf16[16,3200]{1,0:T(8,128)(2,1)S(1)}, bf16[16,3200]{1,0:T(8,128)(2,1)S(1)}, u32[]{:S(2)}, u32[]{:S(2)}) %collective-permute-start.34) | collective-permute-done | bytes 102432 | tf_op jit(solution)/shard_map/ppermute | solution.py:368
  69.2 1.6 %collective-permute-start.38 = (bf16[16,3200]{1,0:T(8,128)(2,1)S(1)}, bf16[16,3200]{1,0:T(8,128)(2,1)S(1)}, u32[]{:S(2)}, u32[]{:S(2)}) collective-permute-start(bf16[16,3200]{1,0:T(8,128)(2,1)S(1)} %collective-permute-done.34.refs_7_), channel_id=1, source_target_pairs={{0,4},{1,3},{4,8},{5,1},{8,12},{9,5},{12,14},{13,9},{14,10},{15,13... | collective-permute-start | bytes 307208 | tf_op jit(solution)/shard_map/ppermute | solution.py:368
  70.8 1.6 %collective-permute-done.37.refs_10_ = bf16[16,3200]{1,0:T(8,128)(2,1)S(1)} collective-permute-done((bf16[16,3200]{1,0:T(8,128)(2,1)S(1)}, bf16[16,3200]{1,0:T(8,128)(2,1)S(1)}, u32[]{:S(2)}, u32[]{:S(2)}) %collective-permute-start.37) | collective-permute-done | bytes 102432 | tf_op jit(solution)/shard_map/ppermute | solution.py:368
  75.2 3.7 %collective-permute-start.39 = (bf16[16,3200]{1,0:T(8,128)(2,1)S(1)}, bf16[16,3200]{1,0:T(8,128)(2,1)S(1)}, u32[]{:S(2)}, u32[]{:S(2)}) collective-permute-start(bf16[16,3200]{1,0:T(8,128)(2,1)S(1)} %collective-permute-done.37.refs_10_), channel_id=1, source_target_pairs={{0,1},{1,0},{2,3},{3,2},{4,5},{5,4},{6,7},{7,6},{8,9},{9,8},{10,11... | collective-permute-start | bytes 307208 | tf_op jit(solution)/shard_map/ppermute | solution.py:358
  79.5 1.7 %collective-permute-start.43 = (bf16[16,3200]{1,0:T(8,128)(2,1)S(1)}, bf16[16,3200]{1,0:T(8,128)(2,1)S(1)}, u32[]{:S(2)}, u32[]{:S(2)}) collective-permute-start(bf16[16,3200]{1,0:T(8,128)(2,1)S(1)} %collective-permute-done.41.refs_14_), channel_id=1, source_target_pairs={{0,1},{1,0},{2,3},{3,2},{4,5},{5,4},{6,7},{7,6},{8,9},{9,8},{10,11... | collective-permute-start | bytes 307208 | tf_op jit(solution)/shard_map/ppermute | solution.py:358
  82.2 5.2 %shard_map.105 = (f32[3,512,512]{2,1,0:T(8,128)S(1)}, bf16[2,16,3200]{2,1,0:T(8,128)(2,1)S(1)}, bf16[6,16,3200]{2,1,0:T(8,128)(2,1)S(1)}, f32[8,128]{1,0:T(8,128)S(1)}, f32[8,128]{1,0:T(8,128)S(1)}) custom-call(s32[1]{0:T(128)} %bitcast.me_ref, s32[17]{0:T(128)S(1)} %pad_add_fusion.ints_ref, bf16[16,3200]{1,0:T(8,128)(2,1)S(1)} %get-tuple-element.41.refs_0_, ...), custom_call_target="tpu_custom_call" | custom-call | flops 4294967296 | bytes 8388608 | tf_op jit(solution)/shard_map/pallas_call | solution.py:230
  89.3 3.7 %collective-permute-start.51 = (bf16[16,3200]{1,0:T(8,128)(2,1)S(1)}, bf16[16,3200]{1,0:T(8,128)(2,1)S(1)}, u32[]{:S(2)}, u32[]{:S(2)}) collective-permute-start(bf16[16,3200]{1,0:T(8,128)(2,1)S(1)} %shard_map.110), channel_id=1, source_target_pairs={{0,4},{1,3},{4,8},{5,1},{8,12},{9,5},{12,14},{13,9},{14,10},{15,13... | collective-permute-start | bytes 307208 | tf_op jit(solution)/shard_map/ppermute | solution.py:368
  93.1 1.6 %collective-permute-start.47 = (bf16[16,3200]{1,0:T(8,128)(2,1)S(1)}, bf16[16,3200]{1,0:T(8,128)(2,1)S(1)}, u32[]{:S(2)}, u32[]{:S(2)}) collective-permute-start(bf16[16,3200]{1,0:T(8,128)(2,1)S(1)} %shard_map.106), channel_id=1, source_target_pairs={{0,4},{1,3},{4,8},{5,1},{8,12},{9,5},{12,14},{13,9},{14,10},{15,13... | collective-permute-start | bytes 307208 | tf_op jit(solution)/shard_map/ppermute | solution.py:368
  95.4 2.5 %collective-permute-start.52 = (bf16[16,3200]{1,0:T(8,128)(2,1)S(1)}, bf16[16,3200]{1,0:T(8,128)(2,1)S(1)}, u32[]{:S(2)}, u32[]{:S(2)}) collective-permute-start(bf16[16,3200]{1,0:T(8,128)(2,1)S(1)} %shard_map.111), channel_id=1, source_target_pairs={{0,4},{1,3},{4,8},{5,1},{8,12},{9,5},{12,14},{13,9},{14,10},{15,13... | collective-permute-start | bytes 307208 | tf_op jit(solution)/shard_map/ppermute | solution.py:368
  97.9 1.6 %collective-permute-start.48 = (bf16[16,3200]{1,0:T(8,128)(2,1)S(1)}, bf16[16,3200]{1,0:T(8,128)(2,1)S(1)}, u32[]{:S(2)}, u32[]{:S(2)}) collective-permute-start(bf16[16,3200]{1,0:T(8,128)(2,1)S(1)} %shard_map.107), channel_id=1, source_target_pairs={{0,4},{1,3},{4,8},{5,1},{8,12},{9,5},{12,14},{13,9},{14,10},{15,13... | collective-permute-start | bytes 307208 | tf_op jit(solution)/shard_map/ppermute | solution.py:368
  100.1 2.5 %collective-permute-start.53 = (bf16[16,3200]{1,0:T(8,128)(2,1)S(1)}, bf16[16,3200]{1,0:T(8,128)(2,1)S(1)}, u32[]{:S(2)}, u32[]{:S(2)}) collective-permute-start(bf16[16,3200]{1,0:T(8,128)(2,1)S(1)} %shard_map.112), channel_id=1, source_target_pairs={{0,4},{1,3},{4,8},{5,1},{8,12},{9,5},{12,14},{13,9},{14,10},{15,13... | collective-permute-start | bytes 307208 | tf_op jit(solution)/shard_map/ppermute | solution.py:368
  102.7 1.6 %collective-permute-start.49 = (bf16[16,3200]{1,0:T(8,128)(2,1)S(1)}, bf16[16,3200]{1,0:T(8,128)(2,1)S(1)}, u32[]{:S(2)}, u32[]{:S(2)}) collective-permute-start(bf16[16,3200]{1,0:T(8,128)(2,1)S(1)} %shard_map.108), channel_id=1, source_target_pairs={{0,4},{1,3},{4,8},{5,1},{8,12},{9,5},{12,14},{13,9},{14,10},{15,13... | collective-permute-start | bytes 307208 | tf_op jit(solution)/shard_map/ppermute | solution.py:368
  105.6 1.8 %collective-permute-done.49.refs_0_ = bf16[16,3200]{1,0:T(8,128)(2,1)S(1)} collective-permute-done((bf16[16,3200]{1,0:T(8,128)(2,1)S(1)}, bf16[16,3200]{1,0:T(8,128)(2,1)S(1)}, u32[]{:S(2)}, u32[]{:S(2)}) %collective-permute-start.49) | collective-permute-done | bytes 102432 | tf_op jit(solution)/shard_map/ppermute | solution.py:368
  (110 shorter events, 35.1 us)
Async XLA Ops:
  1.1 5.4 %collective-permute-start.5 = (bf16[3,32,512]{2,1,0:T(8,128)(2,1)}, bf16[3,32,512]{2,1,0:T(8,128)(2,1)S(1)}, u32[]{:S(2)}, u32[]{:S(2)}) collective-permute-start(bf16[3,32,512]{2,1,0:T(8,128)(2,1)} %wave_ref.5), channel_id=1, source_target_pairs={{0,4},{1,3},{4,8},{5,1},{8,12},{9,5},{12,14},{13,9},{14,10},{15,13... | collective-permute-start | bytes 294920 | tf_op jit(solution)/shard_map/ppermute | solution.py:368
  3.8 4.8 %collective-permute-start.1 = (bf16[3,32,512]{2,1,0:T(8,128)(2,1)S(1)}, bf16[3,32,512]{2,1,0:T(8,128)(2,1)S(1)}, u32[]{:S(2)}, u32[]{:S(2)}) collective-permute-start(bf16[3,32,512]{2,1,0:T(8,128)(2,1)S(1)} %collective-permute-done.refs_1_), channel_id=1, source_target_pairs={{0,4},{1,3},{4,8},{5,1},{8,12},{9,5},{12,14},{13,9},{14,10},{15,13... | collective-permute-start | bytes 294920 | tf_op jit(solution)/shard_map/ppermute | solution.py:368
  6.5 4.6 %collective-permute-start.8 = (bf16[3,32,512]{2,1,0:T(8,128)(2,1)S(1)}, bf16[3,32,512]{2,1,0:T(8,128)(2,1)S(1)}, u32[]{:S(2)}, u32[]{:S(2)}) collective-permute-start(bf16[3,32,512]{2,1,0:T(8,128)(2,1)S(1)} %collective-permute-done.5.refs_2_), channel_id=1, source_target_pairs={{0,4},{1,3},{4,8},{5,1},{8,12},{9,5},{12,14},{13,9},{14,10},{15,13... | collective-permute-start | bytes 294920 | tf_op jit(solution)/shard_map/ppermute | solution.py:368
  9.1 4.6 %collective-permute-start.2 = (bf16[3,32,512]{2,1,0:T(8,128)(2,1)S(1)}, bf16[3,32,512]{2,1,0:T(8,128)(2,1)S(1)}, u32[]{:S(2)}, u32[]{:S(2)}) collective-permute-start(bf16[3,32,512]{2,1,0:T(8,128)(2,1)S(1)} %collective-permute-done.1.refs_3_), channel_id=1, source_target_pairs={{0,4},{1,3},{4,8},{5,1},{8,12},{9,5},{12,14},{13,9},{14,10},{15,13... | collective-permute-start | bytes 294920 | tf_op jit(solution)/shard_map/ppermute | solution.py:368
  11.2 4.6 %collective-permute-start.11 = (bf16[3,32,512]{2,1,0:T(8,128)(2,1)S(1)}, bf16[3,32,512]{2,1,0:T(8,128)(2,1)S(1)}, u32[]{:S(2)}, u32[]{:S(2)}) collective-permute-start(bf16[3,32,512]{2,1,0:T(8,128)(2,1)S(1)} %collective-permute-done.8.refs_6_), channel_id=1, source_target_pairs={{0,4},{1,3},{4,8},{5,1},{8,12},{9,5},{12,14},{13,9},{14,10},{15,13... | collective-permute-start | bytes 294920 | tf_op jit(solution)/shard_map/ppermute | solution.py:368
  13.8 4.6 %collective-permute-start.3 = (bf16[3,32,512]{2,1,0:T(8,128)(2,1)S(1)}, bf16[3,32,512]{2,1,0:T(8,128)(2,1)S(1)}, u32[]{:S(2)}, u32[]{:S(2)}) collective-permute-start(bf16[3,32,512]{2,1,0:T(8,128)(2,1)S(1)} %collective-permute-done.2.refs_7_), channel_id=1, source_target_pairs={{0,4},{1,3},{4,8},{5,1},{8,12},{9,5},{12,14},{13,9},{14,10},{15,13... | collective-permute-start | bytes 294920 | tf_op jit(solution)/shard_map/ppermute | solution.py:368
  15.8 6.1 %collective-permute-start.14 = (bf16[3,32,512]{2,1,0:T(8,128)(2,1)S(1)}, bf16[3,32,512]{2,1,0:T(8,128)(2,1)S(1)}, u32[]{:S(2)}, u32[]{:S(2)}) collective-permute-start(bf16[3,32,512]{2,1,0:T(8,128)(2,1)S(1)} %collective-permute-done.11.refs_10_), channel_id=1, source_target_pairs={{0,0},{1,3},{4,4},{5,1},{8,8},{9,5},{12,12},{13,9},{14,14},{15,13}... | collective-permute-start | bytes 294920 | tf_op jit(solution)/shard_map/ppermute | solution.py:368
  19.7 6.3 %collective-permute-start.12 = (bf16[3,32,512]{2,1,0:T(8,128)(2,1)S(1)}, bf16[3,32,512]{2,1,0:T(8,128)(2,1)S(1)}, u32[]{:S(2)}, u32[]{:S(2)}) collective-permute-start(bf16[3,32,512]{2,1,0:T(8,128)(2,1)S(1)} %collective-permute-done.11.refs_10_), channel_id=1, source_target_pairs={{0,1},{1,0},{2,3},{3,2},{4,5},{5,4},{6,7},{7,6},{8,9},{9,8},{10,11... | collective-permute-start | bytes 294920 | tf_op jit(solution)/shard_map/ppermute | solution.py:358
  21.8 4.2 %collective-permute-start.13 = (bf16[3,32,512]{2,1,0:T(8,128)(2,1)S(1)}, bf16[3,32,512]{2,1,0:T(8,128)(2,1)S(1)}, u32[]{:S(2)}, u32[]{:S(2)}) collective-permute-start(bf16[3,32,512]{2,1,0:T(8,128)(2,1)S(1)} %collective-permute-done.3.refs_11_), channel_id=1, source_target_pairs={{0,1},{1,0},{2,3},{3,2},{4,5},{5,4},{6,7},{7,6},{8,9},{9,8},{10,11... | collective-permute-start | bytes 294920 | tf_op jit(solution)/shard_map/ppermute | solution.py:358
  33.5 6.6 %collective-permute-start.18 = (bf16[6,16,3200]{2,1,0:T(8,128)(2,1)S(1)}, bf16[6,16,3200]{2,1,0:T(8,128)(2,1)S(1)}, u32[]{:S(2)}, u32[]{:S(2)}) collective-permute-start(bf16[6,16,3200]{2,1,0:T(8,128)(2,1)S(1)} %get-tuple-element.38), channel_id=1, source_target_pairs={{0,1},{1,0},{2,3},{3,2},{4,5},{5,4},{6,7},{7,6},{8,9},{9,8},{10,11... | collective-permute-start | bytes 1843208 | tf_op jit(solution)/shard_map/ppermute | solution.py:358
  33.7 6.4 %collective-permute-start.23 = (bf16[16,3200]{1,0:T(8,128)(2,1)S(1)}, bf16[16,3200]{1,0:T(8,128)(2,1)S(1)}, u32[]{:S(2)}, u32[]{:S(2)}) collective-permute-start(bf16[16,3200]{1,0:T(8,128)(2,1)S(1)} %shard_map.100), channel_id=1, source_target_pairs={{0,4},{1,3},{4,8},{5,1},{8,12},{9,5},{12,14},{13,9},{14,10},{15,13... | collective-permute-start | bytes 307208 | tf_op jit(solution)/shard_map/ppermute | solution.py:368
  37.9 4.7 %collective-permute-start.19 = (bf16[16,3200]{1,0:T(8,128)(2,1)S(1)}, bf16[16,3200]{1,0:T(8,128)(2,1)S(1)}, u32[]{:S(2)}, u32[]{:S(2)}) collective-permute-start(bf16[16,3200]{1,0:T(8,128)(2,1)S(1)} %shard_map.96), channel_id=1, source_target_pairs={{0,4},{1,3},{4,8},{5,1},{8,12},{9,5},{12,14},{13,9},{14,10},{15,13... | collective-permute-start | bytes 307208 | tf_op jit(solution)/shard_map/ppermute | solution.py:368
  40.2 4.7 %collective-permute-start.24 = (bf16[16,3200]{1,0:T(8,128)(2,1)S(1)}, bf16[16,3200]{1,0:T(8,128)(2,1)S(1)}, u32[]{:S(2)}, u32[]{:S(2)}) collective-permute-start(bf16[16,3200]{1,0:T(8,128)(2,1)S(1)} %shard_map.101), channel_id=1, source_target_pairs={{0,4},{1,3},{4,8},{5,1},{8,12},{9,5},{12,14},{13,9},{14,10},{15,13... | collective-permute-start | bytes 307208 | tf_op jit(solution)/shard_map/ppermute | solution.py:368
  42.7 4.7 %collective-permute-start.20 = (bf16[16,3200]{1,0:T(8,128)(2,1)S(1)}, bf16[16,3200]{1,0:T(8,128)(2,1)S(1)}, u32[]{:S(2)}, u32[]{:S(2)}) collective-permute-start(bf16[16,3200]{1,0:T(8,128)(2,1)S(1)} %shard_map.97), channel_id=1, source_target_pairs={{0,4},{1,3},{4,8},{5,1},{8,12},{9,5},{12,14},{13,9},{14,10},{15,13... | collective-permute-start | bytes 307208 | tf_op jit(solution)/shard_map/ppermute | solution.py:368
  44.9 4.7 %collective-permute-start.25 = (bf16[16,3200]{1,0:T(8,128)(2,1)S(1)}, bf16[16,3200]{1,0:T(8,128)(2,1)S(1)}, u32[]{:S(2)}, u32[]{:S(2)}) collective-permute-start(bf16[16,3200]{1,0:T(8,128)(2,1)S(1)} %shard_map.102), channel_id=1, source_target_pairs={{0,4},{1,3},{4,8},{5,1},{8,12},{9,5},{12,14},{13,9},{14,10},{15,13... | collective-permute-start | bytes 307208 | tf_op jit(solution)/shard_map/ppermute | solution.py:368
  47.5 4.7 %collective-permute-start.21 = (bf16[16,3200]{1,0:T(8,128)(2,1)S(1)}, bf16[16,3200]{1,0:T(8,128)(2,1)S(1)}, u32[]{:S(2)}, u32[]{:S(2)}) collective-permute-start(bf16[16,3200]{1,0:T(8,128)(2,1)S(1)} %shard_map.98), channel_id=1, source_target_pairs={{0,4},{1,3},{4,8},{5,1},{8,12},{9,5},{12,14},{13,9},{14,10},{15,13... | collective-permute-start | bytes 307208 | tf_op jit(solution)/shard_map/ppermute | solution.py:368
  56.2 4.7 %collective-permute-start.29 = (bf16[16,3200]{1,0:T(8,128)(2,1)S(1)}, bf16[16,3200]{1,0:T(8,128)(2,1)S(1)}, u32[]{:S(2)}, u32[]{:S(2)}) collective-permute-start(bf16[16,3200]{1,0:T(8,128)(2,1)S(1)} %get-tuple-element.41.refs_0_), channel_id=1, source_target_pairs={{0,4},{1,3},{4,8},{5,1},{8,12},{9,5},{12,14},{13,9},{14,10},{15,13... | collective-permute-start | bytes 307208 | tf_op jit(solution)/shard_map/ppermute | solution.py:368
  57.9 4.7 %collective-permute-start.30 = (bf16[16,3200]{1,0:T(8,128)(2,1)S(1)}, bf16[16,3200]{1,0:T(8,128)(2,1)S(1)}, u32[]{:S(2)}, u32[]{:S(2)}) collective-permute-start(bf16[16,3200]{1,0:T(8,128)(2,1)S(1)} %collective-permute-done.28.refs_1_), channel_id=1, source_target_pairs={{0,4},{1,3},{4,8},{5,1},{8,12},{9,5},{12,14},{13,9},{14,10},{15,13... | collective-permute-start | bytes 307208 | tf_op jit(solution)/shard_map/ppermute | solution.py:368
  60.9 4.7 %collective-permute-start.33 = (bf16[16,3200]{1,0:T(8,128)(2,1)S(1)}, bf16[16,3200]{1,0:T(8,128)(2,1)S(1)}, u32[]{:S(2)}, u32[]{:S(2)}) collective-permute-start(bf16[16,3200]{1,0:T(8,128)(2,1)S(1)} %collective-permute-done.29.refs_2_), channel_id=1, source_target_pairs={{0,4},{1,3},{4,8},{5,1},{8,12},{9,5},{12,14},{13,9},{14,10},{15,13... | collective-permute-start | bytes 307208 | tf_op jit(solution)/shard_map/ppermute | solution.py:368
  63.1 4.7 %collective-permute-start.34 = (bf16[16,3200]{1,0:T(8,128)(2,1)S(1)}, bf16[16,3200]{1,0:T(8,128)(2,1)S(1)}, u32[]{:S(2)}, u32[]{:S(2)}) collective-permute-start(bf16[16,3200]{1,0:T(8,128)(2,1)S(1)} %collective-permute-done.30.refs_3_), channel_id=1, source_target_pairs={{0,4},{1,3},{4,8},{5,1},{8,12},{9,5},{12,14},{13,9},{14,10},{15,13... | collective-permute-start | bytes 307208 | tf_op jit(solution)/shard_map/ppermute | solution.py:368
  67.8 4.7 %collective-permute-start.37 = (bf16[16,3200]{1,0:T(8,128)(2,1)S(1)}, bf16[16,3200]{1,0:T(8,128)(2,1)S(1)}, u32[]{:S(2)}, u32[]{:S(2)}) collective-permute-start(bf16[16,3200]{1,0:T(8,128)(2,1)S(1)} %collective-permute-done.33.refs_6_), channel_id=1, source_target_pairs={{0,4},{1,3},{4,8},{5,1},{8,12},{9,5},{12,14},{13,9},{14,10},{15,13... | collective-permute-start | bytes 307208 | tf_op jit(solution)/shard_map/ppermute | solution.py:368
  69.2 4.7 %collective-permute-start.38 = (bf16[16,3200]{1,0:T(8,128)(2,1)S(1)}, bf16[16,3200]{1,0:T(8,128)(2,1)S(1)}, u32[]{:S(2)}, u32[]{:S(2)}) collective-permute-start(bf16[16,3200]{1,0:T(8,128)(2,1)S(1)} %collective-permute-done.34.refs_7_), channel_id=1, source_target_pairs={{0,4},{1,3},{4,8},{5,1},{8,12},{9,5},{12,14},{13,9},{14,10},{15,13... | collective-permute-start | bytes 307208 | tf_op jit(solution)/shard_map/ppermute | solution.py:368
  73.9 5.2 %collective-permute-start.42 = (bf16[16,3200]{1,0:T(8,128)(2,1)S(1)}, bf16[16,3200]{1,0:T(8,128)(2,1)S(1)}, u32[]{:S(2)}, u32[]{:S(2)}) collective-permute-start(bf16[16,3200]{1,0:T(8,128)(2,1)S(1)} %collective-permute-done.38.refs_11_), channel_id=1, source_target_pairs={{0,0},{1,3},{4,4},{5,1},{8,8},{9,5},{12,12},{13,9},{14,14},{15,13}... | collective-permute-start | bytes 307208 | tf_op jit(solution)/shard_map/ppermute | solution.py:368
  74.5 4.9 %collective-permute-start.41 = (bf16[16,3200]{1,0:T(8,128)(2,1)S(1)}, bf16[16,3200]{1,0:T(8,128)(2,1)S(1)}, u32[]{:S(2)}, u32[]{:S(2)}) collective-permute-start(bf16[16,3200]{1,0:T(8,128)(2,1)S(1)} %collective-permute-done.37.refs_10_), channel_id=1, source_target_pairs={{0,0},{1,3},{4,4},{5,1},{8,8},{9,5},{12,12},{13,9},{14,14},{15,13}... | collective-permute-start | bytes 307208 | tf_op jit(solution)/shard_map/ppermute | solution.py:368
  75.2 6.0 %collective-permute-start.39 = (bf16[16,3200]{1,0:T(8,128)(2,1)S(1)}, bf16[16,3200]{1,0:T(8,128)(2,1)S(1)}, u32[]{:S(2)}, u32[]{:S(2)}) collective-permute-start(bf16[16,3200]{1,0:T(8,128)(2,1)S(1)} %collective-permute-done.37.refs_10_), channel_id=1, source_target_pairs={{0,1},{1,0},{2,3},{3,2},{4,5},{5,4},{6,7},{7,6},{8,9},{9,8},{10,11... | collective-permute-start | bytes 307208 | tf_op jit(solution)/shard_map/ppermute | solution.py:358
  88.9 6.4 %collective-permute-start.46 = (bf16[6,16,3200]{2,1,0:T(8,128)(2,1)S(1)}, bf16[6,16,3200]{2,1,0:T(8,128)(2,1)S(1)}, u32[]{:S(2)}, u32[]{:S(2)}) collective-permute-start(bf16[6,16,3200]{2,1,0:T(8,128)(2,1)S(1)} %get-tuple-element.51), channel_id=1, source_target_pairs={{0,1},{1,0},{2,3},{3,2},{4,5},{5,4},{6,7},{7,6},{8,9},{9,8},{10,11... | collective-permute-start | bytes 1843208 | tf_op jit(solution)/shard_map/ppermute | solution.py:358
  89.3 6.0 %collective-permute-start.51 = (bf16[16,3200]{1,0:T(8,128)(2,1)S(1)}, bf16[16,3200]{1,0:T(8,128)(2,1)S(1)}, u32[]{:S(2)}, u32[]{:S(2)}) collective-permute-start(bf16[16,3200]{1,0:T(8,128)(2,1)S(1)} %shard_map.110), channel_id=1, source_target_pairs={{0,4},{1,3},{4,8},{5,1},{8,12},{9,5},{12,14},{13,9},{14,10},{15,13... | collective-permute-start | bytes 307208 | tf_op jit(solution)/shard_map/ppermute | solution.py:368
  93.1 4.7 %collective-permute-start.47 = (bf16[16,3200]{1,0:T(8,128)(2,1)S(1)}, bf16[16,3200]{1,0:T(8,128)(2,1)S(1)}, u32[]{:S(2)}, u32[]{:S(2)}) collective-permute-start(bf16[16,3200]{1,0:T(8,128)(2,1)S(1)} %shard_map.106), channel_id=1, source_target_pairs={{0,4},{1,3},{4,8},{5,1},{8,12},{9,5},{12,14},{13,9},{14,10},{15,13... | collective-permute-start | bytes 307208 | tf_op jit(solution)/shard_map/ppermute | solution.py:368
  95.4 4.7 %collective-permute-start.52 = (bf16[16,3200]{1,0:T(8,128)(2,1)S(1)}, bf16[16,3200]{1,0:T(8,128)(2,1)S(1)}, u32[]{:S(2)}, u32[]{:S(2)}) collective-permute-start(bf16[16,3200]{1,0:T(8,128)(2,1)S(1)} %shard_map.111), channel_id=1, source_target_pairs={{0,4},{1,3},{4,8},{5,1},{8,12},{9,5},{12,14},{13,9},{14,10},{15,13... | collective-permute-start | bytes 307208 | tf_op jit(solution)/shard_map/ppermute | solution.py:368
  97.9 4.7 %collective-permute-start.48 = (bf16[16,3200]{1,0:T(8,128)(2,1)S(1)}, bf16[16,3200]{1,0:T(8,128)(2,1)S(1)}, u32[]{:S(2)}, u32[]{:S(2)}) collective-permute-start(bf16[16,3200]{1,0:T(8,128)(2,1)S(1)} %shard_map.107), channel_id=1, source_target_pairs={{0,4},{1,3},{4,8},{5,1},{8,12},{9,5},{12,14},{13,9},{14,10},{15,13... | collective-permute-start | bytes 307208 | tf_op jit(solution)/shard_map/ppermute | solution.py:368
  100.1 4.7 %collective-permute-start.53 = (bf16[16,3200]{1,0:T(8,128)(2,1)S(1)}, bf16[16,3200]{1,0:T(8,128)(2,1)S(1)}, u32[]{:S(2)}, u32[]{:S(2)}) collective-permute-start(bf16[16,3200]{1,0:T(8,128)(2,1)S(1)} %shard_map.112), channel_id=1, source_target_pairs={{0,4},{1,3},{4,8},{5,1},{8,12},{9,5},{12,14},{13,9},{14,10},{15,13... | collective-permute-start | bytes 307208 | tf_op jit(solution)/shard_map/ppermute | solution.py:368
  102.7 4.7 %collective-permute-start.49 = (bf16[16,3200]{1,0:T(8,128)(2,1)S(1)}, bf16[16,3200]{1,0:T(8,128)(2,1)S(1)}, u32[]{:S(2)}, u32[]{:S(2)}) collective-permute-start(bf16[16,3200]{1,0:T(8,128)(2,1)S(1)} %shard_map.108), channel_id=1, source_target_pairs={{0,4},{1,3},{4,8},{5,1},{8,12},{9,5},{12,14},{13,9},{14,10},{15,13... | collective-permute-start | bytes 307208 | tf_op jit(solution)/shard_map/ppermute | solution.py:368
  (28 other events, 76.3 us)

commit v9 on v8

--- a/solution.py
+++ b/solution.py
@@ -62,24 +62,24 @@
     return chip_at(place + (1 - 2 * core) * distance) * 2 + half
 
 
-ROUNDS = 4
+ROUNDS = 3
 
 
 def sent_devices(me, core):
     devices = []
     for k in range(ROUNDS):
         for half in (core, 1 - core):
-            devices.append(ahead(me, ROUNDS - 1 - k + core, half, core))
-    return devices
+            devices.append(ahead(me, ROUNDS - k, half, core))
+    return devices + [ahead(me, 4, core, core), ahead(me, 0, core, core)]
 
 
 def gathered_devices(me):
     core = me % 2
     devices = [ahead(me, 0, core), ahead(me, 0, 1 - core)]
-    for k in (1, 2, 3):
+    for k in range(1, ROUNDS + 1):
         devices += [ahead(me, -k, core), ahead(me, -k, 1 - core)]
         devices += [ahead(me, k, 1 - core), ahead(me, k, core)]
-    return devices + [ahead(me, 4, 1), ahead(me, 4, 0)]
+    return devices + [ahead(me, 4, core), ahead(me, 4, 1 - core)]
 
 
 def message_parts(sectors, rows, width):
@@ -116,7 +116,7 @@
 
 def blocks_kernel(first, shape, entries, me_ref, ints_ref, *refs):
     sectors, rows, width = shape
-    field_refs, refs = refs[:18], refs[18:]
+    field_refs, refs = refs[:16], refs[16:]
     if first:
         square_ref, *refs = refs
     else:
@@ -137,11 +137,6 @@
 
     me = me_ref[0]
     core = me % 2
-
-    def read(k, part):
-        if k < 14:
-            return field_refs[k][part]
-        return jnp.where(core == 1, field_refs[k][part], field_refs[k + 2][part])
 
     pieces = []
     for k, owner in enumerate(gathered_devices(me)):
@@ -157,16 +152,16 @@
     if first:
         dot = jnp.zeros((8, 128), jnp.float32)
         for k, part, _, _ in pieces:
-            value = read(k, part).astype(jnp.float32)
+            value = field_refs[k][part].astype(jnp.float32)
             dot += fold(value * value)
         scale = jnp.sqrt(jnp.sum(dot) / entries)
         inverse = 1.0 / scale
         out_ref[...] = jnp.full(out_ref.shape, scale, jnp.float32)
         for k, part, s, at in pieces:
-            field[s, at, :] = (read(k, part).astype(jnp.float32) * inverse).astype(jnp.bfloat16)
+            field[s, at, :] = (field_refs[k][part].astype(jnp.float32) * inverse).astype(jnp.bfloat16)
     else:
         for k, part, s, at in pieces:
-            field[s, at, :] = read(k, part)
+            field[s, at, :] = field_refs[k][part]
 
     used = ints_ref[2 * slots]
 
@@ -200,12 +195,12 @@
     dot = jnp.zeros((8, 128), jnp.float32)
     if first:
         for k, part, s, at in pieces:
-            dot += fold(total[s, at, :] * read(k, part).astype(jnp.float32))
+            dot += fold(total[s, at, :] * field_refs[k][part].astype(jnp.float32))
         dot = dot * inverse + square_ref[...] * inverse * inverse
     else:
         at = message_shape(*shape)[1] - LANES
         lanes = sum(
-            read(k, (slice(None), slice(at, at + LANES))).astype(jnp.float32) for k in range(16)
+            ref[:, at : at + LANES].astype(jnp.float32) for ref in field_refs
         )
         along = jnp.sum(lanes) / entries
         out_ref[...] = jnp.full(out_ref.shape, along, jnp.float32)
@@ -241,7 +236,7 @@
         out_shape=[
             jax.ShapeDtypeStruct((sectors, order, width), jnp.float32),
             jax.ShapeDtypeStruct((2, *message), jnp.bfloat16),
-            jax.ShapeDtypeStruct((2 * ROUNDS - 2, *message), jnp.bfloat16),
+            jax.ShapeDtypeStruct((2 * ROUNDS, *message), jnp.bfloat16),
             jax.ShapeDtypeStruct((8, 128), jnp.float32),
             jax.ShapeDtypeStruct((8, 128), jnp.float32),
         ],
@@ -282,29 +277,35 @@
     )(me, total, dot, other, *arrived)
 
 
-def own_terms(shape, sector, ours, theirs):
+def own_terms(shape, sector, me_ref, total_ref, other_ref, _, *arrived_refs):
+    start = pl.multiple_of(me_ref[0] * shape[1], shape[1])
     values = []
-    for s, _, part in message_parts(*shape):
+    for s, row, part in message_parts(*shape):
         if s == sector:
-            values.append(ours[:, part].astype(jnp.float32) + theirs[:, part].astype(jnp.float32))
+            value = total_ref[s, pl.ds(start + row, HALF), :]
+            value += other_ref[other_ref.shape[0] - 1, :, part].astype(jnp.float32)
+            for ref in arrived_refs:
+                value += ref[:, part].astype(jnp.float32)
+            values.append(value)
     return jnp.concatenate(values, axis=0)
 
 
-def own_scalar(ours, theirs):
-    at = ours.shape[1] - LANES
-    return jnp.sum(read_lanes(ours, at) + read_lanes(theirs, at))
-
-
-def step_kernel(entries, scale_ref, wave_ref, diag_ref, ours_ref, theirs_ref, *refs):
-    first_ref, terms_ref, correction_ref, message_ref = refs
+def own_scalar(me_ref, total_ref, other_ref, dot_ref, *arrived_refs):
+    at = other_ref.shape[2] - LANES
+    lanes = down(dot_ref[...]) + read_lanes(other_ref.at[other_ref.shape[0] - 1], at)
+    return jnp.sum(lanes + sum(read_lanes(ref, at) for ref in arrived_refs))
+
+
+def step_kernel(entries, scale_ref, wave_ref, diag_ref, *refs):
+    *sums, first_ref, terms_ref, correction_ref, message_ref = refs
     shape = wave_ref.shape
-    ritz = own_scalar(ours_ref, theirs_ref) / entries
+    ritz = own_scalar(*sums) / entries
     inverse = 1.0 / scale_ref[0:1, 0:1]
     dots = jnp.zeros((8, 128), jnp.float32)
     for s in range(shape[0]):
         start = wave_ref[s].astype(jnp.float32) * inverse
         diag = diag_ref[s].astype(jnp.float32)
-        terms = own_terms(shape, s, ours_ref, theirs_ref)
+        terms = own_terms(shape, s, *sums)
         first = terms + diag * start
         correction = (first - ritz * start) / jnp.maximum(jnp.abs(diag - ritz), 1.0)
         first_ref[s] = first
@@ -321,7 +322,7 @@
     full = jax.ShapeDtypeStruct(wave.shape, jnp.float32)
     return pl.pallas_call(
         functools.partial(step_kernel, entries),
-        in_specs=[VMEM] * 5,
+        in_specs=[VMEM] * 3 + [SMEM] + [VMEM] * (len(sums) - 1),
         out_specs=[VMEM] * 4,
         out_shape=[full, full, full, jax.ShapeDtypeStruct(message_shape(*wave.shape), jnp.bfloat16)],
         compiler_params=PARAMS,
@@ -329,17 +330,17 @@
 
 
 def finish_kernel(entries, along_ref, scale_ref, wave_ref, diag_ref, *refs):
-    terms_ref, correction_ref, ours_ref, theirs_ref, vector_ref, image_ref = refs
+    terms_ref, correction_ref, *sums, vector_ref, image_ref = refs
     shape = wave_ref.shape
     along = along_ref[0:1, 0:1]
-    norm = jnp.sqrt(jnp.full((1, 1), own_scalar(ours_ref, theirs_ref) / entries, jnp.float32))
+    norm = jnp.sqrt(jnp.full((1, 1), own_scalar(*sums) / entries, jnp.float32))
     inverse = 1.0 / norm
     start_scale = 1.0 / scale_ref[0:1, 0:1]
     for s in range(shape[0]):
         start = wave_ref[s].astype(jnp.float32) * start_scale
         second = (correction_ref[s] - along * start) * inverse
         vector_ref[s] = second
-        image = (own_terms(shape, s, ours_ref, theirs_ref) - along * terms_ref[s]) * inverse
+        image = (own_terms(shape, s, *sums) - along * terms_ref[s]) * inverse
         image_ref[s] = image + diag_ref[s].astype(jnp.float32) * second
 
 
@@ -347,7 +348,7 @@
     full = jax.ShapeDtypeStruct(wave.shape, jnp.float32)
     return pl.pallas_call(
         functools.partial(finish_kernel, entries),
-        in_specs=[VMEM] * 8,
+        in_specs=[VMEM] * 6 + [SMEM] + [VMEM] * (len(sums) - 1),
         out_specs=[VMEM] * 2,
         out_shape=[full, full],
         compiler_params=PARAMS,
@@ -358,29 +359,28 @@
     return lax.ppermute(value, "term", [(i, i ^ 1) for i in range(16)])
 
 
-def hop(value, cores=(0, 1)):
+def hop(value, up=1, down=-1):
     order = [0, 2, 4, 6, 7, 5, 3, 1]
     pairs = []
     for place in range(8):
-        for core in (0, 1):
-            there = order[(place + 1 - 2 * core) % 8] if core in cores else order[place]
-            pairs.append((order[place] * 2 + core, there * 2 + core))
+        for core, step in ((0, up), (1, down)):
+            pairs.append((order[place] * 2 + core, order[(place + step) % 8] * 2 + core))
     return lax.ppermute(value, "term", pairs)
+
+
+def opposite(value):
+    return hop(value, 4, 4)
 
 
 def gather(own):
     one, two = own, flip(own)
+    across, two = lax.optimization_barrier((own, two))
     pieces = [one, two]
-    flipped = ()
-    for _ in (1, 2, 3):
+    across = opposite(across)
+    for _ in range(ROUNDS):
         one, two = hop(one), hop(two)
-        pieces += [one, two]
-        if flipped:
-            one, *flipped = lax.optimization_barrier((one, *flipped))
-        flipped = (flip(one), flip(two))
-        pieces += flipped
-    one, two = hop(one, (1,)), hop(two, (1,))
-    return pieces + [one, two, flip(one), flip(two)], two
+        pieces += [one, two, flip(one), flip(two)]
+    return pieces + [across, flip(across)], two
 
 
 def scatter(shape, me, total, near, far, dot):
@@ -389,12 +389,11 @@
     far = flip(far)
     one = hop(chain(shape, 0, 0, me, total, dot, near))
     two = hop(chain(shape, 1, 1, me, total, dot, near))
+    across = opposite(chain(shape, 6, 4, me, total, dot, far))
     for k in (2, 4):
         one = hop(chain(shape, k, k - 2, me, total, dot, far, one))
         two = hop(chain(shape, k + 1, k - 1, me, total, dot, far, two))
-    one = hop(chain(shape, 6, 4, me, total, dot, far, one), (1,))
-    two = hop(chain(shape, 7, 5, me, total, dot, far, two), (1,))
-    return one, flip(two)
+    return me, total, far, dot, one, flip(two), across
 
 
 def on_ring(

time: 112 us -> 100 us (0.89); the launches traced: 110 us -> 99.8 us
  starting transfers between devices: 67.6 us -> 43.4 us
  waiting for transfers between devices: 24.8 us -> 38.5 us
    ppermute x32 -> x28, starting transfers between devices: 53.7 us -> 38.6 us  [hop(): return lax.ppermute(value, 'term', pairs)]
    ppermute x32 -> x28, waiting for transfers between devices: 19.2 us -> 34.4 us  [hop(): return lax.ppermute(value, 'term', pairs)]
    ppermute x24 -> x22, starting transfers between devices: 13.9 us -> 4.81 us  [flip(): return lax.ppermute(value, 'term', [(i, i ^ 1) for i in range(16)])]
    ppermute x24 -> x22, waiting for transfers between devices: 5.54 us -> 4.12 us  [flip(): return lax.ppermute(value, 'term', [(i, i ^ 1) for i in range(16)])]
  transfers between devices with their start and end apart: 56 -> 50, of which waited for: 23 -> 25; matrix products, arithmetic and copies ran while one was open for 1% -> 1% of each run, Pallas kernels for 1% -> 1%
where the time goes in v9:
time: 100 us; the launch traced here: 99.8 us
  starting transfers between devices  43.4 us (43%)
  waiting for transfers between devices  38.5 us (38%)
  Pallas kernels  13.9 us (14%)
  local copies, waits for them, and re-layouts  1.8 us (2%)
  between operations  1.52 us (2%)
    ppermute x28, starting transfers between devices, hop(): return lax.ppermute(value, 'term', pairs)  38.6 us
    ppermute x28, waiting for transfers between devices, hop(): return lax.ppermute(value, 'term', pairs)  34.4 us
    pallas_call x2, Pallas kernels, apply_blocks(): pl.pallas_call(functools.partial(blocks_kernel, first, shape, entries), i...  11.3 us
    ppermute x22, starting transfers between devices, flip(): return lax.ppermute(value, 'term', [(i, i ^ 1) for i in range(16)])  4.81 us
    ppermute x22, waiting for transfers between devices, flip(): return lax.ppermute(value, 'term', [(i, i ^ 1) for i in range(16)])  4.12 us
  transfers between devices with their start and end apart: 50, of which 25 were waited for; matrix products, arithmetic and copies ran while one was open for 1% of the time, Pallas kernels for 1%

profile of v9, /device:TPU:0, one launch (start us, length us, event | category | flops | bytes accessed | tf_op | source)
XLA Modules:
  0.0 99.8 jit_solution(6362324265137357021)
XLA Ops:
  1.1 2.6 %collective-permute-start.4 = (bf16[3,32,512]{2,1,0:T(8,128)(2,1)}, bf16[3,32,512]{2,1,0:T(8,128)(2,1)S(1)}, u32[]{:S(2)}, u32[]{:S(2)}) collective-permute-start(bf16[3,32,512]{2,1,0:T(8,128)(2,1)} %wave_ref.5), channel_id=1, source_target_pairs={{0,4},{1,3},{4,8},{5,1},{8,12},{9,5},{12,14},{13,9},{14,10},{15,13... | collective-permute-start | bytes 294920 | tf_op jit(solution)/shard_map/ppermute | solution.py:368
  3.8 1.6 %collective-permute-start.1 = (bf16[3,32,512]{2,1,0:T(8,128)(2,1)S(1)}, bf16[3,32,512]{2,1,0:T(8,128)(2,1)S(1)}, u32[]{:S(2)}, u32[]{:S(2)}) collective-permute-start(bf16[3,32,512]{2,1,0:T(8,128)(2,1)S(1)} %collective-permute-done.refs_1_), channel_id=1, source_target_pairs={{0,4},{1,3},{4,8},{5,1},{8,12},{9,5},{12,14},{13,9},{14,10},{15,13... | collective-permute-start | bytes 294920 | tf_op jit(solution)/shard_map/ppermute | solution.py:368
  5.4 1.2 %collective-permute-done.4.refs_2_ = bf16[3,32,512]{2,1,0:T(8,128)(2,1)S(1)} collective-permute-done((bf16[3,32,512]{2,1,0:T(8,128)(2,1)}, bf16[3,32,512]{2,1,0:T(8,128)(2,1)S(1)}, u32[]{:S(2)}, u32[]{:S(2)}) %collective-permute-start.4) | collective-permute-done | bytes 98336 | tf_op jit(solution)/shard_map/ppermute | solution.py:368
  6.5 2.1 %collective-permute-start.7 = (bf16[3,32,512]{2,1,0:T(8,128)(2,1)S(1)}, bf16[3,32,512]{2,1,0:T(8,128)(2,1)S(1)}, u32[]{:S(2)}, u32[]{:S(2)}) collective-permute-start(bf16[3,32,512]{2,1,0:T(8,128)(2,1)S(1)} %collective-permute-done.4.refs_2_), channel_id=1, source_target_pairs={{0,4},{1,3},{4,8},{5,1},{8,12},{9,5},{12,14},{13,9},{14,10},{15,13... | collective-permute-start | bytes 294920 | tf_op jit(solution)/shard_map/ppermute | solution.py:368
  8.6 1.6 %collective-permute-start.2 = (bf16[3,32,512]{2,1,0:T(8,128)(2,1)S(1)}, bf16[3,32,512]{2,1,0:T(8,128)(2,1)S(1)}, u32[]{:S(2)}, u32[]{:S(2)}) collective-permute-start(bf16[3,32,512]{2,1,0:T(8,128)(2,1)S(1)} %collective-permute-done.1.refs_3_), channel_id=1, source_target_pairs={{0,4},{1,3},{4,8},{5,1},{8,12},{9,5},{12,14},{13,9},{14,10},{15,13... | collective-permute-start | bytes 294920 | tf_op jit(solution)/shard_map/ppermute | solution.py:368
  10.2 3.1 %collective-permute-start.13 = (bf16[3,32,512]{2,1,0:T(8,128)(2,1)}, bf16[3,32,512]{2,1,0:T(8,128)(2,1)S(1)}, u32[]{:S(2)}, u32[]{:S(2)}) collective-permute-start(bf16[3,32,512]{2,1,0:T(8,128)(2,1)} %wave_ref.5), channel_id=1, source_target_pairs={{0,14},{1,15},{4,10},{5,11},{8,6},{9,7},{12,2},{13,3},{14,0},{15,1... | collective-permute-start | bytes 294920 | tf_op jit(solution)/shard_map/ppermute | solution.py:368
  13.3 1.5 %collective-permute-start.8 = (bf16[3,32,512]{2,1,0:T(8,128)(2,1)S(1)}, bf16[3,32,512]{2,1,0:T(8,128)(2,1)S(1)}, u32[]{:S(2)}, u32[]{:S(2)}) collective-permute-start(bf16[3,32,512]{2,1,0:T(8,128)(2,1)S(1)} %collective-permute-done.7.refs_6_), channel_id=1, source_target_pairs={{0,1},{1,0},{2,3},{3,2},{4,5},{5,4},{6,7},{7,6},{8,9},{9,8},{10,11... | collective-permute-start | bytes 294920 | tf_op jit(solution)/shard_map/ppermute | solution.py:359
  16.3 2.3 %collective-permute-done.13.refs_14_ = bf16[3,32,512]{2,1,0:T(8,128)(2,1)S(1)} collective-permute-done((bf16[3,32,512]{2,1,0:T(8,128)(2,1)}, bf16[3,32,512]{2,1,0:T(8,128)(2,1)S(1)}, u32[]{:S(2)}, u32[]{:S(2)}) %collective-permute-start.13) | collective-permute-done | bytes 98336 | tf_op jit(solution)/shard_map/ppermute | solution.py:368
  23.2 5.9 %shard_map.95 = (f32[3,512,512]{2,1,0:T(8,128)S(1)}, bf16[2,16,3200]{2,1,0:T(8,128)(2,1)S(1)}, bf16[6,16,3200]{2,1,0:T(8,128)(2,1)S(1)}, f32[8,128]{1,0:T(8,128)S(1)}, f32[8,128]{1,0:T(8,128)S(1)}) custom-call(s32[1]{0:T(128)} %bitcast.me_ref.refs_0_.refs_2_, s32[17]{0:T(128)S(1)} %pad_add_fusion.ints_ref, ...), custom_call_target="tpu_custom_call" | custom-call | flops 4294967296 | bytes 8388608 | tf_op jit(solution)/shard_map/pallas_call | solution.py:225
  29.7 1.1 %collective-permute-done.15.other_ref = bf16[2,16,3200]{2,1,0:T(8,128)(2,1)S(1)} collective-permute-done((bf16[2,16,3200]{2,1,0:T(8,128)(2,1)S(1)}, bf16[2,16,3200]{2,1,0:T(8,128)(2,1)S(1)}, u32[]{:S(2)}, u32[]{:S(2)}) %collective-permute-start.15) | collective-permute-done | bytes 204832 | tf_op jit(solution)/shard_map/ppermute | solution.py:359
  31.2 1.7 %collective-permute-start.20 = (bf16[16,3200]{1,0:T(8,128)(2,1)S(1)}, bf16[16,3200]{1,0:T(8,128)(2,1)S(1)}, u32[]{:S(2)}, u32[]{:S(2)}) collective-permute-start(bf16[16,3200]{1,0:T(8,128)(2,1)S(1)} %shard_map.99), channel_id=1, source_target_pairs={{0,4},{1,3},{4,8},{5,1},{8,12},{9,5},{12,14},{13,9},{14,10},{15,13... | collective-permute-start | bytes 307208 | tf_op jit(solution)/shard_map/ppermute | solution.py:368
  33.6 3.4 %collective-permute-done.20.refs_0_ = bf16[16,3200]{1,0:T(8,128)(2,1)S(1)} collective-permute-done((bf16[16,3200]{1,0:T(8,128)(2,1)S(1)}, bf16[16,3200]{1,0:T(8,128)(2,1)S(1)}, u32[]{:S(2)}, u32[]{:S(2)}) %collective-permute-start.20) | collective-permute-done | bytes 102432 | tf_op jit(solution)/shard_map/ppermute | solution.py:368
  38.1 1.3 %collective-permute-start.18 = (bf16[16,3200]{1,0:T(8,128)(2,1)S(1)}, bf16[16,3200]{1,0:T(8,128)(2,1)S(1)}, u32[]{:S(2)}, u32[]{:S(2)}) collective-permute-start(bf16[16,3200]{1,0:T(8,128)(2,1)S(1)} %shard_map.97), channel_id=1, source_target_pairs={{0,4},{1,3},{4,8},{5,1},{8,12},{9,5},{12,14},{13,9},{14,10},{15,13... | collective-permute-start | bytes 307208 | tf_op jit(solution)/shard_map/ppermute | solution.py:368
  39.5 2.3 %collective-permute-done.21.refs_0_ = bf16[16,3200]{1,0:T(8,128)(2,1)S(1)} collective-permute-done((bf16[16,3200]{1,0:T(8,128)(2,1)S(1)}, bf16[16,3200]{1,0:T(8,128)(2,1)S(1)}, u32[]{:S(2)}, u32[]{:S(2)}) %collective-permute-start.21) | collective-permute-done | bytes 102432 | tf_op jit(solution)/shard_map/ppermute | solution.py:368
  42.5 3.4 %collective-permute-start.24 = (bf16[16,3200]{1,0:T(8,128)(2,1)S(1)}, bf16[16,3200]{1,0:T(8,128)(2,1)S(1)}, u32[]{:S(2)}, u32[]{:S(2)}) collective-permute-start(bf16[16,3200]{1,0:T(8,128)(2,1)S(1)} %shard_map.102), channel_id=1, source_target_pairs={{0,14},{1,15},{4,10},{5,11},{8,6},{9,7},{12,2},{13,3},{14,0},{15,1... | collective-permute-start | bytes 307208 | tf_op jit(solution)/shard_map/ppermute | solution.py:368
  45.9 1.5 %collective-permute-start.19 = (bf16[16,3200]{1,0:T(8,128)(2,1)S(1)}, bf16[16,3200]{1,0:T(8,128)(2,1)S(1)}, u32[]{:S(2)}, u32[]{:S(2)}) collective-permute-start(bf16[16,3200]{1,0:T(8,128)(2,1)S(1)} %shard_map.98), channel_id=1, source_target_pairs={{0,4},{1,3},{4,8},{5,1},{8,12},{9,5},{12,14},{13,9},{14,10},{15,13... | collective-permute-start | bytes 307208 | tf_op jit(solution)/shard_map/ppermute | solution.py:368
  47.4 3.3 %collective-permute-done.24.refs_6_ = bf16[16,3200]{1,0:T(8,128)(2,1)S(1)} collective-permute-done((bf16[16,3200]{1,0:T(8,128)(2,1)S(1)}, bf16[16,3200]{1,0:T(8,128)(2,1)S(1)}, u32[]{:S(2)}, u32[]{:S(2)}) %collective-permute-start.24) | collective-permute-done | bytes 102432 | tf_op jit(solution)/shard_map/ppermute | solution.py:368
  50.7 1.0 collective-permute-done.19.refs_4_
  53.9 1.2 %collective-permute-start.27 = (bf16[16,3200]{1,0:T(8,128)(2,1)S(1)}, bf16[16,3200]{1,0:T(8,128)(2,1)S(1)}, u32[]{:S(2)}, u32[]{:S(2)}) collective-permute-start(bf16[16,3200]{1,0:T(8,128)(2,1)S(1)} %collective-permute-done.25.refs_1_), channel_id=1, source_target_pairs={{0,4},{1,3},{4,8},{5,1},{8,12},{9,5},{12,14},{13,9},{14,10},{15,13... | collective-permute-start | bytes 307208 | tf_op jit(solution)/shard_map/ppermute | solution.py:368
  55.0 2.2 %collective-permute-done.26.refs_2_ = bf16[16,3200]{1,0:T(8,128)(2,1)S(1)} collective-permute-done((bf16[16,3200]{1,0:T(8,128)(2,1)S(1)}, bf16[16,3200]{1,0:T(8,128)(2,1)S(1)}, u32[]{:S(2)}, u32[]{:S(2)}) %collective-permute-start.26) | collective-permute-done | bytes 102432 | tf_op jit(solution)/shard_map/ppermute | solution.py:368
  58.5 1.2 %collective-permute-start.31 = (bf16[16,3200]{1,0:T(8,128)(2,1)S(1)}, bf16[16,3200]{1,0:T(8,128)(2,1)S(1)}, u32[]{:S(2)}, u32[]{:S(2)}) collective-permute-start(bf16[16,3200]{1,0:T(8,128)(2,1)S(1)} %collective-permute-done.27.refs_3_), channel_id=1, source_target_pairs={{0,4},{1,3},{4,8},{5,1},{8,12},{9,5},{12,14},{13,9},{14,10},{15,13... | collective-permute-start | bytes 307208 | tf_op jit(solution)/shard_map/ppermute | solution.py:368
  59.7 2.5 %collective-permute-start.38 = (bf16[16,3200]{1,0:T(8,128)(2,1)S(1)}, bf16[16,3200]{1,0:T(8,128)(2,1)S(1)}, u32[]{:S(2)}, u32[]{:S(2)}) collective-permute-start(bf16[16,3200]{1,0:T(8,128)(2,1)S(1)} %get-tuple-element.43.refs_0_), channel_id=1, source_target_pairs={{0,14},{1,15},{4,10},{5,11},{8,6},{9,7},{12,2},{13,3},{14,0},{15,1... | collective-permute-start | bytes 307208 | tf_op jit(solution)/shard_map/ppermute | solution.py:368
  63.2 1.2 %collective-permute-start.35 = (bf16[16,3200]{1,0:T(8,128)(2,1)S(1)}, bf16[16,3200]{1,0:T(8,128)(2,1)S(1)}, u32[]{:S(2)}, u32[]{:S(2)}) collective-permute-start(bf16[16,3200]{1,0:T(8,128)(2,1)S(1)} %collective-permute-done.31.refs_7_), channel_id=1, source_target_pairs={{0,4},{1,3},{4,8},{5,1},{8,12},{9,5},{12,14},{13,9},{14,10},{15,13... | collective-permute-start | bytes 307208 | tf_op jit(solution)/shard_map/ppermute | solution.py:368
  64.4 3.5 %collective-permute-done.38.refs_14_ = bf16[16,3200]{1,0:T(8,128)(2,1)S(1)} collective-permute-done((bf16[16,3200]{1,0:T(8,128)(2,1)S(1)}, bf16[16,3200]{1,0:T(8,128)(2,1)S(1)}, u32[]{:S(2)}, u32[]{:S(2)}) %collective-permute-start.38) | collective-permute-done | bytes 102432 | tf_op jit(solution)/shard_map/ppermute | solution.py:368
  71.3 5.4 %shard_map.104 = (f32[3,512,512]{2,1,0:T(8,128)S(1)}, bf16[2,16,3200]{2,1,0:T(8,128)(2,1)S(1)}, bf16[6,16,3200]{2,1,0:T(8,128)(2,1)S(1)}, f32[8,128]{1,0:T(8,128)S(1)}, f32[8,128]{1,0:T(8,128)S(1)}) custom-call(s32[1]{0:T(128)} %bitcast.me_ref.refs_0_.refs_2_, s32[17]{0:T(128)S(1)} %pad_add_fusion.ints_ref, bf16[16,3200]{1,0:T(8,128)(2,1)S(1)} %get-tuple-element.43.refs_0_, ...), custom_call_target="tpu_custom_call" | custom-call | flops 4294967296 | bytes 8388608 | tf_op jit(solution)/shard_map/pallas_call | solution.py:225
  76.9 1.3 %collective-permute-done.40.other_ref = bf16[2,16,3200]{2,1,0:T(8,128)(2,1)S(1)} collective-permute-done((bf16[2,16,3200]{2,1,0:T(8,128)(2,1)S(1)}, bf16[2,16,3200]{2,1,0:T(8,128)(2,1)S(1)}, u32[]{:S(2)}, u32[]{:S(2)}) %collective-permute-start.40) | collective-permute-done | bytes 204832 | tf_op jit(solution)/shard_map/ppermute | solution.py:359
  78.4 1.6 %collective-permute-start.45 = (bf16[16,3200]{1,0:T(8,128)(2,1)S(1)}, bf16[16,3200]{1,0:T(8,128)(2,1)S(1)}, u32[]{:S(2)}, u32[]{:S(2)}) collective-permute-start(bf16[16,3200]{1,0:T(8,128)(2,1)S(1)} %shard_map.108), channel_id=1, source_target_pairs={{0,4},{1,3},{4,8},{5,1},{8,12},{9,5},{12,14},{13,9},{14,10},{15,13... | collective-permute-start | bytes 307208 | tf_op jit(solution)/shard_map/ppermute | solution.py:368
  80.8 3.4 %collective-permute-done.45.refs_0_ = bf16[16,3200]{1,0:T(8,128)(2,1)S(1)} collective-permute-done((bf16[16,3200]{1,0:T(8,128)(2,1)S(1)}, bf16[16,3200]{1,0:T(8,128)(2,1)S(1)}, u32[]{:S(2)}, u32[]{:S(2)}) %collective-permute-start.45) | collective-permute-done | bytes 102432 | tf_op jit(solution)/shard_map/ppermute | solution.py:368
  86.1 2.8 %collective-permute-done.46.refs_0_ = bf16[16,3200]{1,0:T(8,128)(2,1)S(1)} collective-permute-done((bf16[16,3200]{1,0:T(8,128)(2,1)S(1)}, bf16[16,3200]{1,0:T(8,128)(2,1)S(1)}, u32[]{:S(2)}, u32[]{:S(2)}) %collective-permute-start.46) | collective-permute-done | bytes 102432 | tf_op jit(solution)/shard_map/ppermute | solution.py:368
  89.5 3.4 %collective-permute-start.49 = (bf16[16,3200]{1,0:T(8,128)(2,1)S(1)}, bf16[16,3200]{1,0:T(8,128)(2,1)S(1)}, u32[]{:S(2)}, u32[]{:S(2)}) collective-permute-start(bf16[16,3200]{1,0:T(8,128)(2,1)S(1)} %shard_map.111), channel_id=1, source_target_pairs={{0,14},{1,15},{4,10},{5,11},{8,6},{9,7},{12,2},{13,3},{14,0},{15,1... | collective-permute-start | bytes 307208 | tf_op jit(solution)/shard_map/ppermute | solution.py:368
  93.0 1.6 %collective-permute-start.44 = (bf16[16,3200]{1,0:T(8,128)(2,1)S(1)}, bf16[16,3200]{1,0:T(8,128)(2,1)S(1)}, u32[]{:S(2)}, u32[]{:S(2)}) collective-permute-start(bf16[16,3200]{1,0:T(8,128)(2,1)S(1)} %shard_map.107), channel_id=1, source_target_pairs={{0,4},{1,3},{4,8},{5,1},{8,12},{9,5},{12,14},{13,9},{14,10},{15,13... | collective-permute-start | bytes 307208 | tf_op jit(solution)/shard_map/ppermute | solution.py:368
  94.6 3.3 %collective-permute-done.49.refs_8_ = bf16[16,3200]{1,0:T(8,128)(2,1)S(1)} collective-permute-done((bf16[16,3200]{1,0:T(8,128)(2,1)S(1)}, bf16[16,3200]{1,0:T(8,128)(2,1)S(1)}, u32[]{:S(2)}, u32[]{:S(2)}) %collective-permute-start.49) | collective-permute-done | bytes 102432 | tf_op jit(solution)/shard_map/ppermute | solution.py:368
  (96 shorter events, 23.2 us)
Async XLA Ops:
  1.1 5.4 %collective-permute-start.4 = (bf16[3,32,512]{2,1,0:T(8,128)(2,1)}, bf16[3,32,512]{2,1,0:T(8,128)(2,1)S(1)}, u32[]{:S(2)}, u32[]{:S(2)}) collective-permute-start(bf16[3,32,512]{2,1,0:T(8,128)(2,1)} %wave_ref.5), channel_id=1, source_target_pairs={{0,4},{1,3},{4,8},{5,1},{8,12},{9,5},{12,14},{13,9},{14,10},{15,13... | collective-permute-start | bytes 294920 | tf_op jit(solution)/shard_map/ppermute | solution.py:368
  3.8 4.8 %collective-permute-start.1 = (bf16[3,32,512]{2,1,0:T(8,128)(2,1)S(1)}, bf16[3,32,512]{2,1,0:T(8,128)(2,1)S(1)}, u32[]{:S(2)}, u32[]{:S(2)}) collective-permute-start(bf16[3,32,512]{2,1,0:T(8,128)(2,1)S(1)} %collective-permute-done.refs_1_), channel_id=1, source_target_pairs={{0,4},{1,3},{4,8},{5,1},{8,12},{9,5},{12,14},{13,9},{14,10},{15,13... | collective-permute-start | bytes 294920 | tf_op jit(solution)/shard_map/ppermute | solution.py:368
  6.5 6.7 %collective-permute-start.7 = (bf16[3,32,512]{2,1,0:T(8,128)(2,1)S(1)}, bf16[3,32,512]{2,1,0:T(8,128)(2,1)S(1)}, u32[]{:S(2)}, u32[]{:S(2)}) collective-permute-start(bf16[3,32,512]{2,1,0:T(8,128)(2,1)S(1)} %collective-permute-done.4.refs_2_), channel_id=1, source_target_pairs={{0,4},{1,3},{4,8},{5,1},{8,12},{9,5},{12,14},{13,9},{14,10},{15,13... | collective-permute-start | bytes 294920 | tf_op jit(solution)/shard_map/ppermute | solution.py:368
  8.6 6.2 %collective-permute-start.2 = (bf16[3,32,512]{2,1,0:T(8,128)(2,1)S(1)}, bf16[3,32,512]{2,1,0:T(8,128)(2,1)S(1)}, u32[]{:S(2)}, u32[]{:S(2)}) collective-permute-start(bf16[3,32,512]{2,1,0:T(8,128)(2,1)S(1)} %collective-permute-done.1.refs_3_), channel_id=1, source_target_pairs={{0,4},{1,3},{4,8},{5,1},{8,12},{9,5},{12,14},{13,9},{14,10},{15,13... | collective-permute-start | bytes 294920 | tf_op jit(solution)/shard_map/ppermute | solution.py:368
  10.2 5.7 %collective-permute-start.5 = (bf16[3,32,512]{2,1,0:T(8,128)(2,1)S(1)}, bf16[3,32,512]{2,1,0:T(8,128)(2,1)S(1)}, u32[]{:S(2)}, u32[]{:S(2)}) collective-permute-start(bf16[3,32,512]{2,1,0:T(8,128)(2,1)S(1)} %collective-permute-done.4.refs_2_), channel_id=1, source_target_pairs={{0,1},{1,0},{2,3},{3,2},{4,5},{5,4},{6,7},{7,6},{8,9},{9,8},{10,11... | collective-permute-start | bytes 294920 | tf_op jit(solution)/shard_map/ppermute | solution.py:359
  10.2 8.3 %collective-permute-start.13 = (bf16[3,32,512]{2,1,0:T(8,128)(2,1)}, bf16[3,32,512]{2,1,0:T(8,128)(2,1)S(1)}, u32[]{:S(2)}, u32[]{:S(2)}) collective-permute-start(bf16[3,32,512]{2,1,0:T(8,128)(2,1)} %wave_ref.5), channel_id=1, source_target_pairs={{0,14},{1,15},{4,10},{5,11},{8,6},{9,7},{12,2},{13,3},{14,0},{15,1... | collective-permute-start | bytes 294920 | tf_op jit(solution)/shard_map/ppermute | solution.py:368
  13.3 6.2 %collective-permute-start.10 = (bf16[3,32,512]{2,1,0:T(8,128)(2,1)S(1)}, bf16[3,32,512]{2,1,0:T(8,128)(2,1)S(1)}, u32[]{:S(2)}, u32[]{:S(2)}) collective-permute-start(bf16[3,32,512]{2,1,0:T(8,128)(2,1)S(1)} %collective-permute-done.7.refs_6_), channel_id=1, source_target_pairs={{0,4},{1,3},{4,8},{5,1},{8,12},{9,5},{12,14},{13,9},{14,10},{15,13... | collective-permute-start | bytes 294920 | tf_op jit(solution)/shard_map/ppermute | solution.py:368
  13.3 6.2 %collective-permute-start.8 = (bf16[3,32,512]{2,1,0:T(8,128)(2,1)S(1)}, bf16[3,32,512]{2,1,0:T(8,128)(2,1)S(1)}, u32[]{:S(2)}, u32[]{:S(2)}) collective-permute-start(bf16[3,32,512]{2,1,0:T(8,128)(2,1)S(1)} %collective-permute-done.7.refs_6_), channel_id=1, source_target_pairs={{0,1},{1,0},{2,3},{3,2},{4,5},{5,4},{6,7},{7,6},{8,9},{9,8},{10,11... | collective-permute-start | bytes 294920 | tf_op jit(solution)/shard_map/ppermute | solution.py:359
  14.8 5.7 %collective-permute-start.3 = (bf16[3,32,512]{2,1,0:T(8,128)(2,1)S(1)}, bf16[3,32,512]{2,1,0:T(8,128)(2,1)S(1)}, u32[]{:S(2)}, u32[]{:S(2)}) collective-permute-start(bf16[3,32,512]{2,1,0:T(8,128)(2,1)S(1)} %collective-permute-done.2.refs_7_), channel_id=1, source_target_pairs={{0,4},{1,3},{4,8},{5,1},{8,12},{9,5},{12,14},{13,9},{14,10},{15,13... | collective-permute-start | bytes 294920 | tf_op jit(solution)/shard_map/ppermute | solution.py:368
  15.9 7.2 %collective-permute-start.6 = (bf16[3,32,512]{2,1,0:T(8,128)(2,1)S(1)}, bf16[3,32,512]{2,1,0:T(8,128)(2,1)S(1)}, u32[]{:S(2)}, u32[]{:S(2)}) collective-permute-start(bf16[3,32,512]{2,1,0:T(8,128)(2,1)S(1)} %collective-permute-done.1.refs_3_), channel_id=1, source_target_pairs={{0,1},{1,0},{2,3},{3,2},{4,5},{5,4},{6,7},{7,6},{8,9},{9,8},{10,11... | collective-permute-start | bytes 294920 | tf_op jit(solution)/shard_map/ppermute | solution.py:359
  30.8 6.2 %collective-permute-start.16 = (bf16[6,16,3200]{2,1,0:T(8,128)(2,1)S(1)}, bf16[6,16,3200]{2,1,0:T(8,128)(2,1)S(1)}, u32[]{:S(2)}, u32[]{:S(2)}) collective-permute-start(bf16[6,16,3200]{2,1,0:T(8,128)(2,1)S(1)} %get-tuple-element.37), channel_id=1, source_target_pairs={{0,1},{1,0},{2,3},{3,2},{4,5},{5,4},{6,7},{7,6},{8,9},{9,8},{10,11... | collective-permute-start | bytes 1843208 | tf_op jit(solution)/shard_map/ppermute | solution.py:359
  31.2 5.8 %collective-permute-start.20 = (bf16[16,3200]{1,0:T(8,128)(2,1)S(1)}, bf16[16,3200]{1,0:T(8,128)(2,1)S(1)}, u32[]{:S(2)}, u32[]{:S(2)}) collective-permute-start(bf16[16,3200]{1,0:T(8,128)(2,1)S(1)} %shard_map.99), channel_id=1, source_target_pairs={{0,4},{1,3},{4,8},{5,1},{8,12},{9,5},{12,14},{13,9},{14,10},{15,13... | collective-permute-start | bytes 307208 | tf_op jit(solution)/shard_map/ppermute | solution.py:368
  32.9 5.2 %collective-permute-start.17 = (bf16[16,3200]{1,0:T(8,128)(2,1)S(1)}, bf16[16,3200]{1,0:T(8,128)(2,1)S(1)}, u32[]{:S(2)}, u32[]{:S(2)}) collective-permute-start(bf16[16,3200]{1,0:T(8,128)(2,1)S(1)} %shard_map.96), channel_id=1, source_target_pairs={{0,4},{1,3},{4,8},{5,1},{8,12},{9,5},{12,14},{13,9},{14,10},{15,13... | collective-permute-start | bytes 307208 | tf_op jit(solution)/shard_map/ppermute | solution.py:368
  37.0 4.7 %collective-permute-start.21 = (bf16[16,3200]{1,0:T(8,128)(2,1)S(1)}, bf16[16,3200]{1,0:T(8,128)(2,1)S(1)}, u32[]{:S(2)}, u32[]{:S(2)}) collective-permute-start(bf16[16,3200]{1,0:T(8,128)(2,1)S(1)} %shard_map.100), channel_id=1, source_target_pairs={{0,4},{1,3},{4,8},{5,1},{8,12},{9,5},{12,14},{13,9},{14,10},{15,13... | collective-permute-start | bytes 307208 | tf_op jit(solution)/shard_map/ppermute | solution.py:368
  38.1 7.7 %collective-permute-start.18 = (bf16[16,3200]{1,0:T(8,128)(2,1)S(1)}, bf16[16,3200]{1,0:T(8,128)(2,1)S(1)}, u32[]{:S(2)}, u32[]{:S(2)}) collective-permute-start(bf16[16,3200]{1,0:T(8,128)(2,1)S(1)} %shard_map.97), channel_id=1, source_target_pairs={{0,4},{1,3},{4,8},{5,1},{8,12},{9,5},{12,14},{13,9},{14,10},{15,13... | collective-permute-start | bytes 307208 | tf_op jit(solution)/shard_map/ppermute | solution.py:368
  41.8 5.5 %collective-permute-start.22 = (bf16[16,3200]{1,0:T(8,128)(2,1)S(1)}, bf16[16,3200]{1,0:T(8,128)(2,1)S(1)}, u32[]{:S(2)}, u32[]{:S(2)}) collective-permute-start(bf16[16,3200]{1,0:T(8,128)(2,1)S(1)} %shard_map.101), channel_id=1, source_target_pairs={{0,4},{1,3},{4,8},{5,1},{8,12},{9,5},{12,14},{13,9},{14,10},{15,13... | collective-permute-start | bytes 307208 | tf_op jit(solution)/shard_map/ppermute | solution.py:368
  42.5 8.2 %collective-permute-start.24 = (bf16[16,3200]{1,0:T(8,128)(2,1)S(1)}, bf16[16,3200]{1,0:T(8,128)(2,1)S(1)}, u32[]{:S(2)}, u32[]{:S(2)}) collective-permute-start(bf16[16,3200]{1,0:T(8,128)(2,1)S(1)} %shard_map.102), channel_id=1, source_target_pairs={{0,14},{1,15},{4,10},{5,11},{8,6},{9,7},{12,2},{13,3},{14,0},{15,1... | collective-permute-start | bytes 307208 | tf_op jit(solution)/shard_map/ppermute | solution.py:368
  45.9 5.8 %collective-permute-start.19 = (bf16[16,3200]{1,0:T(8,128)(2,1)S(1)}, bf16[16,3200]{1,0:T(8,128)(2,1)S(1)}, u32[]{:S(2)}, u32[]{:S(2)}) collective-permute-start(bf16[16,3200]{1,0:T(8,128)(2,1)S(1)} %shard_map.98), channel_id=1, source_target_pairs={{0,4},{1,3},{4,8},{5,1},{8,12},{9,5},{12,14},{13,9},{14,10},{15,13... | collective-permute-start | bytes 307208 | tf_op jit(solution)/shard_map/ppermute | solution.py:368
  57.2 4.9 %collective-permute-start.30 = (bf16[16,3200]{1,0:T(8,128)(2,1)S(1)}, bf16[16,3200]{1,0:T(8,128)(2,1)S(1)}, u32[]{:S(2)}, u32[]{:S(2)}) collective-permute-start(bf16[16,3200]{1,0:T(8,128)(2,1)S(1)} %collective-permute-done.26.refs_2_), channel_id=1, source_target_pairs={{0,4},{1,3},{4,8},{5,1},{8,12},{9,5},{12,14},{13,9},{14,10},{15,13... | collective-permute-start | bytes 307208 | tf_op jit(solution)/shard_map/ppermute | solution.py:368
  59.7 8.2 %collective-permute-start.38 = (bf16[16,3200]{1,0:T(8,128)(2,1)S(1)}, bf16[16,3200]{1,0:T(8,128)(2,1)S(1)}, u32[]{:S(2)}, u32[]{:S(2)}) collective-permute-start(bf16[16,3200]{1,0:T(8,128)(2,1)S(1)} %get-tuple-element.43.refs_0_), channel_id=1, source_target_pairs={{0,14},{1,15},{4,10},{5,11},{8,6},{9,7},{12,2},{13,3},{14,0},{15,1... | collective-permute-start | bytes 307208 | tf_op jit(solution)/shard_map/ppermute | solution.py:368
  62.1 6.7 %collective-permute-start.34 = (bf16[16,3200]{1,0:T(8,128)(2,1)S(1)}, bf16[16,3200]{1,0:T(8,128)(2,1)S(1)}, u32[]{:S(2)}, u32[]{:S(2)}) collective-permute-start(bf16[16,3200]{1,0:T(8,128)(2,1)S(1)} %collective-permute-done.30.refs_6_), channel_id=1, source_target_pairs={{0,4},{1,3},{4,8},{5,1},{8,12},{9,5},{12,14},{13,9},{14,10},{15,13... | collective-permute-start | bytes 307208 | tf_op jit(solution)/shard_map/ppermute | solution.py:368
  62.8 6.1 %collective-permute-start.32 = (bf16[16,3200]{1,0:T(8,128)(2,1)S(1)}, bf16[16,3200]{1,0:T(8,128)(2,1)S(1)}, u32[]{:S(2)}, u32[]{:S(2)}) collective-permute-start(bf16[16,3200]{1,0:T(8,128)(2,1)S(1)} %collective-permute-done.30.refs_6_), channel_id=1, source_target_pairs={{0,1},{1,0},{2,3},{3,2},{4,5},{5,4},{6,7},{7,6},{8,9},{9,8},{10,11... | collective-permute-start | bytes 307208 | tf_op jit(solution)/shard_map/ppermute | solution.py:359
  63.2 6.8 %collective-permute-start.35 = (bf16[16,3200]{1,0:T(8,128)(2,1)S(1)}, bf16[16,3200]{1,0:T(8,128)(2,1)S(1)}, u32[]{:S(2)}, u32[]{:S(2)}) collective-permute-start(bf16[16,3200]{1,0:T(8,128)(2,1)S(1)} %collective-permute-done.31.refs_7_), channel_id=1, source_target_pairs={{0,4},{1,3},{4,8},{5,1},{8,12},{9,5},{12,14},{13,9},{14,10},{15,13... | collective-permute-start | bytes 307208 | tf_op jit(solution)/shard_map/ppermute | solution.py:368
  64.4 5.6 %collective-permute-start.29 = (bf16[16,3200]{1,0:T(8,128)(2,1)S(1)}, bf16[16,3200]{1,0:T(8,128)(2,1)S(1)}, u32[]{:S(2)}, u32[]{:S(2)}) collective-permute-start(bf16[16,3200]{1,0:T(8,128)(2,1)S(1)} %collective-permute-done.27.refs_3_), channel_id=1, source_target_pairs={{0,1},{1,0},{2,3},{3,2},{4,5},{5,4},{6,7},{7,6},{8,9},{9,8},{10,11... | collective-permute-start | bytes 307208 | tf_op jit(solution)/shard_map/ppermute | solution.py:359
  78.2 6.0 %collective-permute-start.41 = (bf16[6,16,3200]{2,1,0:T(8,128)(2,1)S(1)}, bf16[6,16,3200]{2,1,0:T(8,128)(2,1)S(1)}, u32[]{:S(2)}, u32[]{:S(2)}) collective-permute-start(bf16[6,16,3200]{2,1,0:T(8,128)(2,1)S(1)} %get-tuple-element.50), channel_id=1, source_target_pairs={{0,1},{1,0},{2,3},{3,2},{4,5},{5,4},{6,7},{7,6},{8,9},{9,8},{10,11... | collective-permute-start | bytes 1843208 | tf_op jit(solution)/shard_map/ppermute | solution.py:359
  78.4 5.8 %collective-permute-start.45 = (bf16[16,3200]{1,0:T(8,128)(2,1)S(1)}, bf16[16,3200]{1,0:T(8,128)(2,1)S(1)}, u32[]{:S(2)}, u32[]{:S(2)}) collective-permute-start(bf16[16,3200]{1,0:T(8,128)(2,1)S(1)} %shard_map.108), channel_id=1, source_target_pairs={{0,4},{1,3},{4,8},{5,1},{8,12},{9,5},{12,14},{13,9},{14,10},{15,13... | collective-permute-start | bytes 307208 | tf_op jit(solution)/shard_map/ppermute | solution.py:368
  80.0 5.3 %collective-permute-start.42 = (bf16[16,3200]{1,0:T(8,128)(2,1)S(1)}, bf16[16,3200]{1,0:T(8,128)(2,1)S(1)}, u32[]{:S(2)}, u32[]{:S(2)}) collective-permute-start(bf16[16,3200]{1,0:T(8,128)(2,1)S(1)} %shard_map.105), channel_id=1, source_target_pairs={{0,4},{1,3},{4,8},{5,1},{8,12},{9,5},{12,14},{13,9},{14,10},{15,13... | collective-permute-start | bytes 307208 | tf_op jit(solution)/shard_map/ppermute | solution.py:368
  84.2 4.7 %collective-permute-start.46 = (bf16[16,3200]{1,0:T(8,128)(2,1)S(1)}, bf16[16,3200]{1,0:T(8,128)(2,1)S(1)}, u32[]{:S(2)}, u32[]{:S(2)}) collective-permute-start(bf16[16,3200]{1,0:T(8,128)(2,1)S(1)} %shard_map.109), channel_id=1, source_target_pairs={{0,4},{1,3},{4,8},{5,1},{8,12},{9,5},{12,14},{13,9},{14,10},{15,13... | collective-permute-start | bytes 307208 | tf_op jit(solution)/shard_map/ppermute | solution.py:368
  85.3 7.6 %collective-permute-start.43 = (bf16[16,3200]{1,0:T(8,128)(2,1)S(1)}, bf16[16,3200]{1,0:T(8,128)(2,1)S(1)}, u32[]{:S(2)}, u32[]{:S(2)}) collective-permute-start(bf16[16,3200]{1,0:T(8,128)(2,1)S(1)} %shard_map.106), channel_id=1, source_target_pairs={{0,4},{1,3},{4,8},{5,1},{8,12},{9,5},{12,14},{13,9},{14,10},{15,13... | collective-permute-start | bytes 307208 | tf_op jit(solution)/shard_map/ppermute | solution.py:368
  89.0 5.5 %collective-permute-start.47 = (bf16[16,3200]{1,0:T(8,128)(2,1)S(1)}, bf16[16,3200]{1,0:T(8,128)(2,1)S(1)}, u32[]{:S(2)}, u32[]{:S(2)}) collective-permute-start(bf16[16,3200]{1,0:T(8,128)(2,1)S(1)} %shard_map.110), channel_id=1, source_target_pairs={{0,4},{1,3},{4,8},{5,1},{8,12},{9,5},{12,14},{13,9},{14,10},{15,13... | collective-permute-start | bytes 307208 | tf_op jit(solution)/shard_map/ppermute | solution.py:368
  89.5 8.3 %collective-permute-start.49 = (bf16[16,3200]{1,0:T(8,128)(2,1)S(1)}, bf16[16,3200]{1,0:T(8,128)(2,1)S(1)}, u32[]{:S(2)}, u32[]{:S(2)}) collective-permute-start(bf16[16,3200]{1,0:T(8,128)(2,1)S(1)} %shard_map.111), channel_id=1, source_target_pairs={{0,14},{1,15},{4,10},{5,11},{8,6},{9,7},{12,2},{13,3},{14,0},{15,1... | collective-permute-start | bytes 307208 | tf_op jit(solution)/shard_map/ppermute | solution.py:368
  93.0 5.8 %collective-permute-start.44 = (bf16[16,3200]{1,0:T(8,128)(2,1)S(1)}, bf16[16,3200]{1,0:T(8,128)(2,1)S(1)}, u32[]{:S(2)}, u32[]{:S(2)}) collective-permute-start(bf16[16,3200]{1,0:T(8,128)(2,1)S(1)} %shard_map.107), channel_id=1, source_target_pairs={{0,4},{1,3},{4,8},{5,1},{8,12},{9,5},{12,14},{13,9},{14,10},{15,13... | collective-permute-start | bytes 307208 | tf_op jit(solution)/shard_map/ppermute | solution.py:368
  (22 other events, 77.1 us)

commit v10 on v9

--- a/solution.py
+++ b/solution.py
@@ -92,8 +92,21 @@
     return (HALF, rows // HALF * sectors * width + LANES)
 
 
-def prepare_kernel(wave_ref, diag_ref, _, own_ref, square_ref):
-    own_ref[...] = wave_ref[...]
+def copy_kernel(in_ref, out_ref):
+    out_ref[...] = in_ref[...]
+
+
+def copied(value):
+    return pl.pallas_call(
+        copy_kernel,
+        in_specs=[VMEM],
+        out_specs=VMEM,
+        out_shape=jax.ShapeDtypeStruct(value.shape, value.dtype),
+        compiler_params=PARAMS,
+    )(value)
+
+
+def square_kernel(wave_ref, diag_ref, square_ref):
     square = jnp.zeros((8, 128), jnp.float32)
     for s in range(wave_ref.shape[0]):
         wave = wave_ref[s].astype(jnp.float32)
@@ -101,17 +114,14 @@
     square_ref[...] = square
 
 
-def prepare(wave, diag, after):
+def weighted_square(wave, diag):
     return pl.pallas_call(
-        prepare_kernel,
-        in_specs=[VMEM, VMEM, HBM],
-        out_specs=[VMEM, VMEM],
-        out_shape=[
-            jax.ShapeDtypeStruct(wave.shape, wave.dtype),
-            jax.ShapeDtypeStruct((8, 128), jnp.float32),
-        ],
+        square_kernel,
+        in_specs=[VMEM, VMEM],
+        out_specs=VMEM,
+        out_shape=jax.ShapeDtypeStruct((8, 128), jnp.float32),
         compiler_params=PARAMS,
-    )(wave, diag, after)
+    )(wave, diag)
 
 
 def blocks_kernel(first, shape, entries, me_ref, ints_ref, *refs):
@@ -372,15 +382,26 @@
     return hop(value, 4, 4)
 
 
-def gather(own):
+def gather(own, beside=()):
     one, two = own, flip(own)
     across, two = lax.optimization_barrier((own, two))
     pieces = [one, two]
     across = opposite(across)
-    for _ in range(ROUNDS):
+    results = []
+    for k in range(ROUNDS):
         one, two = hop(one), hop(two)
+        if k < len(beside):
+            results.append(beside[k](*results))
+        if k < ROUNDS - 1:
+            ready = results[-1:] if beside else []
+            if k == 1:
+                two, across, ready = lax.optimization_barrier((two, across, ready))
+            else:
+                two, ready = lax.optimization_barrier((two, ready))
+            if ready:
+                results[-1] = ready[0]
         pieces += [one, two, flip(one), flip(two)]
-    return pieces + [across, flip(across)], two
+    return pieces + [across, flip(across)], results
 
 
 def scatter(shape, me, total, near, far, dot):
@@ -392,6 +413,8 @@
     across = opposite(chain(shape, 6, 4, me, total, dot, far))
     for k in (2, 4):
         one = hop(chain(shape, k, k - 2, me, total, dot, far, one))
+        if k == 4:
+            two, across = lax.optimization_barrier((two, across))
         two = hop(chain(shape, k + 1, k - 1, me, total, dot, far, two))
     return me, total, far, dot, one, flip(two), across
 
@@ -403,11 +426,15 @@
     sectors, rows, width = shape
     entries = float(sectors * rows * lax.axis_size("term") * width)
     me = lax.axis_index("term").astype(jnp.int32).reshape(1)
-    ints = jnp.concatenate([block_source, block_target, live_count])
     blocks = (left_blocks, right_blocks, shape)
 
-    fields, last = gather(wavefunction)
-    fields[0], square = prepare(wavefunction, diagonal, last)
+    beside = (
+        lambda: jnp.concatenate([block_source, block_target, live_count]),
+        lambda _: copied(wavefunction),
+        lambda _, own: weighted_square(own, diagonal),
+    )
+    (_, *fields), (ints, own, square) = gather(wavefunction, beside)
+    fields = [own, *fields]
     total, near, far, dot, scale = apply_blocks(me, ints, fields, (square,), *blocks, True, entries)
     first_image, terms, correction, message = davidson_step(
         scale, wavefunction, diagonal, scatter(shape, me, total, near, far, dot), entries

time: 100 us -> 99.3 us (level)
  waiting for transfers between devices: 38.5 us -> 21.2 us
  starting transfers between devices: 43.4 us -> 60 us
    ppermute x28, waiting for transfers between devices: 34.4 us -> 17.4 us  [hop(): return lax.ppermute(value, 'term', pairs)]
    ppermute x28, starting transfers between devices: 38.6 us -> 52.4 us  [hop(): return lax.ppermute(value, 'term', pairs)]
    ppermute x22, starting transfers between devices: 4.81 us -> 7.59 us  [flip(): return lax.ppermute(value, 'term', [(i, i ^ 1) for i in range(16)])]
  transfers between devices with their start and end apart: 50 -> 50, of which waited for: 25 -> 19; matrix products, arithmetic and copies ran while one was open for 1% -> 1% of each run, Pallas kernels for 1% -> 1%
where the time goes in v10:
time: 99.3 us; the launch traced here: 99.1 us
  starting transfers between devices  60 us (60%)
  waiting for transfers between devices  21.2 us (21%)
  Pallas kernels  13.8 us (14%)
  local copies, waits for them, and re-layouts  1.8 us (2%)
  between operations  1.53 us (2%)
    ppermute x28, starting transfers between devices, hop(): return lax.ppermute(value, 'term', pairs)  52.4 us
    ppermute x28, waiting for transfers between devices, hop(): return lax.ppermute(value, 'term', pairs)  17.4 us
    pallas_call x2, Pallas kernels, apply_blocks(): pl.pallas_call(functools.partial(blocks_kernel, first, shape, entries), i...  11.3 us
    ppermute x22, starting transfers between devices, flip(): return lax.ppermute(value, 'term', [(i, i ^ 1) for i in range(16)])  7.59 us
    ppermute x22, waiting for transfers between devices, flip(): return lax.ppermute(value, 'term', [(i, i ^ 1) for i in range(16)])  3.81 us
  transfers between devices with their start and end apart: 50, of which 19 were waited for; matrix products, arithmetic and copies ran while one was open for 1% of the time, Pallas kernels for 1%

profile of v10, /device:TPU:0, one launch (start us, length us, event | category | flops | bytes accessed | tf_op | source)
XLA Modules:
  0.0 99.1 jit_solution(13729374261602376577)
XLA Ops:
  1.1 2.6 %collective-permute-start.4 = (bf16[3,32,512]{2,1,0:T(8,128)(2,1)}, bf16[3,32,512]{2,1,0:T(8,128)(2,1)S(1)}, u32[]{:S(2)}, u32[]{:S(2)}) collective-permute-start(bf16[3,32,512]{2,1,0:T(8,128)(2,1)} %wave_ref.3), channel_id=1, source_target_pairs={{0,4},{1,3},{4,8},{5,1},{8,12},{9,5},{12,14},{13,9},{14,10},{15,13... | collective-permute-start | bytes 294920 | tf_op jit(solution)/shard_map/ppermute | solution.py:378
  4.4 1.6 %collective-permute-start.1 = (bf16[3,32,512]{2,1,0:T(8,128)(2,1)S(1)}, bf16[3,32,512]{2,1,0:T(8,128)(2,1)S(1)}, u32[]{:S(2)}, u32[]{:S(2)}) collective-permute-start(bf16[3,32,512]{2,1,0:T(8,128)(2,1)S(1)} %collective-permute-done.refs_1_), channel_id=1, source_target_pairs={{0,4},{1,3},{4,8},{5,1},{8,12},{9,5},{12,14},{13,9},{14,10},{15,13... | collective-permute-start | bytes 294920 | tf_op jit(solution)/shard_map/ppermute | solution.py:378
  6.8 2.6 %collective-permute-start.3 = (bf16[3,32,512]{2,1,0:T(8,128)(2,1)}, bf16[3,32,512]{2,1,0:T(8,128)(2,1)S(1)}, u32[]{:S(2)}, u32[]{:S(2)}) collective-permute-start(bf16[3,32,512]{2,1,0:T(8,128)(2,1)} %wave_ref.3), channel_id=1, source_target_pairs={{0,14},{1,15},{4,10},{5,11},{8,6},{9,7},{12,2},{13,3},{14,0},{15,1... | collective-permute-start | bytes 294920 | tf_op jit(solution)/shard_map/ppermute | solution.py:378
  11.7 3.7 %collective-permute-done.7.refs_6_ = bf16[3,32,512]{2,1,0:T(8,128)(2,1)S(1)} collective-permute-done((bf16[3,32,512]{2,1,0:T(8,128)(2,1)S(1)}, bf16[3,32,512]{2,1,0:T(8,128)(2,1)S(1)}, u32[]{:S(2)}, u32[]{:S(2)}) %collective-permute-start.7) | collective-permute-done | bytes 98336 | tf_op jit(solution)/shard_map/ppermute | solution.py:378
  16.4 1.7 %collective-permute-start.11 = (bf16[3,32,512]{2,1,0:T(8,128)(2,1)S(1)}, bf16[3,32,512]{2,1,0:T(8,128)(2,1)S(1)}, u32[]{:S(2)}, u32[]{:S(2)}) collective-permute-start(bf16[3,32,512]{2,1,0:T(8,128)(2,1)S(1)} %collective-permute-done.2.refs_7_), channel_id=1, source_target_pairs={{0,4},{1,3},{4,8},{5,1},{8,12},{9,5},{12,14},{13,9},{14,10},{15,13... | collective-permute-start | bytes 294920 | tf_op jit(solution)/shard_map/ppermute | solution.py:378
  18.6 1.4 %collective-permute-done.10.refs_10_ = bf16[3,32,512]{2,1,0:T(8,128)(2,1)S(1)} collective-permute-done((bf16[3,32,512]{2,1,0:T(8,128)(2,1)S(1)}, bf16[3,32,512]{2,1,0:T(8,128)(2,1)S(1)}, u32[]{:S(2)}, u32[]{:S(2)}) %collective-permute-start.10) | collective-permute-done | bytes 98336 | tf_op jit(solution)/shard_map/ppermute | solution.py:378
  22.3 5.9 %shard_map.96 = (f32[3,512,512]{2,1,0:T(8,128)S(1)}, bf16[2,16,3200]{2,1,0:T(8,128)(2,1)S(1)}, bf16[6,16,3200]{2,1,0:T(8,128)(2,1)S(1)}, f32[8,128]{1,0:T(8,128)S(1)}, f32[8,128]{1,0:T(8,128)S(1)}) custom-call(s32[1]{0:T(128)} %bitcast.me_ref.refs_0_.refs_2_, s32[17]{0:T(128)S(1)} %pad_add_fusion.ints_ref, ...), custom_call_target="tpu_custom_call" | custom-call | flops 4294967296 | bytes 8388608 | tf_op jit(solution)/shard_map/pallas_call | solution.py:235
  28.2 1.5 %collective-permute-start.15 = (bf16[2,16,3200]{2,1,0:T(8,128)(2,1)S(1)}, bf16[2,16,3200]{2,1,0:T(8,128)(2,1)S(1)}, u32[]{:S(2)}, u32[]{:S(2)}) collective-permute-start(bf16[2,16,3200]{2,1,0:T(8,128)(2,1)S(1)} %get-tuple-element.47), channel_id=1, source_target_pairs={{0,1},{1,0},{2,3},{3,2},{4,5},{5,4},{6,7},{7,6},{8,9},{9,8},{10,11... | collective-permute-start | bytes 614408 | tf_op jit(solution)/shard_map/ppermute | solution.py:369
  31.3 3.0 %collective-permute-start.20 = (bf16[16,3200]{1,0:T(8,128)(2,1)S(1)}, bf16[16,3200]{1,0:T(8,128)(2,1)S(1)}, u32[]{:S(2)}, u32[]{:S(2)}) collective-permute-start(bf16[16,3200]{1,0:T(8,128)(2,1)S(1)} %shard_map.100), channel_id=1, source_target_pairs={{0,4},{1,3},{4,8},{5,1},{8,12},{9,5},{12,14},{13,9},{14,10},{15,13... | collective-permute-start | bytes 307208 | tf_op jit(solution)/shard_map/ppermute | solution.py:378
  35.4 1.6 %collective-permute-start.22 = (bf16[16,3200]{1,0:T(8,128)(2,1)S(1)}, bf16[16,3200]{1,0:T(8,128)(2,1)S(1)}, u32[]{:S(2)}, u32[]{:S(2)}) collective-permute-start(bf16[16,3200]{1,0:T(8,128)(2,1)S(1)} %shard_map.102), channel_id=1, source_target_pairs={{0,14},{1,15},{4,10},{5,11},{8,6},{9,7},{12,2},{13,3},{14,0},{15,1... | collective-permute-start | bytes 307208 | tf_op jit(solution)/shard_map/ppermute | solution.py:378
  37.1 1.9 %collective-permute-start.21 = (bf16[16,3200]{1,0:T(8,128)(2,1)S(1)}, bf16[16,3200]{1,0:T(8,128)(2,1)S(1)}, u32[]{:S(2)}, u32[]{:S(2)}) collective-permute-start(bf16[16,3200]{1,0:T(8,128)(2,1)S(1)} %shard_map.101), channel_id=1, source_target_pairs={{0,4},{1,3},{4,8},{5,1},{8,12},{9,5},{12,14},{13,9},{14,10},{15,13... | collective-permute-start | bytes 307208 | tf_op jit(solution)/shard_map/ppermute | solution.py:378
  39.3 2.5 %collective-permute-start.18 = (bf16[16,3200]{1,0:T(8,128)(2,1)S(1)}, bf16[16,3200]{1,0:T(8,128)(2,1)S(1)}, u32[]{:S(2)}, u32[]{:S(2)}) collective-permute-start(bf16[16,3200]{1,0:T(8,128)(2,1)S(1)} %shard_map.98), channel_id=1, source_target_pairs={{0,4},{1,3},{4,8},{5,1},{8,12},{9,5},{12,14},{13,9},{14,10},{15,13... | collective-permute-start | bytes 307208 | tf_op jit(solution)/shard_map/ppermute | solution.py:378
  43.0 1.5 %collective-permute-start.23 = (bf16[16,3200]{1,0:T(8,128)(2,1)S(1)}, bf16[16,3200]{1,0:T(8,128)(2,1)S(1)}, u32[]{:S(2)}, u32[]{:S(2)}) collective-permute-start(bf16[16,3200]{1,0:T(8,128)(2,1)S(1)} %shard_map.103), channel_id=1, source_target_pairs={{0,4},{1,3},{4,8},{5,1},{8,12},{9,5},{12,14},{13,9},{14,10},{15,13... | collective-permute-start | bytes 307208 | tf_op jit(solution)/shard_map/ppermute | solution.py:378
  44.6 2.2 %collective-permute-start.19 = (bf16[16,3200]{1,0:T(8,128)(2,1)S(1)}, bf16[16,3200]{1,0:T(8,128)(2,1)S(1)}, u32[]{:S(2)}, u32[]{:S(2)}) collective-permute-start(bf16[16,3200]{1,0:T(8,128)(2,1)S(1)} %shard_map.99), channel_id=1, source_target_pairs={{0,4},{1,3},{4,8},{5,1},{8,12},{9,5},{12,14},{13,9},{14,10},{15,13... | collective-permute-start | bytes 307208 | tf_op jit(solution)/shard_map/ppermute | solution.py:378
  47.7 1.6 %collective-permute-done.19.refs_4_ = bf16[16,3200]{1,0:T(8,128)(2,1)S(1)} collective-permute-done((bf16[16,3200]{1,0:T(8,128)(2,1)S(1)}, bf16[16,3200]{1,0:T(8,128)(2,1)S(1)}, u32[]{:S(2)}, u32[]{:S(2)}) %collective-permute-start.19) | collective-permute-done | bytes 102432 | tf_op jit(solution)/shard_map/ppermute | solution.py:378
  50.2 2.1 %collective-permute-start.26 = (bf16[16,3200]{1,0:T(8,128)(2,1)S(1)}, bf16[16,3200]{1,0:T(8,128)(2,1)S(1)}, u32[]{:S(2)}, u32[]{:S(2)}) collective-permute-start(bf16[16,3200]{1,0:T(8,128)(2,1)S(1)} %get-tuple-element.57.refs_0_), channel_id=1, source_target_pairs={{0,4},{1,3},{4,8},{5,1},{8,12},{9,5},{12,14},{13,9},{14,10},{15,13... | collective-permute-start | bytes 307208 | tf_op jit(solution)/shard_map/ppermute | solution.py:378
  52.4 2.4 %collective-permute-start.27 = (bf16[16,3200]{1,0:T(8,128)(2,1)S(1)}, bf16[16,3200]{1,0:T(8,128)(2,1)S(1)}, u32[]{:S(2)}, u32[]{:S(2)}) collective-permute-start(bf16[16,3200]{1,0:T(8,128)(2,1)S(1)} %collective-permute-done.25.refs_1_), channel_id=1, source_target_pairs={{0,4},{1,3},{4,8},{5,1},{8,12},{9,5},{12,14},{13,9},{14,10},{15,13... | collective-permute-start | bytes 307208 | tf_op jit(solution)/shard_map/ppermute | solution.py:378
  54.9 2.1 %collective-permute-start.30 = (bf16[16,3200]{1,0:T(8,128)(2,1)S(1)}, bf16[16,3200]{1,0:T(8,128)(2,1)S(1)}, u32[]{:S(2)}, u32[]{:S(2)}) collective-permute-start(bf16[16,3200]{1,0:T(8,128)(2,1)S(1)} %collective-permute-done.26.refs_2_), channel_id=1, source_target_pairs={{0,4},{1,3},{4,8},{5,1},{8,12},{9,5},{12,14},{13,9},{14,10},{15,13... | collective-permute-start | bytes 307208 | tf_op jit(solution)/shard_map/ppermute | solution.py:378
  57.0 1.9 %collective-permute-start.32 = (bf16[16,3200]{1,0:T(8,128)(2,1)S(1)}, bf16[16,3200]{1,0:T(8,128)(2,1)S(1)}, u32[]{:S(2)}, u32[]{:S(2)}) collective-permute-start(bf16[16,3200]{1,0:T(8,128)(2,1)S(1)} %get-tuple-element.57.refs_0_), channel_id=1, source_target_pairs={{0,14},{1,15},{4,10},{5,11},{8,6},{9,7},{12,2},{13,3},{14,0},{15,1... | collective-permute-start | bytes 307208 | tf_op jit(solution)/shard_map/ppermute | solution.py:378
  60.6 3.2 %collective-permute-start.35 = (bf16[16,3200]{1,0:T(8,128)(2,1)S(1)}, bf16[16,3200]{1,0:T(8,128)(2,1)S(1)}, u32[]{:S(2)}, u32[]{:S(2)}) collective-permute-start(bf16[16,3200]{1,0:T(8,128)(2,1)S(1)} %collective-permute-done.30.refs_6_), channel_id=1, source_target_pairs={{0,4},{1,3},{4,8},{5,1},{8,12},{9,5},{12,14},{13,9},{14,10},{15,13... | collective-permute-start | bytes 307208 | tf_op jit(solution)/shard_map/ppermute | solution.py:378
  64.9 1.5 %collective-permute-start.36 = (bf16[16,3200]{1,0:T(8,128)(2,1)S(1)}, bf16[16,3200]{1,0:T(8,128)(2,1)S(1)}, u32[]{:S(2)}, u32[]{:S(2)}) collective-permute-start(bf16[16,3200]{1,0:T(8,128)(2,1)S(1)} %collective-permute-done.31.refs_7_), channel_id=1, source_target_pairs={{0,4},{1,3},{4,8},{5,1},{8,12},{9,5},{12,14},{13,9},{14,10},{15,13... | collective-permute-start | bytes 307208 | tf_op jit(solution)/shard_map/ppermute | solution.py:378
  67.4 2.2 %collective-permute-done.36.refs_11_ = bf16[16,3200]{1,0:T(8,128)(2,1)S(1)} collective-permute-done((bf16[16,3200]{1,0:T(8,128)(2,1)S(1)}, bf16[16,3200]{1,0:T(8,128)(2,1)S(1)}, u32[]{:S(2)}, u32[]{:S(2)}) %collective-permute-start.36) | collective-permute-done | bytes 102432 | tf_op jit(solution)/shard_map/ppermute | solution.py:378
  69.6 1.3 %collective-permute-done.38.refs_13_ = bf16[16,3200]{1,0:T(8,128)(2,1)S(1)} collective-permute-done((bf16[16,3200]{1,0:T(8,128)(2,1)S(1)}, bf16[16,3200]{1,0:T(8,128)(2,1)S(1)}, u32[]{:S(2)}, u32[]{:S(2)}) %collective-permute-start.38) | collective-permute-done | bytes 102432 | tf_op jit(solution)/shard_map/ppermute | solution.py:369
  70.9 5.4 %shard_map.105 = (f32[3,512,512]{2,1,0:T(8,128)S(1)}, bf16[2,16,3200]{2,1,0:T(8,128)(2,1)S(1)}, bf16[6,16,3200]{2,1,0:T(8,128)(2,1)S(1)}, f32[8,128]{1,0:T(8,128)S(1)}, f32[8,128]{1,0:T(8,128)S(1)}) custom-call(s32[1]{0:T(128)} %bitcast.me_ref.refs_0_.refs_2_, s32[17]{0:T(128)S(1)} %pad_add_fusion.ints_ref, bf16[16,3200]{1,0:T(8,128)(2,1)S(1)} %get-tuple-element.57.refs_0_, ...), custom_call_target="tpu_custom_call" | custom-call | flops 4294967296 | bytes 8388608 | tf_op jit(solution)/shard_map/pallas_call | solution.py:235
  76.2 1.5 %collective-permute-start.40 = (bf16[2,16,3200]{2,1,0:T(8,128)(2,1)S(1)}, bf16[2,16,3200]{2,1,0:T(8,128)(2,1)S(1)}, u32[]{:S(2)}, u32[]{:S(2)}) collective-permute-start(bf16[2,16,3200]{2,1,0:T(8,128)(2,1)S(1)} %get-tuple-element.64), channel_id=1, source_target_pairs={{0,1},{1,0},{2,3},{3,2},{4,5},{5,4},{6,7},{7,6},{8,9},{9,8},{10,11... | collective-permute-start | bytes 614408 | tf_op jit(solution)/shard_map/ppermute | solution.py:369
  79.2 2.8 %collective-permute-start.45 = (bf16[16,3200]{1,0:T(8,128)(2,1)S(1)}, bf16[16,3200]{1,0:T(8,128)(2,1)S(1)}, u32[]{:S(2)}, u32[]{:S(2)}) collective-permute-start(bf16[16,3200]{1,0:T(8,128)(2,1)S(1)} %shard_map.109), channel_id=1, source_target_pairs={{0,4},{1,3},{4,8},{5,1},{8,12},{9,5},{12,14},{13,9},{14,10},{15,13... | collective-permute-start | bytes 307208 | tf_op jit(solution)/shard_map/ppermute | solution.py:378
  82.0 2.2 %collective-permute-start.42 = (bf16[16,3200]{1,0:T(8,128)(2,1)S(1)}, bf16[16,3200]{1,0:T(8,128)(2,1)S(1)}, u32[]{:S(2)}, u32[]{:S(2)}) collective-permute-start(bf16[16,3200]{1,0:T(8,128)(2,1)S(1)} %shard_map.106), channel_id=1, source_target_pairs={{0,4},{1,3},{4,8},{5,1},{8,12},{9,5},{12,14},{13,9},{14,10},{15,13... | collective-permute-start | bytes 307208 | tf_op jit(solution)/shard_map/ppermute | solution.py:378
  85.3 1.9 %collective-permute-start.46 = (bf16[16,3200]{1,0:T(8,128)(2,1)S(1)}, bf16[16,3200]{1,0:T(8,128)(2,1)S(1)}, u32[]{:S(2)}, u32[]{:S(2)}) collective-permute-start(bf16[16,3200]{1,0:T(8,128)(2,1)S(1)} %shard_map.110), channel_id=1, source_target_pairs={{0,4},{1,3},{4,8},{5,1},{8,12},{9,5},{12,14},{13,9},{14,10},{15,13... | collective-permute-start | bytes 307208 | tf_op jit(solution)/shard_map/ppermute | solution.py:378
  87.3 3.5 %collective-permute-start.43 = (bf16[16,3200]{1,0:T(8,128)(2,1)S(1)}, bf16[16,3200]{1,0:T(8,128)(2,1)S(1)}, u32[]{:S(2)}, u32[]{:S(2)}) collective-permute-start(bf16[16,3200]{1,0:T(8,128)(2,1)S(1)} %shard_map.107), channel_id=1, source_target_pairs={{0,4},{1,3},{4,8},{5,1},{8,12},{9,5},{12,14},{13,9},{14,10},{15,13... | collective-permute-start | bytes 307208 | tf_op jit(solution)/shard_map/ppermute | solution.py:378
  92.0 1.4 %collective-permute-start.48 = (bf16[16,3200]{1,0:T(8,128)(2,1)S(1)}, bf16[16,3200]{1,0:T(8,128)(2,1)S(1)}, u32[]{:S(2)}, u32[]{:S(2)}) collective-permute-start(bf16[16,3200]{1,0:T(8,128)(2,1)S(1)} %shard_map.112), channel_id=1, source_target_pairs={{0,4},{1,3},{4,8},{5,1},{8,12},{9,5},{12,14},{13,9},{14,10},{15,13... | collective-permute-start | bytes 307208 | tf_op jit(solution)/shard_map/ppermute | solution.py:378
  93.5 2.2 %collective-permute-start.44 = (bf16[16,3200]{1,0:T(8,128)(2,1)S(1)}, bf16[16,3200]{1,0:T(8,128)(2,1)S(1)}, u32[]{:S(2)}, u32[]{:S(2)}) collective-permute-start(bf16[16,3200]{1,0:T(8,128)(2,1)S(1)} %shard_map.108), channel_id=1, source_target_pairs={{0,4},{1,3},{4,8},{5,1},{8,12},{9,5},{12,14},{13,9},{14,10},{15,13... | collective-permute-start | bytes 307208 | tf_op jit(solution)/shard_map/ppermute | solution.py:378
  96.7 1.5 %collective-permute-done.44.refs_6_ = bf16[16,3200]{1,0:T(8,128)(2,1)S(1)} collective-permute-done((bf16[16,3200]{1,0:T(8,128)(2,1)S(1)}, bf16[16,3200]{1,0:T(8,128)(2,1)S(1)}, u32[]{:S(2)}, u32[]{:S(2)}) %collective-permute-start.44) | collective-permute-done | bytes 102432 | tf_op jit(solution)/shard_map/ppermute | solution.py:378
  (97 shorter events, 23.2 us)
Async XLA Ops:
  1.1 8.3 %collective-permute-start.4 = (bf16[3,32,512]{2,1,0:T(8,128)(2,1)}, bf16[3,32,512]{2,1,0:T(8,128)(2,1)S(1)}, u32[]{:S(2)}, u32[]{:S(2)}) collective-permute-start(bf16[3,32,512]{2,1,0:T(8,128)(2,1)} %wave_ref.3), channel_id=1, source_target_pairs={{0,4},{1,3},{4,8},{5,1},{8,12},{9,5},{12,14},{13,9},{14,10},{15,13... | collective-permute-start | bytes 294920 | tf_op jit(solution)/shard_map/ppermute | solution.py:378
  4.4 5.0 %collective-permute-start.1 = (bf16[3,32,512]{2,1,0:T(8,128)(2,1)S(1)}, bf16[3,32,512]{2,1,0:T(8,128)(2,1)S(1)}, u32[]{:S(2)}, u32[]{:S(2)}) collective-permute-start(bf16[3,32,512]{2,1,0:T(8,128)(2,1)S(1)} %collective-permute-done.refs_1_), channel_id=1, source_target_pairs={{0,4},{1,3},{4,8},{5,1},{8,12},{9,5},{12,14},{13,9},{14,10},{15,13... | collective-permute-start | bytes 294920 | tf_op jit(solution)/shard_map/ppermute | solution.py:378
  6.8 8.7 %collective-permute-start.3 = (bf16[3,32,512]{2,1,0:T(8,128)(2,1)}, bf16[3,32,512]{2,1,0:T(8,128)(2,1)S(1)}, u32[]{:S(2)}, u32[]{:S(2)}) collective-permute-start(bf16[3,32,512]{2,1,0:T(8,128)(2,1)} %wave_ref.3), channel_id=1, source_target_pairs={{0,14},{1,15},{4,10},{5,11},{8,6},{9,7},{12,2},{13,3},{14,0},{15,1... | collective-permute-start | bytes 294920 | tf_op jit(solution)/shard_map/ppermute | solution.py:378
  9.4 5.9 %collective-permute-start.7 = (bf16[3,32,512]{2,1,0:T(8,128)(2,1)S(1)}, bf16[3,32,512]{2,1,0:T(8,128)(2,1)S(1)}, u32[]{:S(2)}, u32[]{:S(2)}) collective-permute-start(bf16[3,32,512]{2,1,0:T(8,128)(2,1)S(1)} %collective-permute-done.4.refs_2_), channel_id=1, source_target_pairs={{0,4},{1,3},{4,8},{5,1},{8,12},{9,5},{12,14},{13,9},{14,10},{15,13... | collective-permute-start | bytes 294920 | tf_op jit(solution)/shard_map/ppermute | solution.py:378
  9.4 7.0 %collective-permute-start.2 = (bf16[3,32,512]{2,1,0:T(8,128)(2,1)S(1)}, bf16[3,32,512]{2,1,0:T(8,128)(2,1)S(1)}, u32[]{:S(2)}, u32[]{:S(2)}) collective-permute-start(bf16[3,32,512]{2,1,0:T(8,128)(2,1)S(1)} %collective-permute-done.1.refs_3_), channel_id=1, source_target_pairs={{0,4},{1,3},{4,8},{5,1},{8,12},{9,5},{12,14},{13,9},{14,10},{15,13... | collective-permute-start | bytes 294920 | tf_op jit(solution)/shard_map/ppermute | solution.py:378
  11.6 6.5 %collective-permute-start.5 = (bf16[3,32,512]{2,1,0:T(8,128)(2,1)S(1)}, bf16[3,32,512]{2,1,0:T(8,128)(2,1)S(1)}, u32[]{:S(2)}, u32[]{:S(2)}) collective-permute-start(bf16[3,32,512]{2,1,0:T(8,128)(2,1)S(1)} %collective-permute-done.4.refs_2_), channel_id=1, source_target_pairs={{0,1},{1,0},{2,3},{3,2},{4,5},{5,4},{6,7},{7,6},{8,9},{9,8},{10,11... | collective-permute-start | bytes 294920 | tf_op jit(solution)/shard_map/ppermute | solution.py:369
  15.4 4.6 %collective-permute-start.10 = (bf16[3,32,512]{2,1,0:T(8,128)(2,1)S(1)}, bf16[3,32,512]{2,1,0:T(8,128)(2,1)S(1)}, u32[]{:S(2)}, u32[]{:S(2)}) collective-permute-start(bf16[3,32,512]{2,1,0:T(8,128)(2,1)S(1)} %collective-permute-done.7.refs_6_), channel_id=1, source_target_pairs={{0,4},{1,3},{4,8},{5,1},{8,12},{9,5},{12,14},{13,9},{14,10},{15,13... | collective-permute-start | bytes 294920 | tf_op jit(solution)/shard_map/ppermute | solution.py:378
  16.4 4.6 %collective-permute-start.11 = (bf16[3,32,512]{2,1,0:T(8,128)(2,1)S(1)}, bf16[3,32,512]{2,1,0:T(8,128)(2,1)S(1)}, u32[]{:S(2)}, u32[]{:S(2)}) collective-permute-start(bf16[3,32,512]{2,1,0:T(8,128)(2,1)S(1)} %collective-permute-done.2.refs_7_), channel_id=1, source_target_pairs={{0,4},{1,3},{4,8},{5,1},{8,12},{9,5},{12,14},{13,9},{14,10},{15,13... | collective-permute-start | bytes 294920 | tf_op jit(solution)/shard_map/ppermute | solution.py:378
  30.8 4.5 %collective-permute-start.16 = (bf16[6,16,3200]{2,1,0:T(8,128)(2,1)S(1)}, bf16[6,16,3200]{2,1,0:T(8,128)(2,1)S(1)}, u32[]{:S(2)}, u32[]{:S(2)}) collective-permute-start(bf16[6,16,3200]{2,1,0:T(8,128)(2,1)S(1)} %get-tuple-element.49), channel_id=1, source_target_pairs={{0,1},{1,0},{2,3},{3,2},{4,5},{5,4},{6,7},{7,6},{8,9},{9,8},{10,11... | collective-permute-start | bytes 1843208 | tf_op jit(solution)/shard_map/ppermute | solution.py:369
  31.3 5.8 %collective-permute-start.20 = (bf16[16,3200]{1,0:T(8,128)(2,1)S(1)}, bf16[16,3200]{1,0:T(8,128)(2,1)S(1)}, u32[]{:S(2)}, u32[]{:S(2)}) collective-permute-start(bf16[16,3200]{1,0:T(8,128)(2,1)S(1)} %shard_map.100), channel_id=1, source_target_pairs={{0,4},{1,3},{4,8},{5,1},{8,12},{9,5},{12,14},{13,9},{14,10},{15,13... | collective-permute-start | bytes 307208 | tf_op jit(solution)/shard_map/ppermute | solution.py:378
  34.3 5.0 %collective-permute-start.17 = (bf16[16,3200]{1,0:T(8,128)(2,1)S(1)}, bf16[16,3200]{1,0:T(8,128)(2,1)S(1)}, u32[]{:S(2)}, u32[]{:S(2)}) collective-permute-start(bf16[16,3200]{1,0:T(8,128)(2,1)S(1)} %shard_map.97), channel_id=1, source_target_pairs={{0,4},{1,3},{4,8},{5,1},{8,12},{9,5},{12,14},{13,9},{14,10},{15,13... | collective-permute-start | bytes 307208 | tf_op jit(solution)/shard_map/ppermute | solution.py:378
  35.4 7.6 %collective-permute-start.22 = (bf16[16,3200]{1,0:T(8,128)(2,1)S(1)}, bf16[16,3200]{1,0:T(8,128)(2,1)S(1)}, u32[]{:S(2)}, u32[]{:S(2)}) collective-permute-start(bf16[16,3200]{1,0:T(8,128)(2,1)S(1)} %shard_map.102), channel_id=1, source_target_pairs={{0,14},{1,15},{4,10},{5,11},{8,6},{9,7},{12,2},{13,3},{14,0},{15,1... | collective-permute-start | bytes 307208 | tf_op jit(solution)/shard_map/ppermute | solution.py:378
  37.1 5.9 %collective-permute-start.21 = (bf16[16,3200]{1,0:T(8,128)(2,1)S(1)}, bf16[16,3200]{1,0:T(8,128)(2,1)S(1)}, u32[]{:S(2)}, u32[]{:S(2)}) collective-permute-start(bf16[16,3200]{1,0:T(8,128)(2,1)S(1)} %shard_map.101), channel_id=1, source_target_pairs={{0,4},{1,3},{4,8},{5,1},{8,12},{9,5},{12,14},{13,9},{14,10},{15,13... | collective-permute-start | bytes 307208 | tf_op jit(solution)/shard_map/ppermute | solution.py:378
  39.3 5.2 %collective-permute-start.18 = (bf16[16,3200]{1,0:T(8,128)(2,1)S(1)}, bf16[16,3200]{1,0:T(8,128)(2,1)S(1)}, u32[]{:S(2)}, u32[]{:S(2)}) collective-permute-start(bf16[16,3200]{1,0:T(8,128)(2,1)S(1)} %shard_map.98), channel_id=1, source_target_pairs={{0,4},{1,3},{4,8},{5,1},{8,12},{9,5},{12,14},{13,9},{14,10},{15,13... | collective-permute-start | bytes 307208 | tf_op jit(solution)/shard_map/ppermute | solution.py:378
  43.0 4.7 %collective-permute-start.23 = (bf16[16,3200]{1,0:T(8,128)(2,1)S(1)}, bf16[16,3200]{1,0:T(8,128)(2,1)S(1)}, u32[]{:S(2)}, u32[]{:S(2)}) collective-permute-start(bf16[16,3200]{1,0:T(8,128)(2,1)S(1)} %shard_map.103), channel_id=1, source_target_pairs={{0,4},{1,3},{4,8},{5,1},{8,12},{9,5},{12,14},{13,9},{14,10},{15,13... | collective-permute-start | bytes 307208 | tf_op jit(solution)/shard_map/ppermute | solution.py:378
  44.6 4.7 %collective-permute-start.19 = (bf16[16,3200]{1,0:T(8,128)(2,1)S(1)}, bf16[16,3200]{1,0:T(8,128)(2,1)S(1)}, u32[]{:S(2)}, u32[]{:S(2)}) collective-permute-start(bf16[16,3200]{1,0:T(8,128)(2,1)S(1)} %shard_map.99), channel_id=1, source_target_pairs={{0,4},{1,3},{4,8},{5,1},{8,12},{9,5},{12,14},{13,9},{14,10},{15,13... | collective-permute-start | bytes 307208 | tf_op jit(solution)/shard_map/ppermute | solution.py:378
  50.2 4.7 %collective-permute-start.26 = (bf16[16,3200]{1,0:T(8,128)(2,1)S(1)}, bf16[16,3200]{1,0:T(8,128)(2,1)S(1)}, u32[]{:S(2)}, u32[]{:S(2)}) collective-permute-start(bf16[16,3200]{1,0:T(8,128)(2,1)S(1)} %get-tuple-element.57.refs_0_), channel_id=1, source_target_pairs={{0,4},{1,3},{4,8},{5,1},{8,12},{9,5},{12,14},{13,9},{14,10},{15,13... | collective-permute-start | bytes 307208 | tf_op jit(solution)/shard_map/ppermute | solution.py:378
  52.4 6.6 %collective-permute-start.27 = (bf16[16,3200]{1,0:T(8,128)(2,1)S(1)}, bf16[16,3200]{1,0:T(8,128)(2,1)S(1)}, u32[]{:S(2)}, u32[]{:S(2)}) collective-permute-start(bf16[16,3200]{1,0:T(8,128)(2,1)S(1)} %collective-permute-done.25.refs_1_), channel_id=1, source_target_pairs={{0,4},{1,3},{4,8},{5,1},{8,12},{9,5},{12,14},{13,9},{14,10},{15,13... | collective-permute-start | bytes 307208 | tf_op jit(solution)/shard_map/ppermute | solution.py:378
  54.9 5.7 %collective-permute-start.30 = (bf16[16,3200]{1,0:T(8,128)(2,1)S(1)}, bf16[16,3200]{1,0:T(8,128)(2,1)S(1)}, u32[]{:S(2)}, u32[]{:S(2)}) collective-permute-start(bf16[16,3200]{1,0:T(8,128)(2,1)S(1)} %collective-permute-done.26.refs_2_), channel_id=1, source_target_pairs={{0,4},{1,3},{4,8},{5,1},{8,12},{9,5},{12,14},{13,9},{14,10},{15,13... | collective-permute-start | bytes 307208 | tf_op jit(solution)/shard_map/ppermute | solution.py:378
  57.0 7.6 %collective-permute-start.32 = (bf16[16,3200]{1,0:T(8,128)(2,1)S(1)}, bf16[16,3200]{1,0:T(8,128)(2,1)S(1)}, u32[]{:S(2)}, u32[]{:S(2)}) collective-permute-start(bf16[16,3200]{1,0:T(8,128)(2,1)S(1)} %get-tuple-element.57.refs_0_), channel_id=1, source_target_pairs={{0,14},{1,15},{4,10},{5,11},{8,6},{9,7},{12,2},{13,3},{14,0},{15,1... | collective-permute-start | bytes 307208 | tf_op jit(solution)/shard_map/ppermute | solution.py:378
  59.0 5.9 %collective-permute-start.31 = (bf16[16,3200]{1,0:T(8,128)(2,1)S(1)}, bf16[16,3200]{1,0:T(8,128)(2,1)S(1)}, u32[]{:S(2)}, u32[]{:S(2)}) collective-permute-start(bf16[16,3200]{1,0:T(8,128)(2,1)S(1)} %collective-permute-done.27.refs_3_), channel_id=1, source_target_pairs={{0,4},{1,3},{4,8},{5,1},{8,12},{9,5},{12,14},{13,9},{14,10},{15,13... | collective-permute-start | bytes 307208 | tf_op jit(solution)/shard_map/ppermute | solution.py:378
  59.4 6.9 %collective-permute-start.28 = (bf16[16,3200]{1,0:T(8,128)(2,1)S(1)}, bf16[16,3200]{1,0:T(8,128)(2,1)S(1)}, u32[]{:S(2)}, u32[]{:S(2)}) collective-permute-start(bf16[16,3200]{1,0:T(8,128)(2,1)S(1)} %collective-permute-done.26.refs_2_), channel_id=1, source_target_pairs={{0,1},{1,0},{2,3},{3,2},{4,5},{5,4},{6,7},{7,6},{8,9},{9,8},{10,11... | collective-permute-start | bytes 307208 | tf_op jit(solution)/shard_map/ppermute | solution.py:369
  60.6 6.3 %collective-permute-start.35 = (bf16[16,3200]{1,0:T(8,128)(2,1)S(1)}, bf16[16,3200]{1,0:T(8,128)(2,1)S(1)}, u32[]{:S(2)}, u32[]{:S(2)}) collective-permute-start(bf16[16,3200]{1,0:T(8,128)(2,1)S(1)} %collective-permute-done.30.refs_6_), channel_id=1, source_target_pairs={{0,4},{1,3},{4,8},{5,1},{8,12},{9,5},{12,14},{13,9},{14,10},{15,13... | collective-permute-start | bytes 307208 | tf_op jit(solution)/shard_map/ppermute | solution.py:378
  64.9 4.7 %collective-permute-start.36 = (bf16[16,3200]{1,0:T(8,128)(2,1)S(1)}, bf16[16,3200]{1,0:T(8,128)(2,1)S(1)}, u32[]{:S(2)}, u32[]{:S(2)}) collective-permute-start(bf16[16,3200]{1,0:T(8,128)(2,1)S(1)} %collective-permute-done.31.refs_7_), channel_id=1, source_target_pairs={{0,4},{1,3},{4,8},{5,1},{8,12},{9,5},{12,14},{13,9},{14,10},{15,13... | collective-permute-start | bytes 307208 | tf_op jit(solution)/shard_map/ppermute | solution.py:378
  78.8 5.4 %collective-permute-start.41 = (bf16[6,16,3200]{2,1,0:T(8,128)(2,1)S(1)}, bf16[6,16,3200]{2,1,0:T(8,128)(2,1)S(1)}, u32[]{:S(2)}, u32[]{:S(2)}) collective-permute-start(bf16[6,16,3200]{2,1,0:T(8,128)(2,1)S(1)} %get-tuple-element.66), channel_id=1, source_target_pairs={{0,1},{1,0},{2,3},{3,2},{4,5},{5,4},{6,7},{7,6},{8,9},{9,8},{10,11... | collective-permute-start | bytes 1843208 | tf_op jit(solution)/shard_map/ppermute | solution.py:369
  79.2 6.0 %collective-permute-start.45 = (bf16[16,3200]{1,0:T(8,128)(2,1)S(1)}, bf16[16,3200]{1,0:T(8,128)(2,1)S(1)}, u32[]{:S(2)}, u32[]{:S(2)}) collective-permute-start(bf16[16,3200]{1,0:T(8,128)(2,1)S(1)} %shard_map.109), channel_id=1, source_target_pairs={{0,4},{1,3},{4,8},{5,1},{8,12},{9,5},{12,14},{13,9},{14,10},{15,13... | collective-permute-start | bytes 307208 | tf_op jit(solution)/shard_map/ppermute | solution.py:378
  82.0 5.2 %collective-permute-start.42 = (bf16[16,3200]{1,0:T(8,128)(2,1)S(1)}, bf16[16,3200]{1,0:T(8,128)(2,1)S(1)}, u32[]{:S(2)}, u32[]{:S(2)}) collective-permute-start(bf16[16,3200]{1,0:T(8,128)(2,1)S(1)} %shard_map.106), channel_id=1, source_target_pairs={{0,4},{1,3},{4,8},{5,1},{8,12},{9,5},{12,14},{13,9},{14,10},{15,13... | collective-permute-start | bytes 307208 | tf_op jit(solution)/shard_map/ppermute | solution.py:378
  84.3 7.6 %collective-permute-start.47 = (bf16[16,3200]{1,0:T(8,128)(2,1)S(1)}, bf16[16,3200]{1,0:T(8,128)(2,1)S(1)}, u32[]{:S(2)}, u32[]{:S(2)}) collective-permute-start(bf16[16,3200]{1,0:T(8,128)(2,1)S(1)} %shard_map.111), channel_id=1, source_target_pairs={{0,14},{1,15},{4,10},{5,11},{8,6},{9,7},{12,2},{13,3},{14,0},{15,1... | collective-permute-start | bytes 307208 | tf_op jit(solution)/shard_map/ppermute | solution.py:378
  85.3 6.6 %collective-permute-start.46 = (bf16[16,3200]{1,0:T(8,128)(2,1)S(1)}, bf16[16,3200]{1,0:T(8,128)(2,1)S(1)}, u32[]{:S(2)}, u32[]{:S(2)}) collective-permute-start(bf16[16,3200]{1,0:T(8,128)(2,1)S(1)} %shard_map.110), channel_id=1, source_target_pairs={{0,4},{1,3},{4,8},{5,1},{8,12},{9,5},{12,14},{13,9},{14,10},{15,13... | collective-permute-start | bytes 307208 | tf_op jit(solution)/shard_map/ppermute | solution.py:378
  87.3 6.1 %collective-permute-start.43 = (bf16[16,3200]{1,0:T(8,128)(2,1)S(1)}, bf16[16,3200]{1,0:T(8,128)(2,1)S(1)}, u32[]{:S(2)}, u32[]{:S(2)}) collective-permute-start(bf16[16,3200]{1,0:T(8,128)(2,1)S(1)} %shard_map.107), channel_id=1, source_target_pairs={{0,4},{1,3},{4,8},{5,1},{8,12},{9,5},{12,14},{13,9},{14,10},{15,13... | collective-permute-start | bytes 307208 | tf_op jit(solution)/shard_map/ppermute | solution.py:378
  92.0 4.7 %collective-permute-start.48 = (bf16[16,3200]{1,0:T(8,128)(2,1)S(1)}, bf16[16,3200]{1,0:T(8,128)(2,1)S(1)}, u32[]{:S(2)}, u32[]{:S(2)}) collective-permute-start(bf16[16,3200]{1,0:T(8,128)(2,1)S(1)} %shard_map.112), channel_id=1, source_target_pairs={{0,4},{1,3},{4,8},{5,1},{8,12},{9,5},{12,14},{13,9},{14,10},{15,13... | collective-permute-start | bytes 307208 | tf_op jit(solution)/shard_map/ppermute | solution.py:378
  93.5 4.7 %collective-permute-start.44 = (bf16[16,3200]{1,0:T(8,128)(2,1)S(1)}, bf16[16,3200]{1,0:T(8,128)(2,1)S(1)}, u32[]{:S(2)}, u32[]{:S(2)}) collective-permute-start(bf16[16,3200]{1,0:T(8,128)(2,1)S(1)} %shard_map.108), channel_id=1, source_target_pairs={{0,4},{1,3},{4,8},{5,1},{8,12},{9,5},{12,14},{13,9},{14,10},{15,13... | collective-permute-start | bytes 307208 | tf_op jit(solution)/shard_map/ppermute | solution.py:378
  (22 other events, 69.8 us)

commit v11 on v10

--- a/solution.py
+++ b/solution.py
@@ -75,11 +75,12 @@
 
 def gathered_devices(me):
     core = me % 2
-    devices = [ahead(me, 0, core), ahead(me, 0, 1 - core)]
-    for k in range(1, ROUNDS + 1):
-        devices += [ahead(me, -k, core), ahead(me, -k, 1 - core)]
-        devices += [ahead(me, k, 1 - core), ahead(me, k, core)]
-    return devices + [ahead(me, 4, core), ahead(me, 4, 1 - core)]
+    devices = []
+    for sign, mine in ((-1, core), (1, 1 - core)):
+        devices += [ahead(me, 0, mine), ahead(me, sign, mine)]
+        for d in (1, 2, 3):
+            devices += [ahead(me, sign * (d + 1), mine), ahead(me, sign * d, 1 - mine)]
+    return devices
 
 
 def message_parts(sectors, rows, width):
@@ -92,41 +93,94 @@
     return (HALF, rows // HALF * sectors * width + LANES)
 
 
-def copy_kernel(in_ref, out_ref):
-    out_ref[...] = in_ref[...]
-
-
-def copied(value):
-    return pl.pallas_call(
-        copy_kernel,
+def message_kernel(wave_ref, all_ref, *out_refs):
+    sectors, rows, width = wave_ref.shape
+    for s in range(sectors):
+        for row, part in halves(rows, width):
+            value = wave_ref[s, row : row + HALF, :]
+            all_ref[s, :, part] = value
+            out_refs[s][0, :, part] = value
+
+
+def as_messages(wave):
+    sectors, rows, width = wave.shape
+    shape = (HALF, rows // HALF * width)
+    return pl.pallas_call(
+        message_kernel,
         in_specs=[VMEM],
+        out_specs=[VMEM] * (1 + sectors),
+        out_shape=[jax.ShapeDtypeStruct((sectors, *shape), wave.dtype)]
+        + [jax.ShapeDtypeStruct((1, *shape), wave.dtype)] * sectors,
+        compiler_params=PARAMS,
+    )(wave)
+
+
+def pair_kernel(s, one_ref, two_ref, out_ref):
+    out_ref[0] = one_ref[0]
+    out_ref[1] = two_ref[s, :, : one_ref.shape[2]]
+
+
+def pair(s, one, two):
+    return pl.pallas_call(
+        functools.partial(pair_kernel, s),
+        in_specs=[VMEM, VMEM],
         out_specs=VMEM,
-        out_shape=jax.ShapeDtypeStruct(value.shape, value.dtype),
-        compiler_params=PARAMS,
-    )(value)
-
-
-def square_kernel(wave_ref, diag_ref, square_ref):
+        out_shape=jax.ShapeDtypeStruct((2, *one.shape[1:]), one.dtype),
+        compiler_params=PARAMS,
+    )(one, two)
+
+
+def pack_kernel(*refs):
+    *in_refs, out_ref = refs
+    at = 0
+    for ref in in_refs:
+        for k in range(ref.shape[0]):
+            out_ref[at, :, : ref.shape[2]] = ref[k]
+            at += 1
+
+
+def pack(*messages):
+    lanes = max(m.shape[2] for m in messages)
+    count = sum(m.shape[0] for m in messages)
+    return pl.pallas_call(
+        pack_kernel,
+        in_specs=[VMEM] * len(messages),
+        out_specs=VMEM,
+        out_shape=jax.ShapeDtypeStruct((count, HALF, lanes), messages[0].dtype),
+        compiler_params=PARAMS,
+    )(*messages)
+
+
+def square_kernel(diag_ref, wave_ref, square_ref):
     square = jnp.zeros((8, 128), jnp.float32)
     for s in range(wave_ref.shape[0]):
-        wave = wave_ref[s].astype(jnp.float32)
-        square += fold(diag_ref[s].astype(jnp.float32) * wave * wave)
+        for row, part in halves(diag_ref.shape[1], diag_ref.shape[2]):
+            wave = wave_ref[s, :, part].astype(jnp.float32)
+            square += fold(diag_ref[s, row : row + HALF, :].astype(jnp.float32) * wave * wave)
     square_ref[...] = square
 
 
-def weighted_square(wave, diag):
+def weighted_square(diag, wave):
     return pl.pallas_call(
         square_kernel,
         in_specs=[VMEM, VMEM],
         out_specs=VMEM,
         out_shape=jax.ShapeDtypeStruct((8, 128), jnp.float32),
         compiler_params=PARAMS,
-    )(wave, diag)
+    )(diag, wave)
 
 
 def blocks_kernel(first, shape, entries, me_ref, ints_ref, *refs):
     sectors, rows, width = shape
-    field_refs, refs = refs[:16], refs[16:]
+    views = []
+    (partner_ref, theirs_ref), refs = refs[:2], refs[2:]
+    for s in range(sectors):
+        mine, refs = refs[:5], refs[5:]
+        views.append(
+            [ref.at[k] for ref in mine for k in range(ref.shape[0])]
+            + [partner_ref.at[s]]
+            + [theirs_ref.at[s * 7 + k] for k in range(7)]
+        )
     if first:
         square_ref, *refs = refs
     else:
@@ -151,27 +205,24 @@
     pieces = []
     for k, owner in enumerate(gathered_devices(me)):
         at = pl.multiple_of(owner * rows, rows)
-        if first:
-            for s in range(sectors):
-                pieces.append((k, (s,), s, pl.ds(at, rows)))
-        else:
-            for s, row, part in message_parts(sectors, rows, width):
-                pieces.append((k, (slice(None), part), s, pl.ds(at + row, HALF)))
+        for s in range(sectors):
+            for row, part in halves(rows, width):
+                pieces.append((views[s][k], part, s, pl.ds(at + row, HALF)))
 
     total[...] = jnp.zeros_like(total)
     if first:
         dot = jnp.zeros((8, 128), jnp.float32)
-        for k, part, _, _ in pieces:
-            value = field_refs[k][part].astype(jnp.float32)
+        for ref, part, _, _ in pieces:
+            value = ref[:, part].astype(jnp.float32)
             dot += fold(value * value)
         scale = jnp.sqrt(jnp.sum(dot) / entries)
         inverse = 1.0 / scale
         out_ref[...] = jnp.full(out_ref.shape, scale, jnp.float32)
-        for k, part, s, at in pieces:
-            field[s, at, :] = (field_refs[k][part].astype(jnp.float32) * inverse).astype(jnp.bfloat16)
+        for ref, part, s, at in pieces:
+            field[s, at, :] = (ref[:, part].astype(jnp.float32) * inverse).astype(jnp.bfloat16)
     else:
-        for k, part, s, at in pieces:
-            field[s, at, :] = field_refs[k][part]
+        for ref, part, s, at in pieces:
+            field[s, at, :] = ref[:, part]
 
     used = ints_ref[2 * slots]
 
@@ -204,14 +255,11 @@
 
     dot = jnp.zeros((8, 128), jnp.float32)
     if first:
-        for k, part, s, at in pieces:
-            dot += fold(total[s, at, :] * field_refs[k][part].astype(jnp.float32))
+        for ref, part, s, at in pieces:
+            dot += fold(total[s, at, :] * ref[:, part].astype(jnp.float32))
         dot = dot * inverse + square_ref[...] * inverse * inverse
     else:
-        at = message_shape(*shape)[1] - LANES
-        lanes = sum(
-            ref[:, at : at + LANES].astype(jnp.float32) for ref in field_refs
-        )
+        lanes = sum(read_lanes(view, rows // HALF * width) for view in views[sectors - 1])
         along = jnp.sum(lanes) / entries
         out_ref[...] = jnp.full(out_ref.shape, along, jnp.float32)
         inverse = 1.0 / scale_ref[0:1, 0:1]
@@ -307,8 +355,10 @@
 
 
 def step_kernel(entries, scale_ref, wave_ref, diag_ref, *refs):
-    *sums, first_ref, terms_ref, correction_ref, message_ref = refs
     shape = wave_ref.shape
+    sectors, rows, width = shape
+    *sums, first_ref, terms_ref, correction_ref, all_ref = refs[:-sectors]
+    message_refs = refs[-sectors:]
     ritz = own_scalar(*sums) / entries
     inverse = 1.0 / scale_ref[0:1, 0:1]
     dots = jnp.zeros((8, 128), jnp.float32)
@@ -322,19 +372,25 @@
         terms_ref[s] = terms
         correction_ref[s] = correction
         dots += fold(start * correction)
-        for t, row, part in message_parts(*shape):
-            if t == s:
-                message_ref[:, part] = correction[row : row + HALF].astype(jnp.bfloat16)
-    write_lanes(message_ref, message_ref.shape[1] - LANES, down(dots))
+        for row, part in halves(rows, width):
+            value = correction[row : row + HALF].astype(jnp.bfloat16)
+            all_ref[s, :, part] = value
+            message_refs[s][0, :, part] = value
+    for ref in (all_ref.at[sectors - 1], message_refs[-1].at[0]):
+        write_lanes(ref, rows // HALF * width, down(dots))
 
 
 def davidson_step(scale, wave, diag, sums, entries):
     full = jax.ShapeDtypeStruct(wave.shape, jnp.float32)
+    sectors, rows, width = wave.shape
+    data = rows // HALF * width
+    shapes = [(sectors, HALF, data + LANES)] + [(1, HALF, data)] * (sectors - 1)
+    shapes.append((1, HALF, data + LANES))
     return pl.pallas_call(
         functools.partial(step_kernel, entries),
         in_specs=[VMEM] * 3 + [SMEM] + [VMEM] * (len(sums) - 1),
-        out_specs=[VMEM] * 4,
-        out_shape=[full, full, full, jax.ShapeDtypeStruct(message_shape(*wave.shape), jnp.bfloat16)],
+        out_specs=[VMEM] * (4 + sectors),
+        out_shape=[full] * 3 + [jax.ShapeDtypeStruct(s, jnp.bfloat16) for s in shapes],
         compiler_params=PARAMS,
     )(scale, wave, diag, *sums)
 
@@ -382,26 +438,24 @@
     return hop(value, 4, 4)
 
 
-def gather(own, beside=()):
-    one, two = own, flip(own)
-    across, two = lax.optimization_barrier((own, two))
-    pieces = [one, two]
-    across = opposite(across)
+def gather(own, messages, beside=()):
+    sectors = len(messages)
+    partner = flip(own)
+    arrived = [hop(m) for m in messages]
+    rounds = [arrived]
     results = []
-    for k in range(ROUNDS):
-        one, two = hop(one), hop(two)
+    for k in range(3):
         if k < len(beside):
-            results.append(beside[k](*results))
-        if k < ROUNDS - 1:
-            ready = results[-1:] if beside else []
-            if k == 1:
-                two, across, ready = lax.optimization_barrier((two, across, ready))
-            else:
-                two, ready = lax.optimization_barrier((two, ready))
-            if ready:
-                results[-1] = ready[0]
-        pieces += [one, two, flip(one), flip(two)]
-    return pieces + [across, flip(across)], results
+            result = beside[k](*results)
+            arrived[-1], result = lax.optimization_barrier((arrived[-1], result))
+            results.append(result)
+        if k == 0:
+            arrived = [pair(s, m, partner) for s, m in enumerate(arrived)]
+        arrived = [hop(m) for m in arrived]
+        rounds.append(arrived)
+    theirs = flip(pack(*(r[s] for s in range(sectors) for r in rounds)))
+    mine = [m for s in range(sectors) for m in (messages[s], *(r[s] for r in rounds))]
+    return [partner, theirs, *mine], results
 
 
 def scatter(shape, me, total, near, far, dot):
@@ -428,18 +482,17 @@
     me = lax.axis_index("term").astype(jnp.int32).reshape(1)
     blocks = (left_blocks, right_blocks, shape)
 
+    own, *messages = as_messages(wavefunction)
     beside = (
         lambda: jnp.concatenate([block_source, block_target, live_count]),
-        lambda _: copied(wavefunction),
-        lambda _, own: weighted_square(own, diagonal),
-    )
-    (_, *fields), (ints, own, square) = gather(wavefunction, beside)
-    fields = [own, *fields]
+        lambda _: weighted_square(diagonal, own),
+    )
+    fields, (ints, square) = gather(own, messages, beside)
     total, near, far, dot, scale = apply_blocks(me, ints, fields, (square,), *blocks, True, entries)
-    first_image, terms, correction, message = davidson_step(
+    first_image, terms, correction, *messages = davidson_step(
         scale, wavefunction, diagonal, scatter(shape, me, total, near, far, dot), entries
     )
-    fields, _ = gather(message)
+    fields, _ = gather(messages[0], messages[1:])
     own = (scale, wavefunction, correction)
     total, near, far, dot, along = apply_blocks(me, ints, fields, own, *blocks, False, entries)
     second_vector, second_image = finish(

time: 99.3 us -> 106 us (1.067)
  waiting for transfers between devices: 21.2 us -> 35.9 us
  starting transfers between devices: 60 us -> 47 us
  Pallas kernels: 13.8 us -> 18.6 us
    ppermute x28 -> x38, waiting for transfers between devices: 17.4 us -> 28.2 us  [hop(): return lax.ppermute(value, 'term', pairs)]
    ppermute x22 -> x10, starting transfers between devices: 7.59 us -> 0.72 us  [flip(): return lax.ppermute(value, 'term', [(i, i ^ 1) for i in range(16)])]
    ppermute x28 -> x38, starting transfers between devices: 52.4 us -> 46.3 us  [hop(): return lax.ppermute(value, 'term', pairs)]
    pallas_call x2, Pallas kernels: 11.3 us -> 15.9 us  [apply_blocks(): pl.pallas_call(functools.partial(blocks_kernel, first, shape, entries), i...]
    ppermute x22 -> x10, waiting for transfers between devices: 3.81 us -> 7.69 us  [flip(): return lax.ppermute(value, 'term', [(i, i ^ 1) for i in range(16)])]
  transfers between devices with their start and end apart: 50 -> 48, of which waited for: 19 -> 30; matrix products, arithmetic and copies ran while one was open for 1% -> 1% of each run, Pallas kernels for 1% -> 1%
where the time goes in v11:
time: 106 us
  starting transfers between devices  47 us (44%)
  waiting for transfers between devices  35.9 us (34%)
  Pallas kernels  18.6 us (18%)
  local copies, waits for them, and re-layouts  1.79 us (2%)
  between operations  1.54 us (1%)
    ppermute x38, starting transfers between devices, hop(): return lax.ppermute(value, 'term', pairs)  46.3 us
    ppermute x38, waiting for transfers between devices, hop(): return lax.ppermute(value, 'term', pairs)  28.2 us
    pallas_call x2, Pallas kernels, apply_blocks(): pl.pallas_call(functools.partial(blocks_kernel, first, shape, entries), i...  15.9 us
    ppermute x10, waiting for transfers between devices, flip(): return lax.ppermute(value, 'term', [(i, i ^ 1) for i in range(16)])  7.69 us
  transfers between devices with their start and end apart: 48, of which 30 were waited for; matrix products, arithmetic and copies ran while one was open for 1% of the time, Pallas kernels for 1%

profile of v11, /device:TPU:0, one launch (start us, length us, event | category | flops | bytes accessed | tf_op | source)
XLA Modules:
  0.0 105.6 jit_solution(2574179385989485482)
XLA Ops:
  1.5 3.1 %collective-permute-start = (bf16[1,16,1024]{2,1,0:T(8,128)(2,1)S(1)}, bf16[1,16,1024]{2,1,0:T(8,128)(2,1)S(1)}, u32[]{:S(2)}, u32[]{:S(2)}) collective-permute-start(bf16[1,16,1024]{2,1,0:T(8,128)(2,1)S(1)} %get-tuple-element.38.refs_12_), channel_id=1, source_target_pairs={{0,4},{1,3},{4,8},{5,1},{8,12},{9,5},{12,14},{13,9},{14,10},{15,13... | collective-permute-start | bytes 98312 | tf_op jit(solution)/shard_map/ppermute | solution.py:434
  4.6 1.6 %collective-permute-start.2 = (bf16[1,16,1024]{2,1,0:T(8,128)(2,1)S(1)}, bf16[1,16,1024]{2,1,0:T(8,128)(2,1)S(1)}, u32[]{:S(2)}, u32[]{:S(2)}) collective-permute-start(bf16[1,16,1024]{2,1,0:T(8,128)(2,1)S(1)} %get-tuple-element.41.refs_2_), channel_id=1, source_target_pairs={{0,4},{1,3},{4,8},{5,1},{8,12},{9,5},{12,14},{13,9},{14,10},{15,13... | collective-permute-start | bytes 98312 | tf_op jit(solution)/shard_map/ppermute | solution.py:434
  6.2 1.6 %collective-permute-start.6 = (bf16[1,16,1024]{2,1,0:T(8,128)(2,1)S(1)}, bf16[1,16,1024]{2,1,0:T(8,128)(2,1)S(1)}, u32[]{:S(2)}, u32[]{:S(2)}) collective-permute-start(bf16[1,16,1024]{2,1,0:T(8,128)(2,1)S(1)} %get-tuple-element.42.refs_7_), channel_id=1, source_target_pairs={{0,4},{1,3},{4,8},{5,1},{8,12},{9,5},{12,14},{13,9},{14,10},{15,13... | collective-permute-start | bytes 98312 | tf_op jit(solution)/shard_map/ppermute | solution.py:434
  9.2 1.6 %collective-permute-start.10 = (bf16[2,16,1024]{2,1,0:T(8,128)(2,1)S(1)}, bf16[2,16,1024]{2,1,0:T(8,128)(2,1)S(1)}, u32[]{:S(2)}, u32[]{:S(2)}) collective-permute-start(bf16[2,16,1024]{2,1,0:T(8,128)(2,1)S(1)} %shard_map.97), channel_id=1, source_target_pairs={{0,4},{1,3},{4,8},{5,1},{8,12},{9,5},{12,14},{13,9},{14,10},{15,13... | collective-permute-start | bytes 196616 | tf_op jit(solution)/shard_map/ppermute | solution.py:434
  13.5 1.6 %collective-permute-done.3.refs_1_.refs_4_ = bf16[2,16,1024]{2,1,0:T(8,128)(2,1)S(1)} collective-permute-done((bf16[2,16,1024]{2,1,0:T(8,128)(2,1)S(1)}, bf16[2,16,1024]{2,1,0:T(8,128)(2,1)S(1)}, u32[]{:S(2)}, u32[]{:S(2)}) %collective-permute-start.3) | collective-permute-done | bytes 65568 | tf_op jit(solution)/shard_map/ppermute | solution.py:434
  16.4 1.2 %collective-permute-start.11 = (bf16[2,16,1024]{2,1,0:T(8,128)(2,1)S(1)}, bf16[2,16,1024]{2,1,0:T(8,128)(2,1)S(1)}, u32[]{:S(2)}, u32[]{:S(2)}) collective-permute-start(bf16[2,16,1024]{2,1,0:T(8,128)(2,1)S(1)} %collective-permute-done.10.refs_9_.refs_14_), channel_id=1, source_target_pairs={{0,4},{1,3},{4,8},{5,1},{8,12},{9,5},{12,14},{13,9},{14,10},{15,13... | collective-permute-start | bytes 196616 | tf_op jit(solution)/shard_map/ppermute | solution.py:434
  17.7 1.7 %collective-permute-done.4.refs_2_.refs_5_ = bf16[2,16,1024]{2,1,0:T(8,128)(2,1)S(1)} collective-permute-done((bf16[2,16,1024]{2,1,0:T(8,128)(2,1)S(1)}, bf16[2,16,1024]{2,1,0:T(8,128)(2,1)S(1)}, u32[]{:S(2)}, u32[]{:S(2)}) %collective-permute-start.4) | collective-permute-done | bytes 65568 | tf_op jit(solution)/shard_map/ppermute | solution.py:434
  20.8 1.2 %collective-permute-start.12 = (bf16[2,16,1024]{2,1,0:T(8,128)(2,1)S(1)}, bf16[2,16,1024]{2,1,0:T(8,128)(2,1)S(1)}, u32[]{:S(2)}, u32[]{:S(2)}) collective-permute-start(bf16[2,16,1024]{2,1,0:T(8,128)(2,1)S(1)} %collective-permute-done.11.refs_10_.refs_15_), channel_id=1, source_target_pairs={{0,4},{1,3},{4,8},{5,1},{8,12},{9,5},{12,14},{13,9},{14,10},{15,13... | collective-permute-start | bytes 196616 | tf_op jit(solution)/shard_map/ppermute | solution.py:434
  21.9 1.7 %collective-permute-done.5.refs_3_.refs_6_ = bf16[2,16,1024]{2,1,0:T(8,128)(2,1)S(1)} collective-permute-done((bf16[2,16,1024]{2,1,0:T(8,128)(2,1)S(1)}, bf16[2,16,1024]{2,1,0:T(8,128)(2,1)S(1)}, u32[]{:S(2)}, u32[]{:S(2)}) %collective-permute-start.5) | collective-permute-done | bytes 65568 | tf_op jit(solution)/shard_map/ppermute | solution.py:434
  25.2 2.1 %collective-permute-done.13.refs_1_ = bf16[21,16,1024]{2,1,0:T(8,128)(2,1)S(1)} collective-permute-done((bf16[21,16,1024]{2,1,0:T(8,128)(2,1)S(1)}, bf16[21,16,1024]{2,1,0:T(8,128)(2,1)S(1)}, u32[]{:S(2)}, u32[]{:S(2)}) %collective-permute-start.13) | collective-permute-done | bytes 688160 | tf_op jit(solution)/shard_map/ppermute | solution.py:425
  27.3 8.0 %shard_map.100 = (f32[3,512,512]{2,1,0:T(8,128)S(1)}, bf16[2,16,3200]{2,1,0:T(8,128)(2,1)S(1)}, bf16[6,16,3200]{2,1,0:T(8,128)(2,1)S(1)}, f32[8,128]{1,0:T(8,128)S(1)}, f32[8,128]{1,0:T(8,128)S(1)}) custom-call(s32[1]{0:T(128)} %bitcast.me_ref.refs_0_.refs_2_, s32[17]{0:T(128)S(1)} %pad_add_fusion.ints_ref, ...), custom_call_target="tpu_custom_call" | custom-call | flops 4294967296 | bytes 8388608 | tf_op jit(solution)/shard_map/pallas_call | solution.py:283
  35.4 1.4 %collective-permute-done.14.other_ref = bf16[2,16,3200]{2,1,0:T(8,128)(2,1)S(1)} collective-permute-done((bf16[2,16,3200]{2,1,0:T(8,128)(2,1)S(1)}, bf16[2,16,3200]{2,1,0:T(8,128)(2,1)S(1)}, u32[]{:S(2)}, u32[]{:S(2)}) %collective-permute-start.14) | collective-permute-done | bytes 204832 | tf_op jit(solution)/shard_map/ppermute | solution.py:425
  37.0 1.2 %collective-permute-start.19 = (bf16[16,3200]{1,0:T(8,128)(2,1)S(1)}, bf16[16,3200]{1,0:T(8,128)(2,1)S(1)}, u32[]{:S(2)}, u32[]{:S(2)}) collective-permute-start(bf16[16,3200]{1,0:T(8,128)(2,1)S(1)} %shard_map.104), channel_id=1, source_target_pairs={{0,4},{1,3},{4,8},{5,1},{8,12},{9,5},{12,14},{13,9},{14,10},{15,13... | collective-permute-start | bytes 307208 | tf_op jit(solution)/shard_map/ppermute | solution.py:434
  39.1 3.3 %collective-permute-start.21 = (bf16[16,3200]{1,0:T(8,128)(2,1)S(1)}, bf16[16,3200]{1,0:T(8,128)(2,1)S(1)}, u32[]{:S(2)}, u32[]{:S(2)}) collective-permute-start(bf16[16,3200]{1,0:T(8,128)(2,1)S(1)} %shard_map.106), channel_id=1, source_target_pairs={{0,14},{1,15},{4,10},{5,11},{8,6},{9,7},{12,2},{13,3},{14,0},{15,1... | collective-permute-start | bytes 307208 | tf_op jit(solution)/shard_map/ppermute | solution.py:434
  43.1 1.2 %collective-permute-start.17 = (bf16[16,3200]{1,0:T(8,128)(2,1)S(1)}, bf16[16,3200]{1,0:T(8,128)(2,1)S(1)}, u32[]{:S(2)}, u32[]{:S(2)}) collective-permute-start(bf16[16,3200]{1,0:T(8,128)(2,1)S(1)} %shard_map.102), channel_id=1, source_target_pairs={{0,4},{1,3},{4,8},{5,1},{8,12},{9,5},{12,14},{13,9},{14,10},{15,13... | collective-permute-start | bytes 307208 | tf_op jit(solution)/shard_map/ppermute | solution.py:434
  44.3 3.2 %collective-permute-done.21.refs_6_ = bf16[16,3200]{1,0:T(8,128)(2,1)S(1)} collective-permute-done((bf16[16,3200]{1,0:T(8,128)(2,1)S(1)}, bf16[16,3200]{1,0:T(8,128)(2,1)S(1)}, u32[]{:S(2)}, u32[]{:S(2)}) %collective-permute-start.21) | collective-permute-done | bytes 102432 | tf_op jit(solution)/shard_map/ppermute | solution.py:434
  50.4 2.9 %collective-permute-done.22 = bf16[16,3200]{1,0:T(8,128)(2,1)S(1)} collective-permute-done((bf16[16,3200]{1,0:T(8,128)(2,1)S(1)}, bf16[16,3200]{1,0:T(8,128)(2,1)S(1)}, u32[]{:S(2)}, u32[]{:S(2)}) %collective-permute-start.22) | collective-permute-done | bytes 102432 | tf_op jit(solution)/shard_map/ppermute | solution.py:434
  53.3 1.1 %collective-permute-done.18.refs_4_ = bf16[16,3200]{1,0:T(8,128)(2,1)S(1)} collective-permute-done((bf16[16,3200]{1,0:T(8,128)(2,1)S(1)}, bf16[16,3200]{1,0:T(8,128)(2,1)S(1)}, u32[]{:S(2)}, u32[]{:S(2)}) %collective-permute-start.18) | collective-permute-done | bytes 102432 | tf_op jit(solution)/shard_map/ppermute | solution.py:434
  57.9 1.7 %collective-permute-done.33.one_ref.refs_8_.refs_13_ = bf16[1,16,1152]{2,1,0:T(8,128)(2,1)S(1)} collective-permute-done((bf16[1,16,1152]{2,1,0:T(8,128)(2,1)S(1)}, bf16[1,16,1152]{2,1,0:T(8,128)(2,1)S(1)}, u32[]{:S(2)}, u32[]{:S(2)}) %collective-permute-start.33) | collective-permute-done | bytes 36896 | tf_op jit(solution)/shard_map/ppermute | solution.py:434
  61.4 2.2 %collective-permute-start.30 = (bf16[2,16,1024]{2,1,0:T(8,128)(2,1)S(1)}, bf16[2,16,1024]{2,1,0:T(8,128)(2,1)S(1)}, u32[]{:S(2)}, u32[]{:S(2)}) collective-permute-start(bf16[2,16,1024]{2,1,0:T(8,128)(2,1)S(1)} %shard_map.110), channel_id=1, source_target_pairs={{0,4},{1,3},{4,8},{5,1},{8,12},{9,5},{12,14},{13,9},{14,10},{15,13... | collective-permute-start | bytes 196616 | tf_op jit(solution)/shard_map/ppermute | solution.py:434
  65.7 2.1 %collective-permute-start.31 = (bf16[2,16,1024]{2,1,0:T(8,128)(2,1)S(1)}, bf16[2,16,1024]{2,1,0:T(8,128)(2,1)S(1)}, u32[]{:S(2)}, u32[]{:S(2)}) collective-permute-start(bf16[2,16,1024]{2,1,0:T(8,128)(2,1)S(1)} %collective-permute-done.30.refs_5_.refs_9_), channel_id=1, source_target_pairs={{0,4},{1,3},{4,8},{5,1},{8,12},{9,5},{12,14},{13,9},{14,10},{15,13... | collective-permute-start | bytes 196616 | tf_op jit(solution)/shard_map/ppermute | solution.py:434
  70.1 2.1 %collective-permute-start.32 = (bf16[2,16,1024]{2,1,0:T(8,128)(2,1)S(1)}, bf16[2,16,1024]{2,1,0:T(8,128)(2,1)S(1)}, u32[]{:S(2)}, u32[]{:S(2)}) collective-permute-start(bf16[2,16,1024]{2,1,0:T(8,128)(2,1)S(1)} %collective-permute-done.31.refs_6_.refs_10_), channel_id=1, source_target_pairs={{0,4},{1,3},{4,8},{5,1},{8,12},{9,5},{12,14},{13,9},{14,10},{15,13... | collective-permute-start | bytes 196616 | tf_op jit(solution)/shard_map/ppermute | solution.py:434
  72.2 1.3 %collective-permute-done.28.refs_3_.refs_6_ = bf16[2,16,1024]{2,1,0:T(8,128)(2,1)S(1)} collective-permute-done((bf16[2,16,1024]{2,1,0:T(8,128)(2,1)S(1)}, bf16[2,16,1024]{2,1,0:T(8,128)(2,1)S(1)}, u32[]{:S(2)}, u32[]{:S(2)}) %collective-permute-start.28) | collective-permute-done | bytes 65568 | tf_op jit(solution)/shard_map/ppermute | solution.py:434
  74.5 2.3 %collective-permute-done.37.refs_1_ = bf16[21,16,1152]{2,1,0:T(8,128)(2,1)S(1)} collective-permute-done((bf16[21,16,1152]{2,1,0:T(8,128)(2,1)S(1)}, bf16[21,16,1152]{2,1,0:T(8,128)(2,1)S(1)}, u32[]{:S(2)}, u32[]{:S(2)}) %collective-permute-start.37) | collective-permute-done | bytes 774176 | tf_op jit(solution)/shard_map/ppermute | solution.py:425
  76.7 7.9 %shard_map.113 = (f32[3,512,512]{2,1,0:T(8,128)S(1)}, bf16[2,16,3200]{2,1,0:T(8,128)(2,1)S(1)}, bf16[6,16,3200]{2,1,0:T(8,128)(2,1)S(1)}, f32[8,128]{1,0:T(8,128)S(1)}, f32[8,128]{1,0:T(8,128)S(1)}) custom-call(s32[1]{0:T(128)} %bitcast.me_ref.refs_0_.refs_2_, s32[17]{0:T(128)S(1)} %pad_add_fusion.ints_ref, ...), custom_call_target="tpu_custom_call" | custom-call | flops 4294967296 | bytes 8388608 | tf_op jit(solution)/shard_map/pallas_call | solution.py:283
  84.7 1.4 %collective-permute-done.38.other_ref = bf16[2,16,3200]{2,1,0:T(8,128)(2,1)S(1)} collective-permute-done((bf16[2,16,3200]{2,1,0:T(8,128)(2,1)S(1)}, bf16[2,16,3200]{2,1,0:T(8,128)(2,1)S(1)}, u32[]{:S(2)}, u32[]{:S(2)}) %collective-permute-start.38) | collective-permute-done | bytes 204832 | tf_op jit(solution)/shard_map/ppermute | solution.py:425
  86.3 2.2 %collective-permute-start.43 = (bf16[16,3200]{1,0:T(8,128)(2,1)S(1)}, bf16[16,3200]{1,0:T(8,128)(2,1)S(1)}, u32[]{:S(2)}, u32[]{:S(2)}) collective-permute-start(bf16[16,3200]{1,0:T(8,128)(2,1)S(1)} %shard_map.117), channel_id=1, source_target_pairs={{0,4},{1,3},{4,8},{5,1},{8,12},{9,5},{12,14},{13,9},{14,10},{15,13... | collective-permute-start | bytes 307208 | tf_op jit(solution)/shard_map/ppermute | solution.py:434
  89.3 3.1 %collective-permute-start.45 = (bf16[16,3200]{1,0:T(8,128)(2,1)S(1)}, bf16[16,3200]{1,0:T(8,128)(2,1)S(1)}, u32[]{:S(2)}, u32[]{:S(2)}) collective-permute-start(bf16[16,3200]{1,0:T(8,128)(2,1)S(1)} %shard_map.119), channel_id=1, source_target_pairs={{0,14},{1,15},{4,10},{5,11},{8,6},{9,7},{12,2},{13,3},{14,0},{15,1... | collective-permute-start | bytes 307208 | tf_op jit(solution)/shard_map/ppermute | solution.py:434
  94.4 3.3 %collective-permute-done.45.refs_8_ = bf16[16,3200]{1,0:T(8,128)(2,1)S(1)} collective-permute-done((bf16[16,3200]{1,0:T(8,128)(2,1)S(1)}, bf16[16,3200]{1,0:T(8,128)(2,1)S(1)}, u32[]{:S(2)}, u32[]{:S(2)}) %collective-permute-start.45) | collective-permute-done | bytes 102432 | tf_op jit(solution)/shard_map/ppermute | solution.py:434
  99.8 1.2 %collective-permute-start.42 = (bf16[16,3200]{1,0:T(8,128)(2,1)S(1)}, bf16[16,3200]{1,0:T(8,128)(2,1)S(1)}, u32[]{:S(2)}, u32[]{:S(2)}) collective-permute-start(bf16[16,3200]{1,0:T(8,128)(2,1)S(1)} %shard_map.116), channel_id=1, source_target_pairs={{0,4},{1,3},{4,8},{5,1},{8,12},{9,5},{12,14},{13,9},{14,10},{15,13... | collective-permute-start | bytes 307208 | tf_op jit(solution)/shard_map/ppermute | solution.py:434
  101.0 2.4 %collective-permute-done.46 = bf16[16,3200]{1,0:T(8,128)(2,1)S(1)} collective-permute-done((bf16[16,3200]{1,0:T(8,128)(2,1)S(1)}, bf16[16,3200]{1,0:T(8,128)(2,1)S(1)}, u32[]{:S(2)}, u32[]{:S(2)}) %collective-permute-start.46) | collective-permute-done | bytes 102432 | tf_op jit(solution)/shard_map/ppermute | solution.py:434
  103.4 1.1 %collective-permute-done.42.refs_6_ = bf16[16,3200]{1,0:T(8,128)(2,1)S(1)} collective-permute-done((bf16[16,3200]{1,0:T(8,128)(2,1)S(1)}, bf16[16,3200]{1,0:T(8,128)(2,1)S(1)}, u32[]{:S(2)}, u32[]{:S(2)}) %collective-permute-start.42) | collective-permute-done | bytes 102432 | tf_op jit(solution)/shard_map/ppermute | solution.py:434
  (101 shorter events, 30.2 us)
Async XLA Ops:
  1.5 7.6 %collective-permute-start = (bf16[1,16,1024]{2,1,0:T(8,128)(2,1)S(1)}, bf16[1,16,1024]{2,1,0:T(8,128)(2,1)S(1)}, u32[]{:S(2)}, u32[]{:S(2)}) collective-permute-start(bf16[1,16,1024]{2,1,0:T(8,128)(2,1)S(1)} %get-tuple-element.38.refs_12_), channel_id=1, source_target_pairs={{0,4},{1,3},{4,8},{5,1},{8,12},{9,5},{12,14},{13,9},{14,10},{15,13... | collective-permute-start | bytes 98312 | tf_op jit(solution)/shard_map/ppermute | solution.py:434
  4.6 6.2 %collective-permute-start.2 = (bf16[1,16,1024]{2,1,0:T(8,128)(2,1)S(1)}, bf16[1,16,1024]{2,1,0:T(8,128)(2,1)S(1)}, u32[]{:S(2)}, u32[]{:S(2)}) collective-permute-start(bf16[1,16,1024]{2,1,0:T(8,128)(2,1)S(1)} %get-tuple-element.41.refs_2_), channel_id=1, source_target_pairs={{0,4},{1,3},{4,8},{5,1},{8,12},{9,5},{12,14},{13,9},{14,10},{15,13... | collective-permute-start | bytes 98312 | tf_op jit(solution)/shard_map/ppermute | solution.py:434
  6.2 5.1 %collective-permute-start.6 = (bf16[1,16,1024]{2,1,0:T(8,128)(2,1)S(1)}, bf16[1,16,1024]{2,1,0:T(8,128)(2,1)S(1)}, u32[]{:S(2)}, u32[]{:S(2)}) collective-permute-start(bf16[1,16,1024]{2,1,0:T(8,128)(2,1)S(1)} %get-tuple-element.42.refs_7_), channel_id=1, source_target_pairs={{0,4},{1,3},{4,8},{5,1},{8,12},{9,5},{12,14},{13,9},{14,10},{15,13... | collective-permute-start | bytes 98312 | tf_op jit(solution)/shard_map/ppermute | solution.py:434
  9.2 4.3 %collective-permute-start.10 = (bf16[2,16,1024]{2,1,0:T(8,128)(2,1)S(1)}, bf16[2,16,1024]{2,1,0:T(8,128)(2,1)S(1)}, u32[]{:S(2)}, u32[]{:S(2)}) collective-permute-start(bf16[2,16,1024]{2,1,0:T(8,128)(2,1)S(1)} %shard_map.97), channel_id=1, source_target_pairs={{0,4},{1,3},{4,8},{5,1},{8,12},{9,5},{12,14},{13,9},{14,10},{15,13... | collective-permute-start | bytes 196616 | tf_op jit(solution)/shard_map/ppermute | solution.py:434
  10.8 4.3 %collective-permute-start.3 = (bf16[2,16,1024]{2,1,0:T(8,128)(2,1)S(1)}, bf16[2,16,1024]{2,1,0:T(8,128)(2,1)S(1)}, u32[]{:S(2)}, u32[]{:S(2)}) collective-permute-start(bf16[2,16,1024]{2,1,0:T(8,128)(2,1)S(1)} %shard_map.95), channel_id=1, source_target_pairs={{0,4},{1,3},{4,8},{5,1},{8,12},{9,5},{12,14},{13,9},{14,10},{15,13... | collective-permute-start | bytes 196616 | tf_op jit(solution)/shard_map/ppermute | solution.py:434
  11.3 4.5 %collective-permute-start.7 = (bf16[2,16,1024]{2,1,0:T(8,128)(2,1)S(1)}, bf16[2,16,1024]{2,1,0:T(8,128)(2,1)S(1)}, u32[]{:S(2)}, u32[]{:S(2)}) collective-permute-start(bf16[2,16,1024]{2,1,0:T(8,128)(2,1)S(1)} %shard_map.96), channel_id=1, source_target_pairs={{0,4},{1,3},{4,8},{5,1},{8,12},{9,5},{12,14},{13,9},{14,10},{15,13... | collective-permute-start | bytes 196616 | tf_op jit(solution)/shard_map/ppermute | solution.py:434
  15.8 4.3 %collective-permute-start.8 = (bf16[2,16,1024]{2,1,0:T(8,128)(2,1)S(1)}, bf16[2,16,1024]{2,1,0:T(8,128)(2,1)S(1)}, u32[]{:S(2)}, u32[]{:S(2)}) collective-permute-start(bf16[2,16,1024]{2,1,0:T(8,128)(2,1)S(1)} %collective-permute-done.7.refs_5_.refs_9_), channel_id=1, source_target_pairs={{0,4},{1,3},{4,8},{5,1},{8,12},{9,5},{12,14},{13,9},{14,10},{15,13... | collective-permute-start | bytes 196616 | tf_op jit(solution)/shard_map/ppermute | solution.py:434
  16.4 4.3 %collective-permute-start.11 = (bf16[2,16,1024]{2,1,0:T(8,128)(2,1)S(1)}, bf16[2,16,1024]{2,1,0:T(8,128)(2,1)S(1)}, u32[]{:S(2)}, u32[]{:S(2)}) collective-permute-start(bf16[2,16,1024]{2,1,0:T(8,128)(2,1)S(1)} %collective-permute-done.10.refs_9_.refs_14_), channel_id=1, source_target_pairs={{0,4},{1,3},{4,8},{5,1},{8,12},{9,5},{12,14},{13,9},{14,10},{15,13... | collective-permute-start | bytes 196616 | tf_op jit(solution)/shard_map/ppermute | solution.py:434
  20.8 4.3 %collective-permute-start.12 = (bf16[2,16,1024]{2,1,0:T(8,128)(2,1)S(1)}, bf16[2,16,1024]{2,1,0:T(8,128)(2,1)S(1)}, u32[]{:S(2)}, u32[]{:S(2)}) collective-permute-start(bf16[2,16,1024]{2,1,0:T(8,128)(2,1)S(1)} %collective-permute-done.11.refs_10_.refs_15_), channel_id=1, source_target_pairs={{0,4},{1,3},{4,8},{5,1},{8,12},{9,5},{12,14},{13,9},{14,10},{15,13... | collective-permute-start | bytes 196616 | tf_op jit(solution)/shard_map/ppermute | solution.py:434
  37.0 5.3 %collective-permute-start.19 = (bf16[16,3200]{1,0:T(8,128)(2,1)S(1)}, bf16[16,3200]{1,0:T(8,128)(2,1)S(1)}, u32[]{:S(2)}, u32[]{:S(2)}) collective-permute-start(bf16[16,3200]{1,0:T(8,128)(2,1)S(1)} %shard_map.104), channel_id=1, source_target_pairs={{0,4},{1,3},{4,8},{5,1},{8,12},{9,5},{12,14},{13,9},{14,10},{15,13... | collective-permute-start | bytes 307208 | tf_op jit(solution)/shard_map/ppermute | solution.py:434
  38.3 4.7 %collective-permute-start.16 = (bf16[16,3200]{1,0:T(8,128)(2,1)S(1)}, bf16[16,3200]{1,0:T(8,128)(2,1)S(1)}, u32[]{:S(2)}, u32[]{:S(2)}) collective-permute-start(bf16[16,3200]{1,0:T(8,128)(2,1)S(1)} %shard_map.101), channel_id=1, source_target_pairs={{0,4},{1,3},{4,8},{5,1},{8,12},{9,5},{12,14},{13,9},{14,10},{15,13... | collective-permute-start | bytes 307208 | tf_op jit(solution)/shard_map/ppermute | solution.py:434
  39.1 8.5 %collective-permute-start.21 = (bf16[16,3200]{1,0:T(8,128)(2,1)S(1)}, bf16[16,3200]{1,0:T(8,128)(2,1)S(1)}, u32[]{:S(2)}, u32[]{:S(2)}) collective-permute-start(bf16[16,3200]{1,0:T(8,128)(2,1)S(1)} %shard_map.106), channel_id=1, source_target_pairs={{0,14},{1,15},{4,10},{5,11},{8,6},{9,7},{12,2},{13,3},{14,0},{15,1... | collective-permute-start | bytes 307208 | tf_op jit(solution)/shard_map/ppermute | solution.py:434
  42.4 6.1 %collective-permute-start.20 = (bf16[16,3200]{1,0:T(8,128)(2,1)S(1)}, bf16[16,3200]{1,0:T(8,128)(2,1)S(1)}, u32[]{:S(2)}, u32[]{:S(2)}) collective-permute-start(bf16[16,3200]{1,0:T(8,128)(2,1)S(1)} %shard_map.105), channel_id=1, source_target_pairs={{0,4},{1,3},{4,8},{5,1},{8,12},{9,5},{12,14},{13,9},{14,10},{15,13... | collective-permute-start | bytes 307208 | tf_op jit(solution)/shard_map/ppermute | solution.py:434
  43.1 6.5 %collective-permute-start.17 = (bf16[16,3200]{1,0:T(8,128)(2,1)S(1)}, bf16[16,3200]{1,0:T(8,128)(2,1)S(1)}, u32[]{:S(2)}, u32[]{:S(2)}) collective-permute-start(bf16[16,3200]{1,0:T(8,128)(2,1)S(1)} %shard_map.102), channel_id=1, source_target_pairs={{0,4},{1,3},{4,8},{5,1},{8,12},{9,5},{12,14},{13,9},{14,10},{15,13... | collective-permute-start | bytes 307208 | tf_op jit(solution)/shard_map/ppermute | solution.py:434
  48.6 4.7 %collective-permute-start.22 = (bf16[16,3200]{1,0:T(8,128)(2,1)S(1)}, bf16[16,3200]{1,0:T(8,128)(2,1)S(1)}, u32[]{:S(2)}, u32[]{:S(2)}) collective-permute-start(bf16[16,3200]{1,0:T(8,128)(2,1)S(1)} %shard_map.107), channel_id=1, source_target_pairs={{0,4},{1,3},{4,8},{5,1},{8,12},{9,5},{12,14},{13,9},{14,10},{15,13... | collective-permute-start | bytes 307208 | tf_op jit(solution)/shard_map/ppermute | solution.py:434
  49.7 4.7 %collective-permute-start.18 = (bf16[16,3200]{1,0:T(8,128)(2,1)S(1)}, bf16[16,3200]{1,0:T(8,128)(2,1)S(1)}, u32[]{:S(2)}, u32[]{:S(2)}) collective-permute-start(bf16[16,3200]{1,0:T(8,128)(2,1)S(1)} %shard_map.103), channel_id=1, source_target_pairs={{0,4},{1,3},{4,8},{5,1},{8,12},{9,5},{12,14},{13,9},{14,10},{15,13... | collective-permute-start | bytes 307208 | tf_op jit(solution)/shard_map/ppermute | solution.py:434
  59.6 4.4 %collective-permute-start.34 = (bf16[2,16,1152]{2,1,0:T(8,128)(2,1)S(1)}, bf16[2,16,1152]{2,1,0:T(8,128)(2,1)S(1)}, u32[]{:S(2)}, u32[]{:S(2)}) collective-permute-start(bf16[2,16,1152]{2,1,0:T(8,128)(2,1)S(1)} %shard_map.111), channel_id=1, source_target_pairs={{0,4},{1,3},{4,8},{5,1},{8,12},{9,5},{12,14},{13,9},{14,10},{15,13... | collective-permute-start | bytes 221192 | tf_op jit(solution)/shard_map/ppermute | solution.py:434
  60.6 4.3 %collective-permute-start.26 = (bf16[2,16,1024]{2,1,0:T(8,128)(2,1)S(1)}, bf16[2,16,1024]{2,1,0:T(8,128)(2,1)S(1)}, u32[]{:S(2)}, u32[]{:S(2)}) collective-permute-start(bf16[2,16,1024]{2,1,0:T(8,128)(2,1)S(1)} %shard_map.109), channel_id=1, source_target_pairs={{0,4},{1,3},{4,8},{5,1},{8,12},{9,5},{12,14},{13,9},{14,10},{15,13... | collective-permute-start | bytes 196616 | tf_op jit(solution)/shard_map/ppermute | solution.py:434
  61.4 4.3 %collective-permute-start.30 = (bf16[2,16,1024]{2,1,0:T(8,128)(2,1)S(1)}, bf16[2,16,1024]{2,1,0:T(8,128)(2,1)S(1)}, u32[]{:S(2)}, u32[]{:S(2)}) collective-permute-start(bf16[2,16,1024]{2,1,0:T(8,128)(2,1)S(1)} %shard_map.110), channel_id=1, source_target_pairs={{0,4},{1,3},{4,8},{5,1},{8,12},{9,5},{12,14},{13,9},{14,10},{15,13... | collective-permute-start | bytes 196616 | tf_op jit(solution)/shard_map/ppermute | solution.py:434
  64.0 4.4 %collective-permute-start.35 = (bf16[2,16,1152]{2,1,0:T(8,128)(2,1)S(1)}, bf16[2,16,1152]{2,1,0:T(8,128)(2,1)S(1)}, u32[]{:S(2)}, u32[]{:S(2)}) collective-permute-start(bf16[2,16,1152]{2,1,0:T(8,128)(2,1)S(1)} %collective-permute-done.34.refs_9_.refs_14_), channel_id=1, source_target_pairs={{0,4},{1,3},{4,8},{5,1},{8,12},{9,5},{12,14},{13,9},{14,10},{15,13... | collective-permute-start | bytes 221192 | tf_op jit(solution)/shard_map/ppermute | solution.py:434
  64.9 4.4 %collective-permute-start.27 = (bf16[2,16,1024]{2,1,0:T(8,128)(2,1)S(1)}, bf16[2,16,1024]{2,1,0:T(8,128)(2,1)S(1)}, u32[]{:S(2)}, u32[]{:S(2)}) collective-permute-start(bf16[2,16,1024]{2,1,0:T(8,128)(2,1)S(1)} %collective-permute-done.26.refs_1_.refs_4_), channel_id=1, source_target_pairs={{0,4},{1,3},{4,8},{5,1},{8,12},{9,5},{12,14},{13,9},{14,10},{15,13... | collective-permute-start | bytes 196616 | tf_op jit(solution)/shard_map/ppermute | solution.py:434
  65.7 4.3 %collective-permute-start.31 = (bf16[2,16,1024]{2,1,0:T(8,128)(2,1)S(1)}, bf16[2,16,1024]{2,1,0:T(8,128)(2,1)S(1)}, u32[]{:S(2)}, u32[]{:S(2)}) collective-permute-start(bf16[2,16,1024]{2,1,0:T(8,128)(2,1)S(1)} %collective-permute-done.30.refs_5_.refs_9_), channel_id=1, source_target_pairs={{0,4},{1,3},{4,8},{5,1},{8,12},{9,5},{12,14},{13,9},{14,10},{15,13... | collective-permute-start | bytes 196616 | tf_op jit(solution)/shard_map/ppermute | solution.py:434
  68.4 6.0 %collective-permute-start.36 = (bf16[2,16,1152]{2,1,0:T(8,128)(2,1)S(1)}, bf16[2,16,1152]{2,1,0:T(8,128)(2,1)S(1)}, u32[]{:S(2)}, u32[]{:S(2)}) collective-permute-start(bf16[2,16,1152]{2,1,0:T(8,128)(2,1)S(1)} %collective-permute-done.35.refs_10_.refs_15_), channel_id=1, source_target_pairs={{0,4},{1,3},{4,8},{5,1},{8,12},{9,5},{12,14},{13,9},{14,10},{15,13... | collective-permute-start | bytes 221192 | tf_op jit(solution)/shard_map/ppermute | solution.py:434
  69.3 4.3 %collective-permute-start.28 = (bf16[2,16,1024]{2,1,0:T(8,128)(2,1)S(1)}, bf16[2,16,1024]{2,1,0:T(8,128)(2,1)S(1)}, u32[]{:S(2)}, u32[]{:S(2)}) collective-permute-start(bf16[2,16,1024]{2,1,0:T(8,128)(2,1)S(1)} %collective-permute-done.27.refs_2_.refs_5_), channel_id=1, source_target_pairs={{0,4},{1,3},{4,8},{5,1},{8,12},{9,5},{12,14},{13,9},{14,10},{15,13... | collective-permute-start | bytes 196616 | tf_op jit(solution)/shard_map/ppermute | solution.py:434
  70.1 4.3 %collective-permute-start.32 = (bf16[2,16,1024]{2,1,0:T(8,128)(2,1)S(1)}, bf16[2,16,1024]{2,1,0:T(8,128)(2,1)S(1)}, u32[]{:S(2)}, u32[]{:S(2)}) collective-permute-start(bf16[2,16,1024]{2,1,0:T(8,128)(2,1)S(1)} %collective-permute-done.31.refs_6_.refs_10_), channel_id=1, source_target_pairs={{0,4},{1,3},{4,8},{5,1},{8,12},{9,5},{12,14},{13,9},{14,10},{15,13... | collective-permute-start | bytes 196616 | tf_op jit(solution)/shard_map/ppermute | solution.py:434
  86.3 6.1 %collective-permute-start.43 = (bf16[16,3200]{1,0:T(8,128)(2,1)S(1)}, bf16[16,3200]{1,0:T(8,128)(2,1)S(1)}, u32[]{:S(2)}, u32[]{:S(2)}) collective-permute-start(bf16[16,3200]{1,0:T(8,128)(2,1)S(1)} %shard_map.117), channel_id=1, source_target_pairs={{0,4},{1,3},{4,8},{5,1},{8,12},{9,5},{12,14},{13,9},{14,10},{15,13... | collective-permute-start | bytes 307208 | tf_op jit(solution)/shard_map/ppermute | solution.py:434
  88.5 4.7 %collective-permute-start.40 = (bf16[16,3200]{1,0:T(8,128)(2,1)S(1)}, bf16[16,3200]{1,0:T(8,128)(2,1)S(1)}, u32[]{:S(2)}, u32[]{:S(2)}) collective-permute-start(bf16[16,3200]{1,0:T(8,128)(2,1)S(1)} %shard_map.114), channel_id=1, source_target_pairs={{0,4},{1,3},{4,8},{5,1},{8,12},{9,5},{12,14},{13,9},{14,10},{15,13... | collective-permute-start | bytes 307208 | tf_op jit(solution)/shard_map/ppermute | solution.py:434
  89.3 8.3 %collective-permute-start.45 = (bf16[16,3200]{1,0:T(8,128)(2,1)S(1)}, bf16[16,3200]{1,0:T(8,128)(2,1)S(1)}, u32[]{:S(2)}, u32[]{:S(2)}) collective-permute-start(bf16[16,3200]{1,0:T(8,128)(2,1)S(1)} %shard_map.119), channel_id=1, source_target_pairs={{0,14},{1,15},{4,10},{5,11},{8,6},{9,7},{12,2},{13,3},{14,0},{15,1... | collective-permute-start | bytes 307208 | tf_op jit(solution)/shard_map/ppermute | solution.py:434
  92.5 6.1 %collective-permute-start.44 = (bf16[16,3200]{1,0:T(8,128)(2,1)S(1)}, bf16[16,3200]{1,0:T(8,128)(2,1)S(1)}, u32[]{:S(2)}, u32[]{:S(2)}) collective-permute-start(bf16[16,3200]{1,0:T(8,128)(2,1)S(1)} %shard_map.118), channel_id=1, source_target_pairs={{0,4},{1,3},{4,8},{5,1},{8,12},{9,5},{12,14},{13,9},{14,10},{15,13... | collective-permute-start | bytes 307208 | tf_op jit(solution)/shard_map/ppermute | solution.py:434
  93.3 6.4 %collective-permute-start.41 = (bf16[16,3200]{1,0:T(8,128)(2,1)S(1)}, bf16[16,3200]{1,0:T(8,128)(2,1)S(1)}, u32[]{:S(2)}, u32[]{:S(2)}) collective-permute-start(bf16[16,3200]{1,0:T(8,128)(2,1)S(1)} %shard_map.115), channel_id=1, source_target_pairs={{0,4},{1,3},{4,8},{5,1},{8,12},{9,5},{12,14},{13,9},{14,10},{15,13... | collective-permute-start | bytes 307208 | tf_op jit(solution)/shard_map/ppermute | solution.py:434
  98.7 4.7 %collective-permute-start.46 = (bf16[16,3200]{1,0:T(8,128)(2,1)S(1)}, bf16[16,3200]{1,0:T(8,128)(2,1)S(1)}, u32[]{:S(2)}, u32[]{:S(2)}) collective-permute-start(bf16[16,3200]{1,0:T(8,128)(2,1)S(1)} %shard_map.120), channel_id=1, source_target_pairs={{0,4},{1,3},{4,8},{5,1},{8,12},{9,5},{12,14},{13,9},{14,10},{15,13... | collective-permute-start | bytes 307208 | tf_op jit(solution)/shard_map/ppermute | solution.py:434
  99.8 4.7 %collective-permute-start.42 = (bf16[16,3200]{1,0:T(8,128)(2,1)S(1)}, bf16[16,3200]{1,0:T(8,128)(2,1)S(1)}, u32[]{:S(2)}, u32[]{:S(2)}) collective-permute-start(bf16[16,3200]{1,0:T(8,128)(2,1)S(1)} %shard_map.116), channel_id=1, source_target_pairs={{0,4},{1,3},{4,8},{5,1},{8,12},{9,5},{12,14},{13,9},{14,10},{15,13... | collective-permute-start | bytes 307208 | tf_op jit(solution)/shard_map/ppermute | solution.py:434
  (20 other events, 70.7 us)

commit v12 on v10

--- a/solution.py
+++ b/solution.py
@@ -79,7 +79,7 @@
     for k in range(1, ROUNDS + 1):
         devices += [ahead(me, -k, core), ahead(me, -k, 1 - core)]
         devices += [ahead(me, k, 1 - core), ahead(me, k, core)]
-    return devices + [ahead(me, 4, core), ahead(me, 4, 1 - core)]
+    return devices + [ahead(me, 4, 1), ahead(me, 4, 0)]
 
 
 def message_parts(sectors, rows, width):
@@ -126,7 +126,7 @@
 
 def blocks_kernel(first, shape, entries, me_ref, ints_ref, *refs):
     sectors, rows, width = shape
-    field_refs, refs = refs[:16], refs[16:]
+    field_refs, refs = refs[:18], refs[18:]
     if first:
         square_ref, *refs = refs
     else:
@@ -147,6 +147,11 @@
 
     me = me_ref[0]
     core = me % 2
+
+    def read(k, part):
+        if k < 14:
+            return field_refs[k][part]
+        return jnp.where(core == 1, field_refs[k][part], field_refs[k + 2][part])
 
     pieces = []
     for k, owner in enumerate(gathered_devices(me)):
@@ -162,16 +167,16 @@
     if first:
         dot = jnp.zeros((8, 128), jnp.float32)
         for k, part, _, _ in pieces:
-            value = field_refs[k][part].astype(jnp.float32)
+            value = read(k, part).astype(jnp.float32)
             dot += fold(value * value)
         scale = jnp.sqrt(jnp.sum(dot) / entries)
         inverse = 1.0 / scale
         out_ref[...] = jnp.full(out_ref.shape, scale, jnp.float32)
         for k, part, s, at in pieces:
-            field[s, at, :] = (field_refs[k][part].astype(jnp.float32) * inverse).astype(jnp.bfloat16)
+            field[s, at, :] = (read(k, part).astype(jnp.float32) * inverse).astype(jnp.bfloat16)
     else:
         for k, part, s, at in pieces:
-            field[s, at, :] = field_refs[k][part]
+            field[s, at, :] = read(k, part)
 
     used = ints_ref[2 * slots]
 
@@ -205,13 +210,12 @@
     dot = jnp.zeros((8, 128), jnp.float32)
     if first:
         for k, part, s, at in pieces:
-            dot += fold(total[s, at, :] * field_refs[k][part].astype(jnp.float32))
+            dot += fold(total[s, at, :] * read(k, part).astype(jnp.float32))
         dot = dot * inverse + square_ref[...] * inverse * inverse
     else:
         at = message_shape(*shape)[1] - LANES
-        lanes = sum(
-            ref[:, at : at + LANES].astype(jnp.float32) for ref in field_refs
-        )
+        part = (slice(None), slice(at, at + LANES))
+        lanes = sum(read(k, part).astype(jnp.float32) for k in range(16))
         along = jnp.sum(lanes) / entries
         out_ref[...] = jnp.full(out_ref.shape, along, jnp.float32)
         inverse = 1.0 / scale_ref[0:1, 0:1]
@@ -382,26 +386,29 @@
     return hop(value, 4, 4)
 
 
+def last_hop(value):
+    order = [0, 2, 4, 6, 7, 5, 3, 1]
+    pairs = []
+    for place in range(8):
+        pairs.append((order[place] * 2, (order[place] ^ 1) * 2))
+        pairs.append((order[place] * 2 + 1, order[(place - 1) % 8] * 2 + 1))
+    return lax.ppermute(value, "term", pairs)
+
+
 def gather(own, beside=()):
     one, two = own, flip(own)
-    across, two = lax.optimization_barrier((own, two))
     pieces = [one, two]
-    across = opposite(across)
     results = []
     for k in range(ROUNDS):
         one, two = hop(one), hop(two)
         if k < len(beside):
-            results.append(beside[k](*results))
-        if k < ROUNDS - 1:
-            ready = results[-1:] if beside else []
-            if k == 1:
-                two, across, ready = lax.optimization_barrier((two, across, ready))
-            else:
-                two, ready = lax.optimization_barrier((two, ready))
-            if ready:
-                results[-1] = ready[0]
+            result = beside[k](*results)
+            if k < ROUNDS - 1:
+                two, result = lax.optimization_barrier((two, result))
+            results.append(result)
         pieces += [one, two, flip(one), flip(two)]
-    return pieces + [across, flip(across)], results
+    one, two = last_hop(one), last_hop(two)
+    return pieces + [one, two, flip(one), flip(two)], results
 
 
 def scatter(shape, me, total, near, far, dot):

time: 99.3 us -> 104 us (1.047)
  waiting for transfers between devices: 21.2 us -> 23.7 us
  starting transfers between devices: 60 us -> 61.9 us
    ppermute x0 -> x4, waiting for transfers between devices: none -> 7.22 us  [last_hop(): return lax.ppermute(value, 'term', pairs)]
    ppermute x28 -> x26, waiting for transfers between devices: 17.4 us -> 12 us  [hop(): return lax.ppermute(value, 'term', pairs)]
    ppermute x22 -> x24, starting transfers between devices: 7.59 us -> 3.2 us  [flip(): return lax.ppermute(value, 'term', [(i, i ^ 1) for i in range(16)])]
    ppermute x28 -> x26, starting transfers between devices: 52.4 us -> 55.6 us  [hop(): return lax.ppermute(value, 'term', pairs)]
    ppermute x0 -> x4, starting transfers between devices: none -> 3.12 us  [last_hop(): return lax.ppermute(value, 'term', pairs)]
    ppermute x22 -> x24, waiting for transfers between devices: 3.81 us -> 4.53 us  [flip(): return lax.ppermute(value, 'term', [(i, i ^ 1) for i in range(16)])]
  transfers between devices with their start and end apart: 50 -> 54, of which waited for: 19 -> 23; matrix products, arithmetic and copies ran while one was open for 1% -> 1% of each run, Pallas kernels for 1% -> 1%
where the time goes in v12:
time: 104 us; the launch traced here: 103 us
  starting transfers between devices  61.9 us (60%)
  waiting for transfers between devices  23.7 us (23%)
  Pallas kernels  13.7 us (13%)
  local copies, waits for them, and re-layouts  1.8 us (2%)
  between operations  1.55 us (1%)
    ppermute x26, starting transfers between devices, hop(): return lax.ppermute(value, 'term', pairs)  55.6 us
    ppermute x26, waiting for transfers between devices, hop(): return lax.ppermute(value, 'term', pairs)  12 us
    pallas_call x2, Pallas kernels, apply_blocks(): pl.pallas_call(functools.partial(blocks_kernel, first, shape, entries), i...  11.1 us
    ppermute x4, waiting for transfers between devices, last_hop(): return lax.ppermute(value, 'term', pairs)  7.22 us
    ppermute x24, waiting for transfers between devices, flip(): return lax.ppermute(value, 'term', [(i, i ^ 1) for i in range(16)])  4.53 us
    ppermute x24, starting transfers between devices, flip(): return lax.ppermute(value, 'term', [(i, i ^ 1) for i in range(16)])  3.2 us
    ppermute x4, starting transfers between devices, last_hop(): return lax.ppermute(value, 'term', pairs)  3.12 us
  transfers between devices with their start and end apart: 54, of which 23 were waited for; matrix products, arithmetic and copies ran while one was open for 1% of the time, Pallas kernels for 1%

profile of v12, /device:TPU:0, one launch (start us, length us, event | category | flops | bytes accessed | tf_op | source)
XLA Modules:
  0.0 103.4 jit_solution(7077191661081721804)
XLA Ops:
  1.1 2.6 %collective-permute-start.3 = (bf16[3,32,512]{2,1,0:T(8,128)(2,1)}, bf16[3,32,512]{2,1,0:T(8,128)(2,1)S(1)}, u32[]{:S(2)}, u32[]{:S(2)}) collective-permute-start(bf16[3,32,512]{2,1,0:T(8,128)(2,1)} %wave_ref.3), channel_id=1, source_target_pairs={{0,4},{1,3},{4,8},{5,1},{8,12},{9,5},{12,14},{13,9},{14,10},{15,13... | collective-permute-start | bytes 294920 | tf_op jit(solution)/shard_map/ppermute | solution.py:382
  4.4 1.6 %collective-permute-start.1 = (bf16[3,32,512]{2,1,0:T(8,128)(2,1)S(1)}, bf16[3,32,512]{2,1,0:T(8,128)(2,1)S(1)}, u32[]{:S(2)}, u32[]{:S(2)}) collective-permute-start(bf16[3,32,512]{2,1,0:T(8,128)(2,1)S(1)} %collective-permute-done.refs_1_), channel_id=1, source_target_pairs={{0,4},{1,3},{4,8},{5,1},{8,12},{9,5},{12,14},{13,9},{14,10},{15,13... | collective-permute-start | bytes 294920 | tf_op jit(solution)/shard_map/ppermute | solution.py:382
  6.8 1.8 %collective-permute-start.6 = (bf16[3,32,512]{2,1,0:T(8,128)(2,1)S(1)}, bf16[3,32,512]{2,1,0:T(8,128)(2,1)S(1)}, u32[]{:S(2)}, u32[]{:S(2)}) collective-permute-start(bf16[3,32,512]{2,1,0:T(8,128)(2,1)S(1)} %collective-permute-done.3.refs_2_), channel_id=1, source_target_pairs={{0,4},{1,3},{4,8},{5,1},{8,12},{9,5},{12,14},{13,9},{14,10},{15,13... | collective-permute-start | bytes 294920 | tf_op jit(solution)/shard_map/ppermute | solution.py:382
  9.1 1.6 %collective-permute-start.2 = (bf16[3,32,512]{2,1,0:T(8,128)(2,1)S(1)}, bf16[3,32,512]{2,1,0:T(8,128)(2,1)S(1)}, u32[]{:S(2)}, u32[]{:S(2)}) collective-permute-start(bf16[3,32,512]{2,1,0:T(8,128)(2,1)S(1)} %collective-permute-done.1.refs_3_), channel_id=1, source_target_pairs={{0,4},{1,3},{4,8},{5,1},{8,12},{9,5},{12,14},{13,9},{14,10},{15,13... | collective-permute-start | bytes 294920 | tf_op jit(solution)/shard_map/ppermute | solution.py:382
  11.6 1.6 %collective-permute-start.9 = (bf16[3,32,512]{2,1,0:T(8,128)(2,1)S(1)}, bf16[3,32,512]{2,1,0:T(8,128)(2,1)S(1)}, u32[]{:S(2)}, u32[]{:S(2)}) collective-permute-start(bf16[3,32,512]{2,1,0:T(8,128)(2,1)S(1)} %collective-permute-done.6.refs_6_), channel_id=1, source_target_pairs={{0,4},{1,3},{4,8},{5,1},{8,12},{9,5},{12,14},{13,9},{14,10},{15,13... | collective-permute-start | bytes 294920 | tf_op jit(solution)/shard_map/ppermute | solution.py:382
  13.7 1.6 %collective-permute-start.10 = (bf16[3,32,512]{2,1,0:T(8,128)(2,1)S(1)}, bf16[3,32,512]{2,1,0:T(8,128)(2,1)S(1)}, u32[]{:S(2)}, u32[]{:S(2)}) collective-permute-start(bf16[3,32,512]{2,1,0:T(8,128)(2,1)S(1)} %collective-permute-done.2.refs_7_), channel_id=1, source_target_pairs={{0,4},{1,3},{4,8},{5,1},{8,12},{9,5},{12,14},{13,9},{14,10},{15,13... | collective-permute-start | bytes 294920 | tf_op jit(solution)/shard_map/ppermute | solution.py:382
  16.3 1.5 %collective-permute-start.13 = (bf16[3,32,512]{2,1,0:T(8,128)(2,1)S(1)}, bf16[3,32,512]{2,1,0:T(8,128)(2,1)S(1)}, u32[]{:S(2)}, u32[]{:S(2)}) collective-permute-start(bf16[3,32,512]{2,1,0:T(8,128)(2,1)S(1)} %collective-permute-done.9.refs_10_), channel_id=1, source_target_pairs={{0,2},{1,3},{4,6},{5,1},{8,10},{9,5},{12,14},{13,9},{14,12},{15,13... | collective-permute-start | bytes 294920 | tf_op jit(solution)/shard_map/ppermute | solution.py:395
  20.9 2.1 %collective-permute-done.14.refs_15_ = bf16[3,32,512]{2,1,0:T(8,128)(2,1)S(1)} collective-permute-done((bf16[3,32,512]{2,1,0:T(8,128)(2,1)S(1)}, bf16[3,32,512]{2,1,0:T(8,128)(2,1)S(1)}, u32[]{:S(2)}, u32[]{:S(2)}) %collective-permute-start.14) | collective-permute-done | bytes 98336 | tf_op jit(solution)/shard_map/ppermute | solution.py:395
  24.3 5.9 %shard_map.96 = (f32[3,512,512]{2,1,0:T(8,128)S(1)}, bf16[2,16,3200]{2,1,0:T(8,128)(2,1)S(1)}, bf16[6,16,3200]{2,1,0:T(8,128)(2,1)S(1)}, f32[8,128]{1,0:T(8,128)S(1)}, f32[8,128]{1,0:T(8,128)S(1)}) custom-call(s32[1]{0:T(128)} %bitcast.me_ref.refs_0_.refs_2_, s32[17]{0:T(128)S(1)} %pad_add_fusion.ints_ref, ...), custom_call_target="tpu_custom_call" | custom-call | flops 4294967296 | bytes 8388608 | tf_op jit(solution)/shard_map/pallas_call | solution.py:239
  30.3 1.4 %collective-permute-done.17.other_ref = bf16[2,16,3200]{2,1,0:T(8,128)(2,1)S(1)} collective-permute-done((bf16[2,16,3200]{2,1,0:T(8,128)(2,1)S(1)}, bf16[2,16,3200]{2,1,0:T(8,128)(2,1)S(1)}, u32[]{:S(2)}, u32[]{:S(2)}) %collective-permute-start.17) | collective-permute-done | bytes 204832 | tf_op jit(solution)/shard_map/ppermute | solution.py:373
  31.9 4.2 %collective-permute-start.22 = (bf16[16,3200]{1,0:T(8,128)(2,1)S(1)}, bf16[16,3200]{1,0:T(8,128)(2,1)S(1)}, u32[]{:S(2)}, u32[]{:S(2)}) collective-permute-start(bf16[16,3200]{1,0:T(8,128)(2,1)S(1)} %shard_map.100), channel_id=1, source_target_pairs={{0,4},{1,3},{4,8},{5,1},{8,12},{9,5},{12,14},{13,9},{14,10},{15,13... | collective-permute-start | bytes 307208 | tf_op jit(solution)/shard_map/ppermute | solution.py:382
  36.1 1.7 %collective-permute-start.19 = (bf16[16,3200]{1,0:T(8,128)(2,1)S(1)}, bf16[16,3200]{1,0:T(8,128)(2,1)S(1)}, u32[]{:S(2)}, u32[]{:S(2)}) collective-permute-start(bf16[16,3200]{1,0:T(8,128)(2,1)S(1)} %shard_map.97), channel_id=1, source_target_pairs={{0,4},{1,3},{4,8},{5,1},{8,12},{9,5},{12,14},{13,9},{14,10},{15,13... | collective-permute-start | bytes 307208 | tf_op jit(solution)/shard_map/ppermute | solution.py:382
  37.9 2.2 %collective-permute-start.24 = (bf16[16,3200]{1,0:T(8,128)(2,1)S(1)}, bf16[16,3200]{1,0:T(8,128)(2,1)S(1)}, u32[]{:S(2)}, u32[]{:S(2)}) collective-permute-start(bf16[16,3200]{1,0:T(8,128)(2,1)S(1)} %shard_map.102), channel_id=1, source_target_pairs={{0,14},{1,15},{4,10},{5,11},{8,6},{9,7},{12,2},{13,3},{14,0},{15,1... | collective-permute-start | bytes 307208 | tf_op jit(solution)/shard_map/ppermute | solution.py:382
  40.9 3.7 %collective-permute-start.20 = (bf16[16,3200]{1,0:T(8,128)(2,1)S(1)}, bf16[16,3200]{1,0:T(8,128)(2,1)S(1)}, u32[]{:S(2)}, u32[]{:S(2)}) collective-permute-start(bf16[16,3200]{1,0:T(8,128)(2,1)S(1)} %shard_map.98), channel_id=1, source_target_pairs={{0,4},{1,3},{4,8},{5,1},{8,12},{9,5},{12,14},{13,9},{14,10},{15,13... | collective-permute-start | bytes 307208 | tf_op jit(solution)/shard_map/ppermute | solution.py:382
  47.4 2.3 %collective-permute-start.21 = (bf16[16,3200]{1,0:T(8,128)(2,1)S(1)}, bf16[16,3200]{1,0:T(8,128)(2,1)S(1)}, u32[]{:S(2)}, u32[]{:S(2)}) collective-permute-start(bf16[16,3200]{1,0:T(8,128)(2,1)S(1)} %shard_map.99), channel_id=1, source_target_pairs={{0,4},{1,3},{4,8},{5,1},{8,12},{9,5},{12,14},{13,9},{14,10},{15,13... | collective-permute-start | bytes 307208 | tf_op jit(solution)/shard_map/ppermute | solution.py:382
  50.8 1.4 %collective-permute-done.21.refs_4_ = bf16[16,3200]{1,0:T(8,128)(2,1)S(1)} collective-permute-done((bf16[16,3200]{1,0:T(8,128)(2,1)S(1)}, bf16[16,3200]{1,0:T(8,128)(2,1)S(1)}, u32[]{:S(2)}, u32[]{:S(2)}) %collective-permute-start.21) | collective-permute-done | bytes 102432 | tf_op jit(solution)/shard_map/ppermute | solution.py:382
  53.1 2.2 %collective-permute-start.28 = (bf16[16,3200]{1,0:T(8,128)(2,1)S(1)}, bf16[16,3200]{1,0:T(8,128)(2,1)S(1)}, u32[]{:S(2)}, u32[]{:S(2)}) collective-permute-start(bf16[16,3200]{1,0:T(8,128)(2,1)S(1)} %get-tuple-element.45.refs_0_), channel_id=1, source_target_pairs={{0,4},{1,3},{4,8},{5,1},{8,12},{9,5},{12,14},{13,9},{14,10},{15,13... | collective-permute-start | bytes 307208 | tf_op jit(solution)/shard_map/ppermute | solution.py:382
  55.3 2.3 %collective-permute-start.29 = (bf16[16,3200]{1,0:T(8,128)(2,1)S(1)}, bf16[16,3200]{1,0:T(8,128)(2,1)S(1)}, u32[]{:S(2)}, u32[]{:S(2)}) collective-permute-start(bf16[16,3200]{1,0:T(8,128)(2,1)S(1)} %collective-permute-done.27.refs_1_), channel_id=1, source_target_pairs={{0,4},{1,3},{4,8},{5,1},{8,12},{9,5},{12,14},{13,9},{14,10},{15,13... | collective-permute-start | bytes 307208 | tf_op jit(solution)/shard_map/ppermute | solution.py:382
  57.8 2.2 %collective-permute-start.32 = (bf16[16,3200]{1,0:T(8,128)(2,1)S(1)}, bf16[16,3200]{1,0:T(8,128)(2,1)S(1)}, u32[]{:S(2)}, u32[]{:S(2)}) collective-permute-start(bf16[16,3200]{1,0:T(8,128)(2,1)S(1)} %collective-permute-done.28.refs_2_), channel_id=1, source_target_pairs={{0,4},{1,3},{4,8},{5,1},{8,12},{9,5},{12,14},{13,9},{14,10},{15,13... | collective-permute-start | bytes 307208 | tf_op jit(solution)/shard_map/ppermute | solution.py:382
  59.9 2.3 %collective-permute-start.33 = (bf16[16,3200]{1,0:T(8,128)(2,1)S(1)}, bf16[16,3200]{1,0:T(8,128)(2,1)S(1)}, u32[]{:S(2)}, u32[]{:S(2)}) collective-permute-start(bf16[16,3200]{1,0:T(8,128)(2,1)S(1)} %collective-permute-done.29.refs_3_), channel_id=1, source_target_pairs={{0,4},{1,3},{4,8},{5,1},{8,12},{9,5},{12,14},{13,9},{14,10},{15,13... | collective-permute-start | bytes 307208 | tf_op jit(solution)/shard_map/ppermute | solution.py:382
  62.4 2.2 %collective-permute-start.36 = (bf16[16,3200]{1,0:T(8,128)(2,1)S(1)}, bf16[16,3200]{1,0:T(8,128)(2,1)S(1)}, u32[]{:S(2)}, u32[]{:S(2)}) collective-permute-start(bf16[16,3200]{1,0:T(8,128)(2,1)S(1)} %collective-permute-done.32.refs_6_), channel_id=1, source_target_pairs={{0,4},{1,3},{4,8},{5,1},{8,12},{9,5},{12,14},{13,9},{14,10},{15,13... | collective-permute-start | bytes 307208 | tf_op jit(solution)/shard_map/ppermute | solution.py:382
  64.6 2.3 %collective-permute-start.37 = (bf16[16,3200]{1,0:T(8,128)(2,1)S(1)}, bf16[16,3200]{1,0:T(8,128)(2,1)S(1)}, u32[]{:S(2)}, u32[]{:S(2)}) collective-permute-start(bf16[16,3200]{1,0:T(8,128)(2,1)S(1)} %collective-permute-done.33.refs_7_), channel_id=1, source_target_pairs={{0,4},{1,3},{4,8},{5,1},{8,12},{9,5},{12,14},{13,9},{14,10},{15,13... | collective-permute-start | bytes 307208 | tf_op jit(solution)/shard_map/ppermute | solution.py:382
  70.0 2.0 %collective-permute-done.40.refs_14_ = bf16[16,3200]{1,0:T(8,128)(2,1)S(1)} collective-permute-done((bf16[16,3200]{1,0:T(8,128)(2,1)S(1)}, bf16[16,3200]{1,0:T(8,128)(2,1)S(1)}, u32[]{:S(2)}, u32[]{:S(2)}) %collective-permute-start.40) | collective-permute-done | bytes 102432 | tf_op jit(solution)/shard_map/ppermute | solution.py:395
  72.1 1.8 %collective-permute-done.41.refs_15_ = bf16[16,3200]{1,0:T(8,128)(2,1)S(1)} collective-permute-done((bf16[16,3200]{1,0:T(8,128)(2,1)S(1)}, bf16[16,3200]{1,0:T(8,128)(2,1)S(1)}, u32[]{:S(2)}, u32[]{:S(2)}) %collective-permute-start.41) | collective-permute-done | bytes 102432 | tf_op jit(solution)/shard_map/ppermute | solution.py:395
  75.2 5.2 %shard_map.105 = (f32[3,512,512]{2,1,0:T(8,128)S(1)}, bf16[2,16,3200]{2,1,0:T(8,128)(2,1)S(1)}, bf16[6,16,3200]{2,1,0:T(8,128)(2,1)S(1)}, f32[8,128]{1,0:T(8,128)S(1)}, f32[8,128]{1,0:T(8,128)S(1)}) custom-call(s32[1]{0:T(128)} %bitcast.me_ref.refs_0_.refs_2_, s32[17]{0:T(128)S(1)} %pad_add_fusion.ints_ref, bf16[16,3200]{1,0:T(8,128)(2,1)S(1)} %get-tuple-element.45.refs_0_, ...), custom_call_target="tpu_custom_call" | custom-call | flops 4294967296 | bytes 8388608 | tf_op jit(solution)/shard_map/pallas_call | solution.py:239
  80.5 1.4 %collective-permute-done.44.other_ref = bf16[2,16,3200]{2,1,0:T(8,128)(2,1)S(1)} collective-permute-done((bf16[2,16,3200]{2,1,0:T(8,128)(2,1)S(1)}, bf16[2,16,3200]{2,1,0:T(8,128)(2,1)S(1)}, u32[]{:S(2)}, u32[]{:S(2)}) %collective-permute-start.44) | collective-permute-done | bytes 204832 | tf_op jit(solution)/shard_map/ppermute | solution.py:373
  82.2 4.9 %collective-permute-start.49 = (bf16[16,3200]{1,0:T(8,128)(2,1)S(1)}, bf16[16,3200]{1,0:T(8,128)(2,1)S(1)}, u32[]{:S(2)}, u32[]{:S(2)}) collective-permute-start(bf16[16,3200]{1,0:T(8,128)(2,1)S(1)} %shard_map.109), channel_id=1, source_target_pairs={{0,4},{1,3},{4,8},{5,1},{8,12},{9,5},{12,14},{13,9},{14,10},{15,13... | collective-permute-start | bytes 307208 | tf_op jit(solution)/shard_map/ppermute | solution.py:382
  89.4 2.5 %collective-permute-start.50 = (bf16[16,3200]{1,0:T(8,128)(2,1)S(1)}, bf16[16,3200]{1,0:T(8,128)(2,1)S(1)}, u32[]{:S(2)}, u32[]{:S(2)}) collective-permute-start(bf16[16,3200]{1,0:T(8,128)(2,1)S(1)} %shard_map.110), channel_id=1, source_target_pairs={{0,4},{1,3},{4,8},{5,1},{8,12},{9,5},{12,14},{13,9},{14,10},{15,13... | collective-permute-start | bytes 307208 | tf_op jit(solution)/shard_map/ppermute | solution.py:382
  93.0 2.1 %collective-permute-start.47 = (bf16[16,3200]{1,0:T(8,128)(2,1)S(1)}, bf16[16,3200]{1,0:T(8,128)(2,1)S(1)}, u32[]{:S(2)}, u32[]{:S(2)}) collective-permute-start(bf16[16,3200]{1,0:T(8,128)(2,1)S(1)} %shard_map.107), channel_id=1, source_target_pairs={{0,4},{1,3},{4,8},{5,1},{8,12},{9,5},{12,14},{13,9},{14,10},{15,13... | collective-permute-start | bytes 307208 | tf_op jit(solution)/shard_map/ppermute | solution.py:382
  96.2 1.5 %collective-permute-start.52 = (bf16[16,3200]{1,0:T(8,128)(2,1)S(1)}, bf16[16,3200]{1,0:T(8,128)(2,1)S(1)}, u32[]{:S(2)}, u32[]{:S(2)}) collective-permute-start(bf16[16,3200]{1,0:T(8,128)(2,1)S(1)} %shard_map.112), channel_id=1, source_target_pairs={{0,4},{1,3},{4,8},{5,1},{8,12},{9,5},{12,14},{13,9},{14,10},{15,13... | collective-permute-start | bytes 307208 | tf_op jit(solution)/shard_map/ppermute | solution.py:382
  97.7 2.2 %collective-permute-start.48 = (bf16[16,3200]{1,0:T(8,128)(2,1)S(1)}, bf16[16,3200]{1,0:T(8,128)(2,1)S(1)}, u32[]{:S(2)}, u32[]{:S(2)}) collective-permute-start(bf16[16,3200]{1,0:T(8,128)(2,1)S(1)} %shard_map.108), channel_id=1, source_target_pairs={{0,4},{1,3},{4,8},{5,1},{8,12},{9,5},{12,14},{13,9},{14,10},{15,13... | collective-permute-start | bytes 307208 | tf_op jit(solution)/shard_map/ppermute | solution.py:382
  100.9 1.6 %collective-permute-done.48.refs_6_ = bf16[16,3200]{1,0:T(8,128)(2,1)S(1)} collective-permute-done((bf16[16,3200]{1,0:T(8,128)(2,1)S(1)}, bf16[16,3200]{1,0:T(8,128)(2,1)S(1)}, u32[]{:S(2)}, u32[]{:S(2)}) %collective-permute-start.48) | collective-permute-done | bytes 102432 | tf_op jit(solution)/shard_map/ppermute | solution.py:382
  (105 shorter events, 25.9 us)
Async XLA Ops:
  1.1 5.7 %collective-permute-start.3 = (bf16[3,32,512]{2,1,0:T(8,128)(2,1)}, bf16[3,32,512]{2,1,0:T(8,128)(2,1)S(1)}, u32[]{:S(2)}, u32[]{:S(2)}) collective-permute-start(bf16[3,32,512]{2,1,0:T(8,128)(2,1)} %wave_ref.3), channel_id=1, source_target_pairs={{0,4},{1,3},{4,8},{5,1},{8,12},{9,5},{12,14},{13,9},{14,10},{15,13... | collective-permute-start | bytes 294920 | tf_op jit(solution)/shard_map/ppermute | solution.py:382
  4.4 4.7 %collective-permute-start.1 = (bf16[3,32,512]{2,1,0:T(8,128)(2,1)S(1)}, bf16[3,32,512]{2,1,0:T(8,128)(2,1)S(1)}, u32[]{:S(2)}, u32[]{:S(2)}) collective-permute-start(bf16[3,32,512]{2,1,0:T(8,128)(2,1)S(1)} %collective-permute-done.refs_1_), channel_id=1, source_target_pairs={{0,4},{1,3},{4,8},{5,1},{8,12},{9,5},{12,14},{13,9},{14,10},{15,13... | collective-permute-start | bytes 294920 | tf_op jit(solution)/shard_map/ppermute | solution.py:382
  6.8 4.8 %collective-permute-start.6 = (bf16[3,32,512]{2,1,0:T(8,128)(2,1)S(1)}, bf16[3,32,512]{2,1,0:T(8,128)(2,1)S(1)}, u32[]{:S(2)}, u32[]{:S(2)}) collective-permute-start(bf16[3,32,512]{2,1,0:T(8,128)(2,1)S(1)} %collective-permute-done.3.refs_2_), channel_id=1, source_target_pairs={{0,4},{1,3},{4,8},{5,1},{8,12},{9,5},{12,14},{13,9},{14,10},{15,13... | collective-permute-start | bytes 294920 | tf_op jit(solution)/shard_map/ppermute | solution.py:382
  9.1 4.6 %collective-permute-start.2 = (bf16[3,32,512]{2,1,0:T(8,128)(2,1)S(1)}, bf16[3,32,512]{2,1,0:T(8,128)(2,1)S(1)}, u32[]{:S(2)}, u32[]{:S(2)}) collective-permute-start(bf16[3,32,512]{2,1,0:T(8,128)(2,1)S(1)} %collective-permute-done.1.refs_3_), channel_id=1, source_target_pairs={{0,4},{1,3},{4,8},{5,1},{8,12},{9,5},{12,14},{13,9},{14,10},{15,13... | collective-permute-start | bytes 294920 | tf_op jit(solution)/shard_map/ppermute | solution.py:382
  11.6 4.7 %collective-permute-start.9 = (bf16[3,32,512]{2,1,0:T(8,128)(2,1)S(1)}, bf16[3,32,512]{2,1,0:T(8,128)(2,1)S(1)}, u32[]{:S(2)}, u32[]{:S(2)}) collective-permute-start(bf16[3,32,512]{2,1,0:T(8,128)(2,1)S(1)} %collective-permute-done.6.refs_6_), channel_id=1, source_target_pairs={{0,4},{1,3},{4,8},{5,1},{8,12},{9,5},{12,14},{13,9},{14,10},{15,13... | collective-permute-start | bytes 294920 | tf_op jit(solution)/shard_map/ppermute | solution.py:382
  13.7 4.6 %collective-permute-start.10 = (bf16[3,32,512]{2,1,0:T(8,128)(2,1)S(1)}, bf16[3,32,512]{2,1,0:T(8,128)(2,1)S(1)}, u32[]{:S(2)}, u32[]{:S(2)}) collective-permute-start(bf16[3,32,512]{2,1,0:T(8,128)(2,1)S(1)} %collective-permute-done.2.refs_7_), channel_id=1, source_target_pairs={{0,4},{1,3},{4,8},{5,1},{8,12},{9,5},{12,14},{13,9},{14,10},{15,13... | collective-permute-start | bytes 294920 | tf_op jit(solution)/shard_map/ppermute | solution.py:382
  19.0 4.9 %collective-permute-start.8 = (bf16[3,32,512]{2,1,0:T(8,128)(2,1)S(1)}, bf16[3,32,512]{2,1,0:T(8,128)(2,1)S(1)}, u32[]{:S(2)}, u32[]{:S(2)}) collective-permute-start(bf16[3,32,512]{2,1,0:T(8,128)(2,1)S(1)} %collective-permute-done.2.refs_7_), channel_id=1, source_target_pairs={{0,1},{1,0},{2,3},{3,2},{4,5},{5,4},{6,7},{7,6},{8,9},{9,8},{10,11... | collective-permute-start | bytes 294920 | tf_op jit(solution)/shard_map/ppermute | solution.py:373
  19.0 4.9 %collective-permute-start.11 = (bf16[3,32,512]{2,1,0:T(8,128)(2,1)S(1)}, bf16[3,32,512]{2,1,0:T(8,128)(2,1)S(1)}, u32[]{:S(2)}, u32[]{:S(2)}) collective-permute-start(bf16[3,32,512]{2,1,0:T(8,128)(2,1)S(1)} %collective-permute-done.9.refs_10_), channel_id=1, source_target_pairs={{0,1},{1,0},{2,3},{3,2},{4,5},{5,4},{6,7},{7,6},{8,9},{9,8},{10,11... | collective-permute-start | bytes 294920 | tf_op jit(solution)/shard_map/ppermute | solution.py:373
  31.7 6.1 %collective-permute-start.18 = (bf16[6,16,3200]{2,1,0:T(8,128)(2,1)S(1)}, bf16[6,16,3200]{2,1,0:T(8,128)(2,1)S(1)}, u32[]{:S(2)}, u32[]{:S(2)}) collective-permute-start(bf16[6,16,3200]{2,1,0:T(8,128)(2,1)S(1)} %get-tuple-element.39), channel_id=1, source_target_pairs={{0,1},{1,0},{2,3},{3,2},{4,5},{5,4},{6,7},{7,6},{8,9},{9,8},{10,11... | collective-permute-start | bytes 1843208 | tf_op jit(solution)/shard_map/ppermute | solution.py:373
  31.9 8.2 %collective-permute-start.22 = (bf16[16,3200]{1,0:T(8,128)(2,1)S(1)}, bf16[16,3200]{1,0:T(8,128)(2,1)S(1)}, u32[]{:S(2)}, u32[]{:S(2)}) collective-permute-start(bf16[16,3200]{1,0:T(8,128)(2,1)S(1)} %shard_map.100), channel_id=1, source_target_pairs={{0,4},{1,3},{4,8},{5,1},{8,12},{9,5},{12,14},{13,9},{14,10},{15,13... | collective-permute-start | bytes 307208 | tf_op jit(solution)/shard_map/ppermute | solution.py:382
  36.1 4.7 %collective-permute-start.19 = (bf16[16,3200]{1,0:T(8,128)(2,1)S(1)}, bf16[16,3200]{1,0:T(8,128)(2,1)S(1)}, u32[]{:S(2)}, u32[]{:S(2)}) collective-permute-start(bf16[16,3200]{1,0:T(8,128)(2,1)S(1)} %shard_map.97), channel_id=1, source_target_pairs={{0,4},{1,3},{4,8},{5,1},{8,12},{9,5},{12,14},{13,9},{14,10},{15,13... | collective-permute-start | bytes 307208 | tf_op jit(solution)/shard_map/ppermute | solution.py:382
  37.9 7.6 %collective-permute-start.24 = (bf16[16,3200]{1,0:T(8,128)(2,1)S(1)}, bf16[16,3200]{1,0:T(8,128)(2,1)S(1)}, u32[]{:S(2)}, u32[]{:S(2)}) collective-permute-start(bf16[16,3200]{1,0:T(8,128)(2,1)S(1)} %shard_map.102), channel_id=1, source_target_pairs={{0,14},{1,15},{4,10},{5,11},{8,6},{9,7},{12,2},{13,3},{14,0},{15,1... | collective-permute-start | bytes 307208 | tf_op jit(solution)/shard_map/ppermute | solution.py:382
  40.2 5.8 %collective-permute-start.23 = (bf16[16,3200]{1,0:T(8,128)(2,1)S(1)}, bf16[16,3200]{1,0:T(8,128)(2,1)S(1)}, u32[]{:S(2)}, u32[]{:S(2)}) collective-permute-start(bf16[16,3200]{1,0:T(8,128)(2,1)S(1)} %shard_map.101), channel_id=1, source_target_pairs={{0,4},{1,3},{4,8},{5,1},{8,12},{9,5},{12,14},{13,9},{14,10},{15,13... | collective-permute-start | bytes 307208 | tf_op jit(solution)/shard_map/ppermute | solution.py:382
  40.9 6.4 %collective-permute-start.20 = (bf16[16,3200]{1,0:T(8,128)(2,1)S(1)}, bf16[16,3200]{1,0:T(8,128)(2,1)S(1)}, u32[]{:S(2)}, u32[]{:S(2)}) collective-permute-start(bf16[16,3200]{1,0:T(8,128)(2,1)S(1)} %shard_map.98), channel_id=1, source_target_pairs={{0,4},{1,3},{4,8},{5,1},{8,12},{9,5},{12,14},{13,9},{14,10},{15,13... | collective-permute-start | bytes 307208 | tf_op jit(solution)/shard_map/ppermute | solution.py:382
  46.0 4.7 %collective-permute-start.25 = (bf16[16,3200]{1,0:T(8,128)(2,1)S(1)}, bf16[16,3200]{1,0:T(8,128)(2,1)S(1)}, u32[]{:S(2)}, u32[]{:S(2)}) collective-permute-start(bf16[16,3200]{1,0:T(8,128)(2,1)S(1)} %shard_map.103), channel_id=1, source_target_pairs={{0,4},{1,3},{4,8},{5,1},{8,12},{9,5},{12,14},{13,9},{14,10},{15,13... | collective-permute-start | bytes 307208 | tf_op jit(solution)/shard_map/ppermute | solution.py:382
  47.4 4.7 %collective-permute-start.21 = (bf16[16,3200]{1,0:T(8,128)(2,1)S(1)}, bf16[16,3200]{1,0:T(8,128)(2,1)S(1)}, u32[]{:S(2)}, u32[]{:S(2)}) collective-permute-start(bf16[16,3200]{1,0:T(8,128)(2,1)S(1)} %shard_map.99), channel_id=1, source_target_pairs={{0,4},{1,3},{4,8},{5,1},{8,12},{9,5},{12,14},{13,9},{14,10},{15,13... | collective-permute-start | bytes 307208 | tf_op jit(solution)/shard_map/ppermute | solution.py:382
  53.1 4.7 %collective-permute-start.28 = (bf16[16,3200]{1,0:T(8,128)(2,1)S(1)}, bf16[16,3200]{1,0:T(8,128)(2,1)S(1)}, u32[]{:S(2)}, u32[]{:S(2)}) collective-permute-start(bf16[16,3200]{1,0:T(8,128)(2,1)S(1)} %get-tuple-element.45.refs_0_), channel_id=1, source_target_pairs={{0,4},{1,3},{4,8},{5,1},{8,12},{9,5},{12,14},{13,9},{14,10},{15,13... | collective-permute-start | bytes 307208 | tf_op jit(solution)/shard_map/ppermute | solution.py:382
  55.3 4.7 %collective-permute-start.29 = (bf16[16,3200]{1,0:T(8,128)(2,1)S(1)}, bf16[16,3200]{1,0:T(8,128)(2,1)S(1)}, u32[]{:S(2)}, u32[]{:S(2)}) collective-permute-start(bf16[16,3200]{1,0:T(8,128)(2,1)S(1)} %collective-permute-done.27.refs_1_), channel_id=1, source_target_pairs={{0,4},{1,3},{4,8},{5,1},{8,12},{9,5},{12,14},{13,9},{14,10},{15,13... | collective-permute-start | bytes 307208 | tf_op jit(solution)/shard_map/ppermute | solution.py:382
  57.8 4.7 %collective-permute-start.32 = (bf16[16,3200]{1,0:T(8,128)(2,1)S(1)}, bf16[16,3200]{1,0:T(8,128)(2,1)S(1)}, u32[]{:S(2)}, u32[]{:S(2)}) collective-permute-start(bf16[16,3200]{1,0:T(8,128)(2,1)S(1)} %collective-permute-done.28.refs_2_), channel_id=1, source_target_pairs={{0,4},{1,3},{4,8},{5,1},{8,12},{9,5},{12,14},{13,9},{14,10},{15,13... | collective-permute-start | bytes 307208 | tf_op jit(solution)/shard_map/ppermute | solution.py:382
  59.9 4.7 %collective-permute-start.33 = (bf16[16,3200]{1,0:T(8,128)(2,1)S(1)}, bf16[16,3200]{1,0:T(8,128)(2,1)S(1)}, u32[]{:S(2)}, u32[]{:S(2)}) collective-permute-start(bf16[16,3200]{1,0:T(8,128)(2,1)S(1)} %collective-permute-done.29.refs_3_), channel_id=1, source_target_pairs={{0,4},{1,3},{4,8},{5,1},{8,12},{9,5},{12,14},{13,9},{14,10},{15,13... | collective-permute-start | bytes 307208 | tf_op jit(solution)/shard_map/ppermute | solution.py:382
  62.4 5.0 %collective-permute-start.36 = (bf16[16,3200]{1,0:T(8,128)(2,1)S(1)}, bf16[16,3200]{1,0:T(8,128)(2,1)S(1)}, u32[]{:S(2)}, u32[]{:S(2)}) collective-permute-start(bf16[16,3200]{1,0:T(8,128)(2,1)S(1)} %collective-permute-done.32.refs_6_), channel_id=1, source_target_pairs={{0,4},{1,3},{4,8},{5,1},{8,12},{9,5},{12,14},{13,9},{14,10},{15,13... | collective-permute-start | bytes 307208 | tf_op jit(solution)/shard_map/ppermute | solution.py:382
  64.6 4.7 %collective-permute-start.37 = (bf16[16,3200]{1,0:T(8,128)(2,1)S(1)}, bf16[16,3200]{1,0:T(8,128)(2,1)S(1)}, u32[]{:S(2)}, u32[]{:S(2)}) collective-permute-start(bf16[16,3200]{1,0:T(8,128)(2,1)S(1)} %collective-permute-done.33.refs_7_), channel_id=1, source_target_pairs={{0,4},{1,3},{4,8},{5,1},{8,12},{9,5},{12,14},{13,9},{14,10},{15,13... | collective-permute-start | bytes 307208 | tf_op jit(solution)/shard_map/ppermute | solution.py:382
  67.4 4.7 %collective-permute-start.40 = (bf16[16,3200]{1,0:T(8,128)(2,1)S(1)}, bf16[16,3200]{1,0:T(8,128)(2,1)S(1)}, u32[]{:S(2)}, u32[]{:S(2)}) collective-permute-start(bf16[16,3200]{1,0:T(8,128)(2,1)S(1)} %collective-permute-done.36.refs_10_), channel_id=1, source_target_pairs={{0,2},{1,3},{4,6},{5,1},{8,10},{9,5},{12,14},{13,9},{14,12},{15,13... | collective-permute-start | bytes 307208 | tf_op jit(solution)/shard_map/ppermute | solution.py:395
  69.3 4.7 %collective-permute-start.41 = (bf16[16,3200]{1,0:T(8,128)(2,1)S(1)}, bf16[16,3200]{1,0:T(8,128)(2,1)S(1)}, u32[]{:S(2)}, u32[]{:S(2)}) collective-permute-start(bf16[16,3200]{1,0:T(8,128)(2,1)S(1)} %collective-permute-done.37.refs_11_), channel_id=1, source_target_pairs={{0,2},{1,3},{4,6},{5,1},{8,10},{9,5},{12,14},{13,9},{14,12},{15,13... | collective-permute-start | bytes 307208 | tf_op jit(solution)/shard_map/ppermute | solution.py:395
  82.0 6.5 %collective-permute-start.45 = (bf16[6,16,3200]{2,1,0:T(8,128)(2,1)S(1)}, bf16[6,16,3200]{2,1,0:T(8,128)(2,1)S(1)}, u32[]{:S(2)}, u32[]{:S(2)}) collective-permute-start(bf16[6,16,3200]{2,1,0:T(8,128)(2,1)S(1)} %get-tuple-element.52), channel_id=1, source_target_pairs={{0,1},{1,0},{2,3},{3,2},{4,5},{5,4},{6,7},{7,6},{8,9},{9,8},{10,11... | collective-permute-start | bytes 1843208 | tf_op jit(solution)/shard_map/ppermute | solution.py:373
  82.2 7.1 %collective-permute-start.49 = (bf16[16,3200]{1,0:T(8,128)(2,1)S(1)}, bf16[16,3200]{1,0:T(8,128)(2,1)S(1)}, u32[]{:S(2)}, u32[]{:S(2)}) collective-permute-start(bf16[16,3200]{1,0:T(8,128)(2,1)S(1)} %shard_map.109), channel_id=1, source_target_pairs={{0,4},{1,3},{4,8},{5,1},{8,12},{9,5},{12,14},{13,9},{14,10},{15,13... | collective-permute-start | bytes 307208 | tf_op jit(solution)/shard_map/ppermute | solution.py:382
  87.1 5.8 %collective-permute-start.46 = (bf16[16,3200]{1,0:T(8,128)(2,1)S(1)}, bf16[16,3200]{1,0:T(8,128)(2,1)S(1)}, u32[]{:S(2)}, u32[]{:S(2)}) collective-permute-start(bf16[16,3200]{1,0:T(8,128)(2,1)S(1)} %shard_map.106), channel_id=1, source_target_pairs={{0,4},{1,3},{4,8},{5,1},{8,12},{9,5},{12,14},{13,9},{14,10},{15,13... | collective-permute-start | bytes 307208 | tf_op jit(solution)/shard_map/ppermute | solution.py:382
  88.5 7.6 %collective-permute-start.51 = (bf16[16,3200]{1,0:T(8,128)(2,1)S(1)}, bf16[16,3200]{1,0:T(8,128)(2,1)S(1)}, u32[]{:S(2)}, u32[]{:S(2)}) collective-permute-start(bf16[16,3200]{1,0:T(8,128)(2,1)S(1)} %shard_map.111), channel_id=1, source_target_pairs={{0,14},{1,15},{4,10},{5,11},{8,6},{9,7},{12,2},{13,3},{14,0},{15,1... | collective-permute-start | bytes 307208 | tf_op jit(solution)/shard_map/ppermute | solution.py:382
  89.4 6.7 %collective-permute-start.50 = (bf16[16,3200]{1,0:T(8,128)(2,1)S(1)}, bf16[16,3200]{1,0:T(8,128)(2,1)S(1)}, u32[]{:S(2)}, u32[]{:S(2)}) collective-permute-start(bf16[16,3200]{1,0:T(8,128)(2,1)S(1)} %shard_map.110), channel_id=1, source_target_pairs={{0,4},{1,3},{4,8},{5,1},{8,12},{9,5},{12,14},{13,9},{14,10},{15,13... | collective-permute-start | bytes 307208 | tf_op jit(solution)/shard_map/ppermute | solution.py:382
  93.0 4.7 %collective-permute-start.47 = (bf16[16,3200]{1,0:T(8,128)(2,1)S(1)}, bf16[16,3200]{1,0:T(8,128)(2,1)S(1)}, u32[]{:S(2)}, u32[]{:S(2)}) collective-permute-start(bf16[16,3200]{1,0:T(8,128)(2,1)S(1)} %shard_map.107), channel_id=1, source_target_pairs={{0,4},{1,3},{4,8},{5,1},{8,12},{9,5},{12,14},{13,9},{14,10},{15,13... | collective-permute-start | bytes 307208 | tf_op jit(solution)/shard_map/ppermute | solution.py:382
  96.2 4.7 %collective-permute-start.52 = (bf16[16,3200]{1,0:T(8,128)(2,1)S(1)}, bf16[16,3200]{1,0:T(8,128)(2,1)S(1)}, u32[]{:S(2)}, u32[]{:S(2)}) collective-permute-start(bf16[16,3200]{1,0:T(8,128)(2,1)S(1)} %shard_map.112), channel_id=1, source_target_pairs={{0,4},{1,3},{4,8},{5,1},{8,12},{9,5},{12,14},{13,9},{14,10},{15,13... | collective-permute-start | bytes 307208 | tf_op jit(solution)/shard_map/ppermute | solution.py:382
  97.7 4.7 %collective-permute-start.48 = (bf16[16,3200]{1,0:T(8,128)(2,1)S(1)}, bf16[16,3200]{1,0:T(8,128)(2,1)S(1)}, u32[]{:S(2)}, u32[]{:S(2)}) collective-permute-start(bf16[16,3200]{1,0:T(8,128)(2,1)S(1)} %shard_map.108), channel_id=1, source_target_pairs={{0,4},{1,3},{4,8},{5,1},{8,12},{9,5},{12,14},{13,9},{14,10},{15,13... | collective-permute-start | bytes 307208 | tf_op jit(solution)/shard_map/ppermute | solution.py:382
  (26 other events, 89.2 us)

commit v13 on v10

--- a/solution.py
+++ b/solution.py
@@ -12,6 +12,7 @@
 HBM = pl.BlockSpec(memory_space=pltpu.HBM)
 PARAMS = pltpu.CompilerParams(vmem_limit_bytes=48 * 1024 * 1024)
 HALF = 16
+GROUP = 4
 LANES = 128
 
 
@@ -175,22 +176,23 @@
 
     used = ints_ref[2 * slots]
 
-    def add_pair(step, carry):
-        one, two = 2 * step, 2 * step + 1
-        for slot in (one, two):
+    def add_some(step, carry):
+        some = [step * GROUP + k for k in range(GROUP)]
+        for slot in some:
             for copy in copies(slot):
                 copy.wait()
 
-        @pl.when(one < used)
+        @pl.when(some[0] < used)
         def _():
             products = [
                 jnp.dot(
                     left[slot], field[ints_ref[slot]], preferred_element_type=jnp.float32
                 ).astype(jnp.bfloat16)
-                for slot in (one, two)
+                for slot in some
             ]
-            products[1] = jnp.where(two < used, products[1], jnp.zeros_like(products[1]))
-            for slot, product in zip((one, two), products):
+            for slot, product in zip(some, products):
+                if slot is not some[0]:
+                    product = jnp.where(slot < used, product, jnp.zeros_like(product))
                 total[ints_ref[slots + slot]] += lax.dot_general(
                     product,
                     right[slot],
@@ -200,7 +202,7 @@
 
         return carry
 
-    lax.fori_loop(0, slots // 2, add_pair, 0)
+    lax.fori_loop(0, slots // GROUP, add_some, 0)
 
     dot = jnp.zeros((8, 128), jnp.float32)
     if first:
@@ -394,10 +396,7 @@
             results.append(beside[k](*results))
         if k < ROUNDS - 1:
             ready = results[-1:] if beside else []
-            if k == 1:
-                two, across, ready = lax.optimization_barrier((two, across, ready))
-            else:
-                two, ready = lax.optimization_barrier((two, ready))
+            two, ready = lax.optimization_barrier((two, ready))
             if ready:
                 results[-1] = ready[0]
         pieces += [one, two, flip(one), flip(two)]
@@ -412,9 +411,9 @@
     two = hop(chain(shape, 1, 1, me, total, dot, near))
     across = opposite(chain(shape, 6, 4, me, total, dot, far))
     for k in (2, 4):
+        if k == 4:
+            one, across = lax.optimization_barrier((one, across))
         one = hop(chain(shape, k, k - 2, me, total, dot, far, one))
-        if k == 4:
-            two, across = lax.optimization_barrier((two, across))
         two = hop(chain(shape, k + 1, k - 1, me, total, dot, far, two))
     return me, total, far, dot, one, flip(two), across
 

time: 99.3 us -> 101 us (1.017)
  waiting for transfers between devices: 21.2 us -> 33.9 us
  starting transfers between devices: 60 us -> 47.9 us
    ppermute x28, waiting for transfers between devices: 17.4 us -> 28.9 us  [hop(): return lax.ppermute(value, 'term', pairs)]
    ppermute x28, starting transfers between devices: 52.4 us -> 43 us  [hop(): return lax.ppermute(value, 'term', pairs)]
    ppermute x22, starting transfers between devices: 7.59 us -> 4.83 us  [flip(): return lax.ppermute(value, 'term', [(i, i ^ 1) for i in range(16)])]
    ppermute x22, waiting for transfers between devices: 3.81 us -> 4.98 us  [flip(): return lax.ppermute(value, 'term', [(i, i ^ 1) for i in range(16)])]
  transfers between devices with their start and end apart: 50 -> 50, of which waited for: 19 -> 28; matrix products, arithmetic and copies ran while one was open for 1% -> 1% of each run, Pallas kernels for 1% -> 1%
where the time goes in v13:
time: 101 us
  starting transfers between devices  47.9 us (47%)
  waiting for transfers between devices  33.9 us (34%)
  Pallas kernels  14.7 us (15%)
  local copies, waits for them, and re-layouts  1.8 us (2%)
  between operations  1.54 us (2%)
    ppermute x28, starting transfers between devices, hop(): return lax.ppermute(value, 'term', pairs)  43 us
    ppermute x28, waiting for transfers between devices, hop(): return lax.ppermute(value, 'term', pairs)  28.9 us
    pallas_call x2, Pallas kernels, apply_blocks(): pl.pallas_call(functools.partial(blocks_kernel, first, shape, entries), i...  12.2 us
    ppermute x22, waiting for transfers between devices, flip(): return lax.ppermute(value, 'term', [(i, i ^ 1) for i in range(16)])  4.98 us
    ppermute x22, starting transfers between devices, flip(): return lax.ppermute(value, 'term', [(i, i ^ 1) for i in range(16)])  4.83 us
  transfers between devices with their start and end apart: 50, of which 28 were waited for; matrix products, arithmetic and copies ran while one was open for 1% of the time, Pallas kernels for 1%

profile of v13, /device:TPU:0, one launch (start us, length us, event | category | flops | bytes accessed | tf_op | source)
XLA Modules:
  0.0 100.6 jit_solution(2561765645795043709)
XLA Ops:
  1.1 2.6 %collective-permute-start.3 = (bf16[3,32,512]{2,1,0:T(8,128)(2,1)}, bf16[3,32,512]{2,1,0:T(8,128)(2,1)S(1)}, u32[]{:S(2)}, u32[]{:S(2)}) collective-permute-start(bf16[3,32,512]{2,1,0:T(8,128)(2,1)} %wave_ref.3), channel_id=1, source_target_pairs={{0,4},{1,3},{4,8},{5,1},{8,12},{9,5},{12,14},{13,9},{14,10},{15,13... | collective-permute-start | bytes 294920 | tf_op jit(solution)/shard_map/ppermute | solution.py:380
  4.4 1.6 %collective-permute-start.1 = (bf16[3,32,512]{2,1,0:T(8,128)(2,1)S(1)}, bf16[3,32,512]{2,1,0:T(8,128)(2,1)S(1)}, u32[]{:S(2)}, u32[]{:S(2)}) collective-permute-start(bf16[3,32,512]{2,1,0:T(8,128)(2,1)S(1)} %collective-permute-done.refs_1_), channel_id=1, source_target_pairs={{0,4},{1,3},{4,8},{5,1},{8,12},{9,5},{12,14},{13,9},{14,10},{15,13... | collective-permute-start | bytes 294920 | tf_op jit(solution)/shard_map/ppermute | solution.py:380
  6.8 1.8 %collective-permute-start.6 = (bf16[3,32,512]{2,1,0:T(8,128)(2,1)S(1)}, bf16[3,32,512]{2,1,0:T(8,128)(2,1)S(1)}, u32[]{:S(2)}, u32[]{:S(2)}) collective-permute-start(bf16[3,32,512]{2,1,0:T(8,128)(2,1)S(1)} %collective-permute-done.3.refs_2_), channel_id=1, source_target_pairs={{0,4},{1,3},{4,8},{5,1},{8,12},{9,5},{12,14},{13,9},{14,10},{15,13... | collective-permute-start | bytes 294920 | tf_op jit(solution)/shard_map/ppermute | solution.py:380
  9.1 1.6 %collective-permute-start.2 = (bf16[3,32,512]{2,1,0:T(8,128)(2,1)S(1)}, bf16[3,32,512]{2,1,0:T(8,128)(2,1)S(1)}, u32[]{:S(2)}, u32[]{:S(2)}) collective-permute-start(bf16[3,32,512]{2,1,0:T(8,128)(2,1)S(1)} %collective-permute-done.1.refs_3_), channel_id=1, source_target_pairs={{0,4},{1,3},{4,8},{5,1},{8,12},{9,5},{12,14},{13,9},{14,10},{15,13... | collective-permute-start | bytes 294920 | tf_op jit(solution)/shard_map/ppermute | solution.py:380
  11.6 2.6 %collective-permute-start.13 = (bf16[3,32,512]{2,1,0:T(8,128)(2,1)S(1)}, bf16[3,32,512]{2,1,0:T(8,128)(2,1)S(1)}, u32[]{:S(2)}, u32[]{:S(2)}) collective-permute-start(bf16[3,32,512]{2,1,0:T(8,128)(2,1)S(1)} %copy-done), channel_id=1, source_target_pairs={{0,14},{1,15},{4,10},{5,11},{8,6},{9,7},{12,2},{13,3},{14,0},{15,1... | collective-permute-start | bytes 294920 | tf_op jit(solution)/shard_map/ppermute | solution.py:380
  14.3 1.8 %collective-permute-start.7 = (bf16[3,32,512]{2,1,0:T(8,128)(2,1)S(1)}, bf16[3,32,512]{2,1,0:T(8,128)(2,1)S(1)}, u32[]{:S(2)}, u32[]{:S(2)}) collective-permute-start(bf16[3,32,512]{2,1,0:T(8,128)(2,1)S(1)} %collective-permute-done.6.refs_6_), channel_id=1, source_target_pairs={{0,1},{1,0},{2,3},{3,2},{4,5},{5,4},{6,7},{7,6},{8,9},{9,8},{10,11... | collective-permute-start | bytes 294920 | tf_op jit(solution)/shard_map/ppermute | solution.py:371
  16.5 2.6 %collective-permute-done.13.refs_14_ = bf16[3,32,512]{2,1,0:T(8,128)(2,1)S(1)} collective-permute-done((bf16[3,32,512]{2,1,0:T(8,128)(2,1)S(1)}, bf16[3,32,512]{2,1,0:T(8,128)(2,1)S(1)}, u32[]{:S(2)}, u32[]{:S(2)}) %collective-permute-start.13) | collective-permute-done | bytes 98336 | tf_op jit(solution)/shard_map/ppermute | solution.py:380
  22.3 6.5 %shard_map.96 = (f32[3,512,512]{2,1,0:T(8,128)S(1)}, bf16[2,16,3200]{2,1,0:T(8,128)(2,1)S(1)}, bf16[6,16,3200]{2,1,0:T(8,128)(2,1)S(1)}, f32[8,128]{1,0:T(8,128)S(1)}, f32[8,128]{1,0:T(8,128)S(1)}) custom-call(s32[1]{0:T(128)} %bitcast.me_ref.refs_0_.refs_2_, s32[17]{0:T(128)S(1)} %pad_add_fusion.ints_ref, ...), custom_call_target="tpu_custom_call" | custom-call | flops 4294967296 | bytes 8388608 | tf_op jit(solution)/shard_map/pallas_call | solution.py:237
  29.1 1.2 %collective-permute-done.15.other_ref = bf16[2,16,3200]{2,1,0:T(8,128)(2,1)S(1)} collective-permute-done((bf16[2,16,3200]{2,1,0:T(8,128)(2,1)S(1)}, bf16[2,16,3200]{2,1,0:T(8,128)(2,1)S(1)}, u32[]{:S(2)}, u32[]{:S(2)}) %collective-permute-start.15) | collective-permute-done | bytes 204832 | tf_op jit(solution)/shard_map/ppermute | solution.py:371
  30.6 3.2 %collective-permute-start.21 = (bf16[16,3200]{1,0:T(8,128)(2,1)S(1)}, bf16[16,3200]{1,0:T(8,128)(2,1)S(1)}, u32[]{:S(2)}, u32[]{:S(2)}) collective-permute-start(bf16[16,3200]{1,0:T(8,128)(2,1)S(1)} %shard_map.101), channel_id=1, source_target_pairs={{0,4},{1,3},{4,8},{5,1},{8,12},{9,5},{12,14},{13,9},{14,10},{15,13... | collective-permute-start | bytes 307208 | tf_op jit(solution)/shard_map/ppermute | solution.py:380
  33.8 1.6 %collective-permute-start.17 = (bf16[16,3200]{1,0:T(8,128)(2,1)S(1)}, bf16[16,3200]{1,0:T(8,128)(2,1)S(1)}, u32[]{:S(2)}, u32[]{:S(2)}) collective-permute-start(bf16[16,3200]{1,0:T(8,128)(2,1)S(1)} %shard_map.97), channel_id=1, source_target_pairs={{0,4},{1,3},{4,8},{5,1},{8,12},{9,5},{12,14},{13,9},{14,10},{15,13... | collective-permute-start | bytes 307208 | tf_op jit(solution)/shard_map/ppermute | solution.py:380
  35.3 1.1 %collective-permute-done.21.refs_0_ = bf16[16,3200]{1,0:T(8,128)(2,1)S(1)} collective-permute-done((bf16[16,3200]{1,0:T(8,128)(2,1)S(1)}, bf16[16,3200]{1,0:T(8,128)(2,1)S(1)}, u32[]{:S(2)}, u32[]{:S(2)}) %collective-permute-start.21) | collective-permute-done | bytes 102432 | tf_op jit(solution)/shard_map/ppermute | solution.py:380
  36.5 2.0 %collective-permute-start.22 = (bf16[16,3200]{1,0:T(8,128)(2,1)S(1)}, bf16[16,3200]{1,0:T(8,128)(2,1)S(1)}, u32[]{:S(2)}, u32[]{:S(2)}) collective-permute-start(bf16[16,3200]{1,0:T(8,128)(2,1)S(1)} %shard_map.102), channel_id=1, source_target_pairs={{0,4},{1,3},{4,8},{5,1},{8,12},{9,5},{12,14},{13,9},{14,10},{15,13... | collective-permute-start | bytes 307208 | tf_op jit(solution)/shard_map/ppermute | solution.py:380
  38.6 2.3 %collective-permute-start.19 = (bf16[16,3200]{1,0:T(8,128)(2,1)S(1)}, bf16[16,3200]{1,0:T(8,128)(2,1)S(1)}, u32[]{:S(2)}, u32[]{:S(2)}) collective-permute-start(bf16[16,3200]{1,0:T(8,128)(2,1)S(1)} %shard_map.99), channel_id=1, source_target_pairs={{0,14},{1,15},{4,10},{5,11},{8,6},{9,7},{12,2},{13,3},{14,0},{15,1... | collective-permute-start | bytes 307208 | tf_op jit(solution)/shard_map/ppermute | solution.py:380
  41.7 2.5 %collective-permute-start.23 = (bf16[16,3200]{1,0:T(8,128)(2,1)S(1)}, bf16[16,3200]{1,0:T(8,128)(2,1)S(1)}, u32[]{:S(2)}, u32[]{:S(2)}) collective-permute-start(bf16[16,3200]{1,0:T(8,128)(2,1)S(1)} %shard_map.103), channel_id=1, source_target_pairs={{0,4},{1,3},{4,8},{5,1},{8,12},{9,5},{12,14},{13,9},{14,10},{15,13... | collective-permute-start | bytes 307208 | tf_op jit(solution)/shard_map/ppermute | solution.py:380
  44.2 1.9 %collective-permute-done.19.refs_6_ = bf16[16,3200]{1,0:T(8,128)(2,1)S(1)} collective-permute-done((bf16[16,3200]{1,0:T(8,128)(2,1)S(1)}, bf16[16,3200]{1,0:T(8,128)(2,1)S(1)}, u32[]{:S(2)}, u32[]{:S(2)}) %collective-permute-start.19) | collective-permute-done | bytes 102432 | tf_op jit(solution)/shard_map/ppermute | solution.py:380
  47.9 3.7 %collective-permute-done.20.refs_4_ = bf16[16,3200]{1,0:T(8,128)(2,1)S(1)} collective-permute-done((bf16[16,3200]{1,0:T(8,128)(2,1)S(1)}, bf16[16,3200]{1,0:T(8,128)(2,1)S(1)}, u32[]{:S(2)}, u32[]{:S(2)}) %collective-permute-start.20) | collective-permute-done | bytes 102432 | tf_op jit(solution)/shard_map/ppermute | solution.py:380
  53.7 1.3 %collective-permute-start.27 = (bf16[16,3200]{1,0:T(8,128)(2,1)S(1)}, bf16[16,3200]{1,0:T(8,128)(2,1)S(1)}, u32[]{:S(2)}, u32[]{:S(2)}) collective-permute-start(bf16[16,3200]{1,0:T(8,128)(2,1)S(1)} %collective-permute-done.25.refs_1_), channel_id=1, source_target_pairs={{0,4},{1,3},{4,8},{5,1},{8,12},{9,5},{12,14},{13,9},{14,10},{15,13... | collective-permute-start | bytes 307208 | tf_op jit(solution)/shard_map/ppermute | solution.py:380
  55.0 2.1 %collective-permute-done.26.refs_2_ = bf16[16,3200]{1,0:T(8,128)(2,1)S(1)} collective-permute-done((bf16[16,3200]{1,0:T(8,128)(2,1)S(1)}, bf16[16,3200]{1,0:T(8,128)(2,1)S(1)}, u32[]{:S(2)}, u32[]{:S(2)}) %collective-permute-start.26) | collective-permute-done | bytes 102432 | tf_op jit(solution)/shard_map/ppermute | solution.py:380
  58.4 1.3 %collective-permute-start.31 = (bf16[16,3200]{1,0:T(8,128)(2,1)S(1)}, bf16[16,3200]{1,0:T(8,128)(2,1)S(1)}, u32[]{:S(2)}, u32[]{:S(2)}) collective-permute-start(bf16[16,3200]{1,0:T(8,128)(2,1)S(1)} %collective-permute-done.27.refs_3_), channel_id=1, source_target_pairs={{0,4},{1,3},{4,8},{5,1},{8,12},{9,5},{12,14},{13,9},{14,10},{15,13... | collective-permute-start | bytes 307208 | tf_op jit(solution)/shard_map/ppermute | solution.py:380
  59.7 2.0 %collective-permute-start.38 = (bf16[16,3200]{1,0:T(8,128)(2,1)S(1)}, bf16[16,3200]{1,0:T(8,128)(2,1)S(1)}, u32[]{:S(2)}, u32[]{:S(2)}) collective-permute-start(bf16[16,3200]{1,0:T(8,128)(2,1)S(1)} %get-tuple-element.53.refs_0_), channel_id=1, source_target_pairs={{0,14},{1,15},{4,10},{5,11},{8,6},{9,7},{12,2},{13,3},{14,0},{15,1... | collective-permute-start | bytes 307208 | tf_op jit(solution)/shard_map/ppermute | solution.py:380
  63.1 1.3 %collective-permute-start.35 = (bf16[16,3200]{1,0:T(8,128)(2,1)S(1)}, bf16[16,3200]{1,0:T(8,128)(2,1)S(1)}, u32[]{:S(2)}, u32[]{:S(2)}) collective-permute-start(bf16[16,3200]{1,0:T(8,128)(2,1)S(1)} %collective-permute-done.31.refs_7_), channel_id=1, source_target_pairs={{0,4},{1,3},{4,8},{5,1},{8,12},{9,5},{12,14},{13,9},{14,10},{15,13... | collective-permute-start | bytes 307208 | tf_op jit(solution)/shard_map/ppermute | solution.py:380
  64.4 3.6 %collective-permute-done.38.refs_14_ = bf16[16,3200]{1,0:T(8,128)(2,1)S(1)} collective-permute-done((bf16[16,3200]{1,0:T(8,128)(2,1)S(1)}, bf16[16,3200]{1,0:T(8,128)(2,1)S(1)}, u32[]{:S(2)}, u32[]{:S(2)}) %collective-permute-start.38) | collective-permute-done | bytes 102432 | tf_op jit(solution)/shard_map/ppermute | solution.py:380
  71.0 5.7 %shard_map.105 = (f32[3,512,512]{2,1,0:T(8,128)S(1)}, bf16[2,16,3200]{2,1,0:T(8,128)(2,1)S(1)}, bf16[6,16,3200]{2,1,0:T(8,128)(2,1)S(1)}, f32[8,128]{1,0:T(8,128)S(1)}, f32[8,128]{1,0:T(8,128)S(1)}) custom-call(s32[1]{0:T(128)} %bitcast.me_ref.refs_0_.refs_2_, s32[17]{0:T(128)S(1)} %pad_add_fusion.ints_ref, bf16[16,3200]{1,0:T(8,128)(2,1)S(1)} %get-tuple-element.53.refs_0_, ...), custom_call_target="tpu_custom_call" | custom-call | flops 4294967296 | bytes 8388608 | tf_op jit(solution)/shard_map/pallas_call | solution.py:237
  76.9 1.3 %collective-permute-done.40.other_ref = bf16[2,16,3200]{2,1,0:T(8,128)(2,1)S(1)} collective-permute-done((bf16[2,16,3200]{2,1,0:T(8,128)(2,1)S(1)}, bf16[2,16,3200]{2,1,0:T(8,128)(2,1)S(1)}, u32[]{:S(2)}, u32[]{:S(2)}) %collective-permute-start.40) | collective-permute-done | bytes 204832 | tf_op jit(solution)/shard_map/ppermute | solution.py:371
  78.4 3.0 %collective-permute-start.46 = (bf16[16,3200]{1,0:T(8,128)(2,1)S(1)}, bf16[16,3200]{1,0:T(8,128)(2,1)S(1)}, u32[]{:S(2)}, u32[]{:S(2)}) collective-permute-start(bf16[16,3200]{1,0:T(8,128)(2,1)S(1)} %shard_map.110), channel_id=1, source_target_pairs={{0,4},{1,3},{4,8},{5,1},{8,12},{9,5},{12,14},{13,9},{14,10},{15,13... | collective-permute-start | bytes 307208 | tf_op jit(solution)/shard_map/ppermute | solution.py:380
  81.4 2.0 %collective-permute-start.42 = (bf16[16,3200]{1,0:T(8,128)(2,1)S(1)}, bf16[16,3200]{1,0:T(8,128)(2,1)S(1)}, u32[]{:S(2)}, u32[]{:S(2)}) collective-permute-start(bf16[16,3200]{1,0:T(8,128)(2,1)S(1)} %shard_map.106), channel_id=1, source_target_pairs={{0,4},{1,3},{4,8},{5,1},{8,12},{9,5},{12,14},{13,9},{14,10},{15,13... | collective-permute-start | bytes 307208 | tf_op jit(solution)/shard_map/ppermute | solution.py:380
  84.4 1.8 %collective-permute-start.47 = (bf16[16,3200]{1,0:T(8,128)(2,1)S(1)}, bf16[16,3200]{1,0:T(8,128)(2,1)S(1)}, u32[]{:S(2)}, u32[]{:S(2)}) collective-permute-start(bf16[16,3200]{1,0:T(8,128)(2,1)S(1)} %shard_map.111), channel_id=1, source_target_pairs={{0,4},{1,3},{4,8},{5,1},{8,12},{9,5},{12,14},{13,9},{14,10},{15,13... | collective-permute-start | bytes 307208 | tf_op jit(solution)/shard_map/ppermute | solution.py:380
  86.2 2.8 %collective-permute-start.44 = (bf16[16,3200]{1,0:T(8,128)(2,1)S(1)}, bf16[16,3200]{1,0:T(8,128)(2,1)S(1)}, u32[]{:S(2)}, u32[]{:S(2)}) collective-permute-start(bf16[16,3200]{1,0:T(8,128)(2,1)S(1)} %shard_map.108), channel_id=1, source_target_pairs={{0,14},{1,15},{4,10},{5,11},{8,6},{9,7},{12,2},{13,3},{14,0},{15,1... | collective-permute-start | bytes 307208 | tf_op jit(solution)/shard_map/ppermute | solution.py:380
  89.3 2.5 %collective-permute-start.48 = (bf16[16,3200]{1,0:T(8,128)(2,1)S(1)}, bf16[16,3200]{1,0:T(8,128)(2,1)S(1)}, u32[]{:S(2)}, u32[]{:S(2)}) collective-permute-start(bf16[16,3200]{1,0:T(8,128)(2,1)S(1)} %shard_map.112), channel_id=1, source_target_pairs={{0,4},{1,3},{4,8},{5,1},{8,12},{9,5},{12,14},{13,9},{14,10},{15,13... | collective-permute-start | bytes 307208 | tf_op jit(solution)/shard_map/ppermute | solution.py:380
  91.8 2.1 %collective-permute-done.44.refs_8_ = bf16[16,3200]{1,0:T(8,128)(2,1)S(1)} collective-permute-done((bf16[16,3200]{1,0:T(8,128)(2,1)S(1)}, bf16[16,3200]{1,0:T(8,128)(2,1)S(1)}, u32[]{:S(2)}, u32[]{:S(2)}) %collective-permute-start.44) | collective-permute-done | bytes 102432 | tf_op jit(solution)/shard_map/ppermute | solution.py:380
  96.0 3.7 %collective-permute-done.45.refs_6_ = bf16[16,3200]{1,0:T(8,128)(2,1)S(1)} collective-permute-done((bf16[16,3200]{1,0:T(8,128)(2,1)S(1)}, bf16[16,3200]{1,0:T(8,128)(2,1)S(1)}, u32[]{:S(2)}, u32[]{:S(2)}) %collective-permute-start.45) | collective-permute-done | bytes 102432 | tf_op jit(solution)/shard_map/ppermute | solution.py:380
  (97 shorter events, 22.0 us)
Async XLA Ops:
  1.1 5.7 %collective-permute-start.3 = (bf16[3,32,512]{2,1,0:T(8,128)(2,1)}, bf16[3,32,512]{2,1,0:T(8,128)(2,1)S(1)}, u32[]{:S(2)}, u32[]{:S(2)}) collective-permute-start(bf16[3,32,512]{2,1,0:T(8,128)(2,1)} %wave_ref.3), channel_id=1, source_target_pairs={{0,4},{1,3},{4,8},{5,1},{8,12},{9,5},{12,14},{13,9},{14,10},{15,13... | collective-permute-start | bytes 294920 | tf_op jit(solution)/shard_map/ppermute | solution.py:380
  4.4 4.7 %collective-permute-start.1 = (bf16[3,32,512]{2,1,0:T(8,128)(2,1)S(1)}, bf16[3,32,512]{2,1,0:T(8,128)(2,1)S(1)}, u32[]{:S(2)}, u32[]{:S(2)}) collective-permute-start(bf16[3,32,512]{2,1,0:T(8,128)(2,1)S(1)} %collective-permute-done.refs_1_), channel_id=1, source_target_pairs={{0,4},{1,3},{4,8},{5,1},{8,12},{9,5},{12,14},{13,9},{14,10},{15,13... | collective-permute-start | bytes 294920 | tf_op jit(solution)/shard_map/ppermute | solution.py:380
  6.8 7.4 %collective-permute-start.6 = (bf16[3,32,512]{2,1,0:T(8,128)(2,1)S(1)}, bf16[3,32,512]{2,1,0:T(8,128)(2,1)S(1)}, u32[]{:S(2)}, u32[]{:S(2)}) collective-permute-start(bf16[3,32,512]{2,1,0:T(8,128)(2,1)S(1)} %collective-permute-done.3.refs_2_), channel_id=1, source_target_pairs={{0,4},{1,3},{4,8},{5,1},{8,12},{9,5},{12,14},{13,9},{14,10},{15,13... | collective-permute-start | bytes 294920 | tf_op jit(solution)/shard_map/ppermute | solution.py:380
  9.1 6.9 %collective-permute-start.2 = (bf16[3,32,512]{2,1,0:T(8,128)(2,1)S(1)}, bf16[3,32,512]{2,1,0:T(8,128)(2,1)S(1)}, u32[]{:S(2)}, u32[]{:S(2)}) collective-permute-start(bf16[3,32,512]{2,1,0:T(8,128)(2,1)S(1)} %collective-permute-done.1.refs_3_), channel_id=1, source_target_pairs={{0,4},{1,3},{4,8},{5,1},{8,12},{9,5},{12,14},{13,9},{14,10},{15,13... | collective-permute-start | bytes 294920 | tf_op jit(solution)/shard_map/ppermute | solution.py:380
  11.6 7.5 %collective-permute-start.13 = (bf16[3,32,512]{2,1,0:T(8,128)(2,1)S(1)}, bf16[3,32,512]{2,1,0:T(8,128)(2,1)S(1)}, u32[]{:S(2)}, u32[]{:S(2)}) collective-permute-start(bf16[3,32,512]{2,1,0:T(8,128)(2,1)S(1)} %copy-done), channel_id=1, source_target_pairs={{0,14},{1,15},{4,10},{5,11},{8,6},{9,7},{12,2},{13,3},{14,0},{15,1... | collective-permute-start | bytes 294920 | tf_op jit(solution)/shard_map/ppermute | solution.py:380
  14.2 5.7 %collective-permute-start.9 = (bf16[3,32,512]{2,1,0:T(8,128)(2,1)S(1)}, bf16[3,32,512]{2,1,0:T(8,128)(2,1)S(1)}, u32[]{:S(2)}, u32[]{:S(2)}) collective-permute-start(bf16[3,32,512]{2,1,0:T(8,128)(2,1)S(1)} %collective-permute-done.6.refs_6_), channel_id=1, source_target_pairs={{0,4},{1,3},{4,8},{5,1},{8,12},{9,5},{12,14},{13,9},{14,10},{15,13... | collective-permute-start | bytes 294920 | tf_op jit(solution)/shard_map/ppermute | solution.py:380
  14.3 5.7 %collective-permute-start.7 = (bf16[3,32,512]{2,1,0:T(8,128)(2,1)S(1)}, bf16[3,32,512]{2,1,0:T(8,128)(2,1)S(1)}, u32[]{:S(2)}, u32[]{:S(2)}) collective-permute-start(bf16[3,32,512]{2,1,0:T(8,128)(2,1)S(1)} %collective-permute-done.6.refs_6_), channel_id=1, source_target_pairs={{0,1},{1,0},{2,3},{3,2},{4,5},{5,4},{6,7},{7,6},{8,9},{9,8},{10,11... | collective-permute-start | bytes 294920 | tf_op jit(solution)/shard_map/ppermute | solution.py:371
  16.1 4.9 %collective-permute-start.10 = (bf16[3,32,512]{2,1,0:T(8,128)(2,1)S(1)}, bf16[3,32,512]{2,1,0:T(8,128)(2,1)S(1)}, u32[]{:S(2)}, u32[]{:S(2)}) collective-permute-start(bf16[3,32,512]{2,1,0:T(8,128)(2,1)S(1)} %collective-permute-done.2.refs_7_), channel_id=1, source_target_pairs={{0,4},{1,3},{4,8},{5,1},{8,12},{9,5},{12,14},{13,9},{14,10},{15,13... | collective-permute-start | bytes 294920 | tf_op jit(solution)/shard_map/ppermute | solution.py:380
  16.5 5.4 %collective-permute-start.5 = (bf16[3,32,512]{2,1,0:T(8,128)(2,1)S(1)}, bf16[3,32,512]{2,1,0:T(8,128)(2,1)S(1)}, u32[]{:S(2)}, u32[]{:S(2)}) collective-permute-start(bf16[3,32,512]{2,1,0:T(8,128)(2,1)S(1)} %collective-permute-done.1.refs_3_), channel_id=1, source_target_pairs={{0,1},{1,0},{2,3},{3,2},{4,5},{5,4},{6,7},{7,6},{8,9},{9,8},{10,11... | collective-permute-start | bytes 294920 | tf_op jit(solution)/shard_map/ppermute | solution.py:371
  30.3 6.1 %collective-permute-start.16 = (bf16[6,16,3200]{2,1,0:T(8,128)(2,1)S(1)}, bf16[6,16,3200]{2,1,0:T(8,128)(2,1)S(1)}, u32[]{:S(2)}, u32[]{:S(2)}) collective-permute-start(bf16[6,16,3200]{2,1,0:T(8,128)(2,1)S(1)} %get-tuple-element.45), channel_id=1, source_target_pairs={{0,1},{1,0},{2,3},{3,2},{4,5},{5,4},{6,7},{7,6},{8,9},{9,8},{10,11... | collective-permute-start | bytes 1843208 | tf_op jit(solution)/shard_map/ppermute | solution.py:371
  30.6 5.9 %collective-permute-start.21 = (bf16[16,3200]{1,0:T(8,128)(2,1)S(1)}, bf16[16,3200]{1,0:T(8,128)(2,1)S(1)}, u32[]{:S(2)}, u32[]{:S(2)}) collective-permute-start(bf16[16,3200]{1,0:T(8,128)(2,1)S(1)} %shard_map.101), channel_id=1, source_target_pairs={{0,4},{1,3},{4,8},{5,1},{8,12},{9,5},{12,14},{13,9},{14,10},{15,13... | collective-permute-start | bytes 307208 | tf_op jit(solution)/shard_map/ppermute | solution.py:380
  33.8 7.1 %collective-permute-start.17 = (bf16[16,3200]{1,0:T(8,128)(2,1)S(1)}, bf16[16,3200]{1,0:T(8,128)(2,1)S(1)}, u32[]{:S(2)}, u32[]{:S(2)}) collective-permute-start(bf16[16,3200]{1,0:T(8,128)(2,1)S(1)} %shard_map.97), channel_id=1, source_target_pairs={{0,4},{1,3},{4,8},{5,1},{8,12},{9,5},{12,14},{13,9},{14,10},{15,13... | collective-permute-start | bytes 307208 | tf_op jit(solution)/shard_map/ppermute | solution.py:380
  36.5 5.2 %collective-permute-start.22 = (bf16[16,3200]{1,0:T(8,128)(2,1)S(1)}, bf16[16,3200]{1,0:T(8,128)(2,1)S(1)}, u32[]{:S(2)}, u32[]{:S(2)}) collective-permute-start(bf16[16,3200]{1,0:T(8,128)(2,1)S(1)} %shard_map.102), channel_id=1, source_target_pairs={{0,4},{1,3},{4,8},{5,1},{8,12},{9,5},{12,14},{13,9},{14,10},{15,13... | collective-permute-start | bytes 307208 | tf_op jit(solution)/shard_map/ppermute | solution.py:380
  38.6 7.6 %collective-permute-start.19 = (bf16[16,3200]{1,0:T(8,128)(2,1)S(1)}, bf16[16,3200]{1,0:T(8,128)(2,1)S(1)}, u32[]{:S(2)}, u32[]{:S(2)}) collective-permute-start(bf16[16,3200]{1,0:T(8,128)(2,1)S(1)} %shard_map.99), channel_id=1, source_target_pairs={{0,14},{1,15},{4,10},{5,11},{8,6},{9,7},{12,2},{13,3},{14,0},{15,1... | collective-permute-start | bytes 307208 | tf_op jit(solution)/shard_map/ppermute | solution.py:380
  40.9 5.8 %collective-permute-start.18 = (bf16[16,3200]{1,0:T(8,128)(2,1)S(1)}, bf16[16,3200]{1,0:T(8,128)(2,1)S(1)}, u32[]{:S(2)}, u32[]{:S(2)}) collective-permute-start(bf16[16,3200]{1,0:T(8,128)(2,1)S(1)} %shard_map.98), channel_id=1, source_target_pairs={{0,4},{1,3},{4,8},{5,1},{8,12},{9,5},{12,14},{13,9},{14,10},{15,13... | collective-permute-start | bytes 307208 | tf_op jit(solution)/shard_map/ppermute | solution.py:380
  41.7 6.1 %collective-permute-start.23 = (bf16[16,3200]{1,0:T(8,128)(2,1)S(1)}, bf16[16,3200]{1,0:T(8,128)(2,1)S(1)}, u32[]{:S(2)}, u32[]{:S(2)}) collective-permute-start(bf16[16,3200]{1,0:T(8,128)(2,1)S(1)} %shard_map.103), channel_id=1, source_target_pairs={{0,4},{1,3},{4,8},{5,1},{8,12},{9,5},{12,14},{13,9},{14,10},{15,13... | collective-permute-start | bytes 307208 | tf_op jit(solution)/shard_map/ppermute | solution.py:380
  46.8 4.7 %collective-permute-start.20 = (bf16[16,3200]{1,0:T(8,128)(2,1)S(1)}, bf16[16,3200]{1,0:T(8,128)(2,1)S(1)}, u32[]{:S(2)}, u32[]{:S(2)}) collective-permute-start(bf16[16,3200]{1,0:T(8,128)(2,1)S(1)} %shard_map.100), channel_id=1, source_target_pairs={{0,4},{1,3},{4,8},{5,1},{8,12},{9,5},{12,14},{13,9},{14,10},{15,13... | collective-permute-start | bytes 307208 | tf_op jit(solution)/shard_map/ppermute | solution.py:380
  52.4 4.7 %collective-permute-start.26 = (bf16[16,3200]{1,0:T(8,128)(2,1)S(1)}, bf16[16,3200]{1,0:T(8,128)(2,1)S(1)}, u32[]{:S(2)}, u32[]{:S(2)}) collective-permute-start(bf16[16,3200]{1,0:T(8,128)(2,1)S(1)} %get-tuple-element.53.refs_0_), channel_id=1, source_target_pairs={{0,4},{1,3},{4,8},{5,1},{8,12},{9,5},{12,14},{13,9},{14,10},{15,13... | collective-permute-start | bytes 307208 | tf_op jit(solution)/shard_map/ppermute | solution.py:380
  59.7 4.7 %collective-permute-start.28 = (bf16[16,3200]{1,0:T(8,128)(2,1)S(1)}, bf16[16,3200]{1,0:T(8,128)(2,1)S(1)}, u32[]{:S(2)}, u32[]{:S(2)}) collective-permute-start(bf16[16,3200]{1,0:T(8,128)(2,1)S(1)} %collective-permute-done.26.refs_2_), channel_id=1, source_target_pairs={{0,1},{1,0},{2,3},{3,2},{4,5},{5,4},{6,7},{7,6},{8,9},{9,8},{10,11... | collective-permute-start | bytes 307208 | tf_op jit(solution)/shard_map/ppermute | solution.py:371
  59.7 8.3 %collective-permute-start.38 = (bf16[16,3200]{1,0:T(8,128)(2,1)S(1)}, bf16[16,3200]{1,0:T(8,128)(2,1)S(1)}, u32[]{:S(2)}, u32[]{:S(2)}) collective-permute-start(bf16[16,3200]{1,0:T(8,128)(2,1)S(1)} %get-tuple-element.53.refs_0_), channel_id=1, source_target_pairs={{0,14},{1,15},{4,10},{5,11},{8,6},{9,7},{12,2},{13,3},{14,0},{15,1... | collective-permute-start | bytes 307208 | tf_op jit(solution)/shard_map/ppermute | solution.py:380
  61.8 6.9 %collective-permute-start.34 = (bf16[16,3200]{1,0:T(8,128)(2,1)S(1)}, bf16[16,3200]{1,0:T(8,128)(2,1)S(1)}, u32[]{:S(2)}, u32[]{:S(2)}) collective-permute-start(bf16[16,3200]{1,0:T(8,128)(2,1)S(1)} %collective-permute-done.30.refs_6_), channel_id=1, source_target_pairs={{0,4},{1,3},{4,8},{5,1},{8,12},{9,5},{12,14},{13,9},{14,10},{15,13... | collective-permute-start | bytes 307208 | tf_op jit(solution)/shard_map/ppermute | solution.py:380
  62.3 6.3 %collective-permute-start.32 = (bf16[16,3200]{1,0:T(8,128)(2,1)S(1)}, bf16[16,3200]{1,0:T(8,128)(2,1)S(1)}, u32[]{:S(2)}, u32[]{:S(2)}) collective-permute-start(bf16[16,3200]{1,0:T(8,128)(2,1)S(1)} %collective-permute-done.30.refs_6_), channel_id=1, source_target_pairs={{0,1},{1,0},{2,3},{3,2},{4,5},{5,4},{6,7},{7,6},{8,9},{9,8},{10,11... | collective-permute-start | bytes 307208 | tf_op jit(solution)/shard_map/ppermute | solution.py:371
  63.1 6.6 %collective-permute-start.35 = (bf16[16,3200]{1,0:T(8,128)(2,1)S(1)}, bf16[16,3200]{1,0:T(8,128)(2,1)S(1)}, u32[]{:S(2)}, u32[]{:S(2)}) collective-permute-start(bf16[16,3200]{1,0:T(8,128)(2,1)S(1)} %collective-permute-done.31.refs_7_), channel_id=1, source_target_pairs={{0,4},{1,3},{4,8},{5,1},{8,12},{9,5},{12,14},{13,9},{14,10},{15,13... | collective-permute-start | bytes 307208 | tf_op jit(solution)/shard_map/ppermute | solution.py:380
  64.4 5.4 %collective-permute-start.29 = (bf16[16,3200]{1,0:T(8,128)(2,1)S(1)}, bf16[16,3200]{1,0:T(8,128)(2,1)S(1)}, u32[]{:S(2)}, u32[]{:S(2)}) collective-permute-start(bf16[16,3200]{1,0:T(8,128)(2,1)S(1)} %collective-permute-done.27.refs_3_), channel_id=1, source_target_pairs={{0,1},{1,0},{2,3},{3,2},{4,5},{5,4},{6,7},{7,6},{8,9},{9,8},{10,11... | collective-permute-start | bytes 307208 | tf_op jit(solution)/shard_map/ppermute | solution.py:371
  78.2 6.1 %collective-permute-start.41 = (bf16[6,16,3200]{2,1,0:T(8,128)(2,1)S(1)}, bf16[6,16,3200]{2,1,0:T(8,128)(2,1)S(1)}, u32[]{:S(2)}, u32[]{:S(2)}) collective-permute-start(bf16[6,16,3200]{2,1,0:T(8,128)(2,1)S(1)} %get-tuple-element.60), channel_id=1, source_target_pairs={{0,1},{1,0},{2,3},{3,2},{4,5},{5,4},{6,7},{7,6},{8,9},{9,8},{10,11... | collective-permute-start | bytes 1843208 | tf_op jit(solution)/shard_map/ppermute | solution.py:371
  78.4 5.9 %collective-permute-start.46 = (bf16[16,3200]{1,0:T(8,128)(2,1)S(1)}, bf16[16,3200]{1,0:T(8,128)(2,1)S(1)}, u32[]{:S(2)}, u32[]{:S(2)}) collective-permute-start(bf16[16,3200]{1,0:T(8,128)(2,1)S(1)} %shard_map.110), channel_id=1, source_target_pairs={{0,4},{1,3},{4,8},{5,1},{8,12},{9,5},{12,14},{13,9},{14,10},{15,13... | collective-permute-start | bytes 307208 | tf_op jit(solution)/shard_map/ppermute | solution.py:380
  81.4 7.6 %collective-permute-start.42 = (bf16[16,3200]{1,0:T(8,128)(2,1)S(1)}, bf16[16,3200]{1,0:T(8,128)(2,1)S(1)}, u32[]{:S(2)}, u32[]{:S(2)}) collective-permute-start(bf16[16,3200]{1,0:T(8,128)(2,1)S(1)} %shard_map.106), channel_id=1, source_target_pairs={{0,4},{1,3},{4,8},{5,1},{8,12},{9,5},{12,14},{13,9},{14,10},{15,13... | collective-permute-start | bytes 307208 | tf_op jit(solution)/shard_map/ppermute | solution.py:380
  84.4 4.8 %collective-permute-start.47 = (bf16[16,3200]{1,0:T(8,128)(2,1)S(1)}, bf16[16,3200]{1,0:T(8,128)(2,1)S(1)}, u32[]{:S(2)}, u32[]{:S(2)}) collective-permute-start(bf16[16,3200]{1,0:T(8,128)(2,1)S(1)} %shard_map.111), channel_id=1, source_target_pairs={{0,4},{1,3},{4,8},{5,1},{8,12},{9,5},{12,14},{13,9},{14,10},{15,13... | collective-permute-start | bytes 307208 | tf_op jit(solution)/shard_map/ppermute | solution.py:380
  86.2 7.7 %collective-permute-start.44 = (bf16[16,3200]{1,0:T(8,128)(2,1)S(1)}, bf16[16,3200]{1,0:T(8,128)(2,1)S(1)}, u32[]{:S(2)}, u32[]{:S(2)}) collective-permute-start(bf16[16,3200]{1,0:T(8,128)(2,1)S(1)} %shard_map.108), channel_id=1, source_target_pairs={{0,14},{1,15},{4,10},{5,11},{8,6},{9,7},{12,2},{13,3},{14,0},{15,1... | collective-permute-start | bytes 307208 | tf_op jit(solution)/shard_map/ppermute | solution.py:380
  89.1 5.8 %collective-permute-start.43 = (bf16[16,3200]{1,0:T(8,128)(2,1)S(1)}, bf16[16,3200]{1,0:T(8,128)(2,1)S(1)}, u32[]{:S(2)}, u32[]{:S(2)}) collective-permute-start(bf16[16,3200]{1,0:T(8,128)(2,1)S(1)} %shard_map.107), channel_id=1, source_target_pairs={{0,4},{1,3},{4,8},{5,1},{8,12},{9,5},{12,14},{13,9},{14,10},{15,13... | collective-permute-start | bytes 307208 | tf_op jit(solution)/shard_map/ppermute | solution.py:380
  89.3 6.7 %collective-permute-start.48 = (bf16[16,3200]{1,0:T(8,128)(2,1)S(1)}, bf16[16,3200]{1,0:T(8,128)(2,1)S(1)}, u32[]{:S(2)}, u32[]{:S(2)}) collective-permute-start(bf16[16,3200]{1,0:T(8,128)(2,1)S(1)} %shard_map.112), channel_id=1, source_target_pairs={{0,4},{1,3},{4,8},{5,1},{8,12},{9,5},{12,14},{13,9},{14,10},{15,13... | collective-permute-start | bytes 307208 | tf_op jit(solution)/shard_map/ppermute | solution.py:380
  94.9 4.7 %collective-permute-start.45 = (bf16[16,3200]{1,0:T(8,128)(2,1)S(1)}, bf16[16,3200]{1,0:T(8,128)(2,1)S(1)}, u32[]{:S(2)}, u32[]{:S(2)}) collective-permute-start(bf16[16,3200]{1,0:T(8,128)(2,1)S(1)} %shard_map.109), channel_id=1, source_target_pairs={{0,4},{1,3},{4,8},{5,1},{8,12},{9,5},{12,14},{13,9},{14,10},{15,13... | collective-permute-start | bytes 307208 | tf_op jit(solution)/shard_map/ppermute | solution.py:380
  (22 other events, 68.9 us)

commit v14 on v13

--- a/solution.py
+++ b/solution.py
@@ -10,9 +10,10 @@
 VMEM = pl.BlockSpec(memory_space=pltpu.VMEM)
 SMEM = pl.BlockSpec(memory_space=pltpu.SMEM)
 HBM = pl.BlockSpec(memory_space=pltpu.HBM)
-PARAMS = pltpu.CompilerParams(vmem_limit_bytes=48 * 1024 * 1024)
+PARAMS = pltpu.CompilerParams(vmem_limit_bytes=16 * 1024 * 1024)
+FIRST = pltpu.CompilerParams(vmem_limit_bytes=48 * 1024 * 1024)
 HALF = 16
-GROUP = 4
+GROUP = 2
 LANES = 128
 
 
@@ -132,19 +133,23 @@
         square_ref, *refs = refs
     else:
         scale_ref, wave_ref, correction_ref, *refs = refs
-    left_hbm, right_hbm, *refs = refs
-    total, near_ref, far_ref, dot_ref, out_ref, left, right, field, left_sem, right_sem = refs
-    slots = left.shape[0]
-
-    def copies(slot):
-        return (
-            pltpu.make_async_copy(left_hbm.at[slot], left.at[slot], left_sem.at[slot]),
-            pltpu.make_async_copy(right_hbm.at[slot], right.at[slot], right_sem.at[slot]),
-        )
-
-    for slot in range(slots):
-        for copy in copies(slot):
-            copy.start()
+    left_in, right_in, *refs = refs
+    total, near_ref, far_ref, dot_ref, out_ref, field, *refs = refs
+    slots = left_in.shape[0]
+    if first:
+        left, right, left_sem, right_sem = refs
+
+        def copies(slot):
+            return (
+                pltpu.make_async_copy(left_in.at[slot], left.at[slot], left_sem.at[slot]),
+                pltpu.make_async_copy(right_in.at[slot], right.at[slot], right_sem.at[slot]),
+            )
+
+        for slot in range(slots):
+            for copy in copies(slot):
+                copy.start()
+    else:
+        left, right = left_in, right_in
 
     me = me_ref[0]
     core = me % 2
@@ -178,9 +183,10 @@
 
     def add_some(step, carry):
         some = [step * GROUP + k for k in range(GROUP)]
-        for slot in some:
-            for copy in copies(slot):
-                copy.wait()
+        if first:
+            for slot in some:
+                for copy in copies(slot):
+                    copy.wait()
 
         @pl.when(some[0] < used)
         def _():
@@ -234,17 +240,17 @@
     slots, order, width = left.shape
     sectors = shape[0]
     message = message_shape(*shape)
+    scratch = []
+    if first:
+        scratch = [pltpu.VMEM(b.shape, b.dtype) for b in (left, right)]
+        scratch += [pltpu.SemaphoreType.DMA((slots,))] * 2
     return pl.pallas_call(
         functools.partial(blocks_kernel, first, shape, entries),
-        in_specs=[SMEM, SMEM] + [VMEM] * (len(fields) + len(own)) + [HBM] * 2,
+        in_specs=[SMEM, SMEM]
+        + [VMEM] * (len(fields) + len(own))
+        + [HBM if first else VMEM] * 2,
         out_specs=[VMEM] * 5,
-        scratch_shapes=[
-            pltpu.VMEM(left.shape, left.dtype),
-            pltpu.VMEM(right.shape, right.dtype),
-            pltpu.VMEM((sectors, order, width), jnp.bfloat16),
-            pltpu.SemaphoreType.DMA((slots,)),
-            pltpu.SemaphoreType.DMA((slots,)),
-        ],
+        scratch_shapes=[pltpu.VMEM((sectors, order, width), jnp.bfloat16)] + scratch,
         out_shape=[
             jax.ShapeDtypeStruct((sectors, order, width), jnp.float32),
             jax.ShapeDtypeStruct((2, *message), jnp.bfloat16),
@@ -252,7 +258,7 @@
             jax.ShapeDtypeStruct((8, 128), jnp.float32),
             jax.ShapeDtypeStruct((8, 128), jnp.float32),
         ],
-        compiler_params=PARAMS,
+        compiler_params=FIRST if first else PARAMS,
         cost_estimate=pl.CostEstimate(
             flops=4 * slots * order * order * width,
             bytes_accessed=4 * slots * order * order,
@@ -411,9 +417,9 @@
     two = hop(chain(shape, 1, 1, me, total, dot, near))
     across = opposite(chain(shape, 6, 4, me, total, dot, far))
     for k in (2, 4):
+        one = hop(chain(shape, k, k - 2, me, total, dot, far, one))
         if k == 4:
-            one, across = lax.optimization_barrier((one, across))
-        one = hop(chain(shape, k, k - 2, me, total, dot, far, one))
+            two, across = lax.optimization_barrier((two, across))
         two = hop(chain(shape, k + 1, k - 1, me, total, dot, far, two))
     return me, total, far, dot, one, flip(two), across
 
@@ -425,8 +431,6 @@
     sectors, rows, width = shape
     entries = float(sectors * rows * lax.axis_size("term") * width)
     me = lax.axis_index("term").astype(jnp.int32).reshape(1)
-    blocks = (left_blocks, right_blocks, shape)
-
     beside = (
         lambda: jnp.concatenate([block_source, block_target, live_count]),
         lambda _: copied(wavefunction),
@@ -434,6 +438,7 @@
     )
     (_, *fields), (ints, own, square) = gather(wavefunction, beside)
     fields = [own, *fields]
+    blocks = (left_blocks, right_blocks, shape)
     total, near, far, dot, scale = apply_blocks(me, ints, fields, (square,), *blocks, True, entries)
     first_image, terms, correction, message = davidson_step(
         scale, wavefunction, diagonal, scatter(shape, me, total, near, far, dot), entries

time: 101 us -> 97 us (0.960)
  starting transfers between devices: 47.9 us -> 57.6 us
  waiting for transfers between devices: 33.9 us -> 24.6 us
  Pallas kernels: 14.7 us -> 10.1 us
    ppermute x28, waiting for transfers between devices: 28.9 us -> 19.6 us  [hop(): return lax.ppermute(value, 'term', pairs)]
    ppermute x22, starting transfers between devices: 4.83 us -> 11.8 us  [flip(): return lax.ppermute(value, 'term', [(i, i ^ 1) for i in range(16)])]
    pallas_call x2, Pallas kernels: 12.2 us -> 7.54 us  [apply_blocks(): pl.pallas_call(functools.partial(blocks_kernel, first, shape, entries), i...]
    ppermute x28, starting transfers between devices: 43 us -> 45.8 us  [hop(): return lax.ppermute(value, 'term', pairs)]
  transfers between devices with their start and end apart: 50 -> 50, of which waited for: 28 -> 30; matrix products, arithmetic and copies ran while one was open for 1% -> 1% of each run, Pallas kernels for 1% -> 1%
where the time goes in v14:
time: 97 us; the launch traced here: 96.4 us
  starting transfers between devices  57.6 us (59%)
  waiting for transfers between devices  24.6 us (25%)
  Pallas kernels  10.1 us (10%)
  local copies, waits for them, and re-layouts  1.81 us (2%)
  between operations  1.52 us (2%)
    ppermute x28, starting transfers between devices, hop(): return lax.ppermute(value, 'term', pairs)  45.8 us
    ppermute x28, waiting for transfers between devices, hop(): return lax.ppermute(value, 'term', pairs)  19.6 us
    ppermute x22, starting transfers between devices, flip(): return lax.ppermute(value, 'term', [(i, i ^ 1) for i in range(16)])  11.8 us
    pallas_call x2, Pallas kernels, apply_blocks(): pl.pallas_call(functools.partial(blocks_kernel, first, shape, entries), i...  7.54 us
    ppermute x22, waiting for transfers between devices, flip(): return lax.ppermute(value, 'term', [(i, i ^ 1) for i in range(16)])  4.97 us
  transfers between devices with their start and end apart: 50, of which 30 were waited for; matrix products, arithmetic and copies ran while one was open for 1% of the time, Pallas kernels for 1%

profile of v14, /device:TPU:0, one launch (start us, length us, event | category | flops | bytes accessed | tf_op | source)
XLA Modules:
  0.0 96.4 jit_solution(924244932803267995)
XLA Ops:
  1.1 2.6 %collective-permute-start.3 = (bf16[3,32,512]{2,1,0:T(8,128)(2,1)}, bf16[3,32,512]{2,1,0:T(8,128)(2,1)S(1)}, u32[]{:S(2)}, u32[]{:S(2)}) collective-permute-start(bf16[3,32,512]{2,1,0:T(8,128)(2,1)} %wave_ref.3), channel_id=1, source_target_pairs={{0,4},{1,3},{4,8},{5,1},{8,12},{9,5},{12,14},{13,9},{14,10},{15,13... | collective-permute-start | bytes 294920 | tf_op jit(solution)/shard_map/ppermute | solution.py:386
  4.4 1.6 %collective-permute-start.1 = (bf16[3,32,512]{2,1,0:T(8,128)(2,1)S(1)}, bf16[3,32,512]{2,1,0:T(8,128)(2,1)S(1)}, u32[]{:S(2)}, u32[]{:S(2)}) collective-permute-start(bf16[3,32,512]{2,1,0:T(8,128)(2,1)S(1)} %collective-permute-done.refs_1_), channel_id=1, source_target_pairs={{0,4},{1,3},{4,8},{5,1},{8,12},{9,5},{12,14},{13,9},{14,10},{15,13... | collective-permute-start | bytes 294920 | tf_op jit(solution)/shard_map/ppermute | solution.py:386
  6.8 1.8 %collective-permute-start.6 = (bf16[3,32,512]{2,1,0:T(8,128)(2,1)S(1)}, bf16[3,32,512]{2,1,0:T(8,128)(2,1)S(1)}, u32[]{:S(2)}, u32[]{:S(2)}) collective-permute-start(bf16[3,32,512]{2,1,0:T(8,128)(2,1)S(1)} %collective-permute-done.3.refs_2_), channel_id=1, source_target_pairs={{0,4},{1,3},{4,8},{5,1},{8,12},{9,5},{12,14},{13,9},{14,10},{15,13... | collective-permute-start | bytes 294920 | tf_op jit(solution)/shard_map/ppermute | solution.py:386
  9.1 1.6 %collective-permute-start.2 = (bf16[3,32,512]{2,1,0:T(8,128)(2,1)S(1)}, bf16[3,32,512]{2,1,0:T(8,128)(2,1)S(1)}, u32[]{:S(2)}, u32[]{:S(2)}) collective-permute-start(bf16[3,32,512]{2,1,0:T(8,128)(2,1)S(1)} %collective-permute-done.1.refs_3_), channel_id=1, source_target_pairs={{0,4},{1,3},{4,8},{5,1},{8,12},{9,5},{12,14},{13,9},{14,10},{15,13... | collective-permute-start | bytes 294920 | tf_op jit(solution)/shard_map/ppermute | solution.py:386
  11.6 2.6 %collective-permute-start.13 = (bf16[3,32,512]{2,1,0:T(8,128)(2,1)S(1)}, bf16[3,32,512]{2,1,0:T(8,128)(2,1)S(1)}, u32[]{:S(2)}, u32[]{:S(2)}) collective-permute-start(bf16[3,32,512]{2,1,0:T(8,128)(2,1)S(1)} %copy-done), channel_id=1, source_target_pairs={{0,14},{1,15},{4,10},{5,11},{8,6},{9,7},{12,2},{13,3},{14,0},{15,1... | collective-permute-start | bytes 294920 | tf_op jit(solution)/shard_map/ppermute | solution.py:386
  14.3 1.8 %collective-permute-start.7 = (bf16[3,32,512]{2,1,0:T(8,128)(2,1)S(1)}, bf16[3,32,512]{2,1,0:T(8,128)(2,1)S(1)}, u32[]{:S(2)}, u32[]{:S(2)}) collective-permute-start(bf16[3,32,512]{2,1,0:T(8,128)(2,1)S(1)} %collective-permute-done.6.refs_6_), channel_id=1, source_target_pairs={{0,1},{1,0},{2,3},{3,2},{4,5},{5,4},{6,7},{7,6},{8,9},{9,8},{10,11... | collective-permute-start | bytes 294920 | tf_op jit(solution)/shard_map/ppermute | solution.py:377
  16.5 2.6 %collective-permute-done.13.refs_14_ = bf16[3,32,512]{2,1,0:T(8,128)(2,1)S(1)} collective-permute-done((bf16[3,32,512]{2,1,0:T(8,128)(2,1)S(1)}, bf16[3,32,512]{2,1,0:T(8,128)(2,1)S(1)}, u32[]{:S(2)}, u32[]{:S(2)}) %collective-permute-start.13) | collective-permute-done | bytes 98336 | tf_op jit(solution)/shard_map/ppermute | solution.py:386
  22.3 5.2 %shard_map.96 = (f32[3,512,512]{2,1,0:T(8,128)S(1)}, bf16[2,16,3200]{2,1,0:T(8,128)(2,1)S(1)}, bf16[6,16,3200]{2,1,0:T(8,128)(2,1)S(1)}, f32[8,128]{1,0:T(8,128)S(1)}, f32[8,128]{1,0:T(8,128)S(1)}) custom-call(s32[1]{0:T(128)} %bitcast.me_ref.refs_0_.refs_2_, s32[17]{0:T(128)S(1)} %pad_add_fusion.ints_ref, ...), custom_call_target="tpu_custom_call" | custom-call | flops 4294967296 | bytes 8388608 | tf_op jit(solution)/shard_map/pallas_call | solution.py:247
  27.4 3.6 %collective-permute-start.15 = (bf16[2,16,3200]{2,1,0:T(8,128)(2,1)S(1)}, bf16[2,16,3200]{2,1,0:T(8,128)(2,1)S(1)}, u32[]{:S(2)}, u32[]{:S(2)}) collective-permute-start(bf16[2,16,3200]{2,1,0:T(8,128)(2,1)S(1)} %get-tuple-element.43), channel_id=1, source_target_pairs={{0,1},{1,0},{2,3},{3,2},{4,5},{5,4},{6,7},{7,6},{8,9},{9,8},{10,11... | collective-permute-start | bytes 614408 | tf_op jit(solution)/shard_map/ppermute | solution.py:377
  31.0 1.1 %collective-permute-done.15.other_ref = bf16[2,16,3200]{2,1,0:T(8,128)(2,1)S(1)} collective-permute-done((bf16[2,16,3200]{2,1,0:T(8,128)(2,1)S(1)}, bf16[2,16,3200]{2,1,0:T(8,128)(2,1)S(1)}, u32[]{:S(2)}, u32[]{:S(2)}) %collective-permute-start.15) | collective-permute-done | bytes 204832 | tf_op jit(solution)/shard_map/ppermute | solution.py:377
  34.2 2.5 %collective-permute-start.22 = (bf16[16,3200]{1,0:T(8,128)(2,1)S(1)}, bf16[16,3200]{1,0:T(8,128)(2,1)S(1)}, u32[]{:S(2)}, u32[]{:S(2)}) collective-permute-start(bf16[16,3200]{1,0:T(8,128)(2,1)S(1)} %shard_map.102), channel_id=1, source_target_pairs={{0,14},{1,15},{4,10},{5,11},{8,6},{9,7},{12,2},{13,3},{14,0},{15,1... | collective-permute-start | bytes 307208 | tf_op jit(solution)/shard_map/ppermute | solution.py:386
  38.4 2.9 %collective-permute-start.18 = (bf16[16,3200]{1,0:T(8,128)(2,1)S(1)}, bf16[16,3200]{1,0:T(8,128)(2,1)S(1)}, u32[]{:S(2)}, u32[]{:S(2)}) collective-permute-start(bf16[16,3200]{1,0:T(8,128)(2,1)S(1)} %shard_map.98), channel_id=1, source_target_pairs={{0,4},{1,3},{4,8},{5,1},{8,12},{9,5},{12,14},{13,9},{14,10},{15,13... | collective-permute-start | bytes 307208 | tf_op jit(solution)/shard_map/ppermute | solution.py:386
  44.4 2.1 %collective-permute-start.19 = (bf16[16,3200]{1,0:T(8,128)(2,1)S(1)}, bf16[16,3200]{1,0:T(8,128)(2,1)S(1)}, u32[]{:S(2)}, u32[]{:S(2)}) collective-permute-start(bf16[16,3200]{1,0:T(8,128)(2,1)S(1)} %shard_map.99), channel_id=1, source_target_pairs={{0,4},{1,3},{4,8},{5,1},{8,12},{9,5},{12,14},{13,9},{14,10},{15,13... | collective-permute-start | bytes 307208 | tf_op jit(solution)/shard_map/ppermute | solution.py:386
  46.6 1.5 %collective-permute-done.23 = bf16[16,3200]{1,0:T(8,128)(2,1)S(1)} collective-permute-done((bf16[16,3200]{1,0:T(8,128)(2,1)S(1)}, bf16[16,3200]{1,0:T(8,128)(2,1)S(1)}, u32[]{:S(2)}, u32[]{:S(2)}) %collective-permute-start.23) | collective-permute-done | bytes 102432 | tf_op jit(solution)/shard_map/ppermute | solution.py:386
  48.1 1.1 %collective-permute-done.19.refs_4_ = bf16[16,3200]{1,0:T(8,128)(2,1)S(1)} collective-permute-done((bf16[16,3200]{1,0:T(8,128)(2,1)S(1)}, bf16[16,3200]{1,0:T(8,128)(2,1)S(1)}, u32[]{:S(2)}, u32[]{:S(2)}) %collective-permute-start.19) | collective-permute-done | bytes 102432 | tf_op jit(solution)/shard_map/ppermute | solution.py:386
  50.4 1.7 %collective-permute-start.26 = (bf16[16,3200]{1,0:T(8,128)(2,1)S(1)}, bf16[16,3200]{1,0:T(8,128)(2,1)S(1)}, u32[]{:S(2)}, u32[]{:S(2)}) collective-permute-start(bf16[16,3200]{1,0:T(8,128)(2,1)S(1)} %get-tuple-element.53.refs_0_), channel_id=1, source_target_pairs={{0,4},{1,3},{4,8},{5,1},{8,12},{9,5},{12,14},{13,9},{14,10},{15,13... | collective-permute-start | bytes 307208 | tf_op jit(solution)/shard_map/ppermute | solution.py:386
  52.2 2.1 %collective-permute-start.27 = (bf16[16,3200]{1,0:T(8,128)(2,1)S(1)}, bf16[16,3200]{1,0:T(8,128)(2,1)S(1)}, u32[]{:S(2)}, u32[]{:S(2)}) collective-permute-start(bf16[16,3200]{1,0:T(8,128)(2,1)S(1)} %collective-permute-done.25.refs_1_), channel_id=1, source_target_pairs={{0,4},{1,3},{4,8},{5,1},{8,12},{9,5},{12,14},{13,9},{14,10},{15,13... | collective-permute-start | bytes 307208 | tf_op jit(solution)/shard_map/ppermute | solution.py:386
  55.1 1.7 %collective-permute-start.30 = (bf16[16,3200]{1,0:T(8,128)(2,1)S(1)}, bf16[16,3200]{1,0:T(8,128)(2,1)S(1)}, u32[]{:S(2)}, u32[]{:S(2)}) collective-permute-start(bf16[16,3200]{1,0:T(8,128)(2,1)S(1)} %collective-permute-done.26.refs_2_), channel_id=1, source_target_pairs={{0,4},{1,3},{4,8},{5,1},{8,12},{9,5},{12,14},{13,9},{14,10},{15,13... | collective-permute-start | bytes 307208 | tf_op jit(solution)/shard_map/ppermute | solution.py:386
  56.8 2.1 %collective-permute-start.31 = (bf16[16,3200]{1,0:T(8,128)(2,1)S(1)}, bf16[16,3200]{1,0:T(8,128)(2,1)S(1)}, u32[]{:S(2)}, u32[]{:S(2)}) collective-permute-start(bf16[16,3200]{1,0:T(8,128)(2,1)S(1)} %collective-permute-done.27.refs_3_), channel_id=1, source_target_pairs={{0,4},{1,3},{4,8},{5,1},{8,12},{9,5},{12,14},{13,9},{14,10},{15,13... | collective-permute-start | bytes 307208 | tf_op jit(solution)/shard_map/ppermute | solution.py:386
  58.9 1.5 %collective-permute-start.38 = (bf16[16,3200]{1,0:T(8,128)(2,1)S(1)}, bf16[16,3200]{1,0:T(8,128)(2,1)S(1)}, u32[]{:S(2)}, u32[]{:S(2)}) collective-permute-start(bf16[16,3200]{1,0:T(8,128)(2,1)S(1)} %get-tuple-element.53.refs_0_), channel_id=1, source_target_pairs={{0,14},{1,15},{4,10},{5,11},{8,6},{9,7},{12,2},{13,3},{14,0},{15,1... | collective-permute-start | bytes 307208 | tf_op jit(solution)/shard_map/ppermute | solution.py:386
  61.7 3.9 %collective-permute-start.35 = (bf16[16,3200]{1,0:T(8,128)(2,1)S(1)}, bf16[16,3200]{1,0:T(8,128)(2,1)S(1)}, u32[]{:S(2)}, u32[]{:S(2)}) collective-permute-start(bf16[16,3200]{1,0:T(8,128)(2,1)S(1)} %collective-permute-done.31.refs_7_), channel_id=1, source_target_pairs={{0,4},{1,3},{4,8},{5,1},{8,12},{9,5},{12,14},{13,9},{14,10},{15,13... | collective-permute-start | bytes 307208 | tf_op jit(solution)/shard_map/ppermute | solution.py:386
  65.5 1.7 %collective-permute-done.38.refs_14_ = bf16[16,3200]{1,0:T(8,128)(2,1)S(1)} collective-permute-done((bf16[16,3200]{1,0:T(8,128)(2,1)S(1)}, bf16[16,3200]{1,0:T(8,128)(2,1)S(1)}, u32[]{:S(2)}, u32[]{:S(2)}) %collective-permute-start.38) | collective-permute-done | bytes 102432 | tf_op jit(solution)/shard_map/ppermute | solution.py:386
  69.7 2.4 %shard_map.105 = (f32[3,512,512]{2,1,0:T(8,128)S(1)}, bf16[2,16,3200]{2,1,0:T(8,128)(2,1)S(1)}, bf16[6,16,3200]{2,1,0:T(8,128)(2,1)S(1)}, f32[8,128]{1,0:T(8,128)S(1)}, f32[8,128]{1,0:T(8,128)S(1)}) custom-call(s32[1]{0:T(128)} %bitcast.me_ref.refs_0_.refs_2_, s32[17]{0:T(128)S(1)} %pad_add_fusion.ints_ref, bf16[16,3200]{1,0:T(8,128)(2,1)S(1)} %get-tuple-element.53.refs_0_, ...), custom_call_target="tpu_custom_call" | custom-call | flops 4294967296 | bytes 8388608 | tf_op jit(solution)/shard_map/pallas_call | solution.py:247
  72.1 4.0 %collective-permute-start.40 = (bf16[2,16,3200]{2,1,0:T(8,128)(2,1)S(1)}, bf16[2,16,3200]{2,1,0:T(8,128)(2,1)S(1)}, u32[]{:S(2)}, u32[]{:S(2)}) collective-permute-start(bf16[2,16,3200]{2,1,0:T(8,128)(2,1)S(1)} %get-tuple-element.58), channel_id=1, source_target_pairs={{0,1},{1,0},{2,3},{3,2},{4,5},{5,4},{6,7},{7,6},{8,9},{9,8},{10,11... | collective-permute-start | bytes 614408 | tf_op jit(solution)/shard_map/ppermute | solution.py:377
  76.0 1.1 %collective-permute-done.40.other_ref = bf16[2,16,3200]{2,1,0:T(8,128)(2,1)S(1)} collective-permute-done((bf16[2,16,3200]{2,1,0:T(8,128)(2,1)S(1)}, bf16[2,16,3200]{2,1,0:T(8,128)(2,1)S(1)}, u32[]{:S(2)}, u32[]{:S(2)}) %collective-permute-start.40) | collective-permute-done | bytes 204832 | tf_op jit(solution)/shard_map/ppermute | solution.py:377
  77.5 2.0 %collective-permute-start.45 = (bf16[16,3200]{1,0:T(8,128)(2,1)S(1)}, bf16[16,3200]{1,0:T(8,128)(2,1)S(1)}, u32[]{:S(2)}, u32[]{:S(2)}) collective-permute-start(bf16[16,3200]{1,0:T(8,128)(2,1)S(1)} %shard_map.109), channel_id=1, source_target_pairs={{0,4},{1,3},{4,8},{5,1},{8,12},{9,5},{12,14},{13,9},{14,10},{15,13... | collective-permute-start | bytes 307208 | tf_op jit(solution)/shard_map/ppermute | solution.py:386
  79.7 3.5 %collective-permute-start.47 = (bf16[16,3200]{1,0:T(8,128)(2,1)S(1)}, bf16[16,3200]{1,0:T(8,128)(2,1)S(1)}, u32[]{:S(2)}, u32[]{:S(2)}) collective-permute-start(bf16[16,3200]{1,0:T(8,128)(2,1)S(1)} %shard_map.111), channel_id=1, source_target_pairs={{0,14},{1,15},{4,10},{5,11},{8,6},{9,7},{12,2},{13,3},{14,0},{15,1... | collective-permute-start | bytes 307208 | tf_op jit(solution)/shard_map/ppermute | solution.py:386
  84.4 1.7 %collective-permute-start.43 = (bf16[16,3200]{1,0:T(8,128)(2,1)S(1)}, bf16[16,3200]{1,0:T(8,128)(2,1)S(1)}, u32[]{:S(2)}, u32[]{:S(2)}) collective-permute-start(bf16[16,3200]{1,0:T(8,128)(2,1)S(1)} %shard_map.107), channel_id=1, source_target_pairs={{0,4},{1,3},{4,8},{5,1},{8,12},{9,5},{12,14},{13,9},{14,10},{15,13... | collective-permute-start | bytes 307208 | tf_op jit(solution)/shard_map/ppermute | solution.py:386
  86.0 2.4 %collective-permute-done.47.refs_8_ = bf16[16,3200]{1,0:T(8,128)(2,1)S(1)} collective-permute-done((bf16[16,3200]{1,0:T(8,128)(2,1)S(1)}, bf16[16,3200]{1,0:T(8,128)(2,1)S(1)}, u32[]{:S(2)}, u32[]{:S(2)}) %collective-permute-start.47) | collective-permute-done | bytes 102432 | tf_op jit(solution)/shard_map/ppermute | solution.py:386
  90.5 1.9 %collective-permute-start.44 = (bf16[16,3200]{1,0:T(8,128)(2,1)S(1)}, bf16[16,3200]{1,0:T(8,128)(2,1)S(1)}, u32[]{:S(2)}, u32[]{:S(2)}) collective-permute-start(bf16[16,3200]{1,0:T(8,128)(2,1)S(1)} %shard_map.108), channel_id=1, source_target_pairs={{0,4},{1,3},{4,8},{5,1},{8,12},{9,5},{12,14},{13,9},{14,10},{15,13... | collective-permute-start | bytes 307208 | tf_op jit(solution)/shard_map/ppermute | solution.py:386
  92.4 1.7 %collective-permute-done.48 = bf16[16,3200]{1,0:T(8,128)(2,1)S(1)} collective-permute-done((bf16[16,3200]{1,0:T(8,128)(2,1)S(1)}, bf16[16,3200]{1,0:T(8,128)(2,1)S(1)}, u32[]{:S(2)}, u32[]{:S(2)}) %collective-permute-start.48) | collective-permute-done | bytes 102432 | tf_op jit(solution)/shard_map/ppermute | solution.py:386
  94.1 1.1 %collective-permute-done.44.refs_6_ = bf16[16,3200]{1,0:T(8,128)(2,1)S(1)} collective-permute-done((bf16[16,3200]{1,0:T(8,128)(2,1)S(1)}, bf16[16,3200]{1,0:T(8,128)(2,1)S(1)}, u32[]{:S(2)}, u32[]{:S(2)}) %collective-permute-start.44) | collective-permute-done | bytes 102432 | tf_op jit(solution)/shard_map/ppermute | solution.py:386
  (101 shorter events, 23.8 us)
Async XLA Ops:
  1.1 5.7 %collective-permute-start.3 = (bf16[3,32,512]{2,1,0:T(8,128)(2,1)}, bf16[3,32,512]{2,1,0:T(8,128)(2,1)S(1)}, u32[]{:S(2)}, u32[]{:S(2)}) collective-permute-start(bf16[3,32,512]{2,1,0:T(8,128)(2,1)} %wave_ref.3), channel_id=1, source_target_pairs={{0,4},{1,3},{4,8},{5,1},{8,12},{9,5},{12,14},{13,9},{14,10},{15,13... | collective-permute-start | bytes 294920 | tf_op jit(solution)/shard_map/ppermute | solution.py:386
  4.4 4.7 %collective-permute-start.1 = (bf16[3,32,512]{2,1,0:T(8,128)(2,1)S(1)}, bf16[3,32,512]{2,1,0:T(8,128)(2,1)S(1)}, u32[]{:S(2)}, u32[]{:S(2)}) collective-permute-start(bf16[3,32,512]{2,1,0:T(8,128)(2,1)S(1)} %collective-permute-done.refs_1_), channel_id=1, source_target_pairs={{0,4},{1,3},{4,8},{5,1},{8,12},{9,5},{12,14},{13,9},{14,10},{15,13... | collective-permute-start | bytes 294920 | tf_op jit(solution)/shard_map/ppermute | solution.py:386
  6.8 7.4 %collective-permute-start.6 = (bf16[3,32,512]{2,1,0:T(8,128)(2,1)S(1)}, bf16[3,32,512]{2,1,0:T(8,128)(2,1)S(1)}, u32[]{:S(2)}, u32[]{:S(2)}) collective-permute-start(bf16[3,32,512]{2,1,0:T(8,128)(2,1)S(1)} %collective-permute-done.3.refs_2_), channel_id=1, source_target_pairs={{0,4},{1,3},{4,8},{5,1},{8,12},{9,5},{12,14},{13,9},{14,10},{15,13... | collective-permute-start | bytes 294920 | tf_op jit(solution)/shard_map/ppermute | solution.py:386
  9.1 6.9 %collective-permute-start.2 = (bf16[3,32,512]{2,1,0:T(8,128)(2,1)S(1)}, bf16[3,32,512]{2,1,0:T(8,128)(2,1)S(1)}, u32[]{:S(2)}, u32[]{:S(2)}) collective-permute-start(bf16[3,32,512]{2,1,0:T(8,128)(2,1)S(1)} %collective-permute-done.1.refs_3_), channel_id=1, source_target_pairs={{0,4},{1,3},{4,8},{5,1},{8,12},{9,5},{12,14},{13,9},{14,10},{15,13... | collective-permute-start | bytes 294920 | tf_op jit(solution)/shard_map/ppermute | solution.py:386
  11.6 7.5 %collective-permute-start.13 = (bf16[3,32,512]{2,1,0:T(8,128)(2,1)S(1)}, bf16[3,32,512]{2,1,0:T(8,128)(2,1)S(1)}, u32[]{:S(2)}, u32[]{:S(2)}) collective-permute-start(bf16[3,32,512]{2,1,0:T(8,128)(2,1)S(1)} %copy-done), channel_id=1, source_target_pairs={{0,14},{1,15},{4,10},{5,11},{8,6},{9,7},{12,2},{13,3},{14,0},{15,1... | collective-permute-start | bytes 294920 | tf_op jit(solution)/shard_map/ppermute | solution.py:386
  14.2 5.7 %collective-permute-start.9 = (bf16[3,32,512]{2,1,0:T(8,128)(2,1)S(1)}, bf16[3,32,512]{2,1,0:T(8,128)(2,1)S(1)}, u32[]{:S(2)}, u32[]{:S(2)}) collective-permute-start(bf16[3,32,512]{2,1,0:T(8,128)(2,1)S(1)} %collective-permute-done.6.refs_6_), channel_id=1, source_target_pairs={{0,4},{1,3},{4,8},{5,1},{8,12},{9,5},{12,14},{13,9},{14,10},{15,13... | collective-permute-start | bytes 294920 | tf_op jit(solution)/shard_map/ppermute | solution.py:386
  14.3 5.7 %collective-permute-start.7 = (bf16[3,32,512]{2,1,0:T(8,128)(2,1)S(1)}, bf16[3,32,512]{2,1,0:T(8,128)(2,1)S(1)}, u32[]{:S(2)}, u32[]{:S(2)}) collective-permute-start(bf16[3,32,512]{2,1,0:T(8,128)(2,1)S(1)} %collective-permute-done.6.refs_6_), channel_id=1, source_target_pairs={{0,1},{1,0},{2,3},{3,2},{4,5},{5,4},{6,7},{7,6},{8,9},{9,8},{10,11... | collective-permute-start | bytes 294920 | tf_op jit(solution)/shard_map/ppermute | solution.py:377
  16.1 4.9 %collective-permute-start.10 = (bf16[3,32,512]{2,1,0:T(8,128)(2,1)S(1)}, bf16[3,32,512]{2,1,0:T(8,128)(2,1)S(1)}, u32[]{:S(2)}, u32[]{:S(2)}) collective-permute-start(bf16[3,32,512]{2,1,0:T(8,128)(2,1)S(1)} %collective-permute-done.2.refs_7_), channel_id=1, source_target_pairs={{0,4},{1,3},{4,8},{5,1},{8,12},{9,5},{12,14},{13,9},{14,10},{15,13... | collective-permute-start | bytes 294920 | tf_op jit(solution)/shard_map/ppermute | solution.py:386
  16.5 5.4 %collective-permute-start.5 = (bf16[3,32,512]{2,1,0:T(8,128)(2,1)S(1)}, bf16[3,32,512]{2,1,0:T(8,128)(2,1)S(1)}, u32[]{:S(2)}, u32[]{:S(2)}) collective-permute-start(bf16[3,32,512]{2,1,0:T(8,128)(2,1)S(1)} %collective-permute-done.1.refs_3_), channel_id=1, source_target_pairs={{0,1},{1,0},{2,3},{3,2},{4,5},{5,4},{6,7},{7,6},{8,9},{9,8},{10,11... | collective-permute-start | bytes 294920 | tf_op jit(solution)/shard_map/ppermute | solution.py:377
  32.5 4.7 %collective-permute-start.20 = (bf16[16,3200]{1,0:T(8,128)(2,1)S(1)}, bf16[16,3200]{1,0:T(8,128)(2,1)S(1)}, u32[]{:S(2)}, u32[]{:S(2)}) collective-permute-start(bf16[16,3200]{1,0:T(8,128)(2,1)S(1)} %shard_map.100), channel_id=1, source_target_pairs={{0,4},{1,3},{4,8},{5,1},{8,12},{9,5},{12,14},{13,9},{14,10},{15,13... | collective-permute-start | bytes 307208 | tf_op jit(solution)/shard_map/ppermute | solution.py:386
  33.3 5.0 %collective-permute-start.17 = (bf16[16,3200]{1,0:T(8,128)(2,1)S(1)}, bf16[16,3200]{1,0:T(8,128)(2,1)S(1)}, u32[]{:S(2)}, u32[]{:S(2)}) collective-permute-start(bf16[16,3200]{1,0:T(8,128)(2,1)S(1)} %shard_map.97), channel_id=1, source_target_pairs={{0,4},{1,3},{4,8},{5,1},{8,12},{9,5},{12,14},{13,9},{14,10},{15,13... | collective-permute-start | bytes 307208 | tf_op jit(solution)/shard_map/ppermute | solution.py:386
  34.2 8.2 %collective-permute-start.22 = (bf16[16,3200]{1,0:T(8,128)(2,1)S(1)}, bf16[16,3200]{1,0:T(8,128)(2,1)S(1)}, u32[]{:S(2)}, u32[]{:S(2)}) collective-permute-start(bf16[16,3200]{1,0:T(8,128)(2,1)S(1)} %shard_map.102), channel_id=1, source_target_pairs={{0,14},{1,15},{4,10},{5,11},{8,6},{9,7},{12,2},{13,3},{14,0},{15,1... | collective-permute-start | bytes 307208 | tf_op jit(solution)/shard_map/ppermute | solution.py:386
  37.3 6.0 %collective-permute-start.21 = (bf16[16,3200]{1,0:T(8,128)(2,1)S(1)}, bf16[16,3200]{1,0:T(8,128)(2,1)S(1)}, u32[]{:S(2)}, u32[]{:S(2)}) collective-permute-start(bf16[16,3200]{1,0:T(8,128)(2,1)S(1)} %shard_map.101), channel_id=1, source_target_pairs={{0,4},{1,3},{4,8},{5,1},{8,12},{9,5},{12,14},{13,9},{14,10},{15,13... | collective-permute-start | bytes 307208 | tf_op jit(solution)/shard_map/ppermute | solution.py:386
  38.4 6.0 %collective-permute-start.18 = (bf16[16,3200]{1,0:T(8,128)(2,1)S(1)}, bf16[16,3200]{1,0:T(8,128)(2,1)S(1)}, u32[]{:S(2)}, u32[]{:S(2)}) collective-permute-start(bf16[16,3200]{1,0:T(8,128)(2,1)S(1)} %shard_map.98), channel_id=1, source_target_pairs={{0,4},{1,3},{4,8},{5,1},{8,12},{9,5},{12,14},{13,9},{14,10},{15,13... | collective-permute-start | bytes 307208 | tf_op jit(solution)/shard_map/ppermute | solution.py:386
  43.4 4.7 %collective-permute-start.23 = (bf16[16,3200]{1,0:T(8,128)(2,1)S(1)}, bf16[16,3200]{1,0:T(8,128)(2,1)S(1)}, u32[]{:S(2)}, u32[]{:S(2)}) collective-permute-start(bf16[16,3200]{1,0:T(8,128)(2,1)S(1)} %shard_map.103), channel_id=1, source_target_pairs={{0,4},{1,3},{4,8},{5,1},{8,12},{9,5},{12,14},{13,9},{14,10},{15,13... | collective-permute-start | bytes 307208 | tf_op jit(solution)/shard_map/ppermute | solution.py:386
  44.4 4.7 %collective-permute-start.19 = (bf16[16,3200]{1,0:T(8,128)(2,1)S(1)}, bf16[16,3200]{1,0:T(8,128)(2,1)S(1)}, u32[]{:S(2)}, u32[]{:S(2)}) collective-permute-start(bf16[16,3200]{1,0:T(8,128)(2,1)S(1)} %shard_map.99), channel_id=1, source_target_pairs={{0,4},{1,3},{4,8},{5,1},{8,12},{9,5},{12,14},{13,9},{14,10},{15,13... | collective-permute-start | bytes 307208 | tf_op jit(solution)/shard_map/ppermute | solution.py:386
  52.2 4.7 %collective-permute-start.27 = (bf16[16,3200]{1,0:T(8,128)(2,1)S(1)}, bf16[16,3200]{1,0:T(8,128)(2,1)S(1)}, u32[]{:S(2)}, u32[]{:S(2)}) collective-permute-start(bf16[16,3200]{1,0:T(8,128)(2,1)S(1)} %collective-permute-done.25.refs_1_), channel_id=1, source_target_pairs={{0,4},{1,3},{4,8},{5,1},{8,12},{9,5},{12,14},{13,9},{14,10},{15,13... | collective-permute-start | bytes 307208 | tf_op jit(solution)/shard_map/ppermute | solution.py:386
  55.1 5.3 %collective-permute-start.30 = (bf16[16,3200]{1,0:T(8,128)(2,1)S(1)}, bf16[16,3200]{1,0:T(8,128)(2,1)S(1)}, u32[]{:S(2)}, u32[]{:S(2)}) collective-permute-start(bf16[16,3200]{1,0:T(8,128)(2,1)S(1)} %collective-permute-done.26.refs_2_), channel_id=1, source_target_pairs={{0,4},{1,3},{4,8},{5,1},{8,12},{9,5},{12,14},{13,9},{14,10},{15,13... | collective-permute-start | bytes 307208 | tf_op jit(solution)/shard_map/ppermute | solution.py:386
  56.8 4.9 %collective-permute-start.31 = (bf16[16,3200]{1,0:T(8,128)(2,1)S(1)}, bf16[16,3200]{1,0:T(8,128)(2,1)S(1)}, u32[]{:S(2)}, u32[]{:S(2)}) collective-permute-start(bf16[16,3200]{1,0:T(8,128)(2,1)S(1)} %collective-permute-done.27.refs_3_), channel_id=1, source_target_pairs={{0,4},{1,3},{4,8},{5,1},{8,12},{9,5},{12,14},{13,9},{14,10},{15,13... | collective-permute-start | bytes 307208 | tf_op jit(solution)/shard_map/ppermute | solution.py:386
  58.9 6.6 %collective-permute-start.28 = (bf16[16,3200]{1,0:T(8,128)(2,1)S(1)}, bf16[16,3200]{1,0:T(8,128)(2,1)S(1)}, u32[]{:S(2)}, u32[]{:S(2)}) collective-permute-start(bf16[16,3200]{1,0:T(8,128)(2,1)S(1)} %collective-permute-done.26.refs_2_), channel_id=1, source_target_pairs={{0,1},{1,0},{2,3},{3,2},{4,5},{5,4},{6,7},{7,6},{8,9},{9,8},{10,11... | collective-permute-start | bytes 307208 | tf_op jit(solution)/shard_map/ppermute | solution.py:377
  58.9 8.3 %collective-permute-start.38 = (bf16[16,3200]{1,0:T(8,128)(2,1)S(1)}, bf16[16,3200]{1,0:T(8,128)(2,1)S(1)}, u32[]{:S(2)}, u32[]{:S(2)}) collective-permute-start(bf16[16,3200]{1,0:T(8,128)(2,1)S(1)} %get-tuple-element.53.refs_0_), channel_id=1, source_target_pairs={{0,14},{1,15},{4,10},{5,11},{8,6},{9,7},{12,2},{13,3},{14,0},{15,1... | collective-permute-start | bytes 307208 | tf_op jit(solution)/shard_map/ppermute | solution.py:386
  60.4 6.9 %collective-permute-start.34 = (bf16[16,3200]{1,0:T(8,128)(2,1)S(1)}, bf16[16,3200]{1,0:T(8,128)(2,1)S(1)}, u32[]{:S(2)}, u32[]{:S(2)}) collective-permute-start(bf16[16,3200]{1,0:T(8,128)(2,1)S(1)} %collective-permute-done.30.refs_6_), channel_id=1, source_target_pairs={{0,4},{1,3},{4,8},{5,1},{8,12},{9,5},{12,14},{13,9},{14,10},{15,13... | collective-permute-start | bytes 307208 | tf_op jit(solution)/shard_map/ppermute | solution.py:386
  61.5 6.3 %collective-permute-start.32 = (bf16[16,3200]{1,0:T(8,128)(2,1)S(1)}, bf16[16,3200]{1,0:T(8,128)(2,1)S(1)}, u32[]{:S(2)}, u32[]{:S(2)}) collective-permute-start(bf16[16,3200]{1,0:T(8,128)(2,1)S(1)} %collective-permute-done.30.refs_6_), channel_id=1, source_target_pairs={{0,1},{1,0},{2,3},{3,2},{4,5},{5,4},{6,7},{7,6},{8,9},{9,8},{10,11... | collective-permute-start | bytes 307208 | tf_op jit(solution)/shard_map/ppermute | solution.py:377
  61.7 6.7 %collective-permute-start.35 = (bf16[16,3200]{1,0:T(8,128)(2,1)S(1)}, bf16[16,3200]{1,0:T(8,128)(2,1)S(1)}, u32[]{:S(2)}, u32[]{:S(2)}) collective-permute-start(bf16[16,3200]{1,0:T(8,128)(2,1)S(1)} %collective-permute-done.31.refs_7_), channel_id=1, source_target_pairs={{0,4},{1,3},{4,8},{5,1},{8,12},{9,5},{12,14},{13,9},{14,10},{15,13... | collective-permute-start | bytes 307208 | tf_op jit(solution)/shard_map/ppermute | solution.py:386
  72.1 5.1 %collective-permute-start.40 = (bf16[2,16,3200]{2,1,0:T(8,128)(2,1)S(1)}, bf16[2,16,3200]{2,1,0:T(8,128)(2,1)S(1)}, u32[]{:S(2)}, u32[]{:S(2)}) collective-permute-start(bf16[2,16,3200]{2,1,0:T(8,128)(2,1)S(1)} %get-tuple-element.58), channel_id=1, source_target_pairs={{0,1},{1,0},{2,3},{3,2},{4,5},{5,4},{6,7},{7,6},{8,9},{9,8},{10,11... | collective-permute-start | bytes 614408 | tf_op jit(solution)/shard_map/ppermute | solution.py:377
  77.5 5.7 %collective-permute-start.45 = (bf16[16,3200]{1,0:T(8,128)(2,1)S(1)}, bf16[16,3200]{1,0:T(8,128)(2,1)S(1)}, u32[]{:S(2)}, u32[]{:S(2)}) collective-permute-start(bf16[16,3200]{1,0:T(8,128)(2,1)S(1)} %shard_map.109), channel_id=1, source_target_pairs={{0,4},{1,3},{4,8},{5,1},{8,12},{9,5},{12,14},{13,9},{14,10},{15,13... | collective-permute-start | bytes 307208 | tf_op jit(solution)/shard_map/ppermute | solution.py:386
  79.6 4.7 %collective-permute-start.42 = (bf16[16,3200]{1,0:T(8,128)(2,1)S(1)}, bf16[16,3200]{1,0:T(8,128)(2,1)S(1)}, u32[]{:S(2)}, u32[]{:S(2)}) collective-permute-start(bf16[16,3200]{1,0:T(8,128)(2,1)S(1)} %shard_map.106), channel_id=1, source_target_pairs={{0,4},{1,3},{4,8},{5,1},{8,12},{9,5},{12,14},{13,9},{14,10},{15,13... | collective-permute-start | bytes 307208 | tf_op jit(solution)/shard_map/ppermute | solution.py:386
  79.7 8.7 %collective-permute-start.47 = (bf16[16,3200]{1,0:T(8,128)(2,1)S(1)}, bf16[16,3200]{1,0:T(8,128)(2,1)S(1)}, u32[]{:S(2)}, u32[]{:S(2)}) collective-permute-start(bf16[16,3200]{1,0:T(8,128)(2,1)S(1)} %shard_map.111), channel_id=1, source_target_pairs={{0,14},{1,15},{4,10},{5,11},{8,6},{9,7},{12,2},{13,3},{14,0},{15,1... | collective-permute-start | bytes 307208 | tf_op jit(solution)/shard_map/ppermute | solution.py:386
  83.3 6.1 %collective-permute-start.46 = (bf16[16,3200]{1,0:T(8,128)(2,1)S(1)}, bf16[16,3200]{1,0:T(8,128)(2,1)S(1)}, u32[]{:S(2)}, u32[]{:S(2)}) collective-permute-start(bf16[16,3200]{1,0:T(8,128)(2,1)S(1)} %shard_map.110), channel_id=1, source_target_pairs={{0,4},{1,3},{4,8},{5,1},{8,12},{9,5},{12,14},{13,9},{14,10},{15,13... | collective-permute-start | bytes 307208 | tf_op jit(solution)/shard_map/ppermute | solution.py:386
  84.4 6.1 %collective-permute-start.43 = (bf16[16,3200]{1,0:T(8,128)(2,1)S(1)}, bf16[16,3200]{1,0:T(8,128)(2,1)S(1)}, u32[]{:S(2)}, u32[]{:S(2)}) collective-permute-start(bf16[16,3200]{1,0:T(8,128)(2,1)S(1)} %shard_map.107), channel_id=1, source_target_pairs={{0,4},{1,3},{4,8},{5,1},{8,12},{9,5},{12,14},{13,9},{14,10},{15,13... | collective-permute-start | bytes 307208 | tf_op jit(solution)/shard_map/ppermute | solution.py:386
  89.4 4.7 %collective-permute-start.48 = (bf16[16,3200]{1,0:T(8,128)(2,1)S(1)}, bf16[16,3200]{1,0:T(8,128)(2,1)S(1)}, u32[]{:S(2)}, u32[]{:S(2)}) collective-permute-start(bf16[16,3200]{1,0:T(8,128)(2,1)S(1)} %shard_map.112), channel_id=1, source_target_pairs={{0,4},{1,3},{4,8},{5,1},{8,12},{9,5},{12,14},{13,9},{14,10},{15,13... | collective-permute-start | bytes 307208 | tf_op jit(solution)/shard_map/ppermute | solution.py:386
  90.5 4.7 %collective-permute-start.44 = (bf16[16,3200]{1,0:T(8,128)(2,1)S(1)}, bf16[16,3200]{1,0:T(8,128)(2,1)S(1)}, u32[]{:S(2)}, u32[]{:S(2)}) collective-permute-start(bf16[16,3200]{1,0:T(8,128)(2,1)S(1)} %shard_map.108), channel_id=1, source_target_pairs={{0,4},{1,3},{4,8},{5,1},{8,12},{9,5},{12,14},{13,9},{14,10},{15,13... | collective-permute-start | bytes 307208 | tf_op jit(solution)/shard_map/ppermute | solution.py:386
  (24 other events, 117.7 us)

commit v15 on v14

--- a/solution.py
+++ b/solution.py
@@ -11,7 +11,6 @@
 SMEM = pl.BlockSpec(memory_space=pltpu.SMEM)
 HBM = pl.BlockSpec(memory_space=pltpu.HBM)
 PARAMS = pltpu.CompilerParams(vmem_limit_bytes=16 * 1024 * 1024)
-FIRST = pltpu.CompilerParams(vmem_limit_bytes=48 * 1024 * 1024)
 HALF = 16
 GROUP = 2
 LANES = 128
@@ -98,13 +97,14 @@
     out_ref[...] = in_ref[...]
 
 
-def copied(value):
+def copied(value, cost=8 << 30):
     return pl.pallas_call(
         copy_kernel,
         in_specs=[VMEM],
         out_specs=VMEM,
         out_shape=jax.ShapeDtypeStruct(value.shape, value.dtype),
         compiler_params=PARAMS,
+        cost_estimate=pl.CostEstimate(flops=cost, bytes_accessed=1 << 20, transcendentals=0),
     )(value)
 
 
@@ -136,20 +136,7 @@
     left_in, right_in, *refs = refs
     total, near_ref, far_ref, dot_ref, out_ref, field, *refs = refs
     slots = left_in.shape[0]
-    if first:
-        left, right, left_sem, right_sem = refs
-
-        def copies(slot):
-            return (
-                pltpu.make_async_copy(left_in.at[slot], left.at[slot], left_sem.at[slot]),
-                pltpu.make_async_copy(right_in.at[slot], right.at[slot], right_sem.at[slot]),
-            )
-
-        for slot in range(slots):
-            for copy in copies(slot):
-                copy.start()
-    else:
-        left, right = left_in, right_in
+    left, right = left_in, right_in
 
     me = me_ref[0]
     core = me % 2
@@ -183,11 +170,6 @@
 
     def add_some(step, carry):
         some = [step * GROUP + k for k in range(GROUP)]
-        if first:
-            for slot in some:
-                for copy in copies(slot):
-                    copy.wait()
-
         @pl.when(some[0] < used)
         def _():
             products = [
@@ -240,17 +222,13 @@
     slots, order, width = left.shape
     sectors = shape[0]
     message = message_shape(*shape)
-    scratch = []
-    if first:
-        scratch = [pltpu.VMEM(b.shape, b.dtype) for b in (left, right)]
-        scratch += [pltpu.SemaphoreType.DMA((slots,))] * 2
     return pl.pallas_call(
         functools.partial(blocks_kernel, first, shape, entries),
         in_specs=[SMEM, SMEM]
         + [VMEM] * (len(fields) + len(own))
-        + [HBM if first else VMEM] * 2,
+        + [VMEM] * 2,
         out_specs=[VMEM] * 5,
-        scratch_shapes=[pltpu.VMEM((sectors, order, width), jnp.bfloat16)] + scratch,
+        scratch_shapes=[pltpu.VMEM((sectors, order, width), jnp.bfloat16)],
         out_shape=[
             jax.ShapeDtypeStruct((sectors, order, width), jnp.float32),
             jax.ShapeDtypeStruct((2, *message), jnp.bfloat16),
@@ -258,7 +236,7 @@
             jax.ShapeDtypeStruct((8, 128), jnp.float32),
             jax.ShapeDtypeStruct((8, 128), jnp.float32),
         ],
-        compiler_params=FIRST if first else PARAMS,
+        compiler_params=PARAMS,
         cost_estimate=pl.CostEstimate(
             flops=4 * slots * order * order * width,
             bytes_accessed=4 * slots * order * order,
@@ -402,7 +380,11 @@
             results.append(beside[k](*results))
         if k < ROUNDS - 1:
             ready = results[-1:] if beside else []
-            two, ready = lax.optimization_barrier((two, ready))
+            if k == 1:
+                across = copied(across, 0)
+                one, across, ready = lax.optimization_barrier((one, across, ready))
+            else:
+                two, ready = lax.optimization_barrier((two, ready))
             if ready:
                 results[-1] = ready[0]
         pieces += [one, two, flip(one), flip(two)]

time: 97 us -> 99.8 us (1.029); the launches traced: 96.4 us -> 100 us
  Pallas kernels: 10.1 us -> 15.5 us
  starting transfers between devices: 57.6 us -> 53.1 us
  local copies, waits for them, and re-layouts: 1.81 us -> 5.29 us
    ppermute x22, starting transfers between devices: 11.8 us -> 2.42 us  [flip(): return lax.ppermute(value, 'term', [(i, i ^ 1) for i in range(16)])]
    pallas_call x2, Pallas kernels: 7.54 us -> 13 us  [apply_blocks(): pl.pallas_call(functools.partial(blocks_kernel, first, shape, entries), i...]
    ppermute x28, starting transfers between devices: 45.8 us -> 50.7 us  [hop(): return lax.ppermute(value, 'term', pairs)]
    unnamed x12 -> x14, local copies, waits for them, and re-layouts: 1.81 us -> 5.29 us
    ppermute x28, waiting for transfers between devices: 19.6 us -> 18.5 us  [hop(): return lax.ppermute(value, 'term', pairs)]
  transfers between devices with their start and end apart: 50 -> 50, of which waited for: 30 -> 21; matrix products, arithmetic and copies ran while one was open for 1% -> 1% of each run, Pallas kernels for 1% -> 1%
where the time goes in v15:
time: 99.8 us; the launch traced here: 100 us
  starting transfers between devices  53.1 us (53%)
  waiting for transfers between devices  24.1 us (24%)
  Pallas kernels  15.5 us (16%)
  local copies, waits for them, and re-layouts  5.29 us (5%)
  between operations  1.57 us (2%)
    ppermute x28, starting transfers between devices, hop(): return lax.ppermute(value, 'term', pairs)  50.7 us
    ppermute x28, waiting for transfers between devices, hop(): return lax.ppermute(value, 'term', pairs)  18.5 us
    pallas_call x2, Pallas kernels, apply_blocks(): pl.pallas_call(functools.partial(blocks_kernel, first, shape, entries), i...  13 us
    ppermute x22, waiting for transfers between devices, flip(): return lax.ppermute(value, 'term', [(i, i ^ 1) for i in range(16)])  5.58 us
    unnamed x14, local copies, waits for them, and re-layouts  5.29 us
    ppermute x22, starting transfers between devices, flip(): return lax.ppermute(value, 'term', [(i, i ^ 1) for i in range(16)])  2.42 us
  transfers between devices with their start and end apart: 50, of which 21 were waited for; matrix products, arithmetic and copies ran while one was open for 1% of the time, Pallas kernels for 1%

profile of v15, /device:TPU:0, one launch (start us, length us, event | category | flops | bytes accessed | tf_op | source)
XLA Modules:
  0.0 100.3 jit_solution(10642806228191682321)
XLA Ops:
  1.1 2.6 %collective-permute-start.2 = (bf16[3,32,512]{2,1,0:T(8,128)(2,1)}, bf16[3,32,512]{2,1,0:T(8,128)(2,1)S(1)}, u32[]{:S(2)}, u32[]{:S(2)}) collective-permute-start(bf16[3,32,512]{2,1,0:T(8,128)(2,1)} %wave_ref.3), channel_id=1, source_target_pairs={{0,4},{1,3},{4,8},{5,1},{8,12},{9,5},{12,14},{13,9},{14,10},{15,13... | collective-permute-start | bytes 294920 | tf_op jit(solution)/shard_map/ppermute | solution.py:364
  4.4 1.6 %collective-permute-start.1 = (bf16[3,32,512]{2,1,0:T(8,128)(2,1)S(1)}, bf16[3,32,512]{2,1,0:T(8,128)(2,1)S(1)}, u32[]{:S(2)}, u32[]{:S(2)}) collective-permute-start(bf16[3,32,512]{2,1,0:T(8,128)(2,1)S(1)} %collective-permute-done.refs_1_), channel_id=1, source_target_pairs={{0,4},{1,3},{4,8},{5,1},{8,12},{9,5},{12,14},{13,9},{14,10},{15,13... | collective-permute-start | bytes 294920 | tf_op jit(solution)/shard_map/ppermute | solution.py:364
  6.8 2.6 %collective-permute-start.4 = (bf16[3,32,512]{2,1,0:T(8,128)(2,1)}, bf16[3,32,512]{2,1,0:T(8,128)(2,1)S(1)}, u32[]{:S(2)}, u32[]{:S(2)}) collective-permute-start(bf16[3,32,512]{2,1,0:T(8,128)(2,1)} %wave_ref.3), channel_id=1, source_target_pairs={{0,14},{1,15},{4,10},{5,11},{8,6},{9,7},{12,2},{13,3},{14,0},{15,1... | collective-permute-start | bytes 294920 | tf_op jit(solution)/shard_map/ppermute | solution.py:364
  11.7 2.8 %collective-permute-done.4.in_ref = bf16[3,32,512]{2,1,0:T(8,128)(2,1)S(1)} collective-permute-done((bf16[3,32,512]{2,1,0:T(8,128)(2,1)}, bf16[3,32,512]{2,1,0:T(8,128)(2,1)S(1)}, u32[]{:S(2)}, u32[]{:S(2)}) %collective-permute-start.4) | collective-permute-done | bytes 98336 | tf_op jit(solution)/shard_map/ppermute | solution.py:364
  15.4 1.4 %collective-permute-start.10 = (bf16[3,32,512]{2,1,0:T(8,128)(2,1)S(1)}, bf16[3,32,512]{2,1,0:T(8,128)(2,1)S(1)}, u32[]{:S(2)}, u32[]{:S(2)}) collective-permute-start(bf16[3,32,512]{2,1,0:T(8,128)(2,1)S(1)} %collective-permute-done.3.refs_6_), channel_id=1, source_target_pairs={{0,4},{1,3},{4,8},{5,1},{8,12},{9,5},{12,14},{13,9},{14,10},{15,13... | collective-permute-start | bytes 294920 | tf_op jit(solution)/shard_map/ppermute | solution.py:364
  18.6 1.4 %collective-permute-done.10.refs_10_ = bf16[3,32,512]{2,1,0:T(8,128)(2,1)S(1)} collective-permute-done((bf16[3,32,512]{2,1,0:T(8,128)(2,1)S(1)}, bf16[3,32,512]{2,1,0:T(8,128)(2,1)S(1)}, u32[]{:S(2)}, u32[]{:S(2)}) %collective-permute-start.10) | collective-permute-done | bytes 98336 | tf_op jit(solution)/shard_map/ppermute | solution.py:364
  20.0 1.4 %collective-permute-done.11.refs_11_ = bf16[3,32,512]{2,1,0:T(8,128)(2,1)S(1)} collective-permute-done((bf16[3,32,512]{2,1,0:T(8,128)(2,1)S(1)}, bf16[3,32,512]{2,1,0:T(8,128)(2,1)S(1)}, u32[]{:S(2)}, u32[]{:S(2)}) %collective-permute-start.11) | collective-permute-done | bytes 98336 | tf_op jit(solution)/shard_map/ppermute | solution.py:364
  22.7 2.2 %copy-done.3 = bf16[8,512,512]{2,1,0:T(8,128)(2,1)S(1)} copy-done((bf16[8,512,512]{2,1,0:T(8,128)(2,1)S(1)}, bf16[8,512,512]{2,1,0:T(8,128)(2,1)}, u32[]{:S(2)}) %copy-start.3) | copy-done | bytes 4194328
  24.9 2.2 %copy-done.5 = bf16[8,512,512]{2,1,0:T(8,128)(2,1)S(1)} copy-done((bf16[8,512,512]{2,1,0:T(8,128)(2,1)S(1)}, bf16[8,512,512]{2,1,0:T(8,128)(2,1)}, u32[]{:S(2)}) %copy-start.5) | copy-done | bytes 4194328
  27.1 6.8 %shard_map.97 = (f32[3,512,512]{2,1,0:T(8,128)S(1)}, bf16[2,16,3200]{2,1,0:T(8,128)(2,1)S(1)}, bf16[6,16,3200]{2,1,0:T(8,128)(2,1)S(1)}, f32[8,128]{1,0:T(8,128)S(1)}, f32[8,128]{1,0:T(8,128)S(1)}) custom-call(s32[1]{0:T(128)} %bitcast.me_ref.refs_0_.refs_2_, s32[17]{0:T(128)S(1)} %pad_add_fusion.ints_ref, ...), custom_call_target="tpu_custom_call" | custom-call | flops 4294967296 | bytes 8388608 | tf_op jit(solution)/shard_map/pallas_call | solution.py:225
  34.0 1.4 %collective-permute-done.15.other_ref = bf16[2,16,3200]{2,1,0:T(8,128)(2,1)S(1)} collective-permute-done((bf16[2,16,3200]{2,1,0:T(8,128)(2,1)S(1)}, bf16[2,16,3200]{2,1,0:T(8,128)(2,1)S(1)}, u32[]{:S(2)}, u32[]{:S(2)}) %collective-permute-start.15) | collective-permute-done | bytes 204832 | tf_op jit(solution)/shard_map/ppermute | solution.py:355
  36.9 1.5 %collective-permute-start.17 = (bf16[16,3200]{1,0:T(8,128)(2,1)S(1)}, bf16[16,3200]{1,0:T(8,128)(2,1)S(1)}, u32[]{:S(2)}, u32[]{:S(2)}) collective-permute-start(bf16[16,3200]{1,0:T(8,128)(2,1)S(1)} %shard_map.98), channel_id=1, source_target_pairs={{0,4},{1,3},{4,8},{5,1},{8,12},{9,5},{12,14},{13,9},{14,10},{15,13... | collective-permute-start | bytes 307208 | tf_op jit(solution)/shard_map/ppermute | solution.py:364
  38.5 1.5 %collective-permute-start.22 = (bf16[16,3200]{1,0:T(8,128)(2,1)S(1)}, bf16[16,3200]{1,0:T(8,128)(2,1)S(1)}, u32[]{:S(2)}, u32[]{:S(2)}) collective-permute-start(bf16[16,3200]{1,0:T(8,128)(2,1)S(1)} %shard_map.103), channel_id=1, source_target_pairs={{0,14},{1,15},{4,10},{5,11},{8,6},{9,7},{12,2},{13,3},{14,0},{15,1... | collective-permute-start | bytes 307208 | tf_op jit(solution)/shard_map/ppermute | solution.py:364
  40.4 1.3 %collective-permute-start.21 = (bf16[16,3200]{1,0:T(8,128)(2,1)S(1)}, bf16[16,3200]{1,0:T(8,128)(2,1)S(1)}, u32[]{:S(2)}, u32[]{:S(2)}) collective-permute-start(bf16[16,3200]{1,0:T(8,128)(2,1)S(1)} %shard_map.102), channel_id=1, source_target_pairs={{0,4},{1,3},{4,8},{5,1},{8,12},{9,5},{12,14},{13,9},{14,10},{15,13... | collective-permute-start | bytes 307208 | tf_op jit(solution)/shard_map/ppermute | solution.py:364
  41.7 3.3 %collective-permute-start.18 = (bf16[16,3200]{1,0:T(8,128)(2,1)S(1)}, bf16[16,3200]{1,0:T(8,128)(2,1)S(1)}, u32[]{:S(2)}, u32[]{:S(2)}) collective-permute-start(bf16[16,3200]{1,0:T(8,128)(2,1)S(1)} %shard_map.99), channel_id=1, source_target_pairs={{0,4},{1,3},{4,8},{5,1},{8,12},{9,5},{12,14},{13,9},{14,10},{15,13... | collective-permute-start | bytes 307208 | tf_op jit(solution)/shard_map/ppermute | solution.py:364
  47.7 2.2 %collective-permute-start.19 = (bf16[16,3200]{1,0:T(8,128)(2,1)S(1)}, bf16[16,3200]{1,0:T(8,128)(2,1)S(1)}, u32[]{:S(2)}, u32[]{:S(2)}) collective-permute-start(bf16[16,3200]{1,0:T(8,128)(2,1)S(1)} %shard_map.100), channel_id=1, source_target_pairs={{0,4},{1,3},{4,8},{5,1},{8,12},{9,5},{12,14},{13,9},{14,10},{15,13... | collective-permute-start | bytes 307208 | tf_op jit(solution)/shard_map/ppermute | solution.py:364
  53.5 1.9 %collective-permute-start.26 = (bf16[16,3200]{1,0:T(8,128)(2,1)S(1)}, bf16[16,3200]{1,0:T(8,128)(2,1)S(1)}, u32[]{:S(2)}, u32[]{:S(2)}) collective-permute-start(bf16[16,3200]{1,0:T(8,128)(2,1)S(1)} %get-tuple-element.57.refs_0_), channel_id=1, source_target_pairs={{0,4},{1,3},{4,8},{5,1},{8,12},{9,5},{12,14},{13,9},{14,10},{15,13... | collective-permute-start | bytes 307208 | tf_op jit(solution)/shard_map/ppermute | solution.py:364
  55.5 2.4 %collective-permute-start.27 = (bf16[16,3200]{1,0:T(8,128)(2,1)S(1)}, bf16[16,3200]{1,0:T(8,128)(2,1)S(1)}, u32[]{:S(2)}, u32[]{:S(2)}) collective-permute-start(bf16[16,3200]{1,0:T(8,128)(2,1)S(1)} %collective-permute-done.25.refs_1_), channel_id=1, source_target_pairs={{0,4},{1,3},{4,8},{5,1},{8,12},{9,5},{12,14},{13,9},{14,10},{15,13... | collective-permute-start | bytes 307208 | tf_op jit(solution)/shard_map/ppermute | solution.py:364
  58.6 2.1 %collective-permute-start.30 = (bf16[16,3200]{1,0:T(8,128)(2,1)S(1)}, bf16[16,3200]{1,0:T(8,128)(2,1)S(1)}, u32[]{:S(2)}, u32[]{:S(2)}) collective-permute-start(bf16[16,3200]{1,0:T(8,128)(2,1)S(1)} %collective-permute-done.26.refs_2_), channel_id=1, source_target_pairs={{0,4},{1,3},{4,8},{5,1},{8,12},{9,5},{12,14},{13,9},{14,10},{15,13... | collective-permute-start | bytes 307208 | tf_op jit(solution)/shard_map/ppermute | solution.py:364
  60.8 3.7 %collective-permute-start.32 = (bf16[16,3200]{1,0:T(8,128)(2,1)S(1)}, bf16[16,3200]{1,0:T(8,128)(2,1)S(1)}, u32[]{:S(2)}, u32[]{:S(2)}) collective-permute-start(bf16[16,3200]{1,0:T(8,128)(2,1)S(1)} %collective-permute-done.27.refs_3_), channel_id=1, source_target_pairs={{0,4},{1,3},{4,8},{5,1},{8,12},{9,5},{12,14},{13,9},{14,10},{15,13... | collective-permute-start | bytes 307208 | tf_op jit(solution)/shard_map/ppermute | solution.py:364
  65.5 2.0 %collective-permute-start.35 = (bf16[16,3200]{1,0:T(8,128)(2,1)S(1)}, bf16[16,3200]{1,0:T(8,128)(2,1)S(1)}, u32[]{:S(2)}, u32[]{:S(2)}) collective-permute-start(bf16[16,3200]{1,0:T(8,128)(2,1)S(1)} %collective-permute-done.30.refs_6_), channel_id=1, source_target_pairs={{0,4},{1,3},{4,8},{5,1},{8,12},{9,5},{12,14},{13,9},{14,10},{15,13... | collective-permute-start | bytes 307208 | tf_op jit(solution)/shard_map/ppermute | solution.py:364
  67.5 1.6 %collective-permute-start.36 = (bf16[16,3200]{1,0:T(8,128)(2,1)S(1)}, bf16[16,3200]{1,0:T(8,128)(2,1)S(1)}, u32[]{:S(2)}, u32[]{:S(2)}) collective-permute-start(bf16[16,3200]{1,0:T(8,128)(2,1)S(1)} %collective-permute-done.32.refs_7_), channel_id=1, source_target_pairs={{0,4},{1,3},{4,8},{5,1},{8,12},{9,5},{12,14},{13,9},{14,10},{15,13... | collective-permute-start | bytes 307208 | tf_op jit(solution)/shard_map/ppermute | solution.py:364
  70.2 1.9 %collective-permute-done.36.refs_11_ = bf16[16,3200]{1,0:T(8,128)(2,1)S(1)} collective-permute-done((bf16[16,3200]{1,0:T(8,128)(2,1)S(1)}, bf16[16,3200]{1,0:T(8,128)(2,1)S(1)}, u32[]{:S(2)}, u32[]{:S(2)}) %collective-permute-start.36) | collective-permute-done | bytes 102432 | tf_op jit(solution)/shard_map/ppermute | solution.py:364
  73.5 6.2 %shard_map.107 = (f32[3,512,512]{2,1,0:T(8,128)S(1)}, bf16[2,16,3200]{2,1,0:T(8,128)(2,1)S(1)}, bf16[6,16,3200]{2,1,0:T(8,128)(2,1)S(1)}, f32[8,128]{1,0:T(8,128)S(1)}, f32[8,128]{1,0:T(8,128)S(1)}) custom-call(s32[1]{0:T(128)} %bitcast.me_ref.refs_0_.refs_2_, s32[17]{0:T(128)S(1)} %pad_add_fusion.ints_ref, bf16[16,3200]{1,0:T(8,128)(2,1)S(1)} %get-tuple-element.57.refs_0_, ...), custom_call_target="tpu_custom_call" | custom-call | flops 4294967296 | bytes 8388608 | tf_op jit(solution)/shard_map/pallas_call | solution.py:225
  79.7 1.4 %collective-permute-done.40.other_ref = bf16[2,16,3200]{2,1,0:T(8,128)(2,1)S(1)} collective-permute-done((bf16[2,16,3200]{2,1,0:T(8,128)(2,1)S(1)}, bf16[2,16,3200]{2,1,0:T(8,128)(2,1)S(1)}, u32[]{:S(2)}, u32[]{:S(2)}) %collective-permute-start.40) | collective-permute-done | bytes 204832 | tf_op jit(solution)/shard_map/ppermute | solution.py:355
  81.4 1.7 %collective-permute-start.45 = (bf16[16,3200]{1,0:T(8,128)(2,1)S(1)}, bf16[16,3200]{1,0:T(8,128)(2,1)S(1)}, u32[]{:S(2)}, u32[]{:S(2)}) collective-permute-start(bf16[16,3200]{1,0:T(8,128)(2,1)S(1)} %shard_map.111), channel_id=1, source_target_pairs={{0,4},{1,3},{4,8},{5,1},{8,12},{9,5},{12,14},{13,9},{14,10},{15,13... | collective-permute-start | bytes 307208 | tf_op jit(solution)/shard_map/ppermute | solution.py:364
  83.1 2.5 %collective-permute-start.42 = (bf16[16,3200]{1,0:T(8,128)(2,1)S(1)}, bf16[16,3200]{1,0:T(8,128)(2,1)S(1)}, u32[]{:S(2)}, u32[]{:S(2)}) collective-permute-start(bf16[16,3200]{1,0:T(8,128)(2,1)S(1)} %shard_map.108), channel_id=1, source_target_pairs={{0,4},{1,3},{4,8},{5,1},{8,12},{9,5},{12,14},{13,9},{14,10},{15,13... | collective-permute-start | bytes 307208 | tf_op jit(solution)/shard_map/ppermute | solution.py:364
  86.1 2.4 %collective-permute-start.46 = (bf16[16,3200]{1,0:T(8,128)(2,1)S(1)}, bf16[16,3200]{1,0:T(8,128)(2,1)S(1)}, u32[]{:S(2)}, u32[]{:S(2)}) collective-permute-start(bf16[16,3200]{1,0:T(8,128)(2,1)S(1)} %shard_map.112), channel_id=1, source_target_pairs={{0,4},{1,3},{4,8},{5,1},{8,12},{9,5},{12,14},{13,9},{14,10},{15,13... | collective-permute-start | bytes 307208 | tf_op jit(solution)/shard_map/ppermute | solution.py:364
  88.6 3.1 %collective-permute-start.43 = (bf16[16,3200]{1,0:T(8,128)(2,1)S(1)}, bf16[16,3200]{1,0:T(8,128)(2,1)S(1)}, u32[]{:S(2)}, u32[]{:S(2)}) collective-permute-start(bf16[16,3200]{1,0:T(8,128)(2,1)S(1)} %shard_map.109), channel_id=1, source_target_pairs={{0,4},{1,3},{4,8},{5,1},{8,12},{9,5},{12,14},{13,9},{14,10},{15,13... | collective-permute-start | bytes 307208 | tf_op jit(solution)/shard_map/ppermute | solution.py:364
  91.7 1.6 %collective-permute-done.47.refs_8_ = bf16[16,3200]{1,0:T(8,128)(2,1)S(1)} collective-permute-done((bf16[16,3200]{1,0:T(8,128)(2,1)S(1)}, bf16[16,3200]{1,0:T(8,128)(2,1)S(1)}, u32[]{:S(2)}, u32[]{:S(2)}) %collective-permute-start.47) | collective-permute-done | bytes 102432 | tf_op jit(solution)/shard_map/ppermute | solution.py:364
  94.5 2.2 %collective-permute-start.44 = (bf16[16,3200]{1,0:T(8,128)(2,1)S(1)}, bf16[16,3200]{1,0:T(8,128)(2,1)S(1)}, u32[]{:S(2)}, u32[]{:S(2)}) collective-permute-start(bf16[16,3200]{1,0:T(8,128)(2,1)S(1)} %shard_map.110), channel_id=1, source_target_pairs={{0,4},{1,3},{4,8},{5,1},{8,12},{9,5},{12,14},{13,9},{14,10},{15,13... | collective-permute-start | bytes 307208 | tf_op jit(solution)/shard_map/ppermute | solution.py:364
  96.7 1.4 %collective-permute-done.48 = bf16[16,3200]{1,0:T(8,128)(2,1)S(1)} collective-permute-done((bf16[16,3200]{1,0:T(8,128)(2,1)S(1)}, bf16[16,3200]{1,0:T(8,128)(2,1)S(1)}, u32[]{:S(2)}, u32[]{:S(2)}) %collective-permute-start.48) | collective-permute-done | bytes 102432 | tf_op jit(solution)/shard_map/ppermute | solution.py:364
  (105 shorter events, 24.5 us)
Async XLA Ops:
  1.1 8.3 %collective-permute-start.2 = (bf16[3,32,512]{2,1,0:T(8,128)(2,1)}, bf16[3,32,512]{2,1,0:T(8,128)(2,1)S(1)}, u32[]{:S(2)}, u32[]{:S(2)}) collective-permute-start(bf16[3,32,512]{2,1,0:T(8,128)(2,1)} %wave_ref.3), channel_id=1, source_target_pairs={{0,4},{1,3},{4,8},{5,1},{8,12},{9,5},{12,14},{13,9},{14,10},{15,13... | collective-permute-start | bytes 294920 | tf_op jit(solution)/shard_map/ppermute | solution.py:364
  4.4 5.0 %collective-permute-start.1 = (bf16[3,32,512]{2,1,0:T(8,128)(2,1)S(1)}, bf16[3,32,512]{2,1,0:T(8,128)(2,1)S(1)}, u32[]{:S(2)}, u32[]{:S(2)}) collective-permute-start(bf16[3,32,512]{2,1,0:T(8,128)(2,1)S(1)} %collective-permute-done.refs_1_), channel_id=1, source_target_pairs={{0,4},{1,3},{4,8},{5,1},{8,12},{9,5},{12,14},{13,9},{14,10},{15,13... | collective-permute-start | bytes 294920 | tf_op jit(solution)/shard_map/ppermute | solution.py:364
  6.8 7.6 %collective-permute-start.4 = (bf16[3,32,512]{2,1,0:T(8,128)(2,1)}, bf16[3,32,512]{2,1,0:T(8,128)(2,1)S(1)}, u32[]{:S(2)}, u32[]{:S(2)}) collective-permute-start(bf16[3,32,512]{2,1,0:T(8,128)(2,1)} %wave_ref.3), channel_id=1, source_target_pairs={{0,14},{1,15},{4,10},{5,11},{8,6},{9,7},{12,2},{13,3},{14,0},{15,1... | collective-permute-start | bytes 294920 | tf_op jit(solution)/shard_map/ppermute | solution.py:364
  9.4 5.9 %collective-permute-start.3 = (bf16[3,32,512]{2,1,0:T(8,128)(2,1)S(1)}, bf16[3,32,512]{2,1,0:T(8,128)(2,1)S(1)}, u32[]{:S(2)}, u32[]{:S(2)}) collective-permute-start(bf16[3,32,512]{2,1,0:T(8,128)(2,1)S(1)} %collective-permute-done.2.refs_2_), channel_id=1, source_target_pairs={{0,4},{1,3},{4,8},{5,1},{8,12},{9,5},{12,14},{13,9},{14,10},{15,13... | collective-permute-start | bytes 294920 | tf_op jit(solution)/shard_map/ppermute | solution.py:364
  9.4 7.3 %collective-permute-start.7 = (bf16[3,32,512]{2,1,0:T(8,128)(2,1)S(1)}, bf16[3,32,512]{2,1,0:T(8,128)(2,1)S(1)}, u32[]{:S(2)}, u32[]{:S(2)}) collective-permute-start(bf16[3,32,512]{2,1,0:T(8,128)(2,1)S(1)} %collective-permute-done.1.refs_3_), channel_id=1, source_target_pairs={{0,4},{1,3},{4,8},{5,1},{8,12},{9,5},{12,14},{13,9},{14,10},{15,13... | collective-permute-start | bytes 294920 | tf_op jit(solution)/shard_map/ppermute | solution.py:364
  11.6 6.5 %collective-permute-start.5 = (bf16[3,32,512]{2,1,0:T(8,128)(2,1)S(1)}, bf16[3,32,512]{2,1,0:T(8,128)(2,1)S(1)}, u32[]{:S(2)}, u32[]{:S(2)}) collective-permute-start(bf16[3,32,512]{2,1,0:T(8,128)(2,1)S(1)} %collective-permute-done.2.refs_2_), channel_id=1, source_target_pairs={{0,1},{1,0},{2,3},{3,2},{4,5},{5,4},{6,7},{7,6},{8,9},{9,8},{10,11... | collective-permute-start | bytes 294920 | tf_op jit(solution)/shard_map/ppermute | solution.py:355
  15.4 4.6 %collective-permute-start.10 = (bf16[3,32,512]{2,1,0:T(8,128)(2,1)S(1)}, bf16[3,32,512]{2,1,0:T(8,128)(2,1)S(1)}, u32[]{:S(2)}, u32[]{:S(2)}) collective-permute-start(bf16[3,32,512]{2,1,0:T(8,128)(2,1)S(1)} %collective-permute-done.3.refs_6_), channel_id=1, source_target_pairs={{0,4},{1,3},{4,8},{5,1},{8,12},{9,5},{12,14},{13,9},{14,10},{15,13... | collective-permute-start | bytes 294920 | tf_op jit(solution)/shard_map/ppermute | solution.py:364
  16.8 4.6 %collective-permute-start.11 = (bf16[3,32,512]{2,1,0:T(8,128)(2,1)S(1)}, bf16[3,32,512]{2,1,0:T(8,128)(2,1)S(1)}, u32[]{:S(2)}, u32[]{:S(2)}) collective-permute-start(bf16[3,32,512]{2,1,0:T(8,128)(2,1)S(1)} %collective-permute-done.7.refs_7_), channel_id=1, source_target_pairs={{0,4},{1,3},{4,8},{5,1},{8,12},{9,5},{12,14},{13,9},{14,10},{15,13... | collective-permute-start | bytes 294920 | tf_op jit(solution)/shard_map/ppermute | solution.py:364
  35.6 4.7 %collective-permute-start.20 = (bf16[16,3200]{1,0:T(8,128)(2,1)S(1)}, bf16[16,3200]{1,0:T(8,128)(2,1)S(1)}, u32[]{:S(2)}, u32[]{:S(2)}) collective-permute-start(bf16[16,3200]{1,0:T(8,128)(2,1)S(1)} %shard_map.101), channel_id=1, source_target_pairs={{0,4},{1,3},{4,8},{5,1},{8,12},{9,5},{12,14},{13,9},{14,10},{15,13... | collective-permute-start | bytes 307208 | tf_op jit(solution)/shard_map/ppermute | solution.py:364
  36.9 4.7 %collective-permute-start.17 = (bf16[16,3200]{1,0:T(8,128)(2,1)S(1)}, bf16[16,3200]{1,0:T(8,128)(2,1)S(1)}, u32[]{:S(2)}, u32[]{:S(2)}) collective-permute-start(bf16[16,3200]{1,0:T(8,128)(2,1)S(1)} %shard_map.98), channel_id=1, source_target_pairs={{0,4},{1,3},{4,8},{5,1},{8,12},{9,5},{12,14},{13,9},{14,10},{15,13... | collective-permute-start | bytes 307208 | tf_op jit(solution)/shard_map/ppermute | solution.py:364
  38.5 7.6 %collective-permute-start.22 = (bf16[16,3200]{1,0:T(8,128)(2,1)S(1)}, bf16[16,3200]{1,0:T(8,128)(2,1)S(1)}, u32[]{:S(2)}, u32[]{:S(2)}) collective-permute-start(bf16[16,3200]{1,0:T(8,128)(2,1)S(1)} %shard_map.103), channel_id=1, source_target_pairs={{0,14},{1,15},{4,10},{5,11},{8,6},{9,7},{12,2},{13,3},{14,0},{15,1... | collective-permute-start | bytes 307208 | tf_op jit(solution)/shard_map/ppermute | solution.py:364
  40.4 6.0 %collective-permute-start.21 = (bf16[16,3200]{1,0:T(8,128)(2,1)S(1)}, bf16[16,3200]{1,0:T(8,128)(2,1)S(1)}, u32[]{:S(2)}, u32[]{:S(2)}) collective-permute-start(bf16[16,3200]{1,0:T(8,128)(2,1)S(1)} %shard_map.102), channel_id=1, source_target_pairs={{0,4},{1,3},{4,8},{5,1},{8,12},{9,5},{12,14},{13,9},{14,10},{15,13... | collective-permute-start | bytes 307208 | tf_op jit(solution)/shard_map/ppermute | solution.py:364
  41.7 5.9 %collective-permute-start.18 = (bf16[16,3200]{1,0:T(8,128)(2,1)S(1)}, bf16[16,3200]{1,0:T(8,128)(2,1)S(1)}, u32[]{:S(2)}, u32[]{:S(2)}) collective-permute-start(bf16[16,3200]{1,0:T(8,128)(2,1)S(1)} %shard_map.99), channel_id=1, source_target_pairs={{0,4},{1,3},{4,8},{5,1},{8,12},{9,5},{12,14},{13,9},{14,10},{15,13... | collective-permute-start | bytes 307208 | tf_op jit(solution)/shard_map/ppermute | solution.py:364
  46.5 4.7 %collective-permute-start.23 = (bf16[16,3200]{1,0:T(8,128)(2,1)S(1)}, bf16[16,3200]{1,0:T(8,128)(2,1)S(1)}, u32[]{:S(2)}, u32[]{:S(2)}) collective-permute-start(bf16[16,3200]{1,0:T(8,128)(2,1)S(1)} %shard_map.104), channel_id=1, source_target_pairs={{0,4},{1,3},{4,8},{5,1},{8,12},{9,5},{12,14},{13,9},{14,10},{15,13... | collective-permute-start | bytes 307208 | tf_op jit(solution)/shard_map/ppermute | solution.py:364
  47.7 4.7 %collective-permute-start.19 = (bf16[16,3200]{1,0:T(8,128)(2,1)S(1)}, bf16[16,3200]{1,0:T(8,128)(2,1)S(1)}, u32[]{:S(2)}, u32[]{:S(2)}) collective-permute-start(bf16[16,3200]{1,0:T(8,128)(2,1)S(1)} %shard_map.100), channel_id=1, source_target_pairs={{0,4},{1,3},{4,8},{5,1},{8,12},{9,5},{12,14},{13,9},{14,10},{15,13... | collective-permute-start | bytes 307208 | tf_op jit(solution)/shard_map/ppermute | solution.py:364
  53.5 5.1 %collective-permute-start.26 = (bf16[16,3200]{1,0:T(8,128)(2,1)S(1)}, bf16[16,3200]{1,0:T(8,128)(2,1)S(1)}, u32[]{:S(2)}, u32[]{:S(2)}) collective-permute-start(bf16[16,3200]{1,0:T(8,128)(2,1)S(1)} %get-tuple-element.57.refs_0_), channel_id=1, source_target_pairs={{0,4},{1,3},{4,8},{5,1},{8,12},{9,5},{12,14},{13,9},{14,10},{15,13... | collective-permute-start | bytes 307208 | tf_op jit(solution)/shard_map/ppermute | solution.py:364
  55.5 5.3 %collective-permute-start.27 = (bf16[16,3200]{1,0:T(8,128)(2,1)S(1)}, bf16[16,3200]{1,0:T(8,128)(2,1)S(1)}, u32[]{:S(2)}, u32[]{:S(2)}) collective-permute-start(bf16[16,3200]{1,0:T(8,128)(2,1)S(1)} %collective-permute-done.25.refs_1_), channel_id=1, source_target_pairs={{0,4},{1,3},{4,8},{5,1},{8,12},{9,5},{12,14},{13,9},{14,10},{15,13... | collective-permute-start | bytes 307208 | tf_op jit(solution)/shard_map/ppermute | solution.py:364
  57.9 7.6 %collective-permute-start.31 = (bf16[16,3200]{1,0:T(8,128)(2,1)S(1)}, bf16[16,3200]{1,0:T(8,128)(2,1)S(1)}, u32[]{:S(2)}, u32[]{:S(2)}) collective-permute-start(bf16[16,3200]{1,0:T(8,128)(2,1)S(1)} %get-tuple-element.57.refs_0_), channel_id=1, source_target_pairs={{0,14},{1,15},{4,10},{5,11},{8,6},{9,7},{12,2},{13,3},{14,0},{15,1... | collective-permute-start | bytes 307208 | tf_op jit(solution)/shard_map/ppermute | solution.py:364
  58.6 6.8 %collective-permute-start.30 = (bf16[16,3200]{1,0:T(8,128)(2,1)S(1)}, bf16[16,3200]{1,0:T(8,128)(2,1)S(1)}, u32[]{:S(2)}, u32[]{:S(2)}) collective-permute-start(bf16[16,3200]{1,0:T(8,128)(2,1)S(1)} %collective-permute-done.26.refs_2_), channel_id=1, source_target_pairs={{0,4},{1,3},{4,8},{5,1},{8,12},{9,5},{12,14},{13,9},{14,10},{15,13... | collective-permute-start | bytes 307208 | tf_op jit(solution)/shard_map/ppermute | solution.py:364
  60.8 6.8 %collective-permute-start.32 = (bf16[16,3200]{1,0:T(8,128)(2,1)S(1)}, bf16[16,3200]{1,0:T(8,128)(2,1)S(1)}, u32[]{:S(2)}, u32[]{:S(2)}) collective-permute-start(bf16[16,3200]{1,0:T(8,128)(2,1)S(1)} %collective-permute-done.27.refs_3_), channel_id=1, source_target_pairs={{0,4},{1,3},{4,8},{5,1},{8,12},{9,5},{12,14},{13,9},{14,10},{15,13... | collective-permute-start | bytes 307208 | tf_op jit(solution)/shard_map/ppermute | solution.py:364
  64.5 4.7 %collective-permute-start.28 = (bf16[16,3200]{1,0:T(8,128)(2,1)S(1)}, bf16[16,3200]{1,0:T(8,128)(2,1)S(1)}, u32[]{:S(2)}, u32[]{:S(2)}) collective-permute-start(bf16[16,3200]{1,0:T(8,128)(2,1)S(1)} %collective-permute-done.26.refs_2_), channel_id=1, source_target_pairs={{0,1},{1,0},{2,3},{3,2},{4,5},{5,4},{6,7},{7,6},{8,9},{9,8},{10,11... | collective-permute-start | bytes 307208 | tf_op jit(solution)/shard_map/ppermute | solution.py:355
  65.4 4.2 %collective-permute-start.39 = (bf16[16,3200]{1,0:T(8,128)(2,1)S(1)}, bf16[16,3200]{1,0:T(8,128)(2,1)S(1)}, u32[]{:S(2)}, u32[]{:S(2)}) collective-permute-start(bf16[16,3200]{1,0:T(8,128)(2,1)S(1)} %shard_map.106.refs_14_), channel_id=1, source_target_pairs={{0,1},{1,0},{2,3},{3,2},{4,5},{5,4},{6,7},{7,6},{8,9},{9,8},{10,11... | collective-permute-start | bytes 307208 | tf_op jit(solution)/shard_map/ppermute | solution.py:355
  65.5 4.7 %collective-permute-start.35 = (bf16[16,3200]{1,0:T(8,128)(2,1)S(1)}, bf16[16,3200]{1,0:T(8,128)(2,1)S(1)}, u32[]{:S(2)}, u32[]{:S(2)}) collective-permute-start(bf16[16,3200]{1,0:T(8,128)(2,1)S(1)} %collective-permute-done.30.refs_6_), channel_id=1, source_target_pairs={{0,4},{1,3},{4,8},{5,1},{8,12},{9,5},{12,14},{13,9},{14,10},{15,13... | collective-permute-start | bytes 307208 | tf_op jit(solution)/shard_map/ppermute | solution.py:364
  67.5 4.7 %collective-permute-start.36 = (bf16[16,3200]{1,0:T(8,128)(2,1)S(1)}, bf16[16,3200]{1,0:T(8,128)(2,1)S(1)}, u32[]{:S(2)}, u32[]{:S(2)}) collective-permute-start(bf16[16,3200]{1,0:T(8,128)(2,1)S(1)} %collective-permute-done.32.refs_7_), channel_id=1, source_target_pairs={{0,4},{1,3},{4,8},{5,1},{8,12},{9,5},{12,14},{13,9},{14,10},{15,13... | collective-permute-start | bytes 307208 | tf_op jit(solution)/shard_map/ppermute | solution.py:364
  81.2 4.4 %collective-permute-start.41 = (bf16[6,16,3200]{2,1,0:T(8,128)(2,1)S(1)}, bf16[6,16,3200]{2,1,0:T(8,128)(2,1)S(1)}, u32[]{:S(2)}, u32[]{:S(2)}) collective-permute-start(bf16[6,16,3200]{2,1,0:T(8,128)(2,1)S(1)} %get-tuple-element.66), channel_id=1, source_target_pairs={{0,1},{1,0},{2,3},{3,2},{4,5},{5,4},{6,7},{7,6},{8,9},{9,8},{10,11... | collective-permute-start | bytes 1843208 | tf_op jit(solution)/shard_map/ppermute | solution.py:355
  81.4 4.7 %collective-permute-start.45 = (bf16[16,3200]{1,0:T(8,128)(2,1)S(1)}, bf16[16,3200]{1,0:T(8,128)(2,1)S(1)}, u32[]{:S(2)}, u32[]{:S(2)}) collective-permute-start(bf16[16,3200]{1,0:T(8,128)(2,1)S(1)} %shard_map.111), channel_id=1, source_target_pairs={{0,4},{1,3},{4,8},{5,1},{8,12},{9,5},{12,14},{13,9},{14,10},{15,13... | collective-permute-start | bytes 307208 | tf_op jit(solution)/shard_map/ppermute | solution.py:364
  83.1 5.4 %collective-permute-start.42 = (bf16[16,3200]{1,0:T(8,128)(2,1)S(1)}, bf16[16,3200]{1,0:T(8,128)(2,1)S(1)}, u32[]{:S(2)}, u32[]{:S(2)}) collective-permute-start(bf16[16,3200]{1,0:T(8,128)(2,1)S(1)} %shard_map.108), channel_id=1, source_target_pairs={{0,4},{1,3},{4,8},{5,1},{8,12},{9,5},{12,14},{13,9},{14,10},{15,13... | collective-permute-start | bytes 307208 | tf_op jit(solution)/shard_map/ppermute | solution.py:364
  85.6 7.6 %collective-permute-start.47 = (bf16[16,3200]{1,0:T(8,128)(2,1)S(1)}, bf16[16,3200]{1,0:T(8,128)(2,1)S(1)}, u32[]{:S(2)}, u32[]{:S(2)}) collective-permute-start(bf16[16,3200]{1,0:T(8,128)(2,1)S(1)} %shard_map.113), channel_id=1, source_target_pairs={{0,14},{1,15},{4,10},{5,11},{8,6},{9,7},{12,2},{13,3},{14,0},{15,1... | collective-permute-start | bytes 307208 | tf_op jit(solution)/shard_map/ppermute | solution.py:364
  86.1 7.1 %collective-permute-start.46 = (bf16[16,3200]{1,0:T(8,128)(2,1)S(1)}, bf16[16,3200]{1,0:T(8,128)(2,1)S(1)}, u32[]{:S(2)}, u32[]{:S(2)}) collective-permute-start(bf16[16,3200]{1,0:T(8,128)(2,1)S(1)} %shard_map.112), channel_id=1, source_target_pairs={{0,4},{1,3},{4,8},{5,1},{8,12},{9,5},{12,14},{13,9},{14,10},{15,13... | collective-permute-start | bytes 307208 | tf_op jit(solution)/shard_map/ppermute | solution.py:364
  88.6 5.8 %collective-permute-start.43 = (bf16[16,3200]{1,0:T(8,128)(2,1)S(1)}, bf16[16,3200]{1,0:T(8,128)(2,1)S(1)}, u32[]{:S(2)}, u32[]{:S(2)}) collective-permute-start(bf16[16,3200]{1,0:T(8,128)(2,1)S(1)} %shard_map.109), channel_id=1, source_target_pairs={{0,4},{1,3},{4,8},{5,1},{8,12},{9,5},{12,14},{13,9},{14,10},{15,13... | collective-permute-start | bytes 307208 | tf_op jit(solution)/shard_map/ppermute | solution.py:364
  93.3 4.7 %collective-permute-start.48 = (bf16[16,3200]{1,0:T(8,128)(2,1)S(1)}, bf16[16,3200]{1,0:T(8,128)(2,1)S(1)}, u32[]{:S(2)}, u32[]{:S(2)}) collective-permute-start(bf16[16,3200]{1,0:T(8,128)(2,1)S(1)} %shard_map.114), channel_id=1, source_target_pairs={{0,4},{1,3},{4,8},{5,1},{8,12},{9,5},{12,14},{13,9},{14,10},{15,13... | collective-permute-start | bytes 307208 | tf_op jit(solution)/shard_map/ppermute | solution.py:364
  94.5 4.7 %collective-permute-start.44 = (bf16[16,3200]{1,0:T(8,128)(2,1)S(1)}, bf16[16,3200]{1,0:T(8,128)(2,1)S(1)}, u32[]{:S(2)}, u32[]{:S(2)}) collective-permute-start(bf16[16,3200]{1,0:T(8,128)(2,1)S(1)} %shard_map.110), channel_id=1, source_target_pairs={{0,4},{1,3},{4,8},{5,1},{8,12},{9,5},{12,14},{13,9},{14,10},{15,13... | collective-permute-start | bytes 307208 | tf_op jit(solution)/shard_map/ppermute | solution.py:364
  (25 other events, 126.8 us)

commit v16 on v15

--- a/solution.py
+++ b/solution.py
@@ -97,7 +97,7 @@
     out_ref[...] = in_ref[...]
 
 
-def copied(value, cost=8 << 30):
+def copied(value, cost=64 << 30):
     return pl.pallas_call(
         copy_kernel,
         in_specs=[VMEM],
@@ -380,11 +380,7 @@
             results.append(beside[k](*results))
         if k < ROUNDS - 1:
             ready = results[-1:] if beside else []
-            if k == 1:
-                across = copied(across, 0)
-                one, across, ready = lax.optimization_barrier((one, across, ready))
-            else:
-                two, ready = lax.optimization_barrier((two, ready))
+            two, ready = lax.optimization_barrier((two, ready))
             if ready:
                 results[-1] = ready[0]
         pieces += [one, two, flip(one), flip(two)]

time: 99.8 us -> 100 us (level)
  starting transfers between devices: 53.1 us -> 64.2 us
  Pallas kernels: 15.5 us -> 7.97 us
  waiting for transfers between devices: 24.1 us -> 20 us
    ppermute x28, starting transfers between devices: 50.7 us -> 59.9 us  [hop(): return lax.ppermute(value, 'term', pairs)]
    pallas_call x2, Pallas kernels: 13 us -> 5.42 us  [apply_blocks(): pl.pallas_call(functools.partial(blocks_kernel, first, shape, entries), i...]
    ppermute x28, waiting for transfers between devices: 18.5 us -> 14.7 us  [hop(): return lax.ppermute(value, 'term', pairs)]
    ppermute x22, starting transfers between devices: 2.42 us -> 4.28 us  [flip(): return lax.ppermute(value, 'term', [(i, i ^ 1) for i in range(16)])]
  transfers between devices with their start and end apart: 50 -> 50, of which waited for: 21 -> 24; matrix products, arithmetic and copies ran while one was open for 1% -> 1% of each run, Pallas kernels for 1% -> 1%
where the time goes in v16:
time: 100 us; the launch traced here: 99.6 us
  starting transfers between devices  64.2 us (64%)
  waiting for transfers between devices  20 us (20%)
  Pallas kernels  7.97 us (8%)
  local copies, waits for them, and re-layouts  5.29 us (5%)
  between operations  1.5 us (2%)
    ppermute x28, starting transfers between devices, hop(): return lax.ppermute(value, 'term', pairs)  59.9 us
    ppermute x28, waiting for transfers between devices, hop(): return lax.ppermute(value, 'term', pairs)  14.7 us
    pallas_call x2, Pallas kernels, apply_blocks(): pl.pallas_call(functools.partial(blocks_kernel, first, shape, entries), i...  5.42 us
    unnamed x14, local copies, waits for them, and re-layouts  5.29 us
    ppermute x22, waiting for transfers between devices, flip(): return lax.ppermute(value, 'term', [(i, i ^ 1) for i in range(16)])  5.26 us
    ppermute x22, starting transfers between devices, flip(): return lax.ppermute(value, 'term', [(i, i ^ 1) for i in range(16)])  4.28 us
  transfers between devices with their start and end apart: 50, of which 24 were waited for; matrix products, arithmetic and copies ran while one was open for 1% of the time, Pallas kernels for 1%

profile of v16, /device:TPU:0, one launch (start us, length us, event | category | flops | bytes accessed | tf_op | source)
XLA Modules:
  0.0 99.6 jit_solution(14513671420977470529)
XLA Ops:
  1.1 2.6 %collective-permute-start.3 = (bf16[3,32,512]{2,1,0:T(8,128)(2,1)}, bf16[3,32,512]{2,1,0:T(8,128)(2,1)S(1)}, u32[]{:S(2)}, u32[]{:S(2)}) collective-permute-start(bf16[3,32,512]{2,1,0:T(8,128)(2,1)} %wave_ref.3), channel_id=1, source_target_pairs={{0,4},{1,3},{4,8},{5,1},{8,12},{9,5},{12,14},{13,9},{14,10},{15,13... | collective-permute-start | bytes 294920 | tf_op jit(solution)/shard_map/ppermute | solution.py:364
  4.4 1.6 %collective-permute-start.1 = (bf16[3,32,512]{2,1,0:T(8,128)(2,1)S(1)}, bf16[3,32,512]{2,1,0:T(8,128)(2,1)S(1)}, u32[]{:S(2)}, u32[]{:S(2)}) collective-permute-start(bf16[3,32,512]{2,1,0:T(8,128)(2,1)S(1)} %collective-permute-done.refs_1_), channel_id=1, source_target_pairs={{0,4},{1,3},{4,8},{5,1},{8,12},{9,5},{12,14},{13,9},{14,10},{15,13... | collective-permute-start | bytes 294920 | tf_op jit(solution)/shard_map/ppermute | solution.py:364
  6.8 1.8 %collective-permute-start.6 = (bf16[3,32,512]{2,1,0:T(8,128)(2,1)S(1)}, bf16[3,32,512]{2,1,0:T(8,128)(2,1)S(1)}, u32[]{:S(2)}, u32[]{:S(2)}) collective-permute-start(bf16[3,32,512]{2,1,0:T(8,128)(2,1)S(1)} %collective-permute-done.3.refs_2_), channel_id=1, source_target_pairs={{0,4},{1,3},{4,8},{5,1},{8,12},{9,5},{12,14},{13,9},{14,10},{15,13... | collective-permute-start | bytes 294920 | tf_op jit(solution)/shard_map/ppermute | solution.py:364
  9.1 1.6 %collective-permute-start.2 = (bf16[3,32,512]{2,1,0:T(8,128)(2,1)S(1)}, bf16[3,32,512]{2,1,0:T(8,128)(2,1)S(1)}, u32[]{:S(2)}, u32[]{:S(2)}) collective-permute-start(bf16[3,32,512]{2,1,0:T(8,128)(2,1)S(1)} %collective-permute-done.1.refs_3_), channel_id=1, source_target_pairs={{0,4},{1,3},{4,8},{5,1},{8,12},{9,5},{12,14},{13,9},{14,10},{15,13... | collective-permute-start | bytes 294920 | tf_op jit(solution)/shard_map/ppermute | solution.py:364
  11.6 2.6 %collective-permute-start.13 = (bf16[3,32,512]{2,1,0:T(8,128)(2,1)S(1)}, bf16[3,32,512]{2,1,0:T(8,128)(2,1)S(1)}, u32[]{:S(2)}, u32[]{:S(2)}) collective-permute-start(bf16[3,32,512]{2,1,0:T(8,128)(2,1)S(1)} %copy-done.1), channel_id=1, source_target_pairs={{0,14},{1,15},{4,10},{5,11},{8,6},{9,7},{12,2},{13,3},{14,0},{15,1... | collective-permute-start | bytes 294920 | tf_op jit(solution)/shard_map/ppermute | solution.py:364
  14.3 1.8 %collective-permute-start.7 = (bf16[3,32,512]{2,1,0:T(8,128)(2,1)S(1)}, bf16[3,32,512]{2,1,0:T(8,128)(2,1)S(1)}, u32[]{:S(2)}, u32[]{:S(2)}) collective-permute-start(bf16[3,32,512]{2,1,0:T(8,128)(2,1)S(1)} %collective-permute-done.6.refs_6_), channel_id=1, source_target_pairs={{0,1},{1,0},{2,3},{3,2},{4,5},{5,4},{6,7},{7,6},{8,9},{9,8},{10,11... | collective-permute-start | bytes 294920 | tf_op jit(solution)/shard_map/ppermute | solution.py:355
  16.5 2.6 %collective-permute-done.13.refs_14_ = bf16[3,32,512]{2,1,0:T(8,128)(2,1)S(1)} collective-permute-done((bf16[3,32,512]{2,1,0:T(8,128)(2,1)S(1)}, bf16[3,32,512]{2,1,0:T(8,128)(2,1)S(1)}, u32[]{:S(2)}, u32[]{:S(2)}) %collective-permute-start.13) | collective-permute-done | bytes 98336 | tf_op jit(solution)/shard_map/ppermute | solution.py:364
  22.3 2.2 %copy-done.3 = bf16[8,512,512]{2,1,0:T(8,128)(2,1)S(1)} copy-done((bf16[8,512,512]{2,1,0:T(8,128)(2,1)S(1)}, bf16[8,512,512]{2,1,0:T(8,128)(2,1)}, u32[]{:S(2)}) %copy-start.3) | copy-done | bytes 4194328
  24.5 2.2 %copy-done.5 = bf16[8,512,512]{2,1,0:T(8,128)(2,1)S(1)} copy-done((bf16[8,512,512]{2,1,0:T(8,128)(2,1)S(1)}, bf16[8,512,512]{2,1,0:T(8,128)(2,1)}, u32[]{:S(2)}) %copy-start.5) | copy-done | bytes 4194328
  26.7 3.0 %shard_map.96 = (f32[3,512,512]{2,1,0:T(8,128)S(1)}, bf16[2,16,3200]{2,1,0:T(8,128)(2,1)S(1)}, bf16[6,16,3200]{2,1,0:T(8,128)(2,1)S(1)}, f32[8,128]{1,0:T(8,128)S(1)}, f32[8,128]{1,0:T(8,128)S(1)}) custom-call(s32[1]{0:T(128)} %bitcast.me_ref.refs_0_.refs_2_, s32[17]{0:T(128)S(1)} %pad_add_fusion.ints_ref, ...), custom_call_target="tpu_custom_call" | custom-call | flops 4294967296 | bytes 8388608 | tf_op jit(solution)/shard_map/pallas_call | solution.py:225
  29.9 1.3 %collective-permute-done.15.other_ref = bf16[2,16,3200]{2,1,0:T(8,128)(2,1)S(1)} collective-permute-done((bf16[2,16,3200]{2,1,0:T(8,128)(2,1)S(1)}, bf16[2,16,3200]{2,1,0:T(8,128)(2,1)S(1)}, u32[]{:S(2)}, u32[]{:S(2)}) %collective-permute-start.15) | collective-permute-done | bytes 204832 | tf_op jit(solution)/shard_map/ppermute | solution.py:355
  31.4 2.1 %collective-permute-start.20 = (bf16[16,3200]{1,0:T(8,128)(2,1)S(1)}, bf16[16,3200]{1,0:T(8,128)(2,1)S(1)}, u32[]{:S(2)}, u32[]{:S(2)}) collective-permute-start(bf16[16,3200]{1,0:T(8,128)(2,1)S(1)} %shard_map.100), channel_id=1, source_target_pairs={{0,4},{1,3},{4,8},{5,1},{8,12},{9,5},{12,14},{13,9},{14,10},{15,13... | collective-permute-start | bytes 307208 | tf_op jit(solution)/shard_map/ppermute | solution.py:364
  33.5 4.0 %collective-permute-start.17 = (bf16[16,3200]{1,0:T(8,128)(2,1)S(1)}, bf16[16,3200]{1,0:T(8,128)(2,1)S(1)}, u32[]{:S(2)}, u32[]{:S(2)}) collective-permute-start(bf16[16,3200]{1,0:T(8,128)(2,1)S(1)} %shard_map.97), channel_id=1, source_target_pairs={{0,4},{1,3},{4,8},{5,1},{8,12},{9,5},{12,14},{13,9},{14,10},{15,13... | collective-permute-start | bytes 307208 | tf_op jit(solution)/shard_map/ppermute | solution.py:364
  37.6 1.8 %collective-permute-start.22 = (bf16[16,3200]{1,0:T(8,128)(2,1)S(1)}, bf16[16,3200]{1,0:T(8,128)(2,1)S(1)}, u32[]{:S(2)}, u32[]{:S(2)}) collective-permute-start(bf16[16,3200]{1,0:T(8,128)(2,1)S(1)} %shard_map.102), channel_id=1, source_target_pairs={{0,14},{1,15},{4,10},{5,11},{8,6},{9,7},{12,2},{13,3},{14,0},{15,1... | collective-permute-start | bytes 307208 | tf_op jit(solution)/shard_map/ppermute | solution.py:364
  39.9 4.1 %collective-permute-start.18 = (bf16[16,3200]{1,0:T(8,128)(2,1)S(1)}, bf16[16,3200]{1,0:T(8,128)(2,1)S(1)}, u32[]{:S(2)}, u32[]{:S(2)}) collective-permute-start(bf16[16,3200]{1,0:T(8,128)(2,1)S(1)} %shard_map.98), channel_id=1, source_target_pairs={{0,4},{1,3},{4,8},{5,1},{8,12},{9,5},{12,14},{13,9},{14,10},{15,13... | collective-permute-start | bytes 307208 | tf_op jit(solution)/shard_map/ppermute | solution.py:364
  46.8 2.4 %collective-permute-start.19 = (bf16[16,3200]{1,0:T(8,128)(2,1)S(1)}, bf16[16,3200]{1,0:T(8,128)(2,1)S(1)}, u32[]{:S(2)}, u32[]{:S(2)}) collective-permute-start(bf16[16,3200]{1,0:T(8,128)(2,1)S(1)} %shard_map.99), channel_id=1, source_target_pairs={{0,4},{1,3},{4,8},{5,1},{8,12},{9,5},{12,14},{13,9},{14,10},{15,13... | collective-permute-start | bytes 307208 | tf_op jit(solution)/shard_map/ppermute | solution.py:364
  52.7 2.2 %collective-permute-start.26 = (bf16[16,3200]{1,0:T(8,128)(2,1)S(1)}, bf16[16,3200]{1,0:T(8,128)(2,1)S(1)}, u32[]{:S(2)}, u32[]{:S(2)}) collective-permute-start(bf16[16,3200]{1,0:T(8,128)(2,1)S(1)} %get-tuple-element.53.refs_0_), channel_id=1, source_target_pairs={{0,4},{1,3},{4,8},{5,1},{8,12},{9,5},{12,14},{13,9},{14,10},{15,13... | collective-permute-start | bytes 307208 | tf_op jit(solution)/shard_map/ppermute | solution.py:364
  54.8 2.1 %collective-permute-start.27 = (bf16[16,3200]{1,0:T(8,128)(2,1)S(1)}, bf16[16,3200]{1,0:T(8,128)(2,1)S(1)}, u32[]{:S(2)}, u32[]{:S(2)}) collective-permute-start(bf16[16,3200]{1,0:T(8,128)(2,1)S(1)} %collective-permute-done.25.refs_1_), channel_id=1, source_target_pairs={{0,4},{1,3},{4,8},{5,1},{8,12},{9,5},{12,14},{13,9},{14,10},{15,13... | collective-permute-start | bytes 307208 | tf_op jit(solution)/shard_map/ppermute | solution.py:364
  57.3 2.2 %collective-permute-start.30 = (bf16[16,3200]{1,0:T(8,128)(2,1)S(1)}, bf16[16,3200]{1,0:T(8,128)(2,1)S(1)}, u32[]{:S(2)}, u32[]{:S(2)}) collective-permute-start(bf16[16,3200]{1,0:T(8,128)(2,1)S(1)} %collective-permute-done.26.refs_2_), channel_id=1, source_target_pairs={{0,4},{1,3},{4,8},{5,1},{8,12},{9,5},{12,14},{13,9},{14,10},{15,13... | collective-permute-start | bytes 307208 | tf_op jit(solution)/shard_map/ppermute | solution.py:364
  59.5 2.1 %collective-permute-start.31 = (bf16[16,3200]{1,0:T(8,128)(2,1)S(1)}, bf16[16,3200]{1,0:T(8,128)(2,1)S(1)}, u32[]{:S(2)}, u32[]{:S(2)}) collective-permute-start(bf16[16,3200]{1,0:T(8,128)(2,1)S(1)} %collective-permute-done.27.refs_3_), channel_id=1, source_target_pairs={{0,4},{1,3},{4,8},{5,1},{8,12},{9,5},{12,14},{13,9},{14,10},{15,13... | collective-permute-start | bytes 307208 | tf_op jit(solution)/shard_map/ppermute | solution.py:364
  61.6 1.5 %collective-permute-start.38 = (bf16[16,3200]{1,0:T(8,128)(2,1)S(1)}, bf16[16,3200]{1,0:T(8,128)(2,1)S(1)}, u32[]{:S(2)}, u32[]{:S(2)}) collective-permute-start(bf16[16,3200]{1,0:T(8,128)(2,1)S(1)} %get-tuple-element.53.refs_0_), channel_id=1, source_target_pairs={{0,14},{1,15},{4,10},{5,11},{8,6},{9,7},{12,2},{13,3},{14,0},{15,1... | collective-permute-start | bytes 307208 | tf_op jit(solution)/shard_map/ppermute | solution.py:364
  64.3 3.9 %collective-permute-start.35 = (bf16[16,3200]{1,0:T(8,128)(2,1)S(1)}, bf16[16,3200]{1,0:T(8,128)(2,1)S(1)}, u32[]{:S(2)}, u32[]{:S(2)}) collective-permute-start(bf16[16,3200]{1,0:T(8,128)(2,1)S(1)} %collective-permute-done.31.refs_7_), channel_id=1, source_target_pairs={{0,4},{1,3},{4,8},{5,1},{8,12},{9,5},{12,14},{13,9},{14,10},{15,13... | collective-permute-start | bytes 307208 | tf_op jit(solution)/shard_map/ppermute | solution.py:364
  68.2 1.7 %collective-permute-done.38.refs_14_ = bf16[16,3200]{1,0:T(8,128)(2,1)S(1)} collective-permute-done((bf16[16,3200]{1,0:T(8,128)(2,1)S(1)}, bf16[16,3200]{1,0:T(8,128)(2,1)S(1)}, u32[]{:S(2)}, u32[]{:S(2)}) %collective-permute-start.38) | collective-permute-done | bytes 102432 | tf_op jit(solution)/shard_map/ppermute | solution.py:364
  72.3 2.4 %shard_map.105 = (f32[3,512,512]{2,1,0:T(8,128)S(1)}, bf16[2,16,3200]{2,1,0:T(8,128)(2,1)S(1)}, bf16[6,16,3200]{2,1,0:T(8,128)(2,1)S(1)}, f32[8,128]{1,0:T(8,128)S(1)}, f32[8,128]{1,0:T(8,128)S(1)}) custom-call(s32[1]{0:T(128)} %bitcast.me_ref.refs_0_.refs_2_, s32[17]{0:T(128)S(1)} %pad_add_fusion.ints_ref, bf16[16,3200]{1,0:T(8,128)(2,1)S(1)} %get-tuple-element.53.refs_0_, ...), custom_call_target="tpu_custom_call" | custom-call | flops 4294967296 | bytes 8388608 | tf_op jit(solution)/shard_map/pallas_call | solution.py:225
  74.9 1.3 %collective-permute-done.40.other_ref = bf16[2,16,3200]{2,1,0:T(8,128)(2,1)S(1)} collective-permute-done((bf16[2,16,3200]{2,1,0:T(8,128)(2,1)S(1)}, bf16[2,16,3200]{2,1,0:T(8,128)(2,1)S(1)}, u32[]{:S(2)}, u32[]{:S(2)}) %collective-permute-start.40) | collective-permute-done | bytes 204832 | tf_op jit(solution)/shard_map/ppermute | solution.py:355
  76.4 3.2 %collective-permute-start.45 = (bf16[16,3200]{1,0:T(8,128)(2,1)S(1)}, bf16[16,3200]{1,0:T(8,128)(2,1)S(1)}, u32[]{:S(2)}, u32[]{:S(2)}) collective-permute-start(bf16[16,3200]{1,0:T(8,128)(2,1)S(1)} %shard_map.109), channel_id=1, source_target_pairs={{0,4},{1,3},{4,8},{5,1},{8,12},{9,5},{12,14},{13,9},{14,10},{15,13... | collective-permute-start | bytes 307208 | tf_op jit(solution)/shard_map/ppermute | solution.py:364
  79.7 5.0 %collective-permute-start.42 = (bf16[16,3200]{1,0:T(8,128)(2,1)S(1)}, bf16[16,3200]{1,0:T(8,128)(2,1)S(1)}, u32[]{:S(2)}, u32[]{:S(2)}) collective-permute-start(bf16[16,3200]{1,0:T(8,128)(2,1)S(1)} %shard_map.106), channel_id=1, source_target_pairs={{0,4},{1,3},{4,8},{5,1},{8,12},{9,5},{12,14},{13,9},{14,10},{15,13... | collective-permute-start | bytes 307208 | tf_op jit(solution)/shard_map/ppermute | solution.py:364
  86.0 1.6 %collective-permute-start.46 = (bf16[16,3200]{1,0:T(8,128)(2,1)S(1)}, bf16[16,3200]{1,0:T(8,128)(2,1)S(1)}, u32[]{:S(2)}, u32[]{:S(2)}) collective-permute-start(bf16[16,3200]{1,0:T(8,128)(2,1)S(1)} %shard_map.110), channel_id=1, source_target_pairs={{0,4},{1,3},{4,8},{5,1},{8,12},{9,5},{12,14},{13,9},{14,10},{15,13... | collective-permute-start | bytes 307208 | tf_op jit(solution)/shard_map/ppermute | solution.py:364
  87.6 3.7 %collective-permute-start.43 = (bf16[16,3200]{1,0:T(8,128)(2,1)S(1)}, bf16[16,3200]{1,0:T(8,128)(2,1)S(1)}, u32[]{:S(2)}, u32[]{:S(2)}) collective-permute-start(bf16[16,3200]{1,0:T(8,128)(2,1)S(1)} %shard_map.107), channel_id=1, source_target_pairs={{0,4},{1,3},{4,8},{5,1},{8,12},{9,5},{12,14},{13,9},{14,10},{15,13... | collective-permute-start | bytes 307208 | tf_op jit(solution)/shard_map/ppermute | solution.py:364
  92.5 1.4 %collective-permute-start.48 = (bf16[16,3200]{1,0:T(8,128)(2,1)S(1)}, bf16[16,3200]{1,0:T(8,128)(2,1)S(1)}, u32[]{:S(2)}, u32[]{:S(2)}) collective-permute-start(bf16[16,3200]{1,0:T(8,128)(2,1)S(1)} %shard_map.112), channel_id=1, source_target_pairs={{0,4},{1,3},{4,8},{5,1},{8,12},{9,5},{12,14},{13,9},{14,10},{15,13... | collective-permute-start | bytes 307208 | tf_op jit(solution)/shard_map/ppermute | solution.py:364
  94.0 2.2 %collective-permute-start.44 = (bf16[16,3200]{1,0:T(8,128)(2,1)S(1)}, bf16[16,3200]{1,0:T(8,128)(2,1)S(1)}, u32[]{:S(2)}, u32[]{:S(2)}) collective-permute-start(bf16[16,3200]{1,0:T(8,128)(2,1)S(1)} %shard_map.108), channel_id=1, source_target_pairs={{0,4},{1,3},{4,8},{5,1},{8,12},{9,5},{12,14},{13,9},{14,10},{15,13... | collective-permute-start | bytes 307208 | tf_op jit(solution)/shard_map/ppermute | solution.py:364
  97.2 1.5 %collective-permute-done.44.refs_6_ = bf16[16,3200]{1,0:T(8,128)(2,1)S(1)} collective-permute-done((bf16[16,3200]{1,0:T(8,128)(2,1)S(1)}, bf16[16,3200]{1,0:T(8,128)(2,1)S(1)}, u32[]{:S(2)}, u32[]{:S(2)}) %collective-permute-start.44) | collective-permute-done | bytes 102432 | tf_op jit(solution)/shard_map/ppermute | solution.py:364
  (103 shorter events, 22.4 us)
Async XLA Ops:
  1.1 5.7 %collective-permute-start.3 = (bf16[3,32,512]{2,1,0:T(8,128)(2,1)}, bf16[3,32,512]{2,1,0:T(8,128)(2,1)S(1)}, u32[]{:S(2)}, u32[]{:S(2)}) collective-permute-start(bf16[3,32,512]{2,1,0:T(8,128)(2,1)} %wave_ref.3), channel_id=1, source_target_pairs={{0,4},{1,3},{4,8},{5,1},{8,12},{9,5},{12,14},{13,9},{14,10},{15,13... | collective-permute-start | bytes 294920 | tf_op jit(solution)/shard_map/ppermute | solution.py:364
  4.4 4.7 %collective-permute-start.1 = (bf16[3,32,512]{2,1,0:T(8,128)(2,1)S(1)}, bf16[3,32,512]{2,1,0:T(8,128)(2,1)S(1)}, u32[]{:S(2)}, u32[]{:S(2)}) collective-permute-start(bf16[3,32,512]{2,1,0:T(8,128)(2,1)S(1)} %collective-permute-done.refs_1_), channel_id=1, source_target_pairs={{0,4},{1,3},{4,8},{5,1},{8,12},{9,5},{12,14},{13,9},{14,10},{15,13... | collective-permute-start | bytes 294920 | tf_op jit(solution)/shard_map/ppermute | solution.py:364
  6.8 7.4 %collective-permute-start.6 = (bf16[3,32,512]{2,1,0:T(8,128)(2,1)S(1)}, bf16[3,32,512]{2,1,0:T(8,128)(2,1)S(1)}, u32[]{:S(2)}, u32[]{:S(2)}) collective-permute-start(bf16[3,32,512]{2,1,0:T(8,128)(2,1)S(1)} %collective-permute-done.3.refs_2_), channel_id=1, source_target_pairs={{0,4},{1,3},{4,8},{5,1},{8,12},{9,5},{12,14},{13,9},{14,10},{15,13... | collective-permute-start | bytes 294920 | tf_op jit(solution)/shard_map/ppermute | solution.py:364
  9.1 6.9 %collective-permute-start.2 = (bf16[3,32,512]{2,1,0:T(8,128)(2,1)S(1)}, bf16[3,32,512]{2,1,0:T(8,128)(2,1)S(1)}, u32[]{:S(2)}, u32[]{:S(2)}) collective-permute-start(bf16[3,32,512]{2,1,0:T(8,128)(2,1)S(1)} %collective-permute-done.1.refs_3_), channel_id=1, source_target_pairs={{0,4},{1,3},{4,8},{5,1},{8,12},{9,5},{12,14},{13,9},{14,10},{15,13... | collective-permute-start | bytes 294920 | tf_op jit(solution)/shard_map/ppermute | solution.py:364
  11.6 7.5 %collective-permute-start.13 = (bf16[3,32,512]{2,1,0:T(8,128)(2,1)S(1)}, bf16[3,32,512]{2,1,0:T(8,128)(2,1)S(1)}, u32[]{:S(2)}, u32[]{:S(2)}) collective-permute-start(bf16[3,32,512]{2,1,0:T(8,128)(2,1)S(1)} %copy-done.1), channel_id=1, source_target_pairs={{0,14},{1,15},{4,10},{5,11},{8,6},{9,7},{12,2},{13,3},{14,0},{15,1... | collective-permute-start | bytes 294920 | tf_op jit(solution)/shard_map/ppermute | solution.py:364
  14.2 5.7 %collective-permute-start.9 = (bf16[3,32,512]{2,1,0:T(8,128)(2,1)S(1)}, bf16[3,32,512]{2,1,0:T(8,128)(2,1)S(1)}, u32[]{:S(2)}, u32[]{:S(2)}) collective-permute-start(bf16[3,32,512]{2,1,0:T(8,128)(2,1)S(1)} %collective-permute-done.6.refs_6_), channel_id=1, source_target_pairs={{0,4},{1,3},{4,8},{5,1},{8,12},{9,5},{12,14},{13,9},{14,10},{15,13... | collective-permute-start | bytes 294920 | tf_op jit(solution)/shard_map/ppermute | solution.py:364
  14.3 5.7 %collective-permute-start.7 = (bf16[3,32,512]{2,1,0:T(8,128)(2,1)S(1)}, bf16[3,32,512]{2,1,0:T(8,128)(2,1)S(1)}, u32[]{:S(2)}, u32[]{:S(2)}) collective-permute-start(bf16[3,32,512]{2,1,0:T(8,128)(2,1)S(1)} %collective-permute-done.6.refs_6_), channel_id=1, source_target_pairs={{0,1},{1,0},{2,3},{3,2},{4,5},{5,4},{6,7},{7,6},{8,9},{9,8},{10,11... | collective-permute-start | bytes 294920 | tf_op jit(solution)/shard_map/ppermute | solution.py:355
  16.1 4.9 %collective-permute-start.10 = (bf16[3,32,512]{2,1,0:T(8,128)(2,1)S(1)}, bf16[3,32,512]{2,1,0:T(8,128)(2,1)S(1)}, u32[]{:S(2)}, u32[]{:S(2)}) collective-permute-start(bf16[3,32,512]{2,1,0:T(8,128)(2,1)S(1)} %collective-permute-done.2.refs_7_), channel_id=1, source_target_pairs={{0,4},{1,3},{4,8},{5,1},{8,12},{9,5},{12,14},{13,9},{14,10},{15,13... | collective-permute-start | bytes 294920 | tf_op jit(solution)/shard_map/ppermute | solution.py:364
  31.2 6.4 %collective-permute-start.16 = (bf16[6,16,3200]{2,1,0:T(8,128)(2,1)S(1)}, bf16[6,16,3200]{2,1,0:T(8,128)(2,1)S(1)}, u32[]{:S(2)}, u32[]{:S(2)}) collective-permute-start(bf16[6,16,3200]{2,1,0:T(8,128)(2,1)S(1)} %get-tuple-element.45), channel_id=1, source_target_pairs={{0,1},{1,0},{2,3},{3,2},{4,5},{5,4},{6,7},{7,6},{8,9},{9,8},{10,11... | collective-permute-start | bytes 1843208 | tf_op jit(solution)/shard_map/ppermute | solution.py:355
  31.4 8.0 %collective-permute-start.20 = (bf16[16,3200]{1,0:T(8,128)(2,1)S(1)}, bf16[16,3200]{1,0:T(8,128)(2,1)S(1)}, u32[]{:S(2)}, u32[]{:S(2)}) collective-permute-start(bf16[16,3200]{1,0:T(8,128)(2,1)S(1)} %shard_map.100), channel_id=1, source_target_pairs={{0,4},{1,3},{4,8},{5,1},{8,12},{9,5},{12,14},{13,9},{14,10},{15,13... | collective-permute-start | bytes 307208 | tf_op jit(solution)/shard_map/ppermute | solution.py:364
  33.5 6.3 %collective-permute-start.17 = (bf16[16,3200]{1,0:T(8,128)(2,1)S(1)}, bf16[16,3200]{1,0:T(8,128)(2,1)S(1)}, u32[]{:S(2)}, u32[]{:S(2)}) collective-permute-start(bf16[16,3200]{1,0:T(8,128)(2,1)S(1)} %shard_map.97), channel_id=1, source_target_pairs={{0,4},{1,3},{4,8},{5,1},{8,12},{9,5},{12,14},{13,9},{14,10},{15,13... | collective-permute-start | bytes 307208 | tf_op jit(solution)/shard_map/ppermute | solution.py:364
  37.6 7.6 %collective-permute-start.22 = (bf16[16,3200]{1,0:T(8,128)(2,1)S(1)}, bf16[16,3200]{1,0:T(8,128)(2,1)S(1)}, u32[]{:S(2)}, u32[]{:S(2)}) collective-permute-start(bf16[16,3200]{1,0:T(8,128)(2,1)S(1)} %shard_map.102), channel_id=1, source_target_pairs={{0,14},{1,15},{4,10},{5,11},{8,6},{9,7},{12,2},{13,3},{14,0},{15,1... | collective-permute-start | bytes 307208 | tf_op jit(solution)/shard_map/ppermute | solution.py:364
  39.5 6.1 %collective-permute-start.21 = (bf16[16,3200]{1,0:T(8,128)(2,1)S(1)}, bf16[16,3200]{1,0:T(8,128)(2,1)S(1)}, u32[]{:S(2)}, u32[]{:S(2)}) collective-permute-start(bf16[16,3200]{1,0:T(8,128)(2,1)S(1)} %shard_map.101), channel_id=1, source_target_pairs={{0,4},{1,3},{4,8},{5,1},{8,12},{9,5},{12,14},{13,9},{14,10},{15,13... | collective-permute-start | bytes 307208 | tf_op jit(solution)/shard_map/ppermute | solution.py:364
  39.9 6.8 %collective-permute-start.18 = (bf16[16,3200]{1,0:T(8,128)(2,1)S(1)}, bf16[16,3200]{1,0:T(8,128)(2,1)S(1)}, u32[]{:S(2)}, u32[]{:S(2)}) collective-permute-start(bf16[16,3200]{1,0:T(8,128)(2,1)S(1)} %shard_map.98), channel_id=1, source_target_pairs={{0,4},{1,3},{4,8},{5,1},{8,12},{9,5},{12,14},{13,9},{14,10},{15,13... | collective-permute-start | bytes 307208 | tf_op jit(solution)/shard_map/ppermute | solution.py:364
  45.6 4.7 %collective-permute-start.23 = (bf16[16,3200]{1,0:T(8,128)(2,1)S(1)}, bf16[16,3200]{1,0:T(8,128)(2,1)S(1)}, u32[]{:S(2)}, u32[]{:S(2)}) collective-permute-start(bf16[16,3200]{1,0:T(8,128)(2,1)S(1)} %shard_map.103), channel_id=1, source_target_pairs={{0,4},{1,3},{4,8},{5,1},{8,12},{9,5},{12,14},{13,9},{14,10},{15,13... | collective-permute-start | bytes 307208 | tf_op jit(solution)/shard_map/ppermute | solution.py:364
  46.8 4.7 %collective-permute-start.19 = (bf16[16,3200]{1,0:T(8,128)(2,1)S(1)}, bf16[16,3200]{1,0:T(8,128)(2,1)S(1)}, u32[]{:S(2)}, u32[]{:S(2)}) collective-permute-start(bf16[16,3200]{1,0:T(8,128)(2,1)S(1)} %shard_map.99), channel_id=1, source_target_pairs={{0,4},{1,3},{4,8},{5,1},{8,12},{9,5},{12,14},{13,9},{14,10},{15,13... | collective-permute-start | bytes 307208 | tf_op jit(solution)/shard_map/ppermute | solution.py:364
  54.8 4.7 %collective-permute-start.27 = (bf16[16,3200]{1,0:T(8,128)(2,1)S(1)}, bf16[16,3200]{1,0:T(8,128)(2,1)S(1)}, u32[]{:S(2)}, u32[]{:S(2)}) collective-permute-start(bf16[16,3200]{1,0:T(8,128)(2,1)S(1)} %collective-permute-done.25.refs_1_), channel_id=1, source_target_pairs={{0,4},{1,3},{4,8},{5,1},{8,12},{9,5},{12,14},{13,9},{14,10},{15,13... | collective-permute-start | bytes 307208 | tf_op jit(solution)/shard_map/ppermute | solution.py:364
  57.3 5.7 %collective-permute-start.30 = (bf16[16,3200]{1,0:T(8,128)(2,1)S(1)}, bf16[16,3200]{1,0:T(8,128)(2,1)S(1)}, u32[]{:S(2)}, u32[]{:S(2)}) collective-permute-start(bf16[16,3200]{1,0:T(8,128)(2,1)S(1)} %collective-permute-done.26.refs_2_), channel_id=1, source_target_pairs={{0,4},{1,3},{4,8},{5,1},{8,12},{9,5},{12,14},{13,9},{14,10},{15,13... | collective-permute-start | bytes 307208 | tf_op jit(solution)/shard_map/ppermute | solution.py:364
  59.5 4.8 %collective-permute-start.31 = (bf16[16,3200]{1,0:T(8,128)(2,1)S(1)}, bf16[16,3200]{1,0:T(8,128)(2,1)S(1)}, u32[]{:S(2)}, u32[]{:S(2)}) collective-permute-start(bf16[16,3200]{1,0:T(8,128)(2,1)S(1)} %collective-permute-done.27.refs_3_), channel_id=1, source_target_pairs={{0,4},{1,3},{4,8},{5,1},{8,12},{9,5},{12,14},{13,9},{14,10},{15,13... | collective-permute-start | bytes 307208 | tf_op jit(solution)/shard_map/ppermute | solution.py:364
  61.6 6.6 %collective-permute-start.28 = (bf16[16,3200]{1,0:T(8,128)(2,1)S(1)}, bf16[16,3200]{1,0:T(8,128)(2,1)S(1)}, u32[]{:S(2)}, u32[]{:S(2)}) collective-permute-start(bf16[16,3200]{1,0:T(8,128)(2,1)S(1)} %collective-permute-done.26.refs_2_), channel_id=1, source_target_pairs={{0,1},{1,0},{2,3},{3,2},{4,5},{5,4},{6,7},{7,6},{8,9},{9,8},{10,11... | collective-permute-start | bytes 307208 | tf_op jit(solution)/shard_map/ppermute | solution.py:355
  61.6 8.3 %collective-permute-start.38 = (bf16[16,3200]{1,0:T(8,128)(2,1)S(1)}, bf16[16,3200]{1,0:T(8,128)(2,1)S(1)}, u32[]{:S(2)}, u32[]{:S(2)}) collective-permute-start(bf16[16,3200]{1,0:T(8,128)(2,1)S(1)} %get-tuple-element.53.refs_0_), channel_id=1, source_target_pairs={{0,14},{1,15},{4,10},{5,11},{8,6},{9,7},{12,2},{13,3},{14,0},{15,1... | collective-permute-start | bytes 307208 | tf_op jit(solution)/shard_map/ppermute | solution.py:364
  63.1 6.9 %collective-permute-start.34 = (bf16[16,3200]{1,0:T(8,128)(2,1)S(1)}, bf16[16,3200]{1,0:T(8,128)(2,1)S(1)}, u32[]{:S(2)}, u32[]{:S(2)}) collective-permute-start(bf16[16,3200]{1,0:T(8,128)(2,1)S(1)} %collective-permute-done.30.refs_6_), channel_id=1, source_target_pairs={{0,4},{1,3},{4,8},{5,1},{8,12},{9,5},{12,14},{13,9},{14,10},{15,13... | collective-permute-start | bytes 307208 | tf_op jit(solution)/shard_map/ppermute | solution.py:364
  64.1 6.2 %collective-permute-start.32 = (bf16[16,3200]{1,0:T(8,128)(2,1)S(1)}, bf16[16,3200]{1,0:T(8,128)(2,1)S(1)}, u32[]{:S(2)}, u32[]{:S(2)}) collective-permute-start(bf16[16,3200]{1,0:T(8,128)(2,1)S(1)} %collective-permute-done.30.refs_6_), channel_id=1, source_target_pairs={{0,1},{1,0},{2,3},{3,2},{4,5},{5,4},{6,7},{7,6},{8,9},{9,8},{10,11... | collective-permute-start | bytes 307208 | tf_op jit(solution)/shard_map/ppermute | solution.py:355
  64.3 6.7 %collective-permute-start.35 = (bf16[16,3200]{1,0:T(8,128)(2,1)S(1)}, bf16[16,3200]{1,0:T(8,128)(2,1)S(1)}, u32[]{:S(2)}, u32[]{:S(2)}) collective-permute-start(bf16[16,3200]{1,0:T(8,128)(2,1)S(1)} %collective-permute-done.31.refs_7_), channel_id=1, source_target_pairs={{0,4},{1,3},{4,8},{5,1},{8,12},{9,5},{12,14},{13,9},{14,10},{15,13... | collective-permute-start | bytes 307208 | tf_op jit(solution)/shard_map/ppermute | solution.py:364
  76.2 8.5 %collective-permute-start.41 = (bf16[6,16,3200]{2,1,0:T(8,128)(2,1)S(1)}, bf16[6,16,3200]{2,1,0:T(8,128)(2,1)S(1)}, u32[]{:S(2)}, u32[]{:S(2)}) collective-permute-start(bf16[6,16,3200]{2,1,0:T(8,128)(2,1)S(1)} %get-tuple-element.60), channel_id=1, source_target_pairs={{0,1},{1,0},{2,3},{3,2},{4,5},{5,4},{6,7},{7,6},{8,9},{9,8},{10,11... | collective-permute-start | bytes 1843208 | tf_op jit(solution)/shard_map/ppermute | solution.py:355
  76.4 9.4 %collective-permute-start.45 = (bf16[16,3200]{1,0:T(8,128)(2,1)S(1)}, bf16[16,3200]{1,0:T(8,128)(2,1)S(1)}, u32[]{:S(2)}, u32[]{:S(2)}) collective-permute-start(bf16[16,3200]{1,0:T(8,128)(2,1)S(1)} %shard_map.109), channel_id=1, source_target_pairs={{0,4},{1,3},{4,8},{5,1},{8,12},{9,5},{12,14},{13,9},{14,10},{15,13... | collective-permute-start | bytes 307208 | tf_op jit(solution)/shard_map/ppermute | solution.py:364
  79.7 7.8 %collective-permute-start.42 = (bf16[16,3200]{1,0:T(8,128)(2,1)S(1)}, bf16[16,3200]{1,0:T(8,128)(2,1)S(1)}, u32[]{:S(2)}, u32[]{:S(2)}) collective-permute-start(bf16[16,3200]{1,0:T(8,128)(2,1)S(1)} %shard_map.106), channel_id=1, source_target_pairs={{0,4},{1,3},{4,8},{5,1},{8,12},{9,5},{12,14},{13,9},{14,10},{15,13... | collective-permute-start | bytes 307208 | tf_op jit(solution)/shard_map/ppermute | solution.py:364
  84.8 7.6 %collective-permute-start.47 = (bf16[16,3200]{1,0:T(8,128)(2,1)S(1)}, bf16[16,3200]{1,0:T(8,128)(2,1)S(1)}, u32[]{:S(2)}, u32[]{:S(2)}) collective-permute-start(bf16[16,3200]{1,0:T(8,128)(2,1)S(1)} %shard_map.111), channel_id=1, source_target_pairs={{0,14},{1,15},{4,10},{5,11},{8,6},{9,7},{12,2},{13,3},{14,0},{15,1... | collective-permute-start | bytes 307208 | tf_op jit(solution)/shard_map/ppermute | solution.py:364
  86.0 6.4 %collective-permute-start.46 = (bf16[16,3200]{1,0:T(8,128)(2,1)S(1)}, bf16[16,3200]{1,0:T(8,128)(2,1)S(1)}, u32[]{:S(2)}, u32[]{:S(2)}) collective-permute-start(bf16[16,3200]{1,0:T(8,128)(2,1)S(1)} %shard_map.110), channel_id=1, source_target_pairs={{0,4},{1,3},{4,8},{5,1},{8,12},{9,5},{12,14},{13,9},{14,10},{15,13... | collective-permute-start | bytes 307208 | tf_op jit(solution)/shard_map/ppermute | solution.py:364
  87.6 6.3 %collective-permute-start.43 = (bf16[16,3200]{1,0:T(8,128)(2,1)S(1)}, bf16[16,3200]{1,0:T(8,128)(2,1)S(1)}, u32[]{:S(2)}, u32[]{:S(2)}) collective-permute-start(bf16[16,3200]{1,0:T(8,128)(2,1)S(1)} %shard_map.107), channel_id=1, source_target_pairs={{0,4},{1,3},{4,8},{5,1},{8,12},{9,5},{12,14},{13,9},{14,10},{15,13... | collective-permute-start | bytes 307208 | tf_op jit(solution)/shard_map/ppermute | solution.py:364
  92.5 4.7 %collective-permute-start.48 = (bf16[16,3200]{1,0:T(8,128)(2,1)S(1)}, bf16[16,3200]{1,0:T(8,128)(2,1)S(1)}, u32[]{:S(2)}, u32[]{:S(2)}) collective-permute-start(bf16[16,3200]{1,0:T(8,128)(2,1)S(1)} %shard_map.112), channel_id=1, source_target_pairs={{0,4},{1,3},{4,8},{5,1},{8,12},{9,5},{12,14},{13,9},{14,10},{15,13... | collective-permute-start | bytes 307208 | tf_op jit(solution)/shard_map/ppermute | solution.py:364
  94.0 4.7 %collective-permute-start.44 = (bf16[16,3200]{1,0:T(8,128)(2,1)S(1)}, bf16[16,3200]{1,0:T(8,128)(2,1)S(1)}, u32[]{:S(2)}, u32[]{:S(2)}) collective-permute-start(bf16[16,3200]{1,0:T(8,128)(2,1)S(1)} %shard_map.108), channel_id=1, source_target_pairs={{0,4},{1,3},{4,8},{5,1},{8,12},{9,5},{12,14},{13,9},{14,10},{15,13... | collective-permute-start | bytes 307208 | tf_op jit(solution)/shard_map/ppermute | solution.py:364
  (25 other events, 122.9 us)

commit v17 on v14

--- a/solution.py
+++ b/solution.py
@@ -105,6 +105,7 @@
         out_specs=VMEM,
         out_shape=jax.ShapeDtypeStruct(value.shape, value.dtype),
         compiler_params=PARAMS,
+        cost_estimate=pl.CostEstimate(flops=8 << 30, bytes_accessed=1 << 20, transcendentals=0),
     )(value)
 
 
@@ -145,7 +146,7 @@
                 pltpu.make_async_copy(right_in.at[slot], right.at[slot], right_sem.at[slot]),
             )
 
-        for slot in range(slots):
+        for slot in range(GROUP):
             for copy in copies(slot):
                 copy.start()
     else:
@@ -170,6 +171,9 @@
         for k, part, _, _ in pieces:
             value = field_refs[k][part].astype(jnp.float32)
             dot += fold(value * value)
+        for slot in range(GROUP, slots):
+            for copy in copies(slot):
+                copy.start()
         scale = jnp.sqrt(jnp.sum(dot) / entries)
         inverse = 1.0 / scale
         out_ref[...] = jnp.full(out_ref.shape, scale, jnp.float32)

time: 97 us -> 96.6 us (level)
  Pallas kernels: 10.1 us -> 17.2 us
  starting transfers between devices: 57.6 us -> 50.7 us
    ppermute x22, starting transfers between devices: 11.8 us -> 3.95 us  [flip(): return lax.ppermute(value, 'term', [(i, i ^ 1) for i in range(16)])]
    pallas_call x2, Pallas kernels: 7.54 us -> 14.6 us  [apply_blocks(): pl.pallas_call(functools.partial(blocks_kernel, first, shape, entries), i...]
    ppermute x28, waiting for transfers between devices: 19.6 us -> 18.1 us  [hop(): return lax.ppermute(value, 'term', pairs)]
    ppermute x22, waiting for transfers between devices: 4.97 us -> 6.37 us  [flip(): return lax.ppermute(value, 'term', [(i, i ^ 1) for i in range(16)])]
    ppermute x28, starting transfers between devices: 45.8 us -> 46.8 us  [hop(): return lax.ppermute(value, 'term', pairs)]
  transfers between devices with their start and end apart: 50 -> 50, of which waited for: 30 -> 29; matrix products, arithmetic and copies ran while one was open for 1% -> 1% of each run, Pallas kernels for 1% -> 1%
where the time goes in v17:
time: 96.6 us; the launch traced here: 95.5 us
  starting transfers between devices  50.7 us (52%)
  waiting for transfers between devices  24.5 us (25%)
  Pallas kernels  17.2 us (18%)
  between operations  1.51 us (2%)
    ppermute x28, starting transfers between devices, hop(): return lax.ppermute(value, 'term', pairs)  46.8 us
    ppermute x28, waiting for transfers between devices, hop(): return lax.ppermute(value, 'term', pairs)  18.1 us
    pallas_call x2, Pallas kernels, apply_blocks(): pl.pallas_call(functools.partial(blocks_kernel, first, shape, entries), i...  14.6 us
    ppermute x22, waiting for transfers between devices, flip(): return lax.ppermute(value, 'term', [(i, i ^ 1) for i in range(16)])  6.37 us
    ppermute x22, starting transfers between devices, flip(): return lax.ppermute(value, 'term', [(i, i ^ 1) for i in range(16)])  3.95 us
  transfers between devices with their start and end apart: 50, of which 29 were waited for; matrix products, arithmetic and copies ran while one was open for 1% of the time, Pallas kernels for 1%

profile of v17, /device:TPU:0, one launch (start us, length us, event | category | flops | bytes accessed | tf_op | source)
XLA Modules:
  0.0 95.5 jit_solution(14185232049716599608)
XLA Ops:
  1.1 2.6 %collective-permute-start.3 = (bf16[3,32,512]{2,1,0:T(8,128)(2,1)}, bf16[3,32,512]{2,1,0:T(8,128)(2,1)S(1)}, u32[]{:S(2)}, u32[]{:S(2)}) collective-permute-start(bf16[3,32,512]{2,1,0:T(8,128)(2,1)} %wave_ref.3), channel_id=1, source_target_pairs={{0,4},{1,3},{4,8},{5,1},{8,12},{9,5},{12,14},{13,9},{14,10},{15,13... | collective-permute-start | bytes 294920 | tf_op jit(solution)/shard_map/ppermute | solution.py:390
  4.4 1.6 %collective-permute-start.1 = (bf16[3,32,512]{2,1,0:T(8,128)(2,1)S(1)}, bf16[3,32,512]{2,1,0:T(8,128)(2,1)S(1)}, u32[]{:S(2)}, u32[]{:S(2)}) collective-permute-start(bf16[3,32,512]{2,1,0:T(8,128)(2,1)S(1)} %collective-permute-done.refs_1_), channel_id=1, source_target_pairs={{0,4},{1,3},{4,8},{5,1},{8,12},{9,5},{12,14},{13,9},{14,10},{15,13... | collective-permute-start | bytes 294920 | tf_op jit(solution)/shard_map/ppermute | solution.py:390
  6.8 1.8 %collective-permute-start.6 = (bf16[3,32,512]{2,1,0:T(8,128)(2,1)S(1)}, bf16[3,32,512]{2,1,0:T(8,128)(2,1)S(1)}, u32[]{:S(2)}, u32[]{:S(2)}) collective-permute-start(bf16[3,32,512]{2,1,0:T(8,128)(2,1)S(1)} %collective-permute-done.3.refs_2_), channel_id=1, source_target_pairs={{0,4},{1,3},{4,8},{5,1},{8,12},{9,5},{12,14},{13,9},{14,10},{15,13... | collective-permute-start | bytes 294920 | tf_op jit(solution)/shard_map/ppermute | solution.py:390
  9.1 1.6 %collective-permute-start.2 = (bf16[3,32,512]{2,1,0:T(8,128)(2,1)S(1)}, bf16[3,32,512]{2,1,0:T(8,128)(2,1)S(1)}, u32[]{:S(2)}, u32[]{:S(2)}) collective-permute-start(bf16[3,32,512]{2,1,0:T(8,128)(2,1)S(1)} %collective-permute-done.1.refs_3_), channel_id=1, source_target_pairs={{0,4},{1,3},{4,8},{5,1},{8,12},{9,5},{12,14},{13,9},{14,10},{15,13... | collective-permute-start | bytes 294920 | tf_op jit(solution)/shard_map/ppermute | solution.py:390
  11.6 2.6 %collective-permute-start.13 = (bf16[3,32,512]{2,1,0:T(8,128)(2,1)S(1)}, bf16[3,32,512]{2,1,0:T(8,128)(2,1)S(1)}, u32[]{:S(2)}, u32[]{:S(2)}) collective-permute-start(bf16[3,32,512]{2,1,0:T(8,128)(2,1)S(1)} %copy-done.1), channel_id=1, source_target_pairs={{0,14},{1,15},{4,10},{5,11},{8,6},{9,7},{12,2},{13,3},{14,0},{15,1... | collective-permute-start | bytes 294920 | tf_op jit(solution)/shard_map/ppermute | solution.py:390
  14.3 1.8 %collective-permute-start.7 = (bf16[3,32,512]{2,1,0:T(8,128)(2,1)S(1)}, bf16[3,32,512]{2,1,0:T(8,128)(2,1)S(1)}, u32[]{:S(2)}, u32[]{:S(2)}) collective-permute-start(bf16[3,32,512]{2,1,0:T(8,128)(2,1)S(1)} %collective-permute-done.6.refs_6_), channel_id=1, source_target_pairs={{0,1},{1,0},{2,3},{3,2},{4,5},{5,4},{6,7},{7,6},{8,9},{9,8},{10,11... | collective-permute-start | bytes 294920 | tf_op jit(solution)/shard_map/ppermute | solution.py:381
  16.5 2.6 %collective-permute-done.13.refs_14_ = bf16[3,32,512]{2,1,0:T(8,128)(2,1)S(1)} collective-permute-done((bf16[3,32,512]{2,1,0:T(8,128)(2,1)S(1)}, bf16[3,32,512]{2,1,0:T(8,128)(2,1)S(1)}, u32[]{:S(2)}, u32[]{:S(2)}) %collective-permute-start.13) | collective-permute-done | bytes 98336 | tf_op jit(solution)/shard_map/ppermute | solution.py:390
  22.3 8.4 %shard_map.96 = (f32[3,512,512]{2,1,0:T(8,128)S(1)}, bf16[2,16,3200]{2,1,0:T(8,128)(2,1)S(1)}, bf16[6,16,3200]{2,1,0:T(8,128)(2,1)S(1)}, f32[8,128]{1,0:T(8,128)S(1)}, f32[8,128]{1,0:T(8,128)S(1)}) custom-call(s32[1]{0:T(128)} %bitcast.me_ref.refs_0_.refs_2_, s32[17]{0:T(128)S(1)} %pad_add_fusion.ints_ref, ...), custom_call_target="tpu_custom_call" | custom-call | flops 4294967296 | bytes 8388608 | tf_op jit(solution)/shard_map/pallas_call | solution.py:251
  30.8 1.4 %collective-permute-done.15.other_ref = bf16[2,16,3200]{2,1,0:T(8,128)(2,1)S(1)} collective-permute-done((bf16[2,16,3200]{2,1,0:T(8,128)(2,1)S(1)}, bf16[2,16,3200]{2,1,0:T(8,128)(2,1)S(1)}, u32[]{:S(2)}, u32[]{:S(2)}) %collective-permute-start.15) | collective-permute-done | bytes 204832 | tf_op jit(solution)/shard_map/ppermute | solution.py:381
  34.3 1.4 %collective-permute-start.22 = (bf16[16,3200]{1,0:T(8,128)(2,1)S(1)}, bf16[16,3200]{1,0:T(8,128)(2,1)S(1)}, u32[]{:S(2)}, u32[]{:S(2)}) collective-permute-start(bf16[16,3200]{1,0:T(8,128)(2,1)S(1)} %shard_map.102), channel_id=1, source_target_pairs={{0,14},{1,15},{4,10},{5,11},{8,6},{9,7},{12,2},{13,3},{14,0},{15,1... | collective-permute-start | bytes 307208 | tf_op jit(solution)/shard_map/ppermute | solution.py:390
  35.7 1.4 %collective-permute-done.20.refs_0_ = bf16[16,3200]{1,0:T(8,128)(2,1)S(1)} collective-permute-done((bf16[16,3200]{1,0:T(8,128)(2,1)S(1)}, bf16[16,3200]{1,0:T(8,128)(2,1)S(1)}, u32[]{:S(2)}, u32[]{:S(2)}) %collective-permute-start.20) | collective-permute-done | bytes 102432 | tf_op jit(solution)/shard_map/ppermute | solution.py:390
  38.3 2.9 %collective-permute-start.18 = (bf16[16,3200]{1,0:T(8,128)(2,1)S(1)}, bf16[16,3200]{1,0:T(8,128)(2,1)S(1)}, u32[]{:S(2)}, u32[]{:S(2)}) collective-permute-start(bf16[16,3200]{1,0:T(8,128)(2,1)S(1)} %shard_map.98), channel_id=1, source_target_pairs={{0,4},{1,3},{4,8},{5,1},{8,12},{9,5},{12,14},{13,9},{14,10},{15,13... | collective-permute-start | bytes 307208 | tf_op jit(solution)/shard_map/ppermute | solution.py:390
  44.3 2.2 %collective-permute-start.19 = (bf16[16,3200]{1,0:T(8,128)(2,1)S(1)}, bf16[16,3200]{1,0:T(8,128)(2,1)S(1)}, u32[]{:S(2)}, u32[]{:S(2)}) collective-permute-start(bf16[16,3200]{1,0:T(8,128)(2,1)S(1)} %shard_map.99), channel_id=1, source_target_pairs={{0,4},{1,3},{4,8},{5,1},{8,12},{9,5},{12,14},{13,9},{14,10},{15,13... | collective-permute-start | bytes 307208 | tf_op jit(solution)/shard_map/ppermute | solution.py:390
  46.5 1.4 %collective-permute-done.23 = bf16[16,3200]{1,0:T(8,128)(2,1)S(1)} collective-permute-done((bf16[16,3200]{1,0:T(8,128)(2,1)S(1)}, bf16[16,3200]{1,0:T(8,128)(2,1)S(1)}, u32[]{:S(2)}, u32[]{:S(2)}) %collective-permute-start.23) | collective-permute-done | bytes 102432 | tf_op jit(solution)/shard_map/ppermute | solution.py:390
  50.3 1.8 %collective-permute-start.26 = (bf16[16,3200]{1,0:T(8,128)(2,1)S(1)}, bf16[16,3200]{1,0:T(8,128)(2,1)S(1)}, u32[]{:S(2)}, u32[]{:S(2)}) collective-permute-start(bf16[16,3200]{1,0:T(8,128)(2,1)S(1)} %get-tuple-element.53.refs_0_), channel_id=1, source_target_pairs={{0,4},{1,3},{4,8},{5,1},{8,12},{9,5},{12,14},{13,9},{14,10},{15,13... | collective-permute-start | bytes 307208 | tf_op jit(solution)/shard_map/ppermute | solution.py:390
  52.1 2.1 %collective-permute-start.27 = (bf16[16,3200]{1,0:T(8,128)(2,1)S(1)}, bf16[16,3200]{1,0:T(8,128)(2,1)S(1)}, u32[]{:S(2)}, u32[]{:S(2)}) collective-permute-start(bf16[16,3200]{1,0:T(8,128)(2,1)S(1)} %collective-permute-done.25.refs_1_), channel_id=1, source_target_pairs={{0,4},{1,3},{4,8},{5,1},{8,12},{9,5},{12,14},{13,9},{14,10},{15,13... | collective-permute-start | bytes 307208 | tf_op jit(solution)/shard_map/ppermute | solution.py:390
  55.0 1.8 %collective-permute-start.30 = (bf16[16,3200]{1,0:T(8,128)(2,1)S(1)}, bf16[16,3200]{1,0:T(8,128)(2,1)S(1)}, u32[]{:S(2)}, u32[]{:S(2)}) collective-permute-start(bf16[16,3200]{1,0:T(8,128)(2,1)S(1)} %collective-permute-done.26.refs_2_), channel_id=1, source_target_pairs={{0,4},{1,3},{4,8},{5,1},{8,12},{9,5},{12,14},{13,9},{14,10},{15,13... | collective-permute-start | bytes 307208 | tf_op jit(solution)/shard_map/ppermute | solution.py:390
  56.7 2.1 %collective-permute-start.31 = (bf16[16,3200]{1,0:T(8,128)(2,1)S(1)}, bf16[16,3200]{1,0:T(8,128)(2,1)S(1)}, u32[]{:S(2)}, u32[]{:S(2)}) collective-permute-start(bf16[16,3200]{1,0:T(8,128)(2,1)S(1)} %collective-permute-done.27.refs_3_), channel_id=1, source_target_pairs={{0,4},{1,3},{4,8},{5,1},{8,12},{9,5},{12,14},{13,9},{14,10},{15,13... | collective-permute-start | bytes 307208 | tf_op jit(solution)/shard_map/ppermute | solution.py:390
  58.9 1.5 %collective-permute-start.38 = (bf16[16,3200]{1,0:T(8,128)(2,1)S(1)}, bf16[16,3200]{1,0:T(8,128)(2,1)S(1)}, u32[]{:S(2)}, u32[]{:S(2)}) collective-permute-start(bf16[16,3200]{1,0:T(8,128)(2,1)S(1)} %get-tuple-element.53.refs_0_), channel_id=1, source_target_pairs={{0,14},{1,15},{4,10},{5,11},{8,6},{9,7},{12,2},{13,3},{14,0},{15,1... | collective-permute-start | bytes 307208 | tf_op jit(solution)/shard_map/ppermute | solution.py:390
  61.6 3.9 %collective-permute-start.35 = (bf16[16,3200]{1,0:T(8,128)(2,1)S(1)}, bf16[16,3200]{1,0:T(8,128)(2,1)S(1)}, u32[]{:S(2)}, u32[]{:S(2)}) collective-permute-start(bf16[16,3200]{1,0:T(8,128)(2,1)S(1)} %collective-permute-done.31.refs_7_), channel_id=1, source_target_pairs={{0,4},{1,3},{4,8},{5,1},{8,12},{9,5},{12,14},{13,9},{14,10},{15,13... | collective-permute-start | bytes 307208 | tf_op jit(solution)/shard_map/ppermute | solution.py:390
  65.5 1.7 %collective-permute-done.38.refs_14_ = bf16[16,3200]{1,0:T(8,128)(2,1)S(1)} collective-permute-done((bf16[16,3200]{1,0:T(8,128)(2,1)S(1)}, bf16[16,3200]{1,0:T(8,128)(2,1)S(1)}, u32[]{:S(2)}, u32[]{:S(2)}) %collective-permute-start.38) | collective-permute-done | bytes 102432 | tf_op jit(solution)/shard_map/ppermute | solution.py:390
  69.6 6.2 %shard_map.105 = (f32[3,512,512]{2,1,0:T(8,128)S(1)}, bf16[2,16,3200]{2,1,0:T(8,128)(2,1)S(1)}, bf16[6,16,3200]{2,1,0:T(8,128)(2,1)S(1)}, f32[8,128]{1,0:T(8,128)S(1)}, f32[8,128]{1,0:T(8,128)S(1)}) custom-call(s32[1]{0:T(128)} %bitcast.me_ref.refs_0_.refs_2_, s32[17]{0:T(128)S(1)} %pad_add_fusion.ints_ref, bf16[16,3200]{1,0:T(8,128)(2,1)S(1)} %get-tuple-element.53.refs_0_, ...), custom_call_target="tpu_custom_call" | custom-call | flops 4294967296 | bytes 8388608 | tf_op jit(solution)/shard_map/pallas_call | solution.py:251
  75.8 1.4 %collective-permute-done.40.other_ref = bf16[2,16,3200]{2,1,0:T(8,128)(2,1)S(1)} collective-permute-done((bf16[2,16,3200]{2,1,0:T(8,128)(2,1)S(1)}, bf16[2,16,3200]{2,1,0:T(8,128)(2,1)S(1)}, u32[]{:S(2)}, u32[]{:S(2)}) %collective-permute-start.40) | collective-permute-done | bytes 204832 | tf_op jit(solution)/shard_map/ppermute | solution.py:381
  77.5 2.0 %collective-permute-start.45 = (bf16[16,3200]{1,0:T(8,128)(2,1)S(1)}, bf16[16,3200]{1,0:T(8,128)(2,1)S(1)}, u32[]{:S(2)}, u32[]{:S(2)}) collective-permute-start(bf16[16,3200]{1,0:T(8,128)(2,1)S(1)} %shard_map.109), channel_id=1, source_target_pairs={{0,4},{1,3},{4,8},{5,1},{8,12},{9,5},{12,14},{13,9},{14,10},{15,13... | collective-permute-start | bytes 307208 | tf_op jit(solution)/shard_map/ppermute | solution.py:390
  79.5 1.2 %collective-permute-start.42 = (bf16[16,3200]{1,0:T(8,128)(2,1)S(1)}, bf16[16,3200]{1,0:T(8,128)(2,1)S(1)}, u32[]{:S(2)}, u32[]{:S(2)}) collective-permute-start(bf16[16,3200]{1,0:T(8,128)(2,1)S(1)} %shard_map.106), channel_id=1, source_target_pairs={{0,4},{1,3},{4,8},{5,1},{8,12},{9,5},{12,14},{13,9},{14,10},{15,13... | collective-permute-start | bytes 307208 | tf_op jit(solution)/shard_map/ppermute | solution.py:390
  80.7 1.1 %collective-permute-start.47 = (bf16[16,3200]{1,0:T(8,128)(2,1)S(1)}, bf16[16,3200]{1,0:T(8,128)(2,1)S(1)}, u32[]{:S(2)}, u32[]{:S(2)}) collective-permute-start(bf16[16,3200]{1,0:T(8,128)(2,1)S(1)} %shard_map.111), channel_id=1, source_target_pairs={{0,14},{1,15},{4,10},{5,11},{8,6},{9,7},{12,2},{13,3},{14,0},{15,1... | collective-permute-start | bytes 307208 | tf_op jit(solution)/shard_map/ppermute | solution.py:390
  82.2 2.0 %collective-permute-start.46 = (bf16[16,3200]{1,0:T(8,128)(2,1)S(1)}, bf16[16,3200]{1,0:T(8,128)(2,1)S(1)}, u32[]{:S(2)}, u32[]{:S(2)}) collective-permute-start(bf16[16,3200]{1,0:T(8,128)(2,1)S(1)} %shard_map.110), channel_id=1, source_target_pairs={{0,4},{1,3},{4,8},{5,1},{8,12},{9,5},{12,14},{13,9},{14,10},{15,13... | collective-permute-start | bytes 307208 | tf_op jit(solution)/shard_map/ppermute | solution.py:390
  84.3 2.8 %collective-permute-start.43 = (bf16[16,3200]{1,0:T(8,128)(2,1)S(1)}, bf16[16,3200]{1,0:T(8,128)(2,1)S(1)}, u32[]{:S(2)}, u32[]{:S(2)}) collective-permute-start(bf16[16,3200]{1,0:T(8,128)(2,1)S(1)} %shard_map.107), channel_id=1, source_target_pairs={{0,4},{1,3},{4,8},{5,1},{8,12},{9,5},{12,14},{13,9},{14,10},{15,13... | collective-permute-start | bytes 307208 | tf_op jit(solution)/shard_map/ppermute | solution.py:390
  87.1 1.3 %collective-permute-done.47.refs_8_ = bf16[16,3200]{1,0:T(8,128)(2,1)S(1)} collective-permute-done((bf16[16,3200]{1,0:T(8,128)(2,1)S(1)}, bf16[16,3200]{1,0:T(8,128)(2,1)S(1)}, u32[]{:S(2)}, u32[]{:S(2)}) %collective-permute-start.47) | collective-permute-done | bytes 102432 | tf_op jit(solution)/shard_map/ppermute | solution.py:390
  88.4 1.4 %collective-permute-start.48 = (bf16[16,3200]{1,0:T(8,128)(2,1)S(1)}, bf16[16,3200]{1,0:T(8,128)(2,1)S(1)}, u32[]{:S(2)}, u32[]{:S(2)}) collective-permute-start(bf16[16,3200]{1,0:T(8,128)(2,1)S(1)} %shard_map.112), channel_id=1, source_target_pairs={{0,4},{1,3},{4,8},{5,1},{8,12},{9,5},{12,14},{13,9},{14,10},{15,13... | collective-permute-start | bytes 307208 | tf_op jit(solution)/shard_map/ppermute | solution.py:390
  89.9 2.5 %collective-permute-start.44 = (bf16[16,3200]{1,0:T(8,128)(2,1)S(1)}, bf16[16,3200]{1,0:T(8,128)(2,1)S(1)}, u32[]{:S(2)}, u32[]{:S(2)}) collective-permute-start(bf16[16,3200]{1,0:T(8,128)(2,1)S(1)} %shard_map.108), channel_id=1, source_target_pairs={{0,4},{1,3},{4,8},{5,1},{8,12},{9,5},{12,14},{13,9},{14,10},{15,13... | collective-permute-start | bytes 307208 | tf_op jit(solution)/shard_map/ppermute | solution.py:390
  93.2 1.4 %collective-permute-done.44.refs_6_ = bf16[16,3200]{1,0:T(8,128)(2,1)S(1)} collective-permute-done((bf16[16,3200]{1,0:T(8,128)(2,1)S(1)}, bf16[16,3200]{1,0:T(8,128)(2,1)S(1)}, u32[]{:S(2)}, u32[]{:S(2)}) %collective-permute-start.44) | collective-permute-done | bytes 102432 | tf_op jit(solution)/shard_map/ppermute | solution.py:390
  (99 shorter events, 22.1 us)
Async XLA Ops:
  1.1 5.7 %collective-permute-start.3 = (bf16[3,32,512]{2,1,0:T(8,128)(2,1)}, bf16[3,32,512]{2,1,0:T(8,128)(2,1)S(1)}, u32[]{:S(2)}, u32[]{:S(2)}) collective-permute-start(bf16[3,32,512]{2,1,0:T(8,128)(2,1)} %wave_ref.3), channel_id=1, source_target_pairs={{0,4},{1,3},{4,8},{5,1},{8,12},{9,5},{12,14},{13,9},{14,10},{15,13... | collective-permute-start | bytes 294920 | tf_op jit(solution)/shard_map/ppermute | solution.py:390
  4.4 4.7 %collective-permute-start.1 = (bf16[3,32,512]{2,1,0:T(8,128)(2,1)S(1)}, bf16[3,32,512]{2,1,0:T(8,128)(2,1)S(1)}, u32[]{:S(2)}, u32[]{:S(2)}) collective-permute-start(bf16[3,32,512]{2,1,0:T(8,128)(2,1)S(1)} %collective-permute-done.refs_1_), channel_id=1, source_target_pairs={{0,4},{1,3},{4,8},{5,1},{8,12},{9,5},{12,14},{13,9},{14,10},{15,13... | collective-permute-start | bytes 294920 | tf_op jit(solution)/shard_map/ppermute | solution.py:390
  6.8 7.4 %collective-permute-start.6 = (bf16[3,32,512]{2,1,0:T(8,128)(2,1)S(1)}, bf16[3,32,512]{2,1,0:T(8,128)(2,1)S(1)}, u32[]{:S(2)}, u32[]{:S(2)}) collective-permute-start(bf16[3,32,512]{2,1,0:T(8,128)(2,1)S(1)} %collective-permute-done.3.refs_2_), channel_id=1, source_target_pairs={{0,4},{1,3},{4,8},{5,1},{8,12},{9,5},{12,14},{13,9},{14,10},{15,13... | collective-permute-start | bytes 294920 | tf_op jit(solution)/shard_map/ppermute | solution.py:390
  9.1 6.9 %collective-permute-start.2 = (bf16[3,32,512]{2,1,0:T(8,128)(2,1)S(1)}, bf16[3,32,512]{2,1,0:T(8,128)(2,1)S(1)}, u32[]{:S(2)}, u32[]{:S(2)}) collective-permute-start(bf16[3,32,512]{2,1,0:T(8,128)(2,1)S(1)} %collective-permute-done.1.refs_3_), channel_id=1, source_target_pairs={{0,4},{1,3},{4,8},{5,1},{8,12},{9,5},{12,14},{13,9},{14,10},{15,13... | collective-permute-start | bytes 294920 | tf_op jit(solution)/shard_map/ppermute | solution.py:390
  11.6 7.5 %collective-permute-start.13 = (bf16[3,32,512]{2,1,0:T(8,128)(2,1)S(1)}, bf16[3,32,512]{2,1,0:T(8,128)(2,1)S(1)}, u32[]{:S(2)}, u32[]{:S(2)}) collective-permute-start(bf16[3,32,512]{2,1,0:T(8,128)(2,1)S(1)} %copy-done.1), channel_id=1, source_target_pairs={{0,14},{1,15},{4,10},{5,11},{8,6},{9,7},{12,2},{13,3},{14,0},{15,1... | collective-permute-start | bytes 294920 | tf_op jit(solution)/shard_map/ppermute | solution.py:390
  14.2 5.7 %collective-permute-start.9 = (bf16[3,32,512]{2,1,0:T(8,128)(2,1)S(1)}, bf16[3,32,512]{2,1,0:T(8,128)(2,1)S(1)}, u32[]{:S(2)}, u32[]{:S(2)}) collective-permute-start(bf16[3,32,512]{2,1,0:T(8,128)(2,1)S(1)} %collective-permute-done.6.refs_6_), channel_id=1, source_target_pairs={{0,4},{1,3},{4,8},{5,1},{8,12},{9,5},{12,14},{13,9},{14,10},{15,13... | collective-permute-start | bytes 294920 | tf_op jit(solution)/shard_map/ppermute | solution.py:390
  14.3 5.7 %collective-permute-start.7 = (bf16[3,32,512]{2,1,0:T(8,128)(2,1)S(1)}, bf16[3,32,512]{2,1,0:T(8,128)(2,1)S(1)}, u32[]{:S(2)}, u32[]{:S(2)}) collective-permute-start(bf16[3,32,512]{2,1,0:T(8,128)(2,1)S(1)} %collective-permute-done.6.refs_6_), channel_id=1, source_target_pairs={{0,1},{1,0},{2,3},{3,2},{4,5},{5,4},{6,7},{7,6},{8,9},{9,8},{10,11... | collective-permute-start | bytes 294920 | tf_op jit(solution)/shard_map/ppermute | solution.py:381
  16.1 4.9 %collective-permute-start.10 = (bf16[3,32,512]{2,1,0:T(8,128)(2,1)S(1)}, bf16[3,32,512]{2,1,0:T(8,128)(2,1)S(1)}, u32[]{:S(2)}, u32[]{:S(2)}) collective-permute-start(bf16[3,32,512]{2,1,0:T(8,128)(2,1)S(1)} %collective-permute-done.2.refs_7_), channel_id=1, source_target_pairs={{0,4},{1,3},{4,8},{5,1},{8,12},{9,5},{12,14},{13,9},{14,10},{15,13... | collective-permute-start | bytes 294920 | tf_op jit(solution)/shard_map/ppermute | solution.py:390
  16.5 4.5 %collective-permute-start.5 = (bf16[3,32,512]{2,1,0:T(8,128)(2,1)S(1)}, bf16[3,32,512]{2,1,0:T(8,128)(2,1)S(1)}, u32[]{:S(2)}, u32[]{:S(2)}) collective-permute-start(bf16[3,32,512]{2,1,0:T(8,128)(2,1)S(1)} %collective-permute-done.1.refs_3_), channel_id=1, source_target_pairs={{0,1},{1,0},{2,3},{3,2},{4,5},{5,4},{6,7},{7,6},{8,9},{9,8},{10,11... | collective-permute-start | bytes 294920 | tf_op jit(solution)/shard_map/ppermute | solution.py:381
  32.4 4.7 %collective-permute-start.20 = (bf16[16,3200]{1,0:T(8,128)(2,1)S(1)}, bf16[16,3200]{1,0:T(8,128)(2,1)S(1)}, u32[]{:S(2)}, u32[]{:S(2)}) collective-permute-start(bf16[16,3200]{1,0:T(8,128)(2,1)S(1)} %shard_map.100), channel_id=1, source_target_pairs={{0,4},{1,3},{4,8},{5,1},{8,12},{9,5},{12,14},{13,9},{14,10},{15,13... | collective-permute-start | bytes 307208 | tf_op jit(solution)/shard_map/ppermute | solution.py:390
  33.1 5.1 %collective-permute-start.17 = (bf16[16,3200]{1,0:T(8,128)(2,1)S(1)}, bf16[16,3200]{1,0:T(8,128)(2,1)S(1)}, u32[]{:S(2)}, u32[]{:S(2)}) collective-permute-start(bf16[16,3200]{1,0:T(8,128)(2,1)S(1)} %shard_map.97), channel_id=1, source_target_pairs={{0,4},{1,3},{4,8},{5,1},{8,12},{9,5},{12,14},{13,9},{14,10},{15,13... | collective-permute-start | bytes 307208 | tf_op jit(solution)/shard_map/ppermute | solution.py:390
  34.3 7.9 %collective-permute-start.22 = (bf16[16,3200]{1,0:T(8,128)(2,1)S(1)}, bf16[16,3200]{1,0:T(8,128)(2,1)S(1)}, u32[]{:S(2)}, u32[]{:S(2)}) collective-permute-start(bf16[16,3200]{1,0:T(8,128)(2,1)S(1)} %shard_map.102), channel_id=1, source_target_pairs={{0,14},{1,15},{4,10},{5,11},{8,6},{9,7},{12,2},{13,3},{14,0},{15,1... | collective-permute-start | bytes 307208 | tf_op jit(solution)/shard_map/ppermute | solution.py:390
  37.2 6.0 %collective-permute-start.21 = (bf16[16,3200]{1,0:T(8,128)(2,1)S(1)}, bf16[16,3200]{1,0:T(8,128)(2,1)S(1)}, u32[]{:S(2)}, u32[]{:S(2)}) collective-permute-start(bf16[16,3200]{1,0:T(8,128)(2,1)S(1)} %shard_map.101), channel_id=1, source_target_pairs={{0,4},{1,3},{4,8},{5,1},{8,12},{9,5},{12,14},{13,9},{14,10},{15,13... | collective-permute-start | bytes 307208 | tf_op jit(solution)/shard_map/ppermute | solution.py:390
  38.3 6.0 %collective-permute-start.18 = (bf16[16,3200]{1,0:T(8,128)(2,1)S(1)}, bf16[16,3200]{1,0:T(8,128)(2,1)S(1)}, u32[]{:S(2)}, u32[]{:S(2)}) collective-permute-start(bf16[16,3200]{1,0:T(8,128)(2,1)S(1)} %shard_map.98), channel_id=1, source_target_pairs={{0,4},{1,3},{4,8},{5,1},{8,12},{9,5},{12,14},{13,9},{14,10},{15,13... | collective-permute-start | bytes 307208 | tf_op jit(solution)/shard_map/ppermute | solution.py:390
  43.2 4.7 %collective-permute-start.23 = (bf16[16,3200]{1,0:T(8,128)(2,1)S(1)}, bf16[16,3200]{1,0:T(8,128)(2,1)S(1)}, u32[]{:S(2)}, u32[]{:S(2)}) collective-permute-start(bf16[16,3200]{1,0:T(8,128)(2,1)S(1)} %shard_map.103), channel_id=1, source_target_pairs={{0,4},{1,3},{4,8},{5,1},{8,12},{9,5},{12,14},{13,9},{14,10},{15,13... | collective-permute-start | bytes 307208 | tf_op jit(solution)/shard_map/ppermute | solution.py:390
  44.3 4.7 %collective-permute-start.19 = (bf16[16,3200]{1,0:T(8,128)(2,1)S(1)}, bf16[16,3200]{1,0:T(8,128)(2,1)S(1)}, u32[]{:S(2)}, u32[]{:S(2)}) collective-permute-start(bf16[16,3200]{1,0:T(8,128)(2,1)S(1)} %shard_map.99), channel_id=1, source_target_pairs={{0,4},{1,3},{4,8},{5,1},{8,12},{9,5},{12,14},{13,9},{14,10},{15,13... | collective-permute-start | bytes 307208 | tf_op jit(solution)/shard_map/ppermute | solution.py:390
  50.3 4.7 %collective-permute-start.26 = (bf16[16,3200]{1,0:T(8,128)(2,1)S(1)}, bf16[16,3200]{1,0:T(8,128)(2,1)S(1)}, u32[]{:S(2)}, u32[]{:S(2)}) collective-permute-start(bf16[16,3200]{1,0:T(8,128)(2,1)S(1)} %get-tuple-element.53.refs_0_), channel_id=1, source_target_pairs={{0,4},{1,3},{4,8},{5,1},{8,12},{9,5},{12,14},{13,9},{14,10},{15,13... | collective-permute-start | bytes 307208 | tf_op jit(solution)/shard_map/ppermute | solution.py:390
  52.1 4.7 %collective-permute-start.27 = (bf16[16,3200]{1,0:T(8,128)(2,1)S(1)}, bf16[16,3200]{1,0:T(8,128)(2,1)S(1)}, u32[]{:S(2)}, u32[]{:S(2)}) collective-permute-start(bf16[16,3200]{1,0:T(8,128)(2,1)S(1)} %collective-permute-done.25.refs_1_), channel_id=1, source_target_pairs={{0,4},{1,3},{4,8},{5,1},{8,12},{9,5},{12,14},{13,9},{14,10},{15,13... | collective-permute-start | bytes 307208 | tf_op jit(solution)/shard_map/ppermute | solution.py:390
  55.0 5.3 %collective-permute-start.30 = (bf16[16,3200]{1,0:T(8,128)(2,1)S(1)}, bf16[16,3200]{1,0:T(8,128)(2,1)S(1)}, u32[]{:S(2)}, u32[]{:S(2)}) collective-permute-start(bf16[16,3200]{1,0:T(8,128)(2,1)S(1)} %collective-permute-done.26.refs_2_), channel_id=1, source_target_pairs={{0,4},{1,3},{4,8},{5,1},{8,12},{9,5},{12,14},{13,9},{14,10},{15,13... | collective-permute-start | bytes 307208 | tf_op jit(solution)/shard_map/ppermute | solution.py:390
  56.7 4.8 %collective-permute-start.31 = (bf16[16,3200]{1,0:T(8,128)(2,1)S(1)}, bf16[16,3200]{1,0:T(8,128)(2,1)S(1)}, u32[]{:S(2)}, u32[]{:S(2)}) collective-permute-start(bf16[16,3200]{1,0:T(8,128)(2,1)S(1)} %collective-permute-done.27.refs_3_), channel_id=1, source_target_pairs={{0,4},{1,3},{4,8},{5,1},{8,12},{9,5},{12,14},{13,9},{14,10},{15,13... | collective-permute-start | bytes 307208 | tf_op jit(solution)/shard_map/ppermute | solution.py:390
  58.9 6.6 %collective-permute-start.28 = (bf16[16,3200]{1,0:T(8,128)(2,1)S(1)}, bf16[16,3200]{1,0:T(8,128)(2,1)S(1)}, u32[]{:S(2)}, u32[]{:S(2)}) collective-permute-start(bf16[16,3200]{1,0:T(8,128)(2,1)S(1)} %collective-permute-done.26.refs_2_), channel_id=1, source_target_pairs={{0,1},{1,0},{2,3},{3,2},{4,5},{5,4},{6,7},{7,6},{8,9},{9,8},{10,11... | collective-permute-start | bytes 307208 | tf_op jit(solution)/shard_map/ppermute | solution.py:381
  58.9 8.3 %collective-permute-start.38 = (bf16[16,3200]{1,0:T(8,128)(2,1)S(1)}, bf16[16,3200]{1,0:T(8,128)(2,1)S(1)}, u32[]{:S(2)}, u32[]{:S(2)}) collective-permute-start(bf16[16,3200]{1,0:T(8,128)(2,1)S(1)} %get-tuple-element.53.refs_0_), channel_id=1, source_target_pairs={{0,14},{1,15},{4,10},{5,11},{8,6},{9,7},{12,2},{13,3},{14,0},{15,1... | collective-permute-start | bytes 307208 | tf_op jit(solution)/shard_map/ppermute | solution.py:390
  60.3 6.9 %collective-permute-start.34 = (bf16[16,3200]{1,0:T(8,128)(2,1)S(1)}, bf16[16,3200]{1,0:T(8,128)(2,1)S(1)}, u32[]{:S(2)}, u32[]{:S(2)}) collective-permute-start(bf16[16,3200]{1,0:T(8,128)(2,1)S(1)} %collective-permute-done.30.refs_6_), channel_id=1, source_target_pairs={{0,4},{1,3},{4,8},{5,1},{8,12},{9,5},{12,14},{13,9},{14,10},{15,13... | collective-permute-start | bytes 307208 | tf_op jit(solution)/shard_map/ppermute | solution.py:390
  61.4 6.2 %collective-permute-start.32 = (bf16[16,3200]{1,0:T(8,128)(2,1)S(1)}, bf16[16,3200]{1,0:T(8,128)(2,1)S(1)}, u32[]{:S(2)}, u32[]{:S(2)}) collective-permute-start(bf16[16,3200]{1,0:T(8,128)(2,1)S(1)} %collective-permute-done.30.refs_6_), channel_id=1, source_target_pairs={{0,1},{1,0},{2,3},{3,2},{4,5},{5,4},{6,7},{7,6},{8,9},{9,8},{10,11... | collective-permute-start | bytes 307208 | tf_op jit(solution)/shard_map/ppermute | solution.py:381
  61.6 6.7 %collective-permute-start.35 = (bf16[16,3200]{1,0:T(8,128)(2,1)S(1)}, bf16[16,3200]{1,0:T(8,128)(2,1)S(1)}, u32[]{:S(2)}, u32[]{:S(2)}) collective-permute-start(bf16[16,3200]{1,0:T(8,128)(2,1)S(1)} %collective-permute-done.31.refs_7_), channel_id=1, source_target_pairs={{0,4},{1,3},{4,8},{5,1},{8,12},{9,5},{12,14},{13,9},{14,10},{15,13... | collective-permute-start | bytes 307208 | tf_op jit(solution)/shard_map/ppermute | solution.py:390
  77.5 4.7 %collective-permute-start.45 = (bf16[16,3200]{1,0:T(8,128)(2,1)S(1)}, bf16[16,3200]{1,0:T(8,128)(2,1)S(1)}, u32[]{:S(2)}, u32[]{:S(2)}) collective-permute-start(bf16[16,3200]{1,0:T(8,128)(2,1)S(1)} %shard_map.109), channel_id=1, source_target_pairs={{0,4},{1,3},{4,8},{5,1},{8,12},{9,5},{12,14},{13,9},{14,10},{15,13... | collective-permute-start | bytes 307208 | tf_op jit(solution)/shard_map/ppermute | solution.py:390
  79.5 4.7 %collective-permute-start.42 = (bf16[16,3200]{1,0:T(8,128)(2,1)S(1)}, bf16[16,3200]{1,0:T(8,128)(2,1)S(1)}, u32[]{:S(2)}, u32[]{:S(2)}) collective-permute-start(bf16[16,3200]{1,0:T(8,128)(2,1)S(1)} %shard_map.106), channel_id=1, source_target_pairs={{0,4},{1,3},{4,8},{5,1},{8,12},{9,5},{12,14},{13,9},{14,10},{15,13... | collective-permute-start | bytes 307208 | tf_op jit(solution)/shard_map/ppermute | solution.py:390
  80.7 7.6 %collective-permute-start.47 = (bf16[16,3200]{1,0:T(8,128)(2,1)S(1)}, bf16[16,3200]{1,0:T(8,128)(2,1)S(1)}, u32[]{:S(2)}, u32[]{:S(2)}) collective-permute-start(bf16[16,3200]{1,0:T(8,128)(2,1)S(1)} %shard_map.111), channel_id=1, source_target_pairs={{0,14},{1,15},{4,10},{5,11},{8,6},{9,7},{12,2},{13,3},{14,0},{15,1... | collective-permute-start | bytes 307208 | tf_op jit(solution)/shard_map/ppermute | solution.py:390
  82.2 6.1 %collective-permute-start.46 = (bf16[16,3200]{1,0:T(8,128)(2,1)S(1)}, bf16[16,3200]{1,0:T(8,128)(2,1)S(1)}, u32[]{:S(2)}, u32[]{:S(2)}) collective-permute-start(bf16[16,3200]{1,0:T(8,128)(2,1)S(1)} %shard_map.110), channel_id=1, source_target_pairs={{0,4},{1,3},{4,8},{5,1},{8,12},{9,5},{12,14},{13,9},{14,10},{15,13... | collective-permute-start | bytes 307208 | tf_op jit(solution)/shard_map/ppermute | solution.py:390
  84.3 5.5 %collective-permute-start.43 = (bf16[16,3200]{1,0:T(8,128)(2,1)S(1)}, bf16[16,3200]{1,0:T(8,128)(2,1)S(1)}, u32[]{:S(2)}, u32[]{:S(2)}) collective-permute-start(bf16[16,3200]{1,0:T(8,128)(2,1)S(1)} %shard_map.107), channel_id=1, source_target_pairs={{0,4},{1,3},{4,8},{5,1},{8,12},{9,5},{12,14},{13,9},{14,10},{15,13... | collective-permute-start | bytes 307208 | tf_op jit(solution)/shard_map/ppermute | solution.py:390
  88.4 4.7 %collective-permute-start.48 = (bf16[16,3200]{1,0:T(8,128)(2,1)S(1)}, bf16[16,3200]{1,0:T(8,128)(2,1)S(1)}, u32[]{:S(2)}, u32[]{:S(2)}) collective-permute-start(bf16[16,3200]{1,0:T(8,128)(2,1)S(1)} %shard_map.112), channel_id=1, source_target_pairs={{0,4},{1,3},{4,8},{5,1},{8,12},{9,5},{12,14},{13,9},{14,10},{15,13... | collective-permute-start | bytes 307208 | tf_op jit(solution)/shard_map/ppermute | solution.py:390
  89.9 4.7 %collective-permute-start.44 = (bf16[16,3200]{1,0:T(8,128)(2,1)S(1)}, bf16[16,3200]{1,0:T(8,128)(2,1)S(1)}, u32[]{:S(2)}, u32[]{:S(2)}) collective-permute-start(bf16[16,3200]{1,0:T(8,128)(2,1)S(1)} %shard_map.108), channel_id=1, source_target_pairs={{0,4},{1,3},{4,8},{5,1},{8,12},{9,5},{12,14},{13,9},{14,10},{15,13... | collective-permute-start | bytes 307208 | tf_op jit(solution)/shard_map/ppermute | solution.py:390
  (23 other events, 112.8 us)

commit v18 on v14

--- a/solution.py
+++ b/solution.py
@@ -11,8 +11,10 @@
 SMEM = pl.BlockSpec(memory_space=pltpu.SMEM)
 HBM = pl.BlockSpec(memory_space=pltpu.HBM)
 PARAMS = pltpu.CompilerParams(vmem_limit_bytes=16 * 1024 * 1024)
-FIRST = pltpu.CompilerParams(vmem_limit_bytes=48 * 1024 * 1024)
+READY_PARAMS = pltpu.CompilerParams(vmem_limit_bytes=48 * 1024 * 1024)
+FIRST_PARAMS = pltpu.CompilerParams(vmem_limit_bytes=43 * 1024 * 1024)
 HALF = 16
+READY = 4
 GROUP = 2
 LANES = 128
 
@@ -105,7 +107,32 @@
         out_specs=VMEM,
         out_shape=jax.ShapeDtypeStruct(value.shape, value.dtype),
         compiler_params=PARAMS,
+        cost_estimate=pl.CostEstimate(flops=8 << 30, bytes_accessed=1 << 20, transcendentals=0),
     )(value)
+
+
+def ready_kernel(left_in, right_in, _, left, right, left_sem, right_sem):
+    copies = [
+        pltpu.make_async_copy(left_in.at[pl.ds(0, READY)], left, left_sem),
+        pltpu.make_async_copy(right_in.at[pl.ds(0, READY)], right, right_sem),
+    ]
+    for copy in copies:
+        copy.start()
+    for copy in copies:
+        copy.wait()
+
+
+def ready_blocks(left, right, after):
+    shape = (READY, *left.shape[1:])
+    return pl.pallas_call(
+        ready_kernel,
+        in_specs=[HBM] * 3,
+        out_specs=[VMEM] * 2,
+        out_shape=[jax.ShapeDtypeStruct(shape, b.dtype) for b in (left, right)],
+        scratch_shapes=[pltpu.SemaphoreType.DMA] * 2,
+        compiler_params=READY_PARAMS,
+        cost_estimate=pl.CostEstimate(flops=2 << 30, bytes_accessed=4 << 20, transcendentals=0),
+    )(left, right, after)
 
 
 def square_kernel(wave_ref, diag_ref, square_ref):
@@ -130,7 +157,7 @@
     sectors, rows, width = shape
     field_refs, refs = refs[:16], refs[16:]
     if first:
-        square_ref, *refs = refs
+        square_ref, left_ready, right_ready, *refs = refs
     else:
         scale_ref, wave_ref, correction_ref, *refs = refs
     left_in, right_in, *refs = refs
@@ -140,12 +167,13 @@
         left, right, left_sem, right_sem = refs
 
         def copies(slot):
+            k = slot - READY
             return (
-                pltpu.make_async_copy(left_in.at[slot], left.at[slot], left_sem.at[slot]),
-                pltpu.make_async_copy(right_in.at[slot], right.at[slot], right_sem.at[slot]),
+                pltpu.make_async_copy(left_in.at[slot], left.at[k], left_sem.at[k]),
+                pltpu.make_async_copy(right_in.at[slot], right.at[k], right_sem.at[k]),
             )
 
-        for slot in range(slots):
+        for slot in range(READY, slots):
             for copy in copies(slot):
                 copy.start()
     else:
@@ -181,9 +209,9 @@
 
     used = ints_ref[2 * slots]
 
-    def add_some(step, carry):
+    def add_some(left, right, start, copied_here, step, carry):
         some = [step * GROUP + k for k in range(GROUP)]
-        if first:
+        if copied_here:
             for slot in some:
                 for copy in copies(slot):
                     copy.wait()
@@ -192,7 +220,7 @@
         def _():
             products = [
                 jnp.dot(
-                    left[slot], field[ints_ref[slot]], preferred_element_type=jnp.float32
+                    left[slot - start], field[ints_ref[slot]], preferred_element_type=jnp.float32
                 ).astype(jnp.bfloat16)
                 for slot in some
             ]
@@ -201,14 +229,20 @@
                     product = jnp.where(slot < used, product, jnp.zeros_like(product))
                 total[ints_ref[slots + slot]] += lax.dot_general(
                     product,
-                    right[slot],
+                    right[slot - start],
                     (((1,), (1,)), ((), ())),
                     preferred_element_type=jnp.float32,
                 )
 
         return carry
 
-    lax.fori_loop(0, slots // GROUP, add_some, 0)
+    if first:
+        early = functools.partial(add_some, left_ready, right_ready, 0, False)
+        late = functools.partial(add_some, left, right, READY, True)
+        lax.fori_loop(0, READY // GROUP, early, 0)
+        lax.fori_loop(READY // GROUP, slots // GROUP, late, 0)
+    else:
+        lax.fori_loop(0, slots // GROUP, functools.partial(add_some, left, right, 0, False), 0)
 
     dot = jnp.zeros((8, 128), jnp.float32)
     if first:
@@ -242,8 +276,8 @@
     message = message_shape(*shape)
     scratch = []
     if first:
-        scratch = [pltpu.VMEM(b.shape, b.dtype) for b in (left, right)]
-        scratch += [pltpu.SemaphoreType.DMA((slots,))] * 2
+        scratch = [pltpu.VMEM((slots - READY, *b.shape[1:]), b.dtype) for b in (left, right)]
+        scratch += [pltpu.SemaphoreType.DMA((slots - READY,))] * 2
     return pl.pallas_call(
         functools.partial(blocks_kernel, first, shape, entries),
         in_specs=[SMEM, SMEM]
@@ -258,7 +292,7 @@
             jax.ShapeDtypeStruct((8, 128), jnp.float32),
             jax.ShapeDtypeStruct((8, 128), jnp.float32),
         ],
-        compiler_params=FIRST if first else PARAMS,
+        compiler_params=FIRST_PARAMS if first else PARAMS,
         cost_estimate=pl.CostEstimate(
             flops=4 * slots * order * order * width,
             bytes_accessed=4 * slots * order * order,
@@ -390,7 +424,7 @@
     return hop(value, 4, 4)
 
 
-def gather(own, beside=()):
+def gather(own, beside=(), blocks=()):
     one, two = own, flip(own)
     across, two = lax.optimization_barrier((own, two))
     pieces = [one, two]
@@ -405,8 +439,11 @@
             two, ready = lax.optimization_barrier((two, ready))
             if ready:
                 results[-1] = ready[0]
+        if k == 1 and blocks:
+            blocks = ready_blocks(*blocks, two)
+            across, blocks = lax.optimization_barrier((across, blocks))
         pieces += [one, two, flip(one), flip(two)]
-    return pieces + [across, flip(across)], results
+    return pieces + [across, flip(across)], results, blocks
 
 
 def scatter(shape, me, total, near, far, dot):
@@ -436,14 +473,18 @@
         lambda _: copied(wavefunction),
         lambda _, own: weighted_square(own, diagonal),
     )
-    (_, *fields), (ints, own, square) = gather(wavefunction, beside)
+    (_, *fields), (ints, own, square), ready = gather(
+        wavefunction, beside, (left_blocks, right_blocks)
+    )
     fields = [own, *fields]
     blocks = (left_blocks, right_blocks, shape)
-    total, near, far, dot, scale = apply_blocks(me, ints, fields, (square,), *blocks, True, entries)
+    total, near, far, dot, scale = apply_blocks(
+        me, ints, fields, (square, *ready), *blocks, True, entries
+    )
     first_image, terms, correction, message = davidson_step(
         scale, wavefunction, diagonal, scatter(shape, me, total, near, far, dot), entries
     )
-    fields, _ = gather(message)
+    fields, *_ = gather(message)
     own = (scale, wavefunction, correction)
     total, near, far, dot, along = apply_blocks(me, ints, fields, own, *blocks, False, entries)
     second_vector, second_image = finish(

time: 97 us -> 100 us (1.031); the launches traced: 96.4 us -> 100 us
  waiting for transfers between devices: 24.6 us -> 15.5 us
  Pallas kernels: 10.1 us -> 18.9 us
  starting transfers between devices: 57.6 us -> 60.8 us
  local copies, waits for them, and re-layouts: 1.81 us -> 2.95 us
    ppermute x28, starting transfers between devices: 45.8 us -> 56.1 us  [hop(): return lax.ppermute(value, 'term', pairs)]
    ppermute x28, waiting for transfers between devices: 19.6 us -> 10.2 us  [hop(): return lax.ppermute(value, 'term', pairs)]
    ppermute x22, starting transfers between devices: 11.8 us -> 4.7 us  [flip(): return lax.ppermute(value, 'term', [(i, i ^ 1) for i in range(16)])]
    pallas_call x2, Pallas kernels: 7.54 us -> 11.4 us  [apply_blocks(): pl.pallas_call(functools.partial(blocks_kernel, first, shape, entries), i...]
    pallas_call x0 -> x1, Pallas kernels: none -> 2.24 us  [ready_blocks(): pl.pallas_call(ready_kernel, in_specs=[HBM] * 3, out_specs=[VMEM] * 2, ou...]
    unnamed x12 -> x10, local copies, waits for them, and re-layouts: 1.81 us -> 2.95 us
  transfers between devices with their start and end apart: 50 -> 50, of which waited for: 30 -> 21; matrix products, arithmetic and copies ran while one was open for 1% -> 1% of each run, Pallas kernels for 1% -> 4%
where the time goes in v18:
time: 100 us
  starting transfers between devices  60.8 us (61%)
  Pallas kernels  18.9 us (19%)
  waiting for transfers between devices  15.5 us (16%)
  local copies, waits for them, and re-layouts  2.95 us (3%)
  between operations  1.52 us (2%)
    ppermute x28, starting transfers between devices, hop(): return lax.ppermute(value, 'term', pairs)  56.1 us
    pallas_call x2, Pallas kernels, apply_blocks(): pl.pallas_call(functools.partial(blocks_kernel, first, shape, entries), i...  11.4 us
    ppermute x28, waiting for transfers between devices, hop(): return lax.ppermute(value, 'term', pairs)  10.2 us
    ppermute x22, waiting for transfers between devices, flip(): return lax.ppermute(value, 'term', [(i, i ^ 1) for i in range(16)])  5.25 us
    ppermute x22, starting transfers between devices, flip(): return lax.ppermute(value, 'term', [(i, i ^ 1) for i in range(16)])  4.7 us
    unnamed x10, local copies, waits for them, and re-layouts  2.95 us
    pallas_call x1, Pallas kernels, ready_blocks(): pl.pallas_call(ready_kernel, in_specs=[HBM] * 3, out_specs=[VMEM] * 2, ou...  2.24 us
  transfers between devices with their start and end apart: 50, of which 21 were waited for; matrix products, arithmetic and copies ran while one was open for 1% of the time, Pallas kernels for 4%

profile of v18, /device:TPU:0, one launch (start us, length us, event | category | flops | bytes accessed | tf_op | source)
XLA Modules:
  0.0 100.4 jit_solution(17894669074391629962)
XLA Ops:
  1.1 2.6 %collective-permute-start.3 = (bf16[3,32,512]{2,1,0:T(8,128)(2,1)}, bf16[3,32,512]{2,1,0:T(8,128)(2,1)S(1)}, u32[]{:S(2)}, u32[]{:S(2)}) collective-permute-start(bf16[3,32,512]{2,1,0:T(8,128)(2,1)} %wave_ref.3), channel_id=1, source_target_pairs={{0,4},{1,3},{4,8},{5,1},{8,12},{9,5},{12,14},{13,9},{14,10},{15,13... | collective-permute-start | bytes 294920 | tf_op jit(solution)/shard_map/ppermute | solution.py:420
  4.4 1.6 %collective-permute-start.1 = (bf16[3,32,512]{2,1,0:T(8,128)(2,1)S(1)}, bf16[3,32,512]{2,1,0:T(8,128)(2,1)S(1)}, u32[]{:S(2)}, u32[]{:S(2)}) collective-permute-start(bf16[3,32,512]{2,1,0:T(8,128)(2,1)S(1)} %collective-permute-done.refs_1_), channel_id=1, source_target_pairs={{0,4},{1,3},{4,8},{5,1},{8,12},{9,5},{12,14},{13,9},{14,10},{15,13... | collective-permute-start | bytes 294920 | tf_op jit(solution)/shard_map/ppermute | solution.py:420
  6.8 1.8 %collective-permute-start.6 = (bf16[3,32,512]{2,1,0:T(8,128)(2,1)S(1)}, bf16[3,32,512]{2,1,0:T(8,128)(2,1)S(1)}, u32[]{:S(2)}, u32[]{:S(2)}) collective-permute-start(bf16[3,32,512]{2,1,0:T(8,128)(2,1)S(1)} %collective-permute-done.3.refs_2_), channel_id=1, source_target_pairs={{0,4},{1,3},{4,8},{5,1},{8,12},{9,5},{12,14},{13,9},{14,10},{15,13... | collective-permute-start | bytes 294920 | tf_op jit(solution)/shard_map/ppermute | solution.py:420
  9.1 1.6 %collective-permute-start.2 = (bf16[3,32,512]{2,1,0:T(8,128)(2,1)S(1)}, bf16[3,32,512]{2,1,0:T(8,128)(2,1)S(1)}, u32[]{:S(2)}, u32[]{:S(2)}) collective-permute-start(bf16[3,32,512]{2,1,0:T(8,128)(2,1)S(1)} %collective-permute-done.1.refs_3_), channel_id=1, source_target_pairs={{0,4},{1,3},{4,8},{5,1},{8,12},{9,5},{12,14},{13,9},{14,10},{15,13... | collective-permute-start | bytes 294920 | tf_op jit(solution)/shard_map/ppermute | solution.py:420
  11.6 2.6 %collective-permute-start.13 = (bf16[3,32,512]{2,1,0:T(8,128)(2,1)}, bf16[3,32,512]{2,1,0:T(8,128)(2,1)S(1)}, u32[]{:S(2)}, u32[]{:S(2)}) collective-permute-start(bf16[3,32,512]{2,1,0:T(8,128)(2,1)} %wave_ref.3), channel_id=1, source_target_pairs={{0,14},{1,15},{4,10},{5,11},{8,6},{9,7},{12,2},{13,3},{14,0},{15,1... | collective-permute-start | bytes 294920 | tf_op jit(solution)/shard_map/ppermute | solution.py:420
  14.3 1.8 %collective-permute-start.7 = (bf16[3,32,512]{2,1,0:T(8,128)(2,1)S(1)}, bf16[3,32,512]{2,1,0:T(8,128)(2,1)S(1)}, u32[]{:S(2)}, u32[]{:S(2)}) collective-permute-start(bf16[3,32,512]{2,1,0:T(8,128)(2,1)S(1)} %collective-permute-done.6.refs_6_), channel_id=1, source_target_pairs={{0,1},{1,0},{2,3},{3,2},{4,5},{5,4},{6,7},{7,6},{8,9},{9,8},{10,11... | collective-permute-start | bytes 294920 | tf_op jit(solution)/shard_map/ppermute | solution.py:411
  16.5 2.2 %shard_map.95 = (bf16[4,512,512]{2,1,0:T(8,128)(2,1)S(1)}, bf16[4,512,512]{2,1,0:T(8,128)(2,1)S(1)}) custom-call(bf16[8,512,512]{2,1,0:T(8,128)(2,1)} %refs_19_.3, bf16[8,512,512]{2,1,0:T(8,128)(2,1)} %refs_20_.3, bf16[3,32,512]{2,1,0:T(8,128)(2,1)S(1)} %collective-permute-done.2._.refs_7_), custom_call_target="tpu_custom_call" | custom-call | flops 2147483648 | bytes 4194304 | tf_op jit(solution)/shard_map/pallas_call | solution.py:127
  18.8 1.3 %copy-done.3 = bf16[4,512,512]{2,1,0:T(8,128)(2,1)} copy-done((bf16[4,512,512]{2,1,0:T(8,128)(2,1)}, bf16[4,512,512]{2,1,0:T(8,128)(2,1)S(1)}, u32[]{:S(2)}) %copy-start.3) | copy-done | bytes 2097176
  22.6 1.6 %copy-done.4 = bf16[4,512,512]{2,1,0:T(8,128)(2,1)S(1)} copy-done((bf16[4,512,512]{2,1,0:T(8,128)(2,1)S(1)}, bf16[4,512,512]{2,1,0:T(8,128)(2,1)}, u32[]{:S(2)}) %copy-start.4) | copy-done | bytes 2097176
  24.2 6.1 %shard_map.97 = (f32[3,512,512]{2,1,0:T(8,128)S(1)}, bf16[2,16,3200]{2,1,0:T(8,128)(2,1)S(1)}, bf16[6,16,3200]{2,1,0:T(8,128)(2,1)S(1)}, f32[8,128]{1,0:T(8,128)S(1)}, f32[8,128]{1,0:T(8,128)S(1)}) custom-call(s32[1]{0:T(128)} %bitcast.me_ref.refs_0_.refs_2_, s32[17]{0:T(128)S(1)} %pad_add_fusion.ints_ref, ...), custom_call_target="tpu_custom_call" | custom-call | flops 4294967296 | bytes 8388608 | tf_op jit(solution)/shard_map/pallas_call | solution.py:281
  32.1 3.8 %collective-permute-start.17 = (bf16[16,3200]{1,0:T(8,128)(2,1)S(1)}, bf16[16,3200]{1,0:T(8,128)(2,1)S(1)}, u32[]{:S(2)}, u32[]{:S(2)}) collective-permute-start(bf16[16,3200]{1,0:T(8,128)(2,1)S(1)} %shard_map.98), channel_id=1, source_target_pairs={{0,4},{1,3},{4,8},{5,1},{8,12},{9,5},{12,14},{13,9},{14,10},{15,13... | collective-permute-start | bytes 307208 | tf_op jit(solution)/shard_map/ppermute | solution.py:420
  36.0 1.3 %collective-permute-start.22 = (bf16[16,3200]{1,0:T(8,128)(2,1)S(1)}, bf16[16,3200]{1,0:T(8,128)(2,1)S(1)}, u32[]{:S(2)}, u32[]{:S(2)}) collective-permute-start(bf16[16,3200]{1,0:T(8,128)(2,1)S(1)} %shard_map.103), channel_id=1, source_target_pairs={{0,14},{1,15},{4,10},{5,11},{8,6},{9,7},{12,2},{13,3},{14,0},{15,1... | collective-permute-start | bytes 307208 | tf_op jit(solution)/shard_map/ppermute | solution.py:420
  38.2 4.5 %collective-permute-start.18 = (bf16[16,3200]{1,0:T(8,128)(2,1)S(1)}, bf16[16,3200]{1,0:T(8,128)(2,1)S(1)}, u32[]{:S(2)}, u32[]{:S(2)}) collective-permute-start(bf16[16,3200]{1,0:T(8,128)(2,1)S(1)} %shard_map.99), channel_id=1, source_target_pairs={{0,4},{1,3},{4,8},{5,1},{8,12},{9,5},{12,14},{13,9},{14,10},{15,13... | collective-permute-start | bytes 307208 | tf_op jit(solution)/shard_map/ppermute | solution.py:420
  43.7 1.7 %collective-permute-start.23 = (bf16[16,3200]{1,0:T(8,128)(2,1)S(1)}, bf16[16,3200]{1,0:T(8,128)(2,1)S(1)}, u32[]{:S(2)}, u32[]{:S(2)}) collective-permute-start(bf16[16,3200]{1,0:T(8,128)(2,1)S(1)} %shard_map.104), channel_id=1, source_target_pairs={{0,4},{1,3},{4,8},{5,1},{8,12},{9,5},{12,14},{13,9},{14,10},{15,13... | collective-permute-start | bytes 307208 | tf_op jit(solution)/shard_map/ppermute | solution.py:420
  45.5 2.3 %collective-permute-start.19 = (bf16[16,3200]{1,0:T(8,128)(2,1)S(1)}, bf16[16,3200]{1,0:T(8,128)(2,1)S(1)}, u32[]{:S(2)}, u32[]{:S(2)}) collective-permute-start(bf16[16,3200]{1,0:T(8,128)(2,1)S(1)} %shard_map.100), channel_id=1, source_target_pairs={{0,4},{1,3},{4,8},{5,1},{8,12},{9,5},{12,14},{13,9},{14,10},{15,13... | collective-permute-start | bytes 307208 | tf_op jit(solution)/shard_map/ppermute | solution.py:420
  48.4 1.8 %collective-permute-done.19.refs_4_ = bf16[16,3200]{1,0:T(8,128)(2,1)S(1)} collective-permute-done((bf16[16,3200]{1,0:T(8,128)(2,1)S(1)}, bf16[16,3200]{1,0:T(8,128)(2,1)S(1)}, u32[]{:S(2)}, u32[]{:S(2)}) %collective-permute-start.19) | collective-permute-done | bytes 102432 | tf_op jit(solution)/shard_map/ppermute | solution.py:420
  50.2 1.8 %shard_map.105 = (f32[3,32,512]{2,1,0:T(8,128)}, f32[3,32,512]{2,1,0:T(8,128)S(1)}, f32[3,32,512]{2,1,0:T(8,128)S(1)}, bf16[16,3200]{1,0:T(8,128)(2,1)S(1)}) custom-call(f32[8,128]{1,0:T(8,128)S(1)} %get-tuple-element.51.scale_ref.refs_16_, bf16[3,32,512]{2,1,0:T(8,128)(2,1)} %wave_ref.3, bf16[3,32,512]{2,1,0:T(8,128)(2,1)S(1)} %copy-done.2, ...), custom_call_target="tpu_custom_call" | custom-call | tf_op jit(solution)/shard_map/pallas_call | solution.py:375
  52.0 2.3 %collective-permute-start.26 = (bf16[16,3200]{1,0:T(8,128)(2,1)S(1)}, bf16[16,3200]{1,0:T(8,128)(2,1)S(1)}, u32[]{:S(2)}, u32[]{:S(2)}) collective-permute-start(bf16[16,3200]{1,0:T(8,128)(2,1)S(1)} %get-tuple-element.63.refs_0_), channel_id=1, source_target_pairs={{0,4},{1,3},{4,8},{5,1},{8,12},{9,5},{12,14},{13,9},{14,10},{15,13... | collective-permute-start | bytes 307208 | tf_op jit(solution)/shard_map/ppermute | solution.py:420
  54.2 2.3 %collective-permute-start.27 = (bf16[16,3200]{1,0:T(8,128)(2,1)S(1)}, bf16[16,3200]{1,0:T(8,128)(2,1)S(1)}, u32[]{:S(2)}, u32[]{:S(2)}) collective-permute-start(bf16[16,3200]{1,0:T(8,128)(2,1)S(1)} %collective-permute-done.25.refs_1_), channel_id=1, source_target_pairs={{0,4},{1,3},{4,8},{5,1},{8,12},{9,5},{12,14},{13,9},{14,10},{15,13... | collective-permute-start | bytes 307208 | tf_op jit(solution)/shard_map/ppermute | solution.py:420
  56.6 2.3 %collective-permute-start.30 = (bf16[16,3200]{1,0:T(8,128)(2,1)S(1)}, bf16[16,3200]{1,0:T(8,128)(2,1)S(1)}, u32[]{:S(2)}, u32[]{:S(2)}) collective-permute-start(bf16[16,3200]{1,0:T(8,128)(2,1)S(1)} %collective-permute-done.26.refs_2_), channel_id=1, source_target_pairs={{0,4},{1,3},{4,8},{5,1},{8,12},{9,5},{12,14},{13,9},{14,10},{15,13... | collective-permute-start | bytes 307208 | tf_op jit(solution)/shard_map/ppermute | solution.py:420
  58.9 2.3 %collective-permute-start.31 = (bf16[16,3200]{1,0:T(8,128)(2,1)S(1)}, bf16[16,3200]{1,0:T(8,128)(2,1)S(1)}, u32[]{:S(2)}, u32[]{:S(2)}) collective-permute-start(bf16[16,3200]{1,0:T(8,128)(2,1)S(1)} %collective-permute-done.27.refs_3_), channel_id=1, source_target_pairs={{0,4},{1,3},{4,8},{5,1},{8,12},{9,5},{12,14},{13,9},{14,10},{15,13... | collective-permute-start | bytes 307208 | tf_op jit(solution)/shard_map/ppermute | solution.py:420
  61.2 1.5 %collective-permute-start.38 = (bf16[16,3200]{1,0:T(8,128)(2,1)S(1)}, bf16[16,3200]{1,0:T(8,128)(2,1)S(1)}, u32[]{:S(2)}, u32[]{:S(2)}) collective-permute-start(bf16[16,3200]{1,0:T(8,128)(2,1)S(1)} %get-tuple-element.63.refs_0_), channel_id=1, source_target_pairs={{0,14},{1,15},{4,10},{5,11},{8,6},{9,7},{12,2},{13,3},{14,0},{15,1... | collective-permute-start | bytes 307208 | tf_op jit(solution)/shard_map/ppermute | solution.py:420
  64.0 3.7 %collective-permute-start.35 = (bf16[16,3200]{1,0:T(8,128)(2,1)S(1)}, bf16[16,3200]{1,0:T(8,128)(2,1)S(1)}, u32[]{:S(2)}, u32[]{:S(2)}) collective-permute-start(bf16[16,3200]{1,0:T(8,128)(2,1)S(1)} %collective-permute-done.31.refs_7_), channel_id=1, source_target_pairs={{0,4},{1,3},{4,8},{5,1},{8,12},{9,5},{12,14},{13,9},{14,10},{15,13... | collective-permute-start | bytes 307208 | tf_op jit(solution)/shard_map/ppermute | solution.py:420
  67.8 1.7 %collective-permute-done.38.refs_14_ = bf16[16,3200]{1,0:T(8,128)(2,1)S(1)} collective-permute-done((bf16[16,3200]{1,0:T(8,128)(2,1)S(1)}, bf16[16,3200]{1,0:T(8,128)(2,1)S(1)}, u32[]{:S(2)}, u32[]{:S(2)}) %collective-permute-start.38) | collective-permute-done | bytes 102432 | tf_op jit(solution)/shard_map/ppermute | solution.py:420
  71.9 5.3 %shard_map.106 = (f32[3,512,512]{2,1,0:T(8,128)S(1)}, bf16[2,16,3200]{2,1,0:T(8,128)(2,1)S(1)}, bf16[6,16,3200]{2,1,0:T(8,128)(2,1)S(1)}, f32[8,128]{1,0:T(8,128)S(1)}, f32[8,128]{1,0:T(8,128)S(1)}) custom-call(s32[1]{0:T(128)} %bitcast.me_ref.refs_0_.refs_2_, s32[17]{0:T(128)S(1)} %pad_add_fusion.ints_ref, bf16[16,3200]{1,0:T(8,128)(2,1)S(1)} %get-tuple-element.63.refs_0_, ...), custom_call_target="tpu_custom_call" | custom-call | flops 4294967296 | bytes 8388608 | tf_op jit(solution)/shard_map/pallas_call | solution.py:281
  79.0 5.6 %collective-permute-start.42 = (bf16[16,3200]{1,0:T(8,128)(2,1)S(1)}, bf16[16,3200]{1,0:T(8,128)(2,1)S(1)}, u32[]{:S(2)}, u32[]{:S(2)}) collective-permute-start(bf16[16,3200]{1,0:T(8,128)(2,1)S(1)} %shard_map.107), channel_id=1, source_target_pairs={{0,4},{1,3},{4,8},{5,1},{8,12},{9,5},{12,14},{13,9},{14,10},{15,13... | collective-permute-start | bytes 307208 | tf_op jit(solution)/shard_map/ppermute | solution.py:420
  84.8 2.8 %collective-permute-start.46 = (bf16[16,3200]{1,0:T(8,128)(2,1)S(1)}, bf16[16,3200]{1,0:T(8,128)(2,1)S(1)}, u32[]{:S(2)}, u32[]{:S(2)}) collective-permute-start(bf16[16,3200]{1,0:T(8,128)(2,1)S(1)} %shard_map.111), channel_id=1, source_target_pairs={{0,4},{1,3},{4,8},{5,1},{8,12},{9,5},{12,14},{13,9},{14,10},{15,13... | collective-permute-start | bytes 307208 | tf_op jit(solution)/shard_map/ppermute | solution.py:420
  87.7 3.5 %collective-permute-start.43 = (bf16[16,3200]{1,0:T(8,128)(2,1)S(1)}, bf16[16,3200]{1,0:T(8,128)(2,1)S(1)}, u32[]{:S(2)}, u32[]{:S(2)}) collective-permute-start(bf16[16,3200]{1,0:T(8,128)(2,1)S(1)} %shard_map.108), channel_id=1, source_target_pairs={{0,4},{1,3},{4,8},{5,1},{8,12},{9,5},{12,14},{13,9},{14,10},{15,13... | collective-permute-start | bytes 307208 | tf_op jit(solution)/shard_map/ppermute | solution.py:420
  92.4 1.4 %collective-permute-start.48 = (bf16[16,3200]{1,0:T(8,128)(2,1)S(1)}, bf16[16,3200]{1,0:T(8,128)(2,1)S(1)}, u32[]{:S(2)}, u32[]{:S(2)}) collective-permute-start(bf16[16,3200]{1,0:T(8,128)(2,1)S(1)} %shard_map.113), channel_id=1, source_target_pairs={{0,4},{1,3},{4,8},{5,1},{8,12},{9,5},{12,14},{13,9},{14,10},{15,13... | collective-permute-start | bytes 307208 | tf_op jit(solution)/shard_map/ppermute | solution.py:420
  93.9 2.2 %collective-permute-start.44 = (bf16[16,3200]{1,0:T(8,128)(2,1)S(1)}, bf16[16,3200]{1,0:T(8,128)(2,1)S(1)}, u32[]{:S(2)}, u32[]{:S(2)}) collective-permute-start(bf16[16,3200]{1,0:T(8,128)(2,1)S(1)} %shard_map.109), channel_id=1, source_target_pairs={{0,4},{1,3},{4,8},{5,1},{8,12},{9,5},{12,14},{13,9},{14,10},{15,13... | collective-permute-start | bytes 307208 | tf_op jit(solution)/shard_map/ppermute | solution.py:420
  97.1 1.5 %collective-permute-done.44.refs_6_ = bf16[16,3200]{1,0:T(8,128)(2,1)S(1)} collective-permute-done((bf16[16,3200]{1,0:T(8,128)(2,1)S(1)}, bf16[16,3200]{1,0:T(8,128)(2,1)S(1)}, u32[]{:S(2)}, u32[]{:S(2)}) %collective-permute-start.44) | collective-permute-done | bytes 102432 | tf_op jit(solution)/shard_map/ppermute | solution.py:420
  98.6 1.8 %shard_map.114 = (f32[3,32,512]{2,1,0:T(8,128)}, f32[3,32,512]{2,1,0:T(8,128)}) custom-call(f32[8,128]{1,0:T(8,128)S(1)} %get-tuple-element.65.along_ref, f32[8,128]{1,0:T(8,128)S(1)} %get-tuple-element.51.scale_ref.refs_16_, bf16[3,32,512]{2,1,0:T(8,128)(2,1)} %wave_ref.3, bf16[3,32,512]{2,1,0:T(8,128)(2,1)S(1)} %copy-done.2, ...), custom_call_target="tpu_custom_call" | custom-call | tf_op jit(solution)/shard_map/pallas_call | solution.py:401
  (100 shorter events, 18.3 us)
Async XLA Ops:
  1.1 5.7 %collective-permute-start.3 = (bf16[3,32,512]{2,1,0:T(8,128)(2,1)}, bf16[3,32,512]{2,1,0:T(8,128)(2,1)S(1)}, u32[]{:S(2)}, u32[]{:S(2)}) collective-permute-start(bf16[3,32,512]{2,1,0:T(8,128)(2,1)} %wave_ref.3), channel_id=1, source_target_pairs={{0,4},{1,3},{4,8},{5,1},{8,12},{9,5},{12,14},{13,9},{14,10},{15,13... | collective-permute-start | bytes 294920 | tf_op jit(solution)/shard_map/ppermute | solution.py:420
  4.4 4.7 %collective-permute-start.1 = (bf16[3,32,512]{2,1,0:T(8,128)(2,1)S(1)}, bf16[3,32,512]{2,1,0:T(8,128)(2,1)S(1)}, u32[]{:S(2)}, u32[]{:S(2)}) collective-permute-start(bf16[3,32,512]{2,1,0:T(8,128)(2,1)S(1)} %collective-permute-done.refs_1_), channel_id=1, source_target_pairs={{0,4},{1,3},{4,8},{5,1},{8,12},{9,5},{12,14},{13,9},{14,10},{15,13... | collective-permute-start | bytes 294920 | tf_op jit(solution)/shard_map/ppermute | solution.py:420
  6.8 7.4 %collective-permute-start.6 = (bf16[3,32,512]{2,1,0:T(8,128)(2,1)S(1)}, bf16[3,32,512]{2,1,0:T(8,128)(2,1)S(1)}, u32[]{:S(2)}, u32[]{:S(2)}) collective-permute-start(bf16[3,32,512]{2,1,0:T(8,128)(2,1)S(1)} %collective-permute-done.3.refs_2_), channel_id=1, source_target_pairs={{0,4},{1,3},{4,8},{5,1},{8,12},{9,5},{12,14},{13,9},{14,10},{15,13... | collective-permute-start | bytes 294920 | tf_op jit(solution)/shard_map/ppermute | solution.py:420
  9.1 6.9 %collective-permute-start.2 = (bf16[3,32,512]{2,1,0:T(8,128)(2,1)S(1)}, bf16[3,32,512]{2,1,0:T(8,128)(2,1)S(1)}, u32[]{:S(2)}, u32[]{:S(2)}) collective-permute-start(bf16[3,32,512]{2,1,0:T(8,128)(2,1)S(1)} %collective-permute-done.1.refs_3_), channel_id=1, source_target_pairs={{0,4},{1,3},{4,8},{5,1},{8,12},{9,5},{12,14},{13,9},{14,10},{15,13... | collective-permute-start | bytes 294920 | tf_op jit(solution)/shard_map/ppermute | solution.py:420
  11.6 8.5 %collective-permute-start.13 = (bf16[3,32,512]{2,1,0:T(8,128)(2,1)}, bf16[3,32,512]{2,1,0:T(8,128)(2,1)S(1)}, u32[]{:S(2)}, u32[]{:S(2)}) collective-permute-start(bf16[3,32,512]{2,1,0:T(8,128)(2,1)} %wave_ref.3), channel_id=1, source_target_pairs={{0,14},{1,15},{4,10},{5,11},{8,6},{9,7},{12,2},{13,3},{14,0},{15,1... | collective-permute-start | bytes 294920 | tf_op jit(solution)/shard_map/ppermute | solution.py:420
  14.2 5.9 %collective-permute-start.4 = (bf16[3,32,512]{2,1,0:T(8,128)(2,1)S(1)}, bf16[3,32,512]{2,1,0:T(8,128)(2,1)S(1)}, u32[]{:S(2)}, u32[]{:S(2)}) collective-permute-start(bf16[3,32,512]{2,1,0:T(8,128)(2,1)S(1)} %collective-permute-done.3.refs_2_), channel_id=1, source_target_pairs={{0,1},{1,0},{2,3},{3,2},{4,5},{5,4},{6,7},{7,6},{8,9},{9,8},{10,11... | collective-permute-start | bytes 294920 | tf_op jit(solution)/shard_map/ppermute | solution.py:411
  14.3 6.4 %collective-permute-start.9 = (bf16[3,32,512]{2,1,0:T(8,128)(2,1)S(1)}, bf16[3,32,512]{2,1,0:T(8,128)(2,1)S(1)}, u32[]{:S(2)}, u32[]{:S(2)}) collective-permute-start(bf16[3,32,512]{2,1,0:T(8,128)(2,1)S(1)} %collective-permute-done.6.refs_6_), channel_id=1, source_target_pairs={{0,4},{1,3},{4,8},{5,1},{8,12},{9,5},{12,14},{13,9},{14,10},{15,13... | collective-permute-start | bytes 294920 | tf_op jit(solution)/shard_map/ppermute | solution.py:420
  14.3 6.4 %collective-permute-start.7 = (bf16[3,32,512]{2,1,0:T(8,128)(2,1)S(1)}, bf16[3,32,512]{2,1,0:T(8,128)(2,1)S(1)}, u32[]{:S(2)}, u32[]{:S(2)}) collective-permute-start(bf16[3,32,512]{2,1,0:T(8,128)(2,1)S(1)} %collective-permute-done.6.refs_6_), channel_id=1, source_target_pairs={{0,1},{1,0},{2,3},{3,2},{4,5},{5,4},{6,7},{7,6},{8,9},{9,8},{10,11... | collective-permute-start | bytes 294920 | tf_op jit(solution)/shard_map/ppermute | solution.py:411
  16.1 5.1 %collective-permute-start.10 = (bf16[3,32,512]{2,1,0:T(8,128)(2,1)S(1)}, bf16[3,32,512]{2,1,0:T(8,128)(2,1)S(1)}, u32[]{:S(2)}, u32[]{:S(2)}) collective-permute-start(bf16[3,32,512]{2,1,0:T(8,128)(2,1)S(1)} %collective-permute-done.2._.refs_7_), channel_id=1, source_target_pairs={{0,4},{1,3},{4,8},{5,1},{8,12},{9,5},{12,14},{13,9},{14,10},{15,13... | collective-permute-start | bytes 294920 | tf_op jit(solution)/shard_map/ppermute | solution.py:420
  32.0 5.3 %collective-permute-start.20 = (bf16[16,3200]{1,0:T(8,128)(2,1)S(1)}, bf16[16,3200]{1,0:T(8,128)(2,1)S(1)}, u32[]{:S(2)}, u32[]{:S(2)}) collective-permute-start(bf16[16,3200]{1,0:T(8,128)(2,1)S(1)} %shard_map.101), channel_id=1, source_target_pairs={{0,4},{1,3},{4,8},{5,1},{8,12},{9,5},{12,14},{13,9},{14,10},{15,13... | collective-permute-start | bytes 307208 | tf_op jit(solution)/shard_map/ppermute | solution.py:420
  32.1 6.0 %collective-permute-start.17 = (bf16[16,3200]{1,0:T(8,128)(2,1)S(1)}, bf16[16,3200]{1,0:T(8,128)(2,1)S(1)}, u32[]{:S(2)}, u32[]{:S(2)}) collective-permute-start(bf16[16,3200]{1,0:T(8,128)(2,1)S(1)} %shard_map.98), channel_id=1, source_target_pairs={{0,4},{1,3},{4,8},{5,1},{8,12},{9,5},{12,14},{13,9},{14,10},{15,13... | collective-permute-start | bytes 307208 | tf_op jit(solution)/shard_map/ppermute | solution.py:420
  36.0 7.6 %collective-permute-start.22 = (bf16[16,3200]{1,0:T(8,128)(2,1)S(1)}, bf16[16,3200]{1,0:T(8,128)(2,1)S(1)}, u32[]{:S(2)}, u32[]{:S(2)}) collective-permute-start(bf16[16,3200]{1,0:T(8,128)(2,1)S(1)} %shard_map.103), channel_id=1, source_target_pairs={{0,14},{1,15},{4,10},{5,11},{8,6},{9,7},{12,2},{13,3},{14,0},{15,1... | collective-permute-start | bytes 307208 | tf_op jit(solution)/shard_map/ppermute | solution.py:420
  37.4 6.2 %collective-permute-start.21 = (bf16[16,3200]{1,0:T(8,128)(2,1)S(1)}, bf16[16,3200]{1,0:T(8,128)(2,1)S(1)}, u32[]{:S(2)}, u32[]{:S(2)}) collective-permute-start(bf16[16,3200]{1,0:T(8,128)(2,1)S(1)} %shard_map.102), channel_id=1, source_target_pairs={{0,4},{1,3},{4,8},{5,1},{8,12},{9,5},{12,14},{13,9},{14,10},{15,13... | collective-permute-start | bytes 307208 | tf_op jit(solution)/shard_map/ppermute | solution.py:420
  38.2 7.2 %collective-permute-start.18 = (bf16[16,3200]{1,0:T(8,128)(2,1)S(1)}, bf16[16,3200]{1,0:T(8,128)(2,1)S(1)}, u32[]{:S(2)}, u32[]{:S(2)}) collective-permute-start(bf16[16,3200]{1,0:T(8,128)(2,1)S(1)} %shard_map.99), channel_id=1, source_target_pairs={{0,4},{1,3},{4,8},{5,1},{8,12},{9,5},{12,14},{13,9},{14,10},{15,13... | collective-permute-start | bytes 307208 | tf_op jit(solution)/shard_map/ppermute | solution.py:420
  43.7 4.7 %collective-permute-start.23 = (bf16[16,3200]{1,0:T(8,128)(2,1)S(1)}, bf16[16,3200]{1,0:T(8,128)(2,1)S(1)}, u32[]{:S(2)}, u32[]{:S(2)}) collective-permute-start(bf16[16,3200]{1,0:T(8,128)(2,1)S(1)} %shard_map.104), channel_id=1, source_target_pairs={{0,4},{1,3},{4,8},{5,1},{8,12},{9,5},{12,14},{13,9},{14,10},{15,13... | collective-permute-start | bytes 307208 | tf_op jit(solution)/shard_map/ppermute | solution.py:420
  45.5 4.7 %collective-permute-start.19 = (bf16[16,3200]{1,0:T(8,128)(2,1)S(1)}, bf16[16,3200]{1,0:T(8,128)(2,1)S(1)}, u32[]{:S(2)}, u32[]{:S(2)}) collective-permute-start(bf16[16,3200]{1,0:T(8,128)(2,1)S(1)} %shard_map.100), channel_id=1, source_target_pairs={{0,4},{1,3},{4,8},{5,1},{8,12},{9,5},{12,14},{13,9},{14,10},{15,13... | collective-permute-start | bytes 307208 | tf_op jit(solution)/shard_map/ppermute | solution.py:420
  54.2 4.7 %collective-permute-start.27 = (bf16[16,3200]{1,0:T(8,128)(2,1)S(1)}, bf16[16,3200]{1,0:T(8,128)(2,1)S(1)}, u32[]{:S(2)}, u32[]{:S(2)}) collective-permute-start(bf16[16,3200]{1,0:T(8,128)(2,1)S(1)} %collective-permute-done.25.refs_1_), channel_id=1, source_target_pairs={{0,4},{1,3},{4,8},{5,1},{8,12},{9,5},{12,14},{13,9},{14,10},{15,13... | collective-permute-start | bytes 307208 | tf_op jit(solution)/shard_map/ppermute | solution.py:420
  56.6 6.0 %collective-permute-start.30 = (bf16[16,3200]{1,0:T(8,128)(2,1)S(1)}, bf16[16,3200]{1,0:T(8,128)(2,1)S(1)}, u32[]{:S(2)}, u32[]{:S(2)}) collective-permute-start(bf16[16,3200]{1,0:T(8,128)(2,1)S(1)} %collective-permute-done.26.refs_2_), channel_id=1, source_target_pairs={{0,4},{1,3},{4,8},{5,1},{8,12},{9,5},{12,14},{13,9},{14,10},{15,13... | collective-permute-start | bytes 307208 | tf_op jit(solution)/shard_map/ppermute | solution.py:420
  58.9 5.1 %collective-permute-start.31 = (bf16[16,3200]{1,0:T(8,128)(2,1)S(1)}, bf16[16,3200]{1,0:T(8,128)(2,1)S(1)}, u32[]{:S(2)}, u32[]{:S(2)}) collective-permute-start(bf16[16,3200]{1,0:T(8,128)(2,1)S(1)} %collective-permute-done.27.refs_3_), channel_id=1, source_target_pairs={{0,4},{1,3},{4,8},{5,1},{8,12},{9,5},{12,14},{13,9},{14,10},{15,13... | collective-permute-start | bytes 307208 | tf_op jit(solution)/shard_map/ppermute | solution.py:420
  61.2 6.6 %collective-permute-start.28 = (bf16[16,3200]{1,0:T(8,128)(2,1)S(1)}, bf16[16,3200]{1,0:T(8,128)(2,1)S(1)}, u32[]{:S(2)}, u32[]{:S(2)}) collective-permute-start(bf16[16,3200]{1,0:T(8,128)(2,1)S(1)} %collective-permute-done.26.refs_2_), channel_id=1, source_target_pairs={{0,1},{1,0},{2,3},{3,2},{4,5},{5,4},{6,7},{7,6},{8,9},{9,8},{10,11... | collective-permute-start | bytes 307208 | tf_op jit(solution)/shard_map/ppermute | solution.py:411
  61.2 8.3 %collective-permute-start.38 = (bf16[16,3200]{1,0:T(8,128)(2,1)S(1)}, bf16[16,3200]{1,0:T(8,128)(2,1)S(1)}, u32[]{:S(2)}, u32[]{:S(2)}) collective-permute-start(bf16[16,3200]{1,0:T(8,128)(2,1)S(1)} %get-tuple-element.63.refs_0_), channel_id=1, source_target_pairs={{0,14},{1,15},{4,10},{5,11},{8,6},{9,7},{12,2},{13,3},{14,0},{15,1... | collective-permute-start | bytes 307208 | tf_op jit(solution)/shard_map/ppermute | solution.py:420
  62.6 6.9 %collective-permute-start.34 = (bf16[16,3200]{1,0:T(8,128)(2,1)S(1)}, bf16[16,3200]{1,0:T(8,128)(2,1)S(1)}, u32[]{:S(2)}, u32[]{:S(2)}) collective-permute-start(bf16[16,3200]{1,0:T(8,128)(2,1)S(1)} %collective-permute-done.30.refs_6_), channel_id=1, source_target_pairs={{0,4},{1,3},{4,8},{5,1},{8,12},{9,5},{12,14},{13,9},{14,10},{15,13... | collective-permute-start | bytes 307208 | tf_op jit(solution)/shard_map/ppermute | solution.py:420
  63.6 6.4 %collective-permute-start.32 = (bf16[16,3200]{1,0:T(8,128)(2,1)S(1)}, bf16[16,3200]{1,0:T(8,128)(2,1)S(1)}, u32[]{:S(2)}, u32[]{:S(2)}) collective-permute-start(bf16[16,3200]{1,0:T(8,128)(2,1)S(1)} %collective-permute-done.30.refs_6_), channel_id=1, source_target_pairs={{0,1},{1,0},{2,3},{3,2},{4,5},{5,4},{6,7},{7,6},{8,9},{9,8},{10,11... | collective-permute-start | bytes 307208 | tf_op jit(solution)/shard_map/ppermute | solution.py:411
  64.0 6.5 %collective-permute-start.35 = (bf16[16,3200]{1,0:T(8,128)(2,1)S(1)}, bf16[16,3200]{1,0:T(8,128)(2,1)S(1)}, u32[]{:S(2)}, u32[]{:S(2)}) collective-permute-start(bf16[16,3200]{1,0:T(8,128)(2,1)S(1)} %collective-permute-done.31.refs_7_), channel_id=1, source_target_pairs={{0,4},{1,3},{4,8},{5,1},{8,12},{9,5},{12,14},{13,9},{14,10},{15,13... | collective-permute-start | bytes 307208 | tf_op jit(solution)/shard_map/ppermute | solution.py:420
  78.7 5.9 %collective-permute-start.41 = (bf16[6,16,3200]{2,1,0:T(8,128)(2,1)S(1)}, bf16[6,16,3200]{2,1,0:T(8,128)(2,1)S(1)}, u32[]{:S(2)}, u32[]{:S(2)}) collective-permute-start(bf16[6,16,3200]{2,1,0:T(8,128)(2,1)S(1)} %get-tuple-element.70), channel_id=1, source_target_pairs={{0,1},{1,0},{2,3},{3,2},{4,5},{5,4},{6,7},{7,6},{8,9},{9,8},{10,11... | collective-permute-start | bytes 1843208 | tf_op jit(solution)/shard_map/ppermute | solution.py:411
  78.9 5.9 %collective-permute-start.45 = (bf16[16,3200]{1,0:T(8,128)(2,1)S(1)}, bf16[16,3200]{1,0:T(8,128)(2,1)S(1)}, u32[]{:S(2)}, u32[]{:S(2)}) collective-permute-start(bf16[16,3200]{1,0:T(8,128)(2,1)S(1)} %shard_map.110), channel_id=1, source_target_pairs={{0,4},{1,3},{4,8},{5,1},{8,12},{9,5},{12,14},{13,9},{14,10},{15,13... | collective-permute-start | bytes 307208 | tf_op jit(solution)/shard_map/ppermute | solution.py:420
  79.0 8.6 %collective-permute-start.42 = (bf16[16,3200]{1,0:T(8,128)(2,1)S(1)}, bf16[16,3200]{1,0:T(8,128)(2,1)S(1)}, u32[]{:S(2)}, u32[]{:S(2)}) collective-permute-start(bf16[16,3200]{1,0:T(8,128)(2,1)S(1)} %shard_map.107), channel_id=1, source_target_pairs={{0,4},{1,3},{4,8},{5,1},{8,12},{9,5},{12,14},{13,9},{14,10},{15,13... | collective-permute-start | bytes 307208 | tf_op jit(solution)/shard_map/ppermute | solution.py:420
  84.7 7.6 %collective-permute-start.47 = (bf16[16,3200]{1,0:T(8,128)(2,1)S(1)}, bf16[16,3200]{1,0:T(8,128)(2,1)S(1)}, u32[]{:S(2)}, u32[]{:S(2)}) collective-permute-start(bf16[16,3200]{1,0:T(8,128)(2,1)S(1)} %shard_map.112), channel_id=1, source_target_pairs={{0,14},{1,15},{4,10},{5,11},{8,6},{9,7},{12,2},{13,3},{14,0},{15,1... | collective-permute-start | bytes 307208 | tf_op jit(solution)/shard_map/ppermute | solution.py:420
  84.8 7.5 %collective-permute-start.46 = (bf16[16,3200]{1,0:T(8,128)(2,1)S(1)}, bf16[16,3200]{1,0:T(8,128)(2,1)S(1)}, u32[]{:S(2)}, u32[]{:S(2)}) collective-permute-start(bf16[16,3200]{1,0:T(8,128)(2,1)S(1)} %shard_map.111), channel_id=1, source_target_pairs={{0,4},{1,3},{4,8},{5,1},{8,12},{9,5},{12,14},{13,9},{14,10},{15,13... | collective-permute-start | bytes 307208 | tf_op jit(solution)/shard_map/ppermute | solution.py:420
  87.7 6.1 %collective-permute-start.43 = (bf16[16,3200]{1,0:T(8,128)(2,1)S(1)}, bf16[16,3200]{1,0:T(8,128)(2,1)S(1)}, u32[]{:S(2)}, u32[]{:S(2)}) collective-permute-start(bf16[16,3200]{1,0:T(8,128)(2,1)S(1)} %shard_map.108), channel_id=1, source_target_pairs={{0,4},{1,3},{4,8},{5,1},{8,12},{9,5},{12,14},{13,9},{14,10},{15,13... | collective-permute-start | bytes 307208 | tf_op jit(solution)/shard_map/ppermute | solution.py:420
  92.4 4.7 %collective-permute-start.48 = (bf16[16,3200]{1,0:T(8,128)(2,1)S(1)}, bf16[16,3200]{1,0:T(8,128)(2,1)S(1)}, u32[]{:S(2)}, u32[]{:S(2)}) collective-permute-start(bf16[16,3200]{1,0:T(8,128)(2,1)S(1)} %shard_map.113), channel_id=1, source_target_pairs={{0,4},{1,3},{4,8},{5,1},{8,12},{9,5},{12,14},{13,9},{14,10},{15,13... | collective-permute-start | bytes 307208 | tf_op jit(solution)/shard_map/ppermute | solution.py:420
  93.9 4.7 %collective-permute-start.44 = (bf16[16,3200]{1,0:T(8,128)(2,1)S(1)}, bf16[16,3200]{1,0:T(8,128)(2,1)S(1)}, u32[]{:S(2)}, u32[]{:S(2)}) collective-permute-start(bf16[16,3200]{1,0:T(8,128)(2,1)S(1)} %shard_map.109), channel_id=1, source_target_pairs={{0,4},{1,3},{4,8},{5,1},{8,12},{9,5},{12,14},{13,9},{14,10},{15,13... | collective-permute-start | bytes 307208 | tf_op jit(solution)/shard_map/ppermute | solution.py:420
  (23 other events, 106.5 us)

commit v19 on v18

--- a/solution.py
+++ b/solution.py
@@ -12,9 +12,9 @@
 HBM = pl.BlockSpec(memory_space=pltpu.HBM)
 PARAMS = pltpu.CompilerParams(vmem_limit_bytes=16 * 1024 * 1024)
 READY_PARAMS = pltpu.CompilerParams(vmem_limit_bytes=48 * 1024 * 1024)
-FIRST_PARAMS = pltpu.CompilerParams(vmem_limit_bytes=43 * 1024 * 1024)
+FIRST_PARAMS = pltpu.CompilerParams(vmem_limit_bytes=44 * 1024 * 1024)
 HALF = 16
-READY = 4
+READY = 2
 GROUP = 2
 LANES = 128
 
@@ -135,7 +135,8 @@
     )(left, right, after)
 
 
-def square_kernel(wave_ref, diag_ref, square_ref):
+def square_kernel(wave_ref, diag_ref, square_ref, own_ref):
+    own_ref[...] = diag_ref[...]
     square = jnp.zeros((8, 128), jnp.float32)
     for s in range(wave_ref.shape[0]):
         wave = wave_ref[s].astype(jnp.float32)
@@ -147,8 +148,11 @@
     return pl.pallas_call(
         square_kernel,
         in_specs=[VMEM, VMEM],
-        out_specs=VMEM,
-        out_shape=jax.ShapeDtypeStruct((8, 128), jnp.float32),
+        out_specs=[VMEM, VMEM],
+        out_shape=[
+            jax.ShapeDtypeStruct((8, 128), jnp.float32),
+            jax.ShapeDtypeStruct(diag.shape, diag.dtype),
+        ],
         compiler_params=PARAMS,
     )(wave, diag)
 
@@ -473,22 +477,22 @@
         lambda _: copied(wavefunction),
         lambda _, own: weighted_square(own, diagonal),
     )
-    (_, *fields), (ints, own, square), ready = gather(
+    (_, *fields), (ints, wave, (square, diag)), ready = gather(
         wavefunction, beside, (left_blocks, right_blocks)
     )
-    fields = [own, *fields]
+    fields = [wave, *fields]
     blocks = (left_blocks, right_blocks, shape)
     total, near, far, dot, scale = apply_blocks(
         me, ints, fields, (square, *ready), *blocks, True, entries
     )
     first_image, terms, correction, message = davidson_step(
-        scale, wavefunction, diagonal, scatter(shape, me, total, near, far, dot), entries
+        scale, wave, diag, scatter(shape, me, total, near, far, dot), entries
     )
     fields, *_ = gather(message)
-    own = (scale, wavefunction, correction)
+    own = (scale, wave, correction)
     total, near, far, dot, along = apply_blocks(me, ints, fields, own, *blocks, False, entries)
     second_vector, second_image = finish(
-        along, scale, wavefunction, diagonal, terms, correction,
+        along, scale, wave, diag, terms, correction,
         scatter(shape, me, total, near, far, dot), entries,
     )
     return (first_image, second_vector, second_image)

time: 100 us -> 96.6 us (0.966); the launches traced: 100 us -> 95.2 us
  starting transfers between devices: 60.8 us -> 35.4 us
  waiting for transfers between devices: 15.5 us -> 37.8 us
  local copies, waits for them, and re-layouts: 2.95 us -> 1.79 us
    ppermute x28, starting transfers between devices: 56.1 us -> 32 us  [hop(): return lax.ppermute(value, 'term', pairs)]
    ppermute x28, waiting for transfers between devices: 10.2 us -> 30.3 us  [hop(): return lax.ppermute(value, 'term', pairs)]
    pallas_call x2, Pallas kernels: 11.4 us -> 13.9 us  [apply_blocks(): pl.pallas_call(functools.partial(blocks_kernel, first, shape, entries), i...]
    ppermute x22, waiting for transfers between devices: 5.25 us -> 7.52 us  [flip(): return lax.ppermute(value, 'term', [(i, i ^ 1) for i in range(16)])]
    ppermute x22, starting transfers between devices: 4.7 us -> 3.39 us  [flip(): return lax.ppermute(value, 'term', [(i, i ^ 1) for i in range(16)])]
    unnamed x10, local copies, waits for them, and re-layouts: 2.95 us -> 1.79 us
  transfers between devices with their start and end apart: 50 -> 50, of which waited for: 21 -> 34; matrix products, arithmetic and copies ran while one was open for 1% -> 1% of each run, Pallas kernels for 4% -> 2%
where the time goes in v19:
time: 96.6 us; the launch traced here: 95.2 us
  waiting for transfers between devices  37.8 us (39%)
  starting transfers between devices  35.4 us (37%)
  Pallas kernels  18 us (19%)
  local copies, waits for them, and re-layouts  1.79 us (2%)
  between operations  1.5 us (2%)
    ppermute x28, starting transfers between devices, hop(): return lax.ppermute(value, 'term', pairs)  32 us
    ppermute x28, waiting for transfers between devices, hop(): return lax.ppermute(value, 'term', pairs)  30.3 us
    pallas_call x2, Pallas kernels, apply_blocks(): pl.pallas_call(functools.partial(blocks_kernel, first, shape, entries), i...  13.9 us
    ppermute x22, waiting for transfers between devices, flip(): return lax.ppermute(value, 'term', [(i, i ^ 1) for i in range(16)])  7.52 us
    ppermute x22, starting transfers between devices, flip(): return lax.ppermute(value, 'term', [(i, i ^ 1) for i in range(16)])  3.39 us
  transfers between devices with their start and end apart: 50, of which 34 were waited for; matrix products, arithmetic and copies ran while one was open for 1% of the time, Pallas kernels for 2%

profile of v19, /device:TPU:0, one launch (start us, length us, event | category | flops | bytes accessed | tf_op | source)
XLA Modules:
  0.0 95.2 jit_solution(14342228701523278180)
XLA Ops:
  1.1 2.6 %collective-permute-start.3 = (bf16[3,32,512]{2,1,0:T(8,128)(2,1)}, bf16[3,32,512]{2,1,0:T(8,128)(2,1)S(1)}, u32[]{:S(2)}, u32[]{:S(2)}) collective-permute-start(bf16[3,32,512]{2,1,0:T(8,128)(2,1)} %in_ref.1), channel_id=1, source_target_pairs={{0,4},{1,3},{4,8},{5,1},{8,12},{9,5},{12,14},{13,9},{14,10},{15,13... | collective-permute-start | bytes 294920 | tf_op jit(solution)/shard_map/ppermute | solution.py:424
  4.4 1.6 %collective-permute-start.1 = (bf16[3,32,512]{2,1,0:T(8,128)(2,1)S(1)}, bf16[3,32,512]{2,1,0:T(8,128)(2,1)S(1)}, u32[]{:S(2)}, u32[]{:S(2)}) collective-permute-start(bf16[3,32,512]{2,1,0:T(8,128)(2,1)S(1)} %collective-permute-done.refs_1_), channel_id=1, source_target_pairs={{0,4},{1,3},{4,8},{5,1},{8,12},{9,5},{12,14},{13,9},{14,10},{15,13... | collective-permute-start | bytes 294920 | tf_op jit(solution)/shard_map/ppermute | solution.py:424
  6.8 1.8 %collective-permute-start.6 = (bf16[3,32,512]{2,1,0:T(8,128)(2,1)S(1)}, bf16[3,32,512]{2,1,0:T(8,128)(2,1)S(1)}, u32[]{:S(2)}, u32[]{:S(2)}) collective-permute-start(bf16[3,32,512]{2,1,0:T(8,128)(2,1)S(1)} %collective-permute-done.3.refs_2_), channel_id=1, source_target_pairs={{0,4},{1,3},{4,8},{5,1},{8,12},{9,5},{12,14},{13,9},{14,10},{15,13... | collective-permute-start | bytes 294920 | tf_op jit(solution)/shard_map/ppermute | solution.py:424
  9.1 1.6 %collective-permute-start.2 = (bf16[3,32,512]{2,1,0:T(8,128)(2,1)S(1)}, bf16[3,32,512]{2,1,0:T(8,128)(2,1)S(1)}, u32[]{:S(2)}, u32[]{:S(2)}) collective-permute-start(bf16[3,32,512]{2,1,0:T(8,128)(2,1)S(1)} %collective-permute-done.1.refs_3_), channel_id=1, source_target_pairs={{0,4},{1,3},{4,8},{5,1},{8,12},{9,5},{12,14},{13,9},{14,10},{15,13... | collective-permute-start | bytes 294920 | tf_op jit(solution)/shard_map/ppermute | solution.py:424
  12.5 2.6 %collective-permute-start.13 = (bf16[3,32,512]{2,1,0:T(8,128)(2,1)S(1)}, bf16[3,32,512]{2,1,0:T(8,128)(2,1)S(1)}, u32[]{:S(2)}, u32[]{:S(2)}) collective-permute-start(bf16[3,32,512]{2,1,0:T(8,128)(2,1)S(1)} %copy-done.4), channel_id=1, source_target_pairs={{0,14},{1,15},{4,10},{5,11},{8,6},{9,7},{12,2},{13,3},{14,0},{15,1... | collective-permute-start | bytes 294920 | tf_op jit(solution)/shard_map/ppermute | solution.py:424
  16.1 1.6 %shard_map.95 = (bf16[2,512,512]{2,1,0:T(8,128)(2,1)S(1)}, bf16[2,512,512]{2,1,0:T(8,128)(2,1)S(1)}) custom-call(bf16[8,512,512]{2,1,0:T(8,128)(2,1)} %refs_19_.3, bf16[8,512,512]{2,1,0:T(8,128)(2,1)} %refs_20_.3, bf16[3,32,512]{2,1,0:T(8,128)(2,1)S(1)} %collective-permute-done.2._.refs_7_), custom_call_target="tpu_custom_call" | custom-call | flops 2147483648 | bytes 4194304 | tf_op jit(solution)/shard_map/pallas_call | solution.py:127
  17.7 2.3 %collective-permute-done.13.refs_14_ = bf16[3,32,512]{2,1,0:T(8,128)(2,1)S(1)} collective-permute-done((bf16[3,32,512]{2,1,0:T(8,128)(2,1)S(1)}, bf16[3,32,512]{2,1,0:T(8,128)(2,1)S(1)}, u32[]{:S(2)}, u32[]{:S(2)}) %collective-permute-start.13) | collective-permute-done | bytes 98336 | tf_op jit(solution)/shard_map/ppermute | solution.py:424
  21.0 1.0 %collective-permute-done.10.refs_11_ = bf16[3,32,512]{2,1,0:T(8,128)(2,1)S(1)} collective-permute-done((bf16[3,32,512]{2,1,0:T(8,128)(2,1)S(1)}, bf16[3,32,512]{2,1,0:T(8,128)(2,1)S(1)}, u32[]{:S(2)}, u32[]{:S(2)}) %collective-permute-start.10) | collective-permute-done | bytes 98336 | tf_op jit(solution)/shard_map/ppermute | solution.py:424
  22.4 1.1 %collective-permute-done.12.refs_13_ = bf16[3,32,512]{2,1,0:T(8,128)(2,1)} collective-permute-done((bf16[3,32,512]{2,1,0:T(8,128)(2,1)S(1)}, bf16[3,32,512]{2,1,0:T(8,128)(2,1)}, u32[]{:S(2)}, u32[]{:S(2)}) %collective-permute-start.12) | collective-permute-done | bytes 98336 | tf_op jit(solution)/shard_map/ppermute | solution.py:415
  23.4 7.7 %shard_map.97 = (f32[3,512,512]{2,1,0:T(8,128)S(1)}, bf16[2,16,3200]{2,1,0:T(8,128)(2,1)S(1)}, bf16[6,16,3200]{2,1,0:T(8,128)(2,1)S(1)}, f32[8,128]{1,0:T(8,128)S(1)}, f32[8,128]{1,0:T(8,128)S(1)}) custom-call(s32[1]{0:T(128)} %bitcast.me_ref.refs_0_.refs_2_, s32[17]{0:T(128)S(1)} %pad_add_fusion.ints_ref, ...), custom_call_target="tpu_custom_call" | custom-call | flops 4294967296 | bytes 8388608 | tf_op jit(solution)/shard_map/pallas_call | solution.py:285
  31.4 1.3 %collective-permute-done.15.other_ref = bf16[2,16,3200]{2,1,0:T(8,128)(2,1)S(1)} collective-permute-done((bf16[2,16,3200]{2,1,0:T(8,128)(2,1)S(1)}, bf16[2,16,3200]{2,1,0:T(8,128)(2,1)S(1)}, u32[]{:S(2)}, u32[]{:S(2)}) %collective-permute-start.15) | collective-permute-done | bytes 204832 | tf_op jit(solution)/shard_map/ppermute | solution.py:415
  34.8 2.5 %collective-permute-start.22 = (bf16[16,3200]{1,0:T(8,128)(2,1)S(1)}, bf16[16,3200]{1,0:T(8,128)(2,1)S(1)}, u32[]{:S(2)}, u32[]{:S(2)}) collective-permute-start(bf16[16,3200]{1,0:T(8,128)(2,1)S(1)} %shard_map.103), channel_id=1, source_target_pairs={{0,14},{1,15},{4,10},{5,11},{8,6},{9,7},{12,2},{13,3},{14,0},{15,1... | collective-permute-start | bytes 307208 | tf_op jit(solution)/shard_map/ppermute | solution.py:424
  38.8 1.1 %collective-permute-start.18 = (bf16[16,3200]{1,0:T(8,128)(2,1)S(1)}, bf16[16,3200]{1,0:T(8,128)(2,1)S(1)}, u32[]{:S(2)}, u32[]{:S(2)}) collective-permute-start(bf16[16,3200]{1,0:T(8,128)(2,1)S(1)} %shard_map.99), channel_id=1, source_target_pairs={{0,4},{1,3},{4,8},{5,1},{8,12},{9,5},{12,14},{13,9},{14,10},{15,13... | collective-permute-start | bytes 307208 | tf_op jit(solution)/shard_map/ppermute | solution.py:424
  39.9 2.9 %collective-permute-done.22.refs_6_ = bf16[16,3200]{1,0:T(8,128)(2,1)S(1)} collective-permute-done((bf16[16,3200]{1,0:T(8,128)(2,1)S(1)}, bf16[16,3200]{1,0:T(8,128)(2,1)S(1)}, u32[]{:S(2)}, u32[]{:S(2)}) %collective-permute-start.22) | collective-permute-done | bytes 102432 | tf_op jit(solution)/shard_map/ppermute | solution.py:424
  42.7 1.0 %collective-permute-done.21.refs_0_ = bf16[16,3200]{1,0:T(8,128)(2,1)S(1)} collective-permute-done((bf16[16,3200]{1,0:T(8,128)(2,1)S(1)}, bf16[16,3200]{1,0:T(8,128)(2,1)S(1)}, u32[]{:S(2)}, u32[]{:S(2)}) %collective-permute-start.21) | collective-permute-done | bytes 102432 | tf_op jit(solution)/shard_map/ppermute | solution.py:424
  44.8 1.0 %collective-permute-start.19 = (bf16[16,3200]{1,0:T(8,128)(2,1)S(1)}, bf16[16,3200]{1,0:T(8,128)(2,1)S(1)}, u32[]{:S(2)}, u32[]{:S(2)}) collective-permute-start(bf16[16,3200]{1,0:T(8,128)(2,1)S(1)} %shard_map.100), channel_id=1, source_target_pairs={{0,4},{1,3},{4,8},{5,1},{8,12},{9,5},{12,14},{13,9},{14,10},{15,13... | collective-permute-start | bytes 307208 | tf_op jit(solution)/shard_map/ppermute | solution.py:424
  45.9 2.6 %collective-permute-done.23 = bf16[16,3200]{1,0:T(8,128)(2,1)S(1)} collective-permute-done((bf16[16,3200]{1,0:T(8,128)(2,1)S(1)}, bf16[16,3200]{1,0:T(8,128)(2,1)S(1)}, u32[]{:S(2)}, u32[]{:S(2)}) %collective-permute-start.23) | collective-permute-done | bytes 102432 | tf_op jit(solution)/shard_map/ppermute | solution.py:424
  48.5 1.1 %collective-permute-done.19.refs_4_ = bf16[16,3200]{1,0:T(8,128)(2,1)S(1)} collective-permute-done((bf16[16,3200]{1,0:T(8,128)(2,1)S(1)}, bf16[16,3200]{1,0:T(8,128)(2,1)S(1)}, u32[]{:S(2)}, u32[]{:S(2)}) %collective-permute-start.19) | collective-permute-done | bytes 102432 | tf_op jit(solution)/shard_map/ppermute | solution.py:424
  52.8 2.7 %collective-permute-done.26.refs_2_ = bf16[16,3200]{1,0:T(8,128)(2,1)S(1)} collective-permute-done((bf16[16,3200]{1,0:T(8,128)(2,1)S(1)}, bf16[16,3200]{1,0:T(8,128)(2,1)S(1)}, u32[]{:S(2)}, u32[]{:S(2)}) %collective-permute-start.26) | collective-permute-done | bytes 102432 | tf_op jit(solution)/shard_map/ppermute | solution.py:424
  57.4 2.8 %collective-permute-start.38 = (bf16[16,3200]{1,0:T(8,128)(2,1)S(1)}, bf16[16,3200]{1,0:T(8,128)(2,1)S(1)}, u32[]{:S(2)}, u32[]{:S(2)}) collective-permute-start(bf16[16,3200]{1,0:T(8,128)(2,1)S(1)} %get-tuple-element.67.refs_0_), channel_id=1, source_target_pairs={{0,14},{1,15},{4,10},{5,11},{8,6},{9,7},{12,2},{13,3},{14,0},{15,1... | collective-permute-start | bytes 307208 | tf_op jit(solution)/shard_map/ppermute | solution.py:424
  62.5 3.2 %collective-permute-done.38.refs_14_ = bf16[16,3200]{1,0:T(8,128)(2,1)S(1)} collective-permute-done((bf16[16,3200]{1,0:T(8,128)(2,1)S(1)}, bf16[16,3200]{1,0:T(8,128)(2,1)S(1)}, u32[]{:S(2)}, u32[]{:S(2)}) %collective-permute-start.38) | collective-permute-done | bytes 102432 | tf_op jit(solution)/shard_map/ppermute | solution.py:424
  65.7 0.9 collective-permute-done.34.refs_10_
  68.1 0.9 collective-permute-done.37.refs_13_
  69.0 6.2 %shard_map.106 = (f32[3,512,512]{2,1,0:T(8,128)S(1)}, bf16[2,16,3200]{2,1,0:T(8,128)(2,1)S(1)}, bf16[6,16,3200]{2,1,0:T(8,128)(2,1)S(1)}, f32[8,128]{1,0:T(8,128)S(1)}, f32[8,128]{1,0:T(8,128)S(1)}) custom-call(s32[1]{0:T(128)} %bitcast.me_ref.refs_0_.refs_2_, s32[17]{0:T(128)S(1)} %pad_add_fusion.ints_ref, bf16[16,3200]{1,0:T(8,128)(2,1)S(1)} %get-tuple-element.67.refs_0_, ...), custom_call_target="tpu_custom_call" | custom-call | flops 4294967296 | bytes 8388608 | tf_op jit(solution)/shard_map/pallas_call | solution.py:285
  75.4 1.3 %collective-permute-done.40.other_ref = bf16[2,16,3200]{2,1,0:T(8,128)(2,1)S(1)} collective-permute-done((bf16[2,16,3200]{2,1,0:T(8,128)(2,1)S(1)}, bf16[2,16,3200]{2,1,0:T(8,128)(2,1)S(1)}, u32[]{:S(2)}, u32[]{:S(2)}) %collective-permute-start.40) | collective-permute-done | bytes 204832 | tf_op jit(solution)/shard_map/ppermute | solution.py:415
  78.8 3.3 %collective-permute-start.47 = (bf16[16,3200]{1,0:T(8,128)(2,1)S(1)}, bf16[16,3200]{1,0:T(8,128)(2,1)S(1)}, u32[]{:S(2)}, u32[]{:S(2)}) collective-permute-start(bf16[16,3200]{1,0:T(8,128)(2,1)S(1)} %shard_map.112), channel_id=1, source_target_pairs={{0,14},{1,15},{4,10},{5,11},{8,6},{9,7},{12,2},{13,3},{14,0},{15,1... | collective-permute-start | bytes 307208 | tf_op jit(solution)/shard_map/ppermute | solution.py:424
  83.7 3.5 %collective-permute-done.47.refs_8_ = bf16[16,3200]{1,0:T(8,128)(2,1)S(1)} collective-permute-done((bf16[16,3200]{1,0:T(8,128)(2,1)S(1)}, bf16[16,3200]{1,0:T(8,128)(2,1)S(1)}, u32[]{:S(2)}, u32[]{:S(2)}) %collective-permute-start.47) | collective-permute-done | bytes 102432 | tf_op jit(solution)/shard_map/ppermute | solution.py:424
  87.3 0.9 collective-permute-done.46.refs_0_
  88.3 0.9 collective-permute-start.48
  89.6 3.4 %collective-permute-done.48 = bf16[16,3200]{1,0:T(8,128)(2,1)S(1)} collective-permute-done((bf16[16,3200]{1,0:T(8,128)(2,1)S(1)}, bf16[16,3200]{1,0:T(8,128)(2,1)S(1)}, u32[]{:S(2)}, u32[]{:S(2)}) %collective-permute-start.48) | collective-permute-done | bytes 102432 | tf_op jit(solution)/shard_map/ppermute | solution.py:424
  93.0 1.1 %collective-permute-done.44.refs_6_ = bf16[16,3200]{1,0:T(8,128)(2,1)S(1)} collective-permute-done((bf16[16,3200]{1,0:T(8,128)(2,1)S(1)}, bf16[16,3200]{1,0:T(8,128)(2,1)S(1)}, u32[]{:S(2)}, u32[]{:S(2)}) %collective-permute-start.44) | collective-permute-done | bytes 102432 | tf_op jit(solution)/shard_map/ppermute | solution.py:424
  94.3 0.9 shard_map.114
  (100 shorter events, 24.2 us)
Async XLA Ops:
  1.1 5.7 %collective-permute-start.3 = (bf16[3,32,512]{2,1,0:T(8,128)(2,1)}, bf16[3,32,512]{2,1,0:T(8,128)(2,1)S(1)}, u32[]{:S(2)}, u32[]{:S(2)}) collective-permute-start(bf16[3,32,512]{2,1,0:T(8,128)(2,1)} %in_ref.1), channel_id=1, source_target_pairs={{0,4},{1,3},{4,8},{5,1},{8,12},{9,5},{12,14},{13,9},{14,10},{15,13... | collective-permute-start | bytes 294920 | tf_op jit(solution)/shard_map/ppermute | solution.py:424
  4.4 4.7 %collective-permute-start.1 = (bf16[3,32,512]{2,1,0:T(8,128)(2,1)S(1)}, bf16[3,32,512]{2,1,0:T(8,128)(2,1)S(1)}, u32[]{:S(2)}, u32[]{:S(2)}) collective-permute-start(bf16[3,32,512]{2,1,0:T(8,128)(2,1)S(1)} %collective-permute-done.refs_1_), channel_id=1, source_target_pairs={{0,4},{1,3},{4,8},{5,1},{8,12},{9,5},{12,14},{13,9},{14,10},{15,13... | collective-permute-start | bytes 294920 | tf_op jit(solution)/shard_map/ppermute | solution.py:424
  6.8 8.8 %collective-permute-start.6 = (bf16[3,32,512]{2,1,0:T(8,128)(2,1)S(1)}, bf16[3,32,512]{2,1,0:T(8,128)(2,1)S(1)}, u32[]{:S(2)}, u32[]{:S(2)}) collective-permute-start(bf16[3,32,512]{2,1,0:T(8,128)(2,1)S(1)} %collective-permute-done.3.refs_2_), channel_id=1, source_target_pairs={{0,4},{1,3},{4,8},{5,1},{8,12},{9,5},{12,14},{13,9},{14,10},{15,13... | collective-permute-start | bytes 294920 | tf_op jit(solution)/shard_map/ppermute | solution.py:424
  9.1 6.5 %collective-permute-start.2 = (bf16[3,32,512]{2,1,0:T(8,128)(2,1)S(1)}, bf16[3,32,512]{2,1,0:T(8,128)(2,1)S(1)}, u32[]{:S(2)}, u32[]{:S(2)}) collective-permute-start(bf16[3,32,512]{2,1,0:T(8,128)(2,1)S(1)} %collective-permute-done.1.refs_3_), channel_id=1, source_target_pairs={{0,4},{1,3},{4,8},{5,1},{8,12},{9,5},{12,14},{13,9},{14,10},{15,13... | collective-permute-start | bytes 294920 | tf_op jit(solution)/shard_map/ppermute | solution.py:424
  12.5 7.5 %collective-permute-start.13 = (bf16[3,32,512]{2,1,0:T(8,128)(2,1)S(1)}, bf16[3,32,512]{2,1,0:T(8,128)(2,1)S(1)}, u32[]{:S(2)}, u32[]{:S(2)}) collective-permute-start(bf16[3,32,512]{2,1,0:T(8,128)(2,1)S(1)} %copy-done.4), channel_id=1, source_target_pairs={{0,14},{1,15},{4,10},{5,11},{8,6},{9,7},{12,2},{13,3},{14,0},{15,1... | collective-permute-start | bytes 294920 | tf_op jit(solution)/shard_map/ppermute | solution.py:424
  15.1 4.9 %collective-permute-start.4 = (bf16[3,32,512]{2,1,0:T(8,128)(2,1)S(1)}, bf16[3,32,512]{2,1,0:T(8,128)(2,1)S(1)}, u32[]{:S(2)}, u32[]{:S(2)}) collective-permute-start(bf16[3,32,512]{2,1,0:T(8,128)(2,1)S(1)} %collective-permute-done.3.refs_2_), channel_id=1, source_target_pairs={{0,1},{1,0},{2,3},{3,2},{4,5},{5,4},{6,7},{7,6},{8,9},{9,8},{10,11... | collective-permute-start | bytes 294920 | tf_op jit(solution)/shard_map/ppermute | solution.py:415
  15.1 5.4 %collective-permute-start.5 = (bf16[3,32,512]{2,1,0:T(8,128)(2,1)S(1)}, bf16[3,32,512]{2,1,0:T(8,128)(2,1)S(1)}, u32[]{:S(2)}, u32[]{:S(2)}) collective-permute-start(bf16[3,32,512]{2,1,0:T(8,128)(2,1)S(1)} %collective-permute-done.1.refs_3_), channel_id=1, source_target_pairs={{0,1},{1,0},{2,3},{3,2},{4,5},{5,4},{6,7},{7,6},{8,9},{9,8},{10,11... | collective-permute-start | bytes 294920 | tf_op jit(solution)/shard_map/ppermute | solution.py:415
  15.6 5.4 %collective-permute-start.9 = (bf16[3,32,512]{2,1,0:T(8,128)(2,1)S(1)}, bf16[3,32,512]{2,1,0:T(8,128)(2,1)S(1)}, u32[]{:S(2)}, u32[]{:S(2)}) collective-permute-start(bf16[3,32,512]{2,1,0:T(8,128)(2,1)S(1)} %collective-permute-done.6.refs_6_), channel_id=1, source_target_pairs={{0,4},{1,3},{4,8},{5,1},{8,12},{9,5},{12,14},{13,9},{14,10},{15,13... | collective-permute-start | bytes 294920 | tf_op jit(solution)/shard_map/ppermute | solution.py:424
  15.6 6.4 %collective-permute-start.10 = (bf16[3,32,512]{2,1,0:T(8,128)(2,1)S(1)}, bf16[3,32,512]{2,1,0:T(8,128)(2,1)S(1)}, u32[]{:S(2)}, u32[]{:S(2)}) collective-permute-start(bf16[3,32,512]{2,1,0:T(8,128)(2,1)S(1)} %collective-permute-done.2._.refs_7_), channel_id=1, source_target_pairs={{0,4},{1,3},{4,8},{5,1},{8,12},{9,5},{12,14},{13,9},{14,10},{15,13... | collective-permute-start | bytes 294920 | tf_op jit(solution)/shard_map/ppermute | solution.py:424
  32.9 4.7 %collective-permute-start.20 = (bf16[16,3200]{1,0:T(8,128)(2,1)S(1)}, bf16[16,3200]{1,0:T(8,128)(2,1)S(1)}, u32[]{:S(2)}, u32[]{:S(2)}) collective-permute-start(bf16[16,3200]{1,0:T(8,128)(2,1)S(1)} %shard_map.101), channel_id=1, source_target_pairs={{0,4},{1,3},{4,8},{5,1},{8,12},{9,5},{12,14},{13,9},{14,10},{15,13... | collective-permute-start | bytes 307208 | tf_op jit(solution)/shard_map/ppermute | solution.py:424
  33.6 5.1 %collective-permute-start.17 = (bf16[16,3200]{1,0:T(8,128)(2,1)S(1)}, bf16[16,3200]{1,0:T(8,128)(2,1)S(1)}, u32[]{:S(2)}, u32[]{:S(2)}) collective-permute-start(bf16[16,3200]{1,0:T(8,128)(2,1)S(1)} %shard_map.98), channel_id=1, source_target_pairs={{0,4},{1,3},{4,8},{5,1},{8,12},{9,5},{12,14},{13,9},{14,10},{15,13... | collective-permute-start | bytes 307208 | tf_op jit(solution)/shard_map/ppermute | solution.py:424
  34.8 7.9 %collective-permute-start.22 = (bf16[16,3200]{1,0:T(8,128)(2,1)S(1)}, bf16[16,3200]{1,0:T(8,128)(2,1)S(1)}, u32[]{:S(2)}, u32[]{:S(2)}) collective-permute-start(bf16[16,3200]{1,0:T(8,128)(2,1)S(1)} %shard_map.103), channel_id=1, source_target_pairs={{0,14},{1,15},{4,10},{5,11},{8,6},{9,7},{12,2},{13,3},{14,0},{15,1... | collective-permute-start | bytes 307208 | tf_op jit(solution)/shard_map/ppermute | solution.py:424
  37.7 6.0 %collective-permute-start.21 = (bf16[16,3200]{1,0:T(8,128)(2,1)S(1)}, bf16[16,3200]{1,0:T(8,128)(2,1)S(1)}, u32[]{:S(2)}, u32[]{:S(2)}) collective-permute-start(bf16[16,3200]{1,0:T(8,128)(2,1)S(1)} %shard_map.102), channel_id=1, source_target_pairs={{0,4},{1,3},{4,8},{5,1},{8,12},{9,5},{12,14},{13,9},{14,10},{15,13... | collective-permute-start | bytes 307208 | tf_op jit(solution)/shard_map/ppermute | solution.py:424
  38.8 6.0 %collective-permute-start.18 = (bf16[16,3200]{1,0:T(8,128)(2,1)S(1)}, bf16[16,3200]{1,0:T(8,128)(2,1)S(1)}, u32[]{:S(2)}, u32[]{:S(2)}) collective-permute-start(bf16[16,3200]{1,0:T(8,128)(2,1)S(1)} %shard_map.99), channel_id=1, source_target_pairs={{0,4},{1,3},{4,8},{5,1},{8,12},{9,5},{12,14},{13,9},{14,10},{15,13... | collective-permute-start | bytes 307208 | tf_op jit(solution)/shard_map/ppermute | solution.py:424
  43.8 4.7 %collective-permute-start.23 = (bf16[16,3200]{1,0:T(8,128)(2,1)S(1)}, bf16[16,3200]{1,0:T(8,128)(2,1)S(1)}, u32[]{:S(2)}, u32[]{:S(2)}) collective-permute-start(bf16[16,3200]{1,0:T(8,128)(2,1)S(1)} %shard_map.104), channel_id=1, source_target_pairs={{0,4},{1,3},{4,8},{5,1},{8,12},{9,5},{12,14},{13,9},{14,10},{15,13... | collective-permute-start | bytes 307208 | tf_op jit(solution)/shard_map/ppermute | solution.py:424
  44.8 4.7 %collective-permute-start.19 = (bf16[16,3200]{1,0:T(8,128)(2,1)S(1)}, bf16[16,3200]{1,0:T(8,128)(2,1)S(1)}, u32[]{:S(2)}, u32[]{:S(2)}) collective-permute-start(bf16[16,3200]{1,0:T(8,128)(2,1)S(1)} %shard_map.100), channel_id=1, source_target_pairs={{0,4},{1,3},{4,8},{5,1},{8,12},{9,5},{12,14},{13,9},{14,10},{15,13... | collective-permute-start | bytes 307208 | tf_op jit(solution)/shard_map/ppermute | solution.py:424
  50.8 4.7 %collective-permute-start.26 = (bf16[16,3200]{1,0:T(8,128)(2,1)S(1)}, bf16[16,3200]{1,0:T(8,128)(2,1)S(1)}, u32[]{:S(2)}, u32[]{:S(2)}) collective-permute-start(bf16[16,3200]{1,0:T(8,128)(2,1)S(1)} %get-tuple-element.67.refs_0_), channel_id=1, source_target_pairs={{0,4},{1,3},{4,8},{5,1},{8,12},{9,5},{12,14},{13,9},{14,10},{15,13... | collective-permute-start | bytes 307208 | tf_op jit(solution)/shard_map/ppermute | solution.py:424
  55.5 4.8 %collective-permute-start.30 = (bf16[16,3200]{1,0:T(8,128)(2,1)S(1)}, bf16[16,3200]{1,0:T(8,128)(2,1)S(1)}, u32[]{:S(2)}, u32[]{:S(2)}) collective-permute-start(bf16[16,3200]{1,0:T(8,128)(2,1)S(1)} %collective-permute-done.26.refs_2_), channel_id=1, source_target_pairs={{0,4},{1,3},{4,8},{5,1},{8,12},{9,5},{12,14},{13,9},{14,10},{15,13... | collective-permute-start | bytes 307208 | tf_op jit(solution)/shard_map/ppermute | solution.py:424
  56.6 4.7 %collective-permute-start.31 = (bf16[16,3200]{1,0:T(8,128)(2,1)S(1)}, bf16[16,3200]{1,0:T(8,128)(2,1)S(1)}, u32[]{:S(2)}, u32[]{:S(2)}) collective-permute-start(bf16[16,3200]{1,0:T(8,128)(2,1)S(1)} %collective-permute-done.27.refs_3_), channel_id=1, source_target_pairs={{0,4},{1,3},{4,8},{5,1},{8,12},{9,5},{12,14},{13,9},{14,10},{15,13... | collective-permute-start | bytes 307208 | tf_op jit(solution)/shard_map/ppermute | solution.py:424
  57.4 4.8 %collective-permute-start.28 = (bf16[16,3200]{1,0:T(8,128)(2,1)S(1)}, bf16[16,3200]{1,0:T(8,128)(2,1)S(1)}, u32[]{:S(2)}, u32[]{:S(2)}) collective-permute-start(bf16[16,3200]{1,0:T(8,128)(2,1)S(1)} %collective-permute-done.26.refs_2_), channel_id=1, source_target_pairs={{0,1},{1,0},{2,3},{3,2},{4,5},{5,4},{6,7},{7,6},{8,9},{9,8},{10,11... | collective-permute-start | bytes 307208 | tf_op jit(solution)/shard_map/ppermute | solution.py:415
  57.4 8.3 %collective-permute-start.38 = (bf16[16,3200]{1,0:T(8,128)(2,1)S(1)}, bf16[16,3200]{1,0:T(8,128)(2,1)S(1)}, u32[]{:S(2)}, u32[]{:S(2)}) collective-permute-start(bf16[16,3200]{1,0:T(8,128)(2,1)S(1)} %get-tuple-element.67.refs_0_), channel_id=1, source_target_pairs={{0,14},{1,15},{4,10},{5,11},{8,6},{9,7},{12,2},{13,3},{14,0},{15,1... | collective-permute-start | bytes 307208 | tf_op jit(solution)/shard_map/ppermute | solution.py:424
  60.2 6.4 %collective-permute-start.34 = (bf16[16,3200]{1,0:T(8,128)(2,1)S(1)}, bf16[16,3200]{1,0:T(8,128)(2,1)S(1)}, u32[]{:S(2)}, u32[]{:S(2)}) collective-permute-start(bf16[16,3200]{1,0:T(8,128)(2,1)S(1)} %collective-permute-done.30.refs_6_), channel_id=1, source_target_pairs={{0,4},{1,3},{4,8},{5,1},{8,12},{9,5},{12,14},{13,9},{14,10},{15,13... | collective-permute-start | bytes 307208 | tf_op jit(solution)/shard_map/ppermute | solution.py:424
  60.9 5.8 %collective-permute-start.32 = (bf16[16,3200]{1,0:T(8,128)(2,1)S(1)}, bf16[16,3200]{1,0:T(8,128)(2,1)S(1)}, u32[]{:S(2)}, u32[]{:S(2)}) collective-permute-start(bf16[16,3200]{1,0:T(8,128)(2,1)S(1)} %collective-permute-done.30.refs_6_), channel_id=1, source_target_pairs={{0,1},{1,0},{2,3},{3,2},{4,5},{5,4},{6,7},{7,6},{8,9},{9,8},{10,11... | collective-permute-start | bytes 307208 | tf_op jit(solution)/shard_map/ppermute | solution.py:415
  61.3 6.4 %collective-permute-start.35 = (bf16[16,3200]{1,0:T(8,128)(2,1)S(1)}, bf16[16,3200]{1,0:T(8,128)(2,1)S(1)}, u32[]{:S(2)}, u32[]{:S(2)}) collective-permute-start(bf16[16,3200]{1,0:T(8,128)(2,1)S(1)} %collective-permute-done.31.refs_7_), channel_id=1, source_target_pairs={{0,4},{1,3},{4,8},{5,1},{8,12},{9,5},{12,14},{13,9},{14,10},{15,13... | collective-permute-start | bytes 307208 | tf_op jit(solution)/shard_map/ppermute | solution.py:424
  62.2 5.5 %collective-permute-start.29 = (bf16[16,3200]{1,0:T(8,128)(2,1)S(1)}, bf16[16,3200]{1,0:T(8,128)(2,1)S(1)}, u32[]{:S(2)}, u32[]{:S(2)}) collective-permute-start(bf16[16,3200]{1,0:T(8,128)(2,1)S(1)} %collective-permute-done.27.refs_3_), channel_id=1, source_target_pairs={{0,1},{1,0},{2,3},{3,2},{4,5},{5,4},{6,7},{7,6},{8,9},{9,8},{10,11... | collective-permute-start | bytes 307208 | tf_op jit(solution)/shard_map/ppermute | solution.py:415
  76.9 5.2 %collective-permute-start.45 = (bf16[16,3200]{1,0:T(8,128)(2,1)S(1)}, bf16[16,3200]{1,0:T(8,128)(2,1)S(1)}, u32[]{:S(2)}, u32[]{:S(2)}) collective-permute-start(bf16[16,3200]{1,0:T(8,128)(2,1)S(1)} %shard_map.110), channel_id=1, source_target_pairs={{0,4},{1,3},{4,8},{5,1},{8,12},{9,5},{12,14},{13,9},{14,10},{15,13... | collective-permute-start | bytes 307208 | tf_op jit(solution)/shard_map/ppermute | solution.py:424
  77.7 5.0 %collective-permute-start.42 = (bf16[16,3200]{1,0:T(8,128)(2,1)S(1)}, bf16[16,3200]{1,0:T(8,128)(2,1)S(1)}, u32[]{:S(2)}, u32[]{:S(2)}) collective-permute-start(bf16[16,3200]{1,0:T(8,128)(2,1)S(1)} %shard_map.107), channel_id=1, source_target_pairs={{0,4},{1,3},{4,8},{5,1},{8,12},{9,5},{12,14},{13,9},{14,10},{15,13... | collective-permute-start | bytes 307208 | tf_op jit(solution)/shard_map/ppermute | solution.py:424
  78.8 8.5 %collective-permute-start.47 = (bf16[16,3200]{1,0:T(8,128)(2,1)S(1)}, bf16[16,3200]{1,0:T(8,128)(2,1)S(1)}, u32[]{:S(2)}, u32[]{:S(2)}) collective-permute-start(bf16[16,3200]{1,0:T(8,128)(2,1)S(1)} %shard_map.112), channel_id=1, source_target_pairs={{0,14},{1,15},{4,10},{5,11},{8,6},{9,7},{12,2},{13,3},{14,0},{15,1... | collective-permute-start | bytes 307208 | tf_op jit(solution)/shard_map/ppermute | solution.py:424
  82.2 6.0 %collective-permute-start.46 = (bf16[16,3200]{1,0:T(8,128)(2,1)S(1)}, bf16[16,3200]{1,0:T(8,128)(2,1)S(1)}, u32[]{:S(2)}, u32[]{:S(2)}) collective-permute-start(bf16[16,3200]{1,0:T(8,128)(2,1)S(1)} %shard_map.111), channel_id=1, source_target_pairs={{0,4},{1,3},{4,8},{5,1},{8,12},{9,5},{12,14},{13,9},{14,10},{15,13... | collective-permute-start | bytes 307208 | tf_op jit(solution)/shard_map/ppermute | solution.py:424
  82.8 6.5 %collective-permute-start.43 = (bf16[16,3200]{1,0:T(8,128)(2,1)S(1)}, bf16[16,3200]{1,0:T(8,128)(2,1)S(1)}, u32[]{:S(2)}, u32[]{:S(2)}) collective-permute-start(bf16[16,3200]{1,0:T(8,128)(2,1)S(1)} %shard_map.108), channel_id=1, source_target_pairs={{0,4},{1,3},{4,8},{5,1},{8,12},{9,5},{12,14},{13,9},{14,10},{15,13... | collective-permute-start | bytes 307208 | tf_op jit(solution)/shard_map/ppermute | solution.py:424
  88.3 4.7 %collective-permute-start.48 = (bf16[16,3200]{1,0:T(8,128)(2,1)S(1)}, bf16[16,3200]{1,0:T(8,128)(2,1)S(1)}, u32[]{:S(2)}, u32[]{:S(2)}) collective-permute-start(bf16[16,3200]{1,0:T(8,128)(2,1)S(1)} %shard_map.113), channel_id=1, source_target_pairs={{0,4},{1,3},{4,8},{5,1},{8,12},{9,5},{12,14},{13,9},{14,10},{15,13... | collective-permute-start | bytes 307208 | tf_op jit(solution)/shard_map/ppermute | solution.py:424
  89.4 4.7 %collective-permute-start.44 = (bf16[16,3200]{1,0:T(8,128)(2,1)S(1)}, bf16[16,3200]{1,0:T(8,128)(2,1)S(1)}, u32[]{:S(2)}, u32[]{:S(2)}) collective-permute-start(bf16[16,3200]{1,0:T(8,128)(2,1)S(1)} %shard_map.109), channel_id=1, source_target_pairs={{0,4},{1,3},{4,8},{5,1},{8,12},{9,5},{12,14},{13,9},{14,10},{15,13... | collective-permute-start | bytes 307208 | tf_op jit(solution)/shard_map/ppermute | solution.py:424
  (23 other events, 96.6 us)

commit v20 on v17

--- a/solution.py
+++ b/solution.py
@@ -94,19 +94,19 @@
     return (HALF, rows // HALF * sectors * width + LANES)
 
 
-def copy_kernel(in_ref, out_ref):
+def copy_kernel(in_ref, _, out_ref):
     out_ref[...] = in_ref[...]
 
 
-def copied(value):
+def copied(value, after):
     return pl.pallas_call(
         copy_kernel,
-        in_specs=[VMEM],
+        in_specs=[VMEM, HBM],
         out_specs=VMEM,
         out_shape=jax.ShapeDtypeStruct(value.shape, value.dtype),
         compiler_params=PARAMS,
         cost_estimate=pl.CostEstimate(flops=8 << 30, bytes_accessed=1 << 20, transcendentals=0),
-    )(value)
+    )(value, after)
 
 
 def square_kernel(wave_ref, diag_ref, square_ref):
@@ -319,7 +319,7 @@
 
 
 def step_kernel(entries, scale_ref, wave_ref, diag_ref, *refs):
-    *sums, first_ref, terms_ref, correction_ref, message_ref = refs
+    *sums, terms_ref, correction_ref, message_ref = refs
     shape = wave_ref.shape
     ritz = own_scalar(*sums) / entries
     inverse = 1.0 / scale_ref[0:1, 0:1]
@@ -330,7 +330,6 @@
         terms = own_terms(shape, s, *sums)
         first = terms + diag * start
         correction = (first - ritz * start) / jnp.maximum(jnp.abs(diag - ritz), 1.0)
-        first_ref[s] = first
         terms_ref[s] = terms
         correction_ref[s] = correction
         dots += fold(start * correction)
@@ -345,14 +344,14 @@
     return pl.pallas_call(
         functools.partial(step_kernel, entries),
         in_specs=[VMEM] * 3 + [SMEM] + [VMEM] * (len(sums) - 1),
-        out_specs=[VMEM] * 4,
-        out_shape=[full, full, full, jax.ShapeDtypeStruct(message_shape(*wave.shape), jnp.bfloat16)],
+        out_specs=[VMEM] * 3,
+        out_shape=[full, full, jax.ShapeDtypeStruct(message_shape(*wave.shape), jnp.bfloat16)],
         compiler_params=PARAMS,
     )(scale, wave, diag, *sums)
 
 
 def finish_kernel(entries, along_ref, scale_ref, wave_ref, diag_ref, *refs):
-    terms_ref, correction_ref, *sums, vector_ref, image_ref = refs
+    terms_ref, correction_ref, *sums, first_ref, vector_ref, image_ref = refs
     shape = wave_ref.shape
     along = along_ref[0:1, 0:1]
     norm = jnp.sqrt(jnp.full((1, 1), own_scalar(*sums) / entries, jnp.float32))
@@ -360,10 +359,12 @@
     start_scale = 1.0 / scale_ref[0:1, 0:1]
     for s in range(shape[0]):
         start = wave_ref[s].astype(jnp.float32) * start_scale
+        diag = diag_ref[s].astype(jnp.float32)
+        first_ref[s] = terms_ref[s] + diag * start
         second = (correction_ref[s] - along * start) * inverse
         vector_ref[s] = second
         image = (own_terms(shape, s, *sums) - along * terms_ref[s]) * inverse
-        image_ref[s] = image + diag_ref[s].astype(jnp.float32) * second
+        image_ref[s] = image + diag * second
 
 
 def finish(along, scale, wave, diag, terms, correction, sums, entries):
@@ -371,8 +372,8 @@
     return pl.pallas_call(
         functools.partial(finish_kernel, entries),
         in_specs=[VMEM] * 6 + [SMEM] + [VMEM] * (len(sums) - 1),
-        out_specs=[VMEM] * 2,
-        out_shape=[full, full],
+        out_specs=[VMEM] * 3,
+        out_shape=[full] * 3,
         compiler_params=PARAMS,
     )(along, scale, wave, diag, terms, correction, *sums)
 
@@ -394,23 +395,19 @@
     return hop(value, 4, 4)
 
 
-def gather(own, beside=()):
+def gather(own, beside=None):
     one, two = own, flip(own)
     across, two = lax.optimization_barrier((own, two))
     pieces = [one, two]
     across = opposite(across)
-    results = []
+    result = None
     for k in range(ROUNDS):
         one, two = hop(one), hop(two)
-        if k < len(beside):
-            results.append(beside[k](*results))
-        if k < ROUNDS - 1:
-            ready = results[-1:] if beside else []
-            two, ready = lax.optimization_barrier((two, ready))
-            if ready:
-                results[-1] = ready[0]
         pieces += [one, two, flip(one), flip(two)]
-    return pieces + [across, flip(across)], results
+        if k == 1 and beside is not None:
+            result = beside(two)
+            across, result = lax.optimization_barrier((across, result))
+    return pieces + [across, flip(across)], result
 
 
 def scatter(shape, me, total, near, far, dot):
@@ -435,22 +432,22 @@
     sectors, rows, width = shape
     entries = float(sectors * rows * lax.axis_size("term") * width)
     me = lax.axis_index("term").astype(jnp.int32).reshape(1)
-    beside = (
-        lambda: jnp.concatenate([block_source, block_target, live_count]),
-        lambda _: copied(wavefunction),
-        lambda _, own: weighted_square(own, diagonal),
-    )
-    (_, *fields), (ints, own, square) = gather(wavefunction, beside)
-    fields = [own, *fields]
+    def beside(after):
+        ints = jnp.concatenate([block_source, block_target, live_count])
+        return ints, copied(wavefunction, after)
+
+    (_, *fields), (ints, wave) = gather(wavefunction, beside)
+    fields = [wave, *fields]
+    square = weighted_square(wave, diagonal)
     blocks = (left_blocks, right_blocks, shape)
     total, near, far, dot, scale = apply_blocks(me, ints, fields, (square,), *blocks, True, entries)
-    first_image, terms, correction, message = davidson_step(
+    terms, correction, message = davidson_step(
         scale, wavefunction, diagonal, scatter(shape, me, total, near, far, dot), entries
     )
     fields, _ = gather(message)
     own = (scale, wavefunction, correction)
     total, near, far, dot, along = apply_blocks(me, ints, fields, own, *blocks, False, entries)
-    second_vector, second_image = finish(
+    first_image, second_vector, second_image = finish(
         along, scale, wavefunction, diagonal, terms, correction,
         scatter(shape, me, total, near, far, dot), entries,
     )

time: 96.6 us -> 96.1 us (level)
  the two profiles are of different devices: /device:TPU:0 before, /device:TPU:18 now
where the time goes in v20:
time: 96.1 us; the launch traced here: 95.3 us
  waiting for transfers between devices  53.4 us (56%)
  starting transfers between devices  27.2 us (28%)
  Pallas kernels  11.5 us (12%)
  between operations  1.56 us (2%)
    ppermute x28, waiting for transfers between devices, hop(): return lax.ppermute(value, 'term', pairs)  47.3 us
    ppermute x28, starting transfers between devices, hop(): return lax.ppermute(value, 'term', pairs)  21.6 us
    pallas_call x2, Pallas kernels, apply_blocks(): pl.pallas_call(functools.partial(blocks_kernel, first, shape, entries), i...  9.55 us
    ppermute x22, waiting for transfers between devices, flip(): return lax.ppermute(value, 'term', [(i, i ^ 1) for i in range(16)])  6.12 us
    ppermute x22, starting transfers between devices, flip(): return lax.ppermute(value, 'term', [(i, i ^ 1) for i in range(16)])  5.6 us
  transfers between devices with their start and end apart: 50, of which 33 were waited for; matrix products, arithmetic and copies ran while one was open for 1% of the time, Pallas kernels for 1%

profile of v20, /device:TPU:18, one launch (start us, length us, event | category | flops | bytes accessed | tf_op | source)
XLA Modules:
  0.0 95.3 jit_solution(13505619693597189098)
XLA Ops:
  0.7 1.6 %collective-permute-start.4 = (bf16[3,32,512]{2,1,0:T(8,128)(2,1)}, bf16[3,32,512]{2,1,0:T(8,128)(2,1)S(1)}, u32[]{:S(2)}, u32[]{:S(2)}) collective-permute-start(bf16[3,32,512]{2,1,0:T(8,128)(2,1)} %wave_ref.3), channel_id=1, source_target_pairs={{0,4},{1,3},{4,8},{5,1},{8,12},{9,5},{12,14},{13,9},{14,10},{15,13... | collective-permute-start | bytes 294920 | tf_op jit(solution)/shard_map/ppermute | solution.py:391
  2.3 1.5 %collective-permute-start.2 = (bf16[3,32,512]{2,1,0:T(8,128)(2,1)S(1)}, bf16[3,32,512]{2,1,0:T(8,128)(2,1)S(1)}, u32[]{:S(2)}, u32[]{:S(2)}) collective-permute-start(bf16[3,32,512]{2,1,0:T(8,128)(2,1)S(1)} %collective-permute-done.refs_1_), channel_id=1, source_target_pairs={{0,4},{1,3},{4,8},{5,1},{8,12},{9,5},{12,14},{13,9},{14,10},{15,13... | collective-permute-start | bytes 294920 | tf_op jit(solution)/shard_map/ppermute | solution.py:391
  5.6 1.6 %collective-permute-start.7 = (bf16[3,32,512]{2,1,0:T(8,128)(2,1)S(1)}, bf16[3,32,512]{2,1,0:T(8,128)(2,1)S(1)}, u32[]{:S(2)}, u32[]{:S(2)}) collective-permute-start(bf16[3,32,512]{2,1,0:T(8,128)(2,1)S(1)} %collective-permute-done.4.refs_2_), channel_id=1, source_target_pairs={{0,4},{1,3},{4,8},{5,1},{8,12},{9,5},{12,14},{13,9},{14,10},{15,13... | collective-permute-start | bytes 294920 | tf_op jit(solution)/shard_map/ppermute | solution.py:391
  7.2 1.5 %collective-permute-start.3 = (bf16[3,32,512]{2,1,0:T(8,128)(2,1)S(1)}, bf16[3,32,512]{2,1,0:T(8,128)(2,1)S(1)}, u32[]{:S(2)}, u32[]{:S(2)}) collective-permute-start(bf16[3,32,512]{2,1,0:T(8,128)(2,1)S(1)} %collective-permute-done.2.refs_3_), channel_id=1, source_target_pairs={{0,4},{1,3},{4,8},{5,1},{8,12},{9,5},{12,14},{13,9},{14,10},{15,13... | collective-permute-start | bytes 294920 | tf_op jit(solution)/shard_map/ppermute | solution.py:391
  10.2 1.6 %collective-permute-start.10 = (bf16[3,32,512]{2,1,0:T(8,128)(2,1)S(1)}, bf16[3,32,512]{2,1,0:T(8,128)(2,1)S(1)}, u32[]{:S(2)}, u32[]{:S(2)}) collective-permute-start(bf16[3,32,512]{2,1,0:T(8,128)(2,1)S(1)} %collective-permute-done.7.refs_6_), channel_id=1, source_target_pairs={{0,4},{1,3},{4,8},{5,1},{8,12},{9,5},{12,14},{13,9},{14,10},{15,13... | collective-permute-start | bytes 294920 | tf_op jit(solution)/shard_map/ppermute | solution.py:391
  11.8 1.5 %collective-permute-start.11 = (bf16[3,32,512]{2,1,0:T(8,128)(2,1)S(1)}, bf16[3,32,512]{2,1,0:T(8,128)(2,1)S(1)}, u32[]{:S(2)}, u32[]{:S(2)}) collective-permute-start(bf16[3,32,512]{2,1,0:T(8,128)(2,1)S(1)} %collective-permute-done.3._.refs_7_), channel_id=1, source_target_pairs={{0,4},{1,3},{4,8},{5,1},{8,12},{9,5},{12,14},{13,9},{14,10},{15,13... | collective-permute-start | bytes 294920 | tf_op jit(solution)/shard_map/ppermute | solution.py:391
  14.2 2.6 %collective-permute-done.1.refs_14_ = bf16[3,32,512]{2,1,0:T(8,128)(2,1)S(1)} collective-permute-done((bf16[3,32,512]{2,1,0:T(8,128)(2,1)}, bf16[3,32,512]{2,1,0:T(8,128)(2,1)S(1)}, u32[]{:S(2)}, u32[]{:S(2)}) %collective-permute-start.1) | collective-permute-done | bytes 98336 | tf_op jit(solution)/shard_map/ppermute | solution.py:391
  19.7 5.9 %shard_map.96 = (f32[3,512,512]{2,1,0:T(8,128)S(1)}, bf16[2,16,3200]{2,1,0:T(8,128)(2,1)S(1)}, bf16[6,16,3200]{2,1,0:T(8,128)(2,1)S(1)}, f32[8,128]{1,0:T(8,128)S(1)}, f32[8,128]{1,0:T(8,128)S(1)}) custom-call(s32[1]{0:T(128)} %bitcast.me_ref.refs_0_.refs_2_, s32[17]{0:T(128)S(1)} %pad_add_fusion.ints_ref, ...), custom_call_target="tpu_custom_call" | custom-call | flops 4294967296 | bytes 8388608 | tf_op jit(solution)/shard_map/pallas_call | solution.py:251
  25.6 1.5 %collective-permute-start.15 = (bf16[2,16,3200]{2,1,0:T(8,128)(2,1)S(1)}, bf16[2,16,3200]{2,1,0:T(8,128)(2,1)S(1)}, u32[]{:S(2)}, u32[]{:S(2)}) collective-permute-start(bf16[2,16,3200]{2,1,0:T(8,128)(2,1)S(1)} %get-tuple-element.38), channel_id=1, source_target_pairs={{0,1},{1,0},{2,3},{3,2},{4,5},{5,4},{6,7},{7,6},{8,9},{9,8},{10,11... | collective-permute-start | bytes 614408 | tf_op jit(solution)/shard_map/ppermute | solution.py:382
  28.6 3.2 %collective-permute-start.20 = (bf16[16,3200]{1,0:T(8,128)(2,1)S(1)}, bf16[16,3200]{1,0:T(8,128)(2,1)S(1)}, u32[]{:S(2)}, u32[]{:S(2)}) collective-permute-start(bf16[16,3200]{1,0:T(8,128)(2,1)S(1)} %shard_map.100), channel_id=1, source_target_pairs={{0,4},{1,3},{4,8},{5,1},{8,12},{9,5},{12,14},{13,9},{14,10},{15,13... | collective-permute-start | bytes 307208 | tf_op jit(solution)/shard_map/ppermute | solution.py:391
  31.9 1.4 %collective-permute-start.22 = (bf16[16,3200]{1,0:T(8,128)(2,1)S(1)}, bf16[16,3200]{1,0:T(8,128)(2,1)S(1)}, u32[]{:S(2)}, u32[]{:S(2)}) collective-permute-start(bf16[16,3200]{1,0:T(8,128)(2,1)S(1)} %shard_map.102), channel_id=1, source_target_pairs={{0,14},{1,15},{4,10},{5,11},{8,6},{9,7},{12,2},{13,3},{14,0},{15,1... | collective-permute-start | bytes 307208 | tf_op jit(solution)/shard_map/ppermute | solution.py:391
  34.0 2.5 %collective-permute-start.21 = (bf16[16,3200]{1,0:T(8,128)(2,1)S(1)}, bf16[16,3200]{1,0:T(8,128)(2,1)S(1)}, u32[]{:S(2)}, u32[]{:S(2)}) collective-permute-start(bf16[16,3200]{1,0:T(8,128)(2,1)S(1)} %shard_map.101), channel_id=1, source_target_pairs={{0,4},{1,3},{4,8},{5,1},{8,12},{9,5},{12,14},{13,9},{14,10},{15,13... | collective-permute-start | bytes 307208 | tf_op jit(solution)/shard_map/ppermute | solution.py:391
  36.5 3.0 %collective-permute-done.17.refs_0_ = bf16[16,3200]{1,0:T(8,128)(2,1)S(1)} collective-permute-done((bf16[16,3200]{1,0:T(8,128)(2,1)S(1)}, bf16[16,3200]{1,0:T(8,128)(2,1)S(1)}, u32[]{:S(2)}, u32[]{:S(2)}) %collective-permute-start.17) | collective-permute-done | bytes 102432 | tf_op jit(solution)/shard_map/ppermute | solution.py:391
  42.2 2.0 %collective-permute-done.18.refs_0_ = bf16[16,3200]{1,0:T(8,128)(2,1)S(1)} collective-permute-done((bf16[16,3200]{1,0:T(8,128)(2,1)S(1)}, bf16[16,3200]{1,0:T(8,128)(2,1)S(1)}, u32[]{:S(2)}, u32[]{:S(2)}) %collective-permute-start.18) | collective-permute-done | bytes 102432 | tf_op jit(solution)/shard_map/ppermute | solution.py:391
  44.4 2.4 %collective-permute-done.23 = bf16[16,3200]{1,0:T(8,128)(2,1)S(1)} collective-permute-done((bf16[16,3200]{1,0:T(8,128)(2,1)S(1)}, bf16[16,3200]{1,0:T(8,128)(2,1)S(1)}, u32[]{:S(2)}, u32[]{:S(2)}) %collective-permute-start.23) | collective-permute-done | bytes 102432 | tf_op jit(solution)/shard_map/ppermute | solution.py:391
  46.8 2.3 %collective-permute-done.19.refs_4_ = bf16[16,3200]{1,0:T(8,128)(2,1)S(1)} collective-permute-done((bf16[16,3200]{1,0:T(8,128)(2,1)S(1)}, bf16[16,3200]{1,0:T(8,128)(2,1)S(1)}, u32[]{:S(2)}, u32[]{:S(2)}) %collective-permute-start.19) | collective-permute-done | bytes 102432 | tf_op jit(solution)/shard_map/ppermute | solution.py:391
  50.6 3.4 %collective-permute-done.26.refs_2_ = bf16[16,3200]{1,0:T(8,128)(2,1)S(1)} collective-permute-done((bf16[16,3200]{1,0:T(8,128)(2,1)S(1)}, bf16[16,3200]{1,0:T(8,128)(2,1)S(1)}, u32[]{:S(2)}, u32[]{:S(2)}) %collective-permute-start.26) | collective-permute-done | bytes 102432 | tf_op jit(solution)/shard_map/ppermute | solution.py:391
  55.3 3.4 %collective-permute-done.30.refs_6_ = bf16[16,3200]{1,0:T(8,128)(2,1)S(1)} collective-permute-done((bf16[16,3200]{1,0:T(8,128)(2,1)S(1)}, bf16[16,3200]{1,0:T(8,128)(2,1)S(1)}, u32[]{:S(2)}, u32[]{:S(2)}) %collective-permute-start.30) | collective-permute-done | bytes 102432 | tf_op jit(solution)/shard_map/ppermute | solution.py:391
  58.7 4.4 %collective-permute-done.31.refs_7_ = bf16[16,3200]{1,0:T(8,128)(2,1)S(1)} collective-permute-done((bf16[16,3200]{1,0:T(8,128)(2,1)S(1)}, bf16[16,3200]{1,0:T(8,128)(2,1)S(1)}, u32[]{:S(2)}, u32[]{:S(2)}) %collective-permute-start.31) | collective-permute-done | bytes 102432 | tf_op jit(solution)/shard_map/ppermute | solution.py:391
  65.8 2.0 %collective-permute-done.35.refs_11_ = bf16[16,3200]{1,0:T(8,128)(2,1)S(1)} collective-permute-done((bf16[16,3200]{1,0:T(8,128)(2,1)S(1)}, bf16[16,3200]{1,0:T(8,128)(2,1)S(1)}, u32[]{:S(2)}, u32[]{:S(2)}) %collective-permute-start.35) | collective-permute-done | bytes 102432 | tf_op jit(solution)/shard_map/ppermute | solution.py:391
  67.8 1.3 %collective-permute-done.37.refs_13_ = bf16[16,3200]{1,0:T(8,128)(2,1)S(1)} collective-permute-done((bf16[16,3200]{1,0:T(8,128)(2,1)S(1)}, bf16[16,3200]{1,0:T(8,128)(2,1)S(1)}, u32[]{:S(2)}, u32[]{:S(2)}) %collective-permute-start.37) | collective-permute-done | bytes 102432 | tf_op jit(solution)/shard_map/ppermute | solution.py:382
  69.1 3.7 %shard_map.105 = (f32[3,512,512]{2,1,0:T(8,128)S(1)}, bf16[2,16,3200]{2,1,0:T(8,128)(2,1)S(1)}, bf16[6,16,3200]{2,1,0:T(8,128)(2,1)S(1)}, f32[8,128]{1,0:T(8,128)S(1)}, f32[8,128]{1,0:T(8,128)S(1)}) custom-call(s32[1]{0:T(128)} %bitcast.me_ref.refs_0_.refs_2_, s32[17]{0:T(128)S(1)} %pad_add_fusion.ints_ref, bf16[16,3200]{1,0:T(8,128)(2,1)S(1)} %get-tuple-element.47.refs_0_, ...), custom_call_target="tpu_custom_call" | custom-call | flops 4294967296 | bytes 8388608 | tf_op jit(solution)/shard_map/pallas_call | solution.py:251
  72.7 1.5 %collective-permute-start.40 = (bf16[2,16,3200]{2,1,0:T(8,128)(2,1)S(1)}, bf16[2,16,3200]{2,1,0:T(8,128)(2,1)S(1)}, u32[]{:S(2)}, u32[]{:S(2)}) collective-permute-start(bf16[2,16,3200]{2,1,0:T(8,128)(2,1)S(1)} %get-tuple-element.52), channel_id=1, source_target_pairs={{0,1},{1,0},{2,3},{3,2},{4,5},{5,4},{6,7},{7,6},{8,9},{9,8},{10,11... | collective-permute-start | bytes 614408 | tf_op jit(solution)/shard_map/ppermute | solution.py:382
  75.7 1.3 %collective-permute-start.45 = (bf16[16,3200]{1,0:T(8,128)(2,1)S(1)}, bf16[16,3200]{1,0:T(8,128)(2,1)S(1)}, u32[]{:S(2)}, u32[]{:S(2)}) collective-permute-start(bf16[16,3200]{1,0:T(8,128)(2,1)S(1)} %shard_map.109), channel_id=1, source_target_pairs={{0,4},{1,3},{4,8},{5,1},{8,12},{9,5},{12,14},{13,9},{14,10},{15,13... | collective-permute-start | bytes 307208 | tf_op jit(solution)/shard_map/ppermute | solution.py:391
  77.4 1.7 %collective-permute-start.47 = (bf16[16,3200]{1,0:T(8,128)(2,1)S(1)}, bf16[16,3200]{1,0:T(8,128)(2,1)S(1)}, u32[]{:S(2)}, u32[]{:S(2)}) collective-permute-start(bf16[16,3200]{1,0:T(8,128)(2,1)S(1)} %shard_map.111), channel_id=1, source_target_pairs={{0,14},{1,15},{4,10},{5,11},{8,6},{9,7},{12,2},{13,3},{14,0},{15,1... | collective-permute-start | bytes 307208 | tf_op jit(solution)/shard_map/ppermute | solution.py:391
  79.1 1.4 %collective-permute-done.45.refs_0_ = bf16[16,3200]{1,0:T(8,128)(2,1)S(1)} collective-permute-done((bf16[16,3200]{1,0:T(8,128)(2,1)S(1)}, bf16[16,3200]{1,0:T(8,128)(2,1)S(1)}, u32[]{:S(2)}, u32[]{:S(2)}) %collective-permute-start.45) | collective-permute-done | bytes 102432 | tf_op jit(solution)/shard_map/ppermute | solution.py:391
  80.5 1.3 %collective-permute-start.46 = (bf16[16,3200]{1,0:T(8,128)(2,1)S(1)}, bf16[16,3200]{1,0:T(8,128)(2,1)S(1)}, u32[]{:S(2)}, u32[]{:S(2)}) collective-permute-start(bf16[16,3200]{1,0:T(8,128)(2,1)S(1)} %shard_map.110), channel_id=1, source_target_pairs={{0,4},{1,3},{4,8},{5,1},{8,12},{9,5},{12,14},{13,9},{14,10},{15,13... | collective-permute-start | bytes 307208 | tf_op jit(solution)/shard_map/ppermute | solution.py:391
  81.8 3.0 %collective-permute-done.42.refs_0_ = bf16[16,3200]{1,0:T(8,128)(2,1)S(1)} collective-permute-done((bf16[16,3200]{1,0:T(8,128)(2,1)S(1)}, bf16[16,3200]{1,0:T(8,128)(2,1)S(1)}, u32[]{:S(2)}, u32[]{:S(2)}) %collective-permute-start.42) | collective-permute-done | bytes 102432 | tf_op jit(solution)/shard_map/ppermute | solution.py:391
  84.9 1.4 %collective-permute-done.47.refs_8_ = bf16[16,3200]{1,0:T(8,128)(2,1)S(1)} collective-permute-done((bf16[16,3200]{1,0:T(8,128)(2,1)S(1)}, bf16[16,3200]{1,0:T(8,128)(2,1)S(1)}, u32[]{:S(2)}, u32[]{:S(2)}) %collective-permute-start.47) | collective-permute-done | bytes 102432 | tf_op jit(solution)/shard_map/ppermute | solution.py:391
  87.5 2.0 %collective-permute-done.43.refs_0_ = bf16[16,3200]{1,0:T(8,128)(2,1)S(1)} collective-permute-done((bf16[16,3200]{1,0:T(8,128)(2,1)S(1)}, bf16[16,3200]{1,0:T(8,128)(2,1)S(1)}, u32[]{:S(2)}, u32[]{:S(2)}) %collective-permute-start.43) | collective-permute-done | bytes 102432 | tf_op jit(solution)/shard_map/ppermute | solution.py:391
  89.7 2.4 %collective-permute-done.48 = bf16[16,3200]{1,0:T(8,128)(2,1)S(1)} collective-permute-done((bf16[16,3200]{1,0:T(8,128)(2,1)S(1)}, bf16[16,3200]{1,0:T(8,128)(2,1)S(1)}, u32[]{:S(2)}, u32[]{:S(2)}) %collective-permute-start.48) | collective-permute-done | bytes 102432 | tf_op jit(solution)/shard_map/ppermute | solution.py:391
  92.1 2.3 %collective-permute-done.44.refs_6_ = bf16[16,3200]{1,0:T(8,128)(2,1)S(1)} collective-permute-done((bf16[16,3200]{1,0:T(8,128)(2,1)S(1)}, bf16[16,3200]{1,0:T(8,128)(2,1)S(1)}, u32[]{:S(2)}, u32[]{:S(2)}) %collective-permute-start.44) | collective-permute-done | bytes 102432 | tf_op jit(solution)/shard_map/ppermute | solution.py:391
  (99 shorter events, 21.5 us)
Async XLA Ops:
  0.7 4.9 %collective-permute-start.4 = (bf16[3,32,512]{2,1,0:T(8,128)(2,1)}, bf16[3,32,512]{2,1,0:T(8,128)(2,1)S(1)}, u32[]{:S(2)}, u32[]{:S(2)}) collective-permute-start(bf16[3,32,512]{2,1,0:T(8,128)(2,1)} %wave_ref.3), channel_id=1, source_target_pairs={{0,4},{1,3},{4,8},{5,1},{8,12},{9,5},{12,14},{13,9},{14,10},{15,13... | collective-permute-start | bytes 294920 | tf_op jit(solution)/shard_map/ppermute | solution.py:391
  2.3 4.8 %collective-permute-start.2 = (bf16[3,32,512]{2,1,0:T(8,128)(2,1)S(1)}, bf16[3,32,512]{2,1,0:T(8,128)(2,1)S(1)}, u32[]{:S(2)}, u32[]{:S(2)}) collective-permute-start(bf16[3,32,512]{2,1,0:T(8,128)(2,1)S(1)} %collective-permute-done.refs_1_), channel_id=1, source_target_pairs={{0,4},{1,3},{4,8},{5,1},{8,12},{9,5},{12,14},{13,9},{14,10},{15,13... | collective-permute-start | bytes 294920 | tf_op jit(solution)/shard_map/ppermute | solution.py:391
  7.2 4.6 %collective-permute-start.3 = (bf16[3,32,512]{2,1,0:T(8,128)(2,1)S(1)}, bf16[3,32,512]{2,1,0:T(8,128)(2,1)S(1)}, u32[]{:S(2)}, u32[]{:S(2)}) collective-permute-start(bf16[3,32,512]{2,1,0:T(8,128)(2,1)S(1)} %collective-permute-done.2.refs_3_), channel_id=1, source_target_pairs={{0,4},{1,3},{4,8},{5,1},{8,12},{9,5},{12,14},{13,9},{14,10},{15,13... | collective-permute-start | bytes 294920 | tf_op jit(solution)/shard_map/ppermute | solution.py:391
  9.4 7.4 %collective-permute-start.1 = (bf16[3,32,512]{2,1,0:T(8,128)(2,1)}, bf16[3,32,512]{2,1,0:T(8,128)(2,1)S(1)}, u32[]{:S(2)}, u32[]{:S(2)}) collective-permute-start(bf16[3,32,512]{2,1,0:T(8,128)(2,1)} %wave_ref.3), channel_id=1, source_target_pairs={{0,14},{1,15},{4,10},{5,11},{8,6},{9,7},{12,2},{13,3},{14,0},{15,1... | collective-permute-start | bytes 294920 | tf_op jit(solution)/shard_map/ppermute | solution.py:391
  9.5 7.4 %collective-permute-start.5 = (bf16[3,32,512]{2,1,0:T(8,128)(2,1)S(1)}, bf16[3,32,512]{2,1,0:T(8,128)(2,1)S(1)}, u32[]{:S(2)}, u32[]{:S(2)}) collective-permute-start(bf16[3,32,512]{2,1,0:T(8,128)(2,1)S(1)} %collective-permute-done.4.refs_2_), channel_id=1, source_target_pairs={{0,1},{1,0},{2,3},{3,2},{4,5},{5,4},{6,7},{7,6},{8,9},{9,8},{10,11... | collective-permute-start | bytes 294920 | tf_op jit(solution)/shard_map/ppermute | solution.py:382
  10.2 7.2 %collective-permute-start.10 = (bf16[3,32,512]{2,1,0:T(8,128)(2,1)S(1)}, bf16[3,32,512]{2,1,0:T(8,128)(2,1)S(1)}, u32[]{:S(2)}, u32[]{:S(2)}) collective-permute-start(bf16[3,32,512]{2,1,0:T(8,128)(2,1)S(1)} %collective-permute-done.7.refs_6_), channel_id=1, source_target_pairs={{0,4},{1,3},{4,8},{5,1},{8,12},{9,5},{12,14},{13,9},{14,10},{15,13... | collective-permute-start | bytes 294920 | tf_op jit(solution)/shard_map/ppermute | solution.py:391
  11.8 5.7 %collective-permute-start.8 = (bf16[3,32,512]{2,1,0:T(8,128)(2,1)S(1)}, bf16[3,32,512]{2,1,0:T(8,128)(2,1)S(1)}, u32[]{:S(2)}, u32[]{:S(2)}) collective-permute-start(bf16[3,32,512]{2,1,0:T(8,128)(2,1)S(1)} %collective-permute-done.7.refs_6_), channel_id=1, source_target_pairs={{0,1},{1,0},{2,3},{3,2},{4,5},{5,4},{6,7},{7,6},{8,9},{9,8},{10,11... | collective-permute-start | bytes 294920 | tf_op jit(solution)/shard_map/ppermute | solution.py:382
  11.8 6.6 %collective-permute-start.11 = (bf16[3,32,512]{2,1,0:T(8,128)(2,1)S(1)}, bf16[3,32,512]{2,1,0:T(8,128)(2,1)S(1)}, u32[]{:S(2)}, u32[]{:S(2)}) collective-permute-start(bf16[3,32,512]{2,1,0:T(8,128)(2,1)S(1)} %collective-permute-done.3._.refs_7_), channel_id=1, source_target_pairs={{0,4},{1,3},{4,8},{5,1},{8,12},{9,5},{12,14},{13,9},{14,10},{15,13... | collective-permute-start | bytes 294920 | tf_op jit(solution)/shard_map/ppermute | solution.py:391
  28.6 5.4 %collective-permute-start.20 = (bf16[16,3200]{1,0:T(8,128)(2,1)S(1)}, bf16[16,3200]{1,0:T(8,128)(2,1)S(1)}, u32[]{:S(2)}, u32[]{:S(2)}) collective-permute-start(bf16[16,3200]{1,0:T(8,128)(2,1)S(1)} %shard_map.100), channel_id=1, source_target_pairs={{0,4},{1,3},{4,8},{5,1},{8,12},{9,5},{12,14},{13,9},{14,10},{15,13... | collective-permute-start | bytes 307208 | tf_op jit(solution)/shard_map/ppermute | solution.py:391
  31.8 7.7 %collective-permute-start.17 = (bf16[16,3200]{1,0:T(8,128)(2,1)S(1)}, bf16[16,3200]{1,0:T(8,128)(2,1)S(1)}, u32[]{:S(2)}, u32[]{:S(2)}) collective-permute-start(bf16[16,3200]{1,0:T(8,128)(2,1)S(1)} %shard_map.97), channel_id=1, source_target_pairs={{0,4},{1,3},{4,8},{5,1},{8,12},{9,5},{12,14},{13,9},{14,10},{15,13... | collective-permute-start | bytes 307208 | tf_op jit(solution)/shard_map/ppermute | solution.py:391
  31.9 8.9 %collective-permute-start.22 = (bf16[16,3200]{1,0:T(8,128)(2,1)S(1)}, bf16[16,3200]{1,0:T(8,128)(2,1)S(1)}, u32[]{:S(2)}, u32[]{:S(2)}) collective-permute-start(bf16[16,3200]{1,0:T(8,128)(2,1)S(1)} %shard_map.102), channel_id=1, source_target_pairs={{0,14},{1,15},{4,10},{5,11},{8,6},{9,7},{12,2},{13,3},{14,0},{15,1... | collective-permute-start | bytes 307208 | tf_op jit(solution)/shard_map/ppermute | solution.py:391
  34.0 7.9 %collective-permute-start.21 = (bf16[16,3200]{1,0:T(8,128)(2,1)S(1)}, bf16[16,3200]{1,0:T(8,128)(2,1)S(1)}, u32[]{:S(2)}, u32[]{:S(2)}) collective-permute-start(bf16[16,3200]{1,0:T(8,128)(2,1)S(1)} %shard_map.101), channel_id=1, source_target_pairs={{0,4},{1,3},{4,8},{5,1},{8,12},{9,5},{12,14},{13,9},{14,10},{15,13... | collective-permute-start | bytes 307208 | tf_op jit(solution)/shard_map/ppermute | solution.py:391
  39.5 4.7 %collective-permute-start.18 = (bf16[16,3200]{1,0:T(8,128)(2,1)S(1)}, bf16[16,3200]{1,0:T(8,128)(2,1)S(1)}, u32[]{:S(2)}, u32[]{:S(2)}) collective-permute-start(bf16[16,3200]{1,0:T(8,128)(2,1)S(1)} %shard_map.98), channel_id=1, source_target_pairs={{0,4},{1,3},{4,8},{5,1},{8,12},{9,5},{12,14},{13,9},{14,10},{15,13... | collective-permute-start | bytes 307208 | tf_op jit(solution)/shard_map/ppermute | solution.py:391
  42.0 4.7 %collective-permute-start.23 = (bf16[16,3200]{1,0:T(8,128)(2,1)S(1)}, bf16[16,3200]{1,0:T(8,128)(2,1)S(1)}, u32[]{:S(2)}, u32[]{:S(2)}) collective-permute-start(bf16[16,3200]{1,0:T(8,128)(2,1)S(1)} %shard_map.103), channel_id=1, source_target_pairs={{0,4},{1,3},{4,8},{5,1},{8,12},{9,5},{12,14},{13,9},{14,10},{15,13... | collective-permute-start | bytes 307208 | tf_op jit(solution)/shard_map/ppermute | solution.py:391
  44.3 4.7 %collective-permute-start.19 = (bf16[16,3200]{1,0:T(8,128)(2,1)S(1)}, bf16[16,3200]{1,0:T(8,128)(2,1)S(1)}, u32[]{:S(2)}, u32[]{:S(2)}) collective-permute-start(bf16[16,3200]{1,0:T(8,128)(2,1)S(1)} %shard_map.99), channel_id=1, source_target_pairs={{0,4},{1,3},{4,8},{5,1},{8,12},{9,5},{12,14},{13,9},{14,10},{15,13... | collective-permute-start | bytes 307208 | tf_op jit(solution)/shard_map/ppermute | solution.py:391
  49.3 4.7 %collective-permute-start.26 = (bf16[16,3200]{1,0:T(8,128)(2,1)S(1)}, bf16[16,3200]{1,0:T(8,128)(2,1)S(1)}, u32[]{:S(2)}, u32[]{:S(2)}) collective-permute-start(bf16[16,3200]{1,0:T(8,128)(2,1)S(1)} %get-tuple-element.47.refs_0_), channel_id=1, source_target_pairs={{0,4},{1,3},{4,8},{5,1},{8,12},{9,5},{12,14},{13,9},{14,10},{15,13... | collective-permute-start | bytes 307208 | tf_op jit(solution)/shard_map/ppermute | solution.py:391
  50.6 4.7 %collective-permute-start.27 = (bf16[16,3200]{1,0:T(8,128)(2,1)S(1)}, bf16[16,3200]{1,0:T(8,128)(2,1)S(1)}, u32[]{:S(2)}, u32[]{:S(2)}) collective-permute-start(bf16[16,3200]{1,0:T(8,128)(2,1)S(1)} %collective-permute-done.25.refs_1_), channel_id=1, source_target_pairs={{0,4},{1,3},{4,8},{5,1},{8,12},{9,5},{12,14},{13,9},{14,10},{15,13... | collective-permute-start | bytes 307208 | tf_op jit(solution)/shard_map/ppermute | solution.py:391
  54.1 4.7 %collective-permute-start.30 = (bf16[16,3200]{1,0:T(8,128)(2,1)S(1)}, bf16[16,3200]{1,0:T(8,128)(2,1)S(1)}, u32[]{:S(2)}, u32[]{:S(2)}) collective-permute-start(bf16[16,3200]{1,0:T(8,128)(2,1)S(1)} %collective-permute-done.26.refs_2_), channel_id=1, source_target_pairs={{0,4},{1,3},{4,8},{5,1},{8,12},{9,5},{12,14},{13,9},{14,10},{15,13... | collective-permute-start | bytes 307208 | tf_op jit(solution)/shard_map/ppermute | solution.py:391
  55.3 7.8 %collective-permute-start.31 = (bf16[16,3200]{1,0:T(8,128)(2,1)S(1)}, bf16[16,3200]{1,0:T(8,128)(2,1)S(1)}, u32[]{:S(2)}, u32[]{:S(2)}) collective-permute-start(bf16[16,3200]{1,0:T(8,128)(2,1)S(1)} %collective-permute-done.27.refs_3_), channel_id=1, source_target_pairs={{0,4},{1,3},{4,8},{5,1},{8,12},{9,5},{12,14},{13,9},{14,10},{15,13... | collective-permute-start | bytes 307208 | tf_op jit(solution)/shard_map/ppermute | solution.py:391
  55.3 7.8 %collective-permute-start.28 = (bf16[16,3200]{1,0:T(8,128)(2,1)S(1)}, bf16[16,3200]{1,0:T(8,128)(2,1)S(1)}, u32[]{:S(2)}, u32[]{:S(2)}) collective-permute-start(bf16[16,3200]{1,0:T(8,128)(2,1)S(1)} %collective-permute-done.26.refs_2_), channel_id=1, source_target_pairs={{0,1},{1,0},{2,3},{3,2},{4,5},{5,4},{6,7},{7,6},{8,9},{9,8},{10,11... | collective-permute-start | bytes 307208 | tf_op jit(solution)/shard_map/ppermute | solution.py:382
  55.3 8.8 %collective-permute-start.38 = (bf16[16,3200]{1,0:T(8,128)(2,1)S(1)}, bf16[16,3200]{1,0:T(8,128)(2,1)S(1)}, u32[]{:S(2)}, u32[]{:S(2)}) collective-permute-start(bf16[16,3200]{1,0:T(8,128)(2,1)S(1)} %get-tuple-element.47.refs_0_), channel_id=1, source_target_pairs={{0,14},{1,15},{4,10},{5,11},{8,6},{9,7},{12,2},{13,3},{14,0},{15,1... | collective-permute-start | bytes 307208 | tf_op jit(solution)/shard_map/ppermute | solution.py:391
  58.7 6.6 %collective-permute-start.34 = (bf16[16,3200]{1,0:T(8,128)(2,1)S(1)}, bf16[16,3200]{1,0:T(8,128)(2,1)S(1)}, u32[]{:S(2)}, u32[]{:S(2)}) collective-permute-start(bf16[16,3200]{1,0:T(8,128)(2,1)S(1)} %collective-permute-done.30.refs_6_), channel_id=1, source_target_pairs={{0,4},{1,3},{4,8},{5,1},{8,12},{9,5},{12,14},{13,9},{14,10},{15,13... | collective-permute-start | bytes 307208 | tf_op jit(solution)/shard_map/ppermute | solution.py:391
  58.7 6.6 %collective-permute-start.32 = (bf16[16,3200]{1,0:T(8,128)(2,1)S(1)}, bf16[16,3200]{1,0:T(8,128)(2,1)S(1)}, u32[]{:S(2)}, u32[]{:S(2)}) collective-permute-start(bf16[16,3200]{1,0:T(8,128)(2,1)S(1)} %collective-permute-done.30.refs_6_), channel_id=1, source_target_pairs={{0,1},{1,0},{2,3},{3,2},{4,5},{5,4},{6,7},{7,6},{8,9},{9,8},{10,11... | collective-permute-start | bytes 307208 | tf_op jit(solution)/shard_map/ppermute | solution.py:382
  63.1 4.7 %collective-permute-start.35 = (bf16[16,3200]{1,0:T(8,128)(2,1)S(1)}, bf16[16,3200]{1,0:T(8,128)(2,1)S(1)}, u32[]{:S(2)}, u32[]{:S(2)}) collective-permute-start(bf16[16,3200]{1,0:T(8,128)(2,1)S(1)} %collective-permute-done.31.refs_7_), channel_id=1, source_target_pairs={{0,4},{1,3},{4,8},{5,1},{8,12},{9,5},{12,14},{13,9},{14,10},{15,13... | collective-permute-start | bytes 307208 | tf_op jit(solution)/shard_map/ppermute | solution.py:391
  63.1 4.7 %collective-permute-start.29 = (bf16[16,3200]{1,0:T(8,128)(2,1)S(1)}, bf16[16,3200]{1,0:T(8,128)(2,1)S(1)}, u32[]{:S(2)}, u32[]{:S(2)}) collective-permute-start(bf16[16,3200]{1,0:T(8,128)(2,1)S(1)} %collective-permute-done.27.refs_3_), channel_id=1, source_target_pairs={{0,1},{1,0},{2,3},{3,2},{4,5},{5,4},{6,7},{7,6},{8,9},{9,8},{10,11... | collective-permute-start | bytes 307208 | tf_op jit(solution)/shard_map/ppermute | solution.py:382
  75.7 4.7 %collective-permute-start.45 = (bf16[16,3200]{1,0:T(8,128)(2,1)S(1)}, bf16[16,3200]{1,0:T(8,128)(2,1)S(1)}, u32[]{:S(2)}, u32[]{:S(2)}) collective-permute-start(bf16[16,3200]{1,0:T(8,128)(2,1)S(1)} %shard_map.109), channel_id=1, source_target_pairs={{0,4},{1,3},{4,8},{5,1},{8,12},{9,5},{12,14},{13,9},{14,10},{15,13... | collective-permute-start | bytes 307208 | tf_op jit(solution)/shard_map/ppermute | solution.py:391
  77.1 7.7 %collective-permute-start.42 = (bf16[16,3200]{1,0:T(8,128)(2,1)S(1)}, bf16[16,3200]{1,0:T(8,128)(2,1)S(1)}, u32[]{:S(2)}, u32[]{:S(2)}) collective-permute-start(bf16[16,3200]{1,0:T(8,128)(2,1)S(1)} %shard_map.106), channel_id=1, source_target_pairs={{0,4},{1,3},{4,8},{5,1},{8,12},{9,5},{12,14},{13,9},{14,10},{15,13... | collective-permute-start | bytes 307208 | tf_op jit(solution)/shard_map/ppermute | solution.py:391
  77.4 8.9 %collective-permute-start.47 = (bf16[16,3200]{1,0:T(8,128)(2,1)S(1)}, bf16[16,3200]{1,0:T(8,128)(2,1)S(1)}, u32[]{:S(2)}, u32[]{:S(2)}) collective-permute-start(bf16[16,3200]{1,0:T(8,128)(2,1)S(1)} %shard_map.111), channel_id=1, source_target_pairs={{0,14},{1,15},{4,10},{5,11},{8,6},{9,7},{12,2},{13,3},{14,0},{15,1... | collective-permute-start | bytes 307208 | tf_op jit(solution)/shard_map/ppermute | solution.py:391
  80.5 6.8 %collective-permute-start.46 = (bf16[16,3200]{1,0:T(8,128)(2,1)S(1)}, bf16[16,3200]{1,0:T(8,128)(2,1)S(1)}, u32[]{:S(2)}, u32[]{:S(2)}) collective-permute-start(bf16[16,3200]{1,0:T(8,128)(2,1)S(1)} %shard_map.110), channel_id=1, source_target_pairs={{0,4},{1,3},{4,8},{5,1},{8,12},{9,5},{12,14},{13,9},{14,10},{15,13... | collective-permute-start | bytes 307208 | tf_op jit(solution)/shard_map/ppermute | solution.py:391
  84.8 4.7 %collective-permute-start.43 = (bf16[16,3200]{1,0:T(8,128)(2,1)S(1)}, bf16[16,3200]{1,0:T(8,128)(2,1)S(1)}, u32[]{:S(2)}, u32[]{:S(2)}) collective-permute-start(bf16[16,3200]{1,0:T(8,128)(2,1)S(1)} %shard_map.107), channel_id=1, source_target_pairs={{0,4},{1,3},{4,8},{5,1},{8,12},{9,5},{12,14},{13,9},{14,10},{15,13... | collective-permute-start | bytes 307208 | tf_op jit(solution)/shard_map/ppermute | solution.py:391
  87.4 4.7 %collective-permute-start.48 = (bf16[16,3200]{1,0:T(8,128)(2,1)S(1)}, bf16[16,3200]{1,0:T(8,128)(2,1)S(1)}, u32[]{:S(2)}, u32[]{:S(2)}) collective-permute-start(bf16[16,3200]{1,0:T(8,128)(2,1)S(1)} %shard_map.112), channel_id=1, source_target_pairs={{0,4},{1,3},{4,8},{5,1},{8,12},{9,5},{12,14},{13,9},{14,10},{15,13... | collective-permute-start | bytes 307208 | tf_op jit(solution)/shard_map/ppermute | solution.py:391
  89.6 4.7 %collective-permute-start.44 = (bf16[16,3200]{1,0:T(8,128)(2,1)S(1)}, bf16[16,3200]{1,0:T(8,128)(2,1)S(1)}, u32[]{:S(2)}, u32[]{:S(2)}) collective-permute-start(bf16[16,3200]{1,0:T(8,128)(2,1)S(1)} %shard_map.108), channel_id=1, source_target_pairs={{0,4},{1,3},{4,8},{5,1},{8,12},{9,5},{12,14},{13,9},{14,10},{15,13... | collective-permute-start | bytes 307208 | tf_op jit(solution)/shard_map/ppermute | solution.py:391
  (23 other events, 113.9 us)

commit v21 on v20

--- a/solution.py
+++ b/solution.py
@@ -146,9 +146,9 @@
                 pltpu.make_async_copy(right_in.at[slot], right.at[slot], right_sem.at[slot]),
             )
 
-        for slot in range(GROUP):
-            for copy in copies(slot):
-                copy.start()
+        for slot in range(slots):
+            for priority, copy in enumerate(copies(slot)):
+                copy.start(priority=priority)
     else:
         left, right = left_in, right_in
 
@@ -171,9 +171,6 @@
         for k, part, _, _ in pieces:
             value = field_refs[k][part].astype(jnp.float32)
             dot += fold(value * value)
-        for slot in range(GROUP, slots):
-            for copy in copies(slot):
-                copy.start()
         scale = jnp.sqrt(jnp.sum(dot) / entries)
         inverse = 1.0 / scale
         out_ref[...] = jnp.full(out_ref.shape, scale, jnp.float32)
@@ -185,8 +182,10 @@
 
     used = ints_ref[2 * slots]
 
+    group = GROUP if first else 2 * GROUP
+
     def add_some(step, carry):
-        some = [step * GROUP + k for k in range(GROUP)]
+        some = [step * group + k for k in range(group)]
         if first:
             for slot in some:
                 for copy in copies(slot):
@@ -212,7 +211,7 @@
 
         return carry
 
-    lax.fori_loop(0, slots // GROUP, add_some, 0)
+    lax.fori_loop(0, slots // group, add_some, 0)
 
     dot = jnp.zeros((8, 128), jnp.float32)
     if first:

time: 96.1 us -> 97.5 us (1.015)
  the two profiles are of different devices: /device:TPU:18 before, /device:TPU:0 now
where the time goes in v21:
time: 97.5 us; the launch traced here: 97.3 us
  starting transfers between devices  66.3 us (68%)
  waiting for transfers between devices  16.8 us (17%)
  Pallas kernels  11 us (11%)
  between operations  1.49 us (2%)
    ppermute x28, starting transfers between devices, hop(): return lax.ppermute(value, 'term', pairs)  60.1 us
    ppermute x28, waiting for transfers between devices, hop(): return lax.ppermute(value, 'term', pairs)  11.9 us
    pallas_call x2, Pallas kernels, apply_blocks(): pl.pallas_call(functools.partial(blocks_kernel, first, shape, entries), i...  9.04 us
    ppermute x22, starting transfers between devices, flip(): return lax.ppermute(value, 'term', [(i, i ^ 1) for i in range(16)])  6.19 us
    ppermute x22, waiting for transfers between devices, flip(): return lax.ppermute(value, 'term', [(i, i ^ 1) for i in range(16)])  4.96 us
  transfers between devices with their start and end apart: 50, of which 22 were waited for; matrix products, arithmetic and copies ran while one was open for 1% of the time, Pallas kernels for 1%

profile of v21, /device:TPU:0, one launch (start us, length us, event | category | flops | bytes accessed | tf_op | source)
XLA Modules:
  0.0 97.3 jit_solution(2890501695962784978)
XLA Ops:
  1.1 2.6 %collective-permute-start.4 = (bf16[3,32,512]{2,1,0:T(8,128)(2,1)}, bf16[3,32,512]{2,1,0:T(8,128)(2,1)S(1)}, u32[]{:S(2)}, u32[]{:S(2)}) collective-permute-start(bf16[3,32,512]{2,1,0:T(8,128)(2,1)} %wave_ref.3), channel_id=1, source_target_pairs={{0,4},{1,3},{4,8},{5,1},{8,12},{9,5},{12,14},{13,9},{14,10},{15,13... | collective-permute-start | bytes 294920 | tf_op jit(solution)/shard_map/ppermute | solution.py:390
  3.8 1.6 %collective-permute-start.2 = (bf16[3,32,512]{2,1,0:T(8,128)(2,1)S(1)}, bf16[3,32,512]{2,1,0:T(8,128)(2,1)S(1)}, u32[]{:S(2)}, u32[]{:S(2)}) collective-permute-start(bf16[3,32,512]{2,1,0:T(8,128)(2,1)S(1)} %collective-permute-done.refs_1_), channel_id=1, source_target_pairs={{0,4},{1,3},{4,8},{5,1},{8,12},{9,5},{12,14},{13,9},{14,10},{15,13... | collective-permute-start | bytes 294920 | tf_op jit(solution)/shard_map/ppermute | solution.py:390
  6.5 2.1 %collective-permute-start.7 = (bf16[3,32,512]{2,1,0:T(8,128)(2,1)S(1)}, bf16[3,32,512]{2,1,0:T(8,128)(2,1)S(1)}, u32[]{:S(2)}, u32[]{:S(2)}) collective-permute-start(bf16[3,32,512]{2,1,0:T(8,128)(2,1)S(1)} %collective-permute-done.4.refs_2_), channel_id=1, source_target_pairs={{0,4},{1,3},{4,8},{5,1},{8,12},{9,5},{12,14},{13,9},{14,10},{15,13... | collective-permute-start | bytes 294920 | tf_op jit(solution)/shard_map/ppermute | solution.py:390
  8.6 1.6 %collective-permute-start.3 = (bf16[3,32,512]{2,1,0:T(8,128)(2,1)S(1)}, bf16[3,32,512]{2,1,0:T(8,128)(2,1)S(1)}, u32[]{:S(2)}, u32[]{:S(2)}) collective-permute-start(bf16[3,32,512]{2,1,0:T(8,128)(2,1)S(1)} %collective-permute-done.2.refs_3_), channel_id=1, source_target_pairs={{0,4},{1,3},{4,8},{5,1},{8,12},{9,5},{12,14},{13,9},{14,10},{15,13... | collective-permute-start | bytes 294920 | tf_op jit(solution)/shard_map/ppermute | solution.py:390
  10.9 3.1 %collective-permute-start.1 = (bf16[3,32,512]{2,1,0:T(8,128)(2,1)}, bf16[3,32,512]{2,1,0:T(8,128)(2,1)S(1)}, u32[]{:S(2)}, u32[]{:S(2)}) collective-permute-start(bf16[3,32,512]{2,1,0:T(8,128)(2,1)} %wave_ref.3), channel_id=1, source_target_pairs={{0,14},{1,15},{4,10},{5,11},{8,6},{9,7},{12,2},{13,3},{14,0},{15,1... | collective-permute-start | bytes 294920 | tf_op jit(solution)/shard_map/ppermute | solution.py:390
  14.1 1.8 %collective-permute-start.8 = (bf16[3,32,512]{2,1,0:T(8,128)(2,1)S(1)}, bf16[3,32,512]{2,1,0:T(8,128)(2,1)S(1)}, u32[]{:S(2)}, u32[]{:S(2)}) collective-permute-start(bf16[3,32,512]{2,1,0:T(8,128)(2,1)S(1)} %collective-permute-done.7.refs_6_), channel_id=1, source_target_pairs={{0,1},{1,0},{2,3},{3,2},{4,5},{5,4},{6,7},{7,6},{8,9},{9,8},{10,11... | collective-permute-start | bytes 294920 | tf_op jit(solution)/shard_map/ppermute | solution.py:381
  17.2 1.5 %collective-permute-done.1.refs_14_ = bf16[3,32,512]{2,1,0:T(8,128)(2,1)S(1)} collective-permute-done((bf16[3,32,512]{2,1,0:T(8,128)(2,1)}, bf16[3,32,512]{2,1,0:T(8,128)(2,1)S(1)}, u32[]{:S(2)}, u32[]{:S(2)}) %collective-permute-start.1) | collective-permute-done | bytes 98336 | tf_op jit(solution)/shard_map/ppermute | solution.py:390
  22.0 5.6 %shard_map.96 = (f32[3,512,512]{2,1,0:T(8,128)S(1)}, bf16[2,16,3200]{2,1,0:T(8,128)(2,1)S(1)}, bf16[6,16,3200]{2,1,0:T(8,128)(2,1)S(1)}, f32[8,128]{1,0:T(8,128)S(1)}, f32[8,128]{1,0:T(8,128)S(1)}) custom-call(s32[1]{0:T(128)} %bitcast.me_ref.refs_0_.refs_2_, s32[17]{0:T(128)S(1)} %pad_add_fusion.ints_ref, ...), custom_call_target="tpu_custom_call" | custom-call | flops 4294967296 | bytes 8388608 | tf_op jit(solution)/shard_map/pallas_call | solution.py:250
  27.6 1.5 %collective-permute-start.15 = (bf16[2,16,3200]{2,1,0:T(8,128)(2,1)S(1)}, bf16[2,16,3200]{2,1,0:T(8,128)(2,1)S(1)}, u32[]{:S(2)}, u32[]{:S(2)}) collective-permute-start(bf16[2,16,3200]{2,1,0:T(8,128)(2,1)S(1)} %get-tuple-element.38), channel_id=1, source_target_pairs={{0,1},{1,0},{2,3},{3,2},{4,5},{5,4},{6,7},{7,6},{8,9},{9,8},{10,11... | collective-permute-start | bytes 614408 | tf_op jit(solution)/shard_map/ppermute | solution.py:381
  30.5 3.2 %collective-permute-start.20 = (bf16[16,3200]{1,0:T(8,128)(2,1)S(1)}, bf16[16,3200]{1,0:T(8,128)(2,1)S(1)}, u32[]{:S(2)}, u32[]{:S(2)}) collective-permute-start(bf16[16,3200]{1,0:T(8,128)(2,1)S(1)} %shard_map.100), channel_id=1, source_target_pairs={{0,4},{1,3},{4,8},{5,1},{8,12},{9,5},{12,14},{13,9},{14,10},{15,13... | collective-permute-start | bytes 307208 | tf_op jit(solution)/shard_map/ppermute | solution.py:390
  34.3 1.9 %collective-permute-start.22 = (bf16[16,3200]{1,0:T(8,128)(2,1)S(1)}, bf16[16,3200]{1,0:T(8,128)(2,1)S(1)}, u32[]{:S(2)}, u32[]{:S(2)}) collective-permute-start(bf16[16,3200]{1,0:T(8,128)(2,1)S(1)} %shard_map.102), channel_id=1, source_target_pairs={{0,14},{1,15},{4,10},{5,11},{8,6},{9,7},{12,2},{13,3},{14,0},{15,1... | collective-permute-start | bytes 307208 | tf_op jit(solution)/shard_map/ppermute | solution.py:390
  36.4 2.1 %collective-permute-start.21 = (bf16[16,3200]{1,0:T(8,128)(2,1)S(1)}, bf16[16,3200]{1,0:T(8,128)(2,1)S(1)}, u32[]{:S(2)}, u32[]{:S(2)}) collective-permute-start(bf16[16,3200]{1,0:T(8,128)(2,1)S(1)} %shard_map.101), channel_id=1, source_target_pairs={{0,4},{1,3},{4,8},{5,1},{8,12},{9,5},{12,14},{13,9},{14,10},{15,13... | collective-permute-start | bytes 307208 | tf_op jit(solution)/shard_map/ppermute | solution.py:390
  38.6 4.0 %collective-permute-start.18 = (bf16[16,3200]{1,0:T(8,128)(2,1)S(1)}, bf16[16,3200]{1,0:T(8,128)(2,1)S(1)}, u32[]{:S(2)}, u32[]{:S(2)}) collective-permute-start(bf16[16,3200]{1,0:T(8,128)(2,1)S(1)} %shard_map.98), channel_id=1, source_target_pairs={{0,4},{1,3},{4,8},{5,1},{8,12},{9,5},{12,14},{13,9},{14,10},{15,13... | collective-permute-start | bytes 307208 | tf_op jit(solution)/shard_map/ppermute | solution.py:390
  42.9 2.4 %collective-permute-start.23 = (bf16[16,3200]{1,0:T(8,128)(2,1)S(1)}, bf16[16,3200]{1,0:T(8,128)(2,1)S(1)}, u32[]{:S(2)}, u32[]{:S(2)}) collective-permute-start(bf16[16,3200]{1,0:T(8,128)(2,1)S(1)} %shard_map.103), channel_id=1, source_target_pairs={{0,4},{1,3},{4,8},{5,1},{8,12},{9,5},{12,14},{13,9},{14,10},{15,13... | collective-permute-start | bytes 307208 | tf_op jit(solution)/shard_map/ppermute | solution.py:390
  45.3 2.4 %collective-permute-start.19 = (bf16[16,3200]{1,0:T(8,128)(2,1)S(1)}, bf16[16,3200]{1,0:T(8,128)(2,1)S(1)}, u32[]{:S(2)}, u32[]{:S(2)}) collective-permute-start(bf16[16,3200]{1,0:T(8,128)(2,1)S(1)} %shard_map.99), channel_id=1, source_target_pairs={{0,4},{1,3},{4,8},{5,1},{8,12},{9,5},{12,14},{13,9},{14,10},{15,13... | collective-permute-start | bytes 307208 | tf_op jit(solution)/shard_map/ppermute | solution.py:390
  47.7 2.3 %collective-permute-done.19.refs_4_ = bf16[16,3200]{1,0:T(8,128)(2,1)S(1)} collective-permute-done((bf16[16,3200]{1,0:T(8,128)(2,1)S(1)}, bf16[16,3200]{1,0:T(8,128)(2,1)S(1)}, u32[]{:S(2)}, u32[]{:S(2)}) %collective-permute-start.19) | collective-permute-done | bytes 102432 | tf_op jit(solution)/shard_map/ppermute | solution.py:390
  50.3 2.4 %collective-permute-start.26 = (bf16[16,3200]{1,0:T(8,128)(2,1)S(1)}, bf16[16,3200]{1,0:T(8,128)(2,1)S(1)}, u32[]{:S(2)}, u32[]{:S(2)}) collective-permute-start(bf16[16,3200]{1,0:T(8,128)(2,1)S(1)} %get-tuple-element.47.refs_0_), channel_id=1, source_target_pairs={{0,4},{1,3},{4,8},{5,1},{8,12},{9,5},{12,14},{13,9},{14,10},{15,13... | collective-permute-start | bytes 307208 | tf_op jit(solution)/shard_map/ppermute | solution.py:390
  52.8 2.1 %collective-permute-start.27 = (bf16[16,3200]{1,0:T(8,128)(2,1)S(1)}, bf16[16,3200]{1,0:T(8,128)(2,1)S(1)}, u32[]{:S(2)}, u32[]{:S(2)}) collective-permute-start(bf16[16,3200]{1,0:T(8,128)(2,1)S(1)} %collective-permute-done.25.refs_1_), channel_id=1, source_target_pairs={{0,4},{1,3},{4,8},{5,1},{8,12},{9,5},{12,14},{13,9},{14,10},{15,13... | collective-permute-start | bytes 307208 | tf_op jit(solution)/shard_map/ppermute | solution.py:390
  55.1 2.4 %collective-permute-start.30 = (bf16[16,3200]{1,0:T(8,128)(2,1)S(1)}, bf16[16,3200]{1,0:T(8,128)(2,1)S(1)}, u32[]{:S(2)}, u32[]{:S(2)}) collective-permute-start(bf16[16,3200]{1,0:T(8,128)(2,1)S(1)} %collective-permute-done.26.refs_2_), channel_id=1, source_target_pairs={{0,4},{1,3},{4,8},{5,1},{8,12},{9,5},{12,14},{13,9},{14,10},{15,13... | collective-permute-start | bytes 307208 | tf_op jit(solution)/shard_map/ppermute | solution.py:390
  57.4 2.1 %collective-permute-start.31 = (bf16[16,3200]{1,0:T(8,128)(2,1)S(1)}, bf16[16,3200]{1,0:T(8,128)(2,1)S(1)}, u32[]{:S(2)}, u32[]{:S(2)}) collective-permute-start(bf16[16,3200]{1,0:T(8,128)(2,1)S(1)} %collective-permute-done.27.refs_3_), channel_id=1, source_target_pairs={{0,4},{1,3},{4,8},{5,1},{8,12},{9,5},{12,14},{13,9},{14,10},{15,13... | collective-permute-start | bytes 307208 | tf_op jit(solution)/shard_map/ppermute | solution.py:390
  59.6 1.4 %collective-permute-start.38 = (bf16[16,3200]{1,0:T(8,128)(2,1)S(1)}, bf16[16,3200]{1,0:T(8,128)(2,1)S(1)}, u32[]{:S(2)}, u32[]{:S(2)}) collective-permute-start(bf16[16,3200]{1,0:T(8,128)(2,1)S(1)} %get-tuple-element.47.refs_0_), channel_id=1, source_target_pairs={{0,14},{1,15},{4,10},{5,11},{8,6},{9,7},{12,2},{13,3},{14,0},{15,1... | collective-permute-start | bytes 307208 | tf_op jit(solution)/shard_map/ppermute | solution.py:390
  62.4 3.8 %collective-permute-start.35 = (bf16[16,3200]{1,0:T(8,128)(2,1)S(1)}, bf16[16,3200]{1,0:T(8,128)(2,1)S(1)}, u32[]{:S(2)}, u32[]{:S(2)}) collective-permute-start(bf16[16,3200]{1,0:T(8,128)(2,1)S(1)} %collective-permute-done.31.refs_7_), channel_id=1, source_target_pairs={{0,4},{1,3},{4,8},{5,1},{8,12},{9,5},{12,14},{13,9},{14,10},{15,13... | collective-permute-start | bytes 307208 | tf_op jit(solution)/shard_map/ppermute | solution.py:390
  66.1 1.6 %collective-permute-done.38.refs_14_ = bf16[16,3200]{1,0:T(8,128)(2,1)S(1)} collective-permute-done((bf16[16,3200]{1,0:T(8,128)(2,1)S(1)}, bf16[16,3200]{1,0:T(8,128)(2,1)S(1)}, u32[]{:S(2)}, u32[]{:S(2)}) %collective-permute-start.38) | collective-permute-done | bytes 102432 | tf_op jit(solution)/shard_map/ppermute | solution.py:390
  70.2 3.5 %shard_map.105 = (f32[3,512,512]{2,1,0:T(8,128)S(1)}, bf16[2,16,3200]{2,1,0:T(8,128)(2,1)S(1)}, bf16[6,16,3200]{2,1,0:T(8,128)(2,1)S(1)}, f32[8,128]{1,0:T(8,128)S(1)}, f32[8,128]{1,0:T(8,128)S(1)}) custom-call(s32[1]{0:T(128)} %bitcast.me_ref.refs_0_.refs_2_, s32[17]{0:T(128)S(1)} %pad_add_fusion.ints_ref, bf16[16,3200]{1,0:T(8,128)(2,1)S(1)} %get-tuple-element.47.refs_0_, ...), custom_call_target="tpu_custom_call" | custom-call | flops 4294967296 | bytes 8388608 | tf_op jit(solution)/shard_map/pallas_call | solution.py:250
  73.9 1.3 %collective-permute-done.40.other_ref = bf16[2,16,3200]{2,1,0:T(8,128)(2,1)S(1)} collective-permute-done((bf16[2,16,3200]{2,1,0:T(8,128)(2,1)S(1)}, bf16[2,16,3200]{2,1,0:T(8,128)(2,1)S(1)}, u32[]{:S(2)}, u32[]{:S(2)}) %collective-permute-start.40) | collective-permute-done | bytes 204832 | tf_op jit(solution)/shard_map/ppermute | solution.py:381
  75.4 4.4 %collective-permute-start.45 = (bf16[16,3200]{1,0:T(8,128)(2,1)S(1)}, bf16[16,3200]{1,0:T(8,128)(2,1)S(1)}, u32[]{:S(2)}, u32[]{:S(2)}) collective-permute-start(bf16[16,3200]{1,0:T(8,128)(2,1)S(1)} %shard_map.109), channel_id=1, source_target_pairs={{0,4},{1,3},{4,8},{5,1},{8,12},{9,5},{12,14},{13,9},{14,10},{15,13... | collective-permute-start | bytes 307208 | tf_op jit(solution)/shard_map/ppermute | solution.py:390
  79.9 2.4 %collective-permute-start.42 = (bf16[16,3200]{1,0:T(8,128)(2,1)S(1)}, bf16[16,3200]{1,0:T(8,128)(2,1)S(1)}, u32[]{:S(2)}, u32[]{:S(2)}) collective-permute-start(bf16[16,3200]{1,0:T(8,128)(2,1)S(1)} %shard_map.106), channel_id=1, source_target_pairs={{0,4},{1,3},{4,8},{5,1},{8,12},{9,5},{12,14},{13,9},{14,10},{15,13... | collective-permute-start | bytes 307208 | tf_op jit(solution)/shard_map/ppermute | solution.py:390
  83.5 1.6 %collective-permute-start.46 = (bf16[16,3200]{1,0:T(8,128)(2,1)S(1)}, bf16[16,3200]{1,0:T(8,128)(2,1)S(1)}, u32[]{:S(2)}, u32[]{:S(2)}) collective-permute-start(bf16[16,3200]{1,0:T(8,128)(2,1)S(1)} %shard_map.110), channel_id=1, source_target_pairs={{0,4},{1,3},{4,8},{5,1},{8,12},{9,5},{12,14},{13,9},{14,10},{15,13... | collective-permute-start | bytes 307208 | tf_op jit(solution)/shard_map/ppermute | solution.py:390
  85.2 3.7 %collective-permute-start.43 = (bf16[16,3200]{1,0:T(8,128)(2,1)S(1)}, bf16[16,3200]{1,0:T(8,128)(2,1)S(1)}, u32[]{:S(2)}, u32[]{:S(2)}) collective-permute-start(bf16[16,3200]{1,0:T(8,128)(2,1)S(1)} %shard_map.107), channel_id=1, source_target_pairs={{0,4},{1,3},{4,8},{5,1},{8,12},{9,5},{12,14},{13,9},{14,10},{15,13... | collective-permute-start | bytes 307208 | tf_op jit(solution)/shard_map/ppermute | solution.py:390
  90.0 1.4 %collective-permute-start.48 = (bf16[16,3200]{1,0:T(8,128)(2,1)S(1)}, bf16[16,3200]{1,0:T(8,128)(2,1)S(1)}, u32[]{:S(2)}, u32[]{:S(2)}) collective-permute-start(bf16[16,3200]{1,0:T(8,128)(2,1)S(1)} %shard_map.112), channel_id=1, source_target_pairs={{0,4},{1,3},{4,8},{5,1},{8,12},{9,5},{12,14},{13,9},{14,10},{15,13... | collective-permute-start | bytes 307208 | tf_op jit(solution)/shard_map/ppermute | solution.py:390
  91.6 2.2 %collective-permute-start.44 = (bf16[16,3200]{1,0:T(8,128)(2,1)S(1)}, bf16[16,3200]{1,0:T(8,128)(2,1)S(1)}, u32[]{:S(2)}, u32[]{:S(2)}) collective-permute-start(bf16[16,3200]{1,0:T(8,128)(2,1)S(1)} %shard_map.108), channel_id=1, source_target_pairs={{0,4},{1,3},{4,8},{5,1},{8,12},{9,5},{12,14},{13,9},{14,10},{15,13... | collective-permute-start | bytes 307208 | tf_op jit(solution)/shard_map/ppermute | solution.py:390
  94.8 1.5 %collective-permute-done.44.refs_6_ = bf16[16,3200]{1,0:T(8,128)(2,1)S(1)} collective-permute-done((bf16[16,3200]{1,0:T(8,128)(2,1)S(1)}, bf16[16,3200]{1,0:T(8,128)(2,1)S(1)}, u32[]{:S(2)}, u32[]{:S(2)}) %collective-permute-start.44) | collective-permute-done | bytes 102432 | tf_op jit(solution)/shard_map/ppermute | solution.py:390
  (99 shorter events, 18.3 us)
Async XLA Ops:
  1.1 5.4 %collective-permute-start.4 = (bf16[3,32,512]{2,1,0:T(8,128)(2,1)}, bf16[3,32,512]{2,1,0:T(8,128)(2,1)S(1)}, u32[]{:S(2)}, u32[]{:S(2)}) collective-permute-start(bf16[3,32,512]{2,1,0:T(8,128)(2,1)} %wave_ref.3), channel_id=1, source_target_pairs={{0,4},{1,3},{4,8},{5,1},{8,12},{9,5},{12,14},{13,9},{14,10},{15,13... | collective-permute-start | bytes 294920 | tf_op jit(solution)/shard_map/ppermute | solution.py:390
  3.8 4.8 %collective-permute-start.2 = (bf16[3,32,512]{2,1,0:T(8,128)(2,1)S(1)}, bf16[3,32,512]{2,1,0:T(8,128)(2,1)S(1)}, u32[]{:S(2)}, u32[]{:S(2)}) collective-permute-start(bf16[3,32,512]{2,1,0:T(8,128)(2,1)S(1)} %collective-permute-done.refs_1_), channel_id=1, source_target_pairs={{0,4},{1,3},{4,8},{5,1},{8,12},{9,5},{12,14},{13,9},{14,10},{15,13... | collective-permute-start | bytes 294920 | tf_op jit(solution)/shard_map/ppermute | solution.py:390
  6.5 7.5 %collective-permute-start.7 = (bf16[3,32,512]{2,1,0:T(8,128)(2,1)S(1)}, bf16[3,32,512]{2,1,0:T(8,128)(2,1)S(1)}, u32[]{:S(2)}, u32[]{:S(2)}) collective-permute-start(bf16[3,32,512]{2,1,0:T(8,128)(2,1)S(1)} %collective-permute-done.4.refs_2_), channel_id=1, source_target_pairs={{0,4},{1,3},{4,8},{5,1},{8,12},{9,5},{12,14},{13,9},{14,10},{15,13... | collective-permute-start | bytes 294920 | tf_op jit(solution)/shard_map/ppermute | solution.py:390
  8.6 7.2 %collective-permute-start.3 = (bf16[3,32,512]{2,1,0:T(8,128)(2,1)S(1)}, bf16[3,32,512]{2,1,0:T(8,128)(2,1)S(1)}, u32[]{:S(2)}, u32[]{:S(2)}) collective-permute-start(bf16[3,32,512]{2,1,0:T(8,128)(2,1)S(1)} %collective-permute-done.2.refs_3_), channel_id=1, source_target_pairs={{0,4},{1,3},{4,8},{5,1},{8,12},{9,5},{12,14},{13,9},{14,10},{15,13... | collective-permute-start | bytes 294920 | tf_op jit(solution)/shard_map/ppermute | solution.py:390
  10.9 7.7 %collective-permute-start.1 = (bf16[3,32,512]{2,1,0:T(8,128)(2,1)}, bf16[3,32,512]{2,1,0:T(8,128)(2,1)S(1)}, u32[]{:S(2)}, u32[]{:S(2)}) collective-permute-start(bf16[3,32,512]{2,1,0:T(8,128)(2,1)} %wave_ref.3), channel_id=1, source_target_pairs={{0,14},{1,15},{4,10},{5,11},{8,6},{9,7},{12,2},{13,3},{14,0},{15,1... | collective-permute-start | bytes 294920 | tf_op jit(solution)/shard_map/ppermute | solution.py:390
  14.0 5.6 %collective-permute-start.10 = (bf16[3,32,512]{2,1,0:T(8,128)(2,1)S(1)}, bf16[3,32,512]{2,1,0:T(8,128)(2,1)S(1)}, u32[]{:S(2)}, u32[]{:S(2)}) collective-permute-start(bf16[3,32,512]{2,1,0:T(8,128)(2,1)S(1)} %collective-permute-done.7.refs_6_), channel_id=1, source_target_pairs={{0,4},{1,3},{4,8},{5,1},{8,12},{9,5},{12,14},{13,9},{14,10},{15,13... | collective-permute-start | bytes 294920 | tf_op jit(solution)/shard_map/ppermute | solution.py:390
  14.1 5.6 %collective-permute-start.8 = (bf16[3,32,512]{2,1,0:T(8,128)(2,1)S(1)}, bf16[3,32,512]{2,1,0:T(8,128)(2,1)S(1)}, u32[]{:S(2)}, u32[]{:S(2)}) collective-permute-start(bf16[3,32,512]{2,1,0:T(8,128)(2,1)S(1)} %collective-permute-done.7.refs_6_), channel_id=1, source_target_pairs={{0,1},{1,0},{2,3},{3,2},{4,5},{5,4},{6,7},{7,6},{8,9},{9,8},{10,11... | collective-permute-start | bytes 294920 | tf_op jit(solution)/shard_map/ppermute | solution.py:381
  15.9 4.8 %collective-permute-start.11 = (bf16[3,32,512]{2,1,0:T(8,128)(2,1)S(1)}, bf16[3,32,512]{2,1,0:T(8,128)(2,1)S(1)}, u32[]{:S(2)}, u32[]{:S(2)}) collective-permute-start(bf16[3,32,512]{2,1,0:T(8,128)(2,1)S(1)} %collective-permute-done.3._.refs_7_), channel_id=1, source_target_pairs={{0,4},{1,3},{4,8},{5,1},{8,12},{9,5},{12,14},{13,9},{14,10},{15,13... | collective-permute-start | bytes 294920 | tf_op jit(solution)/shard_map/ppermute | solution.py:390
  30.5 5.8 %collective-permute-start.20 = (bf16[16,3200]{1,0:T(8,128)(2,1)S(1)}, bf16[16,3200]{1,0:T(8,128)(2,1)S(1)}, u32[]{:S(2)}, u32[]{:S(2)}) collective-permute-start(bf16[16,3200]{1,0:T(8,128)(2,1)S(1)} %shard_map.100), channel_id=1, source_target_pairs={{0,4},{1,3},{4,8},{5,1},{8,12},{9,5},{12,14},{13,9},{14,10},{15,13... | collective-permute-start | bytes 307208 | tf_op jit(solution)/shard_map/ppermute | solution.py:390
  33.8 4.7 %collective-permute-start.17 = (bf16[16,3200]{1,0:T(8,128)(2,1)S(1)}, bf16[16,3200]{1,0:T(8,128)(2,1)S(1)}, u32[]{:S(2)}, u32[]{:S(2)}) collective-permute-start(bf16[16,3200]{1,0:T(8,128)(2,1)S(1)} %shard_map.97), channel_id=1, source_target_pairs={{0,4},{1,3},{4,8},{5,1},{8,12},{9,5},{12,14},{13,9},{14,10},{15,13... | collective-permute-start | bytes 307208 | tf_op jit(solution)/shard_map/ppermute | solution.py:390
  34.3 8.3 %collective-permute-start.22 = (bf16[16,3200]{1,0:T(8,128)(2,1)S(1)}, bf16[16,3200]{1,0:T(8,128)(2,1)S(1)}, u32[]{:S(2)}, u32[]{:S(2)}) collective-permute-start(bf16[16,3200]{1,0:T(8,128)(2,1)S(1)} %shard_map.102), channel_id=1, source_target_pairs={{0,14},{1,15},{4,10},{5,11},{8,6},{9,7},{12,2},{13,3},{14,0},{15,1... | collective-permute-start | bytes 307208 | tf_op jit(solution)/shard_map/ppermute | solution.py:390
  36.4 6.4 %collective-permute-start.21 = (bf16[16,3200]{1,0:T(8,128)(2,1)S(1)}, bf16[16,3200]{1,0:T(8,128)(2,1)S(1)}, u32[]{:S(2)}, u32[]{:S(2)}) collective-permute-start(bf16[16,3200]{1,0:T(8,128)(2,1)S(1)} %shard_map.101), channel_id=1, source_target_pairs={{0,4},{1,3},{4,8},{5,1},{8,12},{9,5},{12,14},{13,9},{14,10},{15,13... | collective-permute-start | bytes 307208 | tf_op jit(solution)/shard_map/ppermute | solution.py:390
  38.6 6.6 %collective-permute-start.18 = (bf16[16,3200]{1,0:T(8,128)(2,1)S(1)}, bf16[16,3200]{1,0:T(8,128)(2,1)S(1)}, u32[]{:S(2)}, u32[]{:S(2)}) collective-permute-start(bf16[16,3200]{1,0:T(8,128)(2,1)S(1)} %shard_map.98), channel_id=1, source_target_pairs={{0,4},{1,3},{4,8},{5,1},{8,12},{9,5},{12,14},{13,9},{14,10},{15,13... | collective-permute-start | bytes 307208 | tf_op jit(solution)/shard_map/ppermute | solution.py:390
  42.9 4.9 %collective-permute-start.23 = (bf16[16,3200]{1,0:T(8,128)(2,1)S(1)}, bf16[16,3200]{1,0:T(8,128)(2,1)S(1)}, u32[]{:S(2)}, u32[]{:S(2)}) collective-permute-start(bf16[16,3200]{1,0:T(8,128)(2,1)S(1)} %shard_map.103), channel_id=1, source_target_pairs={{0,4},{1,3},{4,8},{5,1},{8,12},{9,5},{12,14},{13,9},{14,10},{15,13... | collective-permute-start | bytes 307208 | tf_op jit(solution)/shard_map/ppermute | solution.py:390
  45.3 4.7 %collective-permute-start.19 = (bf16[16,3200]{1,0:T(8,128)(2,1)S(1)}, bf16[16,3200]{1,0:T(8,128)(2,1)S(1)}, u32[]{:S(2)}, u32[]{:S(2)}) collective-permute-start(bf16[16,3200]{1,0:T(8,128)(2,1)S(1)} %shard_map.99), channel_id=1, source_target_pairs={{0,4},{1,3},{4,8},{5,1},{8,12},{9,5},{12,14},{13,9},{14,10},{15,13... | collective-permute-start | bytes 307208 | tf_op jit(solution)/shard_map/ppermute | solution.py:390
  50.3 4.7 %collective-permute-start.26 = (bf16[16,3200]{1,0:T(8,128)(2,1)S(1)}, bf16[16,3200]{1,0:T(8,128)(2,1)S(1)}, u32[]{:S(2)}, u32[]{:S(2)}) collective-permute-start(bf16[16,3200]{1,0:T(8,128)(2,1)S(1)} %get-tuple-element.47.refs_0_), channel_id=1, source_target_pairs={{0,4},{1,3},{4,8},{5,1},{8,12},{9,5},{12,14},{13,9},{14,10},{15,13... | collective-permute-start | bytes 307208 | tf_op jit(solution)/shard_map/ppermute | solution.py:390
  52.8 4.7 %collective-permute-start.27 = (bf16[16,3200]{1,0:T(8,128)(2,1)S(1)}, bf16[16,3200]{1,0:T(8,128)(2,1)S(1)}, u32[]{:S(2)}, u32[]{:S(2)}) collective-permute-start(bf16[16,3200]{1,0:T(8,128)(2,1)S(1)} %collective-permute-done.25.refs_1_), channel_id=1, source_target_pairs={{0,4},{1,3},{4,8},{5,1},{8,12},{9,5},{12,14},{13,9},{14,10},{15,13... | collective-permute-start | bytes 307208 | tf_op jit(solution)/shard_map/ppermute | solution.py:390
  55.1 5.9 %collective-permute-start.30 = (bf16[16,3200]{1,0:T(8,128)(2,1)S(1)}, bf16[16,3200]{1,0:T(8,128)(2,1)S(1)}, u32[]{:S(2)}, u32[]{:S(2)}) collective-permute-start(bf16[16,3200]{1,0:T(8,128)(2,1)S(1)} %collective-permute-done.26.refs_2_), channel_id=1, source_target_pairs={{0,4},{1,3},{4,8},{5,1},{8,12},{9,5},{12,14},{13,9},{14,10},{15,13... | collective-permute-start | bytes 307208 | tf_op jit(solution)/shard_map/ppermute | solution.py:390
  57.4 4.9 %collective-permute-start.31 = (bf16[16,3200]{1,0:T(8,128)(2,1)S(1)}, bf16[16,3200]{1,0:T(8,128)(2,1)S(1)}, u32[]{:S(2)}, u32[]{:S(2)}) collective-permute-start(bf16[16,3200]{1,0:T(8,128)(2,1)S(1)} %collective-permute-done.27.refs_3_), channel_id=1, source_target_pairs={{0,4},{1,3},{4,8},{5,1},{8,12},{9,5},{12,14},{13,9},{14,10},{15,13... | collective-permute-start | bytes 307208 | tf_op jit(solution)/shard_map/ppermute | solution.py:390
  59.6 6.6 %collective-permute-start.28 = (bf16[16,3200]{1,0:T(8,128)(2,1)S(1)}, bf16[16,3200]{1,0:T(8,128)(2,1)S(1)}, u32[]{:S(2)}, u32[]{:S(2)}) collective-permute-start(bf16[16,3200]{1,0:T(8,128)(2,1)S(1)} %collective-permute-done.26.refs_2_), channel_id=1, source_target_pairs={{0,1},{1,0},{2,3},{3,2},{4,5},{5,4},{6,7},{7,6},{8,9},{9,8},{10,11... | collective-permute-start | bytes 307208 | tf_op jit(solution)/shard_map/ppermute | solution.py:381
  59.6 8.2 %collective-permute-start.38 = (bf16[16,3200]{1,0:T(8,128)(2,1)S(1)}, bf16[16,3200]{1,0:T(8,128)(2,1)S(1)}, u32[]{:S(2)}, u32[]{:S(2)}) collective-permute-start(bf16[16,3200]{1,0:T(8,128)(2,1)S(1)} %get-tuple-element.47.refs_0_), channel_id=1, source_target_pairs={{0,14},{1,15},{4,10},{5,11},{8,6},{9,7},{12,2},{13,3},{14,0},{15,1... | collective-permute-start | bytes 307208 | tf_op jit(solution)/shard_map/ppermute | solution.py:390
  61.0 6.9 %collective-permute-start.34 = (bf16[16,3200]{1,0:T(8,128)(2,1)S(1)}, bf16[16,3200]{1,0:T(8,128)(2,1)S(1)}, u32[]{:S(2)}, u32[]{:S(2)}) collective-permute-start(bf16[16,3200]{1,0:T(8,128)(2,1)S(1)} %collective-permute-done.30.refs_6_), channel_id=1, source_target_pairs={{0,4},{1,3},{4,8},{5,1},{8,12},{9,5},{12,14},{13,9},{14,10},{15,13... | collective-permute-start | bytes 307208 | tf_op jit(solution)/shard_map/ppermute | solution.py:390
  62.1 6.2 %collective-permute-start.32 = (bf16[16,3200]{1,0:T(8,128)(2,1)S(1)}, bf16[16,3200]{1,0:T(8,128)(2,1)S(1)}, u32[]{:S(2)}, u32[]{:S(2)}) collective-permute-start(bf16[16,3200]{1,0:T(8,128)(2,1)S(1)} %collective-permute-done.30.refs_6_), channel_id=1, source_target_pairs={{0,1},{1,0},{2,3},{3,2},{4,5},{5,4},{6,7},{7,6},{8,9},{9,8},{10,11... | collective-permute-start | bytes 307208 | tf_op jit(solution)/shard_map/ppermute | solution.py:381
  62.4 6.5 %collective-permute-start.35 = (bf16[16,3200]{1,0:T(8,128)(2,1)S(1)}, bf16[16,3200]{1,0:T(8,128)(2,1)S(1)}, u32[]{:S(2)}, u32[]{:S(2)}) collective-permute-start(bf16[16,3200]{1,0:T(8,128)(2,1)S(1)} %collective-permute-done.31.refs_7_), channel_id=1, source_target_pairs={{0,4},{1,3},{4,8},{5,1},{8,12},{9,5},{12,14},{13,9},{14,10},{15,13... | collective-permute-start | bytes 307208 | tf_op jit(solution)/shard_map/ppermute | solution.py:390
  75.2 7.1 %collective-permute-start.41 = (bf16[6,16,3200]{2,1,0:T(8,128)(2,1)S(1)}, bf16[6,16,3200]{2,1,0:T(8,128)(2,1)S(1)}, u32[]{:S(2)}, u32[]{:S(2)}) collective-permute-start(bf16[6,16,3200]{2,1,0:T(8,128)(2,1)S(1)} %get-tuple-element.54), channel_id=1, source_target_pairs={{0,1},{1,0},{2,3},{3,2},{4,5},{5,4},{6,7},{7,6},{8,9},{9,8},{10,11... | collective-permute-start | bytes 1843208 | tf_op jit(solution)/shard_map/ppermute | solution.py:381
  75.4 8.0 %collective-permute-start.45 = (bf16[16,3200]{1,0:T(8,128)(2,1)S(1)}, bf16[16,3200]{1,0:T(8,128)(2,1)S(1)}, u32[]{:S(2)}, u32[]{:S(2)}) collective-permute-start(bf16[16,3200]{1,0:T(8,128)(2,1)S(1)} %shard_map.109), channel_id=1, source_target_pairs={{0,4},{1,3},{4,8},{5,1},{8,12},{9,5},{12,14},{13,9},{14,10},{15,13... | collective-permute-start | bytes 307208 | tf_op jit(solution)/shard_map/ppermute | solution.py:390
  79.9 5.3 %collective-permute-start.42 = (bf16[16,3200]{1,0:T(8,128)(2,1)S(1)}, bf16[16,3200]{1,0:T(8,128)(2,1)S(1)}, u32[]{:S(2)}, u32[]{:S(2)}) collective-permute-start(bf16[16,3200]{1,0:T(8,128)(2,1)S(1)} %shard_map.106), channel_id=1, source_target_pairs={{0,4},{1,3},{4,8},{5,1},{8,12},{9,5},{12,14},{13,9},{14,10},{15,13... | collective-permute-start | bytes 307208 | tf_op jit(solution)/shard_map/ppermute | solution.py:390
  82.3 7.6 %collective-permute-start.47 = (bf16[16,3200]{1,0:T(8,128)(2,1)S(1)}, bf16[16,3200]{1,0:T(8,128)(2,1)S(1)}, u32[]{:S(2)}, u32[]{:S(2)}) collective-permute-start(bf16[16,3200]{1,0:T(8,128)(2,1)S(1)} %shard_map.111), channel_id=1, source_target_pairs={{0,14},{1,15},{4,10},{5,11},{8,6},{9,7},{12,2},{13,3},{14,0},{15,1... | collective-permute-start | bytes 307208 | tf_op jit(solution)/shard_map/ppermute | solution.py:390
  83.5 6.4 %collective-permute-start.46 = (bf16[16,3200]{1,0:T(8,128)(2,1)S(1)}, bf16[16,3200]{1,0:T(8,128)(2,1)S(1)}, u32[]{:S(2)}, u32[]{:S(2)}) collective-permute-start(bf16[16,3200]{1,0:T(8,128)(2,1)S(1)} %shard_map.110), channel_id=1, source_target_pairs={{0,4},{1,3},{4,8},{5,1},{8,12},{9,5},{12,14},{13,9},{14,10},{15,13... | collective-permute-start | bytes 307208 | tf_op jit(solution)/shard_map/ppermute | solution.py:390
  85.2 6.3 %collective-permute-start.43 = (bf16[16,3200]{1,0:T(8,128)(2,1)S(1)}, bf16[16,3200]{1,0:T(8,128)(2,1)S(1)}, u32[]{:S(2)}, u32[]{:S(2)}) collective-permute-start(bf16[16,3200]{1,0:T(8,128)(2,1)S(1)} %shard_map.107), channel_id=1, source_target_pairs={{0,4},{1,3},{4,8},{5,1},{8,12},{9,5},{12,14},{13,9},{14,10},{15,13... | collective-permute-start | bytes 307208 | tf_op jit(solution)/shard_map/ppermute | solution.py:390
  90.0 4.7 %collective-permute-start.48 = (bf16[16,3200]{1,0:T(8,128)(2,1)S(1)}, bf16[16,3200]{1,0:T(8,128)(2,1)S(1)}, u32[]{:S(2)}, u32[]{:S(2)}) collective-permute-start(bf16[16,3200]{1,0:T(8,128)(2,1)S(1)} %shard_map.112), channel_id=1, source_target_pairs={{0,4},{1,3},{4,8},{5,1},{8,12},{9,5},{12,14},{13,9},{14,10},{15,13... | collective-permute-start | bytes 307208 | tf_op jit(solution)/shard_map/ppermute | solution.py:390
  91.6 4.7 %collective-permute-start.44 = (bf16[16,3200]{1,0:T(8,128)(2,1)S(1)}, bf16[16,3200]{1,0:T(8,128)(2,1)S(1)}, u32[]{:S(2)}, u32[]{:S(2)}) collective-permute-start(bf16[16,3200]{1,0:T(8,128)(2,1)S(1)} %shard_map.108), channel_id=1, source_target_pairs={{0,4},{1,3},{4,8},{5,1},{8,12},{9,5},{12,14},{13,9},{14,10},{15,13... | collective-permute-start | bytes 307208 | tf_op jit(solution)/shard_map/ppermute | solution.py:390
  (23 other events, 116.2 us)

commit v22 on v20

--- a/solution.py
+++ b/solution.py
@@ -185,8 +185,10 @@
 
     used = ints_ref[2 * slots]
 
+    group = GROUP if first else 2 * GROUP
+
     def add_some(step, carry):
-        some = [step * GROUP + k for k in range(GROUP)]
+        some = [step * group + k for k in range(group)]
         if first:
             for slot in some:
                 for copy in copies(slot):
@@ -212,7 +214,7 @@
 
         return carry
 
-    lax.fori_loop(0, slots // GROUP, add_some, 0)
+    lax.fori_loop(0, slots // group, add_some, 0)
 
     dot = jnp.zeros((8, 128), jnp.float32)
     if first:
@@ -432,6 +434,7 @@
     sectors, rows, width = shape
     entries = float(sectors * rows * lax.axis_size("term") * width)
     me = lax.axis_index("term").astype(jnp.int32).reshape(1)
+
     def beside(after):
         ints = jnp.concatenate([block_source, block_target, live_count])
         return ints, copied(wavefunction, after)

time: 96.1 us -> 96.4 us (level)
  the two profiles are of different devices: /device:TPU:18 before, /device:TPU:0 now
where the time goes in v22:
time: 96.4 us; the launch traced here: 95.3 us
  starting transfers between devices  55.7 us (58%)
  waiting for transfers between devices  25.9 us (27%)
  Pallas kernels  10.6 us (11%)
  between operations  1.49 us (2%)
    ppermute x28, starting transfers between devices, hop(): return lax.ppermute(value, 'term', pairs)  44.7 us
    ppermute x28, waiting for transfers between devices, hop(): return lax.ppermute(value, 'term', pairs)  20.6 us
    ppermute x22, starting transfers between devices, flip(): return lax.ppermute(value, 'term', [(i, i ^ 1) for i in range(16)])  10.9 us
    pallas_call x2, Pallas kernels, apply_blocks(): pl.pallas_call(functools.partial(blocks_kernel, first, shape, entries), i...  8.63 us
    ppermute x22, waiting for transfers between devices, flip(): return lax.ppermute(value, 'term', [(i, i ^ 1) for i in range(16)])  5.21 us
  transfers between devices with their start and end apart: 50, of which 31 were waited for; matrix products, arithmetic and copies ran while one was open for 1% of the time, Pallas kernels for 1%

profile of v22, /device:TPU:0, one launch (start us, length us, event | category | flops | bytes accessed | tf_op | source)
XLA Modules:
  0.0 95.3 jit_solution(13215882793579212637)
XLA Ops:
  1.1 2.6 %collective-permute-start.4 = (bf16[3,32,512]{2,1,0:T(8,128)(2,1)}, bf16[3,32,512]{2,1,0:T(8,128)(2,1)S(1)}, u32[]{:S(2)}, u32[]{:S(2)}) collective-permute-start(bf16[3,32,512]{2,1,0:T(8,128)(2,1)} %wave_ref.3), channel_id=1, source_target_pairs={{0,4},{1,3},{4,8},{5,1},{8,12},{9,5},{12,14},{13,9},{14,10},{15,13... | collective-permute-start | bytes 294920 | tf_op jit(solution)/shard_map/ppermute | solution.py:393
  3.8 1.6 %collective-permute-start.2 = (bf16[3,32,512]{2,1,0:T(8,128)(2,1)S(1)}, bf16[3,32,512]{2,1,0:T(8,128)(2,1)S(1)}, u32[]{:S(2)}, u32[]{:S(2)}) collective-permute-start(bf16[3,32,512]{2,1,0:T(8,128)(2,1)S(1)} %collective-permute-done.refs_1_), channel_id=1, source_target_pairs={{0,4},{1,3},{4,8},{5,1},{8,12},{9,5},{12,14},{13,9},{14,10},{15,13... | collective-permute-start | bytes 294920 | tf_op jit(solution)/shard_map/ppermute | solution.py:393
  6.5 2.1 %collective-permute-start.7 = (bf16[3,32,512]{2,1,0:T(8,128)(2,1)S(1)}, bf16[3,32,512]{2,1,0:T(8,128)(2,1)S(1)}, u32[]{:S(2)}, u32[]{:S(2)}) collective-permute-start(bf16[3,32,512]{2,1,0:T(8,128)(2,1)S(1)} %collective-permute-done.4.refs_2_), channel_id=1, source_target_pairs={{0,4},{1,3},{4,8},{5,1},{8,12},{9,5},{12,14},{13,9},{14,10},{15,13... | collective-permute-start | bytes 294920 | tf_op jit(solution)/shard_map/ppermute | solution.py:393
  8.6 1.6 %collective-permute-start.3 = (bf16[3,32,512]{2,1,0:T(8,128)(2,1)S(1)}, bf16[3,32,512]{2,1,0:T(8,128)(2,1)S(1)}, u32[]{:S(2)}, u32[]{:S(2)}) collective-permute-start(bf16[3,32,512]{2,1,0:T(8,128)(2,1)S(1)} %collective-permute-done.2.refs_3_), channel_id=1, source_target_pairs={{0,4},{1,3},{4,8},{5,1},{8,12},{9,5},{12,14},{13,9},{14,10},{15,13... | collective-permute-start | bytes 294920 | tf_op jit(solution)/shard_map/ppermute | solution.py:393
  10.9 3.1 %collective-permute-start.1 = (bf16[3,32,512]{2,1,0:T(8,128)(2,1)}, bf16[3,32,512]{2,1,0:T(8,128)(2,1)S(1)}, u32[]{:S(2)}, u32[]{:S(2)}) collective-permute-start(bf16[3,32,512]{2,1,0:T(8,128)(2,1)} %wave_ref.3), channel_id=1, source_target_pairs={{0,14},{1,15},{4,10},{5,11},{8,6},{9,7},{12,2},{13,3},{14,0},{15,1... | collective-permute-start | bytes 294920 | tf_op jit(solution)/shard_map/ppermute | solution.py:393
  14.1 1.8 %collective-permute-start.8 = (bf16[3,32,512]{2,1,0:T(8,128)(2,1)S(1)}, bf16[3,32,512]{2,1,0:T(8,128)(2,1)S(1)}, u32[]{:S(2)}, u32[]{:S(2)}) collective-permute-start(bf16[3,32,512]{2,1,0:T(8,128)(2,1)S(1)} %collective-permute-done.7.refs_6_), channel_id=1, source_target_pairs={{0,1},{1,0},{2,3},{3,2},{4,5},{5,4},{6,7},{7,6},{8,9},{9,8},{10,11... | collective-permute-start | bytes 294920 | tf_op jit(solution)/shard_map/ppermute | solution.py:384
  17.2 1.5 %collective-permute-done.1.refs_14_ = bf16[3,32,512]{2,1,0:T(8,128)(2,1)S(1)} collective-permute-done((bf16[3,32,512]{2,1,0:T(8,128)(2,1)}, bf16[3,32,512]{2,1,0:T(8,128)(2,1)S(1)}, u32[]{:S(2)}, u32[]{:S(2)}) %collective-permute-start.1) | collective-permute-done | bytes 98336 | tf_op jit(solution)/shard_map/ppermute | solution.py:393
  22.0 5.2 %shard_map.96 = (f32[3,512,512]{2,1,0:T(8,128)S(1)}, bf16[2,16,3200]{2,1,0:T(8,128)(2,1)S(1)}, bf16[6,16,3200]{2,1,0:T(8,128)(2,1)S(1)}, f32[8,128]{1,0:T(8,128)S(1)}, f32[8,128]{1,0:T(8,128)S(1)}) custom-call(s32[1]{0:T(128)} %bitcast.me_ref.refs_0_.refs_2_, s32[17]{0:T(128)S(1)} %pad_add_fusion.ints_ref, ...), custom_call_target="tpu_custom_call" | custom-call | flops 4294967296 | bytes 8388608 | tf_op jit(solution)/shard_map/pallas_call | solution.py:253
  27.2 3.5 %collective-permute-start.15 = (bf16[2,16,3200]{2,1,0:T(8,128)(2,1)S(1)}, bf16[2,16,3200]{2,1,0:T(8,128)(2,1)S(1)}, u32[]{:S(2)}, u32[]{:S(2)}) collective-permute-start(bf16[2,16,3200]{2,1,0:T(8,128)(2,1)S(1)} %get-tuple-element.38), channel_id=1, source_target_pairs={{0,1},{1,0},{2,3},{3,2},{4,5},{5,4},{6,7},{7,6},{8,9},{9,8},{10,11... | collective-permute-start | bytes 614408 | tf_op jit(solution)/shard_map/ppermute | solution.py:384
  32.3 2.3 %collective-permute-start.17 = (bf16[16,3200]{1,0:T(8,128)(2,1)S(1)}, bf16[16,3200]{1,0:T(8,128)(2,1)S(1)}, u32[]{:S(2)}, u32[]{:S(2)}) collective-permute-start(bf16[16,3200]{1,0:T(8,128)(2,1)S(1)} %shard_map.97), channel_id=1, source_target_pairs={{0,4},{1,3},{4,8},{5,1},{8,12},{9,5},{12,14},{13,9},{14,10},{15,13... | collective-permute-start | bytes 307208 | tf_op jit(solution)/shard_map/ppermute | solution.py:393
  34.6 1.9 %collective-permute-start.22 = (bf16[16,3200]{1,0:T(8,128)(2,1)S(1)}, bf16[16,3200]{1,0:T(8,128)(2,1)S(1)}, u32[]{:S(2)}, u32[]{:S(2)}) collective-permute-start(bf16[16,3200]{1,0:T(8,128)(2,1)S(1)} %shard_map.102), channel_id=1, source_target_pairs={{0,14},{1,15},{4,10},{5,11},{8,6},{9,7},{12,2},{13,3},{14,0},{15,1... | collective-permute-start | bytes 307208 | tf_op jit(solution)/shard_map/ppermute | solution.py:393
  38.0 2.0 %collective-permute-start.18 = (bf16[16,3200]{1,0:T(8,128)(2,1)S(1)}, bf16[16,3200]{1,0:T(8,128)(2,1)S(1)}, u32[]{:S(2)}, u32[]{:S(2)}) collective-permute-start(bf16[16,3200]{1,0:T(8,128)(2,1)S(1)} %shard_map.98), channel_id=1, source_target_pairs={{0,4},{1,3},{4,8},{5,1},{8,12},{9,5},{12,14},{13,9},{14,10},{15,13... | collective-permute-start | bytes 307208 | tf_op jit(solution)/shard_map/ppermute | solution.py:393
  40.1 2.1 %collective-permute-done.22.refs_6_ = bf16[16,3200]{1,0:T(8,128)(2,1)S(1)} collective-permute-done((bf16[16,3200]{1,0:T(8,128)(2,1)S(1)}, bf16[16,3200]{1,0:T(8,128)(2,1)S(1)}, u32[]{:S(2)}, u32[]{:S(2)}) %collective-permute-start.22) | collective-permute-done | bytes 102432 | tf_op jit(solution)/shard_map/ppermute | solution.py:393
  44.1 1.5 %collective-permute-start.19 = (bf16[16,3200]{1,0:T(8,128)(2,1)S(1)}, bf16[16,3200]{1,0:T(8,128)(2,1)S(1)}, u32[]{:S(2)}, u32[]{:S(2)}) collective-permute-start(bf16[16,3200]{1,0:T(8,128)(2,1)S(1)} %shard_map.99), channel_id=1, source_target_pairs={{0,4},{1,3},{4,8},{5,1},{8,12},{9,5},{12,14},{13,9},{14,10},{15,13... | collective-permute-start | bytes 307208 | tf_op jit(solution)/shard_map/ppermute | solution.py:393
  45.6 2.2 %collective-permute-done.23 = bf16[16,3200]{1,0:T(8,128)(2,1)S(1)} collective-permute-done((bf16[16,3200]{1,0:T(8,128)(2,1)S(1)}, bf16[16,3200]{1,0:T(8,128)(2,1)S(1)}, u32[]{:S(2)}, u32[]{:S(2)}) %collective-permute-start.23) | collective-permute-done | bytes 102432 | tf_op jit(solution)/shard_map/ppermute | solution.py:393
  49.6 1.1 %collective-permute-start.26 = (bf16[16,3200]{1,0:T(8,128)(2,1)S(1)}, bf16[16,3200]{1,0:T(8,128)(2,1)S(1)}, u32[]{:S(2)}, u32[]{:S(2)}) collective-permute-start(bf16[16,3200]{1,0:T(8,128)(2,1)S(1)} %get-tuple-element.47.refs_0_), channel_id=1, source_target_pairs={{0,4},{1,3},{4,8},{5,1},{8,12},{9,5},{12,14},{13,9},{14,10},{15,13... | collective-permute-start | bytes 307208 | tf_op jit(solution)/shard_map/ppermute | solution.py:393
  50.7 2.4 %collective-permute-start.27 = (bf16[16,3200]{1,0:T(8,128)(2,1)S(1)}, bf16[16,3200]{1,0:T(8,128)(2,1)S(1)}, u32[]{:S(2)}, u32[]{:S(2)}) collective-permute-start(bf16[16,3200]{1,0:T(8,128)(2,1)S(1)} %collective-permute-done.25.refs_1_), channel_id=1, source_target_pairs={{0,4},{1,3},{4,8},{5,1},{8,12},{9,5},{12,14},{13,9},{14,10},{15,13... | collective-permute-start | bytes 307208 | tf_op jit(solution)/shard_map/ppermute | solution.py:393
  53.1 1.1 %collective-permute-done.26.refs_2_ = bf16[16,3200]{1,0:T(8,128)(2,1)S(1)} collective-permute-done((bf16[16,3200]{1,0:T(8,128)(2,1)S(1)}, bf16[16,3200]{1,0:T(8,128)(2,1)S(1)}, u32[]{:S(2)}, u32[]{:S(2)}) %collective-permute-start.26) | collective-permute-done | bytes 102432 | tf_op jit(solution)/shard_map/ppermute | solution.py:393
  54.2 1.1 %collective-permute-start.30 = (bf16[16,3200]{1,0:T(8,128)(2,1)S(1)}, bf16[16,3200]{1,0:T(8,128)(2,1)S(1)}, u32[]{:S(2)}, u32[]{:S(2)}) collective-permute-start(bf16[16,3200]{1,0:T(8,128)(2,1)S(1)} %collective-permute-done.26.refs_2_), channel_id=1, source_target_pairs={{0,4},{1,3},{4,8},{5,1},{8,12},{9,5},{12,14},{13,9},{14,10},{15,13... | collective-permute-start | bytes 307208 | tf_op jit(solution)/shard_map/ppermute | solution.py:393
  55.4 2.4 %collective-permute-start.31 = (bf16[16,3200]{1,0:T(8,128)(2,1)S(1)}, bf16[16,3200]{1,0:T(8,128)(2,1)S(1)}, u32[]{:S(2)}, u32[]{:S(2)}) collective-permute-start(bf16[16,3200]{1,0:T(8,128)(2,1)S(1)} %collective-permute-done.27.refs_3_), channel_id=1, source_target_pairs={{0,4},{1,3},{4,8},{5,1},{8,12},{9,5},{12,14},{13,9},{14,10},{15,13... | collective-permute-start | bytes 307208 | tf_op jit(solution)/shard_map/ppermute | solution.py:393
  57.7 1.4 %collective-permute-start.38 = (bf16[16,3200]{1,0:T(8,128)(2,1)S(1)}, bf16[16,3200]{1,0:T(8,128)(2,1)S(1)}, u32[]{:S(2)}, u32[]{:S(2)}) collective-permute-start(bf16[16,3200]{1,0:T(8,128)(2,1)S(1)} %get-tuple-element.47.refs_0_), channel_id=1, source_target_pairs={{0,14},{1,15},{4,10},{5,11},{8,6},{9,7},{12,2},{13,3},{14,0},{15,1... | collective-permute-start | bytes 307208 | tf_op jit(solution)/shard_map/ppermute | solution.py:393
  60.3 3.9 %collective-permute-start.35 = (bf16[16,3200]{1,0:T(8,128)(2,1)S(1)}, bf16[16,3200]{1,0:T(8,128)(2,1)S(1)}, u32[]{:S(2)}, u32[]{:S(2)}) collective-permute-start(bf16[16,3200]{1,0:T(8,128)(2,1)S(1)} %collective-permute-done.31.refs_7_), channel_id=1, source_target_pairs={{0,4},{1,3},{4,8},{5,1},{8,12},{9,5},{12,14},{13,9},{14,10},{15,13... | collective-permute-start | bytes 307208 | tf_op jit(solution)/shard_map/ppermute | solution.py:393
  64.3 1.6 %collective-permute-done.38.refs_14_ = bf16[16,3200]{1,0:T(8,128)(2,1)S(1)} collective-permute-done((bf16[16,3200]{1,0:T(8,128)(2,1)S(1)}, bf16[16,3200]{1,0:T(8,128)(2,1)S(1)}, u32[]{:S(2)}, u32[]{:S(2)}) %collective-permute-start.38) | collective-permute-done | bytes 102432 | tf_op jit(solution)/shard_map/ppermute | solution.py:393
  68.4 3.5 %shard_map.105 = (f32[3,512,512]{2,1,0:T(8,128)S(1)}, bf16[2,16,3200]{2,1,0:T(8,128)(2,1)S(1)}, bf16[6,16,3200]{2,1,0:T(8,128)(2,1)S(1)}, f32[8,128]{1,0:T(8,128)S(1)}, f32[8,128]{1,0:T(8,128)S(1)}) custom-call(s32[1]{0:T(128)} %bitcast.me_ref.refs_0_.refs_2_, s32[17]{0:T(128)S(1)} %pad_add_fusion.ints_ref, bf16[16,3200]{1,0:T(8,128)(2,1)S(1)} %get-tuple-element.47.refs_0_, ...), custom_call_target="tpu_custom_call" | custom-call | flops 4294967296 | bytes 8388608 | tf_op jit(solution)/shard_map/pallas_call | solution.py:253
  71.9 2.6 %collective-permute-start.40 = (bf16[2,16,3200]{2,1,0:T(8,128)(2,1)S(1)}, bf16[2,16,3200]{2,1,0:T(8,128)(2,1)S(1)}, u32[]{:S(2)}, u32[]{:S(2)}) collective-permute-start(bf16[2,16,3200]{2,1,0:T(8,128)(2,1)S(1)} %get-tuple-element.52), channel_id=1, source_target_pairs={{0,1},{1,0},{2,3},{3,2},{4,5},{5,4},{6,7},{7,6},{8,9},{9,8},{10,11... | collective-permute-start | bytes 614408 | tf_op jit(solution)/shard_map/ppermute | solution.py:384
  76.0 2.0 %collective-permute-start.45 = (bf16[16,3200]{1,0:T(8,128)(2,1)S(1)}, bf16[16,3200]{1,0:T(8,128)(2,1)S(1)}, u32[]{:S(2)}, u32[]{:S(2)}) collective-permute-start(bf16[16,3200]{1,0:T(8,128)(2,1)S(1)} %shard_map.109), channel_id=1, source_target_pairs={{0,4},{1,3},{4,8},{5,1},{8,12},{9,5},{12,14},{13,9},{14,10},{15,13... | collective-permute-start | bytes 307208 | tf_op jit(solution)/shard_map/ppermute | solution.py:393
  78.0 2.5 %collective-permute-start.42 = (bf16[16,3200]{1,0:T(8,128)(2,1)S(1)}, bf16[16,3200]{1,0:T(8,128)(2,1)S(1)}, u32[]{:S(2)}, u32[]{:S(2)}) collective-permute-start(bf16[16,3200]{1,0:T(8,128)(2,1)S(1)} %shard_map.106), channel_id=1, source_target_pairs={{0,4},{1,3},{4,8},{5,1},{8,12},{9,5},{12,14},{13,9},{14,10},{15,13... | collective-permute-start | bytes 307208 | tf_op jit(solution)/shard_map/ppermute | solution.py:393
  80.5 1.1 %collective-permute-start.47 = (bf16[16,3200]{1,0:T(8,128)(2,1)S(1)}, bf16[16,3200]{1,0:T(8,128)(2,1)S(1)}, u32[]{:S(2)}, u32[]{:S(2)}) collective-permute-start(bf16[16,3200]{1,0:T(8,128)(2,1)S(1)} %shard_map.111), channel_id=1, source_target_pairs={{0,14},{1,15},{4,10},{5,11},{8,6},{9,7},{12,2},{13,3},{14,0},{15,1... | collective-permute-start | bytes 307208 | tf_op jit(solution)/shard_map/ppermute | solution.py:393
  82.8 2.5 %collective-permute-start.43 = (bf16[16,3200]{1,0:T(8,128)(2,1)S(1)}, bf16[16,3200]{1,0:T(8,128)(2,1)S(1)}, u32[]{:S(2)}, u32[]{:S(2)}) collective-permute-start(bf16[16,3200]{1,0:T(8,128)(2,1)S(1)} %shard_map.107), channel_id=1, source_target_pairs={{0,4},{1,3},{4,8},{5,1},{8,12},{9,5},{12,14},{13,9},{14,10},{15,13... | collective-permute-start | bytes 307208 | tf_op jit(solution)/shard_map/ppermute | solution.py:393
  85.3 2.9 %collective-permute-done.47.refs_8_ = bf16[16,3200]{1,0:T(8,128)(2,1)S(1)} collective-permute-done((bf16[16,3200]{1,0:T(8,128)(2,1)S(1)}, bf16[16,3200]{1,0:T(8,128)(2,1)S(1)}, u32[]{:S(2)}, u32[]{:S(2)}) %collective-permute-start.47) | collective-permute-done | bytes 102432 | tf_op jit(solution)/shard_map/ppermute | solution.py:393
  88.9 1.8 %collective-permute-start.44 = (bf16[16,3200]{1,0:T(8,128)(2,1)S(1)}, bf16[16,3200]{1,0:T(8,128)(2,1)S(1)}, u32[]{:S(2)}, u32[]{:S(2)}) collective-permute-start(bf16[16,3200]{1,0:T(8,128)(2,1)S(1)} %shard_map.108), channel_id=1, source_target_pairs={{0,4},{1,3},{4,8},{5,1},{8,12},{9,5},{12,14},{13,9},{14,10},{15,13... | collective-permute-start | bytes 307208 | tf_op jit(solution)/shard_map/ppermute | solution.py:393
  90.8 2.2 %collective-permute-done.48 = bf16[16,3200]{1,0:T(8,128)(2,1)S(1)} collective-permute-done((bf16[16,3200]{1,0:T(8,128)(2,1)S(1)}, bf16[16,3200]{1,0:T(8,128)(2,1)S(1)}, u32[]{:S(2)}, u32[]{:S(2)}) %collective-permute-start.48) | collective-permute-done | bytes 102432 | tf_op jit(solution)/shard_map/ppermute | solution.py:393
  (99 shorter events, 22.8 us)
Async XLA Ops:
  1.1 5.4 %collective-permute-start.4 = (bf16[3,32,512]{2,1,0:T(8,128)(2,1)}, bf16[3,32,512]{2,1,0:T(8,128)(2,1)S(1)}, u32[]{:S(2)}, u32[]{:S(2)}) collective-permute-start(bf16[3,32,512]{2,1,0:T(8,128)(2,1)} %wave_ref.3), channel_id=1, source_target_pairs={{0,4},{1,3},{4,8},{5,1},{8,12},{9,5},{12,14},{13,9},{14,10},{15,13... | collective-permute-start | bytes 294920 | tf_op jit(solution)/shard_map/ppermute | solution.py:393
  3.8 4.8 %collective-permute-start.2 = (bf16[3,32,512]{2,1,0:T(8,128)(2,1)S(1)}, bf16[3,32,512]{2,1,0:T(8,128)(2,1)S(1)}, u32[]{:S(2)}, u32[]{:S(2)}) collective-permute-start(bf16[3,32,512]{2,1,0:T(8,128)(2,1)S(1)} %collective-permute-done.refs_1_), channel_id=1, source_target_pairs={{0,4},{1,3},{4,8},{5,1},{8,12},{9,5},{12,14},{13,9},{14,10},{15,13... | collective-permute-start | bytes 294920 | tf_op jit(solution)/shard_map/ppermute | solution.py:393
  6.5 7.5 %collective-permute-start.7 = (bf16[3,32,512]{2,1,0:T(8,128)(2,1)S(1)}, bf16[3,32,512]{2,1,0:T(8,128)(2,1)S(1)}, u32[]{:S(2)}, u32[]{:S(2)}) collective-permute-start(bf16[3,32,512]{2,1,0:T(8,128)(2,1)S(1)} %collective-permute-done.4.refs_2_), channel_id=1, source_target_pairs={{0,4},{1,3},{4,8},{5,1},{8,12},{9,5},{12,14},{13,9},{14,10},{15,13... | collective-permute-start | bytes 294920 | tf_op jit(solution)/shard_map/ppermute | solution.py:393
  8.6 7.2 %collective-permute-start.3 = (bf16[3,32,512]{2,1,0:T(8,128)(2,1)S(1)}, bf16[3,32,512]{2,1,0:T(8,128)(2,1)S(1)}, u32[]{:S(2)}, u32[]{:S(2)}) collective-permute-start(bf16[3,32,512]{2,1,0:T(8,128)(2,1)S(1)} %collective-permute-done.2.refs_3_), channel_id=1, source_target_pairs={{0,4},{1,3},{4,8},{5,1},{8,12},{9,5},{12,14},{13,9},{14,10},{15,13... | collective-permute-start | bytes 294920 | tf_op jit(solution)/shard_map/ppermute | solution.py:393
  10.9 7.7 %collective-permute-start.1 = (bf16[3,32,512]{2,1,0:T(8,128)(2,1)}, bf16[3,32,512]{2,1,0:T(8,128)(2,1)S(1)}, u32[]{:S(2)}, u32[]{:S(2)}) collective-permute-start(bf16[3,32,512]{2,1,0:T(8,128)(2,1)} %wave_ref.3), channel_id=1, source_target_pairs={{0,14},{1,15},{4,10},{5,11},{8,6},{9,7},{12,2},{13,3},{14,0},{15,1... | collective-permute-start | bytes 294920 | tf_op jit(solution)/shard_map/ppermute | solution.py:393
  14.0 5.6 %collective-permute-start.10 = (bf16[3,32,512]{2,1,0:T(8,128)(2,1)S(1)}, bf16[3,32,512]{2,1,0:T(8,128)(2,1)S(1)}, u32[]{:S(2)}, u32[]{:S(2)}) collective-permute-start(bf16[3,32,512]{2,1,0:T(8,128)(2,1)S(1)} %collective-permute-done.7.refs_6_), channel_id=1, source_target_pairs={{0,4},{1,3},{4,8},{5,1},{8,12},{9,5},{12,14},{13,9},{14,10},{15,13... | collective-permute-start | bytes 294920 | tf_op jit(solution)/shard_map/ppermute | solution.py:393
  14.1 5.6 %collective-permute-start.8 = (bf16[3,32,512]{2,1,0:T(8,128)(2,1)S(1)}, bf16[3,32,512]{2,1,0:T(8,128)(2,1)S(1)}, u32[]{:S(2)}, u32[]{:S(2)}) collective-permute-start(bf16[3,32,512]{2,1,0:T(8,128)(2,1)S(1)} %collective-permute-done.7.refs_6_), channel_id=1, source_target_pairs={{0,1},{1,0},{2,3},{3,2},{4,5},{5,4},{6,7},{7,6},{8,9},{9,8},{10,11... | collective-permute-start | bytes 294920 | tf_op jit(solution)/shard_map/ppermute | solution.py:384
  15.9 4.8 %collective-permute-start.11 = (bf16[3,32,512]{2,1,0:T(8,128)(2,1)S(1)}, bf16[3,32,512]{2,1,0:T(8,128)(2,1)S(1)}, u32[]{:S(2)}, u32[]{:S(2)}) collective-permute-start(bf16[3,32,512]{2,1,0:T(8,128)(2,1)S(1)} %collective-permute-done.3._.refs_7_), channel_id=1, source_target_pairs={{0,4},{1,3},{4,8},{5,1},{8,12},{9,5},{12,14},{13,9},{14,10},{15,13... | collective-permute-start | bytes 294920 | tf_op jit(solution)/shard_map/ppermute | solution.py:393
  32.1 4.7 %collective-permute-start.20 = (bf16[16,3200]{1,0:T(8,128)(2,1)S(1)}, bf16[16,3200]{1,0:T(8,128)(2,1)S(1)}, u32[]{:S(2)}, u32[]{:S(2)}) collective-permute-start(bf16[16,3200]{1,0:T(8,128)(2,1)S(1)} %shard_map.100), channel_id=1, source_target_pairs={{0,4},{1,3},{4,8},{5,1},{8,12},{9,5},{12,14},{13,9},{14,10},{15,13... | collective-permute-start | bytes 307208 | tf_op jit(solution)/shard_map/ppermute | solution.py:393
  32.3 5.7 %collective-permute-start.17 = (bf16[16,3200]{1,0:T(8,128)(2,1)S(1)}, bf16[16,3200]{1,0:T(8,128)(2,1)S(1)}, u32[]{:S(2)}, u32[]{:S(2)}) collective-permute-start(bf16[16,3200]{1,0:T(8,128)(2,1)S(1)} %shard_map.97), channel_id=1, source_target_pairs={{0,4},{1,3},{4,8},{5,1},{8,12},{9,5},{12,14},{13,9},{14,10},{15,13... | collective-permute-start | bytes 307208 | tf_op jit(solution)/shard_map/ppermute | solution.py:393
  34.6 7.5 %collective-permute-start.22 = (bf16[16,3200]{1,0:T(8,128)(2,1)S(1)}, bf16[16,3200]{1,0:T(8,128)(2,1)S(1)}, u32[]{:S(2)}, u32[]{:S(2)}) collective-permute-start(bf16[16,3200]{1,0:T(8,128)(2,1)S(1)} %shard_map.102), channel_id=1, source_target_pairs={{0,14},{1,15},{4,10},{5,11},{8,6},{9,7},{12,2},{13,3},{14,0},{15,1... | collective-permute-start | bytes 307208 | tf_op jit(solution)/shard_map/ppermute | solution.py:393
  36.9 6.1 %collective-permute-start.21 = (bf16[16,3200]{1,0:T(8,128)(2,1)S(1)}, bf16[16,3200]{1,0:T(8,128)(2,1)S(1)}, u32[]{:S(2)}, u32[]{:S(2)}) collective-permute-start(bf16[16,3200]{1,0:T(8,128)(2,1)S(1)} %shard_map.101), channel_id=1, source_target_pairs={{0,4},{1,3},{4,8},{5,1},{8,12},{9,5},{12,14},{13,9},{14,10},{15,13... | collective-permute-start | bytes 307208 | tf_op jit(solution)/shard_map/ppermute | solution.py:393
  38.0 6.1 %collective-permute-start.18 = (bf16[16,3200]{1,0:T(8,128)(2,1)S(1)}, bf16[16,3200]{1,0:T(8,128)(2,1)S(1)}, u32[]{:S(2)}, u32[]{:S(2)}) collective-permute-start(bf16[16,3200]{1,0:T(8,128)(2,1)S(1)} %shard_map.98), channel_id=1, source_target_pairs={{0,4},{1,3},{4,8},{5,1},{8,12},{9,5},{12,14},{13,9},{14,10},{15,13... | collective-permute-start | bytes 307208 | tf_op jit(solution)/shard_map/ppermute | solution.py:393
  43.1 4.7 %collective-permute-start.23 = (bf16[16,3200]{1,0:T(8,128)(2,1)S(1)}, bf16[16,3200]{1,0:T(8,128)(2,1)S(1)}, u32[]{:S(2)}, u32[]{:S(2)}) collective-permute-start(bf16[16,3200]{1,0:T(8,128)(2,1)S(1)} %shard_map.103), channel_id=1, source_target_pairs={{0,4},{1,3},{4,8},{5,1},{8,12},{9,5},{12,14},{13,9},{14,10},{15,13... | collective-permute-start | bytes 307208 | tf_op jit(solution)/shard_map/ppermute | solution.py:393
  44.1 4.7 %collective-permute-start.19 = (bf16[16,3200]{1,0:T(8,128)(2,1)S(1)}, bf16[16,3200]{1,0:T(8,128)(2,1)S(1)}, u32[]{:S(2)}, u32[]{:S(2)}) collective-permute-start(bf16[16,3200]{1,0:T(8,128)(2,1)S(1)} %shard_map.99), channel_id=1, source_target_pairs={{0,4},{1,3},{4,8},{5,1},{8,12},{9,5},{12,14},{13,9},{14,10},{15,13... | collective-permute-start | bytes 307208 | tf_op jit(solution)/shard_map/ppermute | solution.py:393
  49.6 4.7 %collective-permute-start.26 = (bf16[16,3200]{1,0:T(8,128)(2,1)S(1)}, bf16[16,3200]{1,0:T(8,128)(2,1)S(1)}, u32[]{:S(2)}, u32[]{:S(2)}) collective-permute-start(bf16[16,3200]{1,0:T(8,128)(2,1)S(1)} %get-tuple-element.47.refs_0_), channel_id=1, source_target_pairs={{0,4},{1,3},{4,8},{5,1},{8,12},{9,5},{12,14},{13,9},{14,10},{15,13... | collective-permute-start | bytes 307208 | tf_op jit(solution)/shard_map/ppermute | solution.py:393
  50.7 4.7 %collective-permute-start.27 = (bf16[16,3200]{1,0:T(8,128)(2,1)S(1)}, bf16[16,3200]{1,0:T(8,128)(2,1)S(1)}, u32[]{:S(2)}, u32[]{:S(2)}) collective-permute-start(bf16[16,3200]{1,0:T(8,128)(2,1)S(1)} %collective-permute-done.25.refs_1_), channel_id=1, source_target_pairs={{0,4},{1,3},{4,8},{5,1},{8,12},{9,5},{12,14},{13,9},{14,10},{15,13... | collective-permute-start | bytes 307208 | tf_op jit(solution)/shard_map/ppermute | solution.py:393
  54.2 4.9 %collective-permute-start.30 = (bf16[16,3200]{1,0:T(8,128)(2,1)S(1)}, bf16[16,3200]{1,0:T(8,128)(2,1)S(1)}, u32[]{:S(2)}, u32[]{:S(2)}) collective-permute-start(bf16[16,3200]{1,0:T(8,128)(2,1)S(1)} %collective-permute-done.26.refs_2_), channel_id=1, source_target_pairs={{0,4},{1,3},{4,8},{5,1},{8,12},{9,5},{12,14},{13,9},{14,10},{15,13... | collective-permute-start | bytes 307208 | tf_op jit(solution)/shard_map/ppermute | solution.py:393
  55.4 5.0 %collective-permute-start.31 = (bf16[16,3200]{1,0:T(8,128)(2,1)S(1)}, bf16[16,3200]{1,0:T(8,128)(2,1)S(1)}, u32[]{:S(2)}, u32[]{:S(2)}) collective-permute-start(bf16[16,3200]{1,0:T(8,128)(2,1)S(1)} %collective-permute-done.27.refs_3_), channel_id=1, source_target_pairs={{0,4},{1,3},{4,8},{5,1},{8,12},{9,5},{12,14},{13,9},{14,10},{15,13... | collective-permute-start | bytes 307208 | tf_op jit(solution)/shard_map/ppermute | solution.py:393
  57.7 6.6 %collective-permute-start.28 = (bf16[16,3200]{1,0:T(8,128)(2,1)S(1)}, bf16[16,3200]{1,0:T(8,128)(2,1)S(1)}, u32[]{:S(2)}, u32[]{:S(2)}) collective-permute-start(bf16[16,3200]{1,0:T(8,128)(2,1)S(1)} %collective-permute-done.26.refs_2_), channel_id=1, source_target_pairs={{0,1},{1,0},{2,3},{3,2},{4,5},{5,4},{6,7},{7,6},{8,9},{9,8},{10,11... | collective-permute-start | bytes 307208 | tf_op jit(solution)/shard_map/ppermute | solution.py:384
  57.7 8.2 %collective-permute-start.38 = (bf16[16,3200]{1,0:T(8,128)(2,1)S(1)}, bf16[16,3200]{1,0:T(8,128)(2,1)S(1)}, u32[]{:S(2)}, u32[]{:S(2)}) collective-permute-start(bf16[16,3200]{1,0:T(8,128)(2,1)S(1)} %get-tuple-element.47.refs_0_), channel_id=1, source_target_pairs={{0,14},{1,15},{4,10},{5,11},{8,6},{9,7},{12,2},{13,3},{14,0},{15,1... | collective-permute-start | bytes 307208 | tf_op jit(solution)/shard_map/ppermute | solution.py:393
  59.1 6.9 %collective-permute-start.34 = (bf16[16,3200]{1,0:T(8,128)(2,1)S(1)}, bf16[16,3200]{1,0:T(8,128)(2,1)S(1)}, u32[]{:S(2)}, u32[]{:S(2)}) collective-permute-start(bf16[16,3200]{1,0:T(8,128)(2,1)S(1)} %collective-permute-done.30.refs_6_), channel_id=1, source_target_pairs={{0,4},{1,3},{4,8},{5,1},{8,12},{9,5},{12,14},{13,9},{14,10},{15,13... | collective-permute-start | bytes 307208 | tf_op jit(solution)/shard_map/ppermute | solution.py:393
  60.0 6.5 %collective-permute-start.32 = (bf16[16,3200]{1,0:T(8,128)(2,1)S(1)}, bf16[16,3200]{1,0:T(8,128)(2,1)S(1)}, u32[]{:S(2)}, u32[]{:S(2)}) collective-permute-start(bf16[16,3200]{1,0:T(8,128)(2,1)S(1)} %collective-permute-done.30.refs_6_), channel_id=1, source_target_pairs={{0,1},{1,0},{2,3},{3,2},{4,5},{5,4},{6,7},{7,6},{8,9},{9,8},{10,11... | collective-permute-start | bytes 307208 | tf_op jit(solution)/shard_map/ppermute | solution.py:384
  60.3 6.7 %collective-permute-start.35 = (bf16[16,3200]{1,0:T(8,128)(2,1)S(1)}, bf16[16,3200]{1,0:T(8,128)(2,1)S(1)}, u32[]{:S(2)}, u32[]{:S(2)}) collective-permute-start(bf16[16,3200]{1,0:T(8,128)(2,1)S(1)} %collective-permute-done.31.refs_7_), channel_id=1, source_target_pairs={{0,4},{1,3},{4,8},{5,1},{8,12},{9,5},{12,14},{13,9},{14,10},{15,13... | collective-permute-start | bytes 307208 | tf_op jit(solution)/shard_map/ppermute | solution.py:393
  75.5 4.9 %collective-permute-start.41 = (bf16[6,16,3200]{2,1,0:T(8,128)(2,1)S(1)}, bf16[6,16,3200]{2,1,0:T(8,128)(2,1)S(1)}, u32[]{:S(2)}, u32[]{:S(2)}) collective-permute-start(bf16[6,16,3200]{2,1,0:T(8,128)(2,1)S(1)} %get-tuple-element.54), channel_id=1, source_target_pairs={{0,1},{1,0},{2,3},{3,2},{4,5},{5,4},{6,7},{7,6},{8,9},{9,8},{10,11... | collective-permute-start | bytes 1843208 | tf_op jit(solution)/shard_map/ppermute | solution.py:384
  76.0 5.7 %collective-permute-start.45 = (bf16[16,3200]{1,0:T(8,128)(2,1)S(1)}, bf16[16,3200]{1,0:T(8,128)(2,1)S(1)}, u32[]{:S(2)}, u32[]{:S(2)}) collective-permute-start(bf16[16,3200]{1,0:T(8,128)(2,1)S(1)} %shard_map.109), channel_id=1, source_target_pairs={{0,4},{1,3},{4,8},{5,1},{8,12},{9,5},{12,14},{13,9},{14,10},{15,13... | collective-permute-start | bytes 307208 | tf_op jit(solution)/shard_map/ppermute | solution.py:393
  78.0 4.7 %collective-permute-start.42 = (bf16[16,3200]{1,0:T(8,128)(2,1)S(1)}, bf16[16,3200]{1,0:T(8,128)(2,1)S(1)}, u32[]{:S(2)}, u32[]{:S(2)}) collective-permute-start(bf16[16,3200]{1,0:T(8,128)(2,1)S(1)} %shard_map.106), channel_id=1, source_target_pairs={{0,4},{1,3},{4,8},{5,1},{8,12},{9,5},{12,14},{13,9},{14,10},{15,13... | collective-permute-start | bytes 307208 | tf_op jit(solution)/shard_map/ppermute | solution.py:393
  80.5 7.7 %collective-permute-start.47 = (bf16[16,3200]{1,0:T(8,128)(2,1)S(1)}, bf16[16,3200]{1,0:T(8,128)(2,1)S(1)}, u32[]{:S(2)}, u32[]{:S(2)}) collective-permute-start(bf16[16,3200]{1,0:T(8,128)(2,1)S(1)} %shard_map.111), channel_id=1, source_target_pairs={{0,14},{1,15},{4,10},{5,11},{8,6},{9,7},{12,2},{13,3},{14,0},{15,1... | collective-permute-start | bytes 307208 | tf_op jit(solution)/shard_map/ppermute | solution.py:393
  81.7 6.5 %collective-permute-start.46 = (bf16[16,3200]{1,0:T(8,128)(2,1)S(1)}, bf16[16,3200]{1,0:T(8,128)(2,1)S(1)}, u32[]{:S(2)}, u32[]{:S(2)}) collective-permute-start(bf16[16,3200]{1,0:T(8,128)(2,1)S(1)} %shard_map.110), channel_id=1, source_target_pairs={{0,4},{1,3},{4,8},{5,1},{8,12},{9,5},{12,14},{13,9},{14,10},{15,13... | collective-permute-start | bytes 307208 | tf_op jit(solution)/shard_map/ppermute | solution.py:393
  82.8 6.1 %collective-permute-start.43 = (bf16[16,3200]{1,0:T(8,128)(2,1)S(1)}, bf16[16,3200]{1,0:T(8,128)(2,1)S(1)}, u32[]{:S(2)}, u32[]{:S(2)}) collective-permute-start(bf16[16,3200]{1,0:T(8,128)(2,1)S(1)} %shard_map.107), channel_id=1, source_target_pairs={{0,4},{1,3},{4,8},{5,1},{8,12},{9,5},{12,14},{13,9},{14,10},{15,13... | collective-permute-start | bytes 307208 | tf_op jit(solution)/shard_map/ppermute | solution.py:393
  88.3 4.7 %collective-permute-start.48 = (bf16[16,3200]{1,0:T(8,128)(2,1)S(1)}, bf16[16,3200]{1,0:T(8,128)(2,1)S(1)}, u32[]{:S(2)}, u32[]{:S(2)}) collective-permute-start(bf16[16,3200]{1,0:T(8,128)(2,1)S(1)} %shard_map.112), channel_id=1, source_target_pairs={{0,4},{1,3},{4,8},{5,1},{8,12},{9,5},{12,14},{13,9},{14,10},{15,13... | collective-permute-start | bytes 307208 | tf_op jit(solution)/shard_map/ppermute | solution.py:393
  88.9 5.1 %collective-permute-start.44 = (bf16[16,3200]{1,0:T(8,128)(2,1)S(1)}, bf16[16,3200]{1,0:T(8,128)(2,1)S(1)}, u32[]{:S(2)}, u32[]{:S(2)}) collective-permute-start(bf16[16,3200]{1,0:T(8,128)(2,1)S(1)} %shard_map.108), channel_id=1, source_target_pairs={{0,4},{1,3},{4,8},{5,1},{8,12},{9,5},{12,14},{13,9},{14,10},{15,13... | collective-permute-start | bytes 307208 | tf_op jit(solution)/shard_map/ppermute | solution.py:393
  (23 other events, 112.3 us)
